TPU v7x, 32 devices: a whole 2x2x4 slice. The times are simulated.
32 devices in a mesh: dom: 8 (over z, core), repl: 4 (over y, x).
Axes of the slice: x: 2, y: 2, z: 4, core: 2. Of those that a mesh axis runs over, the one named last changes fastest.
Arguments:
- features: bfloat16 [8192, 512], P(('dom', 'repl')), may hold values from -6 to 6
- cotangent: bfloat16 [8192, 512], P(('dom', 'repl')), may hold values from -6 to 6
- weight: bfloat16 [512, 512], replicated, may hold values from -0.25 to 0.25
- tiles: bfloat16 [8, 4, 8, 16, 128, 128], P('dom', 'repl'), may hold values from -0.09375 to 0.09375
- tile_rows: int32 [8, 4, 8, 16], P('dom', 'repl'), may hold values from 0 to 7
- tile_cols: int32 [8, 4, 8, 16], P('dom', 'repl'), may hold values from 0 to 1
- tile_counts: int32 [8, 4, 8], P('dom', 'repl'), may hold values from 1 to 16, as said below
Outputs:
- activated: bfloat16 [8192, 512], P(('dom', 'repl'))
- feature_grad: bfloat16 [8192, 512], P(('dom', 'repl'))
- weight_grad: float32 [512, 512], replicated
Inputs may be any that keep to these rules, and one draw needn't show every extreme that they name: `tile_counts`: live tiles of each row block, column group and column block; some entry equals 16 in every draw.
All inputs are finite; a program needn't handle non-finite values.
Results may differ from a plain program's by a relative error of at most 0.006.
Values may be sent and summed in bfloat16 or wider, within the bound.
No kernel may reach another device: no remote copies, remote signals or barrier semaphores. Data moves between devices by JAX's collectives and lax.ppermute only.
A program may use at most 64 MiB of HBM per device.

v0:
```python
import jax
import jax.numpy as jnp
from jax import lax
from jax.sharding import PartitionSpec as P


def shifted(x, axis, by):
    length = lax.axis_size(axis)
    return lax.ppermute(x, axis, [(i, (i + by) % length) for i in range(length)])


def silu_slope(preact):
    sigma = jax.nn.sigmoid(preact)
    return sigma * (1.0 + preact * (1.0 - sigma))


def place_tiles(indices, prod, count):
    selector = (jnp.arange(count, dtype=jnp.int32)[:, None] == indices[None, :]).astype(jnp.float32)
    return jnp.einsum("rt,taf->raf", selector, prod, precision=lax.Precision.HIGHEST)


def local(features, cotangent, weight, tiles, tile_rows, tile_cols, tile_counts):
    blocks_count = lax.axis_size("dom")
    group_count = lax.axis_size("repl")
    rows_local, width = features.shape
    tile_size = tiles.shape[-1]
    slot_count = tiles.shape[3]
    col_tiles = rows_local // tile_size
    row_tiles = group_count * col_tiles
    slabs = tiles[0, 0]
    row_index = tile_rows[0, 0]
    col_index = tile_cols[0, 0]
    live_counts = tile_counts[0, 0]
    position = lax.axis_index("dom")
    scale = float(rows_local * blocks_count * group_count) ** (-0.5)

    def live_slab(column):
        slab_one = lax.dynamic_index_in_dim(slabs, column, 0, keepdims=False)
        alive = (jnp.arange(slot_count) < live_counts[column]).astype(jnp.bfloat16)
        return slab_one * alive[:, None, None]

    def forward_add(totals, source, column):
        slab_one = live_slab(column)
        picked = source.reshape(col_tiles, tile_size, width)[col_index[column]]
        prod = jnp.einsum("tab,tbf->taf", slab_one, picked, preferred_element_type=jnp.float32)
        return totals + place_tiles(row_index[column], prod, row_tiles)

    totals = forward_add(jnp.zeros((row_tiles, tile_size, width), jnp.float32), features, position)

    def forward_section(section, carry):
        sums, source = carry
        source = shifted(source, "dom", 1)
        return (forward_add(sums, source, (position - section) % blocks_count), source)

    totals, _ = lax.fori_loop(1, blocks_count, forward_section, (totals, features))
    totals = totals.reshape(row_tiles * tile_size, width)
    block_rows = lax.psum(totals, "repl")
    agg_rounded = block_rows.astype(jnp.bfloat16)
    preact = jnp.dot(agg_rounded, weight, preferred_element_type=jnp.float32)
    member = lax.axis_index("repl")
    own_pre = lax.dynamic_slice_in_dim(preact, member * rows_local, rows_local, 0)
    activated = jax.nn.silu(own_pre).astype(jnp.bfloat16)
    block_cot = lax.all_gather(cotangent, "repl", axis=0, tiled=True)
    pre_grad = (block_cot.astype(jnp.float32) * silu_slope(preact)).astype(jnp.bfloat16)
    weight_part = lax.dot_general(
        agg_rounded, pre_grad, (((0,), (0,)), ((), ())), preferred_element_type=jnp.float32
    )
    weight_grad = lax.psum(weight_part, "dom") * scale
    block_grad = lax.dot_general(
        pre_grad, weight, (((1,), (1,)), ((), ())), preferred_element_type=jnp.float32
    ).astype(jnp.bfloat16)
    grad_tiles = block_grad.reshape(row_tiles, tile_size, width)

    def backward_block(column):
        slab_one = live_slab(column)
        picked = grad_tiles[row_index[column]]
        prod = jnp.einsum("tab,taf->tbf", slab_one, picked, preferred_element_type=jnp.float32)
        return place_tiles(col_index[column], prod, col_tiles).reshape(rows_local, width)

    partial_value = backward_block((position - 1) % blocks_count)

    def backward_section(section, running):
        arrived = shifted(running, "dom", 1)
        return arrived + backward_block((position - section - 1) % blocks_count)

    summed = lax.fori_loop(1, blocks_count, backward_section, partial_value)
    feature_grad = summed.astype(jnp.bfloat16)
    return (activated, feature_grad, weight_grad)


def solution(mesh):
    in_specs = (
        P(("dom", "repl"), None),
        P(("dom", "repl"), None),
        P(),
        P("dom", "repl", None, None, None, None),
        P("dom", "repl", None, None),
        P("dom", "repl", None, None),
        P("dom", "repl", None),
    )
    out_specs = (P(("dom", "repl"), None), P(("dom", "repl"), None), P())
    return jax.shard_map(local, mesh=mesh, in_specs=in_specs, out_specs=out_specs, check_vma=False)
```

profile of v0, /device:TPU:0, one launch (start us, length us, event | category | flops | bytes accessed | tf_op | source)
XLA Modules:
  0.0 330.5 jit_solution(1393519253776142268)
XLA Ops:
  14.2 5.3 %fusion.30 = f32[8,128,512]{2,0,1:T(8,128)} fusion(f32[16,128,512]{2,1,0:T(8,128)S(1)} %fusion.33, s32[16]{0:T(128)S(1)} %fusion.50), kind=kOutput, calls=%fused_computation.45 | convolution fusion | flops 100663424 | bytes 6291520 | tf_op jit(solution)/shard_map/rt,taf->raf/dot_general | solution.py:19
  19.6 115.6 %while.32 = (s32[]{:T(128)}, f32[8,128,512]{2,0,1:T(8,128)}, bf16[256,512]{1,0:T(8,128)(2,1)S(1)}, s32[]{:T(128)}, s32[8,16]{1,0:T(8,128)}, /*index=5*/bf16[8,16...) while((s32[]{:T(128)}, f32[8,128,512]{2,0,1:T(8,128)}, ...), condition=%wide.region_1.2_spmd, body=%wide.region_0.1_spmd.sunk | while | flops 369886432 | bytes 37753740 | solution.py:55
  22.7 5.4 %collective-permute-done = bf16[256,512]{1,0:T(8,128)(2,1)S(1)} collective-permute-done((bf16[256,512]{1,0:T(8,128)(2,1)S(1)}, bf16[256,512]{1,0:T(8,128)(2,1)S(1)}, u32[]{:S(2)}, u32[]{:S(2)}) %collective-permute-start) | collective-permute-done | bytes 262176 | tf_op jit(solution)/shard_map/while/body/eval_jaxpr/ppermute | solution.py:9
  30.8 4.8 %fusion.88 = f32[8,128,512]{2,0,1:T(8,128)S(1)} fusion(f32[8,128,512]{2,0,1:T(8,128)S(1)} %copy-done.3, f32[16,128,512]{2,1,0:T(8,128)S(1)} %fusion.86, s32[16]{0:T(128)S(1)} %fusion.87), kind=kOutput, calls=%fused_computation.6.clone.1 | convolution fusion | flops 101187712 | bytes 8388672 | tf_op jit(solution)/shard_map/while/body/eval_jaxpr/rt,taf->raf/dot_general | solution.py:19
  39.6 4.9 %collective-permute-done = bf16[256,512]{1,0:T(8,128)(2,1)S(1)} collective-permute-done((bf16[256,512]{1,0:T(8,128)(2,1)S(1)}, bf16[256,512]{1,0:T(8,128)(2,1)S(1)}, u32[]{:S(2)}, u32[]{:S(2)}) %collective-permute-start) | collective-permute-done | bytes 262176 | tf_op jit(solution)/shard_map/while/body/eval_jaxpr/ppermute | solution.py:9
  47.1 4.8 %fusion.88 = f32[8,128,512]{2,0,1:T(8,128)S(1)} fusion(f32[8,128,512]{2,0,1:T(8,128)S(1)} %copy-done.3, f32[16,128,512]{2,1,0:T(8,128)S(1)} %fusion.86, s32[16]{0:T(128)S(1)} %fusion.87), kind=kOutput, calls=%fused_computation.6.clone.1 | convolution fusion | flops 101187712 | bytes 8388672 | tf_op jit(solution)/shard_map/while/body/eval_jaxpr/rt,taf->raf/dot_general | solution.py:19
  55.9 4.9 %collective-permute-done = bf16[256,512]{1,0:T(8,128)(2,1)S(1)} collective-permute-done((bf16[256,512]{1,0:T(8,128)(2,1)S(1)}, bf16[256,512]{1,0:T(8,128)(2,1)S(1)}, u32[]{:S(2)}, u32[]{:S(2)}) %collective-permute-start) | collective-permute-done | bytes 262176 | tf_op jit(solution)/shard_map/while/body/eval_jaxpr/ppermute | solution.py:9
  63.5 4.8 %fusion.88 = f32[8,128,512]{2,0,1:T(8,128)S(1)} fusion(f32[8,128,512]{2,0,1:T(8,128)S(1)} %copy-done.3, f32[16,128,512]{2,1,0:T(8,128)S(1)} %fusion.86, s32[16]{0:T(128)S(1)} %fusion.87), kind=kOutput, calls=%fused_computation.6.clone.1 | convolution fusion | flops 101187712 | bytes 8388672 | tf_op jit(solution)/shard_map/while/body/eval_jaxpr/rt,taf->raf/dot_general | solution.py:19
  72.3 4.9 %collective-permute-done = bf16[256,512]{1,0:T(8,128)(2,1)S(1)} collective-permute-done((bf16[256,512]{1,0:T(8,128)(2,1)S(1)}, bf16[256,512]{1,0:T(8,128)(2,1)S(1)}, u32[]{:S(2)}, u32[]{:S(2)}) %collective-permute-start) | collective-permute-done | bytes 262176 | tf_op jit(solution)/shard_map/while/body/eval_jaxpr/ppermute | solution.py:9
  79.9 4.8 %fusion.88 = f32[8,128,512]{2,0,1:T(8,128)S(1)} fusion(f32[8,128,512]{2,0,1:T(8,128)S(1)} %copy-done.3, f32[16,128,512]{2,1,0:T(8,128)S(1)} %fusion.86, s32[16]{0:T(128)S(1)} %fusion.87), kind=kOutput, calls=%fused_computation.6.clone.1 | convolution fusion | flops 101187712 | bytes 8388672 | tf_op jit(solution)/shard_map/while/body/eval_jaxpr/rt,taf->raf/dot_general | solution.py:19
  88.7 4.9 %collective-permute-done = bf16[256,512]{1,0:T(8,128)(2,1)S(1)} collective-permute-done((bf16[256,512]{1,0:T(8,128)(2,1)S(1)}, bf16[256,512]{1,0:T(8,128)(2,1)S(1)}, u32[]{:S(2)}, u32[]{:S(2)}) %collective-permute-start) | collective-permute-done | bytes 262176 | tf_op jit(solution)/shard_map/while/body/eval_jaxpr/ppermute | solution.py:9
  96.3 4.8 %fusion.88 = f32[8,128,512]{2,0,1:T(8,128)S(1)} fusion(f32[8,128,512]{2,0,1:T(8,128)S(1)} %copy-done.3, f32[16,128,512]{2,1,0:T(8,128)S(1)} %fusion.86, s32[16]{0:T(128)S(1)} %fusion.87), kind=kOutput, calls=%fused_computation.6.clone.1 | convolution fusion | flops 101187712 | bytes 8388672 | tf_op jit(solution)/shard_map/while/body/eval_jaxpr/rt,taf->raf/dot_general | solution.py:19
  105.1 4.9 %collective-permute-done = bf16[256,512]{1,0:T(8,128)(2,1)S(1)} collective-permute-done((bf16[256,512]{1,0:T(8,128)(2,1)S(1)}, bf16[256,512]{1,0:T(8,128)(2,1)S(1)}, u32[]{:S(2)}, u32[]{:S(2)}) %collective-permute-start) | collective-permute-done | bytes 262176 | tf_op jit(solution)/shard_map/while/body/eval_jaxpr/ppermute | solution.py:9
  112.7 4.8 %fusion.88 = f32[8,128,512]{2,0,1:T(8,128)S(1)} fusion(f32[8,128,512]{2,0,1:T(8,128)S(1)} %copy-done.3, f32[16,128,512]{2,1,0:T(8,128)S(1)} %fusion.86, s32[16]{0:T(128)S(1)} %fusion.87), kind=kOutput, calls=%fused_computation.6.clone.1 | convolution fusion | flops 101187712 | bytes 8388672 | tf_op jit(solution)/shard_map/while/body/eval_jaxpr/rt,taf->raf/dot_general | solution.py:19
  121.5 4.9 %collective-permute-done = bf16[256,512]{1,0:T(8,128)(2,1)S(1)} collective-permute-done((bf16[256,512]{1,0:T(8,128)(2,1)S(1)}, bf16[256,512]{1,0:T(8,128)(2,1)S(1)}, u32[]{:S(2)}, u32[]{:S(2)}) %collective-permute-start) | collective-permute-done | bytes 262176 | tf_op jit(solution)/shard_map/while/body/eval_jaxpr/ppermute | solution.py:9
  129.0 4.8 %fusion.88 = f32[8,128,512]{2,0,1:T(8,128)S(1)} fusion(f32[8,128,512]{2,0,1:T(8,128)S(1)} %copy-done.3, f32[16,128,512]{2,1,0:T(8,128)S(1)} %fusion.86, s32[16]{0:T(128)S(1)} %fusion.87), kind=kOutput, calls=%fused_computation.6.clone.1 | convolution fusion | flops 101187712 | bytes 8388672 | tf_op jit(solution)/shard_map/while/body/eval_jaxpr/rt,taf->raf/dot_general | solution.py:19
  135.2 2.8 copy.11
  139.4 69.0 %all-reduce.4 = bf16[1024,512]{1,0:T(8,128)(2,1)} all-reduce(f32[1024,512]{1,0:T(8,128)S(1)} %bitcast.127), channel_id=1, replica_groups=mesh['dom'=8,'repl'=4] {'repl'}, use_global_device_ids=true, to_apply=%region_2.3 | all-reduce | flops 524288 | bytes 3145728 | tf_op jit(solution)/shard_map/psum | solution.py:57
  208.3 4.1 %multiply_convert_fusion = (bf16[1024,512]{1,0:T(8,128)(2,1)S(1)}, f32[1024,512]{1,0:T(8,128)}) fusion(bf16[1024,512]{1,0:T(8,128)(2,1)} %all-gather.2.cloned.1.call-done, bf16[1024,512]{1,0:T(8,128)(2,1)} %all-reduce.4, bf16[512,512]{1,0:T(8,128)(2,1)S(1)} %copy-done), kind=kOutput, calls=%fused_computation.47 | convolution fusion | flops 542113792 | bytes 5767168 | tf_op jit(solution)/shard_map/dot_general | solution.py:59
  216.9 2.7 fusion.32
  219.6 3.9 %fusion.28 = f32[2,128,512]{2,0,1:T(2,128)S(1)} fusion(f32[16,128,512]{2,1,0:T(8,128)S(1)} %fusion.32, s32[16]{0:T(128)S(1)} %fusion.52), kind=kOutput, calls=%fused_computation.43 | convolution fusion | flops 25165856 | bytes 4718656 | tf_op jit(solution)/shard_map/rt,taf->raf/dot_general | solution.py:19
  224.3 93.4 %while.33 = (s32[]{:T(128)}, f32[256,512]{1,0:T(8,128)}, s32[]{:T(128)}, s32[8,16]{1,0:T(8,128)}, bf16[8,16,128,128]{3,2,1,0:T(8,128)(2,1)}, /*index=5*/s32[8]{0...) while((s32[]{:T(128)}, f32[256,512]{1,0:T(8,128)}, ...), condition=%wide.region_4.5_spmd, body=%wide.region_3.4_spmd.sunk | while | flops 293995648 | bytes 28840864 | solution.py:86
  231.0 3.9 %fusion.95 = f32[2,128,512]{2,0,1:T(2,128)S(1)} fusion(f32[16,128,512]{2,1,0:T(8,128)S(1)} %fusion.93, s32[16]{0:T(128)S(1)} %fusion.94), kind=kOutput, calls=%fused_computation.23.clone.1 | convolution fusion | flops 25165856 | bytes 4718656 | tf_op jit(solution)/shard_map/while/body/eval_jaxpr/rt,taf->raf/dot_general | solution.py:19
  235.0 5.5 %collective-permute-done.1 = f32[256,512]{1,0:T(8,128)S(1)} collective-permute-done((f32[256,512]{1,0:T(8,128)}, f32[256,512]{1,0:T(8,128)S(1)}, u32[]{:S(2)}, u32[]{:S(2)}) %collective-permute-start.1) | collective-permute-done | bytes 524320 | tf_op jit(solution)/shard_map/while/body/eval_jaxpr/ppermute | solution.py:9
  248.0 3.9 %fusion.95 = f32[2,128,512]{2,0,1:T(2,128)S(1)} fusion(f32[16,128,512]{2,1,0:T(8,128)S(1)} %fusion.93, s32[16]{0:T(128)S(1)} %fusion.94), kind=kOutput, calls=%fused_computation.23.clone.1 | convolution fusion | flops 25165856 | bytes 4718656 | tf_op jit(solution)/shard_map/while/body/eval_jaxpr/rt,taf->raf/dot_general | solution.py:19
  259.9 3.9 %fusion.95 = f32[2,128,512]{2,0,1:T(2,128)S(1)} fusion(f32[16,128,512]{2,1,0:T(8,128)S(1)} %fusion.93, s32[16]{0:T(128)S(1)} %fusion.94), kind=kOutput, calls=%fused_computation.23.clone.1 | convolution fusion | flops 25165856 | bytes 4718656 | tf_op jit(solution)/shard_map/while/body/eval_jaxpr/rt,taf->raf/dot_general | solution.py:19
  263.9 5.3 %collective-permute-done.1 = f32[256,512]{1,0:T(8,128)S(1)} collective-permute-done((f32[256,512]{1,0:T(8,128)}, f32[256,512]{1,0:T(8,128)S(1)}, u32[]{:S(2)}, u32[]{:S(2)}) %collective-permute-start.1) | collective-permute-done | bytes 524320 | tf_op jit(solution)/shard_map/while/body/eval_jaxpr/ppermute | solution.py:9
  276.7 3.9 %fusion.95 = f32[2,128,512]{2,0,1:T(2,128)S(1)} fusion(f32[16,128,512]{2,1,0:T(8,128)S(1)} %fusion.93, s32[16]{0:T(128)S(1)} %fusion.94), kind=kOutput, calls=%fused_computation.23.clone.1 | convolution fusion | flops 25165856 | bytes 4718656 | tf_op jit(solution)/shard_map/while/body/eval_jaxpr/rt,taf->raf/dot_general | solution.py:19
  288.7 3.9 %fusion.95 = f32[2,128,512]{2,0,1:T(2,128)S(1)} fusion(f32[16,128,512]{2,1,0:T(8,128)S(1)} %fusion.93, s32[16]{0:T(128)S(1)} %fusion.94), kind=kOutput, calls=%fused_computation.23.clone.1 | convolution fusion | flops 25165856 | bytes 4718656 | tf_op jit(solution)/shard_map/while/body/eval_jaxpr/rt,taf->raf/dot_general | solution.py:19
  300.6 3.9 %fusion.95 = f32[2,128,512]{2,0,1:T(2,128)S(1)} fusion(f32[16,128,512]{2,1,0:T(8,128)S(1)} %fusion.93, s32[16]{0:T(128)S(1)} %fusion.94), kind=kOutput, calls=%fused_computation.23.clone.1 | convolution fusion | flops 25165856 | bytes 4718656 | tf_op jit(solution)/shard_map/while/body/eval_jaxpr/rt,taf->raf/dot_general | solution.py:19
  312.5 3.9 %fusion.95 = f32[2,128,512]{2,0,1:T(2,128)S(1)} fusion(f32[16,128,512]{2,1,0:T(8,128)S(1)} %fusion.93, s32[16]{0:T(128)S(1)} %fusion.94), kind=kOutput, calls=%fused_computation.23.clone.1 | convolution fusion | flops 25165856 | bytes 4718656 | tf_op jit(solution)/shard_map/while/body/eval_jaxpr/rt,taf->raf/dot_general | solution.py:19
  321.4 2.3 broadcast_multiply_fusion
  (223 shorter events, 119.3 us)
Async XLA Ops:
  7.2 201.2 %copy-start = (bf16[512,512]{1,0:T(8,128)(2,1)S(1)}, bf16[512,512]{1,0:T(8,128)(2,1)}, u32[]{:S(2)}) copy-start(bf16[512,512]{1,0:T(8,128)(2,1)} %param.13) | copy-start | bytes 1572868
  7.2 201.1 %all-gather.2.cloned.1.call-start = ((), (), s32[]{:S(2)}) async-start(), calls=%async_computation | async-start | bytes 1310720 | tf_op jit(solution)/shard_map/all_gather | solution.py:63
  8.2 313.1 %all-reduce.3.cloned.1.call-start = ((), (), s32[]{:S(2)}) async-start(), calls=%async_computation.1 | async-start | bytes 2097152 | tf_op jit(solution)/shard_map/psum | solution.py:68
  14.2 5.3 %copy-start.6 = (s32[1,1,8]{2,1,0:T(1,128)S(1)}, s32[1,1,8]{2,1,0:T(1,128)}, u32[]{:S(2)}) copy-start(s32[1,1,8]{2,1,0:T(1,128)} %param.17) | copy-start | bytes 100
  19.6 8.5 %collective-permute-start = (bf16[256,512]{1,0:T(8,128)(2,1)S(1)}, bf16[256,512]{1,0:T(8,128)(2,1)S(1)}, u32[]{:S(2)}, u32[]{:S(2)}) collective-permute-start(bf16[256,512]{1,0:T(8,128)(2,1)S(1)} %get-tuple-element.554), channel_id=1, source_target_pairs={{0,4},{4,8},{8,12},{12,16},{16,20},{20,24},{24,28},{28,0},{1,5},{5... | collective-permute-start | bytes 786440 | tf_op jit(solution)/shard_map/while/body/eval_jaxpr/ppermute | solution.py:9
  28.8 2.0 copy-start.3
  36.9 7.6 %collective-permute-start = (bf16[256,512]{1,0:T(8,128)(2,1)S(1)}, bf16[256,512]{1,0:T(8,128)(2,1)S(1)}, u32[]{:S(2)}, u32[]{:S(2)}) collective-permute-start(bf16[256,512]{1,0:T(8,128)(2,1)S(1)} %get-tuple-element.554), channel_id=1, source_target_pairs={{0,4},{4,8},{8,12},{12,16},{16,20},{20,24},{24,28},{28,0},{1,5},{5... | collective-permute-start | bytes 786440 | tf_op jit(solution)/shard_map/while/body/eval_jaxpr/ppermute | solution.py:9
  45.2 2.0 copy-start.3
  53.3 7.6 %collective-permute-start = (bf16[256,512]{1,0:T(8,128)(2,1)S(1)}, bf16[256,512]{1,0:T(8,128)(2,1)S(1)}, u32[]{:S(2)}, u32[]{:S(2)}) collective-permute-start(bf16[256,512]{1,0:T(8,128)(2,1)S(1)} %get-tuple-element.554), channel_id=1, source_target_pairs={{0,4},{4,8},{8,12},{12,16},{16,20},{20,24},{24,28},{28,0},{1,5},{5... | collective-permute-start | bytes 786440 | tf_op jit(solution)/shard_map/while/body/eval_jaxpr/ppermute | solution.py:9
  61.6 2.0 copy-start.3
  69.7 7.6 %collective-permute-start = (bf16[256,512]{1,0:T(8,128)(2,1)S(1)}, bf16[256,512]{1,0:T(8,128)(2,1)S(1)}, u32[]{:S(2)}, u32[]{:S(2)}) collective-permute-start(bf16[256,512]{1,0:T(8,128)(2,1)S(1)} %get-tuple-element.554), channel_id=1, source_target_pairs={{0,4},{4,8},{8,12},{12,16},{16,20},{20,24},{24,28},{28,0},{1,5},{5... | collective-permute-start | bytes 786440 | tf_op jit(solution)/shard_map/while/body/eval_jaxpr/ppermute | solution.py:9
  77.9 1.9 copy-start.3
  86.0 7.6 %collective-permute-start = (bf16[256,512]{1,0:T(8,128)(2,1)S(1)}, bf16[256,512]{1,0:T(8,128)(2,1)S(1)}, u32[]{:S(2)}, u32[]{:S(2)}) collective-permute-start(bf16[256,512]{1,0:T(8,128)(2,1)S(1)} %get-tuple-element.554), channel_id=1, source_target_pairs={{0,4},{4,8},{8,12},{12,16},{16,20},{20,24},{24,28},{28,0},{1,5},{5... | collective-permute-start | bytes 786440 | tf_op jit(solution)/shard_map/while/body/eval_jaxpr/ppermute | solution.py:9
  102.4 7.6 %collective-permute-start = (bf16[256,512]{1,0:T(8,128)(2,1)S(1)}, bf16[256,512]{1,0:T(8,128)(2,1)S(1)}, u32[]{:S(2)}, u32[]{:S(2)}) collective-permute-start(bf16[256,512]{1,0:T(8,128)(2,1)S(1)} %get-tuple-element.554), channel_id=1, source_target_pairs={{0,4},{4,8},{8,12},{12,16},{16,20},{20,24},{24,28},{28,0},{1,5},{5... | collective-permute-start | bytes 786440 | tf_op jit(solution)/shard_map/while/body/eval_jaxpr/ppermute | solution.py:9
  118.8 7.6 %collective-permute-start = (bf16[256,512]{1,0:T(8,128)(2,1)S(1)}, bf16[256,512]{1,0:T(8,128)(2,1)S(1)}, u32[]{:S(2)}, u32[]{:S(2)}) collective-permute-start(bf16[256,512]{1,0:T(8,128)(2,1)S(1)} %get-tuple-element.554), channel_id=1, source_target_pairs={{0,4},{4,8},{8,12},{12,16},{16,20},{20,24},{24,28},{28,0},{1,5},{5... | collective-permute-start | bytes 786440 | tf_op jit(solution)/shard_map/while/body/eval_jaxpr/ppermute | solution.py:9
  208.3 4.1 %copy-start.5 = (bf16[1024,512]{1,0:T(8,128)(2,1)S(1)}, bf16[1024,512]{1,0:T(8,128)(2,1)}, u32[]{:S(2)}) copy-start(bf16[1024,512]{1,0:T(8,128)(2,1)} %all-reduce.4) | copy-start | bytes 3145732
  224.3 2.0 copy-start.1
  224.3 16.1 %collective-permute-start.1 = (f32[256,512]{1,0:T(8,128)}, f32[256,512]{1,0:T(8,128)S(1)}, u32[]{:S(2)}, u32[]{:S(2)}) collective-permute-start(f32[256,512]{1,0:T(8,128)} %get-tuple-element.590), channel_id=1, source_target_pairs={{0,4},{4,8},{8,12},{12,16},{16,20},{20,24},{24,28},{28,0},{1,5},{5... | collective-permute-start | bytes 1572872 | tf_op jit(solution)/shard_map/while/body/eval_jaxpr/ppermute | solution.py:9
  234.8 6.5 %copy-start.2 = (bf16[8,128,512]{2,1,0:T(8,128)(2,1)S(1)}, bf16[8,128,512]{2,1,0:T(8,128)(2,1)}, u32[]{:S(2)}) copy-start(bf16[8,128,512]{2,1,0:T(8,128)(2,1)} %copy-done.1) | copy-start | bytes 3145732 | tf_op jit(solution)/shard_map/while
  241.3 2.0 copy-start.1
  241.4 10.6 %collective-permute-start.1 = (f32[256,512]{1,0:T(8,128)}, f32[256,512]{1,0:T(8,128)S(1)}, u32[]{:S(2)}, u32[]{:S(2)}) collective-permute-start(f32[256,512]{1,0:T(8,128)} %get-tuple-element.590), channel_id=1, source_target_pairs={{0,4},{4,8},{8,12},{12,16},{16,20},{20,24},{24,28},{28,0},{1,5},{5... | collective-permute-start | bytes 1572872 | tf_op jit(solution)/shard_map/while/body/eval_jaxpr/ppermute | solution.py:9
  253.3 2.0 copy-start.1
  253.3 15.9 %collective-permute-start.1 = (f32[256,512]{1,0:T(8,128)}, f32[256,512]{1,0:T(8,128)S(1)}, u32[]{:S(2)}, u32[]{:S(2)}) collective-permute-start(f32[256,512]{1,0:T(8,128)} %get-tuple-element.590), channel_id=1, source_target_pairs={{0,4},{4,8},{8,12},{12,16},{16,20},{20,24},{24,28},{28,0},{1,5},{5... | collective-permute-start | bytes 1572872 | tf_op jit(solution)/shard_map/while/body/eval_jaxpr/ppermute | solution.py:9
  263.8 6.3 %copy-start.2 = (bf16[8,128,512]{2,1,0:T(8,128)(2,1)S(1)}, bf16[8,128,512]{2,1,0:T(8,128)(2,1)}, u32[]{:S(2)}) copy-start(bf16[8,128,512]{2,1,0:T(8,128)(2,1)} %copy-done.1) | copy-start | bytes 3145732 | tf_op jit(solution)/shard_map/while
  270.1 2.0 copy-start.1
  270.1 11.1 %collective-permute-start.1 = (f32[256,512]{1,0:T(8,128)}, f32[256,512]{1,0:T(8,128)S(1)}, u32[]{:S(2)}, u32[]{:S(2)}) collective-permute-start(f32[256,512]{1,0:T(8,128)} %get-tuple-element.590), channel_id=1, source_target_pairs={{0,4},{4,8},{8,12},{12,16},{16,20},{20,24},{24,28},{28,0},{1,5},{5... | collective-permute-start | bytes 1572872 | tf_op jit(solution)/shard_map/while/body/eval_jaxpr/ppermute | solution.py:9
  282.1 2.0 copy-start.1
  282.1 10.6 %collective-permute-start.1 = (f32[256,512]{1,0:T(8,128)}, f32[256,512]{1,0:T(8,128)S(1)}, u32[]{:S(2)}, u32[]{:S(2)}) collective-permute-start(f32[256,512]{1,0:T(8,128)} %get-tuple-element.590), channel_id=1, source_target_pairs={{0,4},{4,8},{8,12},{12,16},{16,20},{20,24},{24,28},{28,0},{1,5},{5... | collective-permute-start | bytes 1572872 | tf_op jit(solution)/shard_map/while/body/eval_jaxpr/ppermute | solution.py:9
  294.0 2.0 copy-start.1
  294.0 10.6 %collective-permute-start.1 = (f32[256,512]{1,0:T(8,128)}, f32[256,512]{1,0:T(8,128)S(1)}, u32[]{:S(2)}, u32[]{:S(2)}) collective-permute-start(f32[256,512]{1,0:T(8,128)} %get-tuple-element.590), channel_id=1, source_target_pairs={{0,4},{4,8},{8,12},{12,16},{16,20},{20,24},{24,28},{28,0},{1,5},{5... | collective-permute-start | bytes 1572872 | tf_op jit(solution)/shard_map/while/body/eval_jaxpr/ppermute | solution.py:9
  305.9 2.0 copy-start.1
  305.9 10.6 %collective-permute-start.1 = (f32[256,512]{1,0:T(8,128)}, f32[256,512]{1,0:T(8,128)S(1)}, u32[]{:S(2)}, u32[]{:S(2)}) collective-permute-start(f32[256,512]{1,0:T(8,128)} %get-tuple-element.590), channel_id=1, source_target_pairs={{0,4},{4,8},{8,12},{12,16},{16,20},{20,24},{24,28},{28,0},{1,5},{5... | collective-permute-start | bytes 1572872 | tf_op jit(solution)/shard_map/while/body/eval_jaxpr/ppermute | solution.py:9
  (15 other events, 22.4 us)
Sparse Core Ops, SparseCore 0:
  9.9 29.3 all-gather.1
  215.0 62.7 all-reduce.2
where the time goes:
time: 334 us; the launch traced here: 331 us
  matrix products  108 us (32%)
  blocking collectives  69 us (21%)
  local copies, waits for them, and re-layouts  58.6 us (18%)
  waiting for transfers between devices  46.4 us (14%)
  other arithmetic  33 us (10%)
  between operations  14.1 us (4%)
    dot_general x16, matrix products, place_tiles(): jnp.einsum('rt,taf->raf', selector, prod, precision=lax.Precision.HIGHEST)  69.7 us
    psum x1, blocking collectives, local(): block_rows = lax.psum(totals, 'repl')  69 us
    ppermute x14, waiting for transfers between devices, shifted(): lax.ppermute(x, axis, [(i, (i + by) % length) for i in range(length)])  46.4 us
    dot_general x8, matrix products, backward_block(): jnp.einsum('tab,taf->tbf', slab_one, picked, preferred_element_type=jnp.f...  16.5 us
    gather x8, local copies, waits for them, and re-layouts, backward_block(): picked = grad_tiles[row_index[column]]  15.4 us
    dot_general x8, matrix products, forward_add(): jnp.einsum('tab,tbf->taf', slab_one, picked, preferred_element_type=jnp.f...  15.4 us
    eq x16, local copies, waits for them, and re-layouts, place_tiles(): jnp.arange(count, dtype=jnp.int32)[:, None] == indices[None, :]  11.1 us
    while x63, local copies, waits for them, and re-layouts  10.8 us
  transfers between devices with their start and end apart: 16, of which 10 were waited for; matrix products, arithmetic and copies ran while one was open for 54% of the time, Pallas kernels for 0%

commit v1 on v0

v1 whole, which is shorter than its diff:
```python
import functools

import jax
import jax.numpy as jnp
from jax import lax
from jax.experimental import pallas as pl
from jax.experimental.pallas import tpu as pltpu
from jax.sharding import PartitionSpec as P

VMEM_LIMIT = 48 * 1024 * 1024


def exchange(x, axis, mask):
    return lax.ppermute(x, axis, [(i, i ^ mask) for i in range(lax.axis_size(axis))])


def params():
    return pltpu.CompilerParams(vmem_limit_bytes=VMEM_LIMIT)


def densify_kernel(rows_ref, cols_ref, counts_ref, place_ref, tiles_ref, a_ref, acc_ref, *, col_tiles, slots):
    step = pl.program_id(0)
    column = step ^ place_ref[0]
    member = place_ref[1]
    size = tiles_ref.shape[-1]
    acc_ref[...] = jnp.zeros_like(acc_ref)

    def add(slot, carry):
        row = rows_ref[column * slots + slot]
        row = ((row // col_tiles) ^ member) * col_tiles + lax.rem(row, col_tiles)
        spot = row * col_tiles + cols_ref[column * slots + slot]
        acc_ref[spot] += tiles_ref[0, slot].astype(jnp.float32)
        return carry

    lax.fori_loop(0, counts_ref[column], add, 0)
    for spot in range(acc_ref.shape[0]):
        row, col = spot // col_tiles, spot % col_tiles
        a_ref[0, row * size:(row + 1) * size, col * size:(col + 1) * size] = acc_ref[spot].astype(a_ref.dtype)


def densify(tiles, tile_rows, tile_cols, tile_counts, place, group_count, rows_local):
    columns, slots, size, _ = tiles.shape
    col_tiles = rows_local // size
    rows = group_count * rows_local
    return pl.pallas_call(
        functools.partial(densify_kernel, col_tiles=col_tiles, slots=slots),
        out_shape=jax.ShapeDtypeStruct((columns // 2, rows, 2 * rows_local), jnp.bfloat16),
        grid_spec=pltpu.PrefetchScalarGridSpec(
            num_scalar_prefetch=4,
            grid=(columns,),
            in_specs=[pl.BlockSpec((1, slots, size, size), lambda j, r, c, n, p: (j ^ p[0], 0, 0, 0))],
            out_specs=pl.BlockSpec((1, rows, rows_local), lambda j, r, c, n, p: (j // 2, 0, lax.rem(j, 2))),
            scratch_shapes=[pltpu.VMEM((group_count * col_tiles * col_tiles, size, size), jnp.float32)],
        ),
        compiler_params=params(),
        cost_estimate=pl.CostEstimate(flops=columns * slots * size * size, bytes_accessed=8 * rows * columns * rows_local, transcendentals=0),
        name="densify",
    )(tile_rows.reshape(-1), tile_cols.reshape(-1), tile_counts.reshape(-1), place, tiles)


def transpose_kernel(a_ref, out_ref):
    out_ref[0] = a_ref[0].T


def transposed(dense, rows_local):
    pairs, rows, _ = dense.shape
    return pl.pallas_call(
        transpose_kernel,
        out_shape=jax.ShapeDtypeStruct((2 * pairs, rows_local, rows), jnp.bfloat16),
        grid=(2 * pairs,),
        in_specs=[pl.BlockSpec((1, rows, rows_local), lambda j: (j // 2, 0, lax.rem(j, 2)))],
        out_specs=pl.BlockSpec((1, rows_local, rows), lambda j: (j, 0, 0)),
        compiler_params=params(),
        cost_estimate=pl.CostEstimate(flops=0, bytes_accessed=8 * pairs * rows * rows_local, transcendentals=0),
        name="transposed",
    )(dense)


def forward_kernel(*refs, pairs, has_prev):
    dense, sources = refs[:pairs], refs[pairs:3 * pairs]
    prev, out_ref = refs[3 * pairs:-1], refs[-1]
    half = sources[0].shape[0]
    total = prev[0][...] if has_prev else None
    for pair in range(pairs):
        for side in range(2):
            part = jnp.dot(
                dense[pair][0, :, side * half:(side + 1) * half], sources[2 * pair + side][...],
                preferred_element_type=jnp.float32,
            )
            total = part if total is None else total + part
    out_ref[...] = total.astype(out_ref.dtype)


def forward(dense, which, sources, prev, dtype):
    _, rows, depth = dense.shape
    half, width = sources[0].shape

    def block(pair):
        return pl.BlockSpec((1, half, depth), lambda k: (pair, k, 0))

    in_specs = [block(pair) for pair in which]
    in_specs += [pl.BlockSpec((half, width), lambda k: (0, 0)) for _ in sources]
    args = [dense] * len(which) + list(sources)
    if prev is not None:
        in_specs.append(pl.BlockSpec((half, width), lambda k: (k, 0)))
        args.append(prev)
    return pl.pallas_call(
        functools.partial(forward_kernel, pairs=len(which), has_prev=prev is not None),
        out_shape=jax.ShapeDtypeStruct((rows, width), dtype),
        grid=(rows // half,),
        in_specs=in_specs,
        out_specs=pl.BlockSpec((half, width), lambda k: (k, 0)),
        compiler_params=params(),
        cost_estimate=pl.CostEstimate(
            flops=2 * len(which) * rows * depth * width, bytes_accessed=2 * len(which) * rows * depth + 4 * rows * width,
            transcendentals=0),
        name="forward",
    )(*args)


def middle_kernel(place_ref, *refs, groups, part_rows):
    aggs, cots = refs[:groups], refs[groups:2 * groups]
    weight_ref = refs[2 * groups]
    act_ref = refs[2 * groups + 1]
    grads = refs[2 * groups + 2:3 * groups + 2]
    keep_ref, send_ref, part_ref = refs[3 * groups + 2:]
    member, core = place_ref[1], lax.rem(place_ref[0], 2)
    weight = weight_ref[...]
    total = None
    for k in range(groups):
        agg = aggs[k][...]
        preact = jnp.dot(agg, weight, preferred_element_type=jnp.float32)
        sigma = jax.nn.sigmoid(preact)
        if k == 0:
            act_ref[...] = (preact * sigma).astype(act_ref.dtype)
        slope = sigma * (1.0 + preact * (1.0 - sigma))
        pre_grad = (cots[k][...].astype(jnp.float32) * slope).astype(jnp.bfloat16)
        grads[k][...] = lax.dot_general(
            pre_grad, weight, (((1,), (1,)), ((), ())), preferred_element_type=jnp.float32
        ).astype(grads[k].dtype)
        if part_ref.shape[0] == part_rows:
            agg = aggs[k][:, pl.ds(pl.multiple_of(member * part_rows, part_rows), part_rows)]
        part = lax.dot_general(agg, pre_grad, (((0,), (0,)), ((), ())), preferred_element_type=jnp.float32)
        total = part if total is None else total + part
    part_ref[...] = total
    start = 0 if part_ref.shape[0] == part_rows else member * part_rows
    half = part_rows // 2
    keep_ref[...] = part_ref[pl.ds(pl.multiple_of(start + core * half, half), half), :]
    send_ref[...] = part_ref[pl.ds(pl.multiple_of(start + (1 - core) * half, half), half), :]


def middle(aggs, cots, weight, place):
    groups = len(aggs)
    rows, width = aggs[0].shape
    part_rows = width // groups
    whole = pl.BlockSpec(memory_space=pltpu.VMEM)
    scratch_rows = part_rows if part_rows % 128 == 0 else width
    out = pl.pallas_call(
        functools.partial(middle_kernel, groups=groups, part_rows=part_rows),
        out_shape=[jax.ShapeDtypeStruct((rows, width), jnp.bfloat16)] * (1 + groups)
        + [jax.ShapeDtypeStruct((part_rows // 2, width), jnp.float32)] * 2,
        in_specs=[pl.BlockSpec(memory_space=pltpu.SMEM)] + [whole] * (2 * groups + 1),
        out_specs=[whole] * (3 + groups),
        scratch_shapes=[pltpu.VMEM((scratch_rows, width), jnp.float32)],
        compiler_params=params(),
        cost_estimate=pl.CostEstimate(
            flops=2 * groups * rows * width * (2 * width + scratch_rows), bytes_accessed=6 * groups * rows * width,
            transcendentals=groups * rows * width),
        name="middle",
    )(place, *aggs, *cots, weight)
    return out[0], out[1:1 + groups], out[-2], out[-1]


def backward_kernel(*refs, groups):
    at_ref, grads, (own_ref, other_ref) = refs[0], refs[1:1 + groups], refs[1 + groups:]
    rows = grads[0].shape[0]
    for side, out_ref in ((1, other_ref), (0, own_ref)):
        total = None
        for k in range(groups):
            part = jnp.dot(
                at_ref[side, :, k * rows:(k + 1) * rows], grads[k][...], preferred_element_type=jnp.float32
            )
            total = part if total is None else total + part
        out_ref[...] = total.astype(out_ref.dtype)


def backward(dense_t, pair, grads):
    _, cols, rows = dense_t.shape
    groups = len(grads)
    rows_local, width = grads[0].shape
    return pl.pallas_call(
        functools.partial(backward_kernel, groups=groups),
        out_shape=[jax.ShapeDtypeStruct((cols, width), jnp.float32), jax.ShapeDtypeStruct((cols, width), jnp.bfloat16)],
        grid=(1,),
        in_specs=[pl.BlockSpec((2, cols, rows), lambda i: (pair, 0, 0))]
        + [pl.BlockSpec((rows_local, width), lambda i: (0, 0))] * groups,
        out_specs=[pl.BlockSpec((cols, width), lambda i: (0, 0))] * 2,
        compiler_params=params(),
        cost_estimate=pl.CostEstimate(
            flops=4 * cols * rows * width, bytes_accessed=4 * cols * rows + 2 * rows * width + 6 * cols * width,
            transcendentals=0),
        name="backward",
    )(dense_t, *grads)


def local(features, cotangent, weight, tiles, tile_rows, tile_cols, tile_counts):
    blocks = lax.axis_size("dom")
    groups = lax.axis_size("repl")
    pairs = blocks // 2
    rows_local, width = features.shape
    scale = float(rows_local * blocks * groups) ** (-0.5)
    position, member = lax.axis_index("dom"), lax.axis_index("repl")
    place = jnp.stack([position, member]).astype(jnp.int32)

    sources = {0: features}
    bit = blocks // 2
    while bit > 1:
        for j in list(sources):
            sources[j + bit] = exchange(sources[j], "dom", bit)
        bit //= 2
    for j in list(sources):
        sources[j + 1] = exchange(sources[j], "dom", 1)
    cots = [cotangent] + [exchange(cotangent, "repl", k) for k in range(1, groups)]

    dense = densify(tiles[0, 0], tile_rows, tile_cols, tile_counts, place, groups, rows_local)
    dense_t = transposed(dense, rows_local)

    early = list(range(pairs - 1))
    totals = forward(dense, early, [sources[j] for p in early for j in (2 * p, 2 * p + 1)], None, jnp.float32)
    last = pairs - 1
    partial = forward(dense, [last], [sources[2 * last], sources[2 * last + 1]], totals, jnp.bfloat16)

    def piece(k):
        return partial[k * rows_local:(k + 1) * rows_local]

    agg = piece(0).astype(jnp.float32)
    for k in range(1, groups):
        agg = agg + exchange(piece(k), "repl", k).astype(jnp.float32)
    agg_rounded = agg.astype(jnp.bfloat16)
    aggs = [agg_rounded] + [exchange(agg_rounded, "repl", k) for k in range(1, groups)]

    activated, grads, keep, send = middle(aggs, cots, weight, place)

    part = keep + exchange(send, "dom", 1)
    bit = 2
    while bit < blocks:
        part = part + exchange(part, "dom", bit)
        bit *= 2
    part = part * scale
    mine = jnp.stack([part] + [exchange(part, "repl", k) for k in range(1, groups)])
    both = jnp.concatenate([mine, exchange(mine, "dom", 1)])
    core = position % 2
    order = ((jnp.arange(2)[None, :] ^ core) * groups + (jnp.arange(groups)[:, None] ^ member)).reshape(-1)
    weight_grad = both[order].reshape(weight.shape)

    sums = {}
    for pair in reversed(range(pairs)):
        own, other = backward(dense_t, pair, grads)
        sums[pair] = own + exchange(other, "dom", 1).astype(jnp.float32)
    bit = 1
    while bit < pairs:
        for pair in sorted(sums, reverse=True):
            if pair & bit:
                arrived = exchange(sums.pop(pair).astype(jnp.bfloat16), "dom", 2 * bit)
                sums[pair ^ bit] = sums[pair ^ bit] + arrived.astype(jnp.float32)
        bit *= 2
    feature_grad = sums[0].astype(jnp.bfloat16)
    return (activated, feature_grad, weight_grad)


def solution(mesh):
    in_specs = (
        P(("dom", "repl"), None),
        P(("dom", "repl"), None),
        P(),
        P("dom", "repl", None, None, None, None),
        P("dom", "repl", None, None),
        P("dom", "repl", None, None),
        P("dom", "repl", None),
    )
    out_specs = (P(("dom", "repl"), None), P(("dom", "repl"), None), P())
    return jax.shard_map(local, mesh=mesh, in_specs=in_specs, out_specs=out_specs, check_vma=False)
```

time: 334 us -> 121 us (0.36)
  matrix products: 108 us -> 0 us
  blocking collectives: 69 us -> 0 us
  local copies, waits for them, and re-layouts: 58.6 us -> 7.94 us
  starting transfers between devices: 0.57 us -> 35.4 us
  other arithmetic: 33 us -> 1.53 us
  Pallas kernels: 0 us -> 24.9 us
  between operations: 14.1 us -> 0.88 us
  waiting for transfers between devices: 46.4 us -> 50 us
    dot_general x35 -> x0, matrix products: 108 us -> none  [the longest x16 69.7 us: place_tiles(): jnp.einsum('rt,taf->raf', selector, prod, precision=lax.Precision.HIGHEST)]
    psum x1 -> x0, blocking collectives: 69 us -> none  [local(): block_rows = lax.psum(totals, 'repl')]
    ppermute x14 -> x30, starting transfers between devices: 0.49 us -> 35.4 us  [exchange(): lax.ppermute(x, axis, [(i, i ^ mask) for i in range(lax.axis_size(axis))])]
    pallas_call x0 -> x9, Pallas kernels: none -> 24.9 us  [the longest x2 6.95 us: forward(): pl.pallas_call(functools.partial(forward_kernel, pairs=len(which), has_pr...]
    gather x16 -> x1, local copies, waits for them, and re-layouts: 20.8 us -> 1.58 us  [local(): weight_grad = both[order].reshape(weight.shape)]
    while x64 -> x0, local copies, waits for them, and re-layouts: 13.6 us -> none
    convert_element_type x18 -> x5, other arithmetic: 13.8 us -> 1.27 us  [the longest x1 0.87 us: local(): feature_grad = sums[0].astype(jnp.bfloat16)]
    eq x16 -> x0, local copies, waits for them, and re-layouts: 11.1 us -> none  [place_tiles(): jnp.arange(count, dtype=jnp.int32)[:, None] == indices[None, :]]
  transfers between devices with their start and end apart: 16 -> 30, of which waited for: 10 -> 13; matrix products, arithmetic and copies ran while one was open for 54% -> 3% of each run, Pallas kernels for 0% -> 16%
where the time goes in v1:
time: 121 us
  waiting for transfers between devices  50 us (41%)
  starting transfers between devices  35.4 us (29%)
  Pallas kernels  24.9 us (21%)
  local copies, waits for them, and re-layouts  7.94 us (7%)
  other arithmetic  1.53 us (1%)
    ppermute x30, waiting for transfers between devices, exchange(): lax.ppermute(x, axis, [(i, i ^ mask) for i in range(lax.axis_size(axis))])  50 us
    ppermute x30, starting transfers between devices, exchange(): lax.ppermute(x, axis, [(i, i ^ mask) for i in range(lax.axis_size(axis))])  35.4 us
    pallas_call x2, Pallas kernels, forward(): pl.pallas_call(functools.partial(forward_kernel, pairs=len(which), has_pr...  6.95 us
    pallas_call x1, Pallas kernels, densify(): pl.pallas_call(functools.partial(densify_kernel, col_tiles=col_tiles, slo...  6.66 us
    pallas_call x1, Pallas kernels, transposed(): pl.pallas_call(transpose_kernel, out_shape=jax.ShapeDtypeStruct((2 * pair...  5.4 us
    unnamed x17, local copies, waits for them, and re-layouts  4.65 us
    pallas_call x1, Pallas kernels, middle(): pl.pallas_call(functools.partial(middle_kernel, groups=groups, part_rows=...  3.02 us
    pallas_call x4, Pallas kernels, backward(): pl.pallas_call(functools.partial(backward_kernel, groups=groups), out_sha...  2.85 us
  transfers between devices with their start and end apart: 30, of which 13 were waited for; matrix products, arithmetic and copies ran while one was open for 3% of the time, Pallas kernels for 16%

profile of v1, /device:TPU:0, one launch (start us, length us, event | category | flops | bytes accessed | tf_op | source)
XLA Modules:
  0.0 120.6 jit_solution(15654141890288648065)
XLA Ops:
  0.6 4.1 %collective-permute-start = (bf16[256,512]{1,0:T(8,128)(2,1)}, bf16[256,512]{1,0:T(8,128)(2,1)S(1)}, u32[]{:S(2)}, u32[]{:S(2)}) collective-permute-start(bf16[256,512]{1,0:T(8,128)(2,1)} %refs_3_.1), channel_id=1, source_target_pairs={{0,16},{4,20},{8,24},{12,28},{16,0},{20,4},{24,8},{28,12},{1,17},{... | collective-permute-start | bytes 786440 | tf_op jit(solution)/shard_map/ppermute | solution.py:14
  4.7 1.6 %collective-permute-start.4 = (bf16[256,512]{1,0:T(8,128)(2,1)}, bf16[256,512]{1,0:T(8,128)(2,1)S(1)}, u32[]{:S(2)}, u32[]{:S(2)}) collective-permute-start(bf16[256,512]{1,0:T(8,128)(2,1)} %refs_3_.1), channel_id=1, source_target_pairs={{0,8},{4,12},{8,0},{12,4},{16,24},{20,28},{24,16},{28,20},{1,9},{5... | collective-permute-start | bytes 786440 | tf_op jit(solution)/shard_map/ppermute | solution.py:14
  6.3 10.7 %collective-permute-done.refs_7_ = bf16[256,512]{1,0:T(8,128)(2,1)S(1)} collective-permute-done((bf16[256,512]{1,0:T(8,128)(2,1)}, bf16[256,512]{1,0:T(8,128)(2,1)S(1)}, u32[]{:S(2)}, u32[]{:S(2)}) %collective-permute-start) | collective-permute-done | bytes 262176 | tf_op jit(solution)/shard_map/ppermute | solution.py:14
  19.7 4.7 %collective-permute-done.1.refs_1_ = bf16[256,512]{1,0:T(8,128)(2,1)S(1)} collective-permute-done((bf16[256,512]{1,0:T(8,128)(2,1)S(1)}, bf16[256,512]{1,0:T(8,128)(2,1)S(1)}, u32[]{:S(2)}, u32[]{:S(2)}) %collective-permute-start.1) | collective-permute-done | bytes 262176 | tf_op jit(solution)/shard_map/ppermute | solution.py:14
  25.1 6.7 %densify.1.refs_0_.refs_1_.refs_2_.a_ref = bf16[4,1024,512]{2,1,0:T(8,128)(2,1)S(1)} custom-call(s32[128]{0:T(128)S(1)} %reshape.60.rows_ref, s32[128]{0:T(128)S(1)} %reshape.61.cols_ref, s32[8]{0:T(128)S(1)} %bitcast.19, s32[2]{0:T(128)S(1)} %pad_add_fusion.place_ref, bf16[8,16,128,128]{3,2,1,0:T(8,128)(2,1)} %bitcast.20), custom_call_target="tpu_custom_call" | custom-call | flops 2097152 | bytes 16777216 | tf_op jit(solution)/shard_map/densify/pallas_call | solution.py:45
  31.8 2.0 %copy-done = bf16[4,1024,512]{2,1,0:T(8,128)(2,1)} copy-done((bf16[4,1024,512]{2,1,0:T(8,128)(2,1)}, bf16[4,1024,512]{2,1,0:T(8,128)(2,1)S(1)}, u32[]{:S(2)}) %copy-start) | copy-done | bytes 4194328
  33.8 4.0 %forward.2.refs_3_ = f32[1024,512]{1,0:T(8,128)S(1)} custom-call(bf16[4,1024,512]{2,1,0:T(8,128)(2,1)} %copy-done, bf16[4,1024,512]{2,1,0:T(8,128)(2,1)} %copy-done, bf16[4,1024,512]{2,1,0:T(8,128)(2,1)} %copy-done, bf16[256,512]{1,0:T(8,128)(2,1)S(1)} %copy-done.3, bf16[256,512]{1,0:T(8,128)(2,1)S(1)} %collective-permute-done.3.refs_4_, ...), custom_call_target="tpu_custom_call" | custom-call | flops 1610612736 | bytes 5242880 | tf_op jit(solution)/shard_map/forward/pallas_call | solution.py:107
  37.9 2.9 %forward.3 = bf16[1024,512]{1,0:T(8,128)(2,1)S(1)} custom-call(bf16[4,1024,512]{2,1,0:T(8,128)(2,1)} %copy-done, bf16[256,512]{1,0:T(8,128)(2,1)S(1)} %collective-permute-done.1.refs_1_, bf16[256,512]{1,0:T(8,128)(2,1)S(1)} %collective-permute-done.2.refs_2_, f32[1024,512]{1,0:T(8,128)S(1)} %forward.2.refs_3_), custom_call_target="tpu_custom_call" | custom-call | flops 536870912 | bytes 3145728 | tf_op jit(solution)/shard_map/forward/pallas_call | solution.py:107
  40.9 2.3 %collective-permute-start.9 = (bf16[256,512]{1,0:T(8,128)(2,1)S(1)}, bf16[256,512]{1,0:T(8,128)(2,1)S(1)}, u32[]{:S(2)}, u32[]{:S(2)}) collective-permute-start(bf16[256,512]{1,0:T(8,128)(2,1)S(1)} %get-tuple-element.36), channel_id=1, source_target_pairs={{0,3},{1,2},{2,1},{3,0},{4,7},{5,6},{6,5},{7,4},{8,11},{9,10},{10,... | collective-permute-start | bytes 786440 | tf_op jit(solution)/shard_map/ppermute | solution.py:14
  45.8 1.4 %collective-permute-start.14 = (bf16[256,512]{1,0:T(8,128)(2,1)S(1)}, bf16[256,512]{1,0:T(8,128)(2,1)S(1)}, u32[]{:S(2)}, u32[]{:S(2)}) collective-permute-start(bf16[256,512]{1,0:T(8,128)(2,1)S(1)} %copy-done.6), channel_id=1, source_target_pairs={{0,2},{1,3},{2,0},{3,1},{4,6},{5,7},{6,4},{7,5},{8,10},{9,11},{10,... | collective-permute-start | bytes 786440 | tf_op jit(solution)/shard_map/ppermute | solution.py:14
  47.2 3.7 %collective-permute-done.9 = bf16[256,512]{1,0:T(8,128)(2,1)S(1)} collective-permute-done((bf16[256,512]{1,0:T(8,128)(2,1)S(1)}, bf16[256,512]{1,0:T(8,128)(2,1)S(1)}, u32[]{:S(2)}, u32[]{:S(2)}) %collective-permute-start.9) | collective-permute-done | bytes 262176 | tf_op jit(solution)/shard_map/ppermute | solution.py:14
  51.0 2.2 %collective-permute-start.15 = (bf16[256,512]{1,0:T(8,128)(2,1)S(1)}, bf16[256,512]{1,0:T(8,128)(2,1)S(1)}, u32[]{:S(2)}, u32[]{:S(2)}) collective-permute-start(bf16[256,512]{1,0:T(8,128)(2,1)S(1)} %copy-done.6), channel_id=1, source_target_pairs={{0,3},{1,2},{2,1},{3,0},{4,7},{5,6},{6,5},{7,4},{8,11},{9,10},{10,... | collective-permute-start | bytes 786440 | tf_op jit(solution)/shard_map/ppermute | solution.py:14
  53.2 3.0 %collective-permute-done.8 = bf16[256,512]{1,0:T(8,128)(2,1)S(1)} collective-permute-done((bf16[256,512]{1,0:T(8,128)(2,1)S(1)}, bf16[256,512]{1,0:T(8,128)(2,1)S(1)}, u32[]{:S(2)}, u32[]{:S(2)}) %collective-permute-start.8) | collective-permute-done | bytes 262176 | tf_op jit(solution)/shard_map/ppermute | solution.py:14
  56.6 1.5 %collective-permute-start.10 = (bf16[256,512]{1,0:T(8,128)(2,1)S(1)}, bf16[256,512]{1,0:T(8,128)(2,1)S(1)}, u32[]{:S(2)}, u32[]{:S(2)}) collective-permute-start(bf16[256,512]{1,0:T(8,128)(2,1)S(1)} %add_convert_fusion.4.refs_0_), channel_id=1, source_target_pairs={{0,1},{1,0},{2,3},{3,2},{4,5},{5,4},{6,7},{7,6},{8,9},{9,8},{10,11... | collective-permute-start | bytes 786440 | tf_op jit(solution)/shard_map/ppermute | solution.py:14
  59.2 2.9 %collective-permute-done.13.refs_5_ = bf16[256,512]{1,0:T(8,128)(2,1)S(1)} collective-permute-done((bf16[256,512]{1,0:T(8,128)(2,1)S(1)}, bf16[256,512]{1,0:T(8,128)(2,1)S(1)}, u32[]{:S(2)}, u32[]{:S(2)}) %collective-permute-start.13) | collective-permute-done | bytes 262176 | tf_op jit(solution)/shard_map/ppermute | solution.py:14
  62.1 1.6 %collective-permute-start.12 = (bf16[256,512]{1,0:T(8,128)(2,1)S(1)}, bf16[256,512]{1,0:T(8,128)(2,1)S(1)}, u32[]{:S(2)}, u32[]{:S(2)}) collective-permute-start(bf16[256,512]{1,0:T(8,128)(2,1)S(1)} %add_convert_fusion.4.refs_0_), channel_id=1, source_target_pairs={{0,3},{1,2},{2,1},{3,0},{4,7},{5,6},{6,5},{7,4},{8,11},{9,10},{10,... | collective-permute-start | bytes 786440 | tf_op jit(solution)/shard_map/ppermute | solution.py:14
  63.7 5.4 %transposed.1.refs_0_ = bf16[8,256,1024]{2,1,0:T(8,128)(2,1)S(1)} custom-call(bf16[4,1024,512]{2,1,0:T(8,128)(2,1)} %copy-done), custom_call_target="tpu_custom_call" | custom-call | bytes 8388608 | tf_op jit(solution)/shard_map/transposed/pallas_call | solution.py:67
  69.1 2.0 %copy-done.1 = bf16[8,256,1024]{2,1,0:T(8,128)(2,1)} copy-done((bf16[8,256,1024]{2,1,0:T(8,128)(2,1)}, bf16[8,256,1024]{2,1,0:T(8,128)(2,1)S(1)}, u32[]{:S(2)}) %copy-start.1) | copy-done | bytes 4194328
  71.2 2.2 %collective-permute-done.10.refs_1_ = bf16[256,512]{1,0:T(8,128)(2,1)S(1)} collective-permute-done((bf16[256,512]{1,0:T(8,128)(2,1)S(1)}, bf16[256,512]{1,0:T(8,128)(2,1)S(1)}, u32[]{:S(2)}, u32[]{:S(2)}) %collective-permute-start.10) | collective-permute-done | bytes 262176 | tf_op jit(solution)/shard_map/ppermute | solution.py:14
  73.4 5.4 %collective-permute-done.12.refs_3_ = bf16[256,512]{1,0:T(8,128)(2,1)S(1)} collective-permute-done((bf16[256,512]{1,0:T(8,128)(2,1)S(1)}, bf16[256,512]{1,0:T(8,128)(2,1)S(1)}, u32[]{:S(2)}, u32[]{:S(2)}) %collective-permute-start.12) | collective-permute-done | bytes 262176 | tf_op jit(solution)/shard_map/ppermute | solution.py:14
  78.7 3.0 %middle.1 = (bf16[256,512]{1,0:T(8,128)(2,1)}, bf16[256,512]{1,0:T(8,128)(2,1)S(1)}, bf16[256,512]{1,0:T(8,128)(2,1)S(1)}, bf16[256,512]{1,0:T(8,128)(2,1)S(1)},...) custom-call(s32[2]{0:T(128)S(1)} %pad_add_fusion.place_ref, ...), custom_call_target="tpu_custom_call" | custom-call | flops 1207959552 | bytes 3145728 | tf_op jit(solution)/shard_map/middle/pallas_call | solution.py:158
  83.1 2.0 %collective-permute-start.24 = (f32[64,512]{1,0:T(8,128)S(1)}, f32[64,512]{1,0:T(8,128)S(1)}, u32[]{:S(2)}, u32[]{:S(2)}) collective-permute-start(f32[64,512]{1,0:T(8,128)S(1)} %add.87), channel_id=1, source_target_pairs={{0,8},{4,12},{8,0},{12,4},{16,24},{20,28},{24,16},{28,20},{1,9},{5... | collective-permute-start | bytes 393224 | tf_op jit(solution)/shard_map/ppermute | solution.py:14
  88.9 3.7 %collective-permute-start.25 = (f32[64,512]{1,0:T(8,128)S(1)}, f32[64,512]{1,0:T(8,128)S(1)}, u32[]{:S(2)}, u32[]{:S(2)}) collective-permute-start(f32[64,512]{1,0:T(8,128)S(1)} %add.88), channel_id=1, source_target_pairs={{0,16},{4,20},{8,24},{12,28},{16,0},{20,4},{24,8},{28,12},{1,17},{... | collective-permute-start | bytes 393224 | tf_op jit(solution)/shard_map/ppermute | solution.py:14
  92.7 1.8 %collective-permute-start.21 = (bf16[256,512]{1,0:T(8,128)(2,1)S(1)}, bf16[256,512]{1,0:T(8,128)(2,1)S(1)}, u32[]{:S(2)}, u32[]{:S(2)}) collective-permute-start(bf16[256,512]{1,0:T(8,128)(2,1)S(1)} %add_convert_fusion.2), channel_id=1, source_target_pairs={{0,8},{4,12},{8,0},{12,4},{16,24},{20,28},{24,16},{28,20},{1,9},{5... | collective-permute-start | bytes 786440 | tf_op jit(solution)/shard_map/ppermute | solution.py:14
  95.0 3.9 %collective-permute-done.25 = f32[64,512]{1,0:T(8,128)S(1)} collective-permute-done((f32[64,512]{1,0:T(8,128)S(1)}, f32[64,512]{1,0:T(8,128)S(1)}, u32[]{:S(2)}, u32[]{:S(2)}) %collective-permute-start.25) | collective-permute-done | bytes 131104 | tf_op jit(solution)/shard_map/ppermute | solution.py:14
  98.9 1.6 %collective-permute-start.26 = (f32[64,512]{1,0:T(8,128)S(1)}, f32[64,512]{1,0:T(8,128)S(1)}, u32[]{:S(2)}, u32[]{:S(2)}) collective-permute-start(f32[64,512]{1,0:T(8,128)S(1)} %get-tuple-element.34), channel_id=1, source_target_pairs={{0,1},{1,0},{2,3},{3,2},{4,5},{5,4},{6,7},{7,6},{8,9},{9,8},{10,11... | collective-permute-start | bytes 393224 | tf_op jit(solution)/shard_map/ppermute | solution.py:14
  100.4 1.5 %collective-permute-start.27 = (f32[64,512]{1,0:T(8,128)S(1)}, f32[64,512]{1,0:T(8,128)S(1)}, u32[]{:S(2)}, u32[]{:S(2)}) collective-permute-start(f32[64,512]{1,0:T(8,128)S(1)} %get-tuple-element.34), channel_id=1, source_target_pairs={{0,2},{1,3},{2,0},{3,1},{4,6},{5,7},{6,4},{7,5},{8,10},{9,11},{10,... | collective-permute-start | bytes 393224 | tf_op jit(solution)/shard_map/ppermute | solution.py:14
  102.0 1.5 %collective-permute-done.21 = bf16[256,512]{1,0:T(8,128)(2,1)S(1)} collective-permute-done((bf16[256,512]{1,0:T(8,128)(2,1)S(1)}, bf16[256,512]{1,0:T(8,128)(2,1)S(1)}, u32[]{:S(2)}, u32[]{:S(2)}) %collective-permute-start.21) | collective-permute-done | bytes 262176 | tf_op jit(solution)/shard_map/ppermute | solution.py:14
  103.5 2.4 %collective-permute-start.28 = (f32[64,512]{1,0:T(8,128)S(1)}, f32[64,512]{1,0:T(8,128)S(1)}, u32[]{:S(2)}, u32[]{:S(2)}) collective-permute-start(f32[64,512]{1,0:T(8,128)S(1)} %get-tuple-element.34), channel_id=1, source_target_pairs={{0,3},{1,2},{2,1},{3,0},{4,7},{5,6},{6,5},{7,4},{8,11},{9,10},{10,... | collective-permute-start | bytes 393224 | tf_op jit(solution)/shard_map/ppermute | solution.py:14
  107.0 2.3 %collective-permute-done.28 = f32[64,512]{1,0:T(8,128)S(1)} collective-permute-done((f32[64,512]{1,0:T(8,128)S(1)}, f32[64,512]{1,0:T(8,128)S(1)}, u32[]{:S(2)}, u32[]{:S(2)}) %collective-permute-start.28) | collective-permute-done | bytes 131104 | tf_op jit(solution)/shard_map/ppermute | solution.py:14
  109.6 8.6 %collective-permute-done.22 = bf16[256,512]{1,0:T(8,128)(2,1)S(1)} collective-permute-done((bf16[256,512]{1,0:T(8,128)(2,1)S(1)}, bf16[256,512]{1,0:T(8,128)(2,1)S(1)}, u32[]{:S(2)}, u32[]{:S(2)}) %collective-permute-start.22) | collective-permute-done | bytes 262176 | tf_op jit(solution)/shard_map/ppermute | solution.py:14
  119.0 1.6 %gather_fusion = f32[8,64,512]{2,1,0:T(8,128)} fusion(f32[8,64,512]{2,1,0:T(8,128)S(1)} %constant_dynamic-update-slice_fusion, s32[1024]{0:T(1024)S(1)} %pad_clamp_fusion), kind=kCustom, calls=%fused_computation | custom fusion | bytes 2097184 | tf_op jit(solution)/shard_map/gather | solution.py:254
  (75 shorter events, 15.7 us)
Async XLA Ops:
  0.6 16.3 %collective-permute-start = (bf16[256,512]{1,0:T(8,128)(2,1)}, bf16[256,512]{1,0:T(8,128)(2,1)S(1)}, u32[]{:S(2)}, u32[]{:S(2)}) collective-permute-start(bf16[256,512]{1,0:T(8,128)(2,1)} %refs_3_.1), channel_id=1, source_target_pairs={{0,16},{4,20},{8,24},{12,28},{16,0},{20,4},{24,8},{28,12},{1,17},{... | collective-permute-start | bytes 786440 | tf_op jit(solution)/shard_map/ppermute | solution.py:14
  4.7 13.0 %collective-permute-start.4 = (bf16[256,512]{1,0:T(8,128)(2,1)}, bf16[256,512]{1,0:T(8,128)(2,1)S(1)}, u32[]{:S(2)}, u32[]{:S(2)}) collective-permute-start(bf16[256,512]{1,0:T(8,128)(2,1)} %refs_3_.1), channel_id=1, source_target_pairs={{0,8},{4,12},{8,0},{12,4},{16,24},{20,28},{24,16},{28,20},{1,9},{5... | collective-permute-start | bytes 786440 | tf_op jit(solution)/shard_map/ppermute | solution.py:14
  17.0 7.4 %collective-permute-start.1 = (bf16[256,512]{1,0:T(8,128)(2,1)S(1)}, bf16[256,512]{1,0:T(8,128)(2,1)S(1)}, u32[]{:S(2)}, u32[]{:S(2)}) collective-permute-start(bf16[256,512]{1,0:T(8,128)(2,1)S(1)} %collective-permute-done.refs_7_), channel_id=1, source_target_pairs={{0,8},{4,12},{8,0},{12,4},{16,24},{20,28},{24,16},{28,20},{1,9},{5... | collective-permute-start | bytes 786440 | tf_op jit(solution)/shard_map/ppermute | solution.py:14
  17.7 16.1 %collective-permute-start.3 = (bf16[256,512]{1,0:T(8,128)(2,1)}, bf16[256,512]{1,0:T(8,128)(2,1)S(1)}, u32[]{:S(2)}, u32[]{:S(2)}) collective-permute-start(bf16[256,512]{1,0:T(8,128)(2,1)} %refs_3_.1), channel_id=1, source_target_pairs={{0,4},{4,0},{8,12},{12,8},{16,20},{20,16},{24,28},{28,24},{1,5},{5... | collective-permute-start | bytes 786440 | tf_op jit(solution)/shard_map/ppermute | solution.py:14
  17.7 16.1 %collective-permute-start.5 = (bf16[256,512]{1,0:T(8,128)(2,1)S(1)}, bf16[256,512]{1,0:T(8,128)(2,1)S(1)}, u32[]{:S(2)}, u32[]{:S(2)}) collective-permute-start(bf16[256,512]{1,0:T(8,128)(2,1)S(1)} %collective-permute-done.4.refs_5_), channel_id=1, source_target_pairs={{0,4},{4,0},{8,12},{12,8},{16,20},{20,16},{24,28},{28,24},{1,5},{5... | collective-permute-start | bytes 786440 | tf_op jit(solution)/shard_map/ppermute | solution.py:14
  18.2 15.6 %collective-permute-start.6 = (bf16[256,512]{1,0:T(8,128)(2,1)S(1)}, bf16[256,512]{1,0:T(8,128)(2,1)S(1)}, u32[]{:S(2)}, u32[]{:S(2)}) collective-permute-start(bf16[256,512]{1,0:T(8,128)(2,1)S(1)} %collective-permute-done.refs_7_), channel_id=1, source_target_pairs={{0,4},{4,0},{8,12},{12,8},{16,20},{20,16},{24,28},{28,24},{1,5},{5... | collective-permute-start | bytes 786440 | tf_op jit(solution)/shard_map/ppermute | solution.py:14
  24.4 13.5 %collective-permute-start.2 = (bf16[256,512]{1,0:T(8,128)(2,1)S(1)}, bf16[256,512]{1,0:T(8,128)(2,1)S(1)}, u32[]{:S(2)}, u32[]{:S(2)}) collective-permute-start(bf16[256,512]{1,0:T(8,128)(2,1)S(1)} %collective-permute-done.1.refs_1_), channel_id=1, source_target_pairs={{0,4},{4,0},{8,12},{12,8},{16,20},{20,16},{24,28},{28,24},{1,5},{5... | collective-permute-start | bytes 786440 | tf_op jit(solution)/shard_map/ppermute | solution.py:14
  40.9 10.1 %collective-permute-start.9 = (bf16[256,512]{1,0:T(8,128)(2,1)S(1)}, bf16[256,512]{1,0:T(8,128)(2,1)S(1)}, u32[]{:S(2)}, u32[]{:S(2)}) collective-permute-start(bf16[256,512]{1,0:T(8,128)(2,1)S(1)} %get-tuple-element.36), channel_id=1, source_target_pairs={{0,3},{1,2},{2,1},{3,0},{4,7},{5,6},{6,5},{7,4},{8,11},{9,10},{10,... | collective-permute-start | bytes 786440 | tf_op jit(solution)/shard_map/ppermute | solution.py:14
  43.2 13.1 %collective-permute-start.8 = (bf16[256,512]{1,0:T(8,128)(2,1)S(1)}, bf16[256,512]{1,0:T(8,128)(2,1)S(1)}, u32[]{:S(2)}, u32[]{:S(2)}) collective-permute-start(bf16[256,512]{1,0:T(8,128)(2,1)S(1)} %get-tuple-element.37), channel_id=1, source_target_pairs={{0,2},{1,3},{2,0},{3,1},{4,6},{5,7},{6,4},{7,5},{8,10},{9,11},{10,... | collective-permute-start | bytes 786440 | tf_op jit(solution)/shard_map/ppermute | solution.py:14
  43.7 12.7 %collective-permute-start.7 = (bf16[256,512]{1,0:T(8,128)(2,1)S(1)}, bf16[256,512]{1,0:T(8,128)(2,1)S(1)}, u32[]{:S(2)}, u32[]{:S(2)}) collective-permute-start(bf16[256,512]{1,0:T(8,128)(2,1)S(1)} %get-tuple-element.35), channel_id=1, source_target_pairs={{0,1},{1,0},{2,3},{3,2},{4,5},{5,4},{6,7},{7,6},{8,9},{9,8},{10,11... | collective-permute-start | bytes 786440 | tf_op jit(solution)/shard_map/ppermute | solution.py:14
  44.4 17.7 %collective-permute-start.13 = (bf16[256,512]{1,0:T(8,128)(2,1)S(1)}, bf16[256,512]{1,0:T(8,128)(2,1)S(1)}, u32[]{:S(2)}, u32[]{:S(2)}) collective-permute-start(bf16[256,512]{1,0:T(8,128)(2,1)S(1)} %copy-done.6), channel_id=1, source_target_pairs={{0,1},{1,0},{2,3},{3,2},{4,5},{5,4},{6,7},{7,6},{8,9},{9,8},{10,11... | collective-permute-start | bytes 786440 | tf_op jit(solution)/shard_map/ppermute | solution.py:14
  45.8 25.4 %collective-permute-start.14 = (bf16[256,512]{1,0:T(8,128)(2,1)S(1)}, bf16[256,512]{1,0:T(8,128)(2,1)S(1)}, u32[]{:S(2)}, u32[]{:S(2)}) collective-permute-start(bf16[256,512]{1,0:T(8,128)(2,1)S(1)} %copy-done.6), channel_id=1, source_target_pairs={{0,2},{1,3},{2,0},{3,1},{4,6},{5,7},{6,4},{7,5},{8,10},{9,11},{10,... | collective-permute-start | bytes 786440 | tf_op jit(solution)/shard_map/ppermute | solution.py:14
  51.0 20.2 %collective-permute-start.15 = (bf16[256,512]{1,0:T(8,128)(2,1)S(1)}, bf16[256,512]{1,0:T(8,128)(2,1)S(1)}, u32[]{:S(2)}, u32[]{:S(2)}) collective-permute-start(bf16[256,512]{1,0:T(8,128)(2,1)S(1)} %copy-done.6), channel_id=1, source_target_pairs={{0,3},{1,2},{2,1},{3,0},{4,7},{5,6},{6,5},{7,4},{8,11},{9,10},{10,... | collective-permute-start | bytes 786440 | tf_op jit(solution)/shard_map/ppermute | solution.py:14
  56.6 16.8 %collective-permute-start.10 = (bf16[256,512]{1,0:T(8,128)(2,1)S(1)}, bf16[256,512]{1,0:T(8,128)(2,1)S(1)}, u32[]{:S(2)}, u32[]{:S(2)}) collective-permute-start(bf16[256,512]{1,0:T(8,128)(2,1)S(1)} %add_convert_fusion.4.refs_0_), channel_id=1, source_target_pairs={{0,1},{1,0},{2,3},{3,2},{4,5},{5,4},{6,7},{7,6},{8,9},{9,8},{10,11... | collective-permute-start | bytes 786440 | tf_op jit(solution)/shard_map/ppermute | solution.py:14
  58.1 15.2 %collective-permute-start.11 = (bf16[256,512]{1,0:T(8,128)(2,1)S(1)}, bf16[256,512]{1,0:T(8,128)(2,1)S(1)}, u32[]{:S(2)}, u32[]{:S(2)}) collective-permute-start(bf16[256,512]{1,0:T(8,128)(2,1)S(1)} %add_convert_fusion.4.refs_0_), channel_id=1, source_target_pairs={{0,2},{1,3},{2,0},{3,1},{4,6},{5,7},{6,4},{7,5},{8,10},{9,11},{10,... | collective-permute-start | bytes 786440 | tf_op jit(solution)/shard_map/ppermute | solution.py:14
  62.1 16.6 %collective-permute-start.12 = (bf16[256,512]{1,0:T(8,128)(2,1)S(1)}, bf16[256,512]{1,0:T(8,128)(2,1)S(1)}, u32[]{:S(2)}, u32[]{:S(2)}) collective-permute-start(bf16[256,512]{1,0:T(8,128)(2,1)S(1)} %add_convert_fusion.4.refs_0_), channel_id=1, source_target_pairs={{0,3},{1,2},{2,1},{3,0},{4,7},{5,6},{6,5},{7,4},{8,11},{9,10},{10,... | collective-permute-start | bytes 786440 | tf_op jit(solution)/shard_map/ppermute | solution.py:14
  63.7 15.0 %copy-start.5 = (bf16[512,512]{1,0:T(8,128)(2,1)S(1)}, bf16[512,512]{1,0:T(8,128)(2,1)}, u32[]{:S(2)}) copy-start(bf16[512,512]{1,0:T(8,128)(2,1)} %refs_8_.1) | copy-start | bytes 1572868
  71.2 10.6 %copy-start.2 = (bf16[8,256,1024]{2,1,0:T(8,128)(2,1)S(1)}, bf16[8,256,1024]{2,1,0:T(8,128)(2,1)}, u32[]{:S(2)}) copy-start(bf16[8,256,1024]{2,1,0:T(8,128)(2,1)} %copy-done.1) | copy-start | bytes 12582916
  81.7 1.3 %collective-permute-start.23 = (f32[64,512]{1,0:T(8,128)S(1)}, f32[64,512]{1,0:T(8,128)S(1)}, u32[]{:S(2)}, u32[]{:S(2)}) collective-permute-start(f32[64,512]{1,0:T(8,128)S(1)} %get-tuple-element.32), channel_id=1, source_target_pairs={{0,4},{4,0},{8,12},{12,8},{16,20},{20,16},{24,28},{28,24},{1,5},{5... | collective-permute-start | bytes 393224 | tf_op jit(solution)/shard_map/ppermute | solution.py:14
  82.5 10.2 %collective-permute-start.20 = (bf16[256,512]{1,0:T(8,128)(2,1)S(1)}, bf16[256,512]{1,0:T(8,128)(2,1)S(1)}, u32[]{:S(2)}, u32[]{:S(2)}) collective-permute-start(bf16[256,512]{1,0:T(8,128)(2,1)S(1)} %get-tuple-element.30), channel_id=1, source_target_pairs={{0,4},{4,0},{8,12},{12,8},{16,20},{20,16},{24,28},{28,24},{1,5},{5... | collective-permute-start | bytes 786440 | tf_op jit(solution)/shard_map/ppermute | solution.py:14
  83.1 5.8 %collective-permute-start.24 = (f32[64,512]{1,0:T(8,128)S(1)}, f32[64,512]{1,0:T(8,128)S(1)}, u32[]{:S(2)}, u32[]{:S(2)}) collective-permute-start(f32[64,512]{1,0:T(8,128)S(1)} %add.87), channel_id=1, source_target_pairs={{0,8},{4,12},{8,0},{12,4},{16,24},{20,28},{24,16},{28,20},{1,9},{5... | collective-permute-start | bytes 393224 | tf_op jit(solution)/shard_map/ppermute | solution.py:14
  85.8 8.7 %collective-permute-start.17 = (bf16[256,512]{1,0:T(8,128)(2,1)S(1)}, bf16[256,512]{1,0:T(8,128)(2,1)S(1)}, u32[]{:S(2)}, u32[]{:S(2)}) collective-permute-start(bf16[256,512]{1,0:T(8,128)(2,1)S(1)} %get-tuple-element.26), channel_id=1, source_target_pairs={{0,4},{4,0},{8,12},{12,8},{16,20},{20,16},{24,28},{28,24},{1,5},{5... | collective-permute-start | bytes 786440 | tf_op jit(solution)/shard_map/ppermute | solution.py:14
  87.3 13.1 %collective-permute-start.19 = (bf16[256,512]{1,0:T(8,128)(2,1)S(1)}, bf16[256,512]{1,0:T(8,128)(2,1)S(1)}, u32[]{:S(2)}, u32[]{:S(2)}) collective-permute-start(bf16[256,512]{1,0:T(8,128)(2,1)S(1)} %get-tuple-element.28), channel_id=1, source_target_pairs={{0,4},{4,0},{8,12},{12,8},{16,20},{20,16},{24,28},{28,24},{1,5},{5... | collective-permute-start | bytes 786440 | tf_op jit(solution)/shard_map/ppermute | solution.py:14
  87.9 21.7 %collective-permute-start.16 = (bf16[256,512]{1,0:T(8,128)(2,1)S(1)}, bf16[256,512]{1,0:T(8,128)(2,1)S(1)}, u32[]{:S(2)}, u32[]{:S(2)}) collective-permute-start(bf16[256,512]{1,0:T(8,128)(2,1)S(1)} %get-tuple-element.24), channel_id=1, source_target_pairs={{0,4},{4,0},{8,12},{12,8},{16,20},{20,16},{24,28},{28,24},{1,5},{5... | collective-permute-start | bytes 786440 | tf_op jit(solution)/shard_map/ppermute | solution.py:14
  88.9 10.0 %collective-permute-start.25 = (f32[64,512]{1,0:T(8,128)S(1)}, f32[64,512]{1,0:T(8,128)S(1)}, u32[]{:S(2)}, u32[]{:S(2)}) collective-permute-start(f32[64,512]{1,0:T(8,128)S(1)} %add.88), channel_id=1, source_target_pairs={{0,16},{4,20},{8,24},{12,28},{16,0},{20,4},{24,8},{28,12},{1,17},{... | collective-permute-start | bytes 393224 | tf_op jit(solution)/shard_map/ppermute | solution.py:14
  92.7 10.8 %collective-permute-start.21 = (bf16[256,512]{1,0:T(8,128)(2,1)S(1)}, bf16[256,512]{1,0:T(8,128)(2,1)S(1)}, u32[]{:S(2)}, u32[]{:S(2)}) collective-permute-start(bf16[256,512]{1,0:T(8,128)(2,1)S(1)} %add_convert_fusion.2), channel_id=1, source_target_pairs={{0,8},{4,12},{8,0},{12,4},{16,24},{20,28},{24,16},{28,20},{1,9},{5... | collective-permute-start | bytes 786440 | tf_op jit(solution)/shard_map/ppermute | solution.py:14
  94.6 14.9 %collective-permute-start.18 = (bf16[256,512]{1,0:T(8,128)(2,1)S(1)}, bf16[256,512]{1,0:T(8,128)(2,1)S(1)}, u32[]{:S(2)}, u32[]{:S(2)}) collective-permute-start(bf16[256,512]{1,0:T(8,128)(2,1)S(1)} %add_convert_fusion.3), channel_id=1, source_target_pairs={{0,8},{4,12},{8,0},{12,4},{16,24},{20,28},{24,16},{28,20},{1,9},{5... | collective-permute-start | bytes 786440 | tf_op jit(solution)/shard_map/ppermute | solution.py:14
  98.9 7.2 %collective-permute-start.26 = (f32[64,512]{1,0:T(8,128)S(1)}, f32[64,512]{1,0:T(8,128)S(1)}, u32[]{:S(2)}, u32[]{:S(2)}) collective-permute-start(f32[64,512]{1,0:T(8,128)S(1)} %get-tuple-element.34), channel_id=1, source_target_pairs={{0,1},{1,0},{2,3},{3,2},{4,5},{5,4},{6,7},{7,6},{8,9},{9,8},{10,11... | collective-permute-start | bytes 393224 | tf_op jit(solution)/shard_map/ppermute | solution.py:14
  100.4 6.6 %collective-permute-start.27 = (f32[64,512]{1,0:T(8,128)S(1)}, f32[64,512]{1,0:T(8,128)S(1)}, u32[]{:S(2)}, u32[]{:S(2)}) collective-permute-start(f32[64,512]{1,0:T(8,128)S(1)} %get-tuple-element.34), channel_id=1, source_target_pairs={{0,2},{1,3},{2,0},{3,1},{4,6},{5,7},{6,4},{7,5},{8,10},{9,11},{10,... | collective-permute-start | bytes 393224 | tf_op jit(solution)/shard_map/ppermute | solution.py:14
  103.5 5.9 %collective-permute-start.28 = (f32[64,512]{1,0:T(8,128)S(1)}, f32[64,512]{1,0:T(8,128)S(1)}, u32[]{:S(2)}, u32[]{:S(2)}) collective-permute-start(f32[64,512]{1,0:T(8,128)S(1)} %get-tuple-element.34), channel_id=1, source_target_pairs={{0,3},{1,2},{2,1},{3,0},{4,7},{5,6},{6,5},{7,4},{8,11},{9,10},{10,... | collective-permute-start | bytes 393224 | tf_op jit(solution)/shard_map/ppermute | solution.py:14
  106.1 12.0 %collective-permute-start.22 = (bf16[256,512]{1,0:T(8,128)(2,1)S(1)}, bf16[256,512]{1,0:T(8,128)(2,1)S(1)}, u32[]{:S(2)}, u32[]{:S(2)}) collective-permute-start(bf16[256,512]{1,0:T(8,128)(2,1)S(1)} %add_convert_fusion.1), channel_id=1, source_target_pairs={{0,16},{4,20},{8,24},{12,28},{16,0},{20,4},{24,8},{28,12},{1,17},{... | collective-permute-start | bytes 786440 | tf_op jit(solution)/shard_map/ppermute | solution.py:14
  109.4 9.6 %collective-permute-start.29 = (f32[4,64,512]{2,1,0:T(8,128)S(1)}, f32[4,64,512]{2,1,0:T(8,128)S(1)}, u32[]{:S(2)}, u32[]{:S(2)}) collective-permute-start(f32[4,64,512]{2,1,0:T(8,128)S(1)} %pad_maximum_fusion), channel_id=1, source_target_pairs={{0,4},{4,0},{8,12},{12,8},{16,20},{20,16},{24,28},{28,24},{1,5},{5... | collective-permute-start | bytes 1572872 | tf_op jit(solution)/shard_map/ppermute | solution.py:14
  (5 other events, 19.8 us)

commit v2 on v1

v2 whole, which is shorter than its diff:
```python
import functools

import jax
import jax.numpy as jnp
from jax import lax
from jax.experimental import pallas as pl
from jax.experimental.pallas import tpu as pltpu
from jax.sharding import PartitionSpec as P

WHOLE = pl.BlockSpec(memory_space=pltpu.VMEM)
SCALARS = pl.BlockSpec(memory_space=pltpu.SMEM)


def exchange(x, axis, mask):
    return lax.ppermute(x, axis, [(i, i ^ mask) for i in range(lax.axis_size(axis))])


def after(x, *others):
    return lax.optimization_barrier((x, *others))[0]


def params(mib):
    return pltpu.CompilerParams(vmem_limit_bytes=mib * 1024 * 1024)


def like(shape, dtype):
    return jax.ShapeDtypeStruct(shape, dtype)


def bf16_dot(a, b):
    return jnp.dot(a, b, preferred_element_type=jnp.float32)


def densify_kernel(rows_ref, cols_ref, counts_ref, place_ref, tiles_ref, a_ref, acc_ref, *, col_tiles, slots):
    step = pl.program_id(0)
    column = step ^ place_ref[0]
    member = place_ref[1]
    size = tiles_ref.shape[-1]
    acc_ref[...] = jnp.zeros_like(acc_ref)

    def add(slot, carry):
        row = rows_ref[column * slots + slot]
        row = ((row // col_tiles) ^ member) * col_tiles + lax.rem(row, col_tiles)
        spot = row * col_tiles + cols_ref[column * slots + slot]
        acc_ref[spot] += tiles_ref[0, slot].astype(jnp.float32)
        return carry

    lax.fori_loop(0, counts_ref[column], add, 0)
    for spot in range(acc_ref.shape[0]):
        row, col = spot // col_tiles, spot % col_tiles
        a_ref[0, row * size:(row + 1) * size, col * size:(col + 1) * size] = acc_ref[spot].astype(a_ref.dtype)


def densify(tiles, tile_rows, tile_cols, tile_counts, place, group_count, rows_local):
    columns, slots, size, _ = tiles.shape
    col_tiles = rows_local // size
    rows = group_count * rows_local
    return pl.pallas_call(
        functools.partial(densify_kernel, col_tiles=col_tiles, slots=slots),
        out_shape=like((columns, rows, rows_local), jnp.bfloat16),
        grid_spec=pltpu.PrefetchScalarGridSpec(
            num_scalar_prefetch=4,
            grid=(columns,),
            in_specs=[pl.BlockSpec((1, slots, size, size), lambda j, r, c, n, p: (j ^ p[0], 0, 0, 0))],
            out_specs=pl.BlockSpec((1, rows, rows_local), lambda j, r, c, n, p: (j, 0, 0)),
            scratch_shapes=[pltpu.VMEM((group_count * col_tiles * col_tiles, size, size), jnp.float32)],
        ),
        compiler_params=params(12),
        cost_estimate=pl.CostEstimate(
            flops=columns * slots * size * size, bytes_accessed=8 * rows * columns * rows_local, transcendentals=0),
        name="densify",
    )(tile_rows.reshape(-1), tile_cols.reshape(-1), tile_counts.reshape(-1), place, tiles)


def transpose_kernel(a_ref, out_ref):
    out_ref[0] = a_ref[0].T


def transposed(dense):
    columns, rows, cols = dense.shape
    return pl.pallas_call(
        transpose_kernel,
        out_shape=like((columns, cols, rows), jnp.bfloat16),
        grid=(columns,),
        in_specs=[pl.BlockSpec((1, rows, cols), lambda j: (j, 0, 0))],
        out_specs=pl.BlockSpec((1, cols, rows), lambda j: (j, 0, 0)),
        compiler_params=params(12),
        cost_estimate=pl.CostEstimate(flops=0, bytes_accessed=8 * columns * rows * cols, transcendentals=0),
        name="transposed",
    )(dense)


def forward_kernel(*refs, which, groups, has_prev):
    dense_ref, sources, rest = refs[0], refs[1:1 + len(which)], refs[1 + len(which):]
    prev = rest[:groups] if has_prev else None
    outs = rest[groups if has_prev else 0:]
    rows = sources[0].shape[0]
    for k in range(groups):
        total = prev[k][...] if has_prev else None
        for j, source in zip(which, sources):
            part = bf16_dot(dense_ref[j, k * rows:(k + 1) * rows, :], source[...])
            total = part if total is None else total + part
        outs[k][...] = total.astype(outs[k].dtype)


def forward(dense, which, sources, prev, dtypes):
    groups = len(dtypes)
    rows, width = sources[0].shape
    return pl.pallas_call(
        functools.partial(forward_kernel, which=which, groups=groups, has_prev=prev is not None),
        out_shape=[like((rows, width), dtype) for dtype in dtypes],
        in_specs=[WHOLE] * (1 + len(which) + (groups if prev is not None else 0)),
        out_specs=[WHOLE] * groups,
        compiler_params=params(8),
        cost_estimate=pl.CostEstimate(
            flops=2 * len(which) * groups * rows * rows * width,
            bytes_accessed=2 * len(which) * groups * rows * rows + 4 * groups * rows * width, transcendentals=0),
        name="forward",
    )(dense, *sources, *(prev or []))


def middle_kernel(*refs, groups):
    pieces, cot_ref, weight_ref = refs[:groups], refs[groups], refs[groups + 1]
    act_ref, agg_ref, pre_grad_ref, grad_ref = refs[groups + 2:]
    agg = pieces[0][...]
    for piece in pieces[1:]:
        agg = agg + piece[...].astype(jnp.float32)
    agg = agg.astype(jnp.bfloat16)
    agg_ref[...] = agg
    weight = weight_ref[...]
    preact = bf16_dot(agg, weight)
    sigma = jax.nn.sigmoid(preact)
    act_ref[...] = (preact * sigma).astype(act_ref.dtype)
    slope = sigma * (1.0 + preact * (1.0 - sigma))
    pre_grad = (cot_ref[...].astype(jnp.float32) * slope).astype(jnp.bfloat16)
    pre_grad_ref[...] = pre_grad
    grad_ref[...] = lax.dot_general(
        pre_grad, weight, (((1,), (1,)), ((), ())), preferred_element_type=jnp.float32
    ).astype(grad_ref.dtype)


def middle(pieces, cotangent, weight):
    rows, width = cotangent.shape
    return pl.pallas_call(
        functools.partial(middle_kernel, groups=len(pieces)),
        out_shape=[like((rows, width), jnp.bfloat16)] * 4,
        in_specs=[WHOLE] * (2 + len(pieces)),
        out_specs=[WHOLE] * 4,
        compiler_params=params(8),
        cost_estimate=pl.CostEstimate(
            flops=4 * rows * width * width, bytes_accessed=10 * rows * width, transcendentals=rows * width),
        name="middle",
    )(*pieces, cotangent, weight)


def weight_kernel(place_ref, agg_ref, pre_grad_ref, own_ref, *rest, groups):
    sends, part_ref = rest[:-1], rest[-1]
    member = place_ref[1]
    rows = own_ref.shape[0]
    part_ref[...] = lax.dot_general(
        agg_ref[...], pre_grad_ref[...], (((0,), (0,)), ((), ())), preferred_element_type=jnp.float32
    )
    for k in range(groups):
        out = own_ref if k == 0 else sends[k - 1]
        out[...] = part_ref[pl.ds(pl.multiple_of((member ^ k) * rows, rows), rows), :].astype(out.dtype)


def weight_part(agg, pre_grad, place, groups):
    rows, width = agg.shape
    part = (width // groups, width)
    return pl.pallas_call(
        functools.partial(weight_kernel, groups=groups),
        out_shape=[like(part, jnp.float32)] + [like(part, jnp.bfloat16)] * (groups - 1),
        in_specs=[SCALARS, WHOLE, WHOLE],
        out_specs=[WHOLE] * groups,
        scratch_shapes=[pltpu.VMEM((width, width), jnp.float32)],
        compiler_params=params(8),
        cost_estimate=pl.CostEstimate(
            flops=2 * rows * width * width, bytes_accessed=4 * rows * width + 4 * width * width, transcendentals=0),
        name="weight_part",
    )(place, agg, pre_grad)


def backward_kernel(*refs, pair, groups):
    at_ref, grads, (own_ref, other_ref) = refs[0], refs[1:1 + groups], refs[1 + groups:]
    rows = grads[0].shape[0]
    for side, out_ref in ((1, other_ref), (0, own_ref)):
        total = None
        for k in range(groups):
            part = bf16_dot(at_ref[2 * pair + side, :, k * rows:(k + 1) * rows], grads[k][...])
            total = part if total is None else total + part
        out_ref[...] = total.astype(out_ref.dtype)


def backward(dense_t, pair, grads):
    _, cols, rows = dense_t.shape
    width = grads[0].shape[1]
    return pl.pallas_call(
        functools.partial(backward_kernel, pair=pair, groups=len(grads)),
        out_shape=[like((cols, width), jnp.float32), like((cols, width), jnp.bfloat16)],
        in_specs=[WHOLE] * (1 + len(grads)),
        out_specs=[WHOLE] * 2,
        compiler_params=params(8),
        cost_estimate=pl.CostEstimate(
            flops=4 * cols * rows * width, bytes_accessed=4 * cols * rows + 2 * rows * width + 6 * cols * width,
            transcendentals=0),
        name="backward",
    )(dense_t, *grads)


def local(features, cotangent, weight, tiles, tile_rows, tile_cols, tile_counts):
    blocks = lax.axis_size("dom")
    groups = lax.axis_size("repl")
    pairs = blocks // 2
    rows_local, width = features.shape
    scale = float(rows_local * blocks * groups) ** (-0.5)
    position, member = lax.axis_index("dom"), lax.axis_index("repl")
    place = jnp.stack([position, member]).astype(jnp.int32)

    dense = densify(tiles[0, 0], tile_rows, tile_cols, tile_counts, place, groups, rows_local)

    sources = {0: features}
    bit = pairs // 2
    while bit:
        for j in list(sources):
            given = sources[j] if j == 0 else after(sources[j], dense)
            sources[j + 2 * bit] = exchange(given, "dom", 2 * bit)
        bit //= 2
    for j in list(sources):
        sources[j + 1] = exchange(sources[j], "dom", 1)

    early, late = list(range(blocks - 2)), [blocks - 2, blocks - 1]
    totals = forward(dense, early, [sources[j] for j in early], None, [jnp.float32] * groups)
    pieces = forward(
        dense, late, [sources[j] for j in late], totals, [jnp.float32] + [jnp.bfloat16] * (groups - 1))

    arrived = [exchange(pieces[k], "repl", k) for k in range(1, groups)]
    dense_t = transposed(after(dense, *pieces))
    arrived[-1] = after(arrived[-1], dense_t)
    activated, agg, pre_grad, grad = middle([pieces[0]] + arrived, cotangent, weight)
    grads = [grad] + [exchange(grad, "repl", k) for k in range(1, groups)]
    shares = weight_part(agg, pre_grad, place, groups)
    grads[-1] = after(grads[-1], *shares)

    partials = {pair: backward(dense_t, pair, grads) for pair in reversed(range(pairs))}
    swapped = {}
    last = None
    for pair in reversed(range(pairs)):
        own, other = partials[pair]
        swapped[pair] = exchange(other, "dom", 1)
    sums = {pair: partials[pair][0] + swapped[pair].astype(jnp.float32) for pair in swapped}
    bit = 1
    while bit < pairs:
        for pair in sorted(sums, reverse=True):
            if pair & bit:
                given = sums.pop(pair).astype(jnp.bfloat16)
                if last is not None:
                    given = after(given, last)
                last = exchange(given, "dom", 2 * bit)
                sums[pair ^ bit] = sums[pair ^ bit] + last.astype(jnp.float32)
                if bit == 1 and pair == pairs - 1:
                    first_sum, first_received = given, last
        bit *= 2
    feature_grad = sums[0].astype(jnp.bfloat16)

    part = shares[0]
    for k in range(1, groups):
        part = part + exchange(after(shares[k], first_sum), "repl", k).astype(jnp.float32)
    part = after(part, first_received)
    core = position % 2
    part = part.reshape(2, -1, width)
    part = lax.dynamic_index_in_dim(part, core, 0, False) + exchange(
        lax.dynamic_index_in_dim(part, 1 - core, 0, False).astype(jnp.bfloat16), "dom", 1).astype(jnp.float32)
    part = part.astype(jnp.bfloat16)
    terms = [part.astype(jnp.float32)]
    terms += [exchange(part, "dom", 2 * k).astype(jnp.float32) for k in range(1, pairs)]
    while len(terms) > 1:
        terms = [terms[i] + terms[i + 1] for i in range(0, len(terms), 2)]
    part = terms[0] * scale
    mine = jnp.stack([part] + [exchange(part, "repl", k) for k in range(1, groups)])
    both = jnp.concatenate([mine, exchange(mine, "dom", 1)])
    order = ((jnp.arange(2)[None, :] ^ core) * groups + (jnp.arange(groups)[:, None] ^ member)).reshape(-1)
    weight_grad = both[order].reshape(weight.shape)
    return (activated, feature_grad, weight_grad)


def solution(mesh):
    in_specs = (
        P(("dom", "repl"), None),
        P(("dom", "repl"), None),
        P(),
        P("dom", "repl", None, None, None, None),
        P("dom", "repl", None, None),
        P("dom", "repl", None, None),
        P("dom", "repl", None),
    )
    out_specs = (P(("dom", "repl"), None), P(("dom", "repl"), None), P())
    return jax.shard_map(local, mesh=mesh, in_specs=in_specs, out_specs=out_specs, check_vma=False)
```

time: 121 us -> 108 us (0.89)
  Pallas kernels: 24.9 us -> 13.2 us
  local copies, waits for them, and re-layouts: 7.94 us -> 12.5 us
  starting transfers between devices: 35.4 us -> 31.2 us
  waiting for transfers between devices: 50 us -> 48.1 us
    pallas_call x8 -> x9, Pallas kernels: 18.2 us -> 8.96 us  [the longest x4 2.79 us: backward(): pl.pallas_call(functools.partial(backward_kernel, pair=pair, groups=len(g...]
    unnamed x17 -> x21, local copies, waits for them, and re-layouts: 4.65 us -> 9.23 us
    ppermute x30 -> x31, starting transfers between devices: 35.4 us -> 31.2 us  [exchange(): lax.ppermute(x, axis, [(i, i ^ mask) for i in range(lax.axis_size(axis))])]
    pallas_call x1, Pallas kernels: 6.66 us -> 4.24 us  [densify(): pl.pallas_call(functools.partial(densify_kernel, col_tiles=col_tiles, slo...]
    ppermute x30 -> x31, waiting for transfers between devices: 50 us -> 48.1 us  [exchange(): lax.ppermute(x, axis, [(i, i ^ mask) for i in range(lax.axis_size(axis))])]
  transfers between devices with their start and end apart: 30 -> 31, of which waited for: 13 -> 17; matrix products, arithmetic and copies ran while one was open for 3% -> 3% of each run, Pallas kernels for 16% -> 10%
where the time goes in v2:
time: 108 us; the launch traced here: 107 us
  waiting for transfers between devices  48.1 us (45%)
  starting transfers between devices  31.2 us (29%)
  Pallas kernels  13.2 us (12%)
  local copies, waits for them, and re-layouts  12.5 us (12%)
  other arithmetic  1.42 us (1%)
    ppermute x31, waiting for transfers between devices, exchange(): lax.ppermute(x, axis, [(i, i ^ mask) for i in range(lax.axis_size(axis))])  48.1 us
    ppermute x31, starting transfers between devices, exchange(): lax.ppermute(x, axis, [(i, i ^ mask) for i in range(lax.axis_size(axis))])  31.2 us
    unnamed x21, local copies, waits for them, and re-layouts  9.23 us
    pallas_call x1, Pallas kernels, densify(): pl.pallas_call(functools.partial(densify_kernel, col_tiles=col_tiles, slo...  4.24 us
    pallas_call x4, Pallas kernels, backward(): pl.pallas_call(functools.partial(backward_kernel, pair=pair, groups=len(g...  2.79 us
    pallas_call x2, Pallas kernels, forward(): pl.pallas_call(functools.partial(forward_kernel, which=which, groups=grou...  2.49 us
  transfers between devices with their start and end apart: 31, of which 17 were waited for; matrix products, arithmetic and copies ran while one was open for 3% of the time, Pallas kernels for 10%

profile of v2, /device:TPU:0, one launch (start us, length us, event | category | flops | bytes accessed | tf_op | source)
XLA Modules:
  0.0 107.2 jit_solution(7636976455291031081)
XLA Ops:
  0.6 4.1 %collective-permute-start = (bf16[256,512]{1,0:T(8,128)(2,1)}, bf16[256,512]{1,0:T(8,128)(2,1)S(1)}, u32[]{:S(2)}, u32[]{:S(2)}) collective-permute-start(bf16[256,512]{1,0:T(8,128)(2,1)} %refs_1_.1), channel_id=1, source_target_pairs={{0,16},{4,20},{8,24},{12,28},{16,0},{20,4},{24,8},{28,12},{1,17},{... | collective-permute-start | bytes 786440 | tf_op jit(solution)/shard_map/ppermute | solution.py:15
  4.7 1.6 %collective-permute-start.4 = (bf16[256,512]{1,0:T(8,128)(2,1)}, bf16[256,512]{1,0:T(8,128)(2,1)S(1)}, u32[]{:S(2)}, u32[]{:S(2)}) collective-permute-start(bf16[256,512]{1,0:T(8,128)(2,1)} %refs_1_.1), channel_id=1, source_target_pairs={{0,8},{4,12},{8,0},{12,4},{16,24},{20,28},{24,16},{28,20},{1,9},{5... | collective-permute-start | bytes 786440 | tf_op jit(solution)/shard_map/ppermute | solution.py:15
  7.9 2.2 %copy-done.4 = bf16[1,1,8,16,128,128]{5,4,3,2,1,0:T(8,128)(2,1)S(1)} copy-done((bf16[1,1,8,16,128,128]{5,4,3,2,1,0:T(8,128)(2,1)S(1)}, bf16[1,1,8,16,128,128]{5,4,3,2,1,0:T(8,128)(2,1)}, u32[]{:S(2)}) %copy-start.4) | copy-done | bytes 4194328
  10.8 4.2 %densify.1.refs_0_.a_ref = bf16[8,1024,256]{2,1,0:T(8,128)(2,1)S(1)} custom-call(s32[128]{0:T(128)S(1)} %reshape.64.rows_ref, s32[128]{0:T(128)S(1)} %reshape.65.cols_ref, s32[8]{0:T(128)S(1)} %bitcast.27, s32[2]{0:T(128)S(1)} %pad_add_fusion.place_ref, bf16[8,16,128,128]{3,2,1,0:T(8,128)(2,1)S(1)} %bitcast.26), custom_call_target="tpu_custom_call" | custom-call | flops 2097152 | bytes 16777216 | tf_op jit(solution)/shard_map/densify/pallas_call | solution.py:58
  15.0 2.0 %collective-permute-done.refs_5_ = bf16[256,512]{1,0:T(8,128)(2,1)S(1)} collective-permute-done((bf16[256,512]{1,0:T(8,128)(2,1)}, bf16[256,512]{1,0:T(8,128)(2,1)S(1)}, u32[]{:S(2)}, u32[]{:S(2)}) %collective-permute-start) | collective-permute-done | bytes 262176 | tf_op jit(solution)/shard_map/ppermute | solution.py:15
  18.2 6.2 %collective-permute-done.1.refs_1_ = bf16[256,512]{1,0:T(8,128)(2,1)S(1)} collective-permute-done((bf16[256,512]{1,0:T(8,128)(2,1)S(1)}, bf16[256,512]{1,0:T(8,128)(2,1)S(1)}, u32[]{:S(2)}, u32[]{:S(2)}) %collective-permute-start.1) | collective-permute-done | bytes 262176 | tf_op jit(solution)/shard_map/ppermute | solution.py:15
  24.4 1.8 %forward.2 = (f32[256,512]{1,0:T(8,128)S(1)}, f32[256,512]{1,0:T(8,128)S(1)}, f32[256,512]{1,0:T(8,128)S(1)}, f32[256,512]{1,0:T(8,128)S(1)}) custom-call(bf16[8,1024,256]{2,1,0:T(8,128)(2,1)S(1)} %densify.1.refs_0_.a_ref, bf16[256,512]{1,0:T(8,128)(2,1)S(1)} %copy-done.8, bf16[256,512]{1,0:T(8,128)(2,1)S(1)} %collective-permute-done.3.refs_2_, ...), custom_call_target="tpu_custom_call" | custom-call | flops 1610612736 | bytes 5242880 | tf_op jit(solution)/shard_map/forward/pallas_call | solution.py:109
  26.9 2.3 %collective-permute-start.9 = (bf16[256,512]{1,0:T(8,128)(2,1)S(1)}, bf16[256,512]{1,0:T(8,128)(2,1)S(1)}, u32[]{:S(2)}, u32[]{:S(2)}) collective-permute-start(bf16[256,512]{1,0:T(8,128)(2,1)S(1)} %get-tuple-element.45), channel_id=1, source_target_pairs={{0,3},{1,2},{2,1},{3,0},{4,7},{5,6},{6,5},{7,4},{8,11},{9,10},{10,... | collective-permute-start | bytes 786440 | tf_op jit(solution)/shard_map/ppermute | solution.py:15
  30.5 1.6 %transposed.1.refs_0_ = bf16[8,256,1024]{2,1,0:T(8,128)(2,1)S(1)} custom-call(bf16[8,1024,256]{2,1,0:T(8,128)(2,1)S(1)} %densify.1.refs_0_.a_ref), custom_call_target="tpu_custom_call" | custom-call | bytes 16777216 | tf_op jit(solution)/shard_map/transposed/pallas_call | solution.py:81
  32.1 2.0 %copy-done = bf16[8,256,1024]{2,1,0:T(8,128)(2,1)} copy-done((bf16[8,256,1024]{2,1,0:T(8,128)(2,1)}, bf16[8,256,1024]{2,1,0:T(8,128)(2,1)S(1)}, u32[]{:S(2)}) %copy-start) | copy-done | bytes 4194328
  34.1 3.0 %collective-permute-done.9.refs_3_ = bf16[256,512]{1,0:T(8,128)(2,1)S(1)} collective-permute-done((bf16[256,512]{1,0:T(8,128)(2,1)S(1)}, bf16[256,512]{1,0:T(8,128)(2,1)S(1)}, u32[]{:S(2)}, u32[]{:S(2)}) %collective-permute-start.9) | collective-permute-done | bytes 262176 | tf_op jit(solution)/shard_map/ppermute | solution.py:15
  37.1 5.1 %collective-permute-done.7.refs_1_ = bf16[256,512]{1,0:T(8,128)(2,1)S(1)} collective-permute-done((bf16[256,512]{1,0:T(8,128)(2,1)S(1)}, bf16[256,512]{1,0:T(8,128)(2,1)S(1)}, u32[]{:S(2)}, u32[]{:S(2)}) %collective-permute-start.7) | collective-permute-done | bytes 262176 | tf_op jit(solution)/shard_map/ppermute | solution.py:15
  43.4 2.2 %collective-permute-start.12 = (bf16[256,512]{1,0:T(8,128)(2,1)S(1)}, bf16[256,512]{1,0:T(8,128)(2,1)S(1)}, u32[]{:S(2)}, u32[]{:S(2)}) collective-permute-start(bf16[256,512]{1,0:T(8,128)(2,1)S(1)} %get-tuple-element.49.refs_1_), channel_id=1, source_target_pairs={{0,3},{1,2},{2,1},{3,0},{4,7},{5,6},{6,5},{7,4},{8,11},{9,10},{10,... | collective-permute-start | bytes 786440 | tf_op jit(solution)/shard_map/ppermute | solution.py:15
  47.8 5.7 %collective-permute-done.12.refs_4_ = bf16[256,512]{1,0:T(8,128)(2,1)S(1)} collective-permute-done((bf16[256,512]{1,0:T(8,128)(2,1)S(1)}, bf16[256,512]{1,0:T(8,128)(2,1)S(1)}, u32[]{:S(2)}, u32[]{:S(2)}) %collective-permute-start.12) | collective-permute-done | bytes 262176 | tf_op jit(solution)/shard_map/ppermute | solution.py:15
  53.5 4.5 %collective-permute-done.10.refs_2_ = bf16[256,512]{1,0:T(8,128)(2,1)S(1)} collective-permute-done((bf16[256,512]{1,0:T(8,128)(2,1)S(1)}, bf16[256,512]{1,0:T(8,128)(2,1)S(1)}, u32[]{:S(2)}, u32[]{:S(2)}) %collective-permute-start.10) | collective-permute-done | bytes 262176 | tf_op jit(solution)/shard_map/ppermute | solution.py:15
  58.2 2.2 %copy-done.1 = bf16[8,256,1024]{2,1,0:T(8,128)(2,1)S(1)} copy-done((bf16[8,256,1024]{2,1,0:T(8,128)(2,1)S(1)}, bf16[8,256,1024]{2,1,0:T(8,128)(2,1)}, u32[]{:S(2)}) %copy-start.1) | copy-done | bytes 4194328
  61.3 1.4 %collective-permute-done.15 = bf16[256,512]{1,0:T(8,128)(2,1)S(1)} collective-permute-done((bf16[256,512]{1,0:T(8,128)(2,1)S(1)}, bf16[256,512]{1,0:T(8,128)(2,1)S(1)}, u32[]{:S(2)}, u32[]{:S(2)}) %collective-permute-start.15) | collective-permute-done | bytes 262176 | tf_op jit(solution)/shard_map/ppermute | solution.py:15
  62.7 1.4 %collective-permute-start.20 = (bf16[128,512]{1,0:T(8,128)(2,1)S(1)}, bf16[128,512]{1,0:T(8,128)(2,1)S(1)}, u32[]{:S(2)}, u32[]{:S(2)}) collective-permute-start(bf16[128,512]{1,0:T(8,128)(2,1)S(1)} %get-tuple-element.67), channel_id=1, source_target_pairs={{0,1},{1,0},{2,3},{3,2},{4,5},{5,4},{6,7},{7,6},{8,9},{9,8},{10,11... | collective-permute-start | bytes 393224 | tf_op jit(solution)/shard_map/ppermute | solution.py:15
  64.2 1.4 %collective-permute-start.21 = (bf16[128,512]{1,0:T(8,128)(2,1)S(1)}, bf16[128,512]{1,0:T(8,128)(2,1)S(1)}, u32[]{:S(2)}, u32[]{:S(2)}) collective-permute-start(bf16[128,512]{1,0:T(8,128)(2,1)S(1)} %get-tuple-element.68), channel_id=1, source_target_pairs={{0,2},{1,3},{2,0},{3,1},{4,6},{5,7},{6,4},{7,5},{8,10},{9,11},{10,... | collective-permute-start | bytes 393224 | tf_op jit(solution)/shard_map/ppermute | solution.py:15
  66.3 1.6 %collective-permute-start.16 = (bf16[256,512]{1,0:T(8,128)(2,1)S(1)}, bf16[256,512]{1,0:T(8,128)(2,1)S(1)}, u32[]{:S(2)}, u32[]{:S(2)}) collective-permute-start(bf16[256,512]{1,0:T(8,128)(2,1)S(1)} %add_convert_fusion.2), channel_id=1, source_target_pairs={{0,8},{4,12},{8,0},{12,4},{16,24},{20,28},{24,16},{28,20},{1,9},{5... | collective-permute-start | bytes 786440 | tf_op jit(solution)/shard_map/ppermute | solution.py:15
  67.9 2.2 %copy-done.2 = bf16[8,256,1024]{2,1,0:T(8,128)(2,1)S(1)} copy-done((bf16[8,256,1024]{2,1,0:T(8,128)(2,1)S(1)}, bf16[8,256,1024]{2,1,0:T(8,128)(2,1)}, u32[]{:S(2)}) %copy-start.2) | copy-done | bytes 4194328
  70.9 1.3 %collective-permute-done.21 = bf16[128,512]{1,0:T(8,128)(2,1)S(1)} collective-permute-done((bf16[128,512]{1,0:T(8,128)(2,1)S(1)}, bf16[128,512]{1,0:T(8,128)(2,1)S(1)}, u32[]{:S(2)}, u32[]{:S(2)}) %collective-permute-start.21) | collective-permute-done | bytes 131104 | tf_op jit(solution)/shard_map/ppermute | solution.py:15
  72.3 1.5 %collective-permute-done.16 = bf16[256,512]{1,0:T(8,128)(2,1)S(1)} collective-permute-done((bf16[256,512]{1,0:T(8,128)(2,1)S(1)}, bf16[256,512]{1,0:T(8,128)(2,1)S(1)}, u32[]{:S(2)}, u32[]{:S(2)}) %collective-permute-start.16) | collective-permute-done | bytes 262176 | tf_op jit(solution)/shard_map/ppermute | solution.py:15
  76.0 1.7 %collective-permute-start.24 = (bf16[64,512]{1,0:T(8,128)(2,1)S(1)}, bf16[64,512]{1,0:T(8,128)(2,1)S(1)}, u32[]{:S(2)}, u32[]{:S(2)}) collective-permute-start(bf16[64,512]{1,0:T(8,128)(2,1)S(1)} %fusion), channel_id=1, source_target_pairs={{0,8},{4,12},{8,0},{12,4},{16,24},{20,28},{24,16},{28,20},{1,9},{5... | collective-permute-start | bytes 196616 | tf_op jit(solution)/shard_map/ppermute | solution.py:15
  77.7 3.3 %collective-permute-start.25 = (bf16[64,512]{1,0:T(8,128)(2,1)S(1)}, bf16[64,512]{1,0:T(8,128)(2,1)S(1)}, u32[]{:S(2)}, u32[]{:S(2)}) collective-permute-start(bf16[64,512]{1,0:T(8,128)(2,1)S(1)} %fusion), channel_id=1, source_target_pairs={{0,16},{4,20},{8,24},{12,28},{16,0},{20,4},{24,8},{28,12},{1,17},{... | collective-permute-start | bytes 196616 | tf_op jit(solution)/shard_map/ppermute | solution.py:15
  82.1 3.1 %collective-permute-done.25 = bf16[64,512]{1,0:T(8,128)(2,1)S(1)} collective-permute-done((bf16[64,512]{1,0:T(8,128)(2,1)S(1)}, bf16[64,512]{1,0:T(8,128)(2,1)S(1)}, u32[]{:S(2)}, u32[]{:S(2)}) %collective-permute-start.25) | collective-permute-done | bytes 65568 | tf_op jit(solution)/shard_map/ppermute | solution.py:15
  85.2 2.5 %collective-permute-done.26 = bf16[64,512]{1,0:T(8,128)(2,1)S(1)} collective-permute-done((bf16[64,512]{1,0:T(8,128)(2,1)S(1)}, bf16[64,512]{1,0:T(8,128)(2,1)S(1)}, u32[]{:S(2)}, u32[]{:S(2)}) %collective-permute-start.26) | collective-permute-done | bytes 65568 | tf_op jit(solution)/shard_map/ppermute | solution.py:15
  87.8 2.4 %collective-permute-start.29 = (f32[64,512]{1,0:T(8,128)S(1)}, f32[64,512]{1,0:T(8,128)S(1)}, u32[]{:S(2)}, u32[]{:S(2)}) collective-permute-start(f32[64,512]{1,0:T(8,128)S(1)} %get-tuple-element.72), channel_id=1, source_target_pairs={{0,3},{1,2},{2,1},{3,0},{4,7},{5,6},{6,5},{7,4},{8,11},{9,10},{10,... | collective-permute-start | bytes 393224 | tf_op jit(solution)/shard_map/ppermute | solution.py:15
  91.4 1.5 %collective-permute-start.19 = (bf16[256,512]{1,0:T(8,128)(2,1)S(1)}, bf16[256,512]{1,0:T(8,128)(2,1)S(1)}, u32[]{:S(2)}, u32[]{:S(2)}) collective-permute-start(bf16[256,512]{1,0:T(8,128)(2,1)S(1)} %add_convert_fusion.1), channel_id=1, source_target_pairs={{0,16},{4,20},{8,24},{12,28},{16,0},{20,4},{24,8},{28,12},{1,17},{... | collective-permute-start | bytes 786440 | tf_op jit(solution)/shard_map/ppermute | solution.py:15
  93.8 1.4 %collective-permute-done.27 = f32[64,512]{1,0:T(8,128)S(1)} collective-permute-done((f32[64,512]{1,0:T(8,128)S(1)}, f32[64,512]{1,0:T(8,128)S(1)}, u32[]{:S(2)}, u32[]{:S(2)}) %collective-permute-start.27) | collective-permute-done | bytes 131104 | tf_op jit(solution)/shard_map/ppermute | solution.py:15
  95.9 8.9 %collective-permute-done.19 = bf16[256,512]{1,0:T(8,128)(2,1)S(1)} collective-permute-done((bf16[256,512]{1,0:T(8,128)(2,1)S(1)}, bf16[256,512]{1,0:T(8,128)(2,1)S(1)}, u32[]{:S(2)}, u32[]{:S(2)}) %collective-permute-start.19) | collective-permute-done | bytes 262176 | tf_op jit(solution)/shard_map/ppermute | solution.py:15
  105.6 1.6 %gather_fusion = f32[8,64,512]{2,1,0:T(8,128)} fusion(f32[8,64,512]{2,1,0:T(8,128)S(1)} %constant_dynamic-update-slice_fusion, s32[1024]{0:T(1024)S(1)} %pad_clamp_fusion), kind=kCustom, calls=%fused_computation | custom fusion | bytes 2097184 | tf_op jit(solution)/shard_map/gather | solution.py:283
  (81 shorter events, 18.7 us)
Async XLA Ops:
  0.6 16.3 %collective-permute-start = (bf16[256,512]{1,0:T(8,128)(2,1)}, bf16[256,512]{1,0:T(8,128)(2,1)S(1)}, u32[]{:S(2)}, u32[]{:S(2)}) collective-permute-start(bf16[256,512]{1,0:T(8,128)(2,1)} %refs_1_.1), channel_id=1, source_target_pairs={{0,16},{4,20},{8,24},{12,28},{16,0},{20,4},{24,8},{28,12},{1,17},{... | collective-permute-start | bytes 786440 | tf_op jit(solution)/shard_map/ppermute | solution.py:15
  4.7 13.5 %collective-permute-start.4 = (bf16[256,512]{1,0:T(8,128)(2,1)}, bf16[256,512]{1,0:T(8,128)(2,1)S(1)}, u32[]{:S(2)}, u32[]{:S(2)}) collective-permute-start(bf16[256,512]{1,0:T(8,128)(2,1)} %refs_1_.1), channel_id=1, source_target_pairs={{0,8},{4,12},{8,0},{12,4},{16,24},{20,28},{24,16},{28,20},{1,9},{5... | collective-permute-start | bytes 786440 | tf_op jit(solution)/shard_map/ppermute | solution.py:15
  17.0 7.4 %collective-permute-start.1 = (bf16[256,512]{1,0:T(8,128)(2,1)S(1)}, bf16[256,512]{1,0:T(8,128)(2,1)S(1)}, u32[]{:S(2)}, u32[]{:S(2)}) collective-permute-start(bf16[256,512]{1,0:T(8,128)(2,1)S(1)} %collective-permute-done.refs_5_), channel_id=1, source_target_pairs={{0,8},{4,12},{8,0},{12,4},{16,24},{20,28},{24,16},{28,20},{1,9},{5... | collective-permute-start | bytes 786440 | tf_op jit(solution)/shard_map/ppermute | solution.py:15
  17.7 6.7 %collective-permute-start.3 = (bf16[256,512]{1,0:T(8,128)(2,1)S(1)}, bf16[256,512]{1,0:T(8,128)(2,1)S(1)}, u32[]{:S(2)}, u32[]{:S(2)}) collective-permute-start(bf16[256,512]{1,0:T(8,128)(2,1)S(1)} %copy-done.8), channel_id=1, source_target_pairs={{0,4},{4,0},{8,12},{12,8},{16,20},{20,16},{24,28},{28,24},{1,5},{5... | collective-permute-start | bytes 786440 | tf_op jit(solution)/shard_map/ppermute | solution.py:15
  17.7 6.7 %collective-permute-start.6 = (bf16[256,512]{1,0:T(8,128)(2,1)S(1)}, bf16[256,512]{1,0:T(8,128)(2,1)S(1)}, u32[]{:S(2)}, u32[]{:S(2)}) collective-permute-start(bf16[256,512]{1,0:T(8,128)(2,1)S(1)} %collective-permute-done.refs_5_), channel_id=1, source_target_pairs={{0,4},{4,0},{8,12},{12,8},{16,20},{20,16},{24,28},{28,24},{1,5},{5... | collective-permute-start | bytes 786440 | tf_op jit(solution)/shard_map/ppermute | solution.py:15
  18.2 6.2 %collective-permute-start.5 = (bf16[256,512]{1,0:T(8,128)(2,1)S(1)}, bf16[256,512]{1,0:T(8,128)(2,1)S(1)}, u32[]{:S(2)}, u32[]{:S(2)}) collective-permute-start(bf16[256,512]{1,0:T(8,128)(2,1)S(1)} %collective-permute-done.4.refs_3_), channel_id=1, source_target_pairs={{0,4},{4,0},{8,12},{12,8},{16,20},{20,16},{24,28},{28,24},{1,5},{5... | collective-permute-start | bytes 786440 | tf_op jit(solution)/shard_map/ppermute | solution.py:15
  24.4 1.8 %collective-permute-start.2 = (bf16[256,512]{1,0:T(8,128)(2,1)S(1)}, bf16[256,512]{1,0:T(8,128)(2,1)S(1)}, u32[]{:S(2)}, u32[]{:S(2)}) collective-permute-start(bf16[256,512]{1,0:T(8,128)(2,1)S(1)} %collective-permute-done.1.refs_1_), channel_id=1, source_target_pairs={{0,4},{4,0},{8,12},{12,8},{16,20},{20,16},{24,28},{28,24},{1,5},{5... | collective-permute-start | bytes 786440 | tf_op jit(solution)/shard_map/ppermute | solution.py:15
  26.9 10.1 %collective-permute-start.9 = (bf16[256,512]{1,0:T(8,128)(2,1)S(1)}, bf16[256,512]{1,0:T(8,128)(2,1)S(1)}, u32[]{:S(2)}, u32[]{:S(2)}) collective-permute-start(bf16[256,512]{1,0:T(8,128)(2,1)S(1)} %get-tuple-element.45), channel_id=1, source_target_pairs={{0,3},{1,2},{2,1},{3,0},{4,7},{5,6},{6,5},{7,4},{8,11},{9,10},{10,... | collective-permute-start | bytes 786440 | tf_op jit(solution)/shard_map/ppermute | solution.py:15
  29.2 12.9 %collective-permute-start.7 = (bf16[256,512]{1,0:T(8,128)(2,1)S(1)}, bf16[256,512]{1,0:T(8,128)(2,1)S(1)}, u32[]{:S(2)}, u32[]{:S(2)}) collective-permute-start(bf16[256,512]{1,0:T(8,128)(2,1)S(1)} %get-tuple-element.43), channel_id=1, source_target_pairs={{0,1},{1,0},{2,3},{3,2},{4,5},{5,4},{6,7},{7,6},{8,9},{9,8},{10,11... | collective-permute-start | bytes 786440 | tf_op jit(solution)/shard_map/ppermute | solution.py:15
  29.8 12.5 %collective-permute-start.8 = (bf16[256,512]{1,0:T(8,128)(2,1)S(1)}, bf16[256,512]{1,0:T(8,128)(2,1)S(1)}, u32[]{:S(2)}, u32[]{:S(2)}) collective-permute-start(bf16[256,512]{1,0:T(8,128)(2,1)S(1)} %get-tuple-element.44), channel_id=1, source_target_pairs={{0,2},{1,3},{2,0},{3,1},{4,6},{5,7},{6,4},{7,5},{8,10},{9,11},{10,... | collective-permute-start | bytes 786440 | tf_op jit(solution)/shard_map/ppermute | solution.py:15
  30.5 11.7 %copy-start.6 = (bf16[256,512]{1,0:T(8,128)(2,1)S(1)}, bf16[256,512]{1,0:T(8,128)(2,1)}, u32[]{:S(2)}) copy-start(bf16[256,512]{1,0:T(8,128)(2,1)} %refs_4_.1) | copy-start | bytes 786436
  43.4 10.1 %collective-permute-start.12 = (bf16[256,512]{1,0:T(8,128)(2,1)S(1)}, bf16[256,512]{1,0:T(8,128)(2,1)S(1)}, u32[]{:S(2)}, u32[]{:S(2)}) collective-permute-start(bf16[256,512]{1,0:T(8,128)(2,1)S(1)} %get-tuple-element.49.refs_1_), channel_id=1, source_target_pairs={{0,3},{1,2},{2,1},{3,0},{4,7},{5,6},{6,5},{7,4},{8,11},{9,10},{10,... | collective-permute-start | bytes 786440 | tf_op jit(solution)/shard_map/ppermute | solution.py:15
  45.6 12.4 %collective-permute-start.10 = (bf16[256,512]{1,0:T(8,128)(2,1)S(1)}, bf16[256,512]{1,0:T(8,128)(2,1)S(1)}, u32[]{:S(2)}, u32[]{:S(2)}) collective-permute-start(bf16[256,512]{1,0:T(8,128)(2,1)S(1)} %get-tuple-element.49.refs_1_), channel_id=1, source_target_pairs={{0,1},{1,0},{2,3},{3,2},{4,5},{5,4},{6,7},{7,6},{8,9},{9,8},{10,11... | collective-permute-start | bytes 786440 | tf_op jit(solution)/shard_map/ppermute | solution.py:15
  46.2 12.0 %collective-permute-start.11 = (bf16[256,512]{1,0:T(8,128)(2,1)S(1)}, bf16[256,512]{1,0:T(8,128)(2,1)S(1)}, u32[]{:S(2)}, u32[]{:S(2)}) collective-permute-start(bf16[256,512]{1,0:T(8,128)(2,1)S(1)} %get-tuple-element.49.refs_1_), channel_id=1, source_target_pairs={{0,2},{1,3},{2,0},{3,1},{4,6},{5,7},{6,4},{7,5},{8,10},{9,11},{10,... | collective-permute-start | bytes 786440 | tf_op jit(solution)/shard_map/ppermute | solution.py:15
  61.0 1.6 %collective-permute-start.15 = (bf16[256,512]{1,0:T(8,128)(2,1)S(1)}, bf16[256,512]{1,0:T(8,128)(2,1)S(1)}, u32[]{:S(2)}, u32[]{:S(2)}) collective-permute-start(bf16[256,512]{1,0:T(8,128)(2,1)S(1)} %get-tuple-element.62), channel_id=1, source_target_pairs={{0,4},{4,0},{8,12},{12,8},{16,20},{20,16},{24,28},{28,24},{1,5},{5... | collective-permute-start | bytes 786440 | tf_op jit(solution)/shard_map/ppermute | solution.py:15
  62.7 8.2 %collective-permute-start.20 = (bf16[128,512]{1,0:T(8,128)(2,1)S(1)}, bf16[128,512]{1,0:T(8,128)(2,1)S(1)}, u32[]{:S(2)}, u32[]{:S(2)}) collective-permute-start(bf16[128,512]{1,0:T(8,128)(2,1)S(1)} %get-tuple-element.67), channel_id=1, source_target_pairs={{0,1},{1,0},{2,3},{3,2},{4,5},{5,4},{6,7},{7,6},{8,9},{9,8},{10,11... | collective-permute-start | bytes 393224 | tf_op jit(solution)/shard_map/ppermute | solution.py:15
  64.2 8.1 %collective-permute-start.21 = (bf16[128,512]{1,0:T(8,128)(2,1)S(1)}, bf16[128,512]{1,0:T(8,128)(2,1)S(1)}, u32[]{:S(2)}, u32[]{:S(2)}) collective-permute-start(bf16[128,512]{1,0:T(8,128)(2,1)S(1)} %get-tuple-element.68), channel_id=1, source_target_pairs={{0,2},{1,3},{2,0},{3,1},{4,6},{5,7},{6,4},{7,5},{8,10},{9,11},{10,... | collective-permute-start | bytes 393224 | tf_op jit(solution)/shard_map/ppermute | solution.py:15
  65.6 6.7 %collective-permute-start.22 = (bf16[128,512]{1,0:T(8,128)(2,1)S(1)}, bf16[128,512]{1,0:T(8,128)(2,1)S(1)}, u32[]{:S(2)}, u32[]{:S(2)}) collective-permute-start(bf16[128,512]{1,0:T(8,128)(2,1)S(1)} %get-tuple-element.69), channel_id=1, source_target_pairs={{0,3},{1,2},{2,1},{3,0},{4,7},{5,6},{6,5},{7,4},{8,11},{9,10},{10,... | collective-permute-start | bytes 393224 | tf_op jit(solution)/shard_map/ppermute | solution.py:15
  66.3 7.5 %collective-permute-start.16 = (bf16[256,512]{1,0:T(8,128)(2,1)S(1)}, bf16[256,512]{1,0:T(8,128)(2,1)S(1)}, u32[]{:S(2)}, u32[]{:S(2)}) collective-permute-start(bf16[256,512]{1,0:T(8,128)(2,1)S(1)} %add_convert_fusion.2), channel_id=1, source_target_pairs={{0,8},{4,12},{8,0},{12,4},{16,24},{20,28},{24,16},{28,20},{1,9},{5... | collective-permute-start | bytes 786440 | tf_op jit(solution)/shard_map/ppermute | solution.py:15
  70.8 25.1 %collective-permute-start.13 = (bf16[256,512]{1,0:T(8,128)(2,1)S(1)}, bf16[256,512]{1,0:T(8,128)(2,1)S(1)}, u32[]{:S(2)}, u32[]{:S(2)}) collective-permute-start(bf16[256,512]{1,0:T(8,128)(2,1)S(1)} %get-tuple-element.58), channel_id=1, source_target_pairs={{0,4},{4,0},{8,12},{12,8},{16,20},{20,16},{24,28},{28,24},{1,5},{5... | collective-permute-start | bytes 786440 | tf_op jit(solution)/shard_map/ppermute | solution.py:15
  73.8 2.1 %collective-permute-start.23 = (bf16[64,512]{1,0:T(8,128)(2,1)S(1)}, bf16[64,512]{1,0:T(8,128)(2,1)S(1)}, u32[]{:S(2)}, u32[]{:S(2)}) collective-permute-start(bf16[64,512]{1,0:T(8,128)(2,1)S(1)} %fusion.1), channel_id=1, source_target_pairs={{0,4},{4,0},{8,12},{12,8},{16,20},{20,16},{24,28},{28,24},{1,5},{5... | collective-permute-start | bytes 196616 | tf_op jit(solution)/shard_map/ppermute | solution.py:15
  74.6 6.3 %collective-permute-start.14 = (bf16[256,512]{1,0:T(8,128)(2,1)S(1)}, bf16[256,512]{1,0:T(8,128)(2,1)S(1)}, u32[]{:S(2)}, u32[]{:S(2)}) collective-permute-start(bf16[256,512]{1,0:T(8,128)(2,1)S(1)} %get-tuple-element.60), channel_id=1, source_target_pairs={{0,4},{4,0},{8,12},{12,8},{16,20},{20,16},{24,28},{28,24},{1,5},{5... | collective-permute-start | bytes 786440 | tf_op jit(solution)/shard_map/ppermute | solution.py:15
  75.9 14.8 %collective-permute-start.18 = (bf16[256,512]{1,0:T(8,128)(2,1)S(1)}, bf16[256,512]{1,0:T(8,128)(2,1)S(1)}, u32[]{:S(2)}, u32[]{:S(2)}) collective-permute-start(bf16[256,512]{1,0:T(8,128)(2,1)S(1)} %get-tuple-element.65), channel_id=1, source_target_pairs={{0,4},{4,0},{8,12},{12,8},{16,20},{20,16},{24,28},{28,24},{1,5},{5... | collective-permute-start | bytes 786440 | tf_op jit(solution)/shard_map/ppermute | solution.py:15
  76.0 5.1 %collective-permute-start.24 = (bf16[64,512]{1,0:T(8,128)(2,1)S(1)}, bf16[64,512]{1,0:T(8,128)(2,1)S(1)}, u32[]{:S(2)}, u32[]{:S(2)}) collective-permute-start(bf16[64,512]{1,0:T(8,128)(2,1)S(1)} %fusion), channel_id=1, source_target_pairs={{0,8},{4,12},{8,0},{12,4},{16,24},{20,28},{24,16},{28,20},{1,9},{5... | collective-permute-start | bytes 196616 | tf_op jit(solution)/shard_map/ppermute | solution.py:15
  77.7 7.5 %collective-permute-start.25 = (bf16[64,512]{1,0:T(8,128)(2,1)S(1)}, bf16[64,512]{1,0:T(8,128)(2,1)S(1)}, u32[]{:S(2)}, u32[]{:S(2)}) collective-permute-start(bf16[64,512]{1,0:T(8,128)(2,1)S(1)} %fusion), channel_id=1, source_target_pairs={{0,16},{4,20},{8,24},{12,28},{16,0},{20,4},{24,8},{28,12},{1,17},{... | collective-permute-start | bytes 196616 | tf_op jit(solution)/shard_map/ppermute | solution.py:15
  80.9 6.8 %collective-permute-start.26 = (bf16[64,512]{1,0:T(8,128)(2,1)S(1)}, bf16[64,512]{1,0:T(8,128)(2,1)S(1)}, u32[]{:S(2)}, u32[]{:S(2)}) collective-permute-start(bf16[64,512]{1,0:T(8,128)(2,1)S(1)} %fusion), channel_id=1, source_target_pairs={{0,24},{4,28},{8,16},{12,20},{16,8},{20,12},{24,0},{28,4},{1,25},{... | collective-permute-start | bytes 196616 | tf_op jit(solution)/shard_map/ppermute | solution.py:15
  81.0 10.4 %collective-permute-start.17 = (bf16[256,512]{1,0:T(8,128)(2,1)S(1)}, bf16[256,512]{1,0:T(8,128)(2,1)S(1)}, u32[]{:S(2)}, u32[]{:S(2)}) collective-permute-start(bf16[256,512]{1,0:T(8,128)(2,1)S(1)} %add_convert_fusion.3), channel_id=1, source_target_pairs={{0,8},{4,12},{8,0},{12,4},{16,24},{20,28},{24,16},{28,20},{1,9},{5... | collective-permute-start | bytes 786440 | tf_op jit(solution)/shard_map/ppermute | solution.py:15
  87.8 6.0 %collective-permute-start.29 = (f32[64,512]{1,0:T(8,128)S(1)}, f32[64,512]{1,0:T(8,128)S(1)}, u32[]{:S(2)}, u32[]{:S(2)}) collective-permute-start(f32[64,512]{1,0:T(8,128)S(1)} %get-tuple-element.72), channel_id=1, source_target_pairs={{0,3},{1,2},{2,1},{3,0},{4,7},{5,6},{6,5},{7,4},{8,11},{9,10},{10,... | collective-permute-start | bytes 393224 | tf_op jit(solution)/shard_map/ppermute | solution.py:15
  90.2 5.0 %collective-permute-start.27 = (f32[64,512]{1,0:T(8,128)S(1)}, f32[64,512]{1,0:T(8,128)S(1)}, u32[]{:S(2)}, u32[]{:S(2)}) collective-permute-start(f32[64,512]{1,0:T(8,128)S(1)} %get-tuple-element.72), channel_id=1, source_target_pairs={{0,1},{1,0},{2,3},{3,2},{4,5},{5,4},{6,7},{7,6},{8,9},{9,8},{10,11... | collective-permute-start | bytes 393224 | tf_op jit(solution)/shard_map/ppermute | solution.py:15
  90.7 5.0 %collective-permute-start.28 = (f32[64,512]{1,0:T(8,128)S(1)}, f32[64,512]{1,0:T(8,128)S(1)}, u32[]{:S(2)}, u32[]{:S(2)}) collective-permute-start(f32[64,512]{1,0:T(8,128)S(1)} %get-tuple-element.72), channel_id=1, source_target_pairs={{0,2},{1,3},{2,0},{3,1},{4,6},{5,7},{6,4},{7,5},{8,10},{9,11},{10,... | collective-permute-start | bytes 393224 | tf_op jit(solution)/shard_map/ppermute | solution.py:15
  91.4 13.3 %collective-permute-start.19 = (bf16[256,512]{1,0:T(8,128)(2,1)S(1)}, bf16[256,512]{1,0:T(8,128)(2,1)S(1)}, u32[]{:S(2)}, u32[]{:S(2)}) collective-permute-start(bf16[256,512]{1,0:T(8,128)(2,1)S(1)} %add_convert_fusion.1), channel_id=1, source_target_pairs={{0,16},{4,20},{8,24},{12,28},{16,0},{20,4},{24,8},{28,12},{1,17},{... | collective-permute-start | bytes 786440 | tf_op jit(solution)/shard_map/ppermute | solution.py:15
  95.7 9.9 %collective-permute-start.30 = (f32[4,64,512]{2,1,0:T(8,128)S(1)}, f32[4,64,512]{2,1,0:T(8,128)S(1)}, u32[]{:S(2)}, u32[]{:S(2)}) collective-permute-start(f32[4,64,512]{2,1,0:T(8,128)S(1)} %pad_maximum_fusion), channel_id=1, source_target_pairs={{0,4},{4,0},{8,12},{12,8},{16,20},{20,16},{24,28},{28,24},{1,5},{5... | collective-permute-start | bytes 1572872 | tf_op jit(solution)/shard_map/ppermute | solution.py:15
  (8 other events, 31.7 us)

commit v3 on v2

v3 whole, which is shorter than its diff:
```python
import functools

import jax
import jax.numpy as jnp
from jax import lax
from jax.experimental import pallas as pl
from jax.experimental.pallas import tpu as pltpu
from jax.sharding import PartitionSpec as P

WHOLE = pl.BlockSpec(memory_space=pltpu.VMEM)
SCALARS = pl.BlockSpec(memory_space=pltpu.SMEM)
CHUNKS = 2


def exchange(x, axis, mask):
    return lax.ppermute(x, axis, [(i, i ^ mask) for i in range(lax.axis_size(axis))])


def after(x, *others):
    return lax.optimization_barrier((x, *others))[0]


def params(mib):
    return pltpu.CompilerParams(vmem_limit_bytes=mib * 1024 * 1024)


def like(shape, dtype):
    return jax.ShapeDtypeStruct(shape, dtype)


def bf16_dot(a, b):
    return jnp.dot(a, b, preferred_element_type=jnp.float32)


def densify_kernel(rows_ref, cols_ref, counts_ref, place_ref, tiles_ref, a_ref, acc_ref, *, col_tiles, slots):
    step = pl.program_id(0)
    column = step ^ place_ref[0]
    member = place_ref[1]
    size = tiles_ref.shape[-1]
    acc_ref[...] = jnp.zeros_like(acc_ref)

    def add(slot, carry):
        row = rows_ref[column * slots + slot]
        row = ((row // col_tiles) ^ member) * col_tiles + lax.rem(row, col_tiles)
        spot = row * col_tiles + cols_ref[column * slots + slot]
        acc_ref[spot] += tiles_ref[0, slot].astype(jnp.float32)
        return carry

    lax.fori_loop(0, counts_ref[column], add, 0)
    for spot in range(acc_ref.shape[0]):
        row, col = spot // col_tiles, spot % col_tiles
        a_ref[0, row * size:(row + 1) * size, col * size:(col + 1) * size] = acc_ref[spot].astype(a_ref.dtype)


def densify(tiles, tile_rows, tile_cols, tile_counts, place, group_count, rows_local):
    columns, slots, size, _ = tiles.shape
    col_tiles = rows_local // size
    rows = group_count * rows_local
    return pl.pallas_call(
        functools.partial(densify_kernel, col_tiles=col_tiles, slots=slots),
        out_shape=like((columns, rows, rows_local), jnp.bfloat16),
        grid_spec=pltpu.PrefetchScalarGridSpec(
            num_scalar_prefetch=4,
            grid=(columns,),
            in_specs=[pl.BlockSpec((1, slots, size, size), lambda j, r, c, n, p: (j ^ p[0], 0, 0, 0))],
            out_specs=pl.BlockSpec((1, rows, rows_local), lambda j, r, c, n, p: (j, 0, 0)),
            scratch_shapes=[pltpu.VMEM((group_count * col_tiles * col_tiles, size, size), jnp.float32)],
        ),
        compiler_params=params(12),
        cost_estimate=pl.CostEstimate(
            flops=columns * slots * size * size, bytes_accessed=8 * rows * columns * rows_local, transcendentals=0),
        name="densify",
    )(tile_rows.reshape(-1), tile_cols.reshape(-1), tile_counts.reshape(-1), place, tiles)


def transpose_kernel(a_ref, *outs):
    for pair, out_ref in enumerate(outs):
        for side in range(2):
            out_ref[side] = a_ref[2 * pair + side].T


def transposed(dense):
    columns, rows, cols = dense.shape
    return pl.pallas_call(
        transpose_kernel,
        out_shape=[like((2, cols, rows), jnp.bfloat16)] * (columns // 2),
        in_specs=[WHOLE],
        out_specs=[WHOLE] * (columns // 2),
        compiler_params=params(8),
        cost_estimate=pl.CostEstimate(flops=0, bytes_accessed=4 * columns * rows * cols, transcendentals=0),
        name="transposed",
    )(dense)


def forward_kernel(*refs, which, starts, groups, has_prev):
    dense_ref, sources, rest = refs[0], refs[1:1 + len(which)], refs[1 + len(which):]
    prev = rest[:groups] if has_prev else None
    outs = rest[groups if has_prev else 0:]
    rows, width = outs[0].shape
    for k in range(groups):
        total = prev[k][...] if has_prev else None
        for j, start, source in zip(which, starts, sources):
            part = bf16_dot(dense_ref[j, k * rows:(k + 1) * rows, :], source[:, start:start + width])
            total = part if total is None else total + part
        outs[k][...] = total.astype(outs[k].dtype)


def forward(dense, which, sources, start, width, prev, dtypes):
    groups = len(dtypes)
    rows = sources[0].shape[0]
    starts = [0 if source.shape[1] == width else start for source in sources]
    return pl.pallas_call(
        functools.partial(forward_kernel, which=which, starts=starts, groups=groups, has_prev=prev is not None),
        out_shape=[like((rows, width), dtype) for dtype in dtypes],
        in_specs=[WHOLE] * (1 + len(which) + (groups if prev is not None else 0)),
        out_specs=[WHOLE] * groups,
        compiler_params=params(8),
        cost_estimate=pl.CostEstimate(
            flops=2 * len(which) * groups * rows * rows * width,
            bytes_accessed=2 * len(which) * groups * rows * rows + 4 * groups * rows * width, transcendentals=0),
        name="forward",
    )(dense, *sources, *(prev or []))


def middle_kernel(*refs, chunks, groups):
    pieces = refs[:chunks * groups]
    cot_ref, weight_ref = refs[chunks * groups:chunks * groups + 2]
    act_ref, agg_ref, pre_grad_ref = refs[chunks * groups + 2:chunks * groups + 5]
    grads = refs[chunks * groups + 5:]
    part = grads[0].shape[1]
    for c in range(chunks):
        agg = pieces[c * groups][...]
        for k in range(1, groups):
            agg = agg + pieces[c * groups + k][...].astype(jnp.float32)
        agg_ref[:, c * part:(c + 1) * part] = agg.astype(jnp.bfloat16)
    weight = weight_ref[...]
    preact = bf16_dot(agg_ref[...], weight)
    sigma = jax.nn.sigmoid(preact)
    act_ref[...] = (preact * sigma).astype(act_ref.dtype)
    slope = sigma * (1.0 + preact * (1.0 - sigma))
    pre_grad = (cot_ref[...].astype(jnp.float32) * slope).astype(jnp.bfloat16)
    pre_grad_ref[...] = pre_grad
    for c in range(chunks):
        grads[c][...] = lax.dot_general(
            pre_grad, weight_ref[c * part:(c + 1) * part, :], (((1,), (1,)), ((), ())),
            preferred_element_type=jnp.float32,
        ).astype(jnp.bfloat16)


def middle(pieces, cotangent, weight):
    rows, width = cotangent.shape
    chunks = len(pieces)
    whole = like((rows, width), jnp.bfloat16)
    return pl.pallas_call(
        functools.partial(middle_kernel, chunks=chunks, groups=len(pieces[0])),
        out_shape=[whole] * 3 + [like((rows, width // chunks), jnp.bfloat16)] * chunks,
        in_specs=[WHOLE] * (2 + chunks * len(pieces[0])),
        out_specs=[WHOLE] * (3 + chunks),
        compiler_params=params(8),
        cost_estimate=pl.CostEstimate(
            flops=4 * rows * width * width, bytes_accessed=10 * rows * width, transcendentals=rows * width),
        name="middle",
    )(*[piece for chunk in pieces for piece in chunk], cotangent, weight)


def weight_kernel(place_ref, agg_ref, pre_grad_ref, own_ref, send_ref, part_ref):
    core, member = lax.rem(place_ref[0], 2), place_ref[1]
    groups, rows, _ = own_ref.shape
    part_ref[...] = lax.dot_general(
        agg_ref[...], pre_grad_ref[...], (((0,), (0,)), ((), ())), preferred_element_type=jnp.float32
    )
    for k in range(groups):
        for side, out_ref in ((core, own_ref), (1 - core, send_ref)):
            start = ((member ^ k) * 2 + side) * rows
            out_ref[k] = part_ref[pl.ds(pl.multiple_of(start, rows), rows), :].astype(out_ref.dtype)


def weight_part(agg, pre_grad, place, groups):
    rows, width = agg.shape
    part = (groups, width // (2 * groups), width)
    return pl.pallas_call(
        weight_kernel,
        out_shape=[like(part, jnp.float32), like(part, jnp.bfloat16)],
        in_specs=[SCALARS, WHOLE, WHOLE],
        out_specs=[WHOLE] * 2,
        scratch_shapes=[pltpu.VMEM((width, width), jnp.float32)],
        compiler_params=params(8),
        cost_estimate=pl.CostEstimate(
            flops=2 * rows * width * width, bytes_accessed=4 * rows * width + 4 * width * width, transcendentals=0),
        name="weight_part",
    )(place, agg, pre_grad)


def place_kernel(place_ref, *refs, groups):
    mine, other_ref, out_ref = refs[:groups], refs[groups], refs[groups + 1]
    core, member = lax.rem(place_ref[0], 2), place_ref[1]
    rows = mine[0].shape[0]
    for k in range(groups):
        for side, value in ((core, mine[k][...]), (1 - core, other_ref[k * rows:(k + 1) * rows, :])):
            start = ((member ^ k) * 2 + side) * rows
            out_ref[pl.ds(pl.multiple_of(start, rows), rows), :] = value


def place_slices(mine, other, place):
    groups = len(mine)
    rows, width = mine[0].shape
    return pl.pallas_call(
        functools.partial(place_kernel, groups=groups),
        out_shape=like((2 * groups * rows, width), jnp.float32),
        in_specs=[SCALARS] + [WHOLE] * (groups + 1),
        out_specs=WHOLE,
        compiler_params=params(8),
        cost_estimate=pl.CostEstimate(flops=0, bytes_accessed=16 * groups * rows * width, transcendentals=0),
        name="place_slices",
    )(place, *mine, other)


def backward_kernel(*refs, count, groups):
    blocks, grads = refs[:count], refs[count:count + groups]
    owns, other_ref = refs[count + groups:-1], refs[-1]
    rows = grads[0].shape[0]
    for pair in range(count):
        for side in (1, 0):
            total = None
            for k in range(groups):
                part = bf16_dot(blocks[pair][side, :, k * rows:(k + 1) * rows], grads[k][...])
                total = part if total is None else total + part
            if side == 0:
                owns[pair][...] = total
            else:
                size = total.shape[0]
                other_ref[pair * size:(pair + 1) * size, :] = total.astype(other_ref.dtype)


def backward(blocks, grads):
    _, cols, rows = blocks[0].shape
    width = grads[0].shape[1]
    count = len(blocks)
    out = pl.pallas_call(
        functools.partial(backward_kernel, count=count, groups=len(grads)),
        out_shape=[like((cols, width), jnp.float32)] * count + [like((count * cols, width), jnp.bfloat16)],
        in_specs=[WHOLE] * (count + len(grads)),
        out_specs=[WHOLE] * (count + 1),
        compiler_params=params(8),
        cost_estimate=pl.CostEstimate(
            flops=4 * count * cols * rows * width,
            bytes_accessed=4 * count * cols * rows + 2 * rows * width + 6 * count * cols * width, transcendentals=0),
        name="backward",
    )(*blocks, *grads)
    return out[:-1], out[-1]


def local(features, cotangent, weight, tiles, tile_rows, tile_cols, tile_counts):
    blocks = lax.axis_size("dom")
    groups = lax.axis_size("repl")
    pairs = blocks // 2
    rows_local, width = features.shape
    part_width = width // CHUNKS
    scale = float(rows_local * blocks * groups) ** (-0.5)
    position, member = lax.axis_index("dom"), lax.axis_index("repl")
    place = jnp.stack([position, member]).astype(jnp.int32)

    dense = densify(tiles[0, 0], tile_rows, tile_cols, tile_counts, place, groups, rows_local)

    top = pairs // 2
    near = {0: features}
    bit = top // 2
    while bit:
        for pair in list(near):
            near[pair + bit] = exchange(near[pair], "dom", 2 * bit)
        bit //= 2
    near = {pair: (near[pair], exchange(near[pair], "dom", 1)) for pair in near}
    fronts = []
    for c in range(CHUNKS):
        given = features[:, c * part_width:(c + 1) * part_width]
        fronts.append(exchange(given, "dom", 2 * top))
    pieces, arrived = [], []
    for c in range(CHUNKS):
        ready = [far[pairs - 1][0]] if c else [dense]
        far = {top: fronts[c]}
        bit = top // 2
        while bit:
            for pair in list(far):
                far[pair + bit] = exchange(after(far[pair], *ready), "dom", 2 * bit)
            bit //= 2
        if c:
            far[pairs - 1] = after(far[pairs - 1], *pieces[-1])
        far = {pair: (far[pair], exchange(far[pair], "dom", 1)) for pair in far}
        sources = {**near, **far}
        order = list(range(pairs - 1))
        totals = forward(
            dense, [2 * pair + side for pair in order for side in range(2)],
            [sources[pair][side] for pair in order for side in range(2)],
            c * part_width, part_width, None, [jnp.float32] * groups)
        out = forward(
            dense, [2 * pairs - 2, 2 * pairs - 1], list(sources[pairs - 1]), c * part_width, part_width, totals,
            [jnp.float32] + [jnp.bfloat16] * (groups - 1))
        pieces.append(out)
        arrived.append([exchange(out[k], "repl", k) for k in range(1, groups)])
    dense_t = transposed(after(dense, *pieces[-1], *arrived[0]))
    arrived[-1][-1] = after(arrived[-1][-1], *dense_t)

    out = middle([[out[0]] + got for out, got in zip(pieces, arrived)], cotangent, weight)
    activated, agg, pre_grad = out[:3]
    share, share_send = weight_part(agg, pre_grad, place, groups)
    share = share + exchange(share_send, "dom", 1).astype(jnp.float32)

    columns, mark = [], None
    for c in range(CHUNKS):
        grad = out[3 + c] if mark is None else after(out[3 + c], mark)
        grads = [grad] + [exchange(grad, "repl", k) for k in range(1, groups)]
        if c == 0:
            share = after(share, grads[-1])
            part = share[0]
            for k in range(1, groups):
                part = part + exchange(share[k].astype(jnp.bfloat16), "repl", k).astype(jnp.float32)
            part = part.astype(jnp.bfloat16)
        else:
            grads[-1] = after(grads[-1], follow)
        owns, others = {}, {}
        (owns[pairs - 1],), other_top = backward(dense_t[-1:], grads)
        mark = other_top
        rest, other = backward(dense_t[:-1], grads)
        others[pairs - 1] = exchange(other_top, "dom", 1)
        other = exchange(other, "dom", 1)
        for pair in range(pairs - 1):
            owns[pair] = rest[pair]
            others[pair] = other[pair * rows_local:(pair + 1) * rows_local]
        sums = {pair: owns[pair] + others[pair].astype(jnp.float32) for pair in owns}
        bit, last = 1, None
        while bit < pairs:
            for pair in sorted(sums, reverse=True):
                if not pair & bit:
                    continue
                given = sums.pop(pair).astype(jnp.bfloat16)
                first = pair == max([pair, *sums])
                if c == 0 and first:
                    given = jnp.concatenate([given] + [part[:, i * part_width:(i + 1) * part_width] for i in range(CHUNKS)])
                if c and first and bit == 1:
                    given = after(given, second)
                if c == 0:
                    if bit == 1 and first:
                        follow = given
                    elif bit > 1 and first:
                        second = given
                if last is not None and not first:
                    given = after(given, last)
                got = exchange(given, "dom", 2 * bit)
                if c == 0 and first:
                    high = part.shape[0]
                    got, slices = got[:rows_local], got[rows_local:]
                    slices = jnp.concatenate([slices[i * high:(i + 1) * high] for i in range(CHUNKS)], axis=1)
                    part = part.astype(jnp.float32) + slices.astype(jnp.float32)
                    if 2 * bit < pairs:
                        part = part.astype(jnp.bfloat16)
                last = got
                sums[pair ^ bit] = sums[pair ^ bit] + got.astype(jnp.float32)
            bit *= 2
        columns.append(sums[0].astype(jnp.bfloat16))
    feature_grad = jnp.concatenate(columns, axis=1)

    part = part * scale
    mine = [part] + [exchange(part, "repl", k) for k in range(1, groups)]
    other = exchange(jnp.concatenate(mine), "dom", 1)
    weight_grad = place_slices(mine, other, place)
    return (activated, feature_grad, weight_grad)


def solution(mesh):
    in_specs = (
        P(("dom", "repl"), None),
        P(("dom", "repl"), None),
        P(),
        P("dom", "repl", None, None, None, None),
        P("dom", "repl", None, None),
        P("dom", "repl", None, None),
        P("dom", "repl", None),
    )
    out_specs = (P(("dom", "repl"), None), P(("dom", "repl"), None), P())
    return jax.shard_map(local, mesh=mesh, in_specs=in_specs, out_specs=out_specs, check_vma=False)
```

time: 108 us -> 111 us (1.028)
  local copies, waits for them, and re-layouts: 12.5 us -> 5.42 us
  starting transfers between devices: 31.2 us -> 36.6 us
  waiting for transfers between devices: 48.1 us -> 52.2 us
    unnamed x21 -> x10, local copies, waits for them, and re-layouts: 9.23 us -> 2.86 us
    ppermute x31 -> x41, starting transfers between devices: 31.2 us -> 36.6 us  [exchange(): lax.ppermute(x, axis, [(i, i ^ mask) for i in range(lax.axis_size(axis))])]
    ppermute x31 -> x41, waiting for transfers between devices: 48.1 us -> 52.2 us  [exchange(): lax.ppermute(x, axis, [(i, i ^ mask) for i in range(lax.axis_size(axis))])]
    gather x1 -> x0, local copies, waits for them, and re-layouts: 1.59 us -> none  [local(): weight_grad = both[order].reshape(weight.shape)]
    pallas_call x9 -> x12, Pallas kernels: 8.96 us -> 10.5 us  [the longest x4 2.82 us: backward(): pl.pallas_call(functools.partial(backward_kernel, count=count, groups=len...]
  transfers between devices with their start and end apart: 31 -> 41, of which waited for: 17 -> 19; matrix products, arithmetic and copies ran while one was open for 3% -> 4% of each run, Pallas kernels for 10% -> 9%
where the time goes in v3:
time: 111 us; the launch traced here: 110 us
  waiting for transfers between devices  52.2 us (47%)
  starting transfers between devices  36.6 us (33%)
  Pallas kernels  13.7 us (12%)
  local copies, waits for them, and re-layouts  5.42 us (5%)
  other arithmetic  1.37 us (1%)
    ppermute x41, waiting for transfers between devices, exchange(): lax.ppermute(x, axis, [(i, i ^ mask) for i in range(lax.axis_size(axis))])  52.2 us
    ppermute x41, starting transfers between devices, exchange(): lax.ppermute(x, axis, [(i, i ^ mask) for i in range(lax.axis_size(axis))])  36.6 us
    pallas_call x1, Pallas kernels, densify(): pl.pallas_call(functools.partial(densify_kernel, col_tiles=col_tiles, slo...  3.2 us
    unnamed x10, local copies, waits for them, and re-layouts  2.86 us
    pallas_call x4, Pallas kernels, backward(): pl.pallas_call(functools.partial(backward_kernel, count=count, groups=len...  2.82 us
    pallas_call x4, Pallas kernels, forward(): pl.pallas_call(functools.partial(forward_kernel, which=which, starts=star...  2.82 us
  transfers between devices with their start and end apart: 41, of which 19 were waited for; matrix products, arithmetic and copies ran while one was open for 4% of the time, Pallas kernels for 9%

profile of v3, /device:TPU:0, one launch (start us, length us, event | category | flops | bytes accessed | tf_op | source)
XLA Modules:
  0.0 110.3 jit_solution(5054601310572614244)
XLA Ops:
  0.6 3.1 %collective-permute-start.4 = (bf16[256,512]{1,0:T(8,128)(2,1)}, bf16[256,512]{1,0:T(8,128)(2,1)S(1)}, u32[]{:S(2)}, u32[]{:S(2)}) collective-permute-start(bf16[256,512]{1,0:T(8,128)(2,1)} %refs_1_.3), channel_id=1, source_target_pairs={{0,8},{4,12},{8,0},{12,4},{16,24},{20,28},{24,16},{28,20},{1,9},{5... | collective-permute-start | bytes 786440 | tf_op jit(solution)/shard_map/ppermute | solution.py:16
  4.7 2.7 %collective-permute-start = (bf16[256,256]{1,0:T(8,128)(2,1)S(1)}, bf16[256,256]{1,0:T(8,128)(2,1)S(1)}, u32[]{:S(2)}, u32[]{:S(2)}) collective-permute-start(bf16[256,256]{1,0:T(8,128)(2,1)S(1)} %get-tuple-element.111), channel_id=1, source_target_pairs={{0,16},{4,20},{8,24},{12,28},{16,0},{20,4},{24,8},{28,12},{1,17},{... | collective-permute-start | bytes 393224 | tf_op jit(solution)/shard_map/ppermute | solution.py:16
  8.9 4.1 %collective-permute-done.4.refs_3_ = bf16[256,512]{1,0:T(8,128)(2,1)S(1)} collective-permute-done((bf16[256,512]{1,0:T(8,128)(2,1)}, bf16[256,512]{1,0:T(8,128)(2,1)S(1)}, u32[]{:S(2)}, u32[]{:S(2)}) %collective-permute-start.4) | collective-permute-done | bytes 262176 | tf_op jit(solution)/shard_map/ppermute | solution.py:16
  13.1 2.2 %copy-done = bf16[1,1,8,16,128,128]{5,4,3,2,1,0:T(8,128)(2,1)S(1)} copy-done((bf16[1,1,8,16,128,128]{5,4,3,2,1,0:T(8,128)(2,1)S(1)}, bf16[1,1,8,16,128,128]{5,4,3,2,1,0:T(8,128)(2,1)}, u32[]{:S(2)}) %copy-start) | copy-done | bytes 4194328
  16.0 3.2 %densify.1.refs_0_.a_ref = bf16[8,1024,256]{2,1,0:T(8,128)(2,1)S(1)} custom-call(s32[128]{0:T(128)S(1)} %reshape.18.rows_ref, s32[128]{0:T(128)S(1)} %reshape.19.cols_ref, s32[8]{0:T(128)S(1)} %bitcast.23, s32[2]{0:T(128)S(1)} %pad_add_fusion.place_ref, bf16[8,16,128,128]{3,2,1,0:T(8,128)(2,1)S(1)} %bitcast.22), custom_call_target="tpu_custom_call" | custom-call | flops 2097152 | bytes 16777216 | tf_op jit(solution)/shard_map/densify/pallas_call | solution.py:59
  19.3 4.3 %collective-permute-start.10 = (bf16[256,256]{1,0:T(8,128)(2,1)S(1)}, bf16[256,256]{1,0:T(8,128)(2,1)S(1)}, u32[]{:S(2)}, u32[]{:S(2)}) collective-permute-start(bf16[256,256]{1,0:T(8,128)(2,1)S(1)} %get-tuple-element.110), channel_id=1, source_target_pairs={{0,16},{4,20},{8,24},{12,28},{16,0},{20,4},{24,8},{28,12},{1,17},{... | collective-permute-start | bytes 393224 | tf_op jit(solution)/shard_map/ppermute | solution.py:16
  23.7 4.4 %collective-permute-done.1.refs_1_ = bf16[256,256]{1,0:T(8,128)(2,1)S(1)} collective-permute-done((bf16[256,256]{1,0:T(8,128)(2,1)S(1)}, bf16[256,256]{1,0:T(8,128)(2,1)S(1)}, u32[]{:S(2)}, u32[]{:S(2)}) %collective-permute-start.1) | collective-permute-done | bytes 131104 | tf_op jit(solution)/shard_map/ppermute | solution.py:16
  28.0 2.4 %collective-permute-done.10.refs_5_ = bf16[256,256]{1,0:T(8,128)(2,1)S(1)} collective-permute-done((bf16[256,256]{1,0:T(8,128)(2,1)S(1)}, bf16[256,256]{1,0:T(8,128)(2,1)S(1)}, u32[]{:S(2)}, u32[]{:S(2)}) %collective-permute-start.10) | collective-permute-done | bytes 131104 | tf_op jit(solution)/shard_map/ppermute | solution.py:16
  32.3 3.2 %collective-permute-done.11.refs_1_ = bf16[256,256]{1,0:T(8,128)(2,1)S(1)} collective-permute-done((bf16[256,256]{1,0:T(8,128)(2,1)S(1)}, bf16[256,256]{1,0:T(8,128)(2,1)S(1)}, u32[]{:S(2)}, u32[]{:S(2)}) %collective-permute-start.11) | collective-permute-done | bytes 131104 | tf_op jit(solution)/shard_map/ppermute | solution.py:16
  35.4 1.4 %collective-permute-start.7 = (bf16[256,256]{1,0:T(8,128)(2,1)S(1)}, bf16[256,256]{1,0:T(8,128)(2,1)S(1)}, u32[]{:S(2)}, u32[]{:S(2)}) collective-permute-start(bf16[256,256]{1,0:T(8,128)(2,1)S(1)} %get-tuple-element.59), channel_id=1, source_target_pairs={{0,1},{1,0},{2,3},{3,2},{4,5},{5,4},{6,7},{7,6},{8,9},{9,8},{10,11... | collective-permute-start | bytes 393224 | tf_op jit(solution)/shard_map/ppermute | solution.py:16
  36.9 1.7 %collective-permute-start.8 = (bf16[256,256]{1,0:T(8,128)(2,1)S(1)}, bf16[256,256]{1,0:T(8,128)(2,1)S(1)}, u32[]{:S(2)}, u32[]{:S(2)}) collective-permute-start(bf16[256,256]{1,0:T(8,128)(2,1)S(1)} %get-tuple-element.60), channel_id=1, source_target_pairs={{0,2},{1,3},{2,0},{3,1},{4,6},{5,7},{6,4},{7,5},{8,10},{9,11},{10,... | collective-permute-start | bytes 393224 | tf_op jit(solution)/shard_map/ppermute | solution.py:16
  40.4 2.7 %collective-permute-start.16 = (bf16[256,256]{1,0:T(8,128)(2,1)S(1)}, bf16[256,256]{1,0:T(8,128)(2,1)S(1)}, u32[]{:S(2)}, u32[]{:S(2)}) collective-permute-start(bf16[256,256]{1,0:T(8,128)(2,1)S(1)} %get-tuple-element.71), channel_id=1, source_target_pairs={{0,3},{1,2},{2,1},{3,0},{4,7},{5,6},{6,5},{7,4},{8,11},{9,10},{10,... | collective-permute-start | bytes 393224 | tf_op jit(solution)/shard_map/ppermute | solution.py:16
  43.9 4.2 %collective-permute-done.8.refs_2_ = bf16[256,256]{1,0:T(8,128)(2,1)S(1)} collective-permute-done((bf16[256,256]{1,0:T(8,128)(2,1)S(1)}, bf16[256,256]{1,0:T(8,128)(2,1)S(1)}, u32[]{:S(2)}, u32[]{:S(2)}) %collective-permute-start.8) | collective-permute-done | bytes 131104 | tf_op jit(solution)/shard_map/ppermute | solution.py:16
  53.1 1.6 %collective-permute-start.19 = (bf16[256,256]{1,0:T(8,128)(2,1)S(1)}, bf16[256,256]{1,0:T(8,128)(2,1)S(1)}, u32[]{:S(2)}, u32[]{:S(2)}) collective-permute-start(bf16[256,256]{1,0:T(8,128)(2,1)S(1)} %get-tuple-element.79.refs_3_.refs_1_), channel_id=1, source_target_pairs={{0,3},{1,2},{2,1},{3,0},{4,7},{5,6},{6,5},{7,4},{8,11},{9,10},{10,... | collective-permute-start | bytes 393224 | tf_op jit(solution)/shard_map/ppermute | solution.py:16
  54.7 1.4 %collective-permute-start.18 = (bf16[256,256]{1,0:T(8,128)(2,1)S(1)}, bf16[256,256]{1,0:T(8,128)(2,1)S(1)}, u32[]{:S(2)}, u32[]{:S(2)}) collective-permute-start(bf16[256,256]{1,0:T(8,128)(2,1)S(1)} %get-tuple-element.79.refs_3_.refs_1_), channel_id=1, source_target_pairs={{0,2},{1,3},{2,0},{3,1},{4,6},{5,7},{6,4},{7,5},{8,10},{9,11},{10,... | collective-permute-start | bytes 393224 | tf_op jit(solution)/shard_map/ppermute | solution.py:16
  56.7 3.8 %collective-permute-done.19.refs_6_.refs_4_ = bf16[256,256]{1,0:T(8,128)(2,1)S(1)} collective-permute-done((bf16[256,256]{1,0:T(8,128)(2,1)S(1)}, bf16[256,256]{1,0:T(8,128)(2,1)S(1)}, u32[]{:S(2)}, u32[]{:S(2)}) %collective-permute-start.19) | collective-permute-done | bytes 131104 | tf_op jit(solution)/shard_map/ppermute | solution.py:16
  60.4 2.3 %collective-permute-done.18.refs_5_.refs_3_ = bf16[256,256]{1,0:T(8,128)(2,1)S(1)} collective-permute-done((bf16[256,256]{1,0:T(8,128)(2,1)S(1)}, bf16[256,256]{1,0:T(8,128)(2,1)S(1)}, u32[]{:S(2)}, u32[]{:S(2)}) %collective-permute-start.18) | collective-permute-done | bytes 131104 | tf_op jit(solution)/shard_map/ppermute | solution.py:16
  63.5 1.3 %collective-permute-start.31 = (bf16[256,256]{1,0:T(8,128)(2,1)S(1)}, bf16[256,256]{1,0:T(8,128)(2,1)S(1)}, u32[]{:S(2)}, u32[]{:S(2)}) collective-permute-start(bf16[256,256]{1,0:T(8,128)(2,1)S(1)} %get-tuple-element.93.refs_3_.refs_1_), channel_id=1, source_target_pairs={{0,3},{1,2},{2,1},{3,0},{4,7},{5,6},{6,5},{7,4},{8,11},{9,10},{10,... | collective-permute-start | bytes 393224 | tf_op jit(solution)/shard_map/ppermute | solution.py:16
  64.8 1.4 %collective-permute-start.30 = (bf16[256,256]{1,0:T(8,128)(2,1)S(1)}, bf16[256,256]{1,0:T(8,128)(2,1)S(1)}, u32[]{:S(2)}, u32[]{:S(2)}) collective-permute-start(bf16[256,256]{1,0:T(8,128)(2,1)S(1)} %get-tuple-element.93.refs_3_.refs_1_), channel_id=1, source_target_pairs={{0,2},{1,3},{2,0},{3,1},{4,6},{5,7},{6,4},{7,5},{8,10},{9,11},{10,... | collective-permute-start | bytes 393224 | tf_op jit(solution)/shard_map/ppermute | solution.py:16
  68.5 1.4 %collective-permute-start.24 = (bf16[64,512]{1,0:T(8,128)(2,1)S(1)}, bf16[64,512]{1,0:T(8,128)(2,1)S(1)}, u32[]{:S(2)}, u32[]{:S(2)}) collective-permute-start(bf16[64,512]{1,0:T(8,128)(2,1)S(1)} %get-tuple-element.109), channel_id=1, source_target_pairs={{0,2},{1,3},{2,0},{3,1},{4,6},{5,7},{6,4},{7,5},{8,10},{9,11},{10,... | collective-permute-start | bytes 196616 | tf_op jit(solution)/shard_map/ppermute | solution.py:16
  69.9 1.6 %collective-permute-done.23 = bf16[64,512]{1,0:T(8,128)(2,1)S(1)} collective-permute-done((bf16[64,512]{1,0:T(8,128)(2,1)S(1)}, bf16[64,512]{1,0:T(8,128)(2,1)S(1)}, u32[]{:S(2)}, u32[]{:S(2)}) %collective-permute-start.23) | collective-permute-done | bytes 65568 | tf_op jit(solution)/shard_map/ppermute | solution.py:16
  72.5 2.7 %collective-permute-done.24 = bf16[64,512]{1,0:T(8,128)(2,1)S(1)} collective-permute-done((bf16[64,512]{1,0:T(8,128)(2,1)S(1)}, bf16[64,512]{1,0:T(8,128)(2,1)S(1)}, u32[]{:S(2)}, u32[]{:S(2)}) %collective-permute-start.24) | collective-permute-done | bytes 65568 | tf_op jit(solution)/shard_map/ppermute | solution.py:16
  79.1 3.1 %collective-permute-done.26 = bf16[384,256]{1,0:T(8,128)(2,1)S(1)} collective-permute-done((bf16[384,256]{1,0:T(8,128)(2,1)S(1)}, bf16[384,256]{1,0:T(8,128)(2,1)S(1)}, u32[]{:S(2)}, u32[]{:S(2)}) %collective-permute-start.26) | collective-permute-done | bytes 196640 | tf_op jit(solution)/shard_map/ppermute | solution.py:16
  82.3 1.4 %collective-permute-start.28 = (bf16[384,256]{1,0:T(8,128)(2,1)S(1)}, bf16[384,256]{1,0:T(8,128)(2,1)S(1)}, u32[]{:S(2)}, u32[]{:S(2)}) collective-permute-start(bf16[384,256]{1,0:T(8,128)(2,1)S(1)} %pad_maximum_fusion.3), channel_id=1, source_target_pairs={{0,16},{4,20},{8,24},{12,28},{16,0},{20,4},{24,8},{28,12},{1,17},{... | collective-permute-start | bytes 589832 | tf_op jit(solution)/shard_map/ppermute | solution.py:16
  83.8 1.8 %collective-permute-start.34 = (bf16[256,256]{1,0:T(8,128)(2,1)S(1)}, bf16[256,256]{1,0:T(8,128)(2,1)S(1)}, u32[]{:S(2)}, u32[]{:S(2)}) collective-permute-start(bf16[256,256]{1,0:T(8,128)(2,1)S(1)} %add_convert_fusion.2), channel_id=1, source_target_pairs={{0,8},{4,12},{8,0},{12,4},{16,24},{20,28},{24,16},{28,20},{1,9},{5... | collective-permute-start | bytes 393224 | tf_op jit(solution)/shard_map/ppermute | solution.py:16
  85.9 7.7 %collective-permute-done.28 = bf16[384,256]{1,0:T(8,128)(2,1)S(1)} collective-permute-done((bf16[384,256]{1,0:T(8,128)(2,1)S(1)}, bf16[384,256]{1,0:T(8,128)(2,1)S(1)}, u32[]{:S(2)}, u32[]{:S(2)}) %collective-permute-start.28) | collective-permute-done | bytes 196640 | tf_op jit(solution)/shard_map/ppermute | solution.py:16
  93.6 1.4 %collective-permute-start.39 = (f32[64,512]{1,0:T(8,128)S(1)}, f32[64,512]{1,0:T(8,128)S(1)}, u32[]{:S(2)}, u32[]{:S(2)}) collective-permute-start(f32[64,512]{1,0:T(8,128)S(1)} %add_multiply_fusion.refs_0_), channel_id=1, source_target_pairs={{0,3},{1,2},{2,1},{3,0},{4,7},{5,6},{6,5},{7,4},{8,11},{9,10},{10,... | collective-permute-start | bytes 393224 | tf_op jit(solution)/shard_map/ppermute | solution.py:16
  95.0 1.4 %collective-permute-start.38 = (f32[64,512]{1,0:T(8,128)S(1)}, f32[64,512]{1,0:T(8,128)S(1)}, u32[]{:S(2)}, u32[]{:S(2)}) collective-permute-start(f32[64,512]{1,0:T(8,128)S(1)} %add_multiply_fusion.refs_0_), channel_id=1, source_target_pairs={{0,2},{1,3},{2,0},{3,1},{4,6},{5,7},{6,4},{7,5},{8,10},{9,11},{10,... | collective-permute-start | bytes 393224 | tf_op jit(solution)/shard_map/ppermute | solution.py:16
  97.3 3.6 %collective-permute-done.39.refs_3_ = f32[64,512]{1,0:T(8,128)S(1)} collective-permute-done((f32[64,512]{1,0:T(8,128)S(1)}, f32[64,512]{1,0:T(8,128)S(1)}, u32[]{:S(2)}, u32[]{:S(2)}) %collective-permute-start.39) | collective-permute-done | bytes 131104 | tf_op jit(solution)/shard_map/ppermute | solution.py:16
  101.0 1.8 %collective-permute-done.38.refs_2_ = f32[64,512]{1,0:T(8,128)S(1)} collective-permute-done((f32[64,512]{1,0:T(8,128)S(1)}, f32[64,512]{1,0:T(8,128)S(1)}, u32[]{:S(2)}, u32[]{:S(2)}) %collective-permute-start.38) | collective-permute-done | bytes 131104 | tf_op jit(solution)/shard_map/ppermute | solution.py:16
  103.0 4.9 %collective-permute-done.36 = bf16[256,256]{1,0:T(8,128)(2,1)S(1)} collective-permute-done((bf16[256,256]{1,0:T(8,128)(2,1)S(1)}, bf16[256,256]{1,0:T(8,128)(2,1)S(1)}, u32[]{:S(2)}, u32[]{:S(2)}) %collective-permute-start.36) | collective-permute-done | bytes 131104 | tf_op jit(solution)/shard_map/ppermute | solution.py:16
  108.7 1.6 %place_slices.1 = f32[512,512]{1,0:T(8,128)} custom-call(s32[2]{0:T(128)S(1)} %pad_add_fusion.place_ref, f32[64,512]{1,0:T(8,128)S(1)} %add_multiply_fusion.refs_0_, f32[64,512]{1,0:T(8,128)S(1)} %collective-permute-done.37.refs_1_, f32[64,512]{1,0:T(8,128)S(1)} %collective-permute-done.38.refs_2_, f32[64,512]{1,0:T(8,128)S(1)} %collective-permute-done.39.refs_3_, ...), custom_call_target="tpu_custom_call" | custom-call | bytes 2097152 | tf_op jit(solution)/shard_map/place_slices/pallas_call | solution.py:207
  (97 shorter events, 23.5 us)
Async XLA Ops:
  0.6 12.4 %collective-permute-start.4 = (bf16[256,512]{1,0:T(8,128)(2,1)}, bf16[256,512]{1,0:T(8,128)(2,1)S(1)}, u32[]{:S(2)}, u32[]{:S(2)}) collective-permute-start(bf16[256,512]{1,0:T(8,128)(2,1)} %refs_1_.3), channel_id=1, source_target_pairs={{0,8},{4,12},{8,0},{12,4},{16,24},{20,28},{24,16},{28,20},{1,9},{5... | collective-permute-start | bytes 786440 | tf_op jit(solution)/shard_map/ppermute | solution.py:16
  4.7 14.5 %collective-permute-start = (bf16[256,256]{1,0:T(8,128)(2,1)S(1)}, bf16[256,256]{1,0:T(8,128)(2,1)S(1)}, u32[]{:S(2)}, u32[]{:S(2)}) collective-permute-start(bf16[256,256]{1,0:T(8,128)(2,1)S(1)} %get-tuple-element.111), channel_id=1, source_target_pairs={{0,16},{4,20},{8,24},{12,28},{16,0},{20,4},{24,8},{28,12},{1,17},{... | collective-permute-start | bytes 393224 | tf_op jit(solution)/shard_map/ppermute | solution.py:16
  7.4 23.4 %collective-permute-start.3 = (bf16[256,512]{1,0:T(8,128)(2,1)}, bf16[256,512]{1,0:T(8,128)(2,1)S(1)}, u32[]{:S(2)}, u32[]{:S(2)}) collective-permute-start(bf16[256,512]{1,0:T(8,128)(2,1)} %refs_1_.3), channel_id=1, source_target_pairs={{0,4},{4,0},{8,12},{12,8},{16,20},{20,16},{24,28},{28,24},{1,5},{5... | collective-permute-start | bytes 786440 | tf_op jit(solution)/shard_map/ppermute | solution.py:16
  13.0 17.8 %collective-permute-start.5 = (bf16[256,512]{1,0:T(8,128)(2,1)S(1)}, bf16[256,512]{1,0:T(8,128)(2,1)S(1)}, u32[]{:S(2)}, u32[]{:S(2)}) collective-permute-start(bf16[256,512]{1,0:T(8,128)(2,1)S(1)} %collective-permute-done.4.refs_3_), channel_id=1, source_target_pairs={{0,4},{4,0},{8,12},{12,8},{16,20},{20,16},{24,28},{28,24},{1,5},{5... | collective-permute-start | bytes 786440 | tf_op jit(solution)/shard_map/ppermute | solution.py:16
  19.2 8.8 %collective-permute-start.1 = (bf16[256,256]{1,0:T(8,128)(2,1)S(1)}, bf16[256,256]{1,0:T(8,128)(2,1)S(1)}, u32[]{:S(2)}, u32[]{:S(2)}) collective-permute-start(bf16[256,256]{1,0:T(8,128)(2,1)S(1)} %collective-permute-done.refs_5_), channel_id=1, source_target_pairs={{0,8},{4,12},{8,0},{12,4},{16,24},{20,28},{24,16},{28,20},{1,9},{5... | collective-permute-start | bytes 393224 | tf_op jit(solution)/shard_map/ppermute | solution.py:16
  19.3 11.2 %collective-permute-start.10 = (bf16[256,256]{1,0:T(8,128)(2,1)S(1)}, bf16[256,256]{1,0:T(8,128)(2,1)S(1)}, u32[]{:S(2)}, u32[]{:S(2)}) collective-permute-start(bf16[256,256]{1,0:T(8,128)(2,1)S(1)} %get-tuple-element.110), channel_id=1, source_target_pairs={{0,16},{4,20},{8,24},{12,28},{16,0},{20,4},{24,8},{28,12},{1,17},{... | collective-permute-start | bytes 393224 | tf_op jit(solution)/shard_map/ppermute | solution.py:16
  23.6 7.2 %collective-permute-start.6 = (bf16[256,256]{1,0:T(8,128)(2,1)S(1)}, bf16[256,256]{1,0:T(8,128)(2,1)S(1)}, u32[]{:S(2)}, u32[]{:S(2)}) collective-permute-start(bf16[256,256]{1,0:T(8,128)(2,1)S(1)} %collective-permute-done.refs_5_), channel_id=1, source_target_pairs={{0,4},{4,0},{8,12},{12,8},{16,20},{20,16},{24,28},{28,24},{1,5},{5... | collective-permute-start | bytes 393224 | tf_op jit(solution)/shard_map/ppermute | solution.py:16
  30.8 8.1 %collective-permute-start.13 = (bf16[256,256]{1,0:T(8,128)(2,1)S(1)}, bf16[256,256]{1,0:T(8,128)(2,1)S(1)}, u32[]{:S(2)}, u32[]{:S(2)}) collective-permute-start(bf16[256,256]{1,0:T(8,128)(2,1)S(1)} %collective-permute-done.10.refs_5_), channel_id=1, source_target_pairs={{0,4},{4,0},{8,12},{12,8},{16,20},{20,16},{24,28},{28,24},{1,5},{5... | collective-permute-start | bytes 393224 | tf_op jit(solution)/shard_map/ppermute | solution.py:16
  35.4 7.8 %collective-permute-start.7 = (bf16[256,256]{1,0:T(8,128)(2,1)S(1)}, bf16[256,256]{1,0:T(8,128)(2,1)S(1)}, u32[]{:S(2)}, u32[]{:S(2)}) collective-permute-start(bf16[256,256]{1,0:T(8,128)(2,1)S(1)} %get-tuple-element.59), channel_id=1, source_target_pairs={{0,1},{1,0},{2,3},{3,2},{4,5},{5,4},{6,7},{7,6},{8,9},{9,8},{10,11... | collective-permute-start | bytes 393224 | tf_op jit(solution)/shard_map/ppermute | solution.py:16
  36.9 11.2 %collective-permute-start.8 = (bf16[256,256]{1,0:T(8,128)(2,1)S(1)}, bf16[256,256]{1,0:T(8,128)(2,1)S(1)}, u32[]{:S(2)}, u32[]{:S(2)}) collective-permute-start(bf16[256,256]{1,0:T(8,128)(2,1)S(1)} %get-tuple-element.60), channel_id=1, source_target_pairs={{0,2},{1,3},{2,0},{3,1},{4,6},{5,7},{6,4},{7,5},{8,10},{9,11},{10,... | collective-permute-start | bytes 393224 | tf_op jit(solution)/shard_map/ppermute | solution.py:16
  38.6 9.5 %collective-permute-start.9 = (bf16[256,256]{1,0:T(8,128)(2,1)S(1)}, bf16[256,256]{1,0:T(8,128)(2,1)S(1)}, u32[]{:S(2)}, u32[]{:S(2)}) collective-permute-start(bf16[256,256]{1,0:T(8,128)(2,1)S(1)} %get-tuple-element.61), channel_id=1, source_target_pairs={{0,3},{1,2},{2,1},{3,0},{4,7},{5,6},{6,5},{7,4},{8,11},{9,10},{10,... | collective-permute-start | bytes 393224 | tf_op jit(solution)/shard_map/ppermute | solution.py:16
  40.4 8.9 %collective-permute-start.16 = (bf16[256,256]{1,0:T(8,128)(2,1)S(1)}, bf16[256,256]{1,0:T(8,128)(2,1)S(1)}, u32[]{:S(2)}, u32[]{:S(2)}) collective-permute-start(bf16[256,256]{1,0:T(8,128)(2,1)S(1)} %get-tuple-element.71), channel_id=1, source_target_pairs={{0,3},{1,2},{2,1},{3,0},{4,7},{5,6},{6,5},{7,4},{8,11},{9,10},{10,... | collective-permute-start | bytes 393224 | tf_op jit(solution)/shard_map/ppermute | solution.py:16
  43.1 6.7 %collective-permute-start.14 = (bf16[256,256]{1,0:T(8,128)(2,1)S(1)}, bf16[256,256]{1,0:T(8,128)(2,1)S(1)}, u32[]{:S(2)}, u32[]{:S(2)}) collective-permute-start(bf16[256,256]{1,0:T(8,128)(2,1)S(1)} %get-tuple-element.69), channel_id=1, source_target_pairs={{0,1},{1,0},{2,3},{3,2},{4,5},{5,4},{6,7},{7,6},{8,9},{9,8},{10,11... | collective-permute-start | bytes 393224 | tf_op jit(solution)/shard_map/ppermute | solution.py:16
  43.2 7.7 %collective-permute-start.15 = (bf16[256,256]{1,0:T(8,128)(2,1)S(1)}, bf16[256,256]{1,0:T(8,128)(2,1)S(1)}, u32[]{:S(2)}, u32[]{:S(2)}) collective-permute-start(bf16[256,256]{1,0:T(8,128)(2,1)S(1)} %get-tuple-element.70), channel_id=1, source_target_pairs={{0,2},{1,3},{2,0},{3,1},{4,6},{5,7},{6,4},{7,5},{8,10},{9,11},{10,... | collective-permute-start | bytes 393224 | tf_op jit(solution)/shard_map/ppermute | solution.py:16
  53.0 13.1 %collective-permute-start.22 = (bf16[4,64,512]{2,1,0:T(8,128)(2,1)S(1)}, bf16[4,64,512]{2,1,0:T(8,128)(2,1)S(1)}, u32[]{:S(2)}, u32[]{:S(2)}) collective-permute-start(bf16[4,64,512]{2,1,0:T(8,128)(2,1)S(1)} %get-tuple-element.88), channel_id=1, source_target_pairs={{0,4},{4,0},{8,12},{12,8},{16,20},{20,16},{24,28},{28,24},{1,5},{5... | collective-permute-start | bytes 786440 | tf_op jit(solution)/shard_map/ppermute | solution.py:16
  53.1 7.3 %collective-permute-start.19 = (bf16[256,256]{1,0:T(8,128)(2,1)S(1)}, bf16[256,256]{1,0:T(8,128)(2,1)S(1)}, u32[]{:S(2)}, u32[]{:S(2)}) collective-permute-start(bf16[256,256]{1,0:T(8,128)(2,1)S(1)} %get-tuple-element.79.refs_3_.refs_1_), channel_id=1, source_target_pairs={{0,3},{1,2},{2,1},{3,0},{4,7},{5,6},{6,5},{7,4},{8,11},{9,10},{10,... | collective-permute-start | bytes 393224 | tf_op jit(solution)/shard_map/ppermute | solution.py:16
  54.7 8.0 %collective-permute-start.18 = (bf16[256,256]{1,0:T(8,128)(2,1)S(1)}, bf16[256,256]{1,0:T(8,128)(2,1)S(1)}, u32[]{:S(2)}, u32[]{:S(2)}) collective-permute-start(bf16[256,256]{1,0:T(8,128)(2,1)S(1)} %get-tuple-element.79.refs_3_.refs_1_), channel_id=1, source_target_pairs={{0,2},{1,3},{2,0},{3,1},{4,6},{5,7},{6,4},{7,5},{8,10},{9,11},{10,... | collective-permute-start | bytes 393224 | tf_op jit(solution)/shard_map/ppermute | solution.py:16
  56.1 7.0 %collective-permute-start.17 = (bf16[256,256]{1,0:T(8,128)(2,1)S(1)}, bf16[256,256]{1,0:T(8,128)(2,1)S(1)}, u32[]{:S(2)}, u32[]{:S(2)}) collective-permute-start(bf16[256,256]{1,0:T(8,128)(2,1)S(1)} %get-tuple-element.79.refs_3_.refs_1_), channel_id=1, source_target_pairs={{0,1},{1,0},{2,3},{3,2},{4,5},{5,4},{6,7},{7,6},{8,9},{9,8},{10,11... | collective-permute-start | bytes 393224 | tf_op jit(solution)/shard_map/ppermute | solution.py:16
  63.5 13.5 %collective-permute-start.31 = (bf16[256,256]{1,0:T(8,128)(2,1)S(1)}, bf16[256,256]{1,0:T(8,128)(2,1)S(1)}, u32[]{:S(2)}, u32[]{:S(2)}) collective-permute-start(bf16[256,256]{1,0:T(8,128)(2,1)S(1)} %get-tuple-element.93.refs_3_.refs_1_), channel_id=1, source_target_pairs={{0,3},{1,2},{2,1},{3,0},{4,7},{5,6},{6,5},{7,4},{8,11},{9,10},{10,... | collective-permute-start | bytes 393224 | tf_op jit(solution)/shard_map/ppermute | solution.py:16
  64.8 12.2 %collective-permute-start.30 = (bf16[256,256]{1,0:T(8,128)(2,1)S(1)}, bf16[256,256]{1,0:T(8,128)(2,1)S(1)}, u32[]{:S(2)}, u32[]{:S(2)}) collective-permute-start(bf16[256,256]{1,0:T(8,128)(2,1)S(1)} %get-tuple-element.93.refs_3_.refs_1_), channel_id=1, source_target_pairs={{0,2},{1,3},{2,0},{3,1},{4,6},{5,7},{6,4},{7,5},{8,10},{9,11},{10,... | collective-permute-start | bytes 393224 | tf_op jit(solution)/shard_map/ppermute | solution.py:16
  68.5 6.7 %collective-permute-start.24 = (bf16[64,512]{1,0:T(8,128)(2,1)S(1)}, bf16[64,512]{1,0:T(8,128)(2,1)S(1)}, u32[]{:S(2)}, u32[]{:S(2)}) collective-permute-start(bf16[64,512]{1,0:T(8,128)(2,1)S(1)} %get-tuple-element.109), channel_id=1, source_target_pairs={{0,2},{1,3},{2,0},{3,1},{4,6},{5,7},{6,4},{7,5},{8,10},{9,11},{10,... | collective-permute-start | bytes 196616 | tf_op jit(solution)/shard_map/ppermute | solution.py:16
  75.3 6.9 %collective-permute-start.26 = (bf16[384,256]{1,0:T(8,128)(2,1)S(1)}, bf16[384,256]{1,0:T(8,128)(2,1)S(1)}, u32[]{:S(2)}, u32[]{:S(2)}) collective-permute-start(bf16[384,256]{1,0:T(8,128)(2,1)S(1)} %pad_maximum_fusion.2), channel_id=1, source_target_pairs={{0,8},{4,12},{8,0},{12,4},{16,24},{20,28},{24,16},{28,20},{1,9},{5... | collective-permute-start | bytes 589832 | tf_op jit(solution)/shard_map/ppermute | solution.py:16
  77.4 6.3 %collective-permute-start.33 = (bf16[256,256]{1,0:T(8,128)(2,1)S(1)}, bf16[256,256]{1,0:T(8,128)(2,1)S(1)}, u32[]{:S(2)}, u32[]{:S(2)}) collective-permute-start(bf16[256,256]{1,0:T(8,128)(2,1)S(1)} %get-tuple-element.99), channel_id=1, source_target_pairs={{0,4},{4,0},{8,12},{12,8},{16,20},{20,16},{24,28},{28,24},{1,5},{5... | collective-permute-start | bytes 393224 | tf_op jit(solution)/shard_map/ppermute | solution.py:16
  79.0 18.2 %collective-permute-start.32 = (bf16[768,256]{1,0:T(8,128)(2,1)S(1)}, bf16[768,256]{1,0:T(8,128)(2,1)S(1)}, u32[]{:S(2)}, u32[]{:S(2)}) collective-permute-start(bf16[768,256]{1,0:T(8,128)(2,1)S(1)} %get-tuple-element.96), channel_id=1, source_target_pairs={{0,4},{4,0},{8,12},{12,8},{16,20},{20,16},{24,28},{28,24},{1,5},{5... | collective-permute-start | bytes 1179656 | tf_op jit(solution)/shard_map/ppermute | solution.py:16
  82.3 11.2 %collective-permute-start.28 = (bf16[384,256]{1,0:T(8,128)(2,1)S(1)}, bf16[384,256]{1,0:T(8,128)(2,1)S(1)}, u32[]{:S(2)}, u32[]{:S(2)}) collective-permute-start(bf16[384,256]{1,0:T(8,128)(2,1)S(1)} %pad_maximum_fusion.3), channel_id=1, source_target_pairs={{0,16},{4,20},{8,24},{12,28},{16,0},{20,4},{24,8},{28,12},{1,17},{... | collective-permute-start | bytes 589832 | tf_op jit(solution)/shard_map/ppermute | solution.py:16
  83.8 12.6 %collective-permute-start.34 = (bf16[256,256]{1,0:T(8,128)(2,1)S(1)}, bf16[256,256]{1,0:T(8,128)(2,1)S(1)}, u32[]{:S(2)}, u32[]{:S(2)}) collective-permute-start(bf16[256,256]{1,0:T(8,128)(2,1)S(1)} %add_convert_fusion.2), channel_id=1, source_target_pairs={{0,8},{4,12},{8,0},{12,4},{16,24},{20,28},{24,16},{28,20},{1,9},{5... | collective-permute-start | bytes 393224 | tf_op jit(solution)/shard_map/ppermute | solution.py:16
  85.6 17.4 %collective-permute-start.27 = (bf16[256,256]{1,0:T(8,128)(2,1)S(1)}, bf16[256,256]{1,0:T(8,128)(2,1)S(1)}, u32[]{:S(2)}, u32[]{:S(2)}) collective-permute-start(bf16[256,256]{1,0:T(8,128)(2,1)S(1)} %get-tuple-element.90), channel_id=1, source_target_pairs={{0,8},{4,12},{8,0},{12,4},{16,24},{20,28},{24,16},{28,20},{1,9},{5... | collective-permute-start | bytes 393224 | tf_op jit(solution)/shard_map/ppermute | solution.py:16
  93.6 7.3 %collective-permute-start.39 = (f32[64,512]{1,0:T(8,128)S(1)}, f32[64,512]{1,0:T(8,128)S(1)}, u32[]{:S(2)}, u32[]{:S(2)}) collective-permute-start(f32[64,512]{1,0:T(8,128)S(1)} %add_multiply_fusion.refs_0_), channel_id=1, source_target_pairs={{0,3},{1,2},{2,1},{3,0},{4,7},{5,6},{6,5},{7,4},{8,11},{9,10},{10,... | collective-permute-start | bytes 393224 | tf_op jit(solution)/shard_map/ppermute | solution.py:16
  95.0 7.7 %collective-permute-start.38 = (f32[64,512]{1,0:T(8,128)S(1)}, f32[64,512]{1,0:T(8,128)S(1)}, u32[]{:S(2)}, u32[]{:S(2)}) collective-permute-start(f32[64,512]{1,0:T(8,128)S(1)} %add_multiply_fusion.refs_0_), channel_id=1, source_target_pairs={{0,2},{1,3},{2,0},{3,1},{4,6},{5,7},{6,4},{7,5},{8,10},{9,11},{10,... | collective-permute-start | bytes 393224 | tf_op jit(solution)/shard_map/ppermute | solution.py:16
  96.4 6.4 %collective-permute-start.37 = (f32[64,512]{1,0:T(8,128)S(1)}, f32[64,512]{1,0:T(8,128)S(1)}, u32[]{:S(2)}, u32[]{:S(2)}) collective-permute-start(f32[64,512]{1,0:T(8,128)S(1)} %add_multiply_fusion.refs_0_), channel_id=1, source_target_pairs={{0,1},{1,0},{2,3},{3,2},{4,5},{5,4},{6,7},{7,6},{8,9},{9,8},{10,11... | collective-permute-start | bytes 393224 | tf_op jit(solution)/shard_map/ppermute | solution.py:16
  100.9 7.0 %collective-permute-start.36 = (bf16[256,256]{1,0:T(8,128)(2,1)S(1)}, bf16[256,256]{1,0:T(8,128)(2,1)S(1)}, u32[]{:S(2)}, u32[]{:S(2)}) collective-permute-start(bf16[256,256]{1,0:T(8,128)(2,1)S(1)} %get-tuple-element.106), channel_id=1, source_target_pairs={{0,16},{4,20},{8,24},{12,28},{16,0},{20,4},{24,8},{28,12},{1,17},{... | collective-permute-start | bytes 393224 | tf_op jit(solution)/shard_map/ppermute | solution.py:16
  102.9 5.9 %collective-permute-start.40 = (f32[256,512]{1,0:T(8,128)S(1)}, f32[256,512]{1,0:T(8,128)S(1)}, u32[]{:S(2)}, u32[]{:S(2)}) collective-permute-start(f32[256,512]{1,0:T(8,128)S(1)} %pad_maximum_fusion), channel_id=1, source_target_pairs={{0,4},{4,0},{8,12},{12,8},{16,20},{20,16},{24,28},{28,24},{1,5},{5... | collective-permute-start | bytes 1572872 | tf_op jit(solution)/shard_map/ppermute | solution.py:16
  (14 other events, 82.3 us)

commit v4 on v0

v4 whole, which is shorter than its diff:
```python
import functools

import jax
import jax.numpy as jnp
import numpy as np
from jax import lax
from jax.experimental import pallas as pl
from jax.experimental.pallas import tpu as pltpu
from jax.sharding import PartitionSpec as P

WHOLE = pl.BlockSpec(memory_space=pltpu.VMEM)
SCALARS = pl.BlockSpec(memory_space=pltpu.SMEM)
CHUNKS = 1


def bit_count(n):
    return n.bit_length() - 1


def bit_order(core, bits):
    return list(range(bits))[::-1] if core else list(range(bits))


def slot_mask(slot, core, bits):
    mask = 0
    for i, bit in enumerate(bit_order(core, bits)):
        mask |= ((slot >> (bits - 1 - i)) & 1) << bit
    return mask


def swap_cores(x):
    return lax.ppermute(x, "dom", [(i, i ^ 1) for i in range(lax.axis_size("dom"))])


def swap_chips(x, held):
    blocks = lax.axis_size("dom")
    bits = bit_count(blocks // 2)
    return lax.ppermute(x, "dom", [(i, i ^ (2 * slot_mask(held, i % 2, bits))) for i in range(blocks)])


def swap_members(x, held):
    blocks, groups = lax.axis_size("dom"), lax.axis_size("repl")
    bits = bit_count(groups)
    pairs = []
    for i in range(blocks):
        for j in range(groups):
            pairs.append((i * groups + j, i * groups + (j ^ slot_mask(held, i % 2, bits))))
    return lax.ppermute(x, ("dom", "repl"), pairs)


def after(x, *others):
    return lax.optimization_barrier((x, *others))[0]


def params(mib):
    return pltpu.CompilerParams(vmem_limit_bytes=mib * 1024 * 1024)


def like(shape, dtype):
    return jax.ShapeDtypeStruct(shape, dtype)


def bf16_dot(a, b):
    return jnp.dot(a, b, preferred_element_type=jnp.float32)


def tables(blocks, groups):
    bits = bit_count(blocks // 2)
    column = np.zeros((blocks, blocks), np.int32)
    for position in range(blocks):
        for j in range(blocks):
            core = (position % 2) ^ (j % 2)
            column[position, j] = ((position // 2) ^ slot_mask(j // 2, core, bits)) * 2 + core
    bits = bit_count(groups)
    slot = np.zeros((2, groups, groups), np.int32)
    for core in range(2):
        for member in range(groups):
            for k in range(groups):
                slot[core, member, member ^ slot_mask(k, core, bits)] = k
    return jnp.asarray(column), jnp.asarray(slot.reshape(2, -1))


def densify_kernel(rows_ref, cols_ref, counts_ref, column_ref, slot_ref, place_ref, tiles_ref, a_ref, acc_ref, *, col_tiles):
    position, member = place_ref[0], place_ref[1]
    column = column_ref[position, pl.program_id(0)]
    core = lax.rem(position, 2)
    size = tiles_ref.shape[-1]
    groups = acc_ref.shape[0] // (col_tiles * col_tiles)
    acc_ref[...] = jnp.zeros_like(acc_ref)

    def add(tile, carry):
        row = rows_ref[0, 0, column, tile]
        row = slot_ref[core, member * groups + row // col_tiles] * col_tiles + lax.rem(row, col_tiles)
        spot = row * col_tiles + cols_ref[0, 0, column, tile]
        acc_ref[spot] += tiles_ref[0, tile].astype(jnp.float32)
        return carry

    lax.fori_loop(0, counts_ref[0, 0, column], add, 0)
    for spot in range(acc_ref.shape[0]):
        row, col = spot // col_tiles, spot % col_tiles
        a_ref[0, row * size:(row + 1) * size, col * size:(col + 1) * size] = acc_ref[spot].astype(a_ref.dtype)


def densify(tiles, tile_rows, tile_cols, tile_counts, column, slot, place, group_count, rows_local):
    columns, count, size, _ = tiles.shape
    col_tiles = rows_local // size
    rows = group_count * rows_local
    return pl.pallas_call(
        functools.partial(densify_kernel, col_tiles=col_tiles),
        out_shape=like((columns, rows, rows_local), jnp.bfloat16),
        grid_spec=pltpu.PrefetchScalarGridSpec(
            num_scalar_prefetch=6,
            grid=(columns,),
            in_specs=[pl.BlockSpec((1, count, size, size), lambda j, r, c, n, column, slot, p: (column[p[0], j], 0, 0, 0))],
            out_specs=pl.BlockSpec((1, rows, rows_local), lambda j, *_: (j, 0, 0)),
            scratch_shapes=[pltpu.VMEM((group_count * col_tiles * col_tiles, size, size), jnp.float32)],
        ),
        compiler_params=params(12),
        cost_estimate=pl.CostEstimate(
            flops=columns * count * size * size, bytes_accessed=8 * rows * columns * rows_local, transcendentals=0),
        name="densify",
    )(tile_rows, tile_cols, tile_counts, column, slot, place, tiles)


def transpose_kernel(a_ref, *outs):
    part = outs[0].shape[0]
    for i, out_ref in enumerate(outs):
        for j in range(part):
            out_ref[j] = a_ref[i * part + j].T


def transposed(dense):
    columns, rows, cols = dense.shape
    return pl.pallas_call(
        transpose_kernel,
        out_shape=[like((columns // 2, cols, rows), jnp.bfloat16)] * 2,
        in_specs=[WHOLE],
        out_specs=[WHOLE] * 2,
        compiler_params=params(8),
        cost_estimate=pl.CostEstimate(flops=0, bytes_accessed=4 * columns * rows * cols, transcendentals=0),
        name="transposed",
    )(dense)


def forward_kernel(*refs, first, pieces, has_prev):
    dense_ref, sources = refs[0], refs[1:1 + len(pieces)]
    rest = refs[1 + len(pieces):]
    prev, outs = (rest[:2], rest[2:]) if has_prev else (None, rest)
    half, width = outs[0].shape
    rows = dense_ref.shape[2]
    for i, out_ref in enumerate(outs):
        for k in range(half // rows):
            total = prev[i][k * rows:(k + 1) * rows, :] if has_prev else None
            start = i * half + k * rows
            for j, (row, col) in enumerate(pieces):
                part = bf16_dot(
                    dense_ref[first + j, start:start + rows, :], sources[j][row:row + rows, col:col + width])
                total = part if total is None else total + part
            out_ref[k * rows:(k + 1) * rows, :] = total.astype(out_ref.dtype)


def forward(dense, first, sources, width, prev, dtypes):
    _, rows, _ = dense.shape
    arrays = [source[0] for source in sources]
    return pl.pallas_call(
        functools.partial(
            forward_kernel, first=first, pieces=[source[1:] for source in sources], has_prev=prev is not None),
        out_shape=[like((rows // 2, width), dtype) for dtype in dtypes],
        in_specs=[WHOLE] * (1 + len(arrays) + (2 if prev is not None else 0)),
        out_specs=[WHOLE] * 2,
        compiler_params=params(8),
        cost_estimate=pl.CostEstimate(
            flops=2 * len(arrays) * rows * dense.shape[2] * width,
            bytes_accessed=2 * len(arrays) * rows * dense.shape[2] + 4 * rows * width, transcendentals=0),
        name="forward",
    )(dense, *arrays, *(prev or []))


def middle_kernel(*refs, chunks):
    pieces = refs[:2 * chunks]
    cot_ref, weight_ref = refs[2 * chunks:2 * chunks + 2]
    act_ref, agg_ref, pre_grad_ref = refs[2 * chunks + 2:2 * chunks + 5]
    grads = refs[2 * chunks + 5:]
    part = grads[0].shape[1]
    for c in range(chunks):
        agg = pieces[2 * c][...] + pieces[2 * c + 1][...].astype(jnp.float32)
        agg_ref[:, c * part:(c + 1) * part] = agg.astype(jnp.bfloat16)
    preact = bf16_dot(agg_ref[...], weight_ref[...])
    sigma = jax.nn.sigmoid(preact)
    act_ref[...] = (preact * sigma).astype(act_ref.dtype)
    slope = sigma * (1.0 + preact * (1.0 - sigma))
    pre_grad = (cot_ref[...].astype(jnp.float32) * slope).astype(jnp.bfloat16)
    pre_grad_ref[...] = pre_grad
    for c in range(chunks):
        grads[c][...] = lax.dot_general(
            pre_grad, weight_ref[c * part:(c + 1) * part, :], (((1,), (1,)), ((), ())),
            preferred_element_type=jnp.float32,
        ).astype(jnp.bfloat16)


def middle(pieces, cotangent, weight):
    rows, width = cotangent.shape
    chunks = len(pieces)
    whole = like((rows, width), jnp.bfloat16)
    return pl.pallas_call(
        functools.partial(middle_kernel, chunks=chunks),
        out_shape=[whole] * 3 + [like((rows, width // chunks), jnp.bfloat16)] * chunks,
        in_specs=[WHOLE] * (2 + 2 * chunks),
        out_specs=[WHOLE] * (3 + chunks),
        compiler_params=params(8),
        cost_estimate=pl.CostEstimate(
            flops=4 * rows * width * width, bytes_accessed=10 * rows * width, transcendentals=rows * width),
        name="middle",
    )(*[piece for chunk in pieces for piece in chunk], cotangent, weight)


def weight_kernel(place_ref, slot_ref, agg_ref, pre_grad_ref, own_ref, send_ref, part_ref):
    core, member = lax.rem(place_ref[0], 2), place_ref[1]
    groups, rows, _ = own_ref.shape
    part_ref[...] = lax.dot_general(
        agg_ref[...], pre_grad_ref[...], (((0,), (0,)), ((), ())), preferred_element_type=jnp.float32
    )
    for k in range(groups):
        for side, out_ref in ((core, own_ref), (1 - core, send_ref)):
            out_ref[slot_ref[side, member * groups + k]] = part_ref[
                pl.ds(pl.multiple_of((2 * k + side) * rows, rows), rows), :].astype(out_ref.dtype)


def weight_part(agg, pre_grad, slot, place, groups):
    rows, width = agg.shape
    part = (groups, width // (2 * groups), width)
    return pl.pallas_call(
        weight_kernel,
        out_shape=[like(part, jnp.float32), like(part, jnp.bfloat16)],
        in_specs=[SCALARS, SCALARS, WHOLE, WHOLE],
        out_specs=[WHOLE] * 2,
        scratch_shapes=[pltpu.VMEM((width, width), jnp.float32)],
        compiler_params=params(8),
        cost_estimate=pl.CostEstimate(
            flops=2 * rows * width * width, bytes_accessed=4 * rows * width + 4 * width * width, transcendentals=0),
        name="weight_part",
    )(place, slot, agg, pre_grad)


def place_kernel(place_ref, slot_ref, own_ref, other_ref, out_ref):
    core, member = lax.rem(place_ref[0], 2), place_ref[1]
    groups, rows, _ = own_ref.shape
    for k in range(groups):
        for side, ref in ((core, own_ref), (1 - core, other_ref)):
            out_ref[pl.ds(pl.multiple_of((2 * k + side) * rows, rows), rows), :] = ref[slot_ref[side, member * groups + k]]


def place_slices(own, other, slot, place):
    groups, rows, width = own.shape
    return pl.pallas_call(
        place_kernel,
        out_shape=like((2 * groups * rows, width), jnp.float32),
        in_specs=[SCALARS, SCALARS, WHOLE, WHOLE],
        out_specs=WHOLE,
        compiler_params=params(8),
        cost_estimate=pl.CostEstimate(flops=0, bytes_accessed=16 * groups * rows * width, transcendentals=0),
        name="place_slices",
    )(place, slot, own, other)


def backward_kernel(at_ref, *refs):
    grads, (own_ref, other_ref) = refs[:-2], refs[-2:]
    columns, size, _ = at_ref.shape
    for i in list(range(1, columns, 2)) + list(range(0, columns, 2)):
        total, start = None, 0
        for grad in grads:
            stop = start + grad.shape[0]
            part = bf16_dot(at_ref[i, :, start:stop], grad[...])
            total, start = part if total is None else total + part, stop
        out_ref = other_ref if i % 2 else own_ref
        out_ref[(i // 2) * size:(i // 2 + 1) * size, :] = total.astype(out_ref.dtype)


def backward(dense_t, grads):
    columns, cols, rows = dense_t.shape
    width = grads[0].shape[1]
    half = columns // 2 * cols
    return pl.pallas_call(
        backward_kernel,
        out_shape=[like((half, width), jnp.float32), like((half, width), jnp.bfloat16)],
        in_specs=[WHOLE] * (1 + len(grads)),
        out_specs=[WHOLE] * 2,
        compiler_params=params(8),
        cost_estimate=pl.CostEstimate(
            flops=4 * half * rows * width, bytes_accessed=4 * half * rows + 2 * rows * width + 6 * half * width,
            transcendentals=0),
        name="backward",
    )(dense_t, *grads)


def finish_kernel(*refs):
    out_ref = refs[-1]
    width = refs[0].shape[1]
    for c in range(len(refs) // 2):
        total = refs[2 * c][...] + refs[2 * c + 1][...].astype(jnp.float32)
        out_ref[:, c * width:(c + 1) * width] = total.astype(out_ref.dtype)


def finish(parts):
    rows, width = parts[0].shape
    width *= len(parts) // 2
    return pl.pallas_call(
        finish_kernel,
        out_shape=like((rows, width), jnp.bfloat16),
        in_specs=[WHOLE] * len(parts),
        out_specs=WHOLE,
        compiler_params=params(8),
        cost_estimate=pl.CostEstimate(flops=rows * width, bytes_accessed=8 * rows * width, transcendentals=0),
        name="finish",
    )(*parts)


def halve(total, swap, bits):
    for bit in reversed(range(bits)):
        half = total.shape[0] // 2
        arrived = swap(total[half:].astype(jnp.bfloat16), 1 << bit)
        total = total[:half]
        if bit:
            total = total + arrived.astype(jnp.float32)
    return total, arrived


def local(features, cotangent, weight, tiles, tile_rows, tile_cols, tile_counts):
    blocks = lax.axis_size("dom")
    groups = lax.axis_size("repl")
    chips = blocks // 2
    chip_bits, member_bits = bit_count(chips), bit_count(groups)
    rows_local, width = features.shape
    part_width = width // CHUNKS
    scale = float(rows_local * blocks * groups) ** (-0.5)
    place = jnp.stack([lax.axis_index("dom"), lax.axis_index("repl")]).astype(jnp.int32)
    column, slot = tables(blocks, groups)

    near, near_other = [(features, 0)], [(swap_cores(features), 0)]
    for bit in range(chip_bits - 1):
        held = [array[row:row + rows_local] for array, row in near]
        got = swap_chips(jnp.concatenate(held) if bit else held[0], 1 << bit)
        got_other = swap_cores(got)
        near += [(got, k * rows_local) for k in range(1 << bit)]
        near_other += [(got_other, k * rows_local) for k in range(1 << bit)]
    dense = densify(tiles[0, 0], tile_rows, tile_cols, tile_counts, column, slot, place, groups, rows_local)

    pieces = []
    for c in range(CHUNKS):
        cut = slice(c * part_width, (c + 1) * part_width)
        held = jnp.concatenate([array[row:row + rows_local, cut] for array, row in near])
        got = swap_chips(held, chips // 2)
        early = [(*pair[side], c * part_width) for pair in zip(near, near_other) for side in range(2)]
        totals = forward(dense, 0, early, part_width, None, [jnp.float32] * 2)
        got = after(got, *totals)
        got_other = swap_cores(got)
        late = [(array, k * rows_local, 0) for k in range(chips // 2) for array in (got, got_other)]
        low, high = forward(dense, len(early), late, part_width, totals, [jnp.float32, jnp.bfloat16])
        arrived = swap_members(high, groups // 2)
        pieces.append(halve(low + arrived.astype(jnp.float32), swap_members, member_bits - 1))
    dense_t = transposed(after(dense, high))
    pieces[-1] = (pieces[-1][0], after(pieces[-1][1], *dense_t))

    activated, agg, pre_grad, *grad_chunks = middle(pieces, cotangent, weight)

    share, share_send = weight_part(agg, pre_grad, slot, place, groups)
    share = share + swap_cores(share_send).astype(jnp.float32)

    columns = []
    for c in range(CHUNKS):
        grads = [grad_chunks[c]]
        for bit in range(member_bits):
            grads.append(swap_members(jnp.concatenate(grads) if bit else grads[0], 1 << bit))
            if c == 0 and bit == 0:
                total, arrived = halve(after(share, grads[-1]).reshape(-1, width), swap_members, member_bits)
                part = (total + arrived.astype(jnp.float32)).astype(jnp.bfloat16)
        grads[-1] = after(grads[-1], part)
        own, other = backward(dense_t[1], grads)
        high_sum = (own + swap_cores(other).astype(jnp.float32)).astype(jnp.bfloat16)
        own, other = backward(after(dense_t[0], high_sum), grads)
        low_sum = own + swap_cores(other).astype(jnp.float32)
        low_sum = low_sum + swap_chips(high_sum, chips // 2).astype(jnp.float32)
        columns += halve(low_sum, swap_chips, chip_bits - 1)
    feature_grad = finish(columns)

    for bit in range(chip_bits):
        part = part.astype(jnp.float32) + swap_chips(part, 1 << bit).astype(jnp.float32)
        part = part.astype(jnp.bfloat16) if bit < chip_bits - 1 else part * scale
    parts = jnp.concatenate([part] + [swap_members(part, k) for k in range(1, groups)])
    other = swap_cores(parts)
    shape = (groups, -1, width)
    weight_grad = place_slices(parts.reshape(shape), other.reshape(shape), slot, place)
    return (activated, feature_grad, weight_grad)


def solution(mesh):
    in_specs = (
        P(("dom", "repl"), None),
        P(("dom", "repl"), None),
        P(),
        P("dom", "repl", None, None, None, None),
        P("dom", "repl", None, None),
        P("dom", "repl", None, None),
        P("dom", "repl", None),
    )
    out_specs = (P(("dom", "repl"), None), P(("dom", "repl"), None), P())
    return jax.shard_map(local, mesh=mesh, in_specs=in_specs, out_specs=out_specs, check_vma=False)
```

time: 334 us -> 101 us (0.30)
  matrix products: 108 us -> 0 us
  blocking collectives: 69 us -> 0 us
  local copies, waits for them, and re-layouts: 58.6 us -> 5.78 us
  other arithmetic: 33 us -> 1.84 us
  starting transfers between devices: 0.57 us -> 26.2 us
  Pallas kernels: 0 us -> 15.9 us
  between operations: 14.1 us -> 0.88 us
  waiting for transfers between devices: 46.4 us -> 49.8 us
    dot_general x35 -> x0, matrix products: 108 us -> none  [the longest x16 69.7 us: place_tiles(): jnp.einsum('rt,taf->raf', selector, prod, precision=lax.Precision.HIGHEST)]
    psum x1 -> x0, blocking collectives: 69 us -> none  [local(): block_rows = lax.psum(totals, 'repl')]
    ppermute x14 -> x22, starting transfers between devices: 0.49 us -> 26.2 us  [the longest x6 13 us: swap_chips(): lax.ppermute(x, 'dom', [(i, i ^ 2 * slot_mask(held, i % 2, bits)) for i i...]
    gather x16 -> x0, local copies, waits for them, and re-layouts: 20.8 us -> none  [the longest x8 15.4 us: backward_block(): picked = grad_tiles[row_index[column]]]
    pallas_call x0 -> x10, Pallas kernels: none -> 15.9 us  [the longest x1 5.25 us: densify(): pl.pallas_call(functools.partial(densify_kernel, col_tiles=col_tiles), ou...]
    convert_element_type x18 -> x3, other arithmetic: 13.8 us -> 0.2 us  [the longest x1 0.16 us: local(): (own + swap_cores(other).astype(jnp.float32)).astype(jnp.bfloat16)]
    while x64 -> x0, local copies, waits for them, and re-layouts: 13.6 us -> none
    eq x16 -> x0, local copies, waits for them, and re-layouts: 11.1 us -> none  [place_tiles(): jnp.arange(count, dtype=jnp.int32)[:, None] == indices[None, :]]
  transfers between devices with their start and end apart: 16 -> 22, of which waited for: 10 -> 14; matrix products, arithmetic and copies ran while one was open for 54% -> 1% of each run, Pallas kernels for 0% -> 11%
where the time goes in v4:
time: 101 us
  waiting for transfers between devices  49.8 us (49%)
  starting transfers between devices  26.2 us (26%)
  Pallas kernels  15.9 us (16%)
  local copies, waits for them, and re-layouts  5.78 us (6%)
  other arithmetic  1.84 us (2%)
    ppermute x9, waiting for transfers between devices, swap_members(): return lax.ppermute(x, ('dom', 'repl'), pairs)  28.7 us
    ppermute x6, waiting for transfers between devices, swap_chips(): lax.ppermute(x, 'dom', [(i, i ^ 2 * slot_mask(held, i % 2, bits)) for i i...  19.2 us
    ppermute x6, starting transfers between devices, swap_chips(): lax.ppermute(x, 'dom', [(i, i ^ 2 * slot_mask(held, i % 2, bits)) for i i...  13 us
    ppermute x9, starting transfers between devices, swap_members(): return lax.ppermute(x, ('dom', 'repl'), pairs)  12.3 us
    unnamed x20, local copies, waits for them, and re-layouts  5.6 us
    pallas_call x1, Pallas kernels, densify(): pl.pallas_call(functools.partial(densify_kernel, col_tiles=col_tiles), ou...  5.25 us
    pallas_call x2, Pallas kernels, backward(): pl.pallas_call(backward_kernel, out_shape=[like((half, width), jnp.float3...  2.53 us
    pallas_call x2, Pallas kernels, forward(): pl.pallas_call(functools.partial(forward_kernel, first=first, pieces=[sou...  2.49 us
  transfers between devices with their start and end apart: 22, of which 14 were waited for; matrix products, arithmetic and copies ran while one was open for 1% of the time, Pallas kernels for 11%

profile of v4, /device:TPU:0, one launch (start us, length us, event | category | flops | bytes accessed | tf_op | source)
XLA Modules:
  0.0 100.5 jit_solution(16004869388057863003)
XLA Ops:
  0.6 4.1 %collective-permute-start = (bf16[256,512]{1,0:T(8,128)(2,1)}, bf16[256,512]{1,0:T(8,128)(2,1)S(1)}, u32[]{:S(2)}, u32[]{:S(2)}) collective-permute-start(bf16[256,512]{1,0:T(8,128)(2,1)} %refs_1_.1), channel_id=1, source_target_pairs={{0,16},{4,12},{8,24},{12,4},{16,0},{20,28},{24,8},{28,20},{1,17},{... | collective-permute-start | bytes 786440 | tf_op jit(solution)/shard_map/ppermute | solution.py:38
  4.7 6.1 %collective-permute-done.refs_3_ = bf16[256,512]{1,0:T(8,128)(2,1)S(1)} collective-permute-done((bf16[256,512]{1,0:T(8,128)(2,1)}, bf16[256,512]{1,0:T(8,128)(2,1)S(1)}, u32[]{:S(2)}, u32[]{:S(2)}) %collective-permute-start) | collective-permute-done | bytes 262176 | tf_op jit(solution)/shard_map/ppermute | solution.py:38
  11.8 2.5 %collective-permute-start.1 = (bf16[512,512]{1,0:T(8,128)(2,1)S(1)}, bf16[512,512]{1,0:T(8,128)(2,1)S(1)}, u32[]{:S(2)}, u32[]{:S(2)}) collective-permute-start(bf16[512,512]{1,0:T(8,128)(2,1)S(1)} %pad_maximum_fusion), channel_id=1, source_target_pairs={{0,8},{4,20},{8,0},{12,28},{16,24},{20,4},{24,16},{28,12},{1,9},{5... | collective-permute-start | bytes 1572872 | tf_op jit(solution)/shard_map/ppermute | solution.py:38
  14.9 2.2 %copy-done = bf16[1,1,8,16,128,128]{5,4,3,2,1,0:T(8,128)(2,1)S(1)} copy-done((bf16[1,1,8,16,128,128]{5,4,3,2,1,0:T(8,128)(2,1)S(1)}, bf16[1,1,8,16,128,128]{5,4,3,2,1,0:T(8,128)(2,1)}, u32[]{:S(2)}) %copy-start) | copy-done | bytes 4194328
  20.5 5.2 %densify.1.refs_0_.a_ref = bf16[8,1024,256]{2,1,0:T(8,128)(2,1)S(1)} custom-call(s32[1,1,8,16]{3,2,1,0:T(8,128)S(1)} %copy-done.6, s32[1,1,8,16]{3,2,1,0:T(8,128)S(1)} %copy-done.7, s32[1,1,8]{2,1,0:T(1,128)S(1)} %copy-done.9, s32[8,8]{1,0:T(8,128)S(1)} %copy-done.8, s32[2,16]{1,0:T(2,128)S(1)} %copy-done.4, s32[2]{0:T(128)S(1)} %pad_add_fusion.place_ref, ...), custom_call_target="tpu_custom_call" | custom-call | flops 2097152 | bytes 16777216 | tf_op jit(solution)/shard_map/densify/pallas_call | solution.py:108
  25.8 1.2 %forward.2 = (f32[512,512]{1,0:T(8,128)S(1)}, f32[512,512]{1,0:T(8,128)S(1)}) custom-call(bf16[8,1024,256]{2,1,0:T(8,128)(2,1)S(1)} %densify.1.refs_0_.a_ref, bf16[256,512]{1,0:T(8,128)(2,1)S(1)} %copy-done.1, bf16[256,512]{1,0:T(8,128)(2,1)S(1)} %collective-permute-done.2.refs_2_, bf16[256,512]{1,0:T(8,128)(2,1)S(1)} %collective-permute-done.refs_3_, ...), custom_call_target="tpu_custom_call" | custom-call | flops 1073741824 | bytes 4194304 | tf_op jit(solution)/shard_map/forward/pallas_call | solution.py:165
  27.2 1.9 %collective-permute-done.4.refs_2_.refs_4_ = bf16[512,512]{1,0:T(8,128)(2,1)S(1)} collective-permute-done((bf16[512,512]{1,0:T(8,128)(2,1)S(1)}, bf16[512,512]{1,0:T(8,128)(2,1)S(1)}, u32[]{:S(2)}, u32[]{:S(2)}) %collective-permute-start.4) | collective-permute-done | bytes 524320 | tf_op jit(solution)/shard_map/ppermute | solution.py:32
  29.0 1.2 %forward.3 = (f32[512,512]{1,0:T(8,128)S(1)}, bf16[512,512]{1,0:T(8,128)(2,1)S(1)}) custom-call(bf16[8,1024,256]{2,1,0:T(8,128)(2,1)S(1)} %densify.1.refs_0_.a_ref, bf16[512,512]{1,0:T(8,128)(2,1)S(1)} %collective-permute-done.1.refs_1_.refs_3_, bf16[512,512]{1,0:T(8,128)(2,1)S(1)} %collective-permute-done.4.refs_2_.refs_4_, ...), custom_call_target="tpu_custom_call" | custom-call | flops 1073741824 | bytes 4194304 | tf_op jit(solution)/shard_map/forward/pallas_call | solution.py:165
  30.3 1.6 %collective-permute-start.5 = (bf16[512,512]{1,0:T(8,128)(2,1)S(1)}, bf16[512,512]{1,0:T(8,128)(2,1)S(1)}, u32[]{:S(2)}, u32[]{:S(2)}) collective-permute-start(bf16[512,512]{1,0:T(8,128)(2,1)S(1)} %get-tuple-element.29), channel_id=1, source_target_pairs={{0,1},{1,0},{2,3},{3,2},{4,6},{5,7},{6,4},{7,5},{8,9},{9,8},{10,11... | collective-permute-start | bytes 1572872 | tf_op jit(solution)/shard_map/ppermute | solution.py:48
  31.9 7.6 %collective-permute-done.5 = bf16[512,512]{1,0:T(8,128)(2,1)S(1)} collective-permute-done((bf16[512,512]{1,0:T(8,128)(2,1)S(1)}, bf16[512,512]{1,0:T(8,128)(2,1)S(1)}, u32[]{:S(2)}, u32[]{:S(2)}) %collective-permute-start.5) | collective-permute-done | bytes 524320 | tf_op jit(solution)/shard_map/ppermute | solution.py:48
  39.8 1.7 %collective-permute-start.6 = (bf16[256,512]{1,0:T(8,128)(2,1)S(1)}, bf16[256,512]{1,0:T(8,128)(2,1)S(1)}, u32[]{:S(2)}, u32[]{:S(2)}) collective-permute-start(bf16[256,512]{1,0:T(8,128)(2,1)S(1)} %slice.56), channel_id=1, source_target_pairs={{0,2},{1,3},{2,0},{3,1},{4,5},{5,4},{6,7},{7,6},{8,10},{9,11},{10,... | collective-permute-start | bytes 786440 | tf_op jit(solution)/shard_map/ppermute | solution.py:48
  41.4 1.2 %transposed.1 = (bf16[4,256,1024]{2,1,0:T(8,128)(2,1)S(1)}, bf16[4,256,1024]{2,1,0:T(8,128)(2,1)S(1)}) custom-call(bf16[8,1024,256]{2,1,0:T(8,128)(2,1)S(1)} %densify.1.refs_0_.a_ref), custom_call_target="tpu_custom_call" | custom-call | bytes 8388608 | tf_op jit(solution)/shard_map/transposed/pallas_call | solution.py:134
  42.7 3.5 %collective-permute-done.6.refs_1_ = bf16[256,512]{1,0:T(8,128)(2,1)S(1)} collective-permute-done((bf16[256,512]{1,0:T(8,128)(2,1)S(1)}, bf16[256,512]{1,0:T(8,128)(2,1)S(1)}, u32[]{:S(2)}, u32[]{:S(2)}) %collective-permute-start.6) | collective-permute-done | bytes 262176 | tf_op jit(solution)/shard_map/ppermute | solution.py:48
  48.4 1.7 %collective-permute-start.7 = (bf16[256,512]{1,0:T(8,128)(2,1)S(1)}, bf16[256,512]{1,0:T(8,128)(2,1)S(1)}, u32[]{:S(2)}, u32[]{:S(2)}) collective-permute-start(bf16[256,512]{1,0:T(8,128)(2,1)S(1)} %get-tuple-element.35.refs_0_), channel_id=1, source_target_pairs={{0,2},{1,3},{2,0},{3,1},{4,5},{5,4},{6,7},{7,6},{8,10},{9,11},{10,... | collective-permute-start | bytes 786440 | tf_op jit(solution)/shard_map/ppermute | solution.py:48
  50.2 4.7 %collective-permute-done.7.refs_1_ = bf16[256,512]{1,0:T(8,128)(2,1)S(1)} collective-permute-done((bf16[256,512]{1,0:T(8,128)(2,1)S(1)}, bf16[256,512]{1,0:T(8,128)(2,1)S(1)}, u32[]{:S(2)}, u32[]{:S(2)}) %collective-permute-start.7) | collective-permute-done | bytes 262176 | tf_op jit(solution)/shard_map/ppermute | solution.py:48
  54.9 1.6 %collective-permute-start.10 = (bf16[128,512]{1,0:T(8,128)(2,1)S(1)}, bf16[128,512]{1,0:T(8,128)(2,1)S(1)}, u32[]{:S(2)}, u32[]{:S(2)}) collective-permute-start(bf16[128,512]{1,0:T(8,128)(2,1)S(1)} %bitcast.11), channel_id=1, source_target_pairs={{0,1},{1,0},{2,3},{3,2},{4,6},{5,7},{6,4},{7,5},{8,9},{9,8},{10,11... | collective-permute-start | bytes 393224 | tf_op jit(solution)/shard_map/ppermute | solution.py:48
  57.1 2.8 %collective-permute-done.10 = bf16[128,512]{1,0:T(8,128)(2,1)S(1)} collective-permute-done((bf16[128,512]{1,0:T(8,128)(2,1)S(1)}, bf16[128,512]{1,0:T(8,128)(2,1)S(1)}, u32[]{:S(2)}, u32[]{:S(2)}) %collective-permute-start.10) | collective-permute-done | bytes 131104 | tf_op jit(solution)/shard_map/ppermute | solution.py:48
  60.0 1.7 %collective-permute-start.11 = (bf16[64,512]{1,0:T(8,128)(2,1)S(1)}, bf16[64,512]{1,0:T(8,128)(2,1)S(1)}, u32[]{:S(2)}, u32[]{:S(2)}) collective-permute-start(bf16[64,512]{1,0:T(8,128)(2,1)S(1)} %slice.58), channel_id=1, source_target_pairs={{0,2},{1,3},{2,0},{3,1},{4,5},{5,4},{6,7},{7,6},{8,10},{9,11},{10,... | collective-permute-start | bytes 196616 | tf_op jit(solution)/shard_map/ppermute | solution.py:48
  61.6 3.3 %collective-permute-done.11 = bf16[64,512]{1,0:T(8,128)(2,1)S(1)} collective-permute-done((bf16[64,512]{1,0:T(8,128)(2,1)S(1)}, bf16[64,512]{1,0:T(8,128)(2,1)S(1)}, u32[]{:S(2)}, u32[]{:S(2)}) %collective-permute-start.11) | collective-permute-done | bytes 65568 | tf_op jit(solution)/shard_map/ppermute | solution.py:48
  64.9 1.6 %collective-permute-done.8.refs_2_ = bf16[512,512]{1,0:T(8,128)(2,1)S(1)} collective-permute-done((bf16[512,512]{1,0:T(8,128)(2,1)S(1)}, bf16[512,512]{1,0:T(8,128)(2,1)S(1)}, u32[]{:S(2)}, u32[]{:S(2)}) %collective-permute-start.8) | collective-permute-done | bytes 524320 | tf_op jit(solution)/shard_map/ppermute | solution.py:48
  66.5 1.3 %backward.2 = (f32[512,512]{1,0:T(8,128)S(1)}, bf16[512,512]{1,0:T(8,128)(2,1)S(1)}) custom-call(bf16[4,256,1024]{2,1,0:T(8,128)(2,1)S(1)} %get-tuple-element.32.at_ref, bf16[256,512]{1,0:T(8,128)(2,1)S(1)} %get-tuple-element.35.refs_0_, bf16[256,512]{1,0:T(8,128)(2,1)S(1)} %collective-permute-done.7.refs_1_, bf16[512,512]{1,0:T(8,128)(2,1)S(1)} %collective-permute-done.8.refs_2_), custom_call_target="tpu_custom_call" | custom-call | flops 1073741824 | bytes 4718592 | tf_op jit(solution)/shard_map/backward/pallas_call | solution.py:283
  67.9 2.9 %collective-permute-start.16 = (bf16[64,512]{1,0:T(8,128)(2,1)S(1)}, bf16[64,512]{1,0:T(8,128)(2,1)S(1)}, u32[]{:S(2)}, u32[]{:S(2)}) collective-permute-start(bf16[64,512]{1,0:T(8,128)(2,1)S(1)} %fusion), channel_id=1, source_target_pairs={{0,16},{4,12},{8,24},{12,4},{16,0},{20,28},{24,8},{28,20},{1,17},{... | collective-permute-start | bytes 196616 | tf_op jit(solution)/shard_map/ppermute | solution.py:38
  70.8 3.0 %collective-permute-done.16 = bf16[64,512]{1,0:T(8,128)(2,1)S(1)} collective-permute-done((bf16[64,512]{1,0:T(8,128)(2,1)S(1)}, bf16[64,512]{1,0:T(8,128)(2,1)S(1)}, u32[]{:S(2)}, u32[]{:S(2)}) %collective-permute-start.16) | collective-permute-done | bytes 65568 | tf_op jit(solution)/shard_map/ppermute | solution.py:38
  74.4 1.8 %collective-permute-start.14 = (bf16[512,512]{1,0:T(8,128)(2,1)S(1)}, bf16[512,512]{1,0:T(8,128)(2,1)S(1)}, u32[]{:S(2)}, u32[]{:S(2)}) collective-permute-start(bf16[512,512]{1,0:T(8,128)(2,1)S(1)} %add_convert_fusion), channel_id=1, source_target_pairs={{0,8},{4,20},{8,0},{12,28},{16,24},{20,4},{24,16},{28,12},{1,9},{5... | collective-permute-start | bytes 1572872 | tf_op jit(solution)/shard_map/ppermute | solution.py:38
  76.2 1.3 %backward.3 = (f32[512,512]{1,0:T(8,128)S(1)}, bf16[512,512]{1,0:T(8,128)(2,1)S(1)}) custom-call(bf16[4,256,1024]{2,1,0:T(8,128)(2,1)S(1)} %get-tuple-element.44.at_ref, bf16[256,512]{1,0:T(8,128)(2,1)S(1)} %get-tuple-element.35.refs_0_, bf16[256,512]{1,0:T(8,128)(2,1)S(1)} %collective-permute-done.7.refs_1_, bf16[512,512]{1,0:T(8,128)(2,1)S(1)} %collective-permute-done.8.refs_2_), custom_call_target="tpu_custom_call" | custom-call | flops 1073741824 | bytes 4718592 | tf_op jit(solution)/shard_map/backward/pallas_call | solution.py:283
  78.5 2.3 %collective-permute-start.20 = (f32[64,512]{1,0:T(8,128)S(1)}, f32[64,512]{1,0:T(8,128)S(1)}, u32[]{:S(2)}, u32[]{:S(2)}) collective-permute-start(f32[64,512]{1,0:T(8,128)S(1)} %add_multiply_fusion), channel_id=1, source_target_pairs={{0,3},{1,2},{2,1},{3,0},{4,7},{5,6},{6,5},{7,4},{8,11},{9,10},{10,... | collective-permute-start | bytes 393224 | tf_op jit(solution)/shard_map/ppermute | solution.py:48
  82.1 3.0 %collective-permute-done.20 = f32[64,512]{1,0:T(8,128)S(1)} collective-permute-done((f32[64,512]{1,0:T(8,128)S(1)}, f32[64,512]{1,0:T(8,128)S(1)}, u32[]{:S(2)}, u32[]{:S(2)}) %collective-permute-start.20) | collective-permute-done | bytes 131104 | tf_op jit(solution)/shard_map/ppermute | solution.py:48
  85.1 2.2 %collective-permute-done.19 = f32[64,512]{1,0:T(8,128)S(1)} collective-permute-done((f32[64,512]{1,0:T(8,128)S(1)}, f32[64,512]{1,0:T(8,128)S(1)}, u32[]{:S(2)}, u32[]{:S(2)}) %collective-permute-start.19) | collective-permute-done | bytes 131104 | tf_op jit(solution)/shard_map/ppermute | solution.py:48
  87.4 2.0 %collective-permute-done.14 = bf16[512,512]{1,0:T(8,128)(2,1)S(1)} collective-permute-done((bf16[512,512]{1,0:T(8,128)(2,1)S(1)}, bf16[512,512]{1,0:T(8,128)(2,1)S(1)}, u32[]{:S(2)}, u32[]{:S(2)}) %collective-permute-start.14) | collective-permute-done | bytes 524320 | tf_op jit(solution)/shard_map/ppermute | solution.py:38
  89.7 1.4 %collective-permute-start.15 = (bf16[256,512]{1,0:T(8,128)(2,1)S(1)}, bf16[256,512]{1,0:T(8,128)(2,1)S(1)}, u32[]{:S(2)}, u32[]{:S(2)}) collective-permute-start(bf16[256,512]{1,0:T(8,128)(2,1)S(1)} %slice.55), channel_id=1, source_target_pairs={{0,16},{4,12},{8,24},{12,4},{16,0},{20,28},{24,8},{28,20},{1,17},{... | collective-permute-start | bytes 786440 | tf_op jit(solution)/shard_map/ppermute | solution.py:38
  91.1 1.6 %place_slices.1 = f32[512,512]{1,0:T(8,128)} custom-call(s32[2]{0:T(128)S(1)} %pad_add_fusion.place_ref, s32[2,16]{1,0:T(2,128)S(1)} %copy-done.5, f32[4,64,512]{2,1,0:T(8,128)S(1)} %bitcast.9, f32[4,64,512]{2,1,0:T(8,128)S(1)} %bitcast.10), custom_call_target="tpu_custom_call" | custom-call | bytes 2097152 | tf_op jit(solution)/shard_map/place_slices/pallas_call | solution.py:255
  92.7 7.1 %collective-permute-done.15.refs_1_ = bf16[256,512]{1,0:T(8,128)(2,1)S(1)} collective-permute-done((bf16[256,512]{1,0:T(8,128)(2,1)S(1)}, bf16[256,512]{1,0:T(8,128)(2,1)S(1)}, u32[]{:S(2)}, u32[]{:S(2)}) %collective-permute-start.15) | collective-permute-done | bytes 262176 | tf_op jit(solution)/shard_map/ppermute | solution.py:38
  (61 shorter events, 12.3 us)
Async XLA Ops:
  0.6 10.2 %collective-permute-start = (bf16[256,512]{1,0:T(8,128)(2,1)}, bf16[256,512]{1,0:T(8,128)(2,1)S(1)}, u32[]{:S(2)}, u32[]{:S(2)}) collective-permute-start(bf16[256,512]{1,0:T(8,128)(2,1)} %refs_1_.1), channel_id=1, source_target_pairs={{0,16},{4,12},{8,24},{12,4},{16,0},{20,28},{24,8},{28,20},{1,17},{... | collective-permute-start | bytes 786440 | tf_op jit(solution)/shard_map/ppermute | solution.py:38
  11.8 15.2 %collective-permute-start.1 = (bf16[512,512]{1,0:T(8,128)(2,1)S(1)}, bf16[512,512]{1,0:T(8,128)(2,1)S(1)}, u32[]{:S(2)}, u32[]{:S(2)}) collective-permute-start(bf16[512,512]{1,0:T(8,128)(2,1)S(1)} %pad_maximum_fusion), channel_id=1, source_target_pairs={{0,8},{4,20},{8,0},{12,28},{16,24},{20,4},{24,16},{28,12},{1,9},{5... | collective-permute-start | bytes 1572872 | tf_op jit(solution)/shard_map/ppermute | solution.py:38
  14.4 11.4 %collective-permute-start.2 = (bf16[256,512]{1,0:T(8,128)(2,1)}, bf16[256,512]{1,0:T(8,128)(2,1)S(1)}, u32[]{:S(2)}, u32[]{:S(2)}) collective-permute-start(bf16[256,512]{1,0:T(8,128)(2,1)} %refs_1_.1), channel_id=1, source_target_pairs={{0,4},{4,0},{8,12},{12,8},{16,20},{20,16},{24,28},{28,24},{1,5},{5... | collective-permute-start | bytes 786440 | tf_op jit(solution)/shard_map/ppermute | solution.py:32
  14.4 11.4 %collective-permute-start.3 = (bf16[256,512]{1,0:T(8,128)(2,1)S(1)}, bf16[256,512]{1,0:T(8,128)(2,1)S(1)}, u32[]{:S(2)}, u32[]{:S(2)}) collective-permute-start(bf16[256,512]{1,0:T(8,128)(2,1)S(1)} %collective-permute-done.refs_3_), channel_id=1, source_target_pairs={{0,4},{4,0},{8,12},{12,8},{16,20},{20,16},{24,28},{28,24},{1,5},{5... | collective-permute-start | bytes 786440 | tf_op jit(solution)/shard_map/ppermute | solution.py:32
  14.9 2.2 %copy-start = (bf16[1,1,8,16,128,128]{5,4,3,2,1,0:T(8,128)(2,1)S(1)}, bf16[1,1,8,16,128,128]{5,4,3,2,1,0:T(8,128)(2,1)}, u32[]{:S(2)}) copy-start(bf16[1,1,8,16,128,128]{5,4,3,2,1,0:T(8,128)(2,1)} %param.12) | copy-start | bytes 12582916
  17.1 0.7 copy-start.4
  17.8 0.7 copy-start.6
  18.5 0.7 copy-start.7
  19.2 0.7 copy-start.8
  19.9 0.7 copy-start.9
  20.5 5.3 %copy-start.1 = (bf16[256,512]{1,0:T(8,128)(2,1)S(1)}, bf16[256,512]{1,0:T(8,128)(2,1)}, u32[]{:S(2)}) copy-start(bf16[256,512]{1,0:T(8,128)(2,1)} %refs_1_.1) | copy-start | bytes 786436
  27.1 2.0 %collective-permute-start.4 = (bf16[512,512]{1,0:T(8,128)(2,1)S(1)}, bf16[512,512]{1,0:T(8,128)(2,1)S(1)}, u32[]{:S(2)}, u32[]{:S(2)}) collective-permute-start(bf16[512,512]{1,0:T(8,128)(2,1)S(1)} %collective-permute-done.1.refs_1_.refs_3_), channel_id=1, source_target_pairs={{0,4},{4,0},{8,12},{12,8},{16,20},{20,16},{24,28},{28,24},{1,5},{5... | collective-permute-start | bytes 1572872 | tf_op jit(solution)/shard_map/ppermute | solution.py:32
  30.3 9.2 %collective-permute-start.5 = (bf16[512,512]{1,0:T(8,128)(2,1)S(1)}, bf16[512,512]{1,0:T(8,128)(2,1)S(1)}, u32[]{:S(2)}, u32[]{:S(2)}) collective-permute-start(bf16[512,512]{1,0:T(8,128)(2,1)S(1)} %get-tuple-element.29), channel_id=1, source_target_pairs={{0,1},{1,0},{2,3},{3,2},{4,6},{5,7},{6,4},{7,5},{8,9},{9,8},{10,11... | collective-permute-start | bytes 1572872 | tf_op jit(solution)/shard_map/ppermute | solution.py:48
  39.5 6.7 %copy-start.2 = (bf16[512,512]{1,0:T(8,128)(2,1)S(1)}, bf16[512,512]{1,0:T(8,128)(2,1)}, u32[]{:S(2)}) copy-start(bf16[512,512]{1,0:T(8,128)(2,1)} %refs_3_.1) | copy-start | bytes 1572868
  39.5 6.7 %copy-start.3 = (bf16[256,512]{1,0:T(8,128)(2,1)S(1)}, bf16[256,512]{1,0:T(8,128)(2,1)}, u32[]{:S(2)}) copy-start(bf16[256,512]{1,0:T(8,128)(2,1)} %refs_2_.1) | copy-start | bytes 786436
  39.7 7.7 %copy-start.5 = (s32[2,16]{1,0:T(2,128)S(1)}, s32[2,16]{1,0:T(2,128)}, u32[]{:S(2)}) copy-start(s32[2,16]{1,0:T(2,128)} %constant.16.clone.slot_ref) | copy-start | bytes 388
  39.8 6.4 %collective-permute-start.6 = (bf16[256,512]{1,0:T(8,128)(2,1)S(1)}, bf16[256,512]{1,0:T(8,128)(2,1)S(1)}, u32[]{:S(2)}, u32[]{:S(2)}) collective-permute-start(bf16[256,512]{1,0:T(8,128)(2,1)S(1)} %slice.56), channel_id=1, source_target_pairs={{0,2},{1,3},{2,0},{3,1},{4,5},{5,4},{6,7},{7,6},{8,10},{9,11},{10,... | collective-permute-start | bytes 786440 | tf_op jit(solution)/shard_map/ppermute | solution.py:48
  48.3 1.7 %collective-permute-start.9 = (bf16[4,64,512]{2,1,0:T(8,128)(2,1)S(1)}, bf16[4,64,512]{2,1,0:T(8,128)(2,1)S(1)}, u32[]{:S(2)}, u32[]{:S(2)}) collective-permute-start(bf16[4,64,512]{2,1,0:T(8,128)(2,1)S(1)} %get-tuple-element.39), channel_id=1, source_target_pairs={{0,4},{4,0},{8,12},{12,8},{16,20},{20,16},{24,28},{28,24},{1,5},{5... | collective-permute-start | bytes 786440 | tf_op jit(solution)/shard_map/ppermute | solution.py:32
  48.4 6.4 %collective-permute-start.7 = (bf16[256,512]{1,0:T(8,128)(2,1)S(1)}, bf16[256,512]{1,0:T(8,128)(2,1)S(1)}, u32[]{:S(2)}, u32[]{:S(2)}) collective-permute-start(bf16[256,512]{1,0:T(8,128)(2,1)S(1)} %get-tuple-element.35.refs_0_), channel_id=1, source_target_pairs={{0,2},{1,3},{2,0},{3,1},{4,5},{5,4},{6,7},{7,6},{8,10},{9,11},{10,... | collective-permute-start | bytes 786440 | tf_op jit(solution)/shard_map/ppermute | solution.py:48
  54.9 5.0 %collective-permute-start.10 = (bf16[128,512]{1,0:T(8,128)(2,1)S(1)}, bf16[128,512]{1,0:T(8,128)(2,1)S(1)}, u32[]{:S(2)}, u32[]{:S(2)}) collective-permute-start(bf16[128,512]{1,0:T(8,128)(2,1)S(1)} %bitcast.11), channel_id=1, source_target_pairs={{0,1},{1,0},{2,3},{3,2},{4,6},{5,7},{6,4},{7,5},{8,9},{9,8},{10,11... | collective-permute-start | bytes 393224 | tf_op jit(solution)/shard_map/ppermute | solution.py:48
  56.6 9.9 %collective-permute-start.8 = (bf16[512,512]{1,0:T(8,128)(2,1)S(1)}, bf16[512,512]{1,0:T(8,128)(2,1)S(1)}, u32[]{:S(2)}, u32[]{:S(2)}) collective-permute-start(bf16[512,512]{1,0:T(8,128)(2,1)S(1)} %pad_maximum_fusion.1), channel_id=1, source_target_pairs={{0,1},{1,0},{2,3},{3,2},{4,6},{5,7},{6,4},{7,5},{8,9},{9,8},{10,11... | collective-permute-start | bytes 1572872 | tf_op jit(solution)/shard_map/ppermute | solution.py:48
  60.0 4.9 %collective-permute-start.11 = (bf16[64,512]{1,0:T(8,128)(2,1)S(1)}, bf16[64,512]{1,0:T(8,128)(2,1)S(1)}, u32[]{:S(2)}, u32[]{:S(2)}) collective-permute-start(bf16[64,512]{1,0:T(8,128)(2,1)S(1)} %slice.58), channel_id=1, source_target_pairs={{0,2},{1,3},{2,0},{3,1},{4,5},{5,4},{6,7},{7,6},{8,10},{9,11},{10,... | collective-permute-start | bytes 196616 | tf_op jit(solution)/shard_map/ppermute | solution.py:48
  67.8 6.4 %collective-permute-start.12 = (bf16[512,512]{1,0:T(8,128)(2,1)S(1)}, bf16[512,512]{1,0:T(8,128)(2,1)S(1)}, u32[]{:S(2)}, u32[]{:S(2)}) collective-permute-start(bf16[512,512]{1,0:T(8,128)(2,1)S(1)} %get-tuple-element.43), channel_id=1, source_target_pairs={{0,4},{4,0},{8,12},{12,8},{16,20},{20,16},{24,28},{28,24},{1,5},{5... | collective-permute-start | bytes 1572872 | tf_op jit(solution)/shard_map/ppermute | solution.py:32
  67.9 5.9 %collective-permute-start.16 = (bf16[64,512]{1,0:T(8,128)(2,1)S(1)}, bf16[64,512]{1,0:T(8,128)(2,1)S(1)}, u32[]{:S(2)}, u32[]{:S(2)}) collective-permute-start(bf16[64,512]{1,0:T(8,128)(2,1)S(1)} %fusion), channel_id=1, source_target_pairs={{0,16},{4,12},{8,24},{12,4},{16,0},{20,28},{24,8},{28,20},{1,17},{... | collective-permute-start | bytes 196616 | tf_op jit(solution)/shard_map/ppermute | solution.py:38
  73.8 4.6 %collective-permute-start.17 = (bf16[64,512]{1,0:T(8,128)(2,1)S(1)}, bf16[64,512]{1,0:T(8,128)(2,1)S(1)}, u32[]{:S(2)}, u32[]{:S(2)}) collective-permute-start(bf16[64,512]{1,0:T(8,128)(2,1)S(1)} %add_convert_fusion.1), channel_id=1, source_target_pairs={{0,8},{4,20},{8,0},{12,28},{16,24},{20,4},{24,16},{28,12},{1,9},{5... | collective-permute-start | bytes 196616 | tf_op jit(solution)/shard_map/ppermute | solution.py:38
  74.4 15.0 %collective-permute-start.14 = (bf16[512,512]{1,0:T(8,128)(2,1)S(1)}, bf16[512,512]{1,0:T(8,128)(2,1)S(1)}, u32[]{:S(2)}, u32[]{:S(2)}) collective-permute-start(bf16[512,512]{1,0:T(8,128)(2,1)S(1)} %add_convert_fusion), channel_id=1, source_target_pairs={{0,8},{4,20},{8,0},{12,28},{16,24},{20,4},{24,16},{28,12},{1,9},{5... | collective-permute-start | bytes 1572872 | tf_op jit(solution)/shard_map/ppermute | solution.py:38
  77.4 12.0 %collective-permute-start.13 = (bf16[512,512]{1,0:T(8,128)(2,1)S(1)}, bf16[512,512]{1,0:T(8,128)(2,1)S(1)}, u32[]{:S(2)}, u32[]{:S(2)}) collective-permute-start(bf16[512,512]{1,0:T(8,128)(2,1)S(1)} %get-tuple-element.46), channel_id=1, source_target_pairs={{0,4},{4,0},{8,12},{12,8},{16,20},{20,16},{24,28},{28,24},{1,5},{5... | collective-permute-start | bytes 1572872 | tf_op jit(solution)/shard_map/ppermute | solution.py:32
  78.5 6.6 %collective-permute-start.20 = (f32[64,512]{1,0:T(8,128)S(1)}, f32[64,512]{1,0:T(8,128)S(1)}, u32[]{:S(2)}, u32[]{:S(2)}) collective-permute-start(f32[64,512]{1,0:T(8,128)S(1)} %add_multiply_fusion), channel_id=1, source_target_pairs={{0,3},{1,2},{2,1},{3,0},{4,7},{5,6},{6,5},{7,4},{8,11},{9,10},{10,... | collective-permute-start | bytes 393224 | tf_op jit(solution)/shard_map/ppermute | solution.py:48
  80.8 6.5 %collective-permute-start.19 = (f32[64,512]{1,0:T(8,128)S(1)}, f32[64,512]{1,0:T(8,128)S(1)}, u32[]{:S(2)}, u32[]{:S(2)}) collective-permute-start(f32[64,512]{1,0:T(8,128)S(1)} %add_multiply_fusion), channel_id=1, source_target_pairs={{0,1},{1,0},{2,3},{3,2},{4,6},{5,7},{6,4},{7,5},{8,9},{9,8},{10,11... | collective-permute-start | bytes 393224 | tf_op jit(solution)/shard_map/ppermute | solution.py:48
  81.6 5.7 %collective-permute-start.18 = (f32[64,512]{1,0:T(8,128)S(1)}, f32[64,512]{1,0:T(8,128)S(1)}, u32[]{:S(2)}, u32[]{:S(2)}) collective-permute-start(f32[64,512]{1,0:T(8,128)S(1)} %add_multiply_fusion), channel_id=1, source_target_pairs={{0,2},{1,3},{2,0},{3,1},{4,5},{5,4},{6,7},{7,6},{8,10},{9,11},{10,... | collective-permute-start | bytes 393224 | tf_op jit(solution)/shard_map/ppermute | solution.py:48
  87.3 3.7 %collective-permute-start.21 = (f32[256,512]{1,0:T(8,128)S(1)}, f32[256,512]{1,0:T(8,128)S(1)}, u32[]{:S(2)}, u32[]{:S(2)}) collective-permute-start(f32[256,512]{1,0:T(8,128)S(1)} %pad_maximum_fusion.2), channel_id=1, source_target_pairs={{0,4},{4,0},{8,12},{12,8},{16,20},{20,16},{24,28},{28,24},{1,5},{5... | collective-permute-start | bytes 1572872 | tf_op jit(solution)/shard_map/ppermute | solution.py:32
  89.7 10.1 %collective-permute-start.15 = (bf16[256,512]{1,0:T(8,128)(2,1)S(1)}, bf16[256,512]{1,0:T(8,128)(2,1)S(1)}, u32[]{:S(2)}, u32[]{:S(2)}) collective-permute-start(bf16[256,512]{1,0:T(8,128)(2,1)S(1)} %slice.55), channel_id=1, source_target_pairs={{0,16},{4,12},{8,24},{12,4},{16,0},{20,28},{24,8},{28,20},{1,17},{... | collective-permute-start | bytes 786440 | tf_op jit(solution)/shard_map/ppermute | solution.py:38

commit v5 on v2

v5 whole, which is shorter than its diff:
```python
import functools

import jax
import jax.numpy as jnp
from jax import lax
from jax.experimental import pallas as pl
from jax.experimental.pallas import tpu as pltpu
from jax.sharding import PartitionSpec as P

WHOLE = pl.BlockSpec(memory_space=pltpu.VMEM)
SCALARS = pl.BlockSpec(memory_space=pltpu.SMEM)


def bit_count(n):
    return n.bit_length() - 1


def between(index, core, bits):
    reverse = 0
    for i in range(bits):
        reverse = reverse | (((index >> i) & 1) << (bits - 1 - i))
    return core * index + (1 - core) * reverse


def swap_cores(x):
    return lax.ppermute(x, "dom", [(i, i ^ 1) for i in range(lax.axis_size("dom"))])


def swap_chips(x, held):
    blocks = lax.axis_size("dom")
    bits = bit_count(blocks // 2)
    return lax.ppermute(x, "dom", [(i, i ^ (2 * between(held, i % 2, bits))) for i in range(blocks)])


def swap_members(x, held, turn=0):
    blocks, groups = lax.axis_size("dom"), lax.axis_size("repl")
    bits = bit_count(groups)
    pairs = []
    for i in range(blocks):
        for j in range(groups):
            pairs.append((i * groups + j, i * groups + (j ^ between(held, (i % 2) ^ turn, bits))))
    return lax.ppermute(x, ("dom", "repl"), pairs)


def after(x, *others):
    return lax.optimization_barrier((x, *others))[0]


def params(mib):
    return pltpu.CompilerParams(vmem_limit_bytes=mib * 1024 * 1024)


def like(shape, dtype):
    return jax.ShapeDtypeStruct(shape, dtype)


def bf16_dot(a, b):
    return jnp.dot(a, b, preferred_element_type=jnp.float32)


def column_of(position, j, blocks):
    core = (position & 1) ^ (j & 1)
    return (((position >> 1) ^ between(j >> 1, core, bit_count(blocks // 2))) << 1) | core


def densify_kernel(spots_ref, place_ref, tiles_ref, a_ref, acc_ref, *, col_tiles):
    column = column_of(place_ref[0], pl.program_id(0), pl.num_programs(0))
    size = tiles_ref.shape[-1]
    count = tiles_ref.shape[1]
    acc_ref[...] = jnp.zeros_like(acc_ref)

    def add(tile, carry):
        acc_ref[spots_ref[column, tile]] += tiles_ref[0, tile].astype(jnp.float32)
        return carry

    lax.fori_loop(0, spots_ref[column, count], add, 0)
    for spot in range(acc_ref.shape[0]):
        row, col = spot // col_tiles, spot % col_tiles
        a_ref[0, row * size:(row + 1) * size, col * size:(col + 1) * size] = acc_ref[spot].astype(a_ref.dtype)


def densify(tiles, spots, place, group_count, rows_local):
    columns, count, size, _ = tiles.shape
    col_tiles = rows_local // size
    rows = group_count * rows_local
    return pl.pallas_call(
        functools.partial(densify_kernel, col_tiles=col_tiles),
        out_shape=like((columns, rows, rows_local), jnp.bfloat16),
        grid_spec=pltpu.PrefetchScalarGridSpec(
            num_scalar_prefetch=2,
            grid=(columns,),
            in_specs=[pl.BlockSpec((1, count, size, size), lambda j, s, p: (column_of(p[0], j, columns), 0, 0, 0))],
            out_specs=pl.BlockSpec((1, rows, rows_local), lambda j, *_: (j, 0, 0)),
            scratch_shapes=[pltpu.VMEM((group_count * col_tiles * col_tiles, size, size), jnp.float32)],
        ),
        compiler_params=params(12),
        cost_estimate=pl.CostEstimate(
            flops=columns * count * size * size, bytes_accessed=8 * rows * columns * rows_local, transcendentals=0),
        name="densify",
    )(spots, place, tiles)


def transpose_kernel(a_ref, *outs):
    for i, out_ref in enumerate(outs):
        for side in range(2):
            out_ref[side] = a_ref[2 * i + side].T


def transposed(dense):
    columns, rows, cols = dense.shape
    return pl.pallas_call(
        transpose_kernel,
        out_shape=[like((2, cols, rows), jnp.bfloat16)] * (columns // 2),
        in_specs=[WHOLE],
        out_specs=[WHOLE] * (columns // 2),
        compiler_params=params(8),
        cost_estimate=pl.CostEstimate(flops=0, bytes_accessed=4 * columns * rows * cols, transcendentals=0),
        name="transposed",
    )(dense)


def forward_kernel(*refs, first, count, slots, has_prev):
    dense_ref, sources = refs[0], refs[1:1 + count]
    rest = refs[1 + count:]
    prev, outs = (rest[:slots], rest[slots:]) if has_prev else (None, rest)
    rows = outs[0].shape[0]
    for k, out_ref in reversed(list(enumerate(outs))):
        total = prev[k][...] if has_prev else None
        for j, source in enumerate(sources):
            part = bf16_dot(dense_ref[first + j, k * rows:(k + 1) * rows, :], source[...])
            total = part if total is None else total + part
        out_ref[...] = total.astype(out_ref.dtype)


def forward(dense, first, sources, prev, dtypes):
    slots = len(dtypes)
    _, rows, depth = dense.shape
    width = sources[0].shape[1]
    return pl.pallas_call(
        functools.partial(
            forward_kernel, first=first, count=len(sources), slots=slots, has_prev=prev is not None),
        out_shape=[like((rows // slots, width), dtype) for dtype in dtypes],
        in_specs=[WHOLE] * (1 + len(sources) + (slots if prev is not None else 0)),
        out_specs=[WHOLE] * slots,
        compiler_params=params(8),
        cost_estimate=pl.CostEstimate(
            flops=2 * len(sources) * rows * depth * width,
            bytes_accessed=2 * len(sources) * rows * depth + 4 * rows * width, transcendentals=0),
        name="forward",
    )(dense, *sources, *(prev or []))


def middle_kernel(*refs):
    pieces, (cot_ref, weight_ref, act_ref, agg_ref, pre_grad_ref, grad_ref) = refs[:-6], refs[-6:]
    agg = pieces[0][...]
    for piece in pieces[1:]:
        agg = agg + piece[...].astype(jnp.float32)
    agg = agg.astype(jnp.bfloat16)
    agg_ref[...] = agg
    weight = weight_ref[...]
    preact = bf16_dot(agg, weight)
    sigma = jax.nn.sigmoid(preact)
    act_ref[...] = (preact * sigma).astype(act_ref.dtype)
    slope = sigma * (1.0 + preact * (1.0 - sigma))
    pre_grad = (cot_ref[...].astype(jnp.float32) * slope).astype(jnp.bfloat16)
    pre_grad_ref[...] = pre_grad
    grad_ref[...] = lax.dot_general(
        pre_grad, weight, (((1,), (1,)), ((), ())), preferred_element_type=jnp.float32
    ).astype(jnp.bfloat16)


def middle(pieces, cotangent, weight):
    rows, width = cotangent.shape
    return pl.pallas_call(
        middle_kernel,
        out_shape=[like((rows, width), jnp.bfloat16)] * 4,
        in_specs=[WHOLE] * (2 + len(pieces)),
        out_specs=[WHOLE] * 4,
        compiler_params=params(8),
        cost_estimate=pl.CostEstimate(
            flops=4 * rows * width * width, bytes_accessed=10 * rows * width, transcendentals=rows * width),
        name="middle",
    )(*pieces, cotangent, weight)


def weight_kernel(place_ref, agg_ref, pre_grad_ref, *refs, groups):
    owns, send_ref, part_ref = refs[:groups], refs[groups], refs[groups + 1]
    core, member = place_ref[0] & 1, place_ref[1]
    rows = owns[0].shape[0]
    bits = bit_count(groups)
    part_ref[...] = lax.dot_general(
        agg_ref[...], pre_grad_ref[...], (((0,), (0,)), ((), ())), preferred_element_type=jnp.float32
    )

    def piece(k, side):
        start = (2 * (member ^ between(k, 1 - side, bits)) + side) * rows
        return part_ref[pl.ds(pl.multiple_of(start, rows), rows), :]

    for k in range(groups):
        owns[k][...] = piece(k, core)
        send_ref[k * rows:(k + 1) * rows, :] = piece(k, 1 - core).astype(send_ref.dtype)


def weight_part(agg, pre_grad, place, groups):
    rows, width = agg.shape
    part = width // (2 * groups)
    out = pl.pallas_call(
        functools.partial(weight_kernel, groups=groups),
        out_shape=[like((part, width), jnp.float32)] * groups + [like((groups * part, width), jnp.bfloat16)],
        in_specs=[SCALARS, WHOLE, WHOLE],
        out_specs=[WHOLE] * (groups + 1),
        scratch_shapes=[pltpu.VMEM((width, width), jnp.float32)],
        compiler_params=params(8),
        cost_estimate=pl.CostEstimate(
            flops=2 * rows * width * width, bytes_accessed=4 * rows * width + 4 * width * width, transcendentals=0),
        name="weight_part",
    )(place, agg, pre_grad)
    return out[:-1], out[-1]


def place_kernel(place_ref, *refs, groups):
    owns, other_ref, out_ref = refs[:groups], refs[groups], refs[groups + 1]
    core, member = place_ref[0] & 1, place_ref[1]
    rows = owns[0].shape[0]
    bits = bit_count(groups)
    for k in range(groups):
        for side, value in ((core, owns[k][...]), (1 - core, other_ref[k * rows:(k + 1) * rows, :])):
            start = (2 * (member ^ between(k, 1 - side, bits)) + side) * rows
            out_ref[pl.ds(pl.multiple_of(start, rows), rows), :] = value


def place_slices(owns, other, place):
    groups = len(owns)
    rows, width = owns[0].shape
    return pl.pallas_call(
        functools.partial(place_kernel, groups=groups),
        out_shape=like((2 * groups * rows, width), jnp.float32),
        in_specs=[SCALARS] + [WHOLE] * (groups + 1),
        out_specs=WHOLE,
        compiler_params=params(8),
        cost_estimate=pl.CostEstimate(flops=0, bytes_accessed=16 * groups * rows * width, transcendentals=0),
        name="place_slices",
    )(place, *owns, other)


def backward_kernel(*refs, count, slots):
    blocks, grads = refs[:count], refs[count:count + slots]
    owns, other_ref = refs[count + slots:-1], refs[-1]
    rows = owns[0].shape[0]
    for side in (1, 0):
        for i, block in enumerate(blocks):
            total, start = None, 0
            for grad in grads:
                stop = start + grad.shape[0]
                part = bf16_dot(block[side, :, start:stop], grad[...])
                total, start = part if total is None else total + part, stop
            if side:
                other_ref[i * rows:(i + 1) * rows, :] = total.astype(other_ref.dtype)
            else:
                owns[i][...] = total


def backward(blocks, grads):
    _, cols, rows = blocks[0].shape
    width = grads[0].shape[1]
    count = len(blocks)
    out = pl.pallas_call(
        functools.partial(backward_kernel, count=count, slots=len(grads)),
        out_shape=[like((cols, width), jnp.float32)] * count + [like((count * cols, width), jnp.bfloat16)],
        in_specs=[WHOLE] * (count + len(grads)),
        out_specs=[WHOLE] * (count + 1),
        compiler_params=params(8),
        cost_estimate=pl.CostEstimate(
            flops=4 * count * cols * rows * width,
            bytes_accessed=4 * count * cols * rows + 2 * rows * width + 6 * count * cols * width, transcendentals=0),
        name="backward",
    )(*blocks, *grads)
    return out[:-1], out[-1]


def finish_kernel(*refs):
    total = refs[0][...]
    for ref in refs[1:-1]:
        total = total + ref[...].astype(jnp.float32)
    refs[-1][...] = total.astype(refs[-1].dtype)


def finish(parts):
    rows, width = parts[0].shape
    return pl.pallas_call(
        finish_kernel,
        out_shape=like((rows, width), jnp.bfloat16),
        in_specs=[WHOLE] * len(parts),
        out_specs=WHOLE,
        compiler_params=params(8),
        cost_estimate=pl.CostEstimate(flops=rows * width, bytes_accessed=8 * rows * width, transcendentals=0),
        name="finish",
    )(*parts)


def top_bit(slot):
    return 1 << (slot.bit_length() - 1)


def halve(totals, swap):
    while True:
        half = len(totals) // 2
        send = [total.astype(jnp.bfloat16) for total in totals[half:]]
        got = swap(jnp.concatenate(send) if half > 1 else send[0], half)
        if half == 1:
            return [totals[0], got]
        totals = add_slots(totals[:half], got)


def add_slots(totals, got):
    rows = totals[0].shape[0]
    return [total + got[k * rows:(k + 1) * rows].astype(jnp.float32) for k, total in enumerate(totals)]


def collect(totals, swap):
    totals = list(totals)
    arrived = []
    for k in reversed(range(1, len(totals))):
        got = swap(totals[k].astype(jnp.bfloat16), top_bit(k))
        if k == top_bit(k):
            arrived.append(got)
        else:
            totals[k - top_bit(k)] = totals[k - top_bit(k)].astype(jnp.float32) + got.astype(jnp.float32)
    return [totals[0], *arrived]


def local(features, cotangent, weight, tiles, tile_rows, tile_cols, tile_counts):
    blocks = lax.axis_size("dom")
    groups = lax.axis_size("repl")
    chips = blocks // 2
    rows_local, width = features.shape
    scale = float(rows_local * blocks * groups) ** (-0.5)
    position, member = lax.axis_index("dom"), lax.axis_index("repl")
    place = jnp.stack([position, member]).astype(jnp.int32)

    col_tiles = rows_local // tiles.shape[-1]
    row = tile_rows[0, 0]
    row = between((row // col_tiles) ^ member, position & 1, bit_count(groups)) * col_tiles + row % col_tiles
    spots = jnp.concatenate([row * col_tiles + tile_cols[0, 0], tile_counts[0, 0][:, None]], axis=1)
    dense = densify(tiles[0, 0], spots, place, groups, rows_local)

    held = [features]
    for k in range(1, chips):
        held.append(swap_chips(held[k - top_bit(k)], top_bit(k)))
    totals = None
    for first, stop in ((0, chips // 2), (chips // 2, chips)):
        sources = []
        for k in range(first, stop):
            own = held[k] if totals is None else after(held[k], held[-1], *totals)
            sources += [own, swap_cores(own)]
        dtypes = [jnp.float32] * groups
        if stop == chips:
            dtypes = [jnp.float32 if k < groups // 2 else jnp.bfloat16 for k in range(groups)]
        totals = forward(dense, 2 * first, sources, totals, dtypes)

    pieces = collect(totals, swap_members)
    dense_t = transposed(after(dense, *totals))
    pieces[-1] = after(pieces[-1], *dense_t)
    activated, agg, pre_grad, grad = middle(pieces, cotangent, weight)
    owns, send = weight_part(agg, pre_grad, place, groups)
    parts = add_slots(owns, swap_cores(send))

    grads = [grad]
    while sum(x.shape[0] for x in grads) < groups * rows_local:
        slots = sum(x.shape[0] for x in grads) // rows_local
        grads.append(swap_members(jnp.concatenate(grads) if slots > 1 else grad, slots))
        if slots == 1:
            parts[-1] = after(parts[-1], grads[-1])
            kept, got = halve(parts, functools.partial(swap_members, turn=1))
            part = (kept + got.astype(jnp.float32)).astype(jnp.bfloat16)
    grads[-1] = after(grads[-1], part)

    half = chips // 2
    own, other = backward(dense_t[half:], grads)
    high = jnp.concatenate(add_slots(own, swap_cores(other))).astype(jnp.bfloat16)
    own, other = backward([after(dense_t[0], high), *dense_t[1:half]], grads)
    low = add_slots(own, swap_cores(other))
    feature_grad = finish(halve(add_slots(low, swap_chips(high, half)), swap_chips))

    bit = 1
    while bit < chips:
        part = part.astype(jnp.float32) + swap_chips(part, bit).astype(jnp.float32)
        bit *= 2
        part = part.astype(jnp.bfloat16) if bit < chips else part * scale
    parts = [part] + [swap_members(part, k, turn=1) for k in range(1, groups)]
    weight_grad = place_slices(parts, swap_cores(jnp.concatenate(parts)), place)
    return (activated, feature_grad, weight_grad)


def solution(mesh):
    in_specs = (
        P(("dom", "repl"), None),
        P(("dom", "repl"), None),
        P(),
        P("dom", "repl", None, None, None, None),
        P("dom", "repl", None, None),
        P("dom", "repl", None, None),
        P("dom", "repl", None),
    )
    out_specs = (P(("dom", "repl"), None), P(("dom", "repl"), None), P())
    return jax.shard_map(local, mesh=mesh, in_specs=in_specs, out_specs=out_specs, check_vma=False)
```

time: 108 us -> 100 us (0.926)
  local copies, waits for them, and re-layouts: 12.5 us -> 2.93 us
  waiting for transfers between devices: 48.1 us -> 53.2 us
  starting transfers between devices: 31.2 us -> 27.6 us
    unnamed x21 -> x8, local copies, waits for them, and re-layouts: 9.23 us -> 2.2 us
    ppermute x31 -> x25, waiting for transfers between devices: 48.1 us -> 53.2 us  [the longest x10 26.2 us: swap_members(): return lax.ppermute(x, ('dom', 'repl'), pairs)]
    ppermute x31 -> x25, starting transfers between devices: 31.2 us -> 27.6 us  [the longest x10 14.7 us: swap_members(): return lax.ppermute(x, ('dom', 'repl'), pairs)]
    gather x1 -> x0, local copies, waits for them, and re-layouts: 1.59 us -> none  [local(): weight_grad = both[order].reshape(weight.shape)]
    reshape x2 -> x0, local copies, waits for them, and re-layouts: 1.53 us -> none  [the longest x1 0.77 us: densify(): tile_cols.reshape(-1)]
  transfers between devices with their start and end apart: 31 -> 25, of which waited for: 17 -> 15; matrix products, arithmetic and copies ran while one was open for 3% -> 2% of each run, Pallas kernels for 10% -> 9%
where the time goes in v5:
time: 100 us
  waiting for transfers between devices  53.2 us (53%)
  starting transfers between devices  27.6 us (28%)
  Pallas kernels  13.9 us (14%)
  local copies, waits for them, and re-layouts  2.93 us (3%)
  other arithmetic  1.56 us (2%)
    ppermute x10, waiting for transfers between devices, swap_members(): return lax.ppermute(x, ('dom', 'repl'), pairs)  26.2 us
    ppermute x7, waiting for transfers between devices, swap_chips(): lax.ppermute(x, 'dom', [(i, i ^ 2 * between(held, i % 2, bits)) for i in...  25.5 us
    ppermute x10, starting transfers between devices, swap_members(): return lax.ppermute(x, ('dom', 'repl'), pairs)  14.7 us
    ppermute x7, starting transfers between devices, swap_chips(): lax.ppermute(x, 'dom', [(i, i ^ 2 * between(held, i % 2, bits)) for i in...  12 us
    pallas_call x1, Pallas kernels, densify(): pl.pallas_call(functools.partial(densify_kernel, col_tiles=col_tiles), ou...  3.33 us
    pallas_call x2, Pallas kernels, forward(): pl.pallas_call(functools.partial(forward_kernel, first=first, count=len(s...  2.49 us
    pallas_call x2, Pallas kernels, backward(): pl.pallas_call(functools.partial(backward_kernel, count=count, slots=len(...  2.48 us
    unnamed x8, local copies, waits for them, and re-layouts  2.2 us
  transfers between devices with their start and end apart: 25, of which 15 were waited for; matrix products, arithmetic and copies ran while one was open for 2% of the time, Pallas kernels for 9%

profile of v5, /device:TPU:0, one launch (start us, length us, event | category | flops | bytes accessed | tf_op | source)
XLA Modules:
  0.0 100.0 jit_solution(6513871293234721115)
XLA Ops:
  0.6 4.1 %collective-permute-start.1 = (bf16[256,512]{1,0:T(8,128)(2,1)}, bf16[256,512]{1,0:T(8,128)(2,1)S(1)}, u32[]{:S(2)}, u32[]{:S(2)}) collective-permute-start(bf16[256,512]{1,0:T(8,128)(2,1)} %refs_1_.1), channel_id=1, source_target_pairs={{0,16},{4,12},{8,24},{12,4},{16,0},{20,28},{24,8},{28,20},{1,17},{... | collective-permute-start | bytes 786440 | tf_op jit(solution)/shard_map/ppermute | solution.py:32
  4.7 1.6 %collective-permute-start = (bf16[256,512]{1,0:T(8,128)(2,1)}, bf16[256,512]{1,0:T(8,128)(2,1)S(1)}, u32[]{:S(2)}, u32[]{:S(2)}) collective-permute-start(bf16[256,512]{1,0:T(8,128)(2,1)} %refs_1_.1), channel_id=1, source_target_pairs={{0,8},{4,20},{8,0},{12,28},{16,24},{20,4},{24,16},{28,12},{1,9},{5... | collective-permute-start | bytes 786440 | tf_op jit(solution)/shard_map/ppermute | solution.py:32
  6.3 11.0 %collective-permute-done.1.refs_3_ = bf16[256,512]{1,0:T(8,128)(2,1)S(1)} collective-permute-done((bf16[256,512]{1,0:T(8,128)(2,1)}, bf16[256,512]{1,0:T(8,128)(2,1)S(1)}, u32[]{:S(2)}, u32[]{:S(2)}) %collective-permute-start.1) | collective-permute-done | bytes 262176 | tf_op jit(solution)/shard_map/ppermute | solution.py:32
  19.7 2.2 %copy-done = bf16[1,1,8,16,128,128]{5,4,3,2,1,0:T(8,128)(2,1)S(1)} copy-done((bf16[1,1,8,16,128,128]{5,4,3,2,1,0:T(8,128)(2,1)S(1)}, bf16[1,1,8,16,128,128]{5,4,3,2,1,0:T(8,128)(2,1)}, u32[]{:S(2)}) %copy-start) | copy-done | bytes 4194328
  21.8 3.3 %densify.1.refs_0_.a_ref = bf16[8,1024,256]{2,1,0:T(8,128)(2,1)S(1)} custom-call(s32[8,17]{1,0:T(8,128)S(1)} %pad_add_fusion.spots_ref, s32[2]{0:T(128)S(1)} %pad_add_fusion.1.place_ref, bf16[8,16,128,128]{3,2,1,0:T(8,128)(2,1)S(1)} %bitcast.26), custom_call_target="tpu_custom_call" | custom-call | flops 2097152 | bytes 16777216 | tf_op jit(solution)/shard_map/densify/pallas_call | solution.py:86
  25.2 1.2 %forward.2 = (f32[256,512]{1,0:T(8,128)S(1)}, f32[256,512]{1,0:T(8,128)S(1)}, f32[256,512]{1,0:T(8,128)S(1)}, f32[256,512]{1,0:T(8,128)S(1)}) custom-call(bf16[8,1024,256]{2,1,0:T(8,128)(2,1)S(1)} %densify.1.refs_0_.a_ref, bf16[256,512]{1,0:T(8,128)(2,1)S(1)} %copy-done.2, bf16[256,512]{1,0:T(8,128)(2,1)S(1)} %collective-permute-done.3.refs_2_, ...), custom_call_target="tpu_custom_call" | custom-call | flops 1073741824 | bytes 4194304 | tf_op jit(solution)/shard_map/forward/pallas_call | solution.py:139
  29.2 1.2 %forward.3 = (f32[256,512]{1,0:T(8,128)S(1)}, f32[256,512]{1,0:T(8,128)S(1)}, bf16[256,512]{1,0:T(8,128)(2,1)S(1)}, bf16[256,512]{1,0:T(8,128)(2,1)S(1)}) custom-call(bf16[8,1024,256]{2,1,0:T(8,128)(2,1)S(1)} %densify.1.refs_0_.a_ref, bf16[256,512]{1,0:T(8,128)(2,1)S(1)} %collective-permute-done.refs_1_, ...), custom_call_target="tpu_custom_call" | custom-call | flops 1073741824 | bytes 4194304 | tf_op jit(solution)/shard_map/forward/pallas_call | solution.py:139
  30.5 2.0 %collective-permute-start.8 = (bf16[256,512]{1,0:T(8,128)(2,1)S(1)}, bf16[256,512]{1,0:T(8,128)(2,1)S(1)}, u32[]{:S(2)}, u32[]{:S(2)}) collective-permute-start(bf16[256,512]{1,0:T(8,128)(2,1)S(1)} %get-tuple-element.46), channel_id=1, source_target_pairs={{0,1},{1,0},{2,3},{3,2},{4,6},{5,7},{6,4},{7,5},{8,9},{9,8},{10,11... | collective-permute-start | bytes 786440 | tf_op jit(solution)/shard_map/ppermute | solution.py:42
  32.5 4.4 %collective-permute-done.8 = bf16[256,512]{1,0:T(8,128)(2,1)S(1)} collective-permute-done((bf16[256,512]{1,0:T(8,128)(2,1)S(1)}, bf16[256,512]{1,0:T(8,128)(2,1)S(1)}, u32[]{:S(2)}, u32[]{:S(2)}) %collective-permute-start.8) | collective-permute-done | bytes 262176 | tf_op jit(solution)/shard_map/ppermute | solution.py:42
  37.0 2.1 %collective-permute-start.9 = (bf16[256,512]{1,0:T(8,128)(2,1)S(1)}, bf16[256,512]{1,0:T(8,128)(2,1)S(1)}, u32[]{:S(2)}, u32[]{:S(2)}) collective-permute-start(bf16[256,512]{1,0:T(8,128)(2,1)S(1)} %add_convert_fusion.3), channel_id=1, source_target_pairs={{0,2},{1,3},{2,0},{3,1},{4,5},{5,4},{6,7},{7,6},{8,10},{9,11},{10,... | collective-permute-start | bytes 786440 | tf_op jit(solution)/shard_map/ppermute | solution.py:42
  39.1 1.5 %collective-permute-start.7 = (bf16[256,512]{1,0:T(8,128)(2,1)S(1)}, bf16[256,512]{1,0:T(8,128)(2,1)S(1)}, u32[]{:S(2)}, u32[]{:S(2)}) collective-permute-start(bf16[256,512]{1,0:T(8,128)(2,1)S(1)} %get-tuple-element.44), channel_id=1, source_target_pairs={{0,1},{1,0},{2,3},{3,2},{4,6},{5,7},{6,4},{7,5},{8,9},{9,8},{10,11... | collective-permute-start | bytes 786440 | tf_op jit(solution)/shard_map/ppermute | solution.py:42
  40.6 1.2 %transposed.1 = (bf16[2,256,1024]{2,1,0:T(8,128)(2,1)S(1)}, bf16[2,256,1024]{2,1,0:T(8,128)(2,1)S(1)}, bf16[2,256,1024]{2,1,0:T(8,128)(2,1)S(1)}, bf16[2,256,1024]{2,1,0:T(8,128)(2,1)S(1)}) custom-call(bf16[8,1024,256]{2,1,0:T(8,128)(2,1)S(1)} %densify.1.refs_0_.a_ref), custom_call_target="tpu_custom_call" | custom-call | bytes 8388608 | tf_op jit(solution)/shard_map/transposed/pallas_call | solution.py:111
  41.8 4.3 %collective-permute-done.9.refs_2_ = bf16[256,512]{1,0:T(8,128)(2,1)S(1)} collective-permute-done((bf16[256,512]{1,0:T(8,128)(2,1)S(1)}, bf16[256,512]{1,0:T(8,128)(2,1)S(1)}, u32[]{:S(2)}, u32[]{:S(2)}) %collective-permute-start.9) | collective-permute-done | bytes 262176 | tf_op jit(solution)/shard_map/ppermute | solution.py:42
  46.0 1.2 %middle.1 = (bf16[256,512]{1,0:T(8,128)(2,1)}, bf16[256,512]{1,0:T(8,128)(2,1)S(1)}, bf16[256,512]{1,0:T(8,128)(2,1)S(1)}, bf16[256,512]{1,0:T(8,128)(2,1)S(1)}) custom-call(f32[256,512]{1,0:T(8,128)S(1)} %get-tuple-element.43.refs_0_, bf16[256,512]{1,0:T(8,128)(2,1)S(1)} %collective-permute-done.7.refs_1_, ...), custom_call_target="tpu_custom_call" | custom-call | flops 268435456 | bytes 1310720 | tf_op jit(solution)/shard_map/middle/pallas_call | solution.py:174
  48.3 1.9 %collective-permute-start.10 = (bf16[256,512]{1,0:T(8,128)(2,1)S(1)}, bf16[256,512]{1,0:T(8,128)(2,1)S(1)}, u32[]{:S(2)}, u32[]{:S(2)}) collective-permute-start(bf16[256,512]{1,0:T(8,128)(2,1)S(1)} %get-tuple-element.54.refs_2_), channel_id=1, source_target_pairs={{0,2},{1,3},{2,0},{3,1},{4,5},{5,4},{6,7},{7,6},{8,10},{9,11},{10,... | collective-permute-start | bytes 786440 | tf_op jit(solution)/shard_map/ppermute | solution.py:42
  50.3 4.4 %collective-permute-done.10.refs_3_ = bf16[256,512]{1,0:T(8,128)(2,1)S(1)} collective-permute-done((bf16[256,512]{1,0:T(8,128)(2,1)S(1)}, bf16[256,512]{1,0:T(8,128)(2,1)S(1)}, u32[]{:S(2)}, u32[]{:S(2)}) %collective-permute-start.10) | collective-permute-done | bytes 262176 | tf_op jit(solution)/shard_map/ppermute | solution.py:42
  54.7 2.0 %collective-permute-start.13 = (bf16[128,512]{1,0:T(8,128)(2,1)S(1)}, bf16[128,512]{1,0:T(8,128)(2,1)S(1)}, u32[]{:S(2)}, u32[]{:S(2)}) collective-permute-start(bf16[128,512]{1,0:T(8,128)(2,1)S(1)} %pad_maximum_fusion.3), channel_id=1, source_target_pairs={{0,2},{1,3},{2,0},{3,1},{4,5},{5,4},{6,7},{7,6},{8,10},{9,11},{10,... | collective-permute-start | bytes 393224 | tf_op jit(solution)/shard_map/ppermute | solution.py:42
  57.4 3.7 %collective-permute-done.13 = bf16[128,512]{1,0:T(8,128)(2,1)S(1)} collective-permute-done((bf16[128,512]{1,0:T(8,128)(2,1)S(1)}, bf16[128,512]{1,0:T(8,128)(2,1)S(1)}, u32[]{:S(2)}, u32[]{:S(2)}) %collective-permute-start.13) | collective-permute-done | bytes 131104 | tf_op jit(solution)/shard_map/ppermute | solution.py:42
  62.1 4.6 %collective-permute-done.14 = bf16[64,512]{1,0:T(8,128)(2,1)S(1)} collective-permute-done((bf16[64,512]{1,0:T(8,128)(2,1)S(1)}, bf16[64,512]{1,0:T(8,128)(2,1)S(1)}, u32[]{:S(2)}, u32[]{:S(2)}) %collective-permute-start.14) | collective-permute-done | bytes 65568 | tf_op jit(solution)/shard_map/ppermute | solution.py:42
  66.8 1.2 %backward.2 = (f32[256,512]{1,0:T(8,128)S(1)}, f32[256,512]{1,0:T(8,128)S(1)}, bf16[512,512]{1,0:T(8,128)(2,1)S(1)}) custom-call(bf16[2,256,1024]{2,1,0:T(8,128)(2,1)S(1)} %get-tuple-element.50.refs_0_, bf16[2,256,1024]{2,1,0:T(8,128)(2,1)S(1)} %get-tuple-element.51.refs_1_, bf16[256,512]{1,0:T(8,128)(2,1)S(1)} %get-tuple-element.54.refs_2_, ...), custom_call_target="tpu_custom_call" | custom-call | flops 1073741824 | bytes 4718592 | tf_op jit(solution)/shard_map/backward/pallas_call | solution.py:267
  68.1 1.9 %collective-permute-start.19 = (bf16[64,512]{1,0:T(8,128)(2,1)S(1)}, bf16[64,512]{1,0:T(8,128)(2,1)S(1)}, u32[]{:S(2)}, u32[]{:S(2)}) collective-permute-start(bf16[64,512]{1,0:T(8,128)(2,1)S(1)} %add_convert_fusion.5), channel_id=1, source_target_pairs={{0,16},{4,12},{8,24},{12,4},{16,0},{20,28},{24,8},{28,20},{1,17},{... | collective-permute-start | bytes 196616 | tf_op jit(solution)/shard_map/ppermute | solution.py:32
  70.0 3.4 %collective-permute-done.19 = bf16[64,512]{1,0:T(8,128)(2,1)S(1)} collective-permute-done((bf16[64,512]{1,0:T(8,128)(2,1)S(1)}, bf16[64,512]{1,0:T(8,128)(2,1)S(1)}, u32[]{:S(2)}, u32[]{:S(2)}) %collective-permute-start.19) | collective-permute-done | bytes 65568 | tf_op jit(solution)/shard_map/ppermute | solution.py:32
  73.4 1.3 %collective-permute-start.20 = (bf16[64,512]{1,0:T(8,128)(2,1)S(1)}, bf16[64,512]{1,0:T(8,128)(2,1)S(1)}, u32[]{:S(2)}, u32[]{:S(2)}) collective-permute-start(bf16[64,512]{1,0:T(8,128)(2,1)S(1)} %add_convert_fusion.4), channel_id=1, source_target_pairs={{0,8},{4,20},{8,0},{12,28},{16,24},{20,4},{24,16},{28,12},{1,9},{5... | collective-permute-start | bytes 196616 | tf_op jit(solution)/shard_map/ppermute | solution.py:32
  75.7 1.2 %backward.3 = (f32[256,512]{1,0:T(8,128)S(1)}, f32[256,512]{1,0:T(8,128)S(1)}, bf16[512,512]{1,0:T(8,128)(2,1)S(1)}) custom-call(bf16[2,256,1024]{2,1,0:T(8,128)(2,1)S(1)} %get-tuple-element.67.refs_0_, bf16[2,256,1024]{2,1,0:T(8,128)(2,1)S(1)} %get-tuple-element.49.refs_1_, bf16[256,512]{1,0:T(8,128)(2,1)S(1)} %get-tuple-element.54.refs_2_, ...), custom_call_target="tpu_custom_call" | custom-call | flops 1073741824 | bytes 4718592 | tf_op jit(solution)/shard_map/backward/pallas_call | solution.py:267
  77.0 1.8 %collective-permute-done.20 = bf16[64,512]{1,0:T(8,128)(2,1)S(1)} collective-permute-done((bf16[64,512]{1,0:T(8,128)(2,1)S(1)}, bf16[64,512]{1,0:T(8,128)(2,1)S(1)}, u32[]{:S(2)}, u32[]{:S(2)}) %collective-permute-start.20) | collective-permute-done | bytes 65568 | tf_op jit(solution)/shard_map/ppermute | solution.py:32
  80.1 2.2 %collective-permute-start.23 = (f32[64,512]{1,0:T(8,128)S(1)}, f32[64,512]{1,0:T(8,128)S(1)}, u32[]{:S(2)}, u32[]{:S(2)}) collective-permute-start(f32[64,512]{1,0:T(8,128)S(1)} %add_multiply_fusion.refs_0_), channel_id=1, source_target_pairs={{0,3},{1,2},{2,1},{3,0},{4,7},{5,6},{6,5},{7,4},{8,11},{9,10},{10,... | collective-permute-start | bytes 393224 | tf_op jit(solution)/shard_map/ppermute | solution.py:42
  82.4 2.5 %collective-permute-done.21.refs_1_ = f32[64,512]{1,0:T(8,128)S(1)} collective-permute-done((f32[64,512]{1,0:T(8,128)S(1)}, f32[64,512]{1,0:T(8,128)S(1)}, u32[]{:S(2)}, u32[]{:S(2)}) %collective-permute-start.21) | collective-permute-done | bytes 131104 | tf_op jit(solution)/shard_map/ppermute | solution.py:42
  84.9 2.3 %collective-permute-done.22.refs_2_ = f32[64,512]{1,0:T(8,128)S(1)} collective-permute-done((f32[64,512]{1,0:T(8,128)S(1)}, f32[64,512]{1,0:T(8,128)S(1)}, u32[]{:S(2)}, u32[]{:S(2)}) %collective-permute-start.22) | collective-permute-done | bytes 131104 | tf_op jit(solution)/shard_map/ppermute | solution.py:42
  87.3 1.6 %collective-permute-done.17 = bf16[512,512]{1,0:T(8,128)(2,1)S(1)} collective-permute-done((bf16[512,512]{1,0:T(8,128)(2,1)S(1)}, bf16[512,512]{1,0:T(8,128)(2,1)S(1)}, u32[]{:S(2)}, u32[]{:S(2)}) %collective-permute-start.17) | collective-permute-done | bytes 524320 | tf_op jit(solution)/shard_map/ppermute | solution.py:32
  89.1 1.6 %collective-permute-start.18 = (bf16[256,512]{1,0:T(8,128)(2,1)S(1)}, bf16[256,512]{1,0:T(8,128)(2,1)S(1)}, u32[]{:S(2)}, u32[]{:S(2)}) collective-permute-start(bf16[256,512]{1,0:T(8,128)(2,1)S(1)} %get-tuple-element.71), channel_id=1, source_target_pairs={{0,16},{4,12},{8,24},{12,4},{16,0},{20,28},{24,8},{28,20},{1,17},{... | collective-permute-start | bytes 786440 | tf_op jit(solution)/shard_map/ppermute | solution.py:32
  90.7 1.6 %place_slices.1 = f32[512,512]{1,0:T(8,128)} custom-call(s32[2]{0:T(128)S(1)} %pad_add_fusion.1.place_ref, f32[64,512]{1,0:T(8,128)S(1)} %add_multiply_fusion.refs_0_, f32[64,512]{1,0:T(8,128)S(1)} %collective-permute-done.21.refs_1_, f32[64,512]{1,0:T(8,128)S(1)} %collective-permute-done.22.refs_2_, f32[64,512]{1,0:T(8,128)S(1)} %collective-permute-done.23.refs_3_, ...), custom_call_target="tpu_custom_call" | custom-call | bytes 2097152 | tf_op jit(solution)/shard_map/place_slices/pallas_call | solution.py:235
  92.3 7.0 %collective-permute-done.18.refs_1_ = bf16[256,512]{1,0:T(8,128)(2,1)S(1)} collective-permute-done((bf16[256,512]{1,0:T(8,128)(2,1)S(1)}, bf16[256,512]{1,0:T(8,128)(2,1)S(1)}, u32[]{:S(2)}, u32[]{:S(2)}) %collective-permute-start.18) | collective-permute-done | bytes 262176 | tf_op jit(solution)/shard_map/ppermute | solution.py:32
  (53 shorter events, 11.6 us)
Async XLA Ops:
  0.6 16.7 %collective-permute-start.1 = (bf16[256,512]{1,0:T(8,128)(2,1)}, bf16[256,512]{1,0:T(8,128)(2,1)S(1)}, u32[]{:S(2)}, u32[]{:S(2)}) collective-permute-start(bf16[256,512]{1,0:T(8,128)(2,1)} %refs_1_.1), channel_id=1, source_target_pairs={{0,16},{4,12},{8,24},{12,4},{16,0},{20,28},{24,8},{28,20},{1,17},{... | collective-permute-start | bytes 786440 | tf_op jit(solution)/shard_map/ppermute | solution.py:32
  4.7 21.7 %collective-permute-start = (bf16[256,512]{1,0:T(8,128)(2,1)}, bf16[256,512]{1,0:T(8,128)(2,1)S(1)}, u32[]{:S(2)}, u32[]{:S(2)}) collective-permute-start(bf16[256,512]{1,0:T(8,128)(2,1)} %refs_1_.1), channel_id=1, source_target_pairs={{0,8},{4,20},{8,0},{12,28},{16,24},{20,4},{24,16},{28,12},{1,9},{5... | collective-permute-start | bytes 786440 | tf_op jit(solution)/shard_map/ppermute | solution.py:32
  6.3 18.9 %collective-permute-start.3 = (bf16[256,512]{1,0:T(8,128)(2,1)}, bf16[256,512]{1,0:T(8,128)(2,1)S(1)}, u32[]{:S(2)}, u32[]{:S(2)}) collective-permute-start(bf16[256,512]{1,0:T(8,128)(2,1)} %refs_1_.1), channel_id=1, source_target_pairs={{0,4},{4,0},{8,12},{12,8},{16,20},{20,16},{24,28},{28,24},{1,5},{5... | collective-permute-start | bytes 786440 | tf_op jit(solution)/shard_map/ppermute | solution.py:26
  17.3 7.9 %collective-permute-start.4 = (bf16[256,512]{1,0:T(8,128)(2,1)S(1)}, bf16[256,512]{1,0:T(8,128)(2,1)S(1)}, u32[]{:S(2)}, u32[]{:S(2)}) collective-permute-start(bf16[256,512]{1,0:T(8,128)(2,1)S(1)} %collective-permute-done.1.refs_3_), channel_id=1, source_target_pairs={{0,4},{4,0},{8,12},{12,8},{16,20},{20,16},{24,28},{28,24},{1,5},{5... | collective-permute-start | bytes 786440 | tf_op jit(solution)/shard_map/ppermute | solution.py:26
  18.1 9.2 %collective-permute-start.2 = (bf16[256,512]{1,0:T(8,128)(2,1)S(1)}, bf16[256,512]{1,0:T(8,128)(2,1)S(1)}, u32[]{:S(2)}, u32[]{:S(2)}) collective-permute-start(bf16[256,512]{1,0:T(8,128)(2,1)S(1)} %collective-permute-done.1.refs_3_), channel_id=1, source_target_pairs={{0,8},{4,20},{8,0},{12,28},{16,24},{20,4},{24,16},{28,12},{1,9},{5... | collective-permute-start | bytes 786440 | tf_op jit(solution)/shard_map/ppermute | solution.py:32
  19.6 2.2 %copy-start = (bf16[1,1,8,16,128,128]{5,4,3,2,1,0:T(8,128)(2,1)S(1)}, bf16[1,1,8,16,128,128]{5,4,3,2,1,0:T(8,128)(2,1)}, u32[]{:S(2)}) copy-start(bf16[1,1,8,16,128,128]{5,4,3,2,1,0:T(8,128)(2,1)} %param.10) | copy-start | bytes 12582916
  21.8 3.4 %copy-start.2 = (bf16[256,512]{1,0:T(8,128)(2,1)S(1)}, bf16[256,512]{1,0:T(8,128)(2,1)}, u32[]{:S(2)}) copy-start(bf16[256,512]{1,0:T(8,128)(2,1)} %refs_1_.1) | copy-start | bytes 786436
  27.3 1.5 %collective-permute-start.5 = (bf16[256,512]{1,0:T(8,128)(2,1)S(1)}, bf16[256,512]{1,0:T(8,128)(2,1)S(1)}, u32[]{:S(2)}, u32[]{:S(2)}) collective-permute-start(bf16[256,512]{1,0:T(8,128)(2,1)S(1)} %collective-permute-done.refs_1_), channel_id=1, source_target_pairs={{0,4},{4,0},{8,12},{12,8},{16,20},{20,16},{24,28},{28,24},{1,5},{5... | collective-permute-start | bytes 786440 | tf_op jit(solution)/shard_map/ppermute | solution.py:26
  27.3 1.9 %collective-permute-start.6 = (bf16[256,512]{1,0:T(8,128)(2,1)S(1)}, bf16[256,512]{1,0:T(8,128)(2,1)S(1)}, u32[]{:S(2)}, u32[]{:S(2)}) collective-permute-start(bf16[256,512]{1,0:T(8,128)(2,1)S(1)} %collective-permute-done.2.refs_3_), channel_id=1, source_target_pairs={{0,4},{4,0},{8,12},{12,8},{16,20},{20,16},{24,28},{28,24},{1,5},{5... | collective-permute-start | bytes 786440 | tf_op jit(solution)/shard_map/ppermute | solution.py:26
  30.5 15.6 %copy-start.1 = (bf16[512,512]{1,0:T(8,128)(2,1)S(1)}, bf16[512,512]{1,0:T(8,128)(2,1)}, u32[]{:S(2)}) copy-start(bf16[512,512]{1,0:T(8,128)(2,1)} %refs_4_.1) | copy-start | bytes 1572868
  30.5 15.6 %copy-start.3 = (bf16[256,512]{1,0:T(8,128)(2,1)S(1)}, bf16[256,512]{1,0:T(8,128)(2,1)}, u32[]{:S(2)}) copy-start(bf16[256,512]{1,0:T(8,128)(2,1)} %refs_3_.1) | copy-start | bytes 786436
  30.5 6.4 %collective-permute-start.8 = (bf16[256,512]{1,0:T(8,128)(2,1)S(1)}, bf16[256,512]{1,0:T(8,128)(2,1)S(1)}, u32[]{:S(2)}, u32[]{:S(2)}) collective-permute-start(bf16[256,512]{1,0:T(8,128)(2,1)S(1)} %get-tuple-element.46), channel_id=1, source_target_pairs={{0,1},{1,0},{2,3},{3,2},{4,6},{5,7},{6,4},{7,5},{8,9},{9,8},{10,11... | collective-permute-start | bytes 786440 | tf_op jit(solution)/shard_map/ppermute | solution.py:42
  37.0 9.0 %collective-permute-start.9 = (bf16[256,512]{1,0:T(8,128)(2,1)S(1)}, bf16[256,512]{1,0:T(8,128)(2,1)S(1)}, u32[]{:S(2)}, u32[]{:S(2)}) collective-permute-start(bf16[256,512]{1,0:T(8,128)(2,1)S(1)} %add_convert_fusion.3), channel_id=1, source_target_pairs={{0,2},{1,3},{2,0},{3,1},{4,5},{5,4},{6,7},{7,6},{8,10},{9,11},{10,... | collective-permute-start | bytes 786440 | tf_op jit(solution)/shard_map/ppermute | solution.py:42
  39.1 7.0 %collective-permute-start.7 = (bf16[256,512]{1,0:T(8,128)(2,1)S(1)}, bf16[256,512]{1,0:T(8,128)(2,1)S(1)}, u32[]{:S(2)}, u32[]{:S(2)}) collective-permute-start(bf16[256,512]{1,0:T(8,128)(2,1)S(1)} %get-tuple-element.44), channel_id=1, source_target_pairs={{0,1},{1,0},{2,3},{3,2},{4,6},{5,7},{6,4},{7,5},{8,9},{9,8},{10,11... | collective-permute-start | bytes 786440 | tf_op jit(solution)/shard_map/ppermute | solution.py:42
  48.1 2.1 %collective-permute-start.12 = (bf16[256,512]{1,0:T(8,128)(2,1)S(1)}, bf16[256,512]{1,0:T(8,128)(2,1)S(1)}, u32[]{:S(2)}, u32[]{:S(2)}) collective-permute-start(bf16[256,512]{1,0:T(8,128)(2,1)S(1)} %get-tuple-element.58), channel_id=1, source_target_pairs={{0,4},{4,0},{8,12},{12,8},{16,20},{20,16},{24,28},{28,24},{1,5},{5... | collective-permute-start | bytes 786440 | tf_op jit(solution)/shard_map/ppermute | solution.py:26
  48.3 6.4 %collective-permute-start.10 = (bf16[256,512]{1,0:T(8,128)(2,1)S(1)}, bf16[256,512]{1,0:T(8,128)(2,1)S(1)}, u32[]{:S(2)}, u32[]{:S(2)}) collective-permute-start(bf16[256,512]{1,0:T(8,128)(2,1)S(1)} %get-tuple-element.54.refs_2_), channel_id=1, source_target_pairs={{0,2},{1,3},{2,0},{3,1},{4,5},{5,4},{6,7},{7,6},{8,10},{9,11},{10,... | collective-permute-start | bytes 786440 | tf_op jit(solution)/shard_map/ppermute | solution.py:42
  54.7 6.4 %collective-permute-start.13 = (bf16[128,512]{1,0:T(8,128)(2,1)S(1)}, bf16[128,512]{1,0:T(8,128)(2,1)S(1)}, u32[]{:S(2)}, u32[]{:S(2)}) collective-permute-start(bf16[128,512]{1,0:T(8,128)(2,1)S(1)} %pad_maximum_fusion.3), channel_id=1, source_target_pairs={{0,2},{1,3},{2,0},{3,1},{4,5},{5,4},{6,7},{7,6},{8,10},{9,11},{10,... | collective-permute-start | bytes 393224 | tf_op jit(solution)/shard_map/ppermute | solution.py:42
  56.8 10.0 %collective-permute-start.11 = (bf16[512,512]{1,0:T(8,128)(2,1)S(1)}, bf16[512,512]{1,0:T(8,128)(2,1)S(1)}, u32[]{:S(2)}, u32[]{:S(2)}) collective-permute-start(bf16[512,512]{1,0:T(8,128)(2,1)S(1)} %pad_maximum_fusion), channel_id=1, source_target_pairs={{0,1},{1,0},{2,3},{3,2},{4,6},{5,7},{6,4},{7,5},{8,9},{9,8},{10,11... | collective-permute-start | bytes 1572872 | tf_op jit(solution)/shard_map/ppermute | solution.py:42
  61.1 5.6 %collective-permute-start.14 = (bf16[64,512]{1,0:T(8,128)(2,1)S(1)}, bf16[64,512]{1,0:T(8,128)(2,1)S(1)}, u32[]{:S(2)}, u32[]{:S(2)}) collective-permute-start(bf16[64,512]{1,0:T(8,128)(2,1)S(1)} %add_convert_fusion.6), channel_id=1, source_target_pairs={{0,1},{1,0},{2,3},{3,2},{4,6},{5,7},{6,4},{7,5},{8,9},{9,8},{10,11... | collective-permute-start | bytes 196616 | tf_op jit(solution)/shard_map/ppermute | solution.py:42
  68.0 6.7 %collective-permute-start.15 = (bf16[512,512]{1,0:T(8,128)(2,1)S(1)}, bf16[512,512]{1,0:T(8,128)(2,1)S(1)}, u32[]{:S(2)}, u32[]{:S(2)}) collective-permute-start(bf16[512,512]{1,0:T(8,128)(2,1)S(1)} %get-tuple-element.65), channel_id=1, source_target_pairs={{0,4},{4,0},{8,12},{12,8},{16,20},{20,16},{24,28},{28,24},{1,5},{5... | collective-permute-start | bytes 1572872 | tf_op jit(solution)/shard_map/ppermute | solution.py:26
  68.1 5.2 %collective-permute-start.19 = (bf16[64,512]{1,0:T(8,128)(2,1)S(1)}, bf16[64,512]{1,0:T(8,128)(2,1)S(1)}, u32[]{:S(2)}, u32[]{:S(2)}) collective-permute-start(bf16[64,512]{1,0:T(8,128)(2,1)S(1)} %add_convert_fusion.5), channel_id=1, source_target_pairs={{0,16},{4,12},{8,24},{12,4},{16,0},{20,28},{24,8},{28,20},{1,17},{... | collective-permute-start | bytes 196616 | tf_op jit(solution)/shard_map/ppermute | solution.py:32
  73.4 5.5 %collective-permute-start.20 = (bf16[64,512]{1,0:T(8,128)(2,1)S(1)}, bf16[64,512]{1,0:T(8,128)(2,1)S(1)}, u32[]{:S(2)}, u32[]{:S(2)}) collective-permute-start(bf16[64,512]{1,0:T(8,128)(2,1)S(1)} %add_convert_fusion.4), channel_id=1, source_target_pairs={{0,8},{4,20},{8,0},{12,28},{16,24},{20,4},{24,16},{28,12},{1,9},{5... | collective-permute-start | bytes 196616 | tf_op jit(solution)/shard_map/ppermute | solution.py:32
  74.9 14.0 %collective-permute-start.17 = (bf16[512,512]{1,0:T(8,128)(2,1)S(1)}, bf16[512,512]{1,0:T(8,128)(2,1)S(1)}, u32[]{:S(2)}, u32[]{:S(2)}) collective-permute-start(bf16[512,512]{1,0:T(8,128)(2,1)S(1)} %pad_maximum_fusion.1), channel_id=1, source_target_pairs={{0,8},{4,20},{8,0},{12,28},{16,24},{20,4},{24,16},{28,12},{1,9},{5... | collective-permute-start | bytes 1572872 | tf_op jit(solution)/shard_map/ppermute | solution.py:32
  77.0 12.0 %collective-permute-start.16 = (bf16[512,512]{1,0:T(8,128)(2,1)S(1)}, bf16[512,512]{1,0:T(8,128)(2,1)S(1)}, u32[]{:S(2)}, u32[]{:S(2)}) collective-permute-start(bf16[512,512]{1,0:T(8,128)(2,1)S(1)} %get-tuple-element.69), channel_id=1, source_target_pairs={{0,4},{4,0},{8,12},{12,8},{16,20},{20,16},{24,28},{28,24},{1,5},{5... | collective-permute-start | bytes 1572872 | tf_op jit(solution)/shard_map/ppermute | solution.py:26
  78.8 6.1 %collective-permute-start.21 = (f32[64,512]{1,0:T(8,128)S(1)}, f32[64,512]{1,0:T(8,128)S(1)}, u32[]{:S(2)}, u32[]{:S(2)}) collective-permute-start(f32[64,512]{1,0:T(8,128)S(1)} %add_multiply_fusion.refs_0_), channel_id=1, source_target_pairs={{0,1},{1,0},{2,3},{3,2},{4,6},{5,7},{6,4},{7,5},{8,9},{9,8},{10,11... | collective-permute-start | bytes 393224 | tf_op jit(solution)/shard_map/ppermute | solution.py:42
  79.4 7.8 %collective-permute-start.22 = (f32[64,512]{1,0:T(8,128)S(1)}, f32[64,512]{1,0:T(8,128)S(1)}, u32[]{:S(2)}, u32[]{:S(2)}) collective-permute-start(f32[64,512]{1,0:T(8,128)S(1)} %add_multiply_fusion.refs_0_), channel_id=1, source_target_pairs={{0,2},{1,3},{2,0},{3,1},{4,5},{5,4},{6,7},{7,6},{8,10},{9,11},{10,... | collective-permute-start | bytes 393224 | tf_op jit(solution)/shard_map/ppermute | solution.py:42
  80.1 7.1 %collective-permute-start.23 = (f32[64,512]{1,0:T(8,128)S(1)}, f32[64,512]{1,0:T(8,128)S(1)}, u32[]{:S(2)}, u32[]{:S(2)}) collective-permute-start(f32[64,512]{1,0:T(8,128)S(1)} %add_multiply_fusion.refs_0_), channel_id=1, source_target_pairs={{0,3},{1,2},{2,1},{3,0},{4,7},{5,6},{6,5},{7,4},{8,11},{9,10},{10,... | collective-permute-start | bytes 393224 | tf_op jit(solution)/shard_map/ppermute | solution.py:42
  87.2 3.5 %collective-permute-start.24 = (f32[256,512]{1,0:T(8,128)S(1)}, f32[256,512]{1,0:T(8,128)S(1)}, u32[]{:S(2)}, u32[]{:S(2)}) collective-permute-start(f32[256,512]{1,0:T(8,128)S(1)} %pad_maximum_fusion.2), channel_id=1, source_target_pairs={{0,4},{4,0},{8,12},{12,8},{16,20},{20,16},{24,28},{28,24},{1,5},{5... | collective-permute-start | bytes 1572872 | tf_op jit(solution)/shard_map/ppermute | solution.py:26
  89.1 10.1 %collective-permute-start.18 = (bf16[256,512]{1,0:T(8,128)(2,1)S(1)}, bf16[256,512]{1,0:T(8,128)(2,1)S(1)}, u32[]{:S(2)}, u32[]{:S(2)}) collective-permute-start(bf16[256,512]{1,0:T(8,128)(2,1)S(1)} %get-tuple-element.71), channel_id=1, source_target_pairs={{0,16},{4,12},{8,24},{12,4},{16,0},{20,28},{24,8},{28,20},{1,17},{... | collective-permute-start | bytes 786440 | tf_op jit(solution)/shard_map/ppermute | solution.py:32

commit v6 on v5

--- a/solution.py
+++ b/solution.py
@@ -243,59 +243,60 @@
     )(place, *owns, other)
 
 
-def backward_kernel(*refs, count, slots):
-    blocks, grads = refs[:count], refs[count:count + slots]
-    owns, other_ref = refs[count + slots:-1], refs[-1]
-    rows = owns[0].shape[0]
-    for side in (1, 0):
-        for i, block in enumerate(blocks):
-            total, start = None, 0
-            for grad in grads:
-                stop = start + grad.shape[0]
-                part = bf16_dot(block[side, :, start:stop], grad[...])
-                total, start = part if total is None else total + part, stop
-            if side:
-                other_ref[i * rows:(i + 1) * rows, :] = total.astype(other_ref.dtype)
-            else:
-                owns[i][...] = total
-
-
-def backward(blocks, grads):
+def backward_kernel(*refs, side, count, slots):
+    blocks, grads, outs = refs[:count], refs[count:count + slots], refs[count + slots:]
+    rows = blocks[0].shape[1]
+    for i, block in enumerate(blocks):
+        total, start = None, 0
+        for grad in grads:
+            stop = start + grad.shape[0]
+            part = bf16_dot(block[side, :, start:stop], grad[...])
+            total, start = part if total is None else total + part, stop
+        if side:
+            outs[0][i * rows:(i + 1) * rows, :] = total.astype(outs[0].dtype)
+        else:
+            outs[i][...] = total
+
+
+def backward(blocks, grads, side):
     _, cols, rows = blocks[0].shape
     width = grads[0].shape[1]
     count = len(blocks)
-    out = pl.pallas_call(
-        functools.partial(backward_kernel, count=count, slots=len(grads)),
-        out_shape=[like((cols, width), jnp.float32)] * count + [like((count * cols, width), jnp.bfloat16)],
+    own = [like((cols, width), jnp.float32)] * count
+    return pl.pallas_call(
+        functools.partial(backward_kernel, side=side, count=count, slots=len(grads)),
+        out_shape=[like((count * cols, width), jnp.bfloat16)] if side else own,
         in_specs=[WHOLE] * (count + len(grads)),
-        out_specs=[WHOLE] * (count + 1),
+        out_specs=[WHOLE] * (1 if side else count),
         compiler_params=params(8),
         cost_estimate=pl.CostEstimate(
-            flops=4 * count * cols * rows * width,
-            bytes_accessed=4 * count * cols * rows + 2 * rows * width + 6 * count * cols * width, transcendentals=0),
+            flops=2 * count * cols * rows * width,
+            bytes_accessed=2 * count * cols * rows + 2 * rows * width + 4 * count * cols * width, transcendentals=0),
         name="backward",
     )(*blocks, *grads)
-    return out[:-1], out[-1]
-
-
-def finish_kernel(*refs):
-    total = refs[0][...]
-    for ref in refs[1:-1]:
-        total = total + ref[...].astype(jnp.float32)
-    refs[-1][...] = total.astype(refs[-1].dtype)
-
-
-def finish(parts):
-    rows, width = parts[0].shape
-    return pl.pallas_call(
-        finish_kernel,
-        out_shape=like((rows, width), jnp.bfloat16),
-        in_specs=[WHOLE] * len(parts),
-        out_specs=WHOLE,
+
+
+def settle_kernel(*refs, slots, count):
+    totals, arrived, outs = refs[:slots], refs[slots:slots + count], refs[slots + count:]
+    rows = totals[0].shape[0]
+    for k in range(slots):
+        total = totals[k][...]
+        for ref in arrived:
+            total = total + ref[k * rows:(k + 1) * rows, :].astype(jnp.float32)
+        outs[k][...] = total.astype(outs[k].dtype)
+
+
+def settle(totals, arrived, dtypes):
+    rows, width = totals[0].shape
+    return pl.pallas_call(
+        functools.partial(settle_kernel, slots=len(totals), count=len(arrived)),
+        out_shape=[like((rows, width), dtype) for dtype in dtypes],
+        in_specs=[WHOLE] * (len(totals) + len(arrived)),
+        out_specs=[WHOLE] * len(totals),
         compiler_params=params(8),
         cost_estimate=pl.CostEstimate(flops=rows * width, bytes_accessed=8 * rows * width, transcendentals=0),
-        name="finish",
-    )(*parts)
+        name="settle",
+    )(*totals, *arrived)
 
 
 def top_bit(slot):
@@ -346,7 +347,8 @@
 
     held = [features]
     for k in range(1, chips):
-        held.append(swap_chips(held[k - top_bit(k)], top_bit(k)))
+        given = after(features, held[k - 1]) if k == top_bit(k) > 1 else held[k - top_bit(k)]
+        held.append(swap_chips(given, top_bit(k)))
     totals = None
     for first, stop in ((0, chips // 2), (chips // 2, chips)):
         sources = []
@@ -370,17 +372,24 @@
         slots = sum(x.shape[0] for x in grads) // rows_local
         grads.append(swap_members(jnp.concatenate(grads) if slots > 1 else grad, slots))
         if slots == 1:
-            parts[-1] = after(parts[-1], grads[-1])
             kept, got = halve(parts, functools.partial(swap_members, turn=1))
             part = (kept + got.astype(jnp.float32)).astype(jnp.bfloat16)
-    grads[-1] = after(grads[-1], part)
+    part = after(part, grads[-1])
 
     half = chips // 2
-    own, other = backward(dense_t[half:], grads)
-    high = jnp.concatenate(add_slots(own, swap_cores(other))).astype(jnp.bfloat16)
-    own, other = backward([after(dense_t[0], high), *dense_t[1:half]], grads)
-    low = add_slots(own, swap_cores(other))
-    feature_grad = finish(halve(add_slots(low, swap_chips(high, half)), swap_chips))
+    other = backward(dense_t[half:], grads, 1)
+    own = backward([after(dense_t[half], *other), *dense_t[half + 1:]], grads, 0)
+    high = jnp.concatenate(add_slots(own, swap_cores(other[0]))).astype(jnp.bfloat16)
+    grads[0] = after(grads[0], high)
+    other = backward(dense_t[:half], grads, 1)
+    totals = backward(dense_t[:half], grads, 0)
+    arrived = [swap_cores(other[0]), swap_chips(high, half)]
+    while half > 1:
+        half //= 2
+        totals = settle(totals, arrived, [jnp.float32] * half + [jnp.bfloat16] * half)
+        send = jnp.concatenate(totals[half:]) if half > 1 else totals[half]
+        totals, arrived = totals[:half], [swap_chips(send, half)]
+    (feature_grad,) = settle(totals, arrived, [jnp.bfloat16])
 
     bit = 1
     while bit < chips:

time: 100 us -> 106 us (1.060)
  starting transfers between devices: 27.6 us -> 36.2 us
  waiting for transfers between devices: 53.2 us -> 50.1 us
    ppermute x10, starting transfers between devices: 14.7 us -> 22.1 us  [swap_members(): return lax.ppermute(x, ('dom', 'repl'), pairs)]
    ppermute x7, waiting for transfers between devices: 25.5 us -> 22.7 us  [swap_chips(): lax.ppermute(x, 'dom', [(i, i ^ 2 * between(held, i % 2, bits)) for i in...]
    ppermute x7, starting transfers between devices: 12 us -> 13.3 us  [swap_chips(): lax.ppermute(x, 'dom', [(i, i ^ 2 * between(held, i % 2, bits)) for i in...]
    pallas_call x3 -> x6, Pallas kernels: 3.25 us -> 3.72 us  [the longest x4 2.8 us: backward(): pl.pallas_call(functools.partial(backward_kernel, side=side, count=count,...]
  transfers between devices with their start and end apart: 25 -> 25, of which waited for: 15 -> 17; matrix products, arithmetic and copies ran while one was open for 2% -> 2% of each run, Pallas kernels for 9% -> 11%
where the time goes in v6:
time: 106 us
  waiting for transfers between devices  50.1 us (47%)
  starting transfers between devices  36.2 us (34%)
  Pallas kernels  14.4 us (14%)
  local copies, waits for them, and re-layouts  2.93 us (3%)
  other arithmetic  1.34 us (1%)
    ppermute x10, waiting for transfers between devices, swap_members(): return lax.ppermute(x, ('dom', 'repl'), pairs)  26 us
    ppermute x7, waiting for transfers between devices, swap_chips(): lax.ppermute(x, 'dom', [(i, i ^ 2 * between(held, i % 2, bits)) for i in...  22.7 us
    ppermute x10, starting transfers between devices, swap_members(): return lax.ppermute(x, ('dom', 'repl'), pairs)  22.1 us
    ppermute x7, starting transfers between devices, swap_chips(): lax.ppermute(x, 'dom', [(i, i ^ 2 * between(held, i % 2, bits)) for i in...  13.3 us
    pallas_call x1, Pallas kernels, densify(): pl.pallas_call(functools.partial(densify_kernel, col_tiles=col_tiles), ou...  3.33 us
    pallas_call x4, Pallas kernels, backward(): pl.pallas_call(functools.partial(backward_kernel, side=side, count=count,...  2.8 us
    pallas_call x2, Pallas kernels, forward(): pl.pallas_call(functools.partial(forward_kernel, first=first, count=len(s...  2.49 us
    unnamed x8, local copies, waits for them, and re-layouts  2.2 us
  transfers between devices with their start and end apart: 25, of which 17 were waited for; matrix products, arithmetic and copies ran while one was open for 2% of the time, Pallas kernels for 11%

profile of v6, /device:TPU:0, one launch (start us, length us, event | category | flops | bytes accessed | tf_op | source)
XLA Modules:
  0.0 105.9 jit_solution(4647300746432285496)
XLA Ops:
  0.6 4.1 %collective-permute-start = (bf16[256,512]{1,0:T(8,128)(2,1)}, bf16[256,512]{1,0:T(8,128)(2,1)S(1)}, u32[]{:S(2)}, u32[]{:S(2)}) collective-permute-start(bf16[256,512]{1,0:T(8,128)(2,1)} %refs_1_.1), channel_id=1, source_target_pairs={{0,16},{4,12},{8,24},{12,4},{16,0},{20,28},{24,8},{28,20},{1,17},{... | collective-permute-start | bytes 786440 | tf_op jit(solution)/shard_map/ppermute | solution.py:32
  4.7 6.1 %collective-permute-done.refs_3_ = bf16[256,512]{1,0:T(8,128)(2,1)S(1)} collective-permute-done((bf16[256,512]{1,0:T(8,128)(2,1)}, bf16[256,512]{1,0:T(8,128)(2,1)S(1)}, u32[]{:S(2)}, u32[]{:S(2)}) %collective-permute-start) | collective-permute-done | bytes 262176 | tf_op jit(solution)/shard_map/ppermute | solution.py:32
  11.6 2.5 %collective-permute-start.1 = (bf16[256,512]{1,0:T(8,128)(2,1)}, bf16[256,512]{1,0:T(8,128)(2,1)S(1)}, u32[]{:S(2)}, u32[]{:S(2)}) collective-permute-start(bf16[256,512]{1,0:T(8,128)(2,1)} %refs_1_.1), channel_id=1, source_target_pairs={{0,8},{4,20},{8,0},{12,28},{16,24},{20,4},{24,16},{28,12},{1,9},{5... | collective-permute-start | bytes 786440 | tf_op jit(solution)/shard_map/ppermute | solution.py:32
  15.1 2.2 %copy-done = bf16[1,1,8,16,128,128]{5,4,3,2,1,0:T(8,128)(2,1)S(1)} copy-done((bf16[1,1,8,16,128,128]{5,4,3,2,1,0:T(8,128)(2,1)S(1)}, bf16[1,1,8,16,128,128]{5,4,3,2,1,0:T(8,128)(2,1)}, u32[]{:S(2)}) %copy-start) | copy-done | bytes 4194328
  17.2 3.3 %densify.1.refs_0_.a_ref = bf16[8,1024,256]{2,1,0:T(8,128)(2,1)S(1)} custom-call(s32[8,17]{1,0:T(8,128)S(1)} %pad_add_fusion.spots_ref, s32[2]{0:T(128)S(1)} %pad_add_fusion.1.place_ref, bf16[8,16,128,128]{3,2,1,0:T(8,128)(2,1)S(1)} %bitcast.26), custom_call_target="tpu_custom_call" | custom-call | flops 2097152 | bytes 16777216 | tf_op jit(solution)/shard_map/densify/pallas_call | solution.py:86
  20.6 1.2 %forward.2 = (f32[256,512]{1,0:T(8,128)S(1)}, f32[256,512]{1,0:T(8,128)S(1)}, f32[256,512]{1,0:T(8,128)S(1)}, f32[256,512]{1,0:T(8,128)S(1)}) custom-call(bf16[8,1024,256]{2,1,0:T(8,128)(2,1)S(1)} %densify.1.refs_0_.a_ref, bf16[256,512]{1,0:T(8,128)(2,1)S(1)} %copy-done.2, bf16[256,512]{1,0:T(8,128)(2,1)S(1)} %collective-permute-done.3.refs_2_, ...), custom_call_target="tpu_custom_call" | custom-call | flops 1073741824 | bytes 4194304 | tf_op jit(solution)/shard_map/forward/pallas_call | solution.py:139
  21.9 1.8 %collective-permute-done.1.refs_1_ = bf16[256,512]{1,0:T(8,128)(2,1)S(1)} collective-permute-done((bf16[256,512]{1,0:T(8,128)(2,1)}, bf16[256,512]{1,0:T(8,128)(2,1)S(1)}, u32[]{:S(2)}, u32[]{:S(2)}) %collective-permute-start.1) | collective-permute-done | bytes 262176 | tf_op jit(solution)/shard_map/ppermute | solution.py:32
  23.7 3.4 %collective-permute-done.2.refs_3_ = bf16[256,512]{1,0:T(8,128)(2,1)S(1)} collective-permute-done((bf16[256,512]{1,0:T(8,128)(2,1)S(1)}, bf16[256,512]{1,0:T(8,128)(2,1)S(1)}, u32[]{:S(2)}, u32[]{:S(2)}) %collective-permute-start.2) | collective-permute-done | bytes 262176 | tf_op jit(solution)/shard_map/ppermute | solution.py:32
  29.0 1.2 %forward.3 = (f32[256,512]{1,0:T(8,128)S(1)}, f32[256,512]{1,0:T(8,128)S(1)}, bf16[256,512]{1,0:T(8,128)(2,1)S(1)}, bf16[256,512]{1,0:T(8,128)(2,1)S(1)}) custom-call(bf16[8,1024,256]{2,1,0:T(8,128)(2,1)S(1)} %densify.1.refs_0_.a_ref, bf16[256,512]{1,0:T(8,128)(2,1)S(1)} %collective-permute-done.1.refs_1_, ...), custom_call_target="tpu_custom_call" | custom-call | flops 1073741824 | bytes 4194304 | tf_op jit(solution)/shard_map/forward/pallas_call | solution.py:139
  30.3 1.7 %collective-permute-start.8 = (bf16[256,512]{1,0:T(8,128)(2,1)S(1)}, bf16[256,512]{1,0:T(8,128)(2,1)S(1)}, u32[]{:S(2)}, u32[]{:S(2)}) collective-permute-start(bf16[256,512]{1,0:T(8,128)(2,1)S(1)} %get-tuple-element.48), channel_id=1, source_target_pairs={{0,1},{1,0},{2,3},{3,2},{4,6},{5,7},{6,4},{7,5},{8,9},{9,8},{10,11... | collective-permute-start | bytes 786440 | tf_op jit(solution)/shard_map/ppermute | solution.py:42
  32.0 4.7 %collective-permute-done.8 = bf16[256,512]{1,0:T(8,128)(2,1)S(1)} collective-permute-done((bf16[256,512]{1,0:T(8,128)(2,1)S(1)}, bf16[256,512]{1,0:T(8,128)(2,1)S(1)}, u32[]{:S(2)}, u32[]{:S(2)}) %collective-permute-start.8) | collective-permute-done | bytes 262176 | tf_op jit(solution)/shard_map/ppermute | solution.py:42
  36.8 1.8 %collective-permute-start.9 = (bf16[256,512]{1,0:T(8,128)(2,1)S(1)}, bf16[256,512]{1,0:T(8,128)(2,1)S(1)}, u32[]{:S(2)}, u32[]{:S(2)}) collective-permute-start(bf16[256,512]{1,0:T(8,128)(2,1)S(1)} %add_convert_fusion.2), channel_id=1, source_target_pairs={{0,2},{1,3},{2,0},{3,1},{4,5},{5,4},{6,7},{7,6},{8,10},{9,11},{10,... | collective-permute-start | bytes 786440 | tf_op jit(solution)/shard_map/ppermute | solution.py:42
  38.5 1.5 %collective-permute-start.7 = (bf16[256,512]{1,0:T(8,128)(2,1)S(1)}, bf16[256,512]{1,0:T(8,128)(2,1)S(1)}, u32[]{:S(2)}, u32[]{:S(2)}) collective-permute-start(bf16[256,512]{1,0:T(8,128)(2,1)S(1)} %get-tuple-element.46), channel_id=1, source_target_pairs={{0,1},{1,0},{2,3},{3,2},{4,6},{5,7},{6,4},{7,5},{8,9},{9,8},{10,11... | collective-permute-start | bytes 786440 | tf_op jit(solution)/shard_map/ppermute | solution.py:42
  40.0 1.2 %transposed.1 = (bf16[2,256,1024]{2,1,0:T(8,128)(2,1)S(1)}, bf16[2,256,1024]{2,1,0:T(8,128)(2,1)S(1)}, bf16[2,256,1024]{2,1,0:T(8,128)(2,1)S(1)}, bf16[2,256,1024]{2,1,0:T(8,128)(2,1)S(1)}) custom-call(bf16[8,1024,256]{2,1,0:T(8,128)(2,1)S(1)} %densify.1.refs_0_.a_ref), custom_call_target="tpu_custom_call" | custom-call | bytes 8388608 | tf_op jit(solution)/shard_map/transposed/pallas_call | solution.py:111
  41.3 4.5 %collective-permute-done.9.refs_2_ = bf16[256,512]{1,0:T(8,128)(2,1)S(1)} collective-permute-done((bf16[256,512]{1,0:T(8,128)(2,1)S(1)}, bf16[256,512]{1,0:T(8,128)(2,1)S(1)}, u32[]{:S(2)}, u32[]{:S(2)}) %collective-permute-start.9) | collective-permute-done | bytes 262176 | tf_op jit(solution)/shard_map/ppermute | solution.py:42
  45.7 1.2 %middle.1 = (bf16[256,512]{1,0:T(8,128)(2,1)}, bf16[256,512]{1,0:T(8,128)(2,1)S(1)}, bf16[256,512]{1,0:T(8,128)(2,1)S(1)}, bf16[256,512]{1,0:T(8,128)(2,1)S(1)}) custom-call(f32[256,512]{1,0:T(8,128)S(1)} %get-tuple-element.45.refs_0_, bf16[256,512]{1,0:T(8,128)(2,1)S(1)} %collective-permute-done.7.refs_1_, ...), custom_call_target="tpu_custom_call" | custom-call | flops 268435456 | bytes 1310720 | tf_op jit(solution)/shard_map/middle/pallas_call | solution.py:174
  46.9 1.5 %collective-permute-start.10 = (bf16[256,512]{1,0:T(8,128)(2,1)S(1)}, bf16[256,512]{1,0:T(8,128)(2,1)S(1)}, u32[]{:S(2)}, u32[]{:S(2)}) collective-permute-start(bf16[256,512]{1,0:T(8,128)(2,1)S(1)} %get-tuple-element.60.refs_2_), channel_id=1, source_target_pairs={{0,2},{1,3},{2,0},{3,1},{4,5},{5,4},{6,7},{7,6},{8,10},{9,11},{10,... | collective-permute-start | bytes 786440 | tf_op jit(solution)/shard_map/ppermute | solution.py:42
  49.5 3.8 %collective-permute-done.10.refs_3_ = bf16[256,512]{1,0:T(8,128)(2,1)S(1)} collective-permute-done((bf16[256,512]{1,0:T(8,128)(2,1)S(1)}, bf16[256,512]{1,0:T(8,128)(2,1)S(1)}, u32[]{:S(2)}, u32[]{:S(2)}) %collective-permute-start.10) | collective-permute-done | bytes 262176 | tf_op jit(solution)/shard_map/ppermute | solution.py:42
  54.1 1.4 %collective-permute-start.17 = (bf16[128,512]{1,0:T(8,128)(2,1)S(1)}, bf16[128,512]{1,0:T(8,128)(2,1)S(1)}, u32[]{:S(2)}, u32[]{:S(2)}) collective-permute-start(bf16[128,512]{1,0:T(8,128)(2,1)S(1)} %pad_maximum_fusion.3), channel_id=1, source_target_pairs={{0,2},{1,3},{2,0},{3,1},{4,5},{5,4},{6,7},{7,6},{8,10},{9,11},{10,... | collective-permute-start | bytes 393224 | tf_op jit(solution)/shard_map/ppermute | solution.py:42
  55.6 5.0 %collective-permute-done.17 = bf16[128,512]{1,0:T(8,128)(2,1)S(1)} collective-permute-done((bf16[128,512]{1,0:T(8,128)(2,1)S(1)}, bf16[128,512]{1,0:T(8,128)(2,1)S(1)}, u32[]{:S(2)}, u32[]{:S(2)}) %collective-permute-start.17) | collective-permute-done | bytes 131104 | tf_op jit(solution)/shard_map/ppermute | solution.py:42
  60.6 1.4 %collective-permute-start.18 = (bf16[64,512]{1,0:T(8,128)(2,1)S(1)}, bf16[64,512]{1,0:T(8,128)(2,1)S(1)}, u32[]{:S(2)}, u32[]{:S(2)}) collective-permute-start(bf16[64,512]{1,0:T(8,128)(2,1)S(1)} %add_convert_fusion.5), channel_id=1, source_target_pairs={{0,1},{1,0},{2,3},{3,2},{4,6},{5,7},{6,4},{7,5},{8,9},{9,8},{10,11... | collective-permute-start | bytes 196616 | tf_op jit(solution)/shard_map/ppermute | solution.py:42
  65.0 3.0 %collective-permute-start.19 = (bf16[64,512]{1,0:T(8,128)(2,1)S(1)}, bf16[64,512]{1,0:T(8,128)(2,1)S(1)}, u32[]{:S(2)}, u32[]{:S(2)}) collective-permute-start(bf16[64,512]{1,0:T(8,128)(2,1)S(1)} %add_convert_fusion.4), channel_id=1, source_target_pairs={{0,16},{4,12},{8,24},{12,4},{16,0},{20,28},{24,8},{28,20},{1,17},{... | collective-permute-start | bytes 196616 | tf_op jit(solution)/shard_map/ppermute | solution.py:32
  68.7 1.5 %collective-permute-done.19 = bf16[64,512]{1,0:T(8,128)(2,1)S(1)} collective-permute-done((bf16[64,512]{1,0:T(8,128)(2,1)S(1)}, bf16[64,512]{1,0:T(8,128)(2,1)S(1)}, u32[]{:S(2)}, u32[]{:S(2)}) %collective-permute-start.19) | collective-permute-done | bytes 65568 | tf_op jit(solution)/shard_map/ppermute | solution.py:32
  70.3 2.3 %collective-permute-start.20 = (bf16[64,512]{1,0:T(8,128)(2,1)S(1)}, bf16[64,512]{1,0:T(8,128)(2,1)S(1)}, u32[]{:S(2)}, u32[]{:S(2)}) collective-permute-start(bf16[64,512]{1,0:T(8,128)(2,1)S(1)} %add_convert_fusion.3), channel_id=1, source_target_pairs={{0,8},{4,20},{8,0},{12,28},{16,24},{20,4},{24,16},{28,12},{1,9},{5... | collective-permute-start | bytes 196616 | tf_op jit(solution)/shard_map/ppermute | solution.py:32
  73.7 2.4 %collective-permute-done.20 = bf16[64,512]{1,0:T(8,128)(2,1)S(1)} collective-permute-done((bf16[64,512]{1,0:T(8,128)(2,1)S(1)}, bf16[64,512]{1,0:T(8,128)(2,1)S(1)}, u32[]{:S(2)}, u32[]{:S(2)}) %collective-permute-start.20) | collective-permute-done | bytes 65568 | tf_op jit(solution)/shard_map/ppermute | solution.py:32
  76.1 10.4 %collective-permute-start.21 = (f32[64,512]{1,0:T(8,128)S(1)}, f32[64,512]{1,0:T(8,128)S(1)}, u32[]{:S(2)}, u32[]{:S(2)}) collective-permute-start(f32[64,512]{1,0:T(8,128)S(1)} %add_multiply_fusion.refs_0_), channel_id=1, source_target_pairs={{0,1},{1,0},{2,3},{3,2},{4,6},{5,7},{6,4},{7,5},{8,9},{9,8},{10,11... | collective-permute-start | bytes 393224 | tf_op jit(solution)/shard_map/ppermute | solution.py:42
  86.5 1.6 %collective-permute-start.22 = (f32[64,512]{1,0:T(8,128)S(1)}, f32[64,512]{1,0:T(8,128)S(1)}, u32[]{:S(2)}, u32[]{:S(2)}) collective-permute-start(f32[64,512]{1,0:T(8,128)S(1)} %add_multiply_fusion.refs_0_), channel_id=1, source_target_pairs={{0,2},{1,3},{2,0},{3,1},{4,5},{5,4},{6,7},{7,6},{8,10},{9,11},{10,... | collective-permute-start | bytes 393224 | tf_op jit(solution)/shard_map/ppermute | solution.py:42
  88.1 1.3 %collective-permute-done.21.refs_1_ = f32[64,512]{1,0:T(8,128)S(1)} collective-permute-done((f32[64,512]{1,0:T(8,128)S(1)}, f32[64,512]{1,0:T(8,128)S(1)}, u32[]{:S(2)}, u32[]{:S(2)}) %collective-permute-start.21) | collective-permute-done | bytes 131104 | tf_op jit(solution)/shard_map/ppermute | solution.py:42
  89.4 2.0 %collective-permute-done.22.refs_2_ = f32[64,512]{1,0:T(8,128)S(1)} collective-permute-done((f32[64,512]{1,0:T(8,128)S(1)}, f32[64,512]{1,0:T(8,128)S(1)}, u32[]{:S(2)}, u32[]{:S(2)}) %collective-permute-start.22) | collective-permute-done | bytes 131104 | tf_op jit(solution)/shard_map/ppermute | solution.py:42
  91.5 2.5 %collective-permute-done.23.refs_3_ = f32[64,512]{1,0:T(8,128)S(1)} collective-permute-done((f32[64,512]{1,0:T(8,128)S(1)}, f32[64,512]{1,0:T(8,128)S(1)}, u32[]{:S(2)}, u32[]{:S(2)}) %collective-permute-start.23) | collective-permute-done | bytes 131104 | tf_op jit(solution)/shard_map/ppermute | solution.py:42
  96.2 1.6 %place_slices.1 = f32[512,512]{1,0:T(8,128)} custom-call(s32[2]{0:T(128)S(1)} %pad_add_fusion.1.place_ref, f32[64,512]{1,0:T(8,128)S(1)} %add_multiply_fusion.refs_0_, f32[64,512]{1,0:T(8,128)S(1)} %collective-permute-done.21.refs_1_, f32[64,512]{1,0:T(8,128)S(1)} %collective-permute-done.22.refs_2_, f32[64,512]{1,0:T(8,128)S(1)} %collective-permute-done.23.refs_3_, ...), custom_call_target="tpu_custom_call" | custom-call | bytes 2097152 | tf_op jit(solution)/shard_map/place_slices/pallas_call | solution.py:235
  97.7 7.4 %collective-permute-done.15.refs_1_ = bf16[256,512]{1,0:T(8,128)(2,1)S(1)} collective-permute-done((bf16[256,512]{1,0:T(8,128)(2,1)S(1)}, bf16[256,512]{1,0:T(8,128)(2,1)S(1)}, u32[]{:S(2)}, u32[]{:S(2)}) %collective-permute-start.15) | collective-permute-done | bytes 262176 | tf_op jit(solution)/shard_map/ppermute | solution.py:32
  (54 shorter events, 13.1 us)
Async XLA Ops:
  0.6 10.2 %collective-permute-start = (bf16[256,512]{1,0:T(8,128)(2,1)}, bf16[256,512]{1,0:T(8,128)(2,1)S(1)}, u32[]{:S(2)}, u32[]{:S(2)}) collective-permute-start(bf16[256,512]{1,0:T(8,128)(2,1)} %refs_1_.1), channel_id=1, source_target_pairs={{0,16},{4,12},{8,24},{12,4},{16,0},{20,28},{24,8},{28,20},{1,17},{... | collective-permute-start | bytes 786440 | tf_op jit(solution)/shard_map/ppermute | solution.py:32
  4.7 15.9 %collective-permute-start.3 = (bf16[256,512]{1,0:T(8,128)(2,1)}, bf16[256,512]{1,0:T(8,128)(2,1)S(1)}, u32[]{:S(2)}, u32[]{:S(2)}) collective-permute-start(bf16[256,512]{1,0:T(8,128)(2,1)} %refs_1_.1), channel_id=1, source_target_pairs={{0,4},{4,0},{8,12},{12,8},{16,20},{20,16},{24,28},{28,24},{1,5},{5... | collective-permute-start | bytes 786440 | tf_op jit(solution)/shard_map/ppermute | solution.py:26
  10.9 9.7 %collective-permute-start.4 = (bf16[256,512]{1,0:T(8,128)(2,1)S(1)}, bf16[256,512]{1,0:T(8,128)(2,1)S(1)}, u32[]{:S(2)}, u32[]{:S(2)}) collective-permute-start(bf16[256,512]{1,0:T(8,128)(2,1)S(1)} %collective-permute-done.refs_3_), channel_id=1, source_target_pairs={{0,4},{4,0},{8,12},{12,8},{16,20},{20,16},{24,28},{28,24},{1,5},{5... | collective-permute-start | bytes 786440 | tf_op jit(solution)/shard_map/ppermute | solution.py:26
  11.6 12.1 %collective-permute-start.1 = (bf16[256,512]{1,0:T(8,128)(2,1)}, bf16[256,512]{1,0:T(8,128)(2,1)S(1)}, u32[]{:S(2)}, u32[]{:S(2)}) collective-permute-start(bf16[256,512]{1,0:T(8,128)(2,1)} %refs_1_.1), channel_id=1, source_target_pairs={{0,8},{4,20},{8,0},{12,28},{16,24},{20,4},{24,16},{28,12},{1,9},{5... | collective-permute-start | bytes 786440 | tf_op jit(solution)/shard_map/ppermute | solution.py:32
  14.1 13.0 %collective-permute-start.2 = (bf16[256,512]{1,0:T(8,128)(2,1)S(1)}, bf16[256,512]{1,0:T(8,128)(2,1)S(1)}, u32[]{:S(2)}, u32[]{:S(2)}) collective-permute-start(bf16[256,512]{1,0:T(8,128)(2,1)S(1)} %collective-permute-done.refs_3_), channel_id=1, source_target_pairs={{0,8},{4,20},{8,0},{12,28},{16,24},{20,4},{24,16},{28,12},{1,9},{5... | collective-permute-start | bytes 786440 | tf_op jit(solution)/shard_map/ppermute | solution.py:32
  15.1 2.2 %copy-start = (bf16[1,1,8,16,128,128]{5,4,3,2,1,0:T(8,128)(2,1)S(1)}, bf16[1,1,8,16,128,128]{5,4,3,2,1,0:T(8,128)(2,1)}, u32[]{:S(2)}) copy-start(bf16[1,1,8,16,128,128]{5,4,3,2,1,0:T(8,128)(2,1)} %param.10) | copy-start | bytes 12582916
  17.2 3.4 %copy-start.2 = (bf16[256,512]{1,0:T(8,128)(2,1)S(1)}, bf16[256,512]{1,0:T(8,128)(2,1)}, u32[]{:S(2)}) copy-start(bf16[256,512]{1,0:T(8,128)(2,1)} %refs_1_.1) | copy-start | bytes 786436
  27.1 1.5 %collective-permute-start.5 = (bf16[256,512]{1,0:T(8,128)(2,1)S(1)}, bf16[256,512]{1,0:T(8,128)(2,1)S(1)}, u32[]{:S(2)}, u32[]{:S(2)}) collective-permute-start(bf16[256,512]{1,0:T(8,128)(2,1)S(1)} %collective-permute-done.1.refs_1_), channel_id=1, source_target_pairs={{0,4},{4,0},{8,12},{12,8},{16,20},{20,16},{24,28},{28,24},{1,5},{5... | collective-permute-start | bytes 786440 | tf_op jit(solution)/shard_map/ppermute | solution.py:26
  27.1 1.9 %collective-permute-start.6 = (bf16[256,512]{1,0:T(8,128)(2,1)S(1)}, bf16[256,512]{1,0:T(8,128)(2,1)S(1)}, u32[]{:S(2)}, u32[]{:S(2)}) collective-permute-start(bf16[256,512]{1,0:T(8,128)(2,1)S(1)} %collective-permute-done.2.refs_3_), channel_id=1, source_target_pairs={{0,4},{4,0},{8,12},{12,8},{16,20},{20,16},{24,28},{28,24},{1,5},{5... | collective-permute-start | bytes 786440 | tf_op jit(solution)/shard_map/ppermute | solution.py:26
  30.2 15.5 %copy-start.1 = (bf16[512,512]{1,0:T(8,128)(2,1)S(1)}, bf16[512,512]{1,0:T(8,128)(2,1)}, u32[]{:S(2)}) copy-start(bf16[512,512]{1,0:T(8,128)(2,1)} %refs_4_.1) | copy-start | bytes 1572868
  30.3 15.5 %copy-start.3 = (bf16[256,512]{1,0:T(8,128)(2,1)S(1)}, bf16[256,512]{1,0:T(8,128)(2,1)}, u32[]{:S(2)}) copy-start(bf16[256,512]{1,0:T(8,128)(2,1)} %refs_3_.1) | copy-start | bytes 786436
  30.3 6.4 %collective-permute-start.8 = (bf16[256,512]{1,0:T(8,128)(2,1)S(1)}, bf16[256,512]{1,0:T(8,128)(2,1)S(1)}, u32[]{:S(2)}, u32[]{:S(2)}) collective-permute-start(bf16[256,512]{1,0:T(8,128)(2,1)S(1)} %get-tuple-element.48), channel_id=1, source_target_pairs={{0,1},{1,0},{2,3},{3,2},{4,6},{5,7},{6,4},{7,5},{8,9},{9,8},{10,11... | collective-permute-start | bytes 786440 | tf_op jit(solution)/shard_map/ppermute | solution.py:42
  36.8 8.9 %collective-permute-start.9 = (bf16[256,512]{1,0:T(8,128)(2,1)S(1)}, bf16[256,512]{1,0:T(8,128)(2,1)S(1)}, u32[]{:S(2)}, u32[]{:S(2)}) collective-permute-start(bf16[256,512]{1,0:T(8,128)(2,1)S(1)} %add_convert_fusion.2), channel_id=1, source_target_pairs={{0,2},{1,3},{2,0},{3,1},{4,5},{5,4},{6,7},{7,6},{8,10},{9,11},{10,... | collective-permute-start | bytes 786440 | tf_op jit(solution)/shard_map/ppermute | solution.py:42
  38.5 7.2 %collective-permute-start.7 = (bf16[256,512]{1,0:T(8,128)(2,1)S(1)}, bf16[256,512]{1,0:T(8,128)(2,1)S(1)}, u32[]{:S(2)}, u32[]{:S(2)}) collective-permute-start(bf16[256,512]{1,0:T(8,128)(2,1)S(1)} %get-tuple-element.46), channel_id=1, source_target_pairs={{0,1},{1,0},{2,3},{3,2},{4,6},{5,7},{6,4},{7,5},{8,9},{9,8},{10,11... | collective-permute-start | bytes 786440 | tf_op jit(solution)/shard_map/ppermute | solution.py:42
  46.9 6.4 %collective-permute-start.10 = (bf16[256,512]{1,0:T(8,128)(2,1)S(1)}, bf16[256,512]{1,0:T(8,128)(2,1)S(1)}, u32[]{:S(2)}, u32[]{:S(2)}) collective-permute-start(bf16[256,512]{1,0:T(8,128)(2,1)S(1)} %get-tuple-element.60.refs_2_), channel_id=1, source_target_pairs={{0,2},{1,3},{2,0},{3,1},{4,5},{5,4},{6,7},{7,6},{8,10},{9,11},{10,... | collective-permute-start | bytes 786440 | tf_op jit(solution)/shard_map/ppermute | solution.py:42
  49.4 4.7 %collective-permute-start.16 = (bf16[256,512]{1,0:T(8,128)(2,1)S(1)}, bf16[256,512]{1,0:T(8,128)(2,1)S(1)}, u32[]{:S(2)}, u32[]{:S(2)}) collective-permute-start(bf16[256,512]{1,0:T(8,128)(2,1)S(1)} %get-tuple-element.68), channel_id=1, source_target_pairs={{0,4},{4,0},{8,12},{12,8},{16,20},{20,16},{24,28},{28,24},{1,5},{5... | collective-permute-start | bytes 786440 | tf_op jit(solution)/shard_map/ppermute | solution.py:26
  53.3 9.9 %collective-permute-start.11 = (bf16[512,512]{1,0:T(8,128)(2,1)S(1)}, bf16[512,512]{1,0:T(8,128)(2,1)S(1)}, u32[]{:S(2)}, u32[]{:S(2)}) collective-permute-start(bf16[512,512]{1,0:T(8,128)(2,1)S(1)} %pad_maximum_fusion), channel_id=1, source_target_pairs={{0,1},{1,0},{2,3},{3,2},{4,6},{5,7},{6,4},{7,5},{8,9},{9,8},{10,11... | collective-permute-start | bytes 1572872 | tf_op jit(solution)/shard_map/ppermute | solution.py:42
  54.1 6.5 %collective-permute-start.17 = (bf16[128,512]{1,0:T(8,128)(2,1)S(1)}, bf16[128,512]{1,0:T(8,128)(2,1)S(1)}, u32[]{:S(2)}, u32[]{:S(2)}) collective-permute-start(bf16[128,512]{1,0:T(8,128)(2,1)S(1)} %pad_maximum_fusion.3), channel_id=1, source_target_pairs={{0,2},{1,3},{2,0},{3,1},{4,5},{5,4},{6,7},{7,6},{8,10},{9,11},{10,... | collective-permute-start | bytes 393224 | tf_op jit(solution)/shard_map/ppermute | solution.py:42
  60.6 4.3 %collective-permute-start.18 = (bf16[64,512]{1,0:T(8,128)(2,1)S(1)}, bf16[64,512]{1,0:T(8,128)(2,1)S(1)}, u32[]{:S(2)}, u32[]{:S(2)}) collective-permute-start(bf16[64,512]{1,0:T(8,128)(2,1)S(1)} %add_convert_fusion.5), channel_id=1, source_target_pairs={{0,1},{1,0},{2,3},{3,2},{4,6},{5,7},{6,4},{7,5},{8,9},{9,8},{10,11... | collective-permute-start | bytes 196616 | tf_op jit(solution)/shard_map/ppermute | solution.py:42
  63.9 8.7 %collective-permute-start.12 = (bf16[512,512]{1,0:T(8,128)(2,1)S(1)}, bf16[512,512]{1,0:T(8,128)(2,1)S(1)}, u32[]{:S(2)}, u32[]{:S(2)}) collective-permute-start(bf16[512,512]{1,0:T(8,128)(2,1)S(1)} %backward.4), channel_id=1, source_target_pairs={{0,4},{4,0},{8,12},{12,8},{16,20},{20,16},{24,28},{28,24},{1,5},{5... | collective-permute-start | bytes 1572872 | tf_op jit(solution)/shard_map/ppermute | solution.py:26
  65.0 5.2 %collective-permute-start.19 = (bf16[64,512]{1,0:T(8,128)(2,1)S(1)}, bf16[64,512]{1,0:T(8,128)(2,1)S(1)}, u32[]{:S(2)}, u32[]{:S(2)}) collective-permute-start(bf16[64,512]{1,0:T(8,128)(2,1)S(1)} %add_convert_fusion.4), channel_id=1, source_target_pairs={{0,16},{4,12},{8,24},{12,4},{16,0},{20,28},{24,8},{28,20},{1,17},{... | collective-permute-start | bytes 196616 | tf_op jit(solution)/shard_map/ppermute | solution.py:32
  70.3 5.8 %collective-permute-start.20 = (bf16[64,512]{1,0:T(8,128)(2,1)S(1)}, bf16[64,512]{1,0:T(8,128)(2,1)S(1)}, u32[]{:S(2)}, u32[]{:S(2)}) collective-permute-start(bf16[64,512]{1,0:T(8,128)(2,1)S(1)} %add_convert_fusion.3), channel_id=1, source_target_pairs={{0,8},{4,20},{8,0},{12,28},{16,24},{20,4},{24,16},{28,12},{1,9},{5... | collective-permute-start | bytes 196616 | tf_op jit(solution)/shard_map/ppermute | solution.py:32
  72.8 22.0 %collective-permute-start.14 = (bf16[512,512]{1,0:T(8,128)(2,1)S(1)}, bf16[512,512]{1,0:T(8,128)(2,1)S(1)}, u32[]{:S(2)}, u32[]{:S(2)}) collective-permute-start(bf16[512,512]{1,0:T(8,128)(2,1)S(1)} %pad_maximum_fusion.1), channel_id=1, source_target_pairs={{0,8},{4,20},{8,0},{12,28},{16,24},{20,4},{24,16},{28,12},{1,9},{5... | collective-permute-start | bytes 1572872 | tf_op jit(solution)/shard_map/ppermute | solution.py:32
  73.6 21.2 %collective-permute-start.13 = (bf16[512,512]{1,0:T(8,128)(2,1)S(1)}, bf16[512,512]{1,0:T(8,128)(2,1)S(1)}, u32[]{:S(2)}, u32[]{:S(2)}) collective-permute-start(bf16[512,512]{1,0:T(8,128)(2,1)S(1)} %backward.7), channel_id=1, source_target_pairs={{0,4},{4,0},{8,12},{12,8},{16,20},{20,16},{24,28},{28,24},{1,5},{5... | collective-permute-start | bytes 1572872 | tf_op jit(solution)/shard_map/ppermute | solution.py:26
  76.1 13.3 %collective-permute-start.21 = (f32[64,512]{1,0:T(8,128)S(1)}, f32[64,512]{1,0:T(8,128)S(1)}, u32[]{:S(2)}, u32[]{:S(2)}) collective-permute-start(f32[64,512]{1,0:T(8,128)S(1)} %add_multiply_fusion.refs_0_), channel_id=1, source_target_pairs={{0,1},{1,0},{2,3},{3,2},{4,6},{5,7},{6,4},{7,5},{8,9},{9,8},{10,11... | collective-permute-start | bytes 393224 | tf_op jit(solution)/shard_map/ppermute | solution.py:42
  86.5 5.0 %collective-permute-start.22 = (f32[64,512]{1,0:T(8,128)S(1)}, f32[64,512]{1,0:T(8,128)S(1)}, u32[]{:S(2)}, u32[]{:S(2)}) collective-permute-start(f32[64,512]{1,0:T(8,128)S(1)} %add_multiply_fusion.refs_0_), channel_id=1, source_target_pairs={{0,2},{1,3},{2,0},{3,1},{4,5},{5,4},{6,7},{7,6},{8,10},{9,11},{10,... | collective-permute-start | bytes 393224 | tf_op jit(solution)/shard_map/ppermute | solution.py:42
  88.1 5.9 %collective-permute-start.23 = (f32[64,512]{1,0:T(8,128)S(1)}, f32[64,512]{1,0:T(8,128)S(1)}, u32[]{:S(2)}, u32[]{:S(2)}) collective-permute-start(f32[64,512]{1,0:T(8,128)S(1)} %add_multiply_fusion.refs_0_), channel_id=1, source_target_pairs={{0,3},{1,2},{2,1},{3,0},{4,7},{5,6},{6,5},{7,4},{8,11},{9,10},{10,... | collective-permute-start | bytes 393224 | tf_op jit(solution)/shard_map/ppermute | solution.py:42
  94.0 2.1 %collective-permute-start.24 = (f32[256,512]{1,0:T(8,128)S(1)}, f32[256,512]{1,0:T(8,128)S(1)}, u32[]{:S(2)}, u32[]{:S(2)}) collective-permute-start(f32[256,512]{1,0:T(8,128)S(1)} %pad_maximum_fusion.2), channel_id=1, source_target_pairs={{0,4},{4,0},{8,12},{12,8},{16,20},{20,16},{24,28},{28,24},{1,5},{5... | collective-permute-start | bytes 1572872 | tf_op jit(solution)/shard_map/ppermute | solution.py:26
  95.0 10.1 %collective-permute-start.15 = (bf16[256,512]{1,0:T(8,128)(2,1)S(1)}, bf16[256,512]{1,0:T(8,128)(2,1)S(1)}, u32[]{:S(2)}, u32[]{:S(2)}) collective-permute-start(bf16[256,512]{1,0:T(8,128)(2,1)S(1)} %get-tuple-element.64), channel_id=1, source_target_pairs={{0,16},{4,12},{8,24},{12,4},{16,0},{20,28},{24,8},{28,20},{1,17},{... | collective-permute-start | bytes 786440 | tf_op jit(solution)/shard_map/ppermute | solution.py:32

commit v7 on v6

--- a/solution.py
+++ b/solution.py
@@ -349,6 +349,8 @@
     for k in range(1, chips):
         given = after(features, held[k - 1]) if k == top_bit(k) > 1 else held[k - top_bit(k)]
         held.append(swap_chips(given, top_bit(k)))
+        if k == 1:
+            held[1] = after(held[1], spots)
     totals = None
     for first, stop in ((0, chips // 2), (chips // 2, chips)):
         sources = []
@@ -361,7 +363,7 @@
         totals = forward(dense, 2 * first, sources, totals, dtypes)
 
     pieces = collect(totals, swap_members)
-    dense_t = transposed(after(dense, *totals))
+    dense_t = transposed(after(dense, *totals, pieces[1]))
     pieces[-1] = after(pieces[-1], *dense_t)
     activated, agg, pre_grad, grad = middle(pieces, cotangent, weight)
     owns, send = weight_part(agg, pre_grad, place, groups)
@@ -372,9 +374,13 @@
         slots = sum(x.shape[0] for x in grads) // rows_local
         grads.append(swap_members(jnp.concatenate(grads) if slots > 1 else grad, slots))
         if slots == 1:
-            kept, got = halve(parts, functools.partial(swap_members, turn=1))
-            part = (kept + got.astype(jnp.float32)).astype(jnp.bfloat16)
-    part = after(part, grads[-1])
+            part = parts[0]
+            for k in range(1, groups):
+                part = part + swap_members(parts[k].astype(jnp.bfloat16), k, turn=1).astype(jnp.float32)
+            part = part.astype(jnp.bfloat16)
+            near = swap_chips(part, 1)
+            part = part.astype(jnp.float32) + near.astype(jnp.float32)
+    grads[-1] = after(grads[-1], near)
 
     half = chips // 2
     other = backward(dense_t[half:], grads, 1)
@@ -391,11 +397,12 @@
         totals, arrived = totals[:half], [swap_chips(send, half)]
     (feature_grad,) = settle(totals, arrived, [jnp.bfloat16])
 
-    bit = 1
+    bit = 2
     while bit < chips:
+        part = part.astype(jnp.bfloat16)
         part = part.astype(jnp.float32) + swap_chips(part, bit).astype(jnp.float32)
         bit *= 2
-        part = part.astype(jnp.bfloat16) if bit < chips else part * scale
+    part = part * scale
     parts = [part] + [swap_members(part, k, turn=1) for k in range(1, groups)]
     weight_grad = place_slices(parts, swap_cores(jnp.concatenate(parts)), place)
     return (activated, feature_grad, weight_grad)

time: 106 us -> 97.1 us (0.916)
  starting transfers between devices: 36.2 us -> 31.6 us
  waiting for transfers between devices: 50.1 us -> 45.8 us
    ppermute x10 -> x11, starting transfers between devices: 22.1 us -> 14.4 us  [swap_members(): return lax.ppermute(x, ('dom', 'repl'), pairs)]
    ppermute x7, starting transfers between devices: 13.3 us -> 15.8 us  [swap_chips(): lax.ppermute(x, 'dom', [(i, i ^ 2 * between(held, i % 2, bits)) for i in...]
    ppermute x10 -> x11, waiting for transfers between devices: 26 us -> 23.7 us  [swap_members(): return lax.ppermute(x, ('dom', 'repl'), pairs)]
    ppermute x7, waiting for transfers between devices: 22.7 us -> 20.6 us  [swap_chips(): lax.ppermute(x, 'dom', [(i, i ^ 2 * between(held, i % 2, bits)) for i in...]
  transfers between devices with their start and end apart: 25 -> 26, of which waited for: 17 -> 15; matrix products, arithmetic and copies ran while one was open for 2% -> 2% of each run, Pallas kernels for 11% -> 11%
where the time goes in v7:
time: 97.1 us; the launch traced here: 96.9 us
  waiting for transfers between devices  45.8 us (47%)
  starting transfers between devices  31.6 us (33%)
  Pallas kernels  14.4 us (15%)
  local copies, waits for them, and re-layouts  2.93 us (3%)
  other arithmetic  1.33 us (1%)
    ppermute x11, waiting for transfers between devices, swap_members(): return lax.ppermute(x, ('dom', 'repl'), pairs)  23.7 us
    ppermute x7, waiting for transfers between devices, swap_chips(): lax.ppermute(x, 'dom', [(i, i ^ 2 * between(held, i % 2, bits)) for i in...  20.6 us
    ppermute x7, starting transfers between devices, swap_chips(): lax.ppermute(x, 'dom', [(i, i ^ 2 * between(held, i % 2, bits)) for i in...  15.8 us
    ppermute x11, starting transfers between devices, swap_members(): return lax.ppermute(x, ('dom', 'repl'), pairs)  14.4 us
    pallas_call x1, Pallas kernels, densify(): pl.pallas_call(functools.partial(densify_kernel, col_tiles=col_tiles), ou...  3.33 us
    pallas_call x4, Pallas kernels, backward(): pl.pallas_call(functools.partial(backward_kernel, side=side, count=count,...  2.8 us
    pallas_call x2, Pallas kernels, forward(): pl.pallas_call(functools.partial(forward_kernel, first=first, count=len(s...  2.49 us
    unnamed x8, local copies, waits for them, and re-layouts  2.2 us
  transfers between devices with their start and end apart: 26, of which 15 were waited for; matrix products, arithmetic and copies ran while one was open for 2% of the time, Pallas kernels for 11%

profile of v7, /device:TPU:0, one launch (start us, length us, event | category | flops | bytes accessed | tf_op | source)
XLA Modules:
  0.0 96.9 jit_solution(11337315934042666650)
XLA Ops:
  0.6 4.1 %collective-permute-start = (bf16[256,512]{1,0:T(8,128)(2,1)}, bf16[256,512]{1,0:T(8,128)(2,1)S(1)}, u32[]{:S(2)}, u32[]{:S(2)}) collective-permute-start(bf16[256,512]{1,0:T(8,128)(2,1)} %refs_1_.1), channel_id=1, source_target_pairs={{0,16},{4,12},{8,24},{12,4},{16,0},{20,28},{24,8},{28,20},{1,17},{... | collective-permute-start | bytes 786440 | tf_op jit(solution)/shard_map/ppermute | solution.py:32
  6.3 4.6 %collective-permute-done.refs_3_ = bf16[256,512]{1,0:T(8,128)(2,1)S(1)} collective-permute-done((bf16[256,512]{1,0:T(8,128)(2,1)}, bf16[256,512]{1,0:T(8,128)(2,1)S(1)}, u32[]{:S(2)}, u32[]{:S(2)}) %collective-permute-start) | collective-permute-done | bytes 262176 | tf_op jit(solution)/shard_map/ppermute | solution.py:32
  10.9 2.4 %collective-permute-start.1 = (bf16[256,512]{1,0:T(8,128)(2,1)}, bf16[256,512]{1,0:T(8,128)(2,1)S(1)}, u32[]{:S(2)}, u32[]{:S(2)}) collective-permute-start(bf16[256,512]{1,0:T(8,128)(2,1)} %refs_1_.1), channel_id=1, source_target_pairs={{0,8},{4,20},{8,0},{12,28},{16,24},{20,4},{24,16},{28,12},{1,9},{5... | collective-permute-start | bytes 786440 | tf_op jit(solution)/shard_map/ppermute | solution.py:32
  13.4 2.2 %copy-done = bf16[1,1,8,16,128,128]{5,4,3,2,1,0:T(8,128)(2,1)S(1)} copy-done((bf16[1,1,8,16,128,128]{5,4,3,2,1,0:T(8,128)(2,1)S(1)}, bf16[1,1,8,16,128,128]{5,4,3,2,1,0:T(8,128)(2,1)}, u32[]{:S(2)}) %copy-start) | copy-done | bytes 4194328
  15.6 3.3 %densify.1.refs_0_.a_ref = bf16[8,1024,256]{2,1,0:T(8,128)(2,1)S(1)} custom-call(s32[8,17]{1,0:T(8,128)S(1)} %pad_add_fusion.spots_ref, s32[2]{0:T(128)S(1)} %pad_add_fusion.1.place_ref, bf16[8,16,128,128]{3,2,1,0:T(8,128)(2,1)S(1)} %bitcast.26), custom_call_target="tpu_custom_call" | custom-call | flops 2097152 | bytes 16777216 | tf_op jit(solution)/shard_map/densify/pallas_call | solution.py:86
  19.0 1.2 %forward.2 = (f32[256,512]{1,0:T(8,128)S(1)}, f32[256,512]{1,0:T(8,128)S(1)}, f32[256,512]{1,0:T(8,128)S(1)}, f32[256,512]{1,0:T(8,128)S(1)}) custom-call(bf16[8,1024,256]{2,1,0:T(8,128)(2,1)S(1)} %densify.1.refs_0_.a_ref, bf16[256,512]{1,0:T(8,128)(2,1)S(1)} %copy-done.2, bf16[256,512]{1,0:T(8,128)(2,1)S(1)} %collective-permute-done.3.refs_2_, ...), custom_call_target="tpu_custom_call" | custom-call | flops 1073741824 | bytes 4194304 | tf_op jit(solution)/shard_map/forward/pallas_call | solution.py:139
  20.2 2.7 %collective-permute-done.1.refs_1_ = bf16[256,512]{1,0:T(8,128)(2,1)S(1)} collective-permute-done((bf16[256,512]{1,0:T(8,128)(2,1)}, bf16[256,512]{1,0:T(8,128)(2,1)S(1)}, u32[]{:S(2)}, u32[]{:S(2)}) %collective-permute-start.1) | collective-permute-done | bytes 262176 | tf_op jit(solution)/shard_map/ppermute | solution.py:32
  22.9 3.4 %collective-permute-done.2.refs_3_ = bf16[256,512]{1,0:T(8,128)(2,1)S(1)} collective-permute-done((bf16[256,512]{1,0:T(8,128)(2,1)S(1)}, bf16[256,512]{1,0:T(8,128)(2,1)S(1)}, u32[]{:S(2)}, u32[]{:S(2)}) %collective-permute-start.2) | collective-permute-done | bytes 262176 | tf_op jit(solution)/shard_map/ppermute | solution.py:32
  28.2 1.2 %forward.3 = (f32[256,512]{1,0:T(8,128)S(1)}, f32[256,512]{1,0:T(8,128)S(1)}, bf16[256,512]{1,0:T(8,128)(2,1)S(1)}, bf16[256,512]{1,0:T(8,128)(2,1)S(1)}) custom-call(bf16[8,1024,256]{2,1,0:T(8,128)(2,1)S(1)} %densify.1.refs_0_.a_ref, bf16[256,512]{1,0:T(8,128)(2,1)S(1)} %collective-permute-done.1.refs_1_, ...), custom_call_target="tpu_custom_call" | custom-call | flops 1073741824 | bytes 4194304 | tf_op jit(solution)/shard_map/forward/pallas_call | solution.py:139
  29.5 1.7 %collective-permute-start.8 = (bf16[256,512]{1,0:T(8,128)(2,1)S(1)}, bf16[256,512]{1,0:T(8,128)(2,1)S(1)}, u32[]{:S(2)}, u32[]{:S(2)}) collective-permute-start(bf16[256,512]{1,0:T(8,128)(2,1)S(1)} %get-tuple-element.50), channel_id=1, source_target_pairs={{0,1},{1,0},{2,3},{3,2},{4,6},{5,7},{6,4},{7,5},{8,9},{9,8},{10,11... | collective-permute-start | bytes 786440 | tf_op jit(solution)/shard_map/ppermute | solution.py:42
  31.6 4.3 %collective-permute-done.8 = bf16[256,512]{1,0:T(8,128)(2,1)S(1)} collective-permute-done((bf16[256,512]{1,0:T(8,128)(2,1)S(1)}, bf16[256,512]{1,0:T(8,128)(2,1)S(1)}, u32[]{:S(2)}, u32[]{:S(2)}) %collective-permute-start.8) | collective-permute-done | bytes 262176 | tf_op jit(solution)/shard_map/ppermute | solution.py:42
  36.0 1.8 %collective-permute-start.9 = (bf16[256,512]{1,0:T(8,128)(2,1)S(1)}, bf16[256,512]{1,0:T(8,128)(2,1)S(1)}, u32[]{:S(2)}, u32[]{:S(2)}) collective-permute-start(bf16[256,512]{1,0:T(8,128)(2,1)S(1)} %add_convert_fusion.2), channel_id=1, source_target_pairs={{0,2},{1,3},{2,0},{3,1},{4,5},{5,4},{6,7},{7,6},{8,10},{9,11},{10,... | collective-permute-start | bytes 786440 | tf_op jit(solution)/shard_map/ppermute | solution.py:42
  37.8 1.7 %collective-permute-done.7.refs_1_ = bf16[256,512]{1,0:T(8,128)(2,1)S(1)} collective-permute-done((bf16[256,512]{1,0:T(8,128)(2,1)S(1)}, bf16[256,512]{1,0:T(8,128)(2,1)S(1)}, u32[]{:S(2)}, u32[]{:S(2)}) %collective-permute-start.7) | collective-permute-done | bytes 262176 | tf_op jit(solution)/shard_map/ppermute | solution.py:42
  39.5 1.2 %transposed.1 = (bf16[2,256,1024]{2,1,0:T(8,128)(2,1)S(1)}, bf16[2,256,1024]{2,1,0:T(8,128)(2,1)S(1)}, bf16[2,256,1024]{2,1,0:T(8,128)(2,1)S(1)}, bf16[2,256,1024]{2,1,0:T(8,128)(2,1)S(1)}) custom-call(bf16[8,1024,256]{2,1,0:T(8,128)(2,1)S(1)} %densify.1.refs_0_.a_ref), custom_call_target="tpu_custom_call" | custom-call | bytes 8388608 | tf_op jit(solution)/shard_map/transposed/pallas_call | solution.py:111
  40.7 1.8 %collective-permute-done.9.refs_2_ = bf16[256,512]{1,0:T(8,128)(2,1)S(1)} collective-permute-done((bf16[256,512]{1,0:T(8,128)(2,1)S(1)}, bf16[256,512]{1,0:T(8,128)(2,1)S(1)}, u32[]{:S(2)}, u32[]{:S(2)}) %collective-permute-start.9) | collective-permute-done | bytes 262176 | tf_op jit(solution)/shard_map/ppermute | solution.py:42
  43.6 1.7 %collective-permute-start.10 = (bf16[256,512]{1,0:T(8,128)(2,1)S(1)}, bf16[256,512]{1,0:T(8,128)(2,1)S(1)}, u32[]{:S(2)}, u32[]{:S(2)}) collective-permute-start(bf16[256,512]{1,0:T(8,128)(2,1)S(1)} %get-tuple-element.70.refs_2_), channel_id=1, source_target_pairs={{0,2},{1,3},{2,0},{3,1},{4,5},{5,4},{6,7},{7,6},{8,10},{9,11},{10,... | collective-permute-start | bytes 786440 | tf_op jit(solution)/shard_map/ppermute | solution.py:42
  46.3 3.6 %collective-permute-done.10.refs_3_ = bf16[256,512]{1,0:T(8,128)(2,1)S(1)} collective-permute-done((bf16[256,512]{1,0:T(8,128)(2,1)S(1)}, bf16[256,512]{1,0:T(8,128)(2,1)S(1)}, u32[]{:S(2)}, u32[]{:S(2)}) %collective-permute-start.10) | collective-permute-done | bytes 262176 | tf_op jit(solution)/shard_map/ppermute | solution.py:42
  50.0 1.7 %collective-permute-start.11 = (bf16[512,512]{1,0:T(8,128)(2,1)S(1)}, bf16[512,512]{1,0:T(8,128)(2,1)S(1)}, u32[]{:S(2)}, u32[]{:S(2)}) collective-permute-start(bf16[512,512]{1,0:T(8,128)(2,1)S(1)} %pad_maximum_fusion), channel_id=1, source_target_pairs={{0,1},{1,0},{2,3},{3,2},{4,6},{5,7},{6,4},{7,5},{8,9},{9,8},{10,11... | collective-permute-start | bytes 1572872 | tf_op jit(solution)/shard_map/ppermute | solution.py:42
  51.8 1.6 %collective-permute-start.15 = (bf16[64,512]{1,0:T(8,128)(2,1)S(1)}, bf16[64,512]{1,0:T(8,128)(2,1)S(1)}, u32[]{:S(2)}, u32[]{:S(2)}) collective-permute-start(bf16[64,512]{1,0:T(8,128)(2,1)S(1)} %get-tuple-element.78), channel_id=1, source_target_pairs={{0,3},{1,2},{2,1},{3,0},{4,7},{5,6},{6,5},{7,4},{8,11},{9,10},{10,... | collective-permute-start | bytes 196616 | tf_op jit(solution)/shard_map/ppermute | solution.py:42
  53.7 1.7 %collective-permute-start.13 = (bf16[64,512]{1,0:T(8,128)(2,1)S(1)}, bf16[64,512]{1,0:T(8,128)(2,1)S(1)}, u32[]{:S(2)}, u32[]{:S(2)}) collective-permute-start(bf16[64,512]{1,0:T(8,128)(2,1)S(1)} %get-tuple-element.77), channel_id=1, source_target_pairs={{0,1},{1,0},{2,3},{3,2},{4,6},{5,7},{6,4},{7,5},{8,9},{9,8},{10,11... | collective-permute-start | bytes 196616 | tf_op jit(solution)/shard_map/ppermute | solution.py:42
  55.4 6.4 %collective-permute-done.15 = bf16[64,512]{1,0:T(8,128)(2,1)S(1)} collective-permute-done((bf16[64,512]{1,0:T(8,128)(2,1)S(1)}, bf16[64,512]{1,0:T(8,128)(2,1)S(1)}, u32[]{:S(2)}, u32[]{:S(2)}) %collective-permute-start.15) | collective-permute-done | bytes 65568 | tf_op jit(solution)/shard_map/ppermute | solution.py:42
  61.8 3.0 %collective-permute-start.16 = (bf16[64,512]{1,0:T(8,128)(2,1)S(1)}, bf16[64,512]{1,0:T(8,128)(2,1)S(1)}, u32[]{:S(2)}, u32[]{:S(2)}) collective-permute-start(bf16[64,512]{1,0:T(8,128)(2,1)S(1)} %add_convert_fusion.4), channel_id=1, source_target_pairs={{0,16},{4,12},{8,24},{12,4},{16,0},{20,28},{24,8},{28,20},{1,17},{... | collective-permute-start | bytes 196616 | tf_op jit(solution)/shard_map/ppermute | solution.py:32
  64.7 2.3 %collective-permute-done.16 = bf16[64,512]{1,0:T(8,128)(2,1)S(1)} collective-permute-done((bf16[64,512]{1,0:T(8,128)(2,1)S(1)}, bf16[64,512]{1,0:T(8,128)(2,1)S(1)}, u32[]{:S(2)}, u32[]{:S(2)}) %collective-permute-start.16) | collective-permute-done | bytes 65568 | tf_op jit(solution)/shard_map/ppermute | solution.py:32
  67.8 2.3 %collective-permute-start.21 = (bf16[64,512]{1,0:T(8,128)(2,1)S(1)}, bf16[64,512]{1,0:T(8,128)(2,1)S(1)}, u32[]{:S(2)}, u32[]{:S(2)}) collective-permute-start(bf16[64,512]{1,0:T(8,128)(2,1)S(1)} %add_convert_fusion.3), channel_id=1, source_target_pairs={{0,8},{4,20},{8,0},{12,28},{16,24},{20,4},{24,16},{28,12},{1,9},{5... | collective-permute-start | bytes 196616 | tf_op jit(solution)/shard_map/ppermute | solution.py:32
  74.6 1.3 %collective-permute-start.23 = (f32[64,512]{1,0:T(8,128)S(1)}, f32[64,512]{1,0:T(8,128)S(1)}, u32[]{:S(2)}, u32[]{:S(2)}) collective-permute-start(f32[64,512]{1,0:T(8,128)S(1)} %add_multiply_fusion.refs_0_), channel_id=1, source_target_pairs={{0,2},{1,3},{2,0},{3,1},{4,5},{5,4},{6,7},{7,6},{8,10},{9,11},{10,... | collective-permute-start | bytes 393224 | tf_op jit(solution)/shard_map/ppermute | solution.py:42
  75.8 1.2 %collective-permute-start.24 = (f32[64,512]{1,0:T(8,128)S(1)}, f32[64,512]{1,0:T(8,128)S(1)}, u32[]{:S(2)}, u32[]{:S(2)}) collective-permute-start(f32[64,512]{1,0:T(8,128)S(1)} %add_multiply_fusion.refs_0_), channel_id=1, source_target_pairs={{0,3},{1,2},{2,1},{3,0},{4,7},{5,6},{6,5},{7,4},{8,11},{9,10},{10,... | collective-permute-start | bytes 393224 | tf_op jit(solution)/shard_map/ppermute | solution.py:42
  77.1 2.8 %collective-permute-done.22.refs_1_ = f32[64,512]{1,0:T(8,128)S(1)} collective-permute-done((f32[64,512]{1,0:T(8,128)S(1)}, f32[64,512]{1,0:T(8,128)S(1)}, u32[]{:S(2)}, u32[]{:S(2)}) %collective-permute-start.22) | collective-permute-done | bytes 131104 | tf_op jit(solution)/shard_map/ppermute | solution.py:42
  79.9 3.1 %collective-permute-done.24.refs_3_ = f32[64,512]{1,0:T(8,128)S(1)} collective-permute-done((f32[64,512]{1,0:T(8,128)S(1)}, f32[64,512]{1,0:T(8,128)S(1)}, u32[]{:S(2)}, u32[]{:S(2)}) %collective-permute-start.24) | collective-permute-done | bytes 131104 | tf_op jit(solution)/shard_map/ppermute | solution.py:42
  83.9 2.0 %collective-permute-done.19.refs_3_ = bf16[512,512]{1,0:T(8,128)(2,1)S(1)} collective-permute-done((bf16[512,512]{1,0:T(8,128)(2,1)S(1)}, bf16[512,512]{1,0:T(8,128)(2,1)S(1)}, u32[]{:S(2)}, u32[]{:S(2)}) %collective-permute-start.19) | collective-permute-done | bytes 524320 | tf_op jit(solution)/shard_map/ppermute | solution.py:32
  86.0 2.8 %collective-permute-start.20 = (bf16[256,512]{1,0:T(8,128)(2,1)S(1)}, bf16[256,512]{1,0:T(8,128)(2,1)S(1)}, u32[]{:S(2)}, u32[]{:S(2)}) collective-permute-start(bf16[256,512]{1,0:T(8,128)(2,1)S(1)} %get-tuple-element.74), channel_id=1, source_target_pairs={{0,16},{4,12},{8,24},{12,4},{16,0},{20,28},{24,8},{28,20},{1,17},{... | collective-permute-start | bytes 786440 | tf_op jit(solution)/shard_map/ppermute | solution.py:32
  88.9 1.6 %place_slices.1 = f32[512,512]{1,0:T(8,128)} custom-call(s32[2]{0:T(128)S(1)} %pad_add_fusion.1.place_ref, f32[64,512]{1,0:T(8,128)S(1)} %add_multiply_fusion.refs_0_, f32[64,512]{1,0:T(8,128)S(1)} %collective-permute-done.22.refs_1_, f32[64,512]{1,0:T(8,128)S(1)} %collective-permute-done.23.refs_2_, f32[64,512]{1,0:T(8,128)S(1)} %collective-permute-done.24.refs_3_, ...), custom_call_target="tpu_custom_call" | custom-call | bytes 2097152 | tf_op jit(solution)/shard_map/place_slices/pallas_call | solution.py:235
  90.5 5.7 %collective-permute-done.20.refs_1_ = bf16[256,512]{1,0:T(8,128)(2,1)S(1)} collective-permute-done((bf16[256,512]{1,0:T(8,128)(2,1)S(1)}, bf16[256,512]{1,0:T(8,128)(2,1)S(1)}, u32[]{:S(2)}, u32[]{:S(2)}) %collective-permute-start.20) | collective-permute-done | bytes 262176 | tf_op jit(solution)/shard_map/ppermute | solution.py:32
  (54 shorter events, 13.6 us)
Async XLA Ops:
  0.6 10.2 %collective-permute-start = (bf16[256,512]{1,0:T(8,128)(2,1)}, bf16[256,512]{1,0:T(8,128)(2,1)S(1)}, u32[]{:S(2)}, u32[]{:S(2)}) collective-permute-start(bf16[256,512]{1,0:T(8,128)(2,1)} %refs_1_.1), channel_id=1, source_target_pairs={{0,16},{4,12},{8,24},{12,4},{16,0},{20,28},{24,8},{28,20},{1,17},{... | collective-permute-start | bytes 786440 | tf_op jit(solution)/shard_map/ppermute | solution.py:32
  4.7 14.2 %collective-permute-start.3 = (bf16[256,512]{1,0:T(8,128)(2,1)}, bf16[256,512]{1,0:T(8,128)(2,1)S(1)}, u32[]{:S(2)}, u32[]{:S(2)}) collective-permute-start(bf16[256,512]{1,0:T(8,128)(2,1)} %refs_1_.1), channel_id=1, source_target_pairs={{0,4},{4,0},{8,12},{12,8},{16,20},{20,16},{24,28},{28,24},{1,5},{5... | collective-permute-start | bytes 786440 | tf_op jit(solution)/shard_map/ppermute | solution.py:26
  10.9 8.1 %collective-permute-start.4 = (bf16[256,512]{1,0:T(8,128)(2,1)S(1)}, bf16[256,512]{1,0:T(8,128)(2,1)S(1)}, u32[]{:S(2)}, u32[]{:S(2)}) collective-permute-start(bf16[256,512]{1,0:T(8,128)(2,1)S(1)} %collective-permute-done.refs_3_), channel_id=1, source_target_pairs={{0,4},{4,0},{8,12},{12,8},{16,20},{20,16},{24,28},{28,24},{1,5},{5... | collective-permute-start | bytes 786440 | tf_op jit(solution)/shard_map/ppermute | solution.py:26
  10.9 12.1 %collective-permute-start.1 = (bf16[256,512]{1,0:T(8,128)(2,1)}, bf16[256,512]{1,0:T(8,128)(2,1)S(1)}, u32[]{:S(2)}, u32[]{:S(2)}) collective-permute-start(bf16[256,512]{1,0:T(8,128)(2,1)} %refs_1_.1), channel_id=1, source_target_pairs={{0,8},{4,20},{8,0},{12,28},{16,24},{20,4},{24,16},{28,12},{1,9},{5... | collective-permute-start | bytes 786440 | tf_op jit(solution)/shard_map/ppermute | solution.py:32
  13.3 13.0 %collective-permute-start.2 = (bf16[256,512]{1,0:T(8,128)(2,1)S(1)}, bf16[256,512]{1,0:T(8,128)(2,1)S(1)}, u32[]{:S(2)}, u32[]{:S(2)}) collective-permute-start(bf16[256,512]{1,0:T(8,128)(2,1)S(1)} %collective-permute-done.refs_3_), channel_id=1, source_target_pairs={{0,8},{4,20},{8,0},{12,28},{16,24},{20,4},{24,16},{28,12},{1,9},{5... | collective-permute-start | bytes 786440 | tf_op jit(solution)/shard_map/ppermute | solution.py:32
  13.4 2.2 %copy-start = (bf16[1,1,8,16,128,128]{5,4,3,2,1,0:T(8,128)(2,1)S(1)}, bf16[1,1,8,16,128,128]{5,4,3,2,1,0:T(8,128)(2,1)}, u32[]{:S(2)}) copy-start(bf16[1,1,8,16,128,128]{5,4,3,2,1,0:T(8,128)(2,1)} %param.10) | copy-start | bytes 12582916
  15.6 3.4 %copy-start.2 = (bf16[256,512]{1,0:T(8,128)(2,1)S(1)}, bf16[256,512]{1,0:T(8,128)(2,1)}, u32[]{:S(2)}) copy-start(bf16[256,512]{1,0:T(8,128)(2,1)} %refs_1_.1) | copy-start | bytes 786436
  26.3 1.5 %collective-permute-start.5 = (bf16[256,512]{1,0:T(8,128)(2,1)S(1)}, bf16[256,512]{1,0:T(8,128)(2,1)S(1)}, u32[]{:S(2)}, u32[]{:S(2)}) collective-permute-start(bf16[256,512]{1,0:T(8,128)(2,1)S(1)} %collective-permute-done.1.refs_1_), channel_id=1, source_target_pairs={{0,4},{4,0},{8,12},{12,8},{16,20},{20,16},{24,28},{28,24},{1,5},{5... | collective-permute-start | bytes 786440 | tf_op jit(solution)/shard_map/ppermute | solution.py:26
  26.3 1.9 %collective-permute-start.6 = (bf16[256,512]{1,0:T(8,128)(2,1)S(1)}, bf16[256,512]{1,0:T(8,128)(2,1)S(1)}, u32[]{:S(2)}, u32[]{:S(2)}) collective-permute-start(bf16[256,512]{1,0:T(8,128)(2,1)S(1)} %collective-permute-done.2.refs_3_), channel_id=1, source_target_pairs={{0,4},{4,0},{8,12},{12,8},{16,20},{20,16},{24,28},{28,24},{1,5},{5... | collective-permute-start | bytes 786440 | tf_op jit(solution)/shard_map/ppermute | solution.py:26
  29.5 13.0 %copy-start.1 = (bf16[512,512]{1,0:T(8,128)(2,1)S(1)}, bf16[512,512]{1,0:T(8,128)(2,1)}, u32[]{:S(2)}) copy-start(bf16[512,512]{1,0:T(8,128)(2,1)} %refs_4_.1) | copy-start | bytes 1572868
  29.5 13.0 %copy-start.3 = (bf16[256,512]{1,0:T(8,128)(2,1)S(1)}, bf16[256,512]{1,0:T(8,128)(2,1)}, u32[]{:S(2)}) copy-start(bf16[256,512]{1,0:T(8,128)(2,1)} %refs_3_.1) | copy-start | bytes 786436
  29.5 6.4 %collective-permute-start.8 = (bf16[256,512]{1,0:T(8,128)(2,1)S(1)}, bf16[256,512]{1,0:T(8,128)(2,1)S(1)}, u32[]{:S(2)}, u32[]{:S(2)}) collective-permute-start(bf16[256,512]{1,0:T(8,128)(2,1)S(1)} %get-tuple-element.50), channel_id=1, source_target_pairs={{0,1},{1,0},{2,3},{3,2},{4,6},{5,7},{6,4},{7,5},{8,9},{9,8},{10,11... | collective-permute-start | bytes 786440 | tf_op jit(solution)/shard_map/ppermute | solution.py:42
  31.2 8.2 %collective-permute-start.7 = (bf16[256,512]{1,0:T(8,128)(2,1)S(1)}, bf16[256,512]{1,0:T(8,128)(2,1)S(1)}, u32[]{:S(2)}, u32[]{:S(2)}) collective-permute-start(bf16[256,512]{1,0:T(8,128)(2,1)S(1)} %get-tuple-element.48), channel_id=1, source_target_pairs={{0,1},{1,0},{2,3},{3,2},{4,6},{5,7},{6,4},{7,5},{8,9},{9,8},{10,11... | collective-permute-start | bytes 786440 | tf_op jit(solution)/shard_map/ppermute | solution.py:42
  36.0 6.4 %collective-permute-start.9 = (bf16[256,512]{1,0:T(8,128)(2,1)S(1)}, bf16[256,512]{1,0:T(8,128)(2,1)S(1)}, u32[]{:S(2)}, u32[]{:S(2)}) collective-permute-start(bf16[256,512]{1,0:T(8,128)(2,1)S(1)} %add_convert_fusion.2), channel_id=1, source_target_pairs={{0,2},{1,3},{2,0},{3,1},{4,5},{5,4},{6,7},{7,6},{8,10},{9,11},{10,... | collective-permute-start | bytes 786440 | tf_op jit(solution)/shard_map/ppermute | solution.py:42
  43.6 6.4 %collective-permute-start.10 = (bf16[256,512]{1,0:T(8,128)(2,1)S(1)}, bf16[256,512]{1,0:T(8,128)(2,1)S(1)}, u32[]{:S(2)}, u32[]{:S(2)}) collective-permute-start(bf16[256,512]{1,0:T(8,128)(2,1)S(1)} %get-tuple-element.70.refs_2_), channel_id=1, source_target_pairs={{0,2},{1,3},{2,0},{3,1},{4,5},{5,4},{6,7},{7,6},{8,10},{9,11},{10,... | collective-permute-start | bytes 786440 | tf_op jit(solution)/shard_map/ppermute | solution.py:42
  46.3 5.5 %collective-permute-start.12 = (bf16[256,512]{1,0:T(8,128)(2,1)S(1)}, bf16[256,512]{1,0:T(8,128)(2,1)S(1)}, u32[]{:S(2)}, u32[]{:S(2)}) collective-permute-start(bf16[256,512]{1,0:T(8,128)(2,1)S(1)} %get-tuple-element.62), channel_id=1, source_target_pairs={{0,4},{4,0},{8,12},{12,8},{16,20},{20,16},{24,28},{28,24},{1,5},{5... | collective-permute-start | bytes 786440 | tf_op jit(solution)/shard_map/ppermute | solution.py:26
  50.0 17.0 %collective-permute-start.11 = (bf16[512,512]{1,0:T(8,128)(2,1)S(1)}, bf16[512,512]{1,0:T(8,128)(2,1)S(1)}, u32[]{:S(2)}, u32[]{:S(2)}) collective-permute-start(bf16[512,512]{1,0:T(8,128)(2,1)S(1)} %pad_maximum_fusion), channel_id=1, source_target_pairs={{0,1},{1,0},{2,3},{3,2},{4,6},{5,7},{6,4},{7,5},{8,9},{9,8},{10,11... | collective-permute-start | bytes 1572872 | tf_op jit(solution)/shard_map/ppermute | solution.py:42
  51.8 9.9 %collective-permute-start.15 = (bf16[64,512]{1,0:T(8,128)(2,1)S(1)}, bf16[64,512]{1,0:T(8,128)(2,1)S(1)}, u32[]{:S(2)}, u32[]{:S(2)}) collective-permute-start(bf16[64,512]{1,0:T(8,128)(2,1)S(1)} %get-tuple-element.78), channel_id=1, source_target_pairs={{0,3},{1,2},{2,1},{3,0},{4,7},{5,6},{6,5},{7,4},{8,11},{9,10},{10,... | collective-permute-start | bytes 196616 | tf_op jit(solution)/shard_map/ppermute | solution.py:42
  53.4 8.4 %collective-permute-start.14 = (bf16[64,512]{1,0:T(8,128)(2,1)S(1)}, bf16[64,512]{1,0:T(8,128)(2,1)S(1)}, u32[]{:S(2)}, u32[]{:S(2)}) collective-permute-start(bf16[64,512]{1,0:T(8,128)(2,1)S(1)} %get-tuple-element.79), channel_id=1, source_target_pairs={{0,2},{1,3},{2,0},{3,1},{4,5},{5,4},{6,7},{7,6},{8,10},{9,11},{10,... | collective-permute-start | bytes 196616 | tf_op jit(solution)/shard_map/ppermute | solution.py:42
  53.7 8.0 %collective-permute-start.13 = (bf16[64,512]{1,0:T(8,128)(2,1)S(1)}, bf16[64,512]{1,0:T(8,128)(2,1)S(1)}, u32[]{:S(2)}, u32[]{:S(2)}) collective-permute-start(bf16[64,512]{1,0:T(8,128)(2,1)S(1)} %get-tuple-element.77), channel_id=1, source_target_pairs={{0,1},{1,0},{2,3},{3,2},{4,6},{5,7},{6,4},{7,5},{8,9},{9,8},{10,11... | collective-permute-start | bytes 196616 | tf_op jit(solution)/shard_map/ppermute | solution.py:42
  61.8 5.2 %collective-permute-start.16 = (bf16[64,512]{1,0:T(8,128)(2,1)S(1)}, bf16[64,512]{1,0:T(8,128)(2,1)S(1)}, u32[]{:S(2)}, u32[]{:S(2)}) collective-permute-start(bf16[64,512]{1,0:T(8,128)(2,1)S(1)} %add_convert_fusion.4), channel_id=1, source_target_pairs={{0,16},{4,12},{8,24},{12,4},{16,0},{20,28},{24,8},{28,20},{1,17},{... | collective-permute-start | bytes 196616 | tf_op jit(solution)/shard_map/ppermute | solution.py:32
  67.7 3.1 %collective-permute-start.17 = (bf16[512,512]{1,0:T(8,128)(2,1)S(1)}, bf16[512,512]{1,0:T(8,128)(2,1)S(1)}, u32[]{:S(2)}, u32[]{:S(2)}) collective-permute-start(bf16[512,512]{1,0:T(8,128)(2,1)S(1)} %backward.4), channel_id=1, source_target_pairs={{0,4},{4,0},{8,12},{12,8},{16,20},{20,16},{24,28},{28,24},{1,5},{5... | collective-permute-start | bytes 1572872 | tf_op jit(solution)/shard_map/ppermute | solution.py:26
  67.8 5.7 %collective-permute-start.21 = (bf16[64,512]{1,0:T(8,128)(2,1)S(1)}, bf16[64,512]{1,0:T(8,128)(2,1)S(1)}, u32[]{:S(2)}, u32[]{:S(2)}) collective-permute-start(bf16[64,512]{1,0:T(8,128)(2,1)S(1)} %add_convert_fusion.3), channel_id=1, source_target_pairs={{0,8},{4,20},{8,0},{12,28},{16,24},{20,4},{24,16},{28,12},{1,9},{5... | collective-permute-start | bytes 196616 | tf_op jit(solution)/shard_map/ppermute | solution.py:32
  71.0 14.9 %collective-permute-start.19 = (bf16[512,512]{1,0:T(8,128)(2,1)S(1)}, bf16[512,512]{1,0:T(8,128)(2,1)S(1)}, u32[]{:S(2)}, u32[]{:S(2)}) collective-permute-start(bf16[512,512]{1,0:T(8,128)(2,1)S(1)} %pad_maximum_fusion.1), channel_id=1, source_target_pairs={{0,8},{4,20},{8,0},{12,28},{16,24},{20,4},{24,16},{28,12},{1,9},{5... | collective-permute-start | bytes 1572872 | tf_op jit(solution)/shard_map/ppermute | solution.py:32
  72.9 11.0 %collective-permute-start.18 = (bf16[512,512]{1,0:T(8,128)(2,1)S(1)}, bf16[512,512]{1,0:T(8,128)(2,1)S(1)}, u32[]{:S(2)}, u32[]{:S(2)}) collective-permute-start(bf16[512,512]{1,0:T(8,128)(2,1)S(1)} %backward.7), channel_id=1, source_target_pairs={{0,4},{4,0},{8,12},{12,8},{16,20},{20,16},{24,28},{28,24},{1,5},{5... | collective-permute-start | bytes 1572872 | tf_op jit(solution)/shard_map/ppermute | solution.py:26
  73.5 6.4 %collective-permute-start.22 = (f32[64,512]{1,0:T(8,128)S(1)}, f32[64,512]{1,0:T(8,128)S(1)}, u32[]{:S(2)}, u32[]{:S(2)}) collective-permute-start(f32[64,512]{1,0:T(8,128)S(1)} %add_multiply_fusion.refs_0_), channel_id=1, source_target_pairs={{0,1},{1,0},{2,3},{3,2},{4,6},{5,7},{6,4},{7,5},{8,9},{9,8},{10,11... | collective-permute-start | bytes 393224 | tf_op jit(solution)/shard_map/ppermute | solution.py:42
  74.6 5.4 %collective-permute-start.23 = (f32[64,512]{1,0:T(8,128)S(1)}, f32[64,512]{1,0:T(8,128)S(1)}, u32[]{:S(2)}, u32[]{:S(2)}) collective-permute-start(f32[64,512]{1,0:T(8,128)S(1)} %add_multiply_fusion.refs_0_), channel_id=1, source_target_pairs={{0,2},{1,3},{2,0},{3,1},{4,5},{5,4},{6,7},{7,6},{8,10},{9,11},{10,... | collective-permute-start | bytes 393224 | tf_op jit(solution)/shard_map/ppermute | solution.py:42
  75.8 7.2 %collective-permute-start.24 = (f32[64,512]{1,0:T(8,128)S(1)}, f32[64,512]{1,0:T(8,128)S(1)}, u32[]{:S(2)}, u32[]{:S(2)}) collective-permute-start(f32[64,512]{1,0:T(8,128)S(1)} %add_multiply_fusion.refs_0_), channel_id=1, source_target_pairs={{0,3},{1,2},{2,1},{3,0},{4,7},{5,6},{6,5},{7,4},{8,11},{9,10},{10,... | collective-permute-start | bytes 393224 | tf_op jit(solution)/shard_map/ppermute | solution.py:42
  83.1 5.8 %collective-permute-start.25 = (f32[256,512]{1,0:T(8,128)S(1)}, f32[256,512]{1,0:T(8,128)S(1)}, u32[]{:S(2)}, u32[]{:S(2)}) collective-permute-start(f32[256,512]{1,0:T(8,128)S(1)} %pad_maximum_fusion.2), channel_id=1, source_target_pairs={{0,4},{4,0},{8,12},{12,8},{16,20},{20,16},{24,28},{28,24},{1,5},{5... | collective-permute-start | bytes 1572872 | tf_op jit(solution)/shard_map/ppermute | solution.py:26
  86.0 10.1 %collective-permute-start.20 = (bf16[256,512]{1,0:T(8,128)(2,1)S(1)}, bf16[256,512]{1,0:T(8,128)(2,1)S(1)}, u32[]{:S(2)}, u32[]{:S(2)}) collective-permute-start(bf16[256,512]{1,0:T(8,128)(2,1)S(1)} %get-tuple-element.74), channel_id=1, source_target_pairs={{0,16},{4,12},{8,24},{12,4},{16,0},{20,28},{24,8},{28,20},{1,17},{... | collective-permute-start | bytes 786440 | tf_op jit(solution)/shard_map/ppermute | solution.py:32

commit v8 on v7

--- a/solution.py
+++ b/solution.py
@@ -370,16 +370,18 @@
     parts = add_slots(owns, swap_cores(send))
 
     grads = [grad]
-    while sum(x.shape[0] for x in grads) < groups * rows_local:
-        slots = sum(x.shape[0] for x in grads) // rows_local
-        grads.append(swap_members(jnp.concatenate(grads) if slots > 1 else grad, slots))
-        if slots == 1:
-            part = parts[0]
-            for k in range(1, groups):
-                part = part + swap_members(parts[k].astype(jnp.bfloat16), k, turn=1).astype(jnp.float32)
-            part = part.astype(jnp.bfloat16)
-            near = swap_chips(part, 1)
-            part = part.astype(jnp.float32) + near.astype(jnp.float32)
+    for k in range(1, groups):
+        if k == top_bit(k):
+            straight = grads[0]
+        else:
+            straight = after(grads[k - top_bit(k)], grads[top_bit(k)])
+        grads.append(swap_members(straight, top_bit(k)))
+    part = parts[0]
+    for k in range(1, groups):
+        part = part + swap_members(parts[k].astype(jnp.bfloat16), k, turn=1).astype(jnp.float32)
+    part = part.astype(jnp.bfloat16)
+    near = swap_chips(part, 1)
+    part = part.astype(jnp.float32) + near.astype(jnp.float32)
     grads[-1] = after(grads[-1], near)
 
     half = chips // 2

time: 97.1 us -> 92.7 us (0.955)
  waiting for transfers between devices: 45.8 us -> 40.5 us
    ppermute x11 -> x12, waiting for transfers between devices: 23.7 us -> 17.5 us  [swap_members(): return lax.ppermute(x, ('dom', 'repl'), pairs)]
    ppermute x11 -> x12, starting transfers between devices: 14.4 us -> 15.9 us  [swap_members(): return lax.ppermute(x, ('dom', 'repl'), pairs)]
  transfers between devices with their start and end apart: 26 -> 27, of which waited for: 15 -> 16; matrix products, arithmetic and copies ran while one was open for 2% -> 2% of each run, Pallas kernels for 11% -> 10%
where the time goes in v8:
time: 92.7 us; the launch traced here: 92.5 us
  waiting for transfers between devices  40.5 us (44%)
  starting transfers between devices  32.5 us (35%)
  Pallas kernels  14.4 us (16%)
  local copies, waits for them, and re-layouts  2.93 us (3%)
  other arithmetic  1.31 us (1%)
    ppermute x7, waiting for transfers between devices, swap_chips(): lax.ppermute(x, 'dom', [(i, i ^ 2 * between(held, i % 2, bits)) for i in...  21.5 us
    ppermute x12, waiting for transfers between devices, swap_members(): return lax.ppermute(x, ('dom', 'repl'), pairs)  17.5 us
    ppermute x12, starting transfers between devices, swap_members(): return lax.ppermute(x, ('dom', 'repl'), pairs)  15.9 us
    ppermute x7, starting transfers between devices, swap_chips(): lax.ppermute(x, 'dom', [(i, i ^ 2 * between(held, i % 2, bits)) for i in...  15.8 us
    pallas_call x1, Pallas kernels, densify(): pl.pallas_call(functools.partial(densify_kernel, col_tiles=col_tiles), ou...  3.33 us
    pallas_call x4, Pallas kernels, backward(): pl.pallas_call(functools.partial(backward_kernel, side=side, count=count,...  2.81 us
    pallas_call x2, Pallas kernels, forward(): pl.pallas_call(functools.partial(forward_kernel, first=first, count=len(s...  2.49 us
    unnamed x8, local copies, waits for them, and re-layouts  2.2 us
  transfers between devices with their start and end apart: 27, of which 16 were waited for; matrix products, arithmetic and copies ran while one was open for 2% of the time, Pallas kernels for 10%

profile of v8, /device:TPU:0, one launch (start us, length us, event | category | flops | bytes accessed | tf_op | source)
XLA Modules:
  0.0 92.5 jit_solution(16789338668079022149)
XLA Ops:
  0.6 4.1 %collective-permute-start = (bf16[256,512]{1,0:T(8,128)(2,1)}, bf16[256,512]{1,0:T(8,128)(2,1)S(1)}, u32[]{:S(2)}, u32[]{:S(2)}) collective-permute-start(bf16[256,512]{1,0:T(8,128)(2,1)} %refs_1_.1), channel_id=1, source_target_pairs={{0,16},{4,12},{8,24},{12,4},{16,0},{20,28},{24,8},{28,20},{1,17},{... | collective-permute-start | bytes 786440 | tf_op jit(solution)/shard_map/ppermute | solution.py:32
  6.3 4.6 %collective-permute-done.refs_3_ = bf16[256,512]{1,0:T(8,128)(2,1)S(1)} collective-permute-done((bf16[256,512]{1,0:T(8,128)(2,1)}, bf16[256,512]{1,0:T(8,128)(2,1)S(1)}, u32[]{:S(2)}, u32[]{:S(2)}) %collective-permute-start) | collective-permute-done | bytes 262176 | tf_op jit(solution)/shard_map/ppermute | solution.py:32
  10.9 2.4 %collective-permute-start.1 = (bf16[256,512]{1,0:T(8,128)(2,1)}, bf16[256,512]{1,0:T(8,128)(2,1)S(1)}, u32[]{:S(2)}, u32[]{:S(2)}) collective-permute-start(bf16[256,512]{1,0:T(8,128)(2,1)} %refs_1_.1), channel_id=1, source_target_pairs={{0,8},{4,20},{8,0},{12,28},{16,24},{20,4},{24,16},{28,12},{1,9},{5... | collective-permute-start | bytes 786440 | tf_op jit(solution)/shard_map/ppermute | solution.py:32
  13.4 2.2 %copy-done = bf16[1,1,8,16,128,128]{5,4,3,2,1,0:T(8,128)(2,1)S(1)} copy-done((bf16[1,1,8,16,128,128]{5,4,3,2,1,0:T(8,128)(2,1)S(1)}, bf16[1,1,8,16,128,128]{5,4,3,2,1,0:T(8,128)(2,1)}, u32[]{:S(2)}) %copy-start) | copy-done | bytes 4194328
  15.6 3.3 %densify.1.refs_0_.a_ref = bf16[8,1024,256]{2,1,0:T(8,128)(2,1)S(1)} custom-call(s32[8,17]{1,0:T(8,128)S(1)} %pad_add_fusion.spots_ref, s32[2]{0:T(128)S(1)} %pad_add_fusion.1.place_ref, bf16[8,16,128,128]{3,2,1,0:T(8,128)(2,1)S(1)} %bitcast.26), custom_call_target="tpu_custom_call" | custom-call | flops 2097152 | bytes 16777216 | tf_op jit(solution)/shard_map/densify/pallas_call | solution.py:86
  19.0 1.2 %forward.2 = (f32[256,512]{1,0:T(8,128)S(1)}, f32[256,512]{1,0:T(8,128)S(1)}, f32[256,512]{1,0:T(8,128)S(1)}, f32[256,512]{1,0:T(8,128)S(1)}) custom-call(bf16[8,1024,256]{2,1,0:T(8,128)(2,1)S(1)} %densify.1.refs_0_.a_ref, bf16[256,512]{1,0:T(8,128)(2,1)S(1)} %copy-done.2, bf16[256,512]{1,0:T(8,128)(2,1)S(1)} %collective-permute-done.3.refs_2_, ...), custom_call_target="tpu_custom_call" | custom-call | flops 1073741824 | bytes 4194304 | tf_op jit(solution)/shard_map/forward/pallas_call | solution.py:139
  20.2 2.7 %collective-permute-done.1.refs_1_ = bf16[256,512]{1,0:T(8,128)(2,1)S(1)} collective-permute-done((bf16[256,512]{1,0:T(8,128)(2,1)}, bf16[256,512]{1,0:T(8,128)(2,1)S(1)}, u32[]{:S(2)}, u32[]{:S(2)}) %collective-permute-start.1) | collective-permute-done | bytes 262176 | tf_op jit(solution)/shard_map/ppermute | solution.py:32
  22.9 3.4 %collective-permute-done.2.refs_3_ = bf16[256,512]{1,0:T(8,128)(2,1)S(1)} collective-permute-done((bf16[256,512]{1,0:T(8,128)(2,1)S(1)}, bf16[256,512]{1,0:T(8,128)(2,1)S(1)}, u32[]{:S(2)}, u32[]{:S(2)}) %collective-permute-start.2) | collective-permute-done | bytes 262176 | tf_op jit(solution)/shard_map/ppermute | solution.py:32
  28.2 1.2 %forward.3 = (f32[256,512]{1,0:T(8,128)S(1)}, f32[256,512]{1,0:T(8,128)S(1)}, bf16[256,512]{1,0:T(8,128)(2,1)S(1)}, bf16[256,512]{1,0:T(8,128)(2,1)S(1)}) custom-call(bf16[8,1024,256]{2,1,0:T(8,128)(2,1)S(1)} %densify.1.refs_0_.a_ref, bf16[256,512]{1,0:T(8,128)(2,1)S(1)} %collective-permute-done.1.refs_1_, ...), custom_call_target="tpu_custom_call" | custom-call | flops 1073741824 | bytes 4194304 | tf_op jit(solution)/shard_map/forward/pallas_call | solution.py:139
  29.5 1.7 %collective-permute-start.8 = (bf16[256,512]{1,0:T(8,128)(2,1)S(1)}, bf16[256,512]{1,0:T(8,128)(2,1)S(1)}, u32[]{:S(2)}, u32[]{:S(2)}) collective-permute-start(bf16[256,512]{1,0:T(8,128)(2,1)S(1)} %get-tuple-element.51), channel_id=1, source_target_pairs={{0,1},{1,0},{2,3},{3,2},{4,6},{5,7},{6,4},{7,5},{8,9},{9,8},{10,11... | collective-permute-start | bytes 786440 | tf_op jit(solution)/shard_map/ppermute | solution.py:42
  31.6 4.3 %collective-permute-done.8 = bf16[256,512]{1,0:T(8,128)(2,1)S(1)} collective-permute-done((bf16[256,512]{1,0:T(8,128)(2,1)S(1)}, bf16[256,512]{1,0:T(8,128)(2,1)S(1)}, u32[]{:S(2)}, u32[]{:S(2)}) %collective-permute-start.8) | collective-permute-done | bytes 262176 | tf_op jit(solution)/shard_map/ppermute | solution.py:42
  36.0 1.8 %collective-permute-start.9 = (bf16[256,512]{1,0:T(8,128)(2,1)S(1)}, bf16[256,512]{1,0:T(8,128)(2,1)S(1)}, u32[]{:S(2)}, u32[]{:S(2)}) collective-permute-start(bf16[256,512]{1,0:T(8,128)(2,1)S(1)} %add_convert_fusion.2), channel_id=1, source_target_pairs={{0,2},{1,3},{2,0},{3,1},{4,5},{5,4},{6,7},{7,6},{8,10},{9,11},{10,... | collective-permute-start | bytes 786440 | tf_op jit(solution)/shard_map/ppermute | solution.py:42
  37.8 1.7 %collective-permute-done.7.refs_1_ = bf16[256,512]{1,0:T(8,128)(2,1)S(1)} collective-permute-done((bf16[256,512]{1,0:T(8,128)(2,1)S(1)}, bf16[256,512]{1,0:T(8,128)(2,1)S(1)}, u32[]{:S(2)}, u32[]{:S(2)}) %collective-permute-start.7) | collective-permute-done | bytes 262176 | tf_op jit(solution)/shard_map/ppermute | solution.py:42
  39.5 1.2 %transposed.1 = (bf16[2,256,1024]{2,1,0:T(8,128)(2,1)S(1)}, bf16[2,256,1024]{2,1,0:T(8,128)(2,1)S(1)}, bf16[2,256,1024]{2,1,0:T(8,128)(2,1)S(1)}, bf16[2,256,1024]{2,1,0:T(8,128)(2,1)S(1)}) custom-call(bf16[8,1024,256]{2,1,0:T(8,128)(2,1)S(1)} %densify.1.refs_0_.a_ref), custom_call_target="tpu_custom_call" | custom-call | bytes 8388608 | tf_op jit(solution)/shard_map/transposed/pallas_call | solution.py:111
  40.7 1.8 %collective-permute-done.9.refs_2_ = bf16[256,512]{1,0:T(8,128)(2,1)S(1)} collective-permute-done((bf16[256,512]{1,0:T(8,128)(2,1)S(1)}, bf16[256,512]{1,0:T(8,128)(2,1)S(1)}, u32[]{:S(2)}, u32[]{:S(2)}) %collective-permute-start.9) | collective-permute-done | bytes 262176 | tf_op jit(solution)/shard_map/ppermute | solution.py:42
  44.6 1.8 %collective-permute-start.10 = (bf16[256,512]{1,0:T(8,128)(2,1)S(1)}, bf16[256,512]{1,0:T(8,128)(2,1)S(1)}, u32[]{:S(2)}, u32[]{:S(2)}) collective-permute-start(bf16[256,512]{1,0:T(8,128)(2,1)S(1)} %get-tuple-element.72.refs_2_), channel_id=1, source_target_pairs={{0,2},{1,3},{2,0},{3,1},{4,5},{5,4},{6,7},{7,6},{8,10},{9,11},{10,... | collective-permute-start | bytes 786440 | tf_op jit(solution)/shard_map/ppermute | solution.py:42
  46.4 1.5 %collective-permute-start.11 = (bf16[256,512]{1,0:T(8,128)(2,1)S(1)}, bf16[256,512]{1,0:T(8,128)(2,1)S(1)}, u32[]{:S(2)}, u32[]{:S(2)}) collective-permute-start(bf16[256,512]{1,0:T(8,128)(2,1)S(1)} %get-tuple-element.72.refs_2_), channel_id=1, source_target_pairs={{0,1},{1,0},{2,3},{3,2},{4,6},{5,7},{6,4},{7,5},{8,9},{9,8},{10,11... | collective-permute-start | bytes 786440 | tf_op jit(solution)/shard_map/ppermute | solution.py:42
  50.0 1.5 %collective-permute-start.14 = (bf16[64,512]{1,0:T(8,128)(2,1)S(1)}, bf16[64,512]{1,0:T(8,128)(2,1)S(1)}, u32[]{:S(2)}, u32[]{:S(2)}) collective-permute-start(bf16[64,512]{1,0:T(8,128)(2,1)S(1)} %get-tuple-element.79), channel_id=1, source_target_pairs={{0,1},{1,0},{2,3},{3,2},{4,6},{5,7},{6,4},{7,5},{8,9},{9,8},{10,11... | collective-permute-start | bytes 196616 | tf_op jit(solution)/shard_map/ppermute | solution.py:42
  51.5 1.7 %collective-permute-done.10.refs_3_ = bf16[256,512]{1,0:T(8,128)(2,1)S(1)} collective-permute-done((bf16[256,512]{1,0:T(8,128)(2,1)S(1)}, bf16[256,512]{1,0:T(8,128)(2,1)S(1)}, u32[]{:S(2)}, u32[]{:S(2)}) %collective-permute-start.10) | collective-permute-done | bytes 262176 | tf_op jit(solution)/shard_map/ppermute | solution.py:42
  53.2 1.6 %collective-permute-done.11.refs_4_ = bf16[256,512]{1,0:T(8,128)(2,1)S(1)} collective-permute-done((bf16[256,512]{1,0:T(8,128)(2,1)S(1)}, bf16[256,512]{1,0:T(8,128)(2,1)S(1)}, u32[]{:S(2)}, u32[]{:S(2)}) %collective-permute-start.11) | collective-permute-done | bytes 262176 | tf_op jit(solution)/shard_map/ppermute | solution.py:42
  54.7 1.7 %collective-permute-start.12 = (bf16[256,512]{1,0:T(8,128)(2,1)S(1)}, bf16[256,512]{1,0:T(8,128)(2,1)S(1)}, u32[]{:S(2)}, u32[]{:S(2)}) collective-permute-start(bf16[256,512]{1,0:T(8,128)(2,1)S(1)} %collective-permute-done.10.refs_3_), channel_id=1, source_target_pairs={{0,1},{1,0},{2,3},{3,2},{4,6},{5,7},{6,4},{7,5},{8,9},{9,8},{10,11... | collective-permute-start | bytes 786440 | tf_op jit(solution)/shard_map/ppermute | solution.py:42
  56.7 3.0 %collective-permute-start.17 = (bf16[64,512]{1,0:T(8,128)(2,1)S(1)}, bf16[64,512]{1,0:T(8,128)(2,1)S(1)}, u32[]{:S(2)}, u32[]{:S(2)}) collective-permute-start(bf16[64,512]{1,0:T(8,128)(2,1)S(1)} %add_convert_fusion.4), channel_id=1, source_target_pairs={{0,16},{4,12},{8,24},{12,4},{16,0},{20,28},{24,8},{28,20},{1,17},{... | collective-permute-start | bytes 196616 | tf_op jit(solution)/shard_map/ppermute | solution.py:32
  59.7 2.3 %collective-permute-done.17 = bf16[64,512]{1,0:T(8,128)(2,1)S(1)} collective-permute-done((bf16[64,512]{1,0:T(8,128)(2,1)S(1)}, bf16[64,512]{1,0:T(8,128)(2,1)S(1)}, u32[]{:S(2)}, u32[]{:S(2)}) %collective-permute-start.17) | collective-permute-done | bytes 65568 | tf_op jit(solution)/shard_map/ppermute | solution.py:32
  62.8 2.9 %collective-permute-start.22 = (bf16[64,512]{1,0:T(8,128)(2,1)S(1)}, bf16[64,512]{1,0:T(8,128)(2,1)S(1)}, u32[]{:S(2)}, u32[]{:S(2)}) collective-permute-start(bf16[64,512]{1,0:T(8,128)(2,1)S(1)} %add_convert_fusion.3), channel_id=1, source_target_pairs={{0,8},{4,20},{8,0},{12,28},{16,24},{20,4},{24,16},{28,12},{1,9},{5... | collective-permute-start | bytes 196616 | tf_op jit(solution)/shard_map/ppermute | solution.py:32
  68.6 1.4 %collective-permute-start.23 = (f32[64,512]{1,0:T(8,128)S(1)}, f32[64,512]{1,0:T(8,128)S(1)}, u32[]{:S(2)}, u32[]{:S(2)}) collective-permute-start(f32[64,512]{1,0:T(8,128)S(1)} %add_multiply_fusion.refs_0_), channel_id=1, source_target_pairs={{0,1},{1,0},{2,3},{3,2},{4,6},{5,7},{6,4},{7,5},{8,9},{9,8},{10,11... | collective-permute-start | bytes 393224 | tf_op jit(solution)/shard_map/ppermute | solution.py:42
  70.0 1.5 %collective-permute-start.24 = (f32[64,512]{1,0:T(8,128)S(1)}, f32[64,512]{1,0:T(8,128)S(1)}, u32[]{:S(2)}, u32[]{:S(2)}) collective-permute-start(f32[64,512]{1,0:T(8,128)S(1)} %add_multiply_fusion.refs_0_), channel_id=1, source_target_pairs={{0,2},{1,3},{2,0},{3,1},{4,5},{5,4},{6,7},{7,6},{8,10},{9,11},{10,... | collective-permute-start | bytes 393224 | tf_op jit(solution)/shard_map/ppermute | solution.py:42
  72.1 2.8 %collective-permute-done.23.refs_1_ = f32[64,512]{1,0:T(8,128)S(1)} collective-permute-done((f32[64,512]{1,0:T(8,128)S(1)}, f32[64,512]{1,0:T(8,128)S(1)}, u32[]{:S(2)}, u32[]{:S(2)}) %collective-permute-start.23) | collective-permute-done | bytes 131104 | tf_op jit(solution)/shard_map/ppermute | solution.py:42
  74.9 3.4 %collective-permute-done.25.refs_3_ = f32[64,512]{1,0:T(8,128)S(1)} collective-permute-done((f32[64,512]{1,0:T(8,128)S(1)}, f32[64,512]{1,0:T(8,128)S(1)}, u32[]{:S(2)}, u32[]{:S(2)}) %collective-permute-start.25) | collective-permute-done | bytes 131104 | tf_op jit(solution)/shard_map/ppermute | solution.py:42
  79.2 2.3 %collective-permute-done.20.refs_3_ = bf16[512,512]{1,0:T(8,128)(2,1)S(1)} collective-permute-done((bf16[512,512]{1,0:T(8,128)(2,1)S(1)}, bf16[512,512]{1,0:T(8,128)(2,1)S(1)}, u32[]{:S(2)}, u32[]{:S(2)}) %collective-permute-start.20) | collective-permute-done | bytes 524320 | tf_op jit(solution)/shard_map/ppermute | solution.py:32
  81.6 2.2 %collective-permute-start.21 = (bf16[256,512]{1,0:T(8,128)(2,1)S(1)}, bf16[256,512]{1,0:T(8,128)(2,1)S(1)}, u32[]{:S(2)}, u32[]{:S(2)}) collective-permute-start(bf16[256,512]{1,0:T(8,128)(2,1)S(1)} %get-tuple-element.76), channel_id=1, source_target_pairs={{0,16},{4,12},{8,24},{12,4},{16,0},{20,28},{24,8},{28,20},{1,17},{... | collective-permute-start | bytes 786440 | tf_op jit(solution)/shard_map/ppermute | solution.py:32
  83.9 1.6 %place_slices.1 = f32[512,512]{1,0:T(8,128)} custom-call(s32[2]{0:T(128)S(1)} %pad_add_fusion.1.place_ref, f32[64,512]{1,0:T(8,128)S(1)} %add_multiply_fusion.refs_0_, f32[64,512]{1,0:T(8,128)S(1)} %collective-permute-done.23.refs_1_, f32[64,512]{1,0:T(8,128)S(1)} %collective-permute-done.24.refs_2_, f32[64,512]{1,0:T(8,128)S(1)} %collective-permute-done.25.refs_3_, ...), custom_call_target="tpu_custom_call" | custom-call | bytes 2097152 | tf_op jit(solution)/shard_map/place_slices/pallas_call | solution.py:235
  85.4 6.3 %collective-permute-done.21.refs_1_ = bf16[256,512]{1,0:T(8,128)(2,1)S(1)} collective-permute-done((bf16[256,512]{1,0:T(8,128)(2,1)S(1)}, bf16[256,512]{1,0:T(8,128)(2,1)S(1)}, u32[]{:S(2)}, u32[]{:S(2)}) %collective-permute-start.21) | collective-permute-done | bytes 262176 | tf_op jit(solution)/shard_map/ppermute | solution.py:32
  (55 shorter events, 14.7 us)
Async XLA Ops:
  0.6 10.2 %collective-permute-start = (bf16[256,512]{1,0:T(8,128)(2,1)}, bf16[256,512]{1,0:T(8,128)(2,1)S(1)}, u32[]{:S(2)}, u32[]{:S(2)}) collective-permute-start(bf16[256,512]{1,0:T(8,128)(2,1)} %refs_1_.1), channel_id=1, source_target_pairs={{0,16},{4,12},{8,24},{12,4},{16,0},{20,28},{24,8},{28,20},{1,17},{... | collective-permute-start | bytes 786440 | tf_op jit(solution)/shard_map/ppermute | solution.py:32
  4.7 14.2 %collective-permute-start.3 = (bf16[256,512]{1,0:T(8,128)(2,1)}, bf16[256,512]{1,0:T(8,128)(2,1)S(1)}, u32[]{:S(2)}, u32[]{:S(2)}) collective-permute-start(bf16[256,512]{1,0:T(8,128)(2,1)} %refs_1_.1), channel_id=1, source_target_pairs={{0,4},{4,0},{8,12},{12,8},{16,20},{20,16},{24,28},{28,24},{1,5},{5... | collective-permute-start | bytes 786440 | tf_op jit(solution)/shard_map/ppermute | solution.py:26
  10.9 8.1 %collective-permute-start.4 = (bf16[256,512]{1,0:T(8,128)(2,1)S(1)}, bf16[256,512]{1,0:T(8,128)(2,1)S(1)}, u32[]{:S(2)}, u32[]{:S(2)}) collective-permute-start(bf16[256,512]{1,0:T(8,128)(2,1)S(1)} %collective-permute-done.refs_3_), channel_id=1, source_target_pairs={{0,4},{4,0},{8,12},{12,8},{16,20},{20,16},{24,28},{28,24},{1,5},{5... | collective-permute-start | bytes 786440 | tf_op jit(solution)/shard_map/ppermute | solution.py:26
  10.9 12.1 %collective-permute-start.1 = (bf16[256,512]{1,0:T(8,128)(2,1)}, bf16[256,512]{1,0:T(8,128)(2,1)S(1)}, u32[]{:S(2)}, u32[]{:S(2)}) collective-permute-start(bf16[256,512]{1,0:T(8,128)(2,1)} %refs_1_.1), channel_id=1, source_target_pairs={{0,8},{4,20},{8,0},{12,28},{16,24},{20,4},{24,16},{28,12},{1,9},{5... | collective-permute-start | bytes 786440 | tf_op jit(solution)/shard_map/ppermute | solution.py:32
  13.3 13.0 %collective-permute-start.2 = (bf16[256,512]{1,0:T(8,128)(2,1)S(1)}, bf16[256,512]{1,0:T(8,128)(2,1)S(1)}, u32[]{:S(2)}, u32[]{:S(2)}) collective-permute-start(bf16[256,512]{1,0:T(8,128)(2,1)S(1)} %collective-permute-done.refs_3_), channel_id=1, source_target_pairs={{0,8},{4,20},{8,0},{12,28},{16,24},{20,4},{24,16},{28,12},{1,9},{5... | collective-permute-start | bytes 786440 | tf_op jit(solution)/shard_map/ppermute | solution.py:32
  13.4 2.2 %copy-start = (bf16[1,1,8,16,128,128]{5,4,3,2,1,0:T(8,128)(2,1)S(1)}, bf16[1,1,8,16,128,128]{5,4,3,2,1,0:T(8,128)(2,1)}, u32[]{:S(2)}) copy-start(bf16[1,1,8,16,128,128]{5,4,3,2,1,0:T(8,128)(2,1)} %param.10) | copy-start | bytes 12582916
  15.6 3.4 %copy-start.2 = (bf16[256,512]{1,0:T(8,128)(2,1)S(1)}, bf16[256,512]{1,0:T(8,128)(2,1)}, u32[]{:S(2)}) copy-start(bf16[256,512]{1,0:T(8,128)(2,1)} %refs_1_.1) | copy-start | bytes 786436
  26.3 1.5 %collective-permute-start.5 = (bf16[256,512]{1,0:T(8,128)(2,1)S(1)}, bf16[256,512]{1,0:T(8,128)(2,1)S(1)}, u32[]{:S(2)}, u32[]{:S(2)}) collective-permute-start(bf16[256,512]{1,0:T(8,128)(2,1)S(1)} %collective-permute-done.1.refs_1_), channel_id=1, source_target_pairs={{0,4},{4,0},{8,12},{12,8},{16,20},{20,16},{24,28},{28,24},{1,5},{5... | collective-permute-start | bytes 786440 | tf_op jit(solution)/shard_map/ppermute | solution.py:26
  26.3 1.9 %collective-permute-start.6 = (bf16[256,512]{1,0:T(8,128)(2,1)S(1)}, bf16[256,512]{1,0:T(8,128)(2,1)S(1)}, u32[]{:S(2)}, u32[]{:S(2)}) collective-permute-start(bf16[256,512]{1,0:T(8,128)(2,1)S(1)} %collective-permute-done.2.refs_3_), channel_id=1, source_target_pairs={{0,4},{4,0},{8,12},{12,8},{16,20},{20,16},{24,28},{28,24},{1,5},{5... | collective-permute-start | bytes 786440 | tf_op jit(solution)/shard_map/ppermute | solution.py:26
  29.5 13.0 %copy-start.1 = (bf16[512,512]{1,0:T(8,128)(2,1)S(1)}, bf16[512,512]{1,0:T(8,128)(2,1)}, u32[]{:S(2)}) copy-start(bf16[512,512]{1,0:T(8,128)(2,1)} %refs_4_.1) | copy-start | bytes 1572868
  29.5 13.0 %copy-start.3 = (bf16[256,512]{1,0:T(8,128)(2,1)S(1)}, bf16[256,512]{1,0:T(8,128)(2,1)}, u32[]{:S(2)}) copy-start(bf16[256,512]{1,0:T(8,128)(2,1)} %refs_3_.1) | copy-start | bytes 786436
  29.5 6.4 %collective-permute-start.8 = (bf16[256,512]{1,0:T(8,128)(2,1)S(1)}, bf16[256,512]{1,0:T(8,128)(2,1)S(1)}, u32[]{:S(2)}, u32[]{:S(2)}) collective-permute-start(bf16[256,512]{1,0:T(8,128)(2,1)S(1)} %get-tuple-element.51), channel_id=1, source_target_pairs={{0,1},{1,0},{2,3},{3,2},{4,6},{5,7},{6,4},{7,5},{8,9},{9,8},{10,11... | collective-permute-start | bytes 786440 | tf_op jit(solution)/shard_map/ppermute | solution.py:42
  31.2 8.2 %collective-permute-start.7 = (bf16[256,512]{1,0:T(8,128)(2,1)S(1)}, bf16[256,512]{1,0:T(8,128)(2,1)S(1)}, u32[]{:S(2)}, u32[]{:S(2)}) collective-permute-start(bf16[256,512]{1,0:T(8,128)(2,1)S(1)} %get-tuple-element.49), channel_id=1, source_target_pairs={{0,1},{1,0},{2,3},{3,2},{4,6},{5,7},{6,4},{7,5},{8,9},{9,8},{10,11... | collective-permute-start | bytes 786440 | tf_op jit(solution)/shard_map/ppermute | solution.py:42
  36.0 6.4 %collective-permute-start.9 = (bf16[256,512]{1,0:T(8,128)(2,1)S(1)}, bf16[256,512]{1,0:T(8,128)(2,1)S(1)}, u32[]{:S(2)}, u32[]{:S(2)}) collective-permute-start(bf16[256,512]{1,0:T(8,128)(2,1)S(1)} %add_convert_fusion.2), channel_id=1, source_target_pairs={{0,2},{1,3},{2,0},{3,1},{4,5},{5,4},{6,7},{7,6},{8,10},{9,11},{10,... | collective-permute-start | bytes 786440 | tf_op jit(solution)/shard_map/ppermute | solution.py:42
  44.6 3.3 %collective-permute-start.13 = (bf16[256,512]{1,0:T(8,128)(2,1)S(1)}, bf16[256,512]{1,0:T(8,128)(2,1)S(1)}, u32[]{:S(2)}, u32[]{:S(2)}) collective-permute-start(bf16[256,512]{1,0:T(8,128)(2,1)S(1)} %get-tuple-element.64), channel_id=1, source_target_pairs={{0,4},{4,0},{8,12},{12,8},{16,20},{20,16},{24,28},{28,24},{1,5},{5... | collective-permute-start | bytes 786440 | tf_op jit(solution)/shard_map/ppermute | solution.py:26
  44.6 8.6 %collective-permute-start.10 = (bf16[256,512]{1,0:T(8,128)(2,1)S(1)}, bf16[256,512]{1,0:T(8,128)(2,1)S(1)}, u32[]{:S(2)}, u32[]{:S(2)}) collective-permute-start(bf16[256,512]{1,0:T(8,128)(2,1)S(1)} %get-tuple-element.72.refs_2_), channel_id=1, source_target_pairs={{0,2},{1,3},{2,0},{3,1},{4,5},{5,4},{6,7},{7,6},{8,10},{9,11},{10,... | collective-permute-start | bytes 786440 | tf_op jit(solution)/shard_map/ppermute | solution.py:42
  46.4 8.3 %collective-permute-start.11 = (bf16[256,512]{1,0:T(8,128)(2,1)S(1)}, bf16[256,512]{1,0:T(8,128)(2,1)S(1)}, u32[]{:S(2)}, u32[]{:S(2)}) collective-permute-start(bf16[256,512]{1,0:T(8,128)(2,1)S(1)} %get-tuple-element.72.refs_2_), channel_id=1, source_target_pairs={{0,1},{1,0},{2,3},{3,2},{4,6},{5,7},{6,4},{7,5},{8,9},{9,8},{10,11... | collective-permute-start | bytes 786440 | tf_op jit(solution)/shard_map/ppermute | solution.py:42
  47.9 8.7 %collective-permute-start.16 = (bf16[64,512]{1,0:T(8,128)(2,1)S(1)}, bf16[64,512]{1,0:T(8,128)(2,1)S(1)}, u32[]{:S(2)}, u32[]{:S(2)}) collective-permute-start(bf16[64,512]{1,0:T(8,128)(2,1)S(1)} %get-tuple-element.80), channel_id=1, source_target_pairs={{0,3},{1,2},{2,1},{3,0},{4,7},{5,6},{6,5},{7,4},{8,11},{9,10},{10,... | collective-permute-start | bytes 196616 | tf_op jit(solution)/shard_map/ppermute | solution.py:42
  48.9 7.8 %collective-permute-start.15 = (bf16[64,512]{1,0:T(8,128)(2,1)S(1)}, bf16[64,512]{1,0:T(8,128)(2,1)S(1)}, u32[]{:S(2)}, u32[]{:S(2)}) collective-permute-start(bf16[64,512]{1,0:T(8,128)(2,1)S(1)} %get-tuple-element.81), channel_id=1, source_target_pairs={{0,2},{1,3},{2,0},{3,1},{4,5},{5,4},{6,7},{7,6},{8,10},{9,11},{10,... | collective-permute-start | bytes 196616 | tf_op jit(solution)/shard_map/ppermute | solution.py:42
  50.0 6.7 %collective-permute-start.14 = (bf16[64,512]{1,0:T(8,128)(2,1)S(1)}, bf16[64,512]{1,0:T(8,128)(2,1)S(1)}, u32[]{:S(2)}, u32[]{:S(2)}) collective-permute-start(bf16[64,512]{1,0:T(8,128)(2,1)S(1)} %get-tuple-element.79), channel_id=1, source_target_pairs={{0,1},{1,0},{2,3},{3,2},{4,6},{5,7},{6,4},{7,5},{8,9},{9,8},{10,11... | collective-permute-start | bytes 196616 | tf_op jit(solution)/shard_map/ppermute | solution.py:42
  54.7 7.2 %collective-permute-start.12 = (bf16[256,512]{1,0:T(8,128)(2,1)S(1)}, bf16[256,512]{1,0:T(8,128)(2,1)S(1)}, u32[]{:S(2)}, u32[]{:S(2)}) collective-permute-start(bf16[256,512]{1,0:T(8,128)(2,1)S(1)} %collective-permute-done.10.refs_3_), channel_id=1, source_target_pairs={{0,1},{1,0},{2,3},{3,2},{4,6},{5,7},{6,4},{7,5},{8,9},{9,8},{10,11... | collective-permute-start | bytes 786440 | tf_op jit(solution)/shard_map/ppermute | solution.py:42
  56.7 5.2 %collective-permute-start.17 = (bf16[64,512]{1,0:T(8,128)(2,1)S(1)}, bf16[64,512]{1,0:T(8,128)(2,1)S(1)}, u32[]{:S(2)}, u32[]{:S(2)}) collective-permute-start(bf16[64,512]{1,0:T(8,128)(2,1)S(1)} %add_convert_fusion.4), channel_id=1, source_target_pairs={{0,16},{4,12},{8,24},{12,4},{16,0},{20,28},{24,8},{28,20},{1,17},{... | collective-permute-start | bytes 196616 | tf_op jit(solution)/shard_map/ppermute | solution.py:32
  62.7 3.7 %collective-permute-start.18 = (bf16[512,512]{1,0:T(8,128)(2,1)S(1)}, bf16[512,512]{1,0:T(8,128)(2,1)S(1)}, u32[]{:S(2)}, u32[]{:S(2)}) collective-permute-start(bf16[512,512]{1,0:T(8,128)(2,1)S(1)} %backward.4), channel_id=1, source_target_pairs={{0,4},{4,0},{8,12},{12,8},{16,20},{20,16},{24,28},{28,24},{1,5},{5... | collective-permute-start | bytes 1572872 | tf_op jit(solution)/shard_map/ppermute | solution.py:26
  62.8 5.7 %collective-permute-start.22 = (bf16[64,512]{1,0:T(8,128)(2,1)S(1)}, bf16[64,512]{1,0:T(8,128)(2,1)S(1)}, u32[]{:S(2)}, u32[]{:S(2)}) collective-permute-start(bf16[64,512]{1,0:T(8,128)(2,1)S(1)} %add_convert_fusion.3), channel_id=1, source_target_pairs={{0,8},{4,20},{8,0},{12,28},{16,24},{20,4},{24,16},{28,12},{1,9},{5... | collective-permute-start | bytes 196616 | tf_op jit(solution)/shard_map/ppermute | solution.py:32
  66.6 14.9 %collective-permute-start.20 = (bf16[512,512]{1,0:T(8,128)(2,1)S(1)}, bf16[512,512]{1,0:T(8,128)(2,1)S(1)}, u32[]{:S(2)}, u32[]{:S(2)}) collective-permute-start(bf16[512,512]{1,0:T(8,128)(2,1)S(1)} %pad_maximum_fusion), channel_id=1, source_target_pairs={{0,8},{4,20},{8,0},{12,28},{16,24},{20,4},{24,16},{28,12},{1,9},{5... | collective-permute-start | bytes 1572872 | tf_op jit(solution)/shard_map/ppermute | solution.py:32
  68.5 10.7 %collective-permute-start.19 = (bf16[512,512]{1,0:T(8,128)(2,1)S(1)}, bf16[512,512]{1,0:T(8,128)(2,1)S(1)}, u32[]{:S(2)}, u32[]{:S(2)}) collective-permute-start(bf16[512,512]{1,0:T(8,128)(2,1)S(1)} %backward.7), channel_id=1, source_target_pairs={{0,4},{4,0},{8,12},{12,8},{16,20},{20,16},{24,28},{28,24},{1,5},{5... | collective-permute-start | bytes 1572872 | tf_op jit(solution)/shard_map/ppermute | solution.py:26
  68.6 6.3 %collective-permute-start.23 = (f32[64,512]{1,0:T(8,128)S(1)}, f32[64,512]{1,0:T(8,128)S(1)}, u32[]{:S(2)}, u32[]{:S(2)}) collective-permute-start(f32[64,512]{1,0:T(8,128)S(1)} %add_multiply_fusion.refs_0_), channel_id=1, source_target_pairs={{0,1},{1,0},{2,3},{3,2},{4,6},{5,7},{6,4},{7,5},{8,9},{9,8},{10,11... | collective-permute-start | bytes 393224 | tf_op jit(solution)/shard_map/ppermute | solution.py:42
  70.0 5.0 %collective-permute-start.24 = (f32[64,512]{1,0:T(8,128)S(1)}, f32[64,512]{1,0:T(8,128)S(1)}, u32[]{:S(2)}, u32[]{:S(2)}) collective-permute-start(f32[64,512]{1,0:T(8,128)S(1)} %add_multiply_fusion.refs_0_), channel_id=1, source_target_pairs={{0,2},{1,3},{2,0},{3,1},{4,5},{5,4},{6,7},{7,6},{8,10},{9,11},{10,... | collective-permute-start | bytes 393224 | tf_op jit(solution)/shard_map/ppermute | solution.py:42
  71.5 6.9 %collective-permute-start.25 = (f32[64,512]{1,0:T(8,128)S(1)}, f32[64,512]{1,0:T(8,128)S(1)}, u32[]{:S(2)}, u32[]{:S(2)}) collective-permute-start(f32[64,512]{1,0:T(8,128)S(1)} %add_multiply_fusion.refs_0_), channel_id=1, source_target_pairs={{0,3},{1,2},{2,1},{3,0},{4,7},{5,6},{6,5},{7,4},{8,11},{9,10},{10,... | collective-permute-start | bytes 393224 | tf_op jit(solution)/shard_map/ppermute | solution.py:42
  78.4 5.5 %collective-permute-start.26 = (f32[256,512]{1,0:T(8,128)S(1)}, f32[256,512]{1,0:T(8,128)S(1)}, u32[]{:S(2)}, u32[]{:S(2)}) collective-permute-start(f32[256,512]{1,0:T(8,128)S(1)} %pad_maximum_fusion.1), channel_id=1, source_target_pairs={{0,4},{4,0},{8,12},{12,8},{16,20},{20,16},{24,28},{28,24},{1,5},{5... | collective-permute-start | bytes 1572872 | tf_op jit(solution)/shard_map/ppermute | solution.py:26
  81.6 10.1 %collective-permute-start.21 = (bf16[256,512]{1,0:T(8,128)(2,1)S(1)}, bf16[256,512]{1,0:T(8,128)(2,1)S(1)}, u32[]{:S(2)}, u32[]{:S(2)}) collective-permute-start(bf16[256,512]{1,0:T(8,128)(2,1)S(1)} %get-tuple-element.76), channel_id=1, source_target_pairs={{0,16},{4,12},{8,24},{12,4},{16,0},{20,28},{24,8},{28,20},{1,17},{... | collective-permute-start | bytes 786440 | tf_op jit(solution)/shard_map/ppermute | solution.py:32

commit v9 on v8

--- a/solution.py
+++ b/solution.py
@@ -119,7 +119,7 @@
     )(dense)
 
 
-def forward_kernel(*refs, first, count, slots, has_prev):
+def forward_kernel(*refs, first, base, count, slots, has_prev):
     dense_ref, sources = refs[0], refs[1:1 + count]
     rest = refs[1 + count:]
     prev, outs = (rest[:slots], rest[slots:]) if has_prev else (None, rest)
@@ -127,19 +127,19 @@
     for k, out_ref in reversed(list(enumerate(outs))):
         total = prev[k][...] if has_prev else None
         for j, source in enumerate(sources):
-            part = bf16_dot(dense_ref[first + j, k * rows:(k + 1) * rows, :], source[...])
+            part = bf16_dot(dense_ref[first + j, (base + k) * rows:(base + k + 1) * rows, :], source[...])
             total = part if total is None else total + part
         out_ref[...] = total.astype(out_ref.dtype)
 
 
-def forward(dense, first, sources, prev, dtypes):
+def forward(dense, first, sources, base, prev, dtypes):
     slots = len(dtypes)
-    _, rows, depth = dense.shape
-    width = sources[0].shape[1]
+    depth, width = sources[0].shape
+    rows = slots * depth
     return pl.pallas_call(
         functools.partial(
-            forward_kernel, first=first, count=len(sources), slots=slots, has_prev=prev is not None),
-        out_shape=[like((rows // slots, width), dtype) for dtype in dtypes],
+            forward_kernel, first=first, base=base, count=len(sources), slots=slots, has_prev=prev is not None),
+        out_shape=[like((depth, width), dtype) for dtype in dtypes],
         in_specs=[WHOLE] * (1 + len(sources) + (slots if prev is not None else 0)),
         out_specs=[WHOLE] * slots,
         compiler_params=params(8),
@@ -357,10 +357,12 @@
         for k in range(first, stop):
             own = held[k] if totals is None else after(held[k], held[-1], *totals)
             sources += [own, swap_cores(own)]
-        dtypes = [jnp.float32] * groups
-        if stop == chips:
-            dtypes = [jnp.float32 if k < groups // 2 else jnp.bfloat16 for k in range(groups)]
-        totals = forward(dense, 2 * first, sources, totals, dtypes)
+        if stop < chips:
+            totals = forward(dense, 2 * first, sources, 0, None, [jnp.float32] * groups)
+    upper = groups // 2
+    high = forward(dense, 2 * first, sources, upper, totals[upper:], [jnp.bfloat16] * upper)
+    low = forward(after(dense, *high), 2 * first, sources, 0, totals[:upper], [jnp.float32] * upper)
+    totals = low + high
 
     pieces = collect(totals, swap_members)
     dense_t = transposed(after(dense, *totals, pieces[1]))
@@ -380,9 +382,12 @@
     for k in range(1, groups):
         part = part + swap_members(parts[k].astype(jnp.bfloat16), k, turn=1).astype(jnp.float32)
     part = part.astype(jnp.bfloat16)
-    near = swap_chips(part, 1)
-    part = part.astype(jnp.float32) + near.astype(jnp.float32)
-    grads[-1] = after(grads[-1], near)
+    terms = [part] + [swap_chips(part, k) for k in range(1, chips)]
+    grads[-1] = after(grads[-1], *terms[1:])
+    terms = [term.astype(jnp.float32) for term in terms]
+    while len(terms) > 1:
+        terms = [terms[i] + terms[i + 1] for i in range(0, len(terms), 2)]
+    part = terms[0] * scale
 
     half = chips // 2
     other = backward(dense_t[half:], grads, 1)
@@ -399,12 +404,6 @@
         totals, arrived = totals[:half], [swap_chips(send, half)]
     (feature_grad,) = settle(totals, arrived, [jnp.bfloat16])
 
-    bit = 2
-    while bit < chips:
-        part = part.astype(jnp.bfloat16)
-        part = part.astype(jnp.float32) + swap_chips(part, bit).astype(jnp.float32)
-        bit *= 2
-    part = part * scale
     parts = [part] + [swap_members(part, k, turn=1) for k in range(1, groups)]
     weight_grad = place_slices(parts, swap_cores(jnp.concatenate(parts)), place)
     return (activated, feature_grad, weight_grad)

time: 92.7 us -> 96 us (1.036)
  waiting for transfers between devices: 40.5 us -> 46.7 us
  starting transfers between devices: 32.5 us -> 30.3 us
    ppermute x7 -> x8, waiting for transfers between devices: 21.5 us -> 27.6 us  [swap_chips(): lax.ppermute(x, 'dom', [(i, i ^ 2 * between(held, i % 2, bits)) for i in...]
    ppermute x7 -> x8, starting transfers between devices: 15.8 us -> 11.9 us  [swap_chips(): lax.ppermute(x, 'dom', [(i, i ^ 2 * between(held, i % 2, bits)) for i in...]
    ppermute x8, starting transfers between devices: 0.8 us -> 2.49 us  [swap_cores(): lax.ppermute(x, 'dom', [(i, i ^ 1) for i in range(lax.axis_size('dom'))])]
    ppermute x8, waiting for transfers between devices: 1.41 us -> 2.6 us  [swap_cores(): lax.ppermute(x, 'dom', [(i, i ^ 1) for i in range(lax.axis_size('dom'))])]
    pallas_call x1, Pallas kernels: 3.33 us -> 2.29 us  [densify(): pl.pallas_call(functools.partial(densify_kernel, col_tiles=col_tiles), ou...]
    ppermute x12, waiting for transfers between devices: 17.5 us -> 16.5 us  [swap_members(): return lax.ppermute(x, ('dom', 'repl'), pairs)]
    pallas_call x2 -> x3, Pallas kernels: 2.49 us -> 2.66 us  [forward(): pl.pallas_call(functools.partial(forward_kernel, first=first, base=base,...]
  transfers between devices with their start and end apart: 27 -> 28, of which waited for: 16 -> 19; matrix products, arithmetic and copies ran while one was open for 2% -> 2% of each run, Pallas kernels for 10% -> 10%
where the time goes in v9:
time: 96 us; the launch traced here: 95.8 us
  waiting for transfers between devices  46.7 us (49%)
  starting transfers between devices  30.3 us (32%)
  Pallas kernels  13.6 us (14%)
  local copies, waits for them, and re-layouts  2.93 us (3%)
  other arithmetic  1.31 us (1%)
    ppermute x8, waiting for transfers between devices, swap_chips(): lax.ppermute(x, 'dom', [(i, i ^ 2 * between(held, i % 2, bits)) for i in...  27.6 us
    ppermute x12, waiting for transfers between devices, swap_members(): return lax.ppermute(x, ('dom', 'repl'), pairs)  16.5 us
    ppermute x12, starting transfers between devices, swap_members(): return lax.ppermute(x, ('dom', 'repl'), pairs)  15.9 us
    ppermute x8, starting transfers between devices, swap_chips(): lax.ppermute(x, 'dom', [(i, i ^ 2 * between(held, i % 2, bits)) for i in...  11.9 us
    pallas_call x4, Pallas kernels, backward(): pl.pallas_call(functools.partial(backward_kernel, side=side, count=count,...  2.82 us
    pallas_call x3, Pallas kernels, forward(): pl.pallas_call(functools.partial(forward_kernel, first=first, base=base,...  2.66 us
    ppermute x8, waiting for transfers between devices, swap_cores(): lax.ppermute(x, 'dom', [(i, i ^ 1) for i in range(lax.axis_size('dom'))])  2.6 us
    ppermute x8, starting transfers between devices, swap_cores(): lax.ppermute(x, 'dom', [(i, i ^ 1) for i in range(lax.axis_size('dom'))])  2.49 us
  transfers between devices with their start and end apart: 28, of which 19 were waited for; matrix products, arithmetic and copies ran while one was open for 2% of the time, Pallas kernels for 10%

profile of v9, /device:TPU:0, one launch (start us, length us, event | category | flops | bytes accessed | tf_op | source)
XLA Modules:
  0.0 95.8 jit_solution(15733173829618327390)
XLA Ops:
  0.6 4.1 %collective-permute-start = (bf16[256,512]{1,0:T(8,128)(2,1)}, bf16[256,512]{1,0:T(8,128)(2,1)S(1)}, u32[]{:S(2)}, u32[]{:S(2)}) collective-permute-start(bf16[256,512]{1,0:T(8,128)(2,1)} %refs_1_.1), channel_id=1, source_target_pairs={{0,16},{4,12},{8,24},{12,4},{16,0},{20,28},{24,8},{28,20},{1,17},{... | collective-permute-start | bytes 786440 | tf_op jit(solution)/shard_map/ppermute | solution.py:32
  6.3 4.6 %collective-permute-done.refs_3_ = bf16[256,512]{1,0:T(8,128)(2,1)S(1)} collective-permute-done((bf16[256,512]{1,0:T(8,128)(2,1)}, bf16[256,512]{1,0:T(8,128)(2,1)S(1)}, u32[]{:S(2)}, u32[]{:S(2)}) %collective-permute-start) | collective-permute-done | bytes 262176 | tf_op jit(solution)/shard_map/ppermute | solution.py:32
  10.9 2.4 %collective-permute-start.1 = (bf16[256,512]{1,0:T(8,128)(2,1)}, bf16[256,512]{1,0:T(8,128)(2,1)S(1)}, u32[]{:S(2)}, u32[]{:S(2)}) collective-permute-start(bf16[256,512]{1,0:T(8,128)(2,1)} %refs_1_.1), channel_id=1, source_target_pairs={{0,8},{4,20},{8,0},{12,28},{16,24},{20,4},{24,16},{28,12},{1,9},{5... | collective-permute-start | bytes 786440 | tf_op jit(solution)/shard_map/ppermute | solution.py:32
  13.4 2.2 %copy-done = bf16[1,1,8,16,128,128]{5,4,3,2,1,0:T(8,128)(2,1)S(1)} copy-done((bf16[1,1,8,16,128,128]{5,4,3,2,1,0:T(8,128)(2,1)S(1)}, bf16[1,1,8,16,128,128]{5,4,3,2,1,0:T(8,128)(2,1)}, u32[]{:S(2)}) %copy-start) | copy-done | bytes 4194328
  15.6 2.3 %densify.1.refs_0_.a_ref = bf16[8,1024,256]{2,1,0:T(8,128)(2,1)S(1)} custom-call(s32[8,17]{1,0:T(8,128)S(1)} %pad_add_fusion.spots_ref, s32[2]{0:T(128)S(1)} %pad_add_fusion.1.place_ref, bf16[8,16,128,128]{3,2,1,0:T(8,128)(2,1)S(1)} %bitcast.26), custom_call_target="tpu_custom_call" | custom-call | flops 2097152 | bytes 16777216 | tf_op jit(solution)/shard_map/densify/pallas_call | solution.py:86
  17.9 1.2 %forward.3 = (f32[256,512]{1,0:T(8,128)S(1)}, f32[256,512]{1,0:T(8,128)S(1)}, f32[256,512]{1,0:T(8,128)S(1)}, f32[256,512]{1,0:T(8,128)S(1)}) custom-call(bf16[8,1024,256]{2,1,0:T(8,128)(2,1)S(1)} %densify.1.refs_0_.a_ref, bf16[256,512]{1,0:T(8,128)(2,1)S(1)} %copy-done.2, bf16[256,512]{1,0:T(8,128)(2,1)S(1)} %collective-permute-done.3.refs_2_, ...), custom_call_target="tpu_custom_call" | custom-call | flops 1073741824 | bytes 4194304 | tf_op jit(solution)/shard_map/forward/pallas_call | solution.py:139
  19.2 3.7 %collective-permute-done.1.refs_1_ = bf16[256,512]{1,0:T(8,128)(2,1)S(1)} collective-permute-done((bf16[256,512]{1,0:T(8,128)(2,1)}, bf16[256,512]{1,0:T(8,128)(2,1)S(1)}, u32[]{:S(2)}, u32[]{:S(2)}) %collective-permute-start.1) | collective-permute-done | bytes 262176 | tf_op jit(solution)/shard_map/ppermute | solution.py:32
  22.9 3.4 %collective-permute-done.2.refs_3_ = bf16[256,512]{1,0:T(8,128)(2,1)S(1)} collective-permute-done((bf16[256,512]{1,0:T(8,128)(2,1)S(1)}, bf16[256,512]{1,0:T(8,128)(2,1)S(1)}, u32[]{:S(2)}, u32[]{:S(2)}) %collective-permute-start.2) | collective-permute-done | bytes 262176 | tf_op jit(solution)/shard_map/ppermute | solution.py:32
  28.9 1.7 %collective-permute-start.8 = (bf16[256,512]{1,0:T(8,128)(2,1)S(1)}, bf16[256,512]{1,0:T(8,128)(2,1)S(1)}, u32[]{:S(2)}, u32[]{:S(2)}) collective-permute-start(bf16[256,512]{1,0:T(8,128)(2,1)S(1)} %get-tuple-element.50), channel_id=1, source_target_pairs={{0,1},{1,0},{2,3},{3,2},{4,6},{5,7},{6,4},{7,5},{8,9},{9,8},{10,11... | collective-permute-start | bytes 786440 | tf_op jit(solution)/shard_map/ppermute | solution.py:42
  31.7 3.6 %collective-permute-done.8 = bf16[256,512]{1,0:T(8,128)(2,1)S(1)} collective-permute-done((bf16[256,512]{1,0:T(8,128)(2,1)S(1)}, bf16[256,512]{1,0:T(8,128)(2,1)S(1)}, u32[]{:S(2)}, u32[]{:S(2)}) %collective-permute-start.8) | collective-permute-done | bytes 262176 | tf_op jit(solution)/shard_map/ppermute | solution.py:42
  35.4 1.8 %collective-permute-start.9 = (bf16[256,512]{1,0:T(8,128)(2,1)S(1)}, bf16[256,512]{1,0:T(8,128)(2,1)S(1)}, u32[]{:S(2)}, u32[]{:S(2)}) collective-permute-start(bf16[256,512]{1,0:T(8,128)(2,1)S(1)} %add_convert_fusion.2), channel_id=1, source_target_pairs={{0,2},{1,3},{2,0},{3,1},{4,5},{5,4},{6,7},{7,6},{8,10},{9,11},{10,... | collective-permute-start | bytes 786440 | tf_op jit(solution)/shard_map/ppermute | solution.py:42
  37.2 1.7 %collective-permute-done.7.refs_1_ = bf16[256,512]{1,0:T(8,128)(2,1)S(1)} collective-permute-done((bf16[256,512]{1,0:T(8,128)(2,1)S(1)}, bf16[256,512]{1,0:T(8,128)(2,1)S(1)}, u32[]{:S(2)}, u32[]{:S(2)}) %collective-permute-start.7) | collective-permute-done | bytes 262176 | tf_op jit(solution)/shard_map/ppermute | solution.py:42
  38.9 1.2 %transposed.1 = (bf16[2,256,1024]{2,1,0:T(8,128)(2,1)S(1)}, bf16[2,256,1024]{2,1,0:T(8,128)(2,1)S(1)}, bf16[2,256,1024]{2,1,0:T(8,128)(2,1)S(1)}, bf16[2,256,1024]{2,1,0:T(8,128)(2,1)S(1)}) custom-call(bf16[8,1024,256]{2,1,0:T(8,128)(2,1)S(1)} %densify.1.refs_0_.a_ref), custom_call_target="tpu_custom_call" | custom-call | bytes 8388608 | tf_op jit(solution)/shard_map/transposed/pallas_call | solution.py:111
  40.1 1.8 %collective-permute-done.9.refs_2_ = bf16[256,512]{1,0:T(8,128)(2,1)S(1)} collective-permute-done((bf16[256,512]{1,0:T(8,128)(2,1)S(1)}, bf16[256,512]{1,0:T(8,128)(2,1)S(1)}, u32[]{:S(2)}, u32[]{:S(2)}) %collective-permute-start.9) | collective-permute-done | bytes 262176 | tf_op jit(solution)/shard_map/ppermute | solution.py:42
  41.9 1.2 %middle.1 = (bf16[256,512]{1,0:T(8,128)(2,1)}, bf16[256,512]{1,0:T(8,128)(2,1)S(1)}, bf16[256,512]{1,0:T(8,128)(2,1)S(1)}, bf16[256,512]{1,0:T(8,128)(2,1)S(1)}) custom-call(f32[256,512]{1,0:T(8,128)S(1)} %get-tuple-element.52.refs_0_, bf16[256,512]{1,0:T(8,128)(2,1)S(1)} %collective-permute-done.7.refs_1_, ...), custom_call_target="tpu_custom_call" | custom-call | flops 268435456 | bytes 1310720 | tf_op jit(solution)/shard_map/middle/pallas_call | solution.py:174
  44.1 1.8 %collective-permute-start.10 = (bf16[256,512]{1,0:T(8,128)(2,1)S(1)}, bf16[256,512]{1,0:T(8,128)(2,1)S(1)}, u32[]{:S(2)}, u32[]{:S(2)}) collective-permute-start(bf16[256,512]{1,0:T(8,128)(2,1)S(1)} %get-tuple-element.74.refs_2_), channel_id=1, source_target_pairs={{0,2},{1,3},{2,0},{3,1},{4,5},{5,4},{6,7},{7,6},{8,10},{9,11},{10,... | collective-permute-start | bytes 786440 | tf_op jit(solution)/shard_map/ppermute | solution.py:42
  45.9 1.5 %collective-permute-start.11 = (bf16[256,512]{1,0:T(8,128)(2,1)S(1)}, bf16[256,512]{1,0:T(8,128)(2,1)S(1)}, u32[]{:S(2)}, u32[]{:S(2)}) collective-permute-start(bf16[256,512]{1,0:T(8,128)(2,1)S(1)} %get-tuple-element.74.refs_2_), channel_id=1, source_target_pairs={{0,1},{1,0},{2,3},{3,2},{4,6},{5,7},{6,4},{7,5},{8,9},{9,8},{10,11... | collective-permute-start | bytes 786440 | tf_op jit(solution)/shard_map/ppermute | solution.py:42
  49.5 1.5 %collective-permute-start.14 = (bf16[64,512]{1,0:T(8,128)(2,1)S(1)}, bf16[64,512]{1,0:T(8,128)(2,1)S(1)}, u32[]{:S(2)}, u32[]{:S(2)}) collective-permute-start(bf16[64,512]{1,0:T(8,128)(2,1)S(1)} %get-tuple-element.81), channel_id=1, source_target_pairs={{0,1},{1,0},{2,3},{3,2},{4,6},{5,7},{6,4},{7,5},{8,9},{9,8},{10,11... | collective-permute-start | bytes 196616 | tf_op jit(solution)/shard_map/ppermute | solution.py:42
  51.0 1.7 %collective-permute-done.10.refs_3_ = bf16[256,512]{1,0:T(8,128)(2,1)S(1)} collective-permute-done((bf16[256,512]{1,0:T(8,128)(2,1)S(1)}, bf16[256,512]{1,0:T(8,128)(2,1)S(1)}, u32[]{:S(2)}, u32[]{:S(2)}) %collective-permute-start.10) | collective-permute-done | bytes 262176 | tf_op jit(solution)/shard_map/ppermute | solution.py:42
  52.6 1.6 %collective-permute-done.11.refs_4_ = bf16[256,512]{1,0:T(8,128)(2,1)S(1)} collective-permute-done((bf16[256,512]{1,0:T(8,128)(2,1)S(1)}, bf16[256,512]{1,0:T(8,128)(2,1)S(1)}, u32[]{:S(2)}, u32[]{:S(2)}) %collective-permute-start.11) | collective-permute-done | bytes 262176 | tf_op jit(solution)/shard_map/ppermute | solution.py:42
  54.2 1.7 %collective-permute-start.12 = (bf16[256,512]{1,0:T(8,128)(2,1)S(1)}, bf16[256,512]{1,0:T(8,128)(2,1)S(1)}, u32[]{:S(2)}, u32[]{:S(2)}) collective-permute-start(bf16[256,512]{1,0:T(8,128)(2,1)S(1)} %collective-permute-done.10.refs_3_), channel_id=1, source_target_pairs={{0,1},{1,0},{2,3},{3,2},{4,6},{5,7},{6,4},{7,5},{8,9},{9,8},{10,11... | collective-permute-start | bytes 786440 | tf_op jit(solution)/shard_map/ppermute | solution.py:42
  56.2 3.0 %collective-permute-start.17 = (bf16[64,512]{1,0:T(8,128)(2,1)S(1)}, bf16[64,512]{1,0:T(8,128)(2,1)S(1)}, u32[]{:S(2)}, u32[]{:S(2)}) collective-permute-start(bf16[64,512]{1,0:T(8,128)(2,1)S(1)} %add_convert_fusion.3), channel_id=1, source_target_pairs={{0,16},{4,12},{8,24},{12,4},{16,0},{20,28},{24,8},{28,20},{1,17},{... | collective-permute-start | bytes 196616 | tf_op jit(solution)/shard_map/ppermute | solution.py:32
  59.2 2.2 %collective-permute-start.18 = (bf16[64,512]{1,0:T(8,128)(2,1)S(1)}, bf16[64,512]{1,0:T(8,128)(2,1)S(1)}, u32[]{:S(2)}, u32[]{:S(2)}) collective-permute-start(bf16[64,512]{1,0:T(8,128)(2,1)S(1)} %add_convert_fusion.3), channel_id=1, source_target_pairs={{0,8},{4,20},{8,0},{12,28},{16,24},{20,4},{24,16},{28,12},{1,9},{5... | collective-permute-start | bytes 196616 | tf_op jit(solution)/shard_map/ppermute | solution.py:32
  61.5 2.8 %collective-permute-done.18 = bf16[64,512]{1,0:T(8,128)(2,1)S(1)} collective-permute-done((bf16[64,512]{1,0:T(8,128)(2,1)S(1)}, bf16[64,512]{1,0:T(8,128)(2,1)S(1)}, u32[]{:S(2)}, u32[]{:S(2)}) %collective-permute-start.18) | collective-permute-done | bytes 65568 | tf_op jit(solution)/shard_map/ppermute | solution.py:32
  64.2 3.2 %collective-permute-done.19 = bf16[64,512]{1,0:T(8,128)(2,1)S(1)} collective-permute-done((bf16[64,512]{1,0:T(8,128)(2,1)S(1)}, bf16[64,512]{1,0:T(8,128)(2,1)S(1)}, u32[]{:S(2)}, u32[]{:S(2)}) %collective-permute-start.19) | collective-permute-done | bytes 65568 | tf_op jit(solution)/shard_map/ppermute | solution.py:32
  71.1 1.8 %collective-permute-start.21 = (bf16[512,512]{1,0:T(8,128)(2,1)S(1)}, bf16[512,512]{1,0:T(8,128)(2,1)S(1)}, u32[]{:S(2)}, u32[]{:S(2)}) collective-permute-start(bf16[512,512]{1,0:T(8,128)(2,1)S(1)} %backward.7), channel_id=1, source_target_pairs={{0,4},{4,0},{8,12},{12,8},{16,20},{20,16},{24,28},{28,24},{1,5},{5... | collective-permute-start | bytes 1572872 | tf_op jit(solution)/shard_map/ppermute | solution.py:26
  73.4 2.2 %collective-permute-start.25 = (f32[64,512]{1,0:T(8,128)S(1)}, f32[64,512]{1,0:T(8,128)S(1)}, u32[]{:S(2)}, u32[]{:S(2)}) collective-permute-start(f32[64,512]{1,0:T(8,128)S(1)} %add_multiply_fusion.refs_0_), channel_id=1, source_target_pairs={{0,2},{1,3},{2,0},{3,1},{4,5},{5,4},{6,7},{7,6},{8,10},{9,11},{10,... | collective-permute-start | bytes 393224 | tf_op jit(solution)/shard_map/ppermute | solution.py:42
  76.5 2.9 %collective-permute-done.24.refs_1_ = f32[64,512]{1,0:T(8,128)S(1)} collective-permute-done((f32[64,512]{1,0:T(8,128)S(1)}, f32[64,512]{1,0:T(8,128)S(1)}, u32[]{:S(2)}, u32[]{:S(2)}) %collective-permute-start.24) | collective-permute-done | bytes 131104 | tf_op jit(solution)/shard_map/ppermute | solution.py:42
  79.4 3.0 %collective-permute-done.26.refs_3_ = f32[64,512]{1,0:T(8,128)S(1)} collective-permute-done((f32[64,512]{1,0:T(8,128)S(1)}, f32[64,512]{1,0:T(8,128)S(1)}, u32[]{:S(2)}, u32[]{:S(2)}) %collective-permute-start.26) | collective-permute-done | bytes 131104 | tf_op jit(solution)/shard_map/ppermute | solution.py:42
  83.3 2.0 %collective-permute-done.22.refs_3_ = bf16[512,512]{1,0:T(8,128)(2,1)S(1)} collective-permute-done((bf16[512,512]{1,0:T(8,128)(2,1)S(1)}, bf16[512,512]{1,0:T(8,128)(2,1)S(1)}, u32[]{:S(2)}, u32[]{:S(2)}) %collective-permute-start.22) | collective-permute-done | bytes 524320 | tf_op jit(solution)/shard_map/ppermute | solution.py:32
  85.5 1.6 %place_slices.1 = f32[512,512]{1,0:T(8,128)} custom-call(s32[2]{0:T(128)S(1)} %pad_add_fusion.1.place_ref, f32[64,512]{1,0:T(8,128)S(1)} %add_multiply_fusion.refs_0_, f32[64,512]{1,0:T(8,128)S(1)} %collective-permute-done.24.refs_1_, f32[64,512]{1,0:T(8,128)S(1)} %collective-permute-done.25.refs_2_, f32[64,512]{1,0:T(8,128)S(1)} %collective-permute-done.26.refs_3_, ...), custom_call_target="tpu_custom_call" | custom-call | bytes 2097152 | tf_op jit(solution)/shard_map/place_slices/pallas_call | solution.py:235
  87.1 7.9 %collective-permute-done.23.refs_1_ = bf16[256,512]{1,0:T(8,128)(2,1)S(1)} collective-permute-done((bf16[256,512]{1,0:T(8,128)(2,1)S(1)}, bf16[256,512]{1,0:T(8,128)(2,1)S(1)}, u32[]{:S(2)}, u32[]{:S(2)}) %collective-permute-start.23) | collective-permute-done | bytes 262176 | tf_op jit(solution)/shard_map/ppermute | solution.py:32
  (57 shorter events, 15.8 us)
Async XLA Ops:
  0.6 10.2 %collective-permute-start = (bf16[256,512]{1,0:T(8,128)(2,1)}, bf16[256,512]{1,0:T(8,128)(2,1)S(1)}, u32[]{:S(2)}, u32[]{:S(2)}) collective-permute-start(bf16[256,512]{1,0:T(8,128)(2,1)} %refs_1_.1), channel_id=1, source_target_pairs={{0,16},{4,12},{8,24},{12,4},{16,0},{20,28},{24,8},{28,20},{1,17},{... | collective-permute-start | bytes 786440 | tf_op jit(solution)/shard_map/ppermute | solution.py:32
  4.7 13.2 %collective-permute-start.3 = (bf16[256,512]{1,0:T(8,128)(2,1)}, bf16[256,512]{1,0:T(8,128)(2,1)S(1)}, u32[]{:S(2)}, u32[]{:S(2)}) collective-permute-start(bf16[256,512]{1,0:T(8,128)(2,1)} %refs_1_.1), channel_id=1, source_target_pairs={{0,4},{4,0},{8,12},{12,8},{16,20},{20,16},{24,28},{28,24},{1,5},{5... | collective-permute-start | bytes 786440 | tf_op jit(solution)/shard_map/ppermute | solution.py:26
  10.9 7.1 %collective-permute-start.4 = (bf16[256,512]{1,0:T(8,128)(2,1)S(1)}, bf16[256,512]{1,0:T(8,128)(2,1)S(1)}, u32[]{:S(2)}, u32[]{:S(2)}) collective-permute-start(bf16[256,512]{1,0:T(8,128)(2,1)S(1)} %collective-permute-done.refs_3_), channel_id=1, source_target_pairs={{0,4},{4,0},{8,12},{12,8},{16,20},{20,16},{24,28},{28,24},{1,5},{5... | collective-permute-start | bytes 786440 | tf_op jit(solution)/shard_map/ppermute | solution.py:26
  10.9 12.1 %collective-permute-start.1 = (bf16[256,512]{1,0:T(8,128)(2,1)}, bf16[256,512]{1,0:T(8,128)(2,1)S(1)}, u32[]{:S(2)}, u32[]{:S(2)}) collective-permute-start(bf16[256,512]{1,0:T(8,128)(2,1)} %refs_1_.1), channel_id=1, source_target_pairs={{0,8},{4,20},{8,0},{12,28},{16,24},{20,4},{24,16},{28,12},{1,9},{5... | collective-permute-start | bytes 786440 | tf_op jit(solution)/shard_map/ppermute | solution.py:32
  13.3 13.0 %collective-permute-start.2 = (bf16[256,512]{1,0:T(8,128)(2,1)S(1)}, bf16[256,512]{1,0:T(8,128)(2,1)S(1)}, u32[]{:S(2)}, u32[]{:S(2)}) collective-permute-start(bf16[256,512]{1,0:T(8,128)(2,1)S(1)} %collective-permute-done.refs_3_), channel_id=1, source_target_pairs={{0,8},{4,20},{8,0},{12,28},{16,24},{20,4},{24,16},{28,12},{1,9},{5... | collective-permute-start | bytes 786440 | tf_op jit(solution)/shard_map/ppermute | solution.py:32
  13.4 2.2 %copy-start = (bf16[1,1,8,16,128,128]{5,4,3,2,1,0:T(8,128)(2,1)S(1)}, bf16[1,1,8,16,128,128]{5,4,3,2,1,0:T(8,128)(2,1)}, u32[]{:S(2)}) copy-start(bf16[1,1,8,16,128,128]{5,4,3,2,1,0:T(8,128)(2,1)} %param.10) | copy-start | bytes 12582916
  15.6 2.3 %copy-start.2 = (bf16[256,512]{1,0:T(8,128)(2,1)S(1)}, bf16[256,512]{1,0:T(8,128)(2,1)}, u32[]{:S(2)}) copy-start(bf16[256,512]{1,0:T(8,128)(2,1)} %refs_1_.1) | copy-start | bytes 786436
  26.3 1.5 %collective-permute-start.5 = (bf16[256,512]{1,0:T(8,128)(2,1)S(1)}, bf16[256,512]{1,0:T(8,128)(2,1)S(1)}, u32[]{:S(2)}, u32[]{:S(2)}) collective-permute-start(bf16[256,512]{1,0:T(8,128)(2,1)S(1)} %collective-permute-done.1.refs_1_), channel_id=1, source_target_pairs={{0,4},{4,0},{8,12},{12,8},{16,20},{20,16},{24,28},{28,24},{1,5},{5... | collective-permute-start | bytes 786440 | tf_op jit(solution)/shard_map/ppermute | solution.py:26
  26.3 1.9 %collective-permute-start.6 = (bf16[256,512]{1,0:T(8,128)(2,1)S(1)}, bf16[256,512]{1,0:T(8,128)(2,1)S(1)}, u32[]{:S(2)}, u32[]{:S(2)}) collective-permute-start(bf16[256,512]{1,0:T(8,128)(2,1)S(1)} %collective-permute-done.2.refs_3_), channel_id=1, source_target_pairs={{0,4},{4,0},{8,12},{12,8},{16,20},{20,16},{24,28},{28,24},{1,5},{5... | collective-permute-start | bytes 786440 | tf_op jit(solution)/shard_map/ppermute | solution.py:26
  28.9 6.4 %collective-permute-start.8 = (bf16[256,512]{1,0:T(8,128)(2,1)S(1)}, bf16[256,512]{1,0:T(8,128)(2,1)S(1)}, u32[]{:S(2)}, u32[]{:S(2)}) collective-permute-start(bf16[256,512]{1,0:T(8,128)(2,1)S(1)} %get-tuple-element.50), channel_id=1, source_target_pairs={{0,1},{1,0},{2,3},{3,2},{4,6},{5,7},{6,4},{7,5},{8,9},{9,8},{10,11... | collective-permute-start | bytes 786440 | tf_op jit(solution)/shard_map/ppermute | solution.py:42
  30.7 8.2 %collective-permute-start.7 = (bf16[256,512]{1,0:T(8,128)(2,1)S(1)}, bf16[256,512]{1,0:T(8,128)(2,1)S(1)}, u32[]{:S(2)}, u32[]{:S(2)}) collective-permute-start(bf16[256,512]{1,0:T(8,128)(2,1)S(1)} %get-tuple-element.49), channel_id=1, source_target_pairs={{0,1},{1,0},{2,3},{3,2},{4,6},{5,7},{6,4},{7,5},{8,9},{9,8},{10,11... | collective-permute-start | bytes 786440 | tf_op jit(solution)/shard_map/ppermute | solution.py:42
  31.7 10.2 %copy-start.1 = (bf16[512,512]{1,0:T(8,128)(2,1)S(1)}, bf16[512,512]{1,0:T(8,128)(2,1)}, u32[]{:S(2)}) copy-start(bf16[512,512]{1,0:T(8,128)(2,1)} %refs_4_.1) | copy-start | bytes 1572868
  31.7 10.1 %copy-start.3 = (bf16[256,512]{1,0:T(8,128)(2,1)S(1)}, bf16[256,512]{1,0:T(8,128)(2,1)}, u32[]{:S(2)}) copy-start(bf16[256,512]{1,0:T(8,128)(2,1)} %refs_3_.1) | copy-start | bytes 786436
  35.4 6.4 %collective-permute-start.9 = (bf16[256,512]{1,0:T(8,128)(2,1)S(1)}, bf16[256,512]{1,0:T(8,128)(2,1)S(1)}, u32[]{:S(2)}, u32[]{:S(2)}) collective-permute-start(bf16[256,512]{1,0:T(8,128)(2,1)S(1)} %add_convert_fusion.2), channel_id=1, source_target_pairs={{0,2},{1,3},{2,0},{3,1},{4,5},{5,4},{6,7},{7,6},{8,10},{9,11},{10,... | collective-permute-start | bytes 786440 | tf_op jit(solution)/shard_map/ppermute | solution.py:42
  44.0 3.3 %collective-permute-start.13 = (bf16[256,512]{1,0:T(8,128)(2,1)S(1)}, bf16[256,512]{1,0:T(8,128)(2,1)S(1)}, u32[]{:S(2)}, u32[]{:S(2)}) collective-permute-start(bf16[256,512]{1,0:T(8,128)(2,1)S(1)} %get-tuple-element.66), channel_id=1, source_target_pairs={{0,4},{4,0},{8,12},{12,8},{16,20},{20,16},{24,28},{28,24},{1,5},{5... | collective-permute-start | bytes 786440 | tf_op jit(solution)/shard_map/ppermute | solution.py:26
  44.1 8.5 %collective-permute-start.10 = (bf16[256,512]{1,0:T(8,128)(2,1)S(1)}, bf16[256,512]{1,0:T(8,128)(2,1)S(1)}, u32[]{:S(2)}, u32[]{:S(2)}) collective-permute-start(bf16[256,512]{1,0:T(8,128)(2,1)S(1)} %get-tuple-element.74.refs_2_), channel_id=1, source_target_pairs={{0,2},{1,3},{2,0},{3,1},{4,5},{5,4},{6,7},{7,6},{8,10},{9,11},{10,... | collective-permute-start | bytes 786440 | tf_op jit(solution)/shard_map/ppermute | solution.py:42
  45.9 8.3 %collective-permute-start.11 = (bf16[256,512]{1,0:T(8,128)(2,1)S(1)}, bf16[256,512]{1,0:T(8,128)(2,1)S(1)}, u32[]{:S(2)}, u32[]{:S(2)}) collective-permute-start(bf16[256,512]{1,0:T(8,128)(2,1)S(1)} %get-tuple-element.74.refs_2_), channel_id=1, source_target_pairs={{0,1},{1,0},{2,3},{3,2},{4,6},{5,7},{6,4},{7,5},{8,9},{9,8},{10,11... | collective-permute-start | bytes 786440 | tf_op jit(solution)/shard_map/ppermute | solution.py:42
  47.4 8.7 %collective-permute-start.16 = (bf16[64,512]{1,0:T(8,128)(2,1)S(1)}, bf16[64,512]{1,0:T(8,128)(2,1)S(1)}, u32[]{:S(2)}, u32[]{:S(2)}) collective-permute-start(bf16[64,512]{1,0:T(8,128)(2,1)S(1)} %get-tuple-element.82), channel_id=1, source_target_pairs={{0,3},{1,2},{2,1},{3,0},{4,7},{5,6},{6,5},{7,4},{8,11},{9,10},{10,... | collective-permute-start | bytes 196616 | tf_op jit(solution)/shard_map/ppermute | solution.py:42
  48.4 7.8 %collective-permute-start.15 = (bf16[64,512]{1,0:T(8,128)(2,1)S(1)}, bf16[64,512]{1,0:T(8,128)(2,1)S(1)}, u32[]{:S(2)}, u32[]{:S(2)}) collective-permute-start(bf16[64,512]{1,0:T(8,128)(2,1)S(1)} %get-tuple-element.83), channel_id=1, source_target_pairs={{0,2},{1,3},{2,0},{3,1},{4,5},{5,4},{6,7},{7,6},{8,10},{9,11},{10,... | collective-permute-start | bytes 196616 | tf_op jit(solution)/shard_map/ppermute | solution.py:42
  49.5 6.7 %collective-permute-start.14 = (bf16[64,512]{1,0:T(8,128)(2,1)S(1)}, bf16[64,512]{1,0:T(8,128)(2,1)S(1)}, u32[]{:S(2)}, u32[]{:S(2)}) collective-permute-start(bf16[64,512]{1,0:T(8,128)(2,1)S(1)} %get-tuple-element.81), channel_id=1, source_target_pairs={{0,1},{1,0},{2,3},{3,2},{4,6},{5,7},{6,4},{7,5},{8,9},{9,8},{10,11... | collective-permute-start | bytes 196616 | tf_op jit(solution)/shard_map/ppermute | solution.py:42
  54.2 13.2 %collective-permute-start.12 = (bf16[256,512]{1,0:T(8,128)(2,1)S(1)}, bf16[256,512]{1,0:T(8,128)(2,1)S(1)}, u32[]{:S(2)}, u32[]{:S(2)}) collective-permute-start(bf16[256,512]{1,0:T(8,128)(2,1)S(1)} %collective-permute-done.10.refs_3_), channel_id=1, source_target_pairs={{0,1},{1,0},{2,3},{3,2},{4,6},{5,7},{6,4},{7,5},{8,9},{9,8},{10,11... | collective-permute-start | bytes 786440 | tf_op jit(solution)/shard_map/ppermute | solution.py:42
  56.2 5.3 %collective-permute-start.17 = (bf16[64,512]{1,0:T(8,128)(2,1)S(1)}, bf16[64,512]{1,0:T(8,128)(2,1)S(1)}, u32[]{:S(2)}, u32[]{:S(2)}) collective-permute-start(bf16[64,512]{1,0:T(8,128)(2,1)S(1)} %add_convert_fusion.3), channel_id=1, source_target_pairs={{0,16},{4,12},{8,24},{12,4},{16,0},{20,28},{24,8},{28,20},{1,17},{... | collective-permute-start | bytes 196616 | tf_op jit(solution)/shard_map/ppermute | solution.py:32
  59.2 5.0 %collective-permute-start.18 = (bf16[64,512]{1,0:T(8,128)(2,1)S(1)}, bf16[64,512]{1,0:T(8,128)(2,1)S(1)}, u32[]{:S(2)}, u32[]{:S(2)}) collective-permute-start(bf16[64,512]{1,0:T(8,128)(2,1)S(1)} %add_convert_fusion.3), channel_id=1, source_target_pairs={{0,8},{4,20},{8,0},{12,28},{16,24},{20,4},{24,16},{28,12},{1,9},{5... | collective-permute-start | bytes 196616 | tf_op jit(solution)/shard_map/ppermute | solution.py:32
  61.4 6.1 %collective-permute-start.19 = (bf16[64,512]{1,0:T(8,128)(2,1)S(1)}, bf16[64,512]{1,0:T(8,128)(2,1)S(1)}, u32[]{:S(2)}, u32[]{:S(2)}) collective-permute-start(bf16[64,512]{1,0:T(8,128)(2,1)S(1)} %add_convert_fusion.3), channel_id=1, source_target_pairs={{0,24},{4,28},{8,16},{12,20},{16,8},{20,12},{24,0},{28,4},{1,25},{... | collective-permute-start | bytes 196616 | tf_op jit(solution)/shard_map/ppermute | solution.py:32
  68.2 2.0 %collective-permute-start.20 = (bf16[512,512]{1,0:T(8,128)(2,1)S(1)}, bf16[512,512]{1,0:T(8,128)(2,1)S(1)}, u32[]{:S(2)}, u32[]{:S(2)}) collective-permute-start(bf16[512,512]{1,0:T(8,128)(2,1)S(1)} %backward.4), channel_id=1, source_target_pairs={{0,4},{4,0},{8,12},{12,8},{16,20},{20,16},{24,28},{28,24},{1,5},{5... | collective-permute-start | bytes 1572872 | tf_op jit(solution)/shard_map/ppermute | solution.py:26
  70.3 14.9 %collective-permute-start.22 = (bf16[512,512]{1,0:T(8,128)(2,1)S(1)}, bf16[512,512]{1,0:T(8,128)(2,1)S(1)}, u32[]{:S(2)}, u32[]{:S(2)}) collective-permute-start(bf16[512,512]{1,0:T(8,128)(2,1)S(1)} %pad_maximum_fusion), channel_id=1, source_target_pairs={{0,8},{4,20},{8,0},{12,28},{16,24},{20,4},{24,16},{28,12},{1,9},{5... | collective-permute-start | bytes 1572872 | tf_op jit(solution)/shard_map/ppermute | solution.py:32
  71.1 12.1 %collective-permute-start.21 = (bf16[512,512]{1,0:T(8,128)(2,1)S(1)}, bf16[512,512]{1,0:T(8,128)(2,1)S(1)}, u32[]{:S(2)}, u32[]{:S(2)}) collective-permute-start(bf16[512,512]{1,0:T(8,128)(2,1)S(1)} %backward.7), channel_id=1, source_target_pairs={{0,4},{4,0},{8,12},{12,8},{16,20},{20,16},{24,28},{28,24},{1,5},{5... | collective-permute-start | bytes 1572872 | tf_op jit(solution)/shard_map/ppermute | solution.py:26
  72.9 6.4 %collective-permute-start.24 = (f32[64,512]{1,0:T(8,128)S(1)}, f32[64,512]{1,0:T(8,128)S(1)}, u32[]{:S(2)}, u32[]{:S(2)}) collective-permute-start(f32[64,512]{1,0:T(8,128)S(1)} %add_multiply_fusion.refs_0_), channel_id=1, source_target_pairs={{0,1},{1,0},{2,3},{3,2},{4,6},{5,7},{6,4},{7,5},{8,9},{9,8},{10,11... | collective-permute-start | bytes 393224 | tf_op jit(solution)/shard_map/ppermute | solution.py:42
  73.4 6.0 %collective-permute-start.25 = (f32[64,512]{1,0:T(8,128)S(1)}, f32[64,512]{1,0:T(8,128)S(1)}, u32[]{:S(2)}, u32[]{:S(2)}) collective-permute-start(f32[64,512]{1,0:T(8,128)S(1)} %add_multiply_fusion.refs_0_), channel_id=1, source_target_pairs={{0,2},{1,3},{2,0},{3,1},{4,5},{5,4},{6,7},{7,6},{8,10},{9,11},{10,... | collective-permute-start | bytes 393224 | tf_op jit(solution)/shard_map/ppermute | solution.py:42
  75.5 6.9 %collective-permute-start.26 = (f32[64,512]{1,0:T(8,128)S(1)}, f32[64,512]{1,0:T(8,128)S(1)}, u32[]{:S(2)}, u32[]{:S(2)}) collective-permute-start(f32[64,512]{1,0:T(8,128)S(1)} %add_multiply_fusion.refs_0_), channel_id=1, source_target_pairs={{0,3},{1,2},{2,1},{3,0},{4,7},{5,6},{6,5},{7,4},{8,11},{9,10},{10,... | collective-permute-start | bytes 393224 | tf_op jit(solution)/shard_map/ppermute | solution.py:42
  82.5 3.0 %collective-permute-start.27 = (f32[256,512]{1,0:T(8,128)S(1)}, f32[256,512]{1,0:T(8,128)S(1)}, u32[]{:S(2)}, u32[]{:S(2)}) collective-permute-start(f32[256,512]{1,0:T(8,128)S(1)} %pad_maximum_fusion.1), channel_id=1, source_target_pairs={{0,4},{4,0},{8,12},{12,8},{16,20},{20,16},{24,28},{28,24},{1,5},{5... | collective-permute-start | bytes 1572872 | tf_op jit(solution)/shard_map/ppermute | solution.py:26
  85.4 9.6 %collective-permute-start.23 = (bf16[256,512]{1,0:T(8,128)(2,1)S(1)}, bf16[256,512]{1,0:T(8,128)(2,1)S(1)}, u32[]{:S(2)}, u32[]{:S(2)}) collective-permute-start(bf16[256,512]{1,0:T(8,128)(2,1)S(1)} %get-tuple-element.78), channel_id=1, source_target_pairs={{0,16},{4,12},{8,24},{12,4},{16,0},{20,28},{24,8},{28,20},{1,17},{... | collective-permute-start | bytes 786440 | tf_op jit(solution)/shard_map/ppermute | solution.py:32

commit v10 on v9

--- a/solution.py
+++ b/solution.py
@@ -345,20 +345,20 @@
     spots = jnp.concatenate([row * col_tiles + tile_cols[0, 0], tile_counts[0, 0][:, None]], axis=1)
     dense = densify(tiles[0, 0], spots, place, groups, rows_local)
 
-    held = [features]
+    held, beside = [features], swap_cores(features)
     for k in range(1, chips):
-        given = after(features, held[k - 1]) if k == top_bit(k) > 1 else held[k - top_bit(k)]
+        given = after(features, beside) if k == top_bit(k) > 1 else held[k - top_bit(k)]
         held.append(swap_chips(given, top_bit(k)))
         if k == 1:
             held[1] = after(held[1], spots)
-    totals = None
+    totals, half = None, chips // 2
     for first, stop in ((0, chips // 2), (chips // 2, chips)):
         sources = []
         for k in range(first, stop):
             own = held[k] if totals is None else after(held[k], held[-1], *totals)
-            sources += [own, swap_cores(own)]
+            sources += [own, swap_cores(own) if k else beside]
         if stop < chips:
-            totals = forward(dense, 2 * first, sources, 0, None, [jnp.float32] * groups)
+            totals = forward(after(dense, held[half]), 2 * first, sources, 0, None, [jnp.float32] * groups)
     upper = groups // 2
     high = forward(dense, 2 * first, sources, upper, totals[upper:], [jnp.bfloat16] * upper)
     low = forward(after(dense, *high), 2 * first, sources, 0, totals[:upper], [jnp.float32] * upper)
@@ -382,12 +382,9 @@
     for k in range(1, groups):
         part = part + swap_members(parts[k].astype(jnp.bfloat16), k, turn=1).astype(jnp.float32)
     part = part.astype(jnp.bfloat16)
-    terms = [part] + [swap_chips(part, k) for k in range(1, chips)]
-    grads[-1] = after(grads[-1], *terms[1:])
-    terms = [term.astype(jnp.float32) for term in terms]
-    while len(terms) > 1:
-        terms = [terms[i] + terms[i + 1] for i in range(0, len(terms), 2)]
-    part = terms[0] * scale
+    near = swap_chips(part, 1)
+    part = part.astype(jnp.float32) + near.astype(jnp.float32)
+    grads[-1] = after(grads[-1], near)
 
     half = chips // 2
     other = backward(dense_t[half:], grads, 1)
@@ -404,6 +401,12 @@
         totals, arrived = totals[:half], [swap_chips(send, half)]
     (feature_grad,) = settle(totals, arrived, [jnp.bfloat16])
 
+    bit = 2
+    while bit < chips:
+        part = part.astype(jnp.bfloat16)
+        part = part.astype(jnp.float32) + swap_chips(part, bit).astype(jnp.float32)
+        bit *= 2
+    part = part * scale
     parts = [part] + [swap_members(part, k, turn=1) for k in range(1, groups)]
     weight_grad = place_slices(parts, swap_cores(jnp.concatenate(parts)), place)
     return (activated, feature_grad, weight_grad)

time: 96 us -> 94.3 us (0.982)
  waiting for transfers between devices: 46.7 us -> 34 us
  starting transfers between devices: 30.3 us -> 41.1 us
    ppermute x8 -> x7, starting transfers between devices: 11.9 us -> 24 us  [swap_chips(): lax.ppermute(x, 'dom', [(i, i ^ 2 * between(held, i % 2, bits)) for i in...]
    ppermute x8 -> x7, waiting for transfers between devices: 27.6 us -> 15.7 us  [swap_chips(): lax.ppermute(x, 'dom', [(i, i ^ 2 * between(held, i % 2, bits)) for i in...]
    ppermute x8, waiting for transfers between devices: 2.6 us -> 1.41 us  [swap_cores(): lax.ppermute(x, 'dom', [(i, i ^ 1) for i in range(lax.axis_size('dom'))])]
    ppermute x8, starting transfers between devices: 2.49 us -> 1.37 us  [swap_cores(): lax.ppermute(x, 'dom', [(i, i ^ 1) for i in range(lax.axis_size('dom'))])]
  transfers between devices with their start and end apart: 28 -> 27, of which waited for: 19 -> 14; matrix products, arithmetic and copies ran while one was open for 2% -> 2% of each run, Pallas kernels for 10% -> 10%
where the time goes in v10:
time: 94.3 us; the launch traced here: 94.1 us
  starting transfers between devices  41.1 us (44%)
  waiting for transfers between devices  34 us (36%)
  Pallas kernels  13.7 us (15%)
  local copies, waits for them, and re-layouts  2.93 us (3%)
  other arithmetic  1.32 us (1%)
    ppermute x7, starting transfers between devices, swap_chips(): lax.ppermute(x, 'dom', [(i, i ^ 2 * between(held, i % 2, bits)) for i in...  24 us
    ppermute x12, waiting for transfers between devices, swap_members(): return lax.ppermute(x, ('dom', 'repl'), pairs)  16.9 us
    ppermute x12, starting transfers between devices, swap_members(): return lax.ppermute(x, ('dom', 'repl'), pairs)  15.8 us
    ppermute x7, waiting for transfers between devices, swap_chips(): lax.ppermute(x, 'dom', [(i, i ^ 2 * between(held, i % 2, bits)) for i in...  15.7 us
    pallas_call x4, Pallas kernels, backward(): pl.pallas_call(functools.partial(backward_kernel, side=side, count=count,...  2.81 us
    pallas_call x3, Pallas kernels, forward(): pl.pallas_call(functools.partial(forward_kernel, first=first, base=base,...  2.66 us
    pallas_call x1, Pallas kernels, densify(): pl.pallas_call(functools.partial(densify_kernel, col_tiles=col_tiles), ou...  2.44 us
    unnamed x8, local copies, waits for them, and re-layouts  2.2 us
  transfers between devices with their start and end apart: 27, of which 14 were waited for; matrix products, arithmetic and copies ran while one was open for 2% of the time, Pallas kernels for 10%

profile of v10, /device:TPU:0, one launch (start us, length us, event | category | flops | bytes accessed | tf_op | source)
XLA Modules:
  0.0 94.1 jit_solution(13388486046264751795)
XLA Ops:
  1.1 3.7 %collective-permute-start.2 = (bf16[256,512]{1,0:T(8,128)(2,1)}, bf16[256,512]{1,0:T(8,128)(2,1)S(1)}, u32[]{:S(2)}, u32[]{:S(2)}) collective-permute-start(bf16[256,512]{1,0:T(8,128)(2,1)} %refs_1_.1), channel_id=1, source_target_pairs={{0,16},{4,12},{8,24},{12,4},{16,0},{20,28},{24,8},{28,20},{1,17},{... | collective-permute-start | bytes 786440 | tf_op jit(solution)/shard_map/ppermute | solution.py:32
  6.3 1.6 %collective-permute-start.1 = (bf16[256,512]{1,0:T(8,128)(2,1)}, bf16[256,512]{1,0:T(8,128)(2,1)S(1)}, u32[]{:S(2)}, u32[]{:S(2)}) collective-permute-start(bf16[256,512]{1,0:T(8,128)(2,1)} %refs_1_.1), channel_id=1, source_target_pairs={{0,8},{4,20},{8,0},{12,28},{16,24},{20,4},{24,16},{28,12},{1,9},{5... | collective-permute-start | bytes 786440 | tf_op jit(solution)/shard_map/ppermute | solution.py:32
  7.9 4.8 %collective-permute-done.2.refs_3_ = bf16[256,512]{1,0:T(8,128)(2,1)S(1)} collective-permute-done((bf16[256,512]{1,0:T(8,128)(2,1)}, bf16[256,512]{1,0:T(8,128)(2,1)S(1)}, u32[]{:S(2)}, u32[]{:S(2)}) %collective-permute-start.2) | collective-permute-done | bytes 262176 | tf_op jit(solution)/shard_map/ppermute | solution.py:32
  12.7 8.5 %collective-permute-start.3 = (bf16[256,512]{1,0:T(8,128)(2,1)S(1)}, bf16[256,512]{1,0:T(8,128)(2,1)S(1)}, u32[]{:S(2)}, u32[]{:S(2)}) collective-permute-start(bf16[256,512]{1,0:T(8,128)(2,1)S(1)} %collective-permute-done.2.refs_3_), channel_id=1, source_target_pairs={{0,8},{4,20},{8,0},{12,28},{16,24},{20,4},{24,16},{28,12},{1,9},{5... | collective-permute-start | bytes 786440 | tf_op jit(solution)/shard_map/ppermute | solution.py:32
  21.3 2.2 %copy-done = bf16[1,1,8,16,128,128]{5,4,3,2,1,0:T(8,128)(2,1)S(1)} copy-done((bf16[1,1,8,16,128,128]{5,4,3,2,1,0:T(8,128)(2,1)S(1)}, bf16[1,1,8,16,128,128]{5,4,3,2,1,0:T(8,128)(2,1)}, u32[]{:S(2)}) %copy-start) | copy-done | bytes 4194328
  23.5 2.4 %densify.1.refs_0_.a_ref = bf16[8,1024,256]{2,1,0:T(8,128)(2,1)S(1)} custom-call(s32[8,17]{1,0:T(8,128)S(1)} %pad_add_fusion.spots_ref, s32[2]{0:T(128)S(1)} %pad_add_fusion.1.place_ref, bf16[8,16,128,128]{3,2,1,0:T(8,128)(2,1)S(1)} %bitcast.26), custom_call_target="tpu_custom_call" | custom-call | flops 2097152 | bytes 16777216 | tf_op jit(solution)/shard_map/densify/pallas_call | solution.py:86
  25.9 1.2 %forward.3 = (f32[256,512]{1,0:T(8,128)S(1)}, f32[256,512]{1,0:T(8,128)S(1)}, f32[256,512]{1,0:T(8,128)S(1)}, f32[256,512]{1,0:T(8,128)S(1)}) custom-call(bf16[8,1024,256]{2,1,0:T(8,128)(2,1)S(1)} %densify.1.refs_0_.a_ref, bf16[256,512]{1,0:T(8,128)(2,1)S(1)} %copy-done.2, bf16[256,512]{1,0:T(8,128)(2,1)S(1)} %collective-permute-done.refs_2_, ...), custom_call_target="tpu_custom_call" | custom-call | flops 1073741824 | bytes 4194304 | tf_op jit(solution)/shard_map/forward/pallas_call | solution.py:139
  27.8 1.0 %collective-permute-done.5.refs_2_ = bf16[256,512]{1,0:T(8,128)(2,1)S(1)} collective-permute-done((bf16[256,512]{1,0:T(8,128)(2,1)S(1)}, bf16[256,512]{1,0:T(8,128)(2,1)S(1)}, u32[]{:S(2)}, u32[]{:S(2)}) %collective-permute-start.5) | collective-permute-done | bytes 262176 | tf_op jit(solution)/shard_map/ppermute | solution.py:26
  29.9 1.8 %collective-permute-start.8 = (bf16[256,512]{1,0:T(8,128)(2,1)S(1)}, bf16[256,512]{1,0:T(8,128)(2,1)S(1)}, u32[]{:S(2)}, u32[]{:S(2)}) collective-permute-start(bf16[256,512]{1,0:T(8,128)(2,1)S(1)} %get-tuple-element.52), channel_id=1, source_target_pairs={{0,1},{1,0},{2,3},{3,2},{4,6},{5,7},{6,4},{7,5},{8,9},{9,8},{10,11... | collective-permute-start | bytes 786440 | tf_op jit(solution)/shard_map/ppermute | solution.py:42
  32.7 3.6 %collective-permute-done.8 = bf16[256,512]{1,0:T(8,128)(2,1)S(1)} collective-permute-done((bf16[256,512]{1,0:T(8,128)(2,1)S(1)}, bf16[256,512]{1,0:T(8,128)(2,1)S(1)}, u32[]{:S(2)}, u32[]{:S(2)}) %collective-permute-start.8) | collective-permute-done | bytes 262176 | tf_op jit(solution)/shard_map/ppermute | solution.py:42
  36.4 1.9 %collective-permute-start.9 = (bf16[256,512]{1,0:T(8,128)(2,1)S(1)}, bf16[256,512]{1,0:T(8,128)(2,1)S(1)}, u32[]{:S(2)}, u32[]{:S(2)}) collective-permute-start(bf16[256,512]{1,0:T(8,128)(2,1)S(1)} %add_convert_fusion.2), channel_id=1, source_target_pairs={{0,2},{1,3},{2,0},{3,1},{4,5},{5,4},{6,7},{7,6},{8,10},{9,11},{10,... | collective-permute-start | bytes 786440 | tf_op jit(solution)/shard_map/ppermute | solution.py:42
  38.4 1.4 %collective-permute-done.7.refs_1_ = bf16[256,512]{1,0:T(8,128)(2,1)S(1)} collective-permute-done((bf16[256,512]{1,0:T(8,128)(2,1)S(1)}, bf16[256,512]{1,0:T(8,128)(2,1)S(1)}, u32[]{:S(2)}, u32[]{:S(2)}) %collective-permute-start.7) | collective-permute-done | bytes 262176 | tf_op jit(solution)/shard_map/ppermute | solution.py:42
  39.7 1.2 %transposed.1 = (bf16[2,256,1024]{2,1,0:T(8,128)(2,1)S(1)}, bf16[2,256,1024]{2,1,0:T(8,128)(2,1)S(1)}, bf16[2,256,1024]{2,1,0:T(8,128)(2,1)S(1)}, bf16[2,256,1024]{2,1,0:T(8,128)(2,1)S(1)}) custom-call(bf16[8,1024,256]{2,1,0:T(8,128)(2,1)S(1)} %densify.1.refs_0_.a_ref), custom_call_target="tpu_custom_call" | custom-call | bytes 8388608 | tf_op jit(solution)/shard_map/transposed/pallas_call | solution.py:111
  40.9 1.9 %collective-permute-done.9.refs_2_ = bf16[256,512]{1,0:T(8,128)(2,1)S(1)} collective-permute-done((bf16[256,512]{1,0:T(8,128)(2,1)S(1)}, bf16[256,512]{1,0:T(8,128)(2,1)S(1)}, u32[]{:S(2)}, u32[]{:S(2)}) %collective-permute-start.9) | collective-permute-done | bytes 262176 | tf_op jit(solution)/shard_map/ppermute | solution.py:42
  42.9 1.2 %middle.1 = (bf16[256,512]{1,0:T(8,128)(2,1)}, bf16[256,512]{1,0:T(8,128)(2,1)S(1)}, bf16[256,512]{1,0:T(8,128)(2,1)S(1)}, bf16[256,512]{1,0:T(8,128)(2,1)S(1)}) custom-call(f32[256,512]{1,0:T(8,128)S(1)} %get-tuple-element.54.refs_0_, bf16[256,512]{1,0:T(8,128)(2,1)S(1)} %collective-permute-done.7.refs_1_, ...), custom_call_target="tpu_custom_call" | custom-call | flops 268435456 | bytes 1310720 | tf_op jit(solution)/shard_map/middle/pallas_call | solution.py:174
  45.1 1.9 %collective-permute-start.10 = (bf16[256,512]{1,0:T(8,128)(2,1)S(1)}, bf16[256,512]{1,0:T(8,128)(2,1)S(1)}, u32[]{:S(2)}, u32[]{:S(2)}) collective-permute-start(bf16[256,512]{1,0:T(8,128)(2,1)S(1)} %get-tuple-element.76.refs_2_), channel_id=1, source_target_pairs={{0,2},{1,3},{2,0},{3,1},{4,5},{5,4},{6,7},{7,6},{8,10},{9,11},{10,... | collective-permute-start | bytes 786440 | tf_op jit(solution)/shard_map/ppermute | solution.py:42
  49.0 1.6 %collective-permute-start.15 = (bf16[64,512]{1,0:T(8,128)(2,1)S(1)}, bf16[64,512]{1,0:T(8,128)(2,1)S(1)}, u32[]{:S(2)}, u32[]{:S(2)}) collective-permute-start(bf16[64,512]{1,0:T(8,128)(2,1)S(1)} %get-tuple-element.85), channel_id=1, source_target_pairs={{0,2},{1,3},{2,0},{3,1},{4,5},{5,4},{6,7},{7,6},{8,10},{9,11},{10,... | collective-permute-start | bytes 196616 | tf_op jit(solution)/shard_map/ppermute | solution.py:42
  50.6 1.0 %collective-permute-start.14 = (bf16[64,512]{1,0:T(8,128)(2,1)S(1)}, bf16[64,512]{1,0:T(8,128)(2,1)S(1)}, u32[]{:S(2)}, u32[]{:S(2)}) collective-permute-start(bf16[64,512]{1,0:T(8,128)(2,1)S(1)} %get-tuple-element.83), channel_id=1, source_target_pairs={{0,1},{1,0},{2,3},{3,2},{4,6},{5,7},{6,4},{7,5},{8,9},{9,8},{10,11... | collective-permute-start | bytes 196616 | tf_op jit(solution)/shard_map/ppermute | solution.py:42
  51.6 2.8 %collective-permute-done.10.refs_3_ = bf16[256,512]{1,0:T(8,128)(2,1)S(1)} collective-permute-done((bf16[256,512]{1,0:T(8,128)(2,1)S(1)}, bf16[256,512]{1,0:T(8,128)(2,1)S(1)}, u32[]{:S(2)}, u32[]{:S(2)}) %collective-permute-start.10) | collective-permute-done | bytes 262176 | tf_op jit(solution)/shard_map/ppermute | solution.py:42
  55.2 1.7 %collective-permute-start.12 = (bf16[256,512]{1,0:T(8,128)(2,1)S(1)}, bf16[256,512]{1,0:T(8,128)(2,1)S(1)}, u32[]{:S(2)}, u32[]{:S(2)}) collective-permute-start(bf16[256,512]{1,0:T(8,128)(2,1)S(1)} %collective-permute-done.10.refs_3_), channel_id=1, source_target_pairs={{0,1},{1,0},{2,3},{3,2},{4,6},{5,7},{6,4},{7,5},{8,9},{9,8},{10,11... | collective-permute-start | bytes 786440 | tf_op jit(solution)/shard_map/ppermute | solution.py:42
  57.2 4.1 %collective-permute-start.17 = (bf16[64,512]{1,0:T(8,128)(2,1)S(1)}, bf16[64,512]{1,0:T(8,128)(2,1)S(1)}, u32[]{:S(2)}, u32[]{:S(2)}) collective-permute-start(bf16[64,512]{1,0:T(8,128)(2,1)S(1)} %add_convert_fusion.4), channel_id=1, source_target_pairs={{0,16},{4,12},{8,24},{12,4},{16,0},{20,28},{24,8},{28,20},{1,17},{... | collective-permute-start | bytes 196616 | tf_op jit(solution)/shard_map/ppermute | solution.py:32
  61.3 2.3 %collective-permute-done.17 = bf16[64,512]{1,0:T(8,128)(2,1)S(1)} collective-permute-done((bf16[64,512]{1,0:T(8,128)(2,1)S(1)}, bf16[64,512]{1,0:T(8,128)(2,1)S(1)}, u32[]{:S(2)}, u32[]{:S(2)}) %collective-permute-start.17) | collective-permute-done | bytes 65568 | tf_op jit(solution)/shard_map/ppermute | solution.py:32
  64.3 2.9 %collective-permute-start.22 = (bf16[64,512]{1,0:T(8,128)(2,1)S(1)}, bf16[64,512]{1,0:T(8,128)(2,1)S(1)}, u32[]{:S(2)}, u32[]{:S(2)}) collective-permute-start(bf16[64,512]{1,0:T(8,128)(2,1)S(1)} %add_convert_fusion.3), channel_id=1, source_target_pairs={{0,8},{4,20},{8,0},{12,28},{16,24},{20,4},{24,16},{28,12},{1,9},{5... | collective-permute-start | bytes 196616 | tf_op jit(solution)/shard_map/ppermute | solution.py:32
  68.2 1.1 %collective-permute-start.20 = (bf16[512,512]{1,0:T(8,128)(2,1)S(1)}, bf16[512,512]{1,0:T(8,128)(2,1)S(1)}, u32[]{:S(2)}, u32[]{:S(2)}) collective-permute-start(bf16[512,512]{1,0:T(8,128)(2,1)S(1)} %pad_maximum_fusion), channel_id=1, source_target_pairs={{0,8},{4,20},{8,0},{12,28},{16,24},{20,4},{24,16},{28,12},{1,9},{5... | collective-permute-start | bytes 1572872 | tf_op jit(solution)/shard_map/ppermute | solution.py:32
  70.1 1.4 %collective-permute-start.23 = (f32[64,512]{1,0:T(8,128)S(1)}, f32[64,512]{1,0:T(8,128)S(1)}, u32[]{:S(2)}, u32[]{:S(2)}) collective-permute-start(f32[64,512]{1,0:T(8,128)S(1)} %add_multiply_fusion.refs_0_), channel_id=1, source_target_pairs={{0,1},{1,0},{2,3},{3,2},{4,6},{5,7},{6,4},{7,5},{8,9},{9,8},{10,11... | collective-permute-start | bytes 393224 | tf_op jit(solution)/shard_map/ppermute | solution.py:42
  71.5 1.5 %collective-permute-start.24 = (f32[64,512]{1,0:T(8,128)S(1)}, f32[64,512]{1,0:T(8,128)S(1)}, u32[]{:S(2)}, u32[]{:S(2)}) collective-permute-start(f32[64,512]{1,0:T(8,128)S(1)} %add_multiply_fusion.refs_0_), channel_id=1, source_target_pairs={{0,2},{1,3},{2,0},{3,1},{4,5},{5,4},{6,7},{7,6},{8,10},{9,11},{10,... | collective-permute-start | bytes 393224 | tf_op jit(solution)/shard_map/ppermute | solution.py:42
  73.7 2.8 %collective-permute-done.23.refs_1_ = f32[64,512]{1,0:T(8,128)S(1)} collective-permute-done((f32[64,512]{1,0:T(8,128)S(1)}, f32[64,512]{1,0:T(8,128)S(1)}, u32[]{:S(2)}, u32[]{:S(2)}) %collective-permute-start.23) | collective-permute-done | bytes 131104 | tf_op jit(solution)/shard_map/ppermute | solution.py:42
  76.5 3.4 %collective-permute-done.25.refs_3_ = f32[64,512]{1,0:T(8,128)S(1)} collective-permute-done((f32[64,512]{1,0:T(8,128)S(1)}, f32[64,512]{1,0:T(8,128)S(1)}, u32[]{:S(2)}, u32[]{:S(2)}) %collective-permute-start.25) | collective-permute-done | bytes 131104 | tf_op jit(solution)/shard_map/ppermute | solution.py:42
  80.7 2.3 %collective-permute-done.20.refs_3_ = bf16[512,512]{1,0:T(8,128)(2,1)S(1)} collective-permute-done((bf16[512,512]{1,0:T(8,128)(2,1)S(1)}, bf16[512,512]{1,0:T(8,128)(2,1)S(1)}, u32[]{:S(2)}, u32[]{:S(2)}) %collective-permute-start.20) | collective-permute-done | bytes 524320 | tf_op jit(solution)/shard_map/ppermute | solution.py:32
  83.2 2.2 %collective-permute-start.21 = (bf16[256,512]{1,0:T(8,128)(2,1)S(1)}, bf16[256,512]{1,0:T(8,128)(2,1)S(1)}, u32[]{:S(2)}, u32[]{:S(2)}) collective-permute-start(bf16[256,512]{1,0:T(8,128)(2,1)S(1)} %get-tuple-element.80), channel_id=1, source_target_pairs={{0,16},{4,12},{8,24},{12,4},{16,0},{20,28},{24,8},{28,20},{1,17},{... | collective-permute-start | bytes 786440 | tf_op jit(solution)/shard_map/ppermute | solution.py:32
  85.4 1.6 %place_slices.1 = f32[512,512]{1,0:T(8,128)} custom-call(s32[2]{0:T(128)S(1)} %pad_add_fusion.1.place_ref, f32[64,512]{1,0:T(8,128)S(1)} %add_multiply_fusion.refs_0_, f32[64,512]{1,0:T(8,128)S(1)} %collective-permute-done.23.refs_1_, f32[64,512]{1,0:T(8,128)S(1)} %collective-permute-done.24.refs_2_, f32[64,512]{1,0:T(8,128)S(1)} %collective-permute-done.25.refs_3_, ...), custom_call_target="tpu_custom_call" | custom-call | bytes 2097152 | tf_op jit(solution)/shard_map/place_slices/pallas_call | solution.py:235
  87.0 6.3 %collective-permute-done.21.refs_1_ = bf16[256,512]{1,0:T(8,128)(2,1)S(1)} collective-permute-done((bf16[256,512]{1,0:T(8,128)(2,1)S(1)}, bf16[256,512]{1,0:T(8,128)(2,1)S(1)}, u32[]{:S(2)}, u32[]{:S(2)}) %collective-permute-start.21) | collective-permute-done | bytes 262176 | tf_op jit(solution)/shard_map/ppermute | solution.py:32
  (56 shorter events, 14.0 us)
Async XLA Ops:
  0.6 5.7 %collective-permute-start = (bf16[256,512]{1,0:T(8,128)(2,1)}, bf16[256,512]{1,0:T(8,128)(2,1)S(1)}, u32[]{:S(2)}, u32[]{:S(2)}) collective-permute-start(bf16[256,512]{1,0:T(8,128)(2,1)} %refs_1_.1), channel_id=1, source_target_pairs={{0,4},{4,0},{8,12},{12,8},{16,20},{20,16},{24,28},{28,24},{1,5},{5... | collective-permute-start | bytes 786440 | tf_op jit(solution)/shard_map/ppermute | solution.py:26
  1.1 11.6 %collective-permute-start.2 = (bf16[256,512]{1,0:T(8,128)(2,1)}, bf16[256,512]{1,0:T(8,128)(2,1)S(1)}, u32[]{:S(2)}, u32[]{:S(2)}) collective-permute-start(bf16[256,512]{1,0:T(8,128)(2,1)} %refs_1_.1), channel_id=1, source_target_pairs={{0,16},{4,12},{8,24},{12,4},{16,0},{20,28},{24,8},{28,20},{1,17},{... | collective-permute-start | bytes 786440 | tf_op jit(solution)/shard_map/ppermute | solution.py:32
  6.3 19.6 %collective-permute-start.1 = (bf16[256,512]{1,0:T(8,128)(2,1)}, bf16[256,512]{1,0:T(8,128)(2,1)S(1)}, u32[]{:S(2)}, u32[]{:S(2)}) collective-permute-start(bf16[256,512]{1,0:T(8,128)(2,1)} %refs_1_.1), channel_id=1, source_target_pairs={{0,8},{4,20},{8,0},{12,28},{16,24},{20,4},{24,16},{28,12},{1,9},{5... | collective-permute-start | bytes 786440 | tf_op jit(solution)/shard_map/ppermute | solution.py:32
  12.7 13.2 %collective-permute-start.4 = (bf16[256,512]{1,0:T(8,128)(2,1)S(1)}, bf16[256,512]{1,0:T(8,128)(2,1)S(1)}, u32[]{:S(2)}, u32[]{:S(2)}) collective-permute-start(bf16[256,512]{1,0:T(8,128)(2,1)S(1)} %collective-permute-done.2.refs_3_), channel_id=1, source_target_pairs={{0,4},{4,0},{8,12},{12,8},{16,20},{20,16},{24,28},{28,24},{1,5},{5... | collective-permute-start | bytes 786440 | tf_op jit(solution)/shard_map/ppermute | solution.py:26
  12.7 14.5 %collective-permute-start.3 = (bf16[256,512]{1,0:T(8,128)(2,1)S(1)}, bf16[256,512]{1,0:T(8,128)(2,1)S(1)}, u32[]{:S(2)}, u32[]{:S(2)}) collective-permute-start(bf16[256,512]{1,0:T(8,128)(2,1)S(1)} %collective-permute-done.2.refs_3_), channel_id=1, source_target_pairs={{0,8},{4,20},{8,0},{12,28},{16,24},{20,4},{24,16},{28,12},{1,9},{5... | collective-permute-start | bytes 786440 | tf_op jit(solution)/shard_map/ppermute | solution.py:32
  21.3 2.2 %copy-start = (bf16[1,1,8,16,128,128]{5,4,3,2,1,0:T(8,128)(2,1)S(1)}, bf16[1,1,8,16,128,128]{5,4,3,2,1,0:T(8,128)(2,1)}, u32[]{:S(2)}) copy-start(bf16[1,1,8,16,128,128]{5,4,3,2,1,0:T(8,128)(2,1)} %param.10) | copy-start | bytes 12582916
  23.5 2.5 %copy-start.2 = (bf16[256,512]{1,0:T(8,128)(2,1)S(1)}, bf16[256,512]{1,0:T(8,128)(2,1)}, u32[]{:S(2)}) copy-start(bf16[256,512]{1,0:T(8,128)(2,1)} %refs_1_.1) | copy-start | bytes 786436
  27.2 1.6 %collective-permute-start.5 = (bf16[256,512]{1,0:T(8,128)(2,1)S(1)}, bf16[256,512]{1,0:T(8,128)(2,1)S(1)}, u32[]{:S(2)}, u32[]{:S(2)}) collective-permute-start(bf16[256,512]{1,0:T(8,128)(2,1)S(1)} %collective-permute-done.1.refs_1_), channel_id=1, source_target_pairs={{0,4},{4,0},{8,12},{12,8},{16,20},{20,16},{24,28},{28,24},{1,5},{5... | collective-permute-start | bytes 786440 | tf_op jit(solution)/shard_map/ppermute | solution.py:26
  27.3 1.9 %collective-permute-start.6 = (bf16[256,512]{1,0:T(8,128)(2,1)S(1)}, bf16[256,512]{1,0:T(8,128)(2,1)S(1)}, u32[]{:S(2)}, u32[]{:S(2)}) collective-permute-start(bf16[256,512]{1,0:T(8,128)(2,1)S(1)} %collective-permute-done.3.refs_3_), channel_id=1, source_target_pairs={{0,4},{4,0},{8,12},{12,8},{16,20},{20,16},{24,28},{28,24},{1,5},{5... | collective-permute-start | bytes 786440 | tf_op jit(solution)/shard_map/ppermute | solution.py:26
  29.9 6.4 %collective-permute-start.8 = (bf16[256,512]{1,0:T(8,128)(2,1)S(1)}, bf16[256,512]{1,0:T(8,128)(2,1)S(1)}, u32[]{:S(2)}, u32[]{:S(2)}) collective-permute-start(bf16[256,512]{1,0:T(8,128)(2,1)S(1)} %get-tuple-element.52), channel_id=1, source_target_pairs={{0,1},{1,0},{2,3},{3,2},{4,6},{5,7},{6,4},{7,5},{8,9},{9,8},{10,11... | collective-permute-start | bytes 786440 | tf_op jit(solution)/shard_map/ppermute | solution.py:42
  31.6 8.1 %collective-permute-start.7 = (bf16[256,512]{1,0:T(8,128)(2,1)S(1)}, bf16[256,512]{1,0:T(8,128)(2,1)S(1)}, u32[]{:S(2)}, u32[]{:S(2)}) collective-permute-start(bf16[256,512]{1,0:T(8,128)(2,1)S(1)} %get-tuple-element.51), channel_id=1, source_target_pairs={{0,1},{1,0},{2,3},{3,2},{4,6},{5,7},{6,4},{7,5},{8,9},{9,8},{10,11... | collective-permute-start | bytes 786440 | tf_op jit(solution)/shard_map/ppermute | solution.py:42
  32.7 10.2 %copy-start.1 = (bf16[512,512]{1,0:T(8,128)(2,1)S(1)}, bf16[512,512]{1,0:T(8,128)(2,1)}, u32[]{:S(2)}) copy-start(bf16[512,512]{1,0:T(8,128)(2,1)} %refs_4_.1) | copy-start | bytes 1572868
  32.7 10.1 %copy-start.3 = (bf16[256,512]{1,0:T(8,128)(2,1)S(1)}, bf16[256,512]{1,0:T(8,128)(2,1)}, u32[]{:S(2)}) copy-start(bf16[256,512]{1,0:T(8,128)(2,1)} %refs_3_.1) | copy-start | bytes 786436
  36.4 6.4 %collective-permute-start.9 = (bf16[256,512]{1,0:T(8,128)(2,1)S(1)}, bf16[256,512]{1,0:T(8,128)(2,1)S(1)}, u32[]{:S(2)}, u32[]{:S(2)}) collective-permute-start(bf16[256,512]{1,0:T(8,128)(2,1)S(1)} %add_convert_fusion.2), channel_id=1, source_target_pairs={{0,2},{1,3},{2,0},{3,1},{4,5},{5,4},{6,7},{7,6},{8,10},{9,11},{10,... | collective-permute-start | bytes 786440 | tf_op jit(solution)/shard_map/ppermute | solution.py:42
  45.0 3.0 %collective-permute-start.13 = (bf16[256,512]{1,0:T(8,128)(2,1)S(1)}, bf16[256,512]{1,0:T(8,128)(2,1)S(1)}, u32[]{:S(2)}, u32[]{:S(2)}) collective-permute-start(bf16[256,512]{1,0:T(8,128)(2,1)S(1)} %get-tuple-element.68), channel_id=1, source_target_pairs={{0,4},{4,0},{8,12},{12,8},{16,20},{20,16},{24,28},{28,24},{1,5},{5... | collective-permute-start | bytes 786440 | tf_op jit(solution)/shard_map/ppermute | solution.py:26
  45.1 9.3 %collective-permute-start.10 = (bf16[256,512]{1,0:T(8,128)(2,1)S(1)}, bf16[256,512]{1,0:T(8,128)(2,1)S(1)}, u32[]{:S(2)}, u32[]{:S(2)}) collective-permute-start(bf16[256,512]{1,0:T(8,128)(2,1)S(1)} %get-tuple-element.76.refs_2_), channel_id=1, source_target_pairs={{0,2},{1,3},{2,0},{3,1},{4,5},{5,4},{6,7},{7,6},{8,10},{9,11},{10,... | collective-permute-start | bytes 786440 | tf_op jit(solution)/shard_map/ppermute | solution.py:42
  47.0 8.2 %collective-permute-start.11 = (bf16[256,512]{1,0:T(8,128)(2,1)S(1)}, bf16[256,512]{1,0:T(8,128)(2,1)S(1)}, u32[]{:S(2)}, u32[]{:S(2)}) collective-permute-start(bf16[256,512]{1,0:T(8,128)(2,1)S(1)} %get-tuple-element.76.refs_2_), channel_id=1, source_target_pairs={{0,1},{1,0},{2,3},{3,2},{4,6},{5,7},{6,4},{7,5},{8,9},{9,8},{10,11... | collective-permute-start | bytes 786440 | tf_op jit(solution)/shard_map/ppermute | solution.py:42
  48.0 9.1 %collective-permute-start.16 = (bf16[64,512]{1,0:T(8,128)(2,1)S(1)}, bf16[64,512]{1,0:T(8,128)(2,1)S(1)}, u32[]{:S(2)}, u32[]{:S(2)}) collective-permute-start(bf16[64,512]{1,0:T(8,128)(2,1)S(1)} %get-tuple-element.84), channel_id=1, source_target_pairs={{0,3},{1,2},{2,1},{3,0},{4,7},{5,6},{6,5},{7,4},{8,11},{9,10},{10,... | collective-permute-start | bytes 196616 | tf_op jit(solution)/shard_map/ppermute | solution.py:42
  49.0 8.2 %collective-permute-start.15 = (bf16[64,512]{1,0:T(8,128)(2,1)S(1)}, bf16[64,512]{1,0:T(8,128)(2,1)S(1)}, u32[]{:S(2)}, u32[]{:S(2)}) collective-permute-start(bf16[64,512]{1,0:T(8,128)(2,1)S(1)} %get-tuple-element.85), channel_id=1, source_target_pairs={{0,2},{1,3},{2,0},{3,1},{4,5},{5,4},{6,7},{7,6},{8,10},{9,11},{10,... | collective-permute-start | bytes 196616 | tf_op jit(solution)/shard_map/ppermute | solution.py:42
  50.6 6.5 %collective-permute-start.14 = (bf16[64,512]{1,0:T(8,128)(2,1)S(1)}, bf16[64,512]{1,0:T(8,128)(2,1)S(1)}, u32[]{:S(2)}, u32[]{:S(2)}) collective-permute-start(bf16[64,512]{1,0:T(8,128)(2,1)S(1)} %get-tuple-element.83), channel_id=1, source_target_pairs={{0,1},{1,0},{2,3},{3,2},{4,6},{5,7},{6,4},{7,5},{8,9},{9,8},{10,11... | collective-permute-start | bytes 196616 | tf_op jit(solution)/shard_map/ppermute | solution.py:42
  55.2 8.3 %collective-permute-start.12 = (bf16[256,512]{1,0:T(8,128)(2,1)S(1)}, bf16[256,512]{1,0:T(8,128)(2,1)S(1)}, u32[]{:S(2)}, u32[]{:S(2)}) collective-permute-start(bf16[256,512]{1,0:T(8,128)(2,1)S(1)} %collective-permute-done.10.refs_3_), channel_id=1, source_target_pairs={{0,1},{1,0},{2,3},{3,2},{4,6},{5,7},{6,4},{7,5},{8,9},{9,8},{10,11... | collective-permute-start | bytes 786440 | tf_op jit(solution)/shard_map/ppermute | solution.py:42
  57.2 6.3 %collective-permute-start.17 = (bf16[64,512]{1,0:T(8,128)(2,1)S(1)}, bf16[64,512]{1,0:T(8,128)(2,1)S(1)}, u32[]{:S(2)}, u32[]{:S(2)}) collective-permute-start(bf16[64,512]{1,0:T(8,128)(2,1)S(1)} %add_convert_fusion.4), channel_id=1, source_target_pairs={{0,16},{4,12},{8,24},{12,4},{16,0},{20,28},{24,8},{28,20},{1,17},{... | collective-permute-start | bytes 196616 | tf_op jit(solution)/shard_map/ppermute | solution.py:32
  64.2 3.7 %collective-permute-start.18 = (bf16[512,512]{1,0:T(8,128)(2,1)S(1)}, bf16[512,512]{1,0:T(8,128)(2,1)S(1)}, u32[]{:S(2)}, u32[]{:S(2)}) collective-permute-start(bf16[512,512]{1,0:T(8,128)(2,1)S(1)} %backward.4), channel_id=1, source_target_pairs={{0,4},{4,0},{8,12},{12,8},{16,20},{20,16},{24,28},{28,24},{1,5},{5... | collective-permute-start | bytes 1572872 | tf_op jit(solution)/shard_map/ppermute | solution.py:26
  64.3 5.7 %collective-permute-start.22 = (bf16[64,512]{1,0:T(8,128)(2,1)S(1)}, bf16[64,512]{1,0:T(8,128)(2,1)S(1)}, u32[]{:S(2)}, u32[]{:S(2)}) collective-permute-start(bf16[64,512]{1,0:T(8,128)(2,1)S(1)} %add_convert_fusion.3), channel_id=1, source_target_pairs={{0,8},{4,20},{8,0},{12,28},{16,24},{20,4},{24,16},{28,12},{1,9},{5... | collective-permute-start | bytes 196616 | tf_op jit(solution)/shard_map/ppermute | solution.py:32
  68.2 14.9 %collective-permute-start.20 = (bf16[512,512]{1,0:T(8,128)(2,1)S(1)}, bf16[512,512]{1,0:T(8,128)(2,1)S(1)}, u32[]{:S(2)}, u32[]{:S(2)}) collective-permute-start(bf16[512,512]{1,0:T(8,128)(2,1)S(1)} %pad_maximum_fusion), channel_id=1, source_target_pairs={{0,8},{4,20},{8,0},{12,28},{16,24},{20,4},{24,16},{28,12},{1,9},{5... | collective-permute-start | bytes 1572872 | tf_op jit(solution)/shard_map/ppermute | solution.py:32
  70.0 10.7 %collective-permute-start.19 = (bf16[512,512]{1,0:T(8,128)(2,1)S(1)}, bf16[512,512]{1,0:T(8,128)(2,1)S(1)}, u32[]{:S(2)}, u32[]{:S(2)}) collective-permute-start(bf16[512,512]{1,0:T(8,128)(2,1)S(1)} %backward.7), channel_id=1, source_target_pairs={{0,4},{4,0},{8,12},{12,8},{16,20},{20,16},{24,28},{28,24},{1,5},{5... | collective-permute-start | bytes 1572872 | tf_op jit(solution)/shard_map/ppermute | solution.py:26
  70.1 6.3 %collective-permute-start.23 = (f32[64,512]{1,0:T(8,128)S(1)}, f32[64,512]{1,0:T(8,128)S(1)}, u32[]{:S(2)}, u32[]{:S(2)}) collective-permute-start(f32[64,512]{1,0:T(8,128)S(1)} %add_multiply_fusion.refs_0_), channel_id=1, source_target_pairs={{0,1},{1,0},{2,3},{3,2},{4,6},{5,7},{6,4},{7,5},{8,9},{9,8},{10,11... | collective-permute-start | bytes 393224 | tf_op jit(solution)/shard_map/ppermute | solution.py:42
  71.5 5.0 %collective-permute-start.24 = (f32[64,512]{1,0:T(8,128)S(1)}, f32[64,512]{1,0:T(8,128)S(1)}, u32[]{:S(2)}, u32[]{:S(2)}) collective-permute-start(f32[64,512]{1,0:T(8,128)S(1)} %add_multiply_fusion.refs_0_), channel_id=1, source_target_pairs={{0,2},{1,3},{2,0},{3,1},{4,5},{5,4},{6,7},{7,6},{8,10},{9,11},{10,... | collective-permute-start | bytes 393224 | tf_op jit(solution)/shard_map/ppermute | solution.py:42
  73.0 6.9 %collective-permute-start.25 = (f32[64,512]{1,0:T(8,128)S(1)}, f32[64,512]{1,0:T(8,128)S(1)}, u32[]{:S(2)}, u32[]{:S(2)}) collective-permute-start(f32[64,512]{1,0:T(8,128)S(1)} %add_multiply_fusion.refs_0_), channel_id=1, source_target_pairs={{0,3},{1,2},{2,1},{3,0},{4,7},{5,6},{6,5},{7,4},{8,11},{9,10},{10,... | collective-permute-start | bytes 393224 | tf_op jit(solution)/shard_map/ppermute | solution.py:42
  79.9 5.5 %collective-permute-start.26 = (f32[256,512]{1,0:T(8,128)S(1)}, f32[256,512]{1,0:T(8,128)S(1)}, u32[]{:S(2)}, u32[]{:S(2)}) collective-permute-start(f32[256,512]{1,0:T(8,128)S(1)} %pad_maximum_fusion.1), channel_id=1, source_target_pairs={{0,4},{4,0},{8,12},{12,8},{16,20},{20,16},{24,28},{28,24},{1,5},{5... | collective-permute-start | bytes 1572872 | tf_op jit(solution)/shard_map/ppermute | solution.py:26
  83.2 10.1 %collective-permute-start.21 = (bf16[256,512]{1,0:T(8,128)(2,1)S(1)}, bf16[256,512]{1,0:T(8,128)(2,1)S(1)}, u32[]{:S(2)}, u32[]{:S(2)}) collective-permute-start(bf16[256,512]{1,0:T(8,128)(2,1)S(1)} %get-tuple-element.80), channel_id=1, source_target_pairs={{0,16},{4,12},{8,24},{12,4},{16,0},{20,28},{24,8},{28,20},{1,17},{... | collective-permute-start | bytes 786440 | tf_op jit(solution)/shard_map/ppermute | solution.py:32

commit v11 on v10

--- a/solution.py
+++ b/solution.py
@@ -119,26 +119,27 @@
     )(dense)
 
 
-def forward_kernel(*refs, first, base, count, slots, has_prev):
+def forward_kernel(*refs, which, base, slots, has_prev):
+    count = len(which)
     dense_ref, sources = refs[0], refs[1:1 + count]
     rest = refs[1 + count:]
     prev, outs = (rest[:slots], rest[slots:]) if has_prev else (None, rest)
     rows = outs[0].shape[0]
     for k, out_ref in reversed(list(enumerate(outs))):
         total = prev[k][...] if has_prev else None
-        for j, source in enumerate(sources):
-            part = bf16_dot(dense_ref[first + j, (base + k) * rows:(base + k + 1) * rows, :], source[...])
+        for j, source in zip(which, sources):
+            part = bf16_dot(dense_ref[j, (base + k) * rows:(base + k + 1) * rows, :], source[...])
             total = part if total is None else total + part
         out_ref[...] = total.astype(out_ref.dtype)
 
 
-def forward(dense, first, sources, base, prev, dtypes):
+def forward(dense, which, sources, base, prev, dtypes):
     slots = len(dtypes)
     depth, width = sources[0].shape
     rows = slots * depth
     return pl.pallas_call(
         functools.partial(
-            forward_kernel, first=first, base=base, count=len(sources), slots=slots, has_prev=prev is not None),
+            forward_kernel, which=which, base=base, slots=slots, has_prev=prev is not None),
         out_shape=[like((depth, width), dtype) for dtype in dtypes],
         in_specs=[WHOLE] * (1 + len(sources) + (slots if prev is not None else 0)),
         out_specs=[WHOLE] * slots,
@@ -345,23 +346,21 @@
     spots = jnp.concatenate([row * col_tiles + tile_cols[0, 0], tile_counts[0, 0][:, None]], axis=1)
     dense = densify(tiles[0, 0], spots, place, groups, rows_local)
 
-    held, beside = [features], swap_cores(features)
+    held = [features]
     for k in range(1, chips):
-        given = after(features, beside) if k == top_bit(k) > 1 else held[k - top_bit(k)]
+        given = after(features, held[k - 1]) if k == top_bit(k) > 1 else held[k - top_bit(k)]
         held.append(swap_chips(given, top_bit(k)))
         if k == 1:
             held[1] = after(held[1], spots)
-    totals, half = None, chips // 2
-    for first, stop in ((0, chips // 2), (chips // 2, chips)):
-        sources = []
-        for k in range(first, stop):
-            own = held[k] if totals is None else after(held[k], held[-1], *totals)
-            sources += [own, swap_cores(own) if k else beside]
-        if stop < chips:
-            totals = forward(after(dense, held[half]), 2 * first, sources, 0, None, [jnp.float32] * groups)
-    upper = groups // 2
-    high = forward(dense, 2 * first, sources, upper, totals[upper:], [jnp.bfloat16] * upper)
-    low = forward(after(dense, *high), 2 * first, sources, 0, totals[:upper], [jnp.float32] * upper)
+    half, upper = chips // 2, groups // 2
+    sources = [x for own in held[:half] for x in (own, swap_cores(own))]
+    totals = forward(dense, list(range(2 * half)), sources, 0, None, [jnp.float32] * groups)
+    far = [after(own, *totals) for own in held[half:]]
+    others = [swap_cores(own) for own in far]
+    totals = forward(dense, list(range(2 * half, 2 * chips, 2)), far, 0, totals, [jnp.float32] * groups)
+    odd = list(range(2 * half + 1, 2 * chips, 2))
+    high = forward(dense, odd, others, upper, totals[upper:], [jnp.bfloat16] * upper)
+    low = forward(after(dense, *high), odd, others, 0, totals[:upper], [jnp.float32] * upper)
     totals = low + high
 
     pieces = collect(totals, swap_members)

time: 94.3 us -> 91.5 us (0.970)
  starting transfers between devices: 41.1 us -> 32 us
  waiting for transfers between devices: 34 us -> 40.2 us
    ppermute x7, starting transfers between devices: 24 us -> 15.8 us  [swap_chips(): lax.ppermute(x, 'dom', [(i, i ^ 2 * between(held, i % 2, bits)) for i in...]
    ppermute x7, waiting for transfers between devices: 15.7 us -> 22.3 us  [swap_chips(): lax.ppermute(x, 'dom', [(i, i ^ 2 * between(held, i % 2, bits)) for i in...]
    ppermute x8, starting transfers between devices: 1.37 us -> 0.29 us  [swap_cores(): lax.ppermute(x, 'dom', [(i, i ^ 1) for i in range(lax.axis_size('dom'))])]
    pallas_call x3 -> x4, Pallas kernels: 2.66 us -> 2.82 us  [forward(): pl.pallas_call(functools.partial(forward_kernel, which=which, base=base,...]
  transfers between devices with their start and end apart: 27 -> 27, of which waited for: 14 -> 15; matrix products, arithmetic and copies ran while one was open for 2% -> 2% of each run, Pallas kernels for 10% -> 11%
where the time goes in v11:
time: 91.5 us; the launch traced here: 91.3 us
  waiting for transfers between devices  40.2 us (44%)
  starting transfers between devices  32 us (35%)
  Pallas kernels  14 us (15%)
  local copies, waits for them, and re-layouts  2.93 us (3%)
  other arithmetic  1.31 us (1%)
    ppermute x7, waiting for transfers between devices, swap_chips(): lax.ppermute(x, 'dom', [(i, i ^ 2 * between(held, i % 2, bits)) for i in...  22.3 us
    ppermute x12, waiting for transfers between devices, swap_members(): return lax.ppermute(x, ('dom', 'repl'), pairs)  17.1 us
    ppermute x12, starting transfers between devices, swap_members(): return lax.ppermute(x, ('dom', 'repl'), pairs)  15.9 us
    ppermute x7, starting transfers between devices, swap_chips(): lax.ppermute(x, 'dom', [(i, i ^ 2 * between(held, i % 2, bits)) for i in...  15.8 us
    pallas_call x4, Pallas kernels, forward(): pl.pallas_call(functools.partial(forward_kernel, which=which, base=base,...  2.82 us
    pallas_call x4, Pallas kernels, backward(): pl.pallas_call(functools.partial(backward_kernel, side=side, count=count,...  2.82 us
    pallas_call x1, Pallas kernels, densify(): pl.pallas_call(functools.partial(densify_kernel, col_tiles=col_tiles), ou...  2.6 us
    unnamed x8, local copies, waits for them, and re-layouts  2.2 us
  transfers between devices with their start and end apart: 27, of which 15 were waited for; matrix products, arithmetic and copies ran while one was open for 2% of the time, Pallas kernels for 11%

profile of v11, /device:TPU:0, one launch (start us, length us, event | category | flops | bytes accessed | tf_op | source)
XLA Modules:
  0.0 91.3 jit_solution(6849331960993689094)
XLA Ops:
  0.6 4.1 %collective-permute-start = (bf16[256,512]{1,0:T(8,128)(2,1)}, bf16[256,512]{1,0:T(8,128)(2,1)S(1)}, u32[]{:S(2)}, u32[]{:S(2)}) collective-permute-start(bf16[256,512]{1,0:T(8,128)(2,1)} %refs_1_.1), channel_id=1, source_target_pairs={{0,16},{4,12},{8,24},{12,4},{16,0},{20,28},{24,8},{28,20},{1,17},{... | collective-permute-start | bytes 786440 | tf_op jit(solution)/shard_map/ppermute | solution.py:32
  6.3 4.6 %collective-permute-done.refs_3_ = bf16[256,512]{1,0:T(8,128)(2,1)S(1)} collective-permute-done((bf16[256,512]{1,0:T(8,128)(2,1)}, bf16[256,512]{1,0:T(8,128)(2,1)S(1)}, u32[]{:S(2)}, u32[]{:S(2)}) %collective-permute-start) | collective-permute-done | bytes 262176 | tf_op jit(solution)/shard_map/ppermute | solution.py:32
  10.9 2.4 %collective-permute-start.1 = (bf16[256,512]{1,0:T(8,128)(2,1)}, bf16[256,512]{1,0:T(8,128)(2,1)S(1)}, u32[]{:S(2)}, u32[]{:S(2)}) collective-permute-start(bf16[256,512]{1,0:T(8,128)(2,1)} %refs_1_.1), channel_id=1, source_target_pairs={{0,8},{4,20},{8,0},{12,28},{16,24},{20,4},{24,16},{28,12},{1,9},{5... | collective-permute-start | bytes 786440 | tf_op jit(solution)/shard_map/ppermute | solution.py:32
  13.4 2.2 %copy-done = bf16[1,1,8,16,128,128]{5,4,3,2,1,0:T(8,128)(2,1)S(1)} copy-done((bf16[1,1,8,16,128,128]{5,4,3,2,1,0:T(8,128)(2,1)S(1)}, bf16[1,1,8,16,128,128]{5,4,3,2,1,0:T(8,128)(2,1)}, u32[]{:S(2)}) %copy-start) | copy-done | bytes 4194328
  15.6 2.6 %densify.1.refs_0_.a_ref = bf16[8,1024,256]{2,1,0:T(8,128)(2,1)S(1)} custom-call(s32[8,17]{1,0:T(8,128)S(1)} %pad_add_fusion.spots_ref, s32[2]{0:T(128)S(1)} %pad_add_fusion.1.place_ref, bf16[8,16,128,128]{3,2,1,0:T(8,128)(2,1)S(1)} %bitcast.26), custom_call_target="tpu_custom_call" | custom-call | flops 2097152 | bytes 16777216 | tf_op jit(solution)/shard_map/densify/pallas_call | solution.py:86
  18.2 1.2 %forward.4 = (f32[256,512]{1,0:T(8,128)S(1)}, f32[256,512]{1,0:T(8,128)S(1)}, f32[256,512]{1,0:T(8,128)S(1)}, f32[256,512]{1,0:T(8,128)S(1)}) custom-call(bf16[8,1024,256]{2,1,0:T(8,128)(2,1)S(1)} %densify.1.refs_0_.a_ref, bf16[256,512]{1,0:T(8,128)(2,1)S(1)} %copy-done.2, bf16[256,512]{1,0:T(8,128)(2,1)S(1)} %collective-permute-done.2.refs_2_, ...), custom_call_target="tpu_custom_call" | custom-call | flops 1073741824 | bytes 4194304 | tf_op jit(solution)/shard_map/forward/pallas_call | solution.py:140
  19.5 3.4 %collective-permute-done.1.refs_1_ = bf16[256,512]{1,0:T(8,128)(2,1)S(1)} collective-permute-done((bf16[256,512]{1,0:T(8,128)(2,1)}, bf16[256,512]{1,0:T(8,128)(2,1)S(1)}, u32[]{:S(2)}, u32[]{:S(2)}) %collective-permute-start.1) | collective-permute-done | bytes 262176 | tf_op jit(solution)/shard_map/ppermute | solution.py:32
  22.9 3.4 %collective-permute-done.5.refs_2_ = bf16[256,512]{1,0:T(8,128)(2,1)S(1)} collective-permute-done((bf16[256,512]{1,0:T(8,128)(2,1)S(1)}, bf16[256,512]{1,0:T(8,128)(2,1)S(1)}, u32[]{:S(2)}, u32[]{:S(2)}) %collective-permute-start.5) | collective-permute-done | bytes 262176 | tf_op jit(solution)/shard_map/ppermute | solution.py:32
  28.3 1.7 %collective-permute-start.8 = (bf16[256,512]{1,0:T(8,128)(2,1)S(1)}, bf16[256,512]{1,0:T(8,128)(2,1)S(1)}, u32[]{:S(2)}, u32[]{:S(2)}) collective-permute-start(bf16[256,512]{1,0:T(8,128)(2,1)S(1)} %get-tuple-element.56), channel_id=1, source_target_pairs={{0,1},{1,0},{2,3},{3,2},{4,6},{5,7},{6,4},{7,5},{8,9},{9,8},{10,11... | collective-permute-start | bytes 786440 | tf_op jit(solution)/shard_map/ppermute | solution.py:42
  30.8 3.9 %collective-permute-done.8 = bf16[256,512]{1,0:T(8,128)(2,1)S(1)} collective-permute-done((bf16[256,512]{1,0:T(8,128)(2,1)S(1)}, bf16[256,512]{1,0:T(8,128)(2,1)S(1)}, u32[]{:S(2)}, u32[]{:S(2)}) %collective-permute-start.8) | collective-permute-done | bytes 262176 | tf_op jit(solution)/shard_map/ppermute | solution.py:42
  34.8 1.8 %collective-permute-start.9 = (bf16[256,512]{1,0:T(8,128)(2,1)S(1)}, bf16[256,512]{1,0:T(8,128)(2,1)S(1)}, u32[]{:S(2)}, u32[]{:S(2)}) collective-permute-start(bf16[256,512]{1,0:T(8,128)(2,1)S(1)} %add_convert_fusion.2), channel_id=1, source_target_pairs={{0,2},{1,3},{2,0},{3,1},{4,5},{5,4},{6,7},{7,6},{8,10},{9,11},{10,... | collective-permute-start | bytes 786440 | tf_op jit(solution)/shard_map/ppermute | solution.py:42
  36.6 1.7 %collective-permute-done.7.refs_1_ = bf16[256,512]{1,0:T(8,128)(2,1)S(1)} collective-permute-done((bf16[256,512]{1,0:T(8,128)(2,1)S(1)}, bf16[256,512]{1,0:T(8,128)(2,1)S(1)}, u32[]{:S(2)}, u32[]{:S(2)}) %collective-permute-start.7) | collective-permute-done | bytes 262176 | tf_op jit(solution)/shard_map/ppermute | solution.py:42
  38.2 1.2 %transposed.1 = (bf16[2,256,1024]{2,1,0:T(8,128)(2,1)S(1)}, bf16[2,256,1024]{2,1,0:T(8,128)(2,1)S(1)}, bf16[2,256,1024]{2,1,0:T(8,128)(2,1)S(1)}, bf16[2,256,1024]{2,1,0:T(8,128)(2,1)S(1)}) custom-call(bf16[8,1024,256]{2,1,0:T(8,128)(2,1)S(1)} %densify.1.refs_0_.a_ref), custom_call_target="tpu_custom_call" | custom-call | bytes 8388608 | tf_op jit(solution)/shard_map/transposed/pallas_call | solution.py:111
  39.5 1.8 %collective-permute-done.9.refs_2_ = bf16[256,512]{1,0:T(8,128)(2,1)S(1)} collective-permute-done((bf16[256,512]{1,0:T(8,128)(2,1)S(1)}, bf16[256,512]{1,0:T(8,128)(2,1)S(1)}, u32[]{:S(2)}, u32[]{:S(2)}) %collective-permute-start.9) | collective-permute-done | bytes 262176 | tf_op jit(solution)/shard_map/ppermute | solution.py:42
  41.2 1.2 %middle.1 = (bf16[256,512]{1,0:T(8,128)(2,1)}, bf16[256,512]{1,0:T(8,128)(2,1)S(1)}, bf16[256,512]{1,0:T(8,128)(2,1)S(1)}, bf16[256,512]{1,0:T(8,128)(2,1)S(1)}) custom-call(f32[256,512]{1,0:T(8,128)S(1)} %get-tuple-element.60.refs_0_, bf16[256,512]{1,0:T(8,128)(2,1)S(1)} %collective-permute-done.7.refs_1_, ...), custom_call_target="tpu_custom_call" | custom-call | flops 268435456 | bytes 1310720 | tf_op jit(solution)/shard_map/middle/pallas_call | solution.py:175
  43.4 1.8 %collective-permute-start.10 = (bf16[256,512]{1,0:T(8,128)(2,1)S(1)}, bf16[256,512]{1,0:T(8,128)(2,1)S(1)}, u32[]{:S(2)}, u32[]{:S(2)}) collective-permute-start(bf16[256,512]{1,0:T(8,128)(2,1)S(1)} %get-tuple-element.82.refs_2_), channel_id=1, source_target_pairs={{0,2},{1,3},{2,0},{3,1},{4,5},{5,4},{6,7},{7,6},{8,10},{9,11},{10,... | collective-permute-start | bytes 786440 | tf_op jit(solution)/shard_map/ppermute | solution.py:42
  45.2 1.5 %collective-permute-start.11 = (bf16[256,512]{1,0:T(8,128)(2,1)S(1)}, bf16[256,512]{1,0:T(8,128)(2,1)S(1)}, u32[]{:S(2)}, u32[]{:S(2)}) collective-permute-start(bf16[256,512]{1,0:T(8,128)(2,1)S(1)} %get-tuple-element.82.refs_2_), channel_id=1, source_target_pairs={{0,1},{1,0},{2,3},{3,2},{4,6},{5,7},{6,4},{7,5},{8,9},{9,8},{10,11... | collective-permute-start | bytes 786440 | tf_op jit(solution)/shard_map/ppermute | solution.py:42
  48.8 1.5 %collective-permute-start.14 = (bf16[64,512]{1,0:T(8,128)(2,1)S(1)}, bf16[64,512]{1,0:T(8,128)(2,1)S(1)}, u32[]{:S(2)}, u32[]{:S(2)}) collective-permute-start(bf16[64,512]{1,0:T(8,128)(2,1)S(1)} %get-tuple-element.89), channel_id=1, source_target_pairs={{0,1},{1,0},{2,3},{3,2},{4,6},{5,7},{6,4},{7,5},{8,9},{9,8},{10,11... | collective-permute-start | bytes 196616 | tf_op jit(solution)/shard_map/ppermute | solution.py:42
  50.3 1.7 %collective-permute-done.10.refs_3_ = bf16[256,512]{1,0:T(8,128)(2,1)S(1)} collective-permute-done((bf16[256,512]{1,0:T(8,128)(2,1)S(1)}, bf16[256,512]{1,0:T(8,128)(2,1)S(1)}, u32[]{:S(2)}, u32[]{:S(2)}) %collective-permute-start.10) | collective-permute-done | bytes 262176 | tf_op jit(solution)/shard_map/ppermute | solution.py:42
  52.0 1.6 %collective-permute-done.11.refs_4_ = bf16[256,512]{1,0:T(8,128)(2,1)S(1)} collective-permute-done((bf16[256,512]{1,0:T(8,128)(2,1)S(1)}, bf16[256,512]{1,0:T(8,128)(2,1)S(1)}, u32[]{:S(2)}, u32[]{:S(2)}) %collective-permute-start.11) | collective-permute-done | bytes 262176 | tf_op jit(solution)/shard_map/ppermute | solution.py:42
  53.5 1.7 %collective-permute-start.12 = (bf16[256,512]{1,0:T(8,128)(2,1)S(1)}, bf16[256,512]{1,0:T(8,128)(2,1)S(1)}, u32[]{:S(2)}, u32[]{:S(2)}) collective-permute-start(bf16[256,512]{1,0:T(8,128)(2,1)S(1)} %collective-permute-done.10.refs_3_), channel_id=1, source_target_pairs={{0,1},{1,0},{2,3},{3,2},{4,6},{5,7},{6,4},{7,5},{8,9},{9,8},{10,11... | collective-permute-start | bytes 786440 | tf_op jit(solution)/shard_map/ppermute | solution.py:42
  55.5 3.0 %collective-permute-start.17 = (bf16[64,512]{1,0:T(8,128)(2,1)S(1)}, bf16[64,512]{1,0:T(8,128)(2,1)S(1)}, u32[]{:S(2)}, u32[]{:S(2)}) collective-permute-start(bf16[64,512]{1,0:T(8,128)(2,1)S(1)} %add_convert_fusion.4), channel_id=1, source_target_pairs={{0,16},{4,12},{8,24},{12,4},{16,0},{20,28},{24,8},{28,20},{1,17},{... | collective-permute-start | bytes 196616 | tf_op jit(solution)/shard_map/ppermute | solution.py:32
  58.5 2.3 %collective-permute-done.17 = bf16[64,512]{1,0:T(8,128)(2,1)S(1)} collective-permute-done((bf16[64,512]{1,0:T(8,128)(2,1)S(1)}, bf16[64,512]{1,0:T(8,128)(2,1)S(1)}, u32[]{:S(2)}, u32[]{:S(2)}) %collective-permute-start.17) | collective-permute-done | bytes 65568 | tf_op jit(solution)/shard_map/ppermute | solution.py:32
  61.6 2.9 %collective-permute-start.22 = (bf16[64,512]{1,0:T(8,128)(2,1)S(1)}, bf16[64,512]{1,0:T(8,128)(2,1)S(1)}, u32[]{:S(2)}, u32[]{:S(2)}) collective-permute-start(bf16[64,512]{1,0:T(8,128)(2,1)S(1)} %add_convert_fusion.3), channel_id=1, source_target_pairs={{0,8},{4,20},{8,0},{12,28},{16,24},{20,4},{24,16},{28,12},{1,9},{5... | collective-permute-start | bytes 196616 | tf_op jit(solution)/shard_map/ppermute | solution.py:32
  67.4 1.4 %collective-permute-start.23 = (f32[64,512]{1,0:T(8,128)S(1)}, f32[64,512]{1,0:T(8,128)S(1)}, u32[]{:S(2)}, u32[]{:S(2)}) collective-permute-start(f32[64,512]{1,0:T(8,128)S(1)} %add_multiply_fusion.refs_0_), channel_id=1, source_target_pairs={{0,1},{1,0},{2,3},{3,2},{4,6},{5,7},{6,4},{7,5},{8,9},{9,8},{10,11... | collective-permute-start | bytes 393224 | tf_op jit(solution)/shard_map/ppermute | solution.py:42
  68.7 1.5 %collective-permute-start.24 = (f32[64,512]{1,0:T(8,128)S(1)}, f32[64,512]{1,0:T(8,128)S(1)}, u32[]{:S(2)}, u32[]{:S(2)}) collective-permute-start(f32[64,512]{1,0:T(8,128)S(1)} %add_multiply_fusion.refs_0_), channel_id=1, source_target_pairs={{0,2},{1,3},{2,0},{3,1},{4,5},{5,4},{6,7},{7,6},{8,10},{9,11},{10,... | collective-permute-start | bytes 393224 | tf_op jit(solution)/shard_map/ppermute | solution.py:42
  70.9 2.8 %collective-permute-done.23.refs_1_ = f32[64,512]{1,0:T(8,128)S(1)} collective-permute-done((f32[64,512]{1,0:T(8,128)S(1)}, f32[64,512]{1,0:T(8,128)S(1)}, u32[]{:S(2)}, u32[]{:S(2)}) %collective-permute-start.23) | collective-permute-done | bytes 131104 | tf_op jit(solution)/shard_map/ppermute | solution.py:42
  73.7 3.4 %collective-permute-done.25.refs_3_ = f32[64,512]{1,0:T(8,128)S(1)} collective-permute-done((f32[64,512]{1,0:T(8,128)S(1)}, f32[64,512]{1,0:T(8,128)S(1)}, u32[]{:S(2)}, u32[]{:S(2)}) %collective-permute-start.25) | collective-permute-done | bytes 131104 | tf_op jit(solution)/shard_map/ppermute | solution.py:42
  78.0 2.3 %collective-permute-done.20.refs_3_ = bf16[512,512]{1,0:T(8,128)(2,1)S(1)} collective-permute-done((bf16[512,512]{1,0:T(8,128)(2,1)S(1)}, bf16[512,512]{1,0:T(8,128)(2,1)S(1)}, u32[]{:S(2)}, u32[]{:S(2)}) %collective-permute-start.20) | collective-permute-done | bytes 524320 | tf_op jit(solution)/shard_map/ppermute | solution.py:32
  80.4 2.2 %collective-permute-start.21 = (bf16[256,512]{1,0:T(8,128)(2,1)S(1)}, bf16[256,512]{1,0:T(8,128)(2,1)S(1)}, u32[]{:S(2)}, u32[]{:S(2)}) collective-permute-start(bf16[256,512]{1,0:T(8,128)(2,1)S(1)} %get-tuple-element.86), channel_id=1, source_target_pairs={{0,16},{4,12},{8,24},{12,4},{16,0},{20,28},{24,8},{28,20},{1,17},{... | collective-permute-start | bytes 786440 | tf_op jit(solution)/shard_map/ppermute | solution.py:32
  82.6 1.6 %place_slices.1 = f32[512,512]{1,0:T(8,128)} custom-call(s32[2]{0:T(128)S(1)} %pad_add_fusion.1.place_ref, f32[64,512]{1,0:T(8,128)S(1)} %add_multiply_fusion.refs_0_, f32[64,512]{1,0:T(8,128)S(1)} %collective-permute-done.23.refs_1_, f32[64,512]{1,0:T(8,128)S(1)} %collective-permute-done.24.refs_2_, f32[64,512]{1,0:T(8,128)S(1)} %collective-permute-done.25.refs_3_, ...), custom_call_target="tpu_custom_call" | custom-call | bytes 2097152 | tf_op jit(solution)/shard_map/place_slices/pallas_call | solution.py:236
  84.2 6.3 %collective-permute-done.21.refs_1_ = bf16[256,512]{1,0:T(8,128)(2,1)S(1)} collective-permute-done((bf16[256,512]{1,0:T(8,128)(2,1)S(1)}, bf16[256,512]{1,0:T(8,128)(2,1)S(1)}, u32[]{:S(2)}, u32[]{:S(2)}) %collective-permute-start.21) | collective-permute-done | bytes 262176 | tf_op jit(solution)/shard_map/ppermute | solution.py:32
  (57 shorter events, 13.9 us)
Async XLA Ops:
  0.6 10.2 %collective-permute-start = (bf16[256,512]{1,0:T(8,128)(2,1)}, bf16[256,512]{1,0:T(8,128)(2,1)S(1)}, u32[]{:S(2)}, u32[]{:S(2)}) collective-permute-start(bf16[256,512]{1,0:T(8,128)(2,1)} %refs_1_.1), channel_id=1, source_target_pairs={{0,16},{4,12},{8,24},{12,4},{16,0},{20,28},{24,8},{28,20},{1,17},{... | collective-permute-start | bytes 786440 | tf_op jit(solution)/shard_map/ppermute | solution.py:32
  4.7 13.5 %collective-permute-start.2 = (bf16[256,512]{1,0:T(8,128)(2,1)}, bf16[256,512]{1,0:T(8,128)(2,1)S(1)}, u32[]{:S(2)}, u32[]{:S(2)}) collective-permute-start(bf16[256,512]{1,0:T(8,128)(2,1)} %refs_1_.1), channel_id=1, source_target_pairs={{0,4},{4,0},{8,12},{12,8},{16,20},{20,16},{24,28},{28,24},{1,5},{5... | collective-permute-start | bytes 786440 | tf_op jit(solution)/shard_map/ppermute | solution.py:26
  10.9 7.4 %collective-permute-start.3 = (bf16[256,512]{1,0:T(8,128)(2,1)S(1)}, bf16[256,512]{1,0:T(8,128)(2,1)S(1)}, u32[]{:S(2)}, u32[]{:S(2)}) collective-permute-start(bf16[256,512]{1,0:T(8,128)(2,1)S(1)} %collective-permute-done.refs_3_), channel_id=1, source_target_pairs={{0,4},{4,0},{8,12},{12,8},{16,20},{20,16},{24,28},{28,24},{1,5},{5... | collective-permute-start | bytes 786440 | tf_op jit(solution)/shard_map/ppermute | solution.py:26
  10.9 12.1 %collective-permute-start.1 = (bf16[256,512]{1,0:T(8,128)(2,1)}, bf16[256,512]{1,0:T(8,128)(2,1)S(1)}, u32[]{:S(2)}, u32[]{:S(2)}) collective-permute-start(bf16[256,512]{1,0:T(8,128)(2,1)} %refs_1_.1), channel_id=1, source_target_pairs={{0,8},{4,20},{8,0},{12,28},{16,24},{20,4},{24,16},{28,12},{1,9},{5... | collective-permute-start | bytes 786440 | tf_op jit(solution)/shard_map/ppermute | solution.py:32
  13.3 13.0 %collective-permute-start.5 = (bf16[256,512]{1,0:T(8,128)(2,1)S(1)}, bf16[256,512]{1,0:T(8,128)(2,1)S(1)}, u32[]{:S(2)}, u32[]{:S(2)}) collective-permute-start(bf16[256,512]{1,0:T(8,128)(2,1)S(1)} %collective-permute-done.refs_3_), channel_id=1, source_target_pairs={{0,8},{4,20},{8,0},{12,28},{16,24},{20,4},{24,16},{28,12},{1,9},{5... | collective-permute-start | bytes 786440 | tf_op jit(solution)/shard_map/ppermute | solution.py:32
  13.4 2.2 %copy-start = (bf16[1,1,8,16,128,128]{5,4,3,2,1,0:T(8,128)(2,1)S(1)}, bf16[1,1,8,16,128,128]{5,4,3,2,1,0:T(8,128)(2,1)}, u32[]{:S(2)}) copy-start(bf16[1,1,8,16,128,128]{5,4,3,2,1,0:T(8,128)(2,1)} %param.10) | copy-start | bytes 12582916
  15.6 2.6 %copy-start.2 = (bf16[256,512]{1,0:T(8,128)(2,1)S(1)}, bf16[256,512]{1,0:T(8,128)(2,1)}, u32[]{:S(2)}) copy-start(bf16[256,512]{1,0:T(8,128)(2,1)} %refs_1_.1) | copy-start | bytes 786436
  22.9 4.1 %collective-permute-start.4 = (bf16[256,512]{1,0:T(8,128)(2,1)S(1)}, bf16[256,512]{1,0:T(8,128)(2,1)S(1)}, u32[]{:S(2)}, u32[]{:S(2)}) collective-permute-start(bf16[256,512]{1,0:T(8,128)(2,1)S(1)} %collective-permute-done.1.refs_1_), channel_id=1, source_target_pairs={{0,4},{4,0},{8,12},{12,8},{16,20},{20,16},{24,28},{28,24},{1,5},{5... | collective-permute-start | bytes 786440 | tf_op jit(solution)/shard_map/ppermute | solution.py:26
  26.3 1.5 %collective-permute-start.6 = (bf16[256,512]{1,0:T(8,128)(2,1)S(1)}, bf16[256,512]{1,0:T(8,128)(2,1)S(1)}, u32[]{:S(2)}, u32[]{:S(2)}) collective-permute-start(bf16[256,512]{1,0:T(8,128)(2,1)S(1)} %collective-permute-done.5.refs_2_), channel_id=1, source_target_pairs={{0,4},{4,0},{8,12},{12,8},{16,20},{20,16},{24,28},{28,24},{1,5},{5... | collective-permute-start | bytes 786440 | tf_op jit(solution)/shard_map/ppermute | solution.py:26
  28.3 6.4 %collective-permute-start.8 = (bf16[256,512]{1,0:T(8,128)(2,1)S(1)}, bf16[256,512]{1,0:T(8,128)(2,1)S(1)}, u32[]{:S(2)}, u32[]{:S(2)}) collective-permute-start(bf16[256,512]{1,0:T(8,128)(2,1)S(1)} %get-tuple-element.56), channel_id=1, source_target_pairs={{0,1},{1,0},{2,3},{3,2},{4,6},{5,7},{6,4},{7,5},{8,9},{9,8},{10,11... | collective-permute-start | bytes 786440 | tf_op jit(solution)/shard_map/ppermute | solution.py:42
  30.0 8.2 %collective-permute-start.7 = (bf16[256,512]{1,0:T(8,128)(2,1)S(1)}, bf16[256,512]{1,0:T(8,128)(2,1)S(1)}, u32[]{:S(2)}, u32[]{:S(2)}) collective-permute-start(bf16[256,512]{1,0:T(8,128)(2,1)S(1)} %get-tuple-element.55), channel_id=1, source_target_pairs={{0,1},{1,0},{2,3},{3,2},{4,6},{5,7},{6,4},{7,5},{8,9},{9,8},{10,11... | collective-permute-start | bytes 786440 | tf_op jit(solution)/shard_map/ppermute | solution.py:42
  30.4 10.9 %copy-start.1 = (bf16[512,512]{1,0:T(8,128)(2,1)S(1)}, bf16[512,512]{1,0:T(8,128)(2,1)}, u32[]{:S(2)}) copy-start(bf16[512,512]{1,0:T(8,128)(2,1)} %refs_4_.1) | copy-start | bytes 1572868
  30.4 10.9 %copy-start.3 = (bf16[256,512]{1,0:T(8,128)(2,1)S(1)}, bf16[256,512]{1,0:T(8,128)(2,1)}, u32[]{:S(2)}) copy-start(bf16[256,512]{1,0:T(8,128)(2,1)} %refs_3_.1) | copy-start | bytes 786436
  34.8 6.4 %collective-permute-start.9 = (bf16[256,512]{1,0:T(8,128)(2,1)S(1)}, bf16[256,512]{1,0:T(8,128)(2,1)S(1)}, u32[]{:S(2)}, u32[]{:S(2)}) collective-permute-start(bf16[256,512]{1,0:T(8,128)(2,1)S(1)} %add_convert_fusion.2), channel_id=1, source_target_pairs={{0,2},{1,3},{2,0},{3,1},{4,5},{5,4},{6,7},{7,6},{8,10},{9,11},{10,... | collective-permute-start | bytes 786440 | tf_op jit(solution)/shard_map/ppermute | solution.py:42
  43.3 3.3 %collective-permute-start.13 = (bf16[256,512]{1,0:T(8,128)(2,1)S(1)}, bf16[256,512]{1,0:T(8,128)(2,1)S(1)}, u32[]{:S(2)}, u32[]{:S(2)}) collective-permute-start(bf16[256,512]{1,0:T(8,128)(2,1)S(1)} %get-tuple-element.74), channel_id=1, source_target_pairs={{0,4},{4,0},{8,12},{12,8},{16,20},{20,16},{24,28},{28,24},{1,5},{5... | collective-permute-start | bytes 786440 | tf_op jit(solution)/shard_map/ppermute | solution.py:26
  43.4 8.6 %collective-permute-start.10 = (bf16[256,512]{1,0:T(8,128)(2,1)S(1)}, bf16[256,512]{1,0:T(8,128)(2,1)S(1)}, u32[]{:S(2)}, u32[]{:S(2)}) collective-permute-start(bf16[256,512]{1,0:T(8,128)(2,1)S(1)} %get-tuple-element.82.refs_2_), channel_id=1, source_target_pairs={{0,2},{1,3},{2,0},{3,1},{4,5},{5,4},{6,7},{7,6},{8,10},{9,11},{10,... | collective-permute-start | bytes 786440 | tf_op jit(solution)/shard_map/ppermute | solution.py:42
  45.2 8.3 %collective-permute-start.11 = (bf16[256,512]{1,0:T(8,128)(2,1)S(1)}, bf16[256,512]{1,0:T(8,128)(2,1)S(1)}, u32[]{:S(2)}, u32[]{:S(2)}) collective-permute-start(bf16[256,512]{1,0:T(8,128)(2,1)S(1)} %get-tuple-element.82.refs_2_), channel_id=1, source_target_pairs={{0,1},{1,0},{2,3},{3,2},{4,6},{5,7},{6,4},{7,5},{8,9},{9,8},{10,11... | collective-permute-start | bytes 786440 | tf_op jit(solution)/shard_map/ppermute | solution.py:42
  46.7 8.7 %collective-permute-start.16 = (bf16[64,512]{1,0:T(8,128)(2,1)S(1)}, bf16[64,512]{1,0:T(8,128)(2,1)S(1)}, u32[]{:S(2)}, u32[]{:S(2)}) collective-permute-start(bf16[64,512]{1,0:T(8,128)(2,1)S(1)} %get-tuple-element.90), channel_id=1, source_target_pairs={{0,3},{1,2},{2,1},{3,0},{4,7},{5,6},{6,5},{7,4},{8,11},{9,10},{10,... | collective-permute-start | bytes 196616 | tf_op jit(solution)/shard_map/ppermute | solution.py:42
  47.7 7.8 %collective-permute-start.15 = (bf16[64,512]{1,0:T(8,128)(2,1)S(1)}, bf16[64,512]{1,0:T(8,128)(2,1)S(1)}, u32[]{:S(2)}, u32[]{:S(2)}) collective-permute-start(bf16[64,512]{1,0:T(8,128)(2,1)S(1)} %get-tuple-element.91), channel_id=1, source_target_pairs={{0,2},{1,3},{2,0},{3,1},{4,5},{5,4},{6,7},{7,6},{8,10},{9,11},{10,... | collective-permute-start | bytes 196616 | tf_op jit(solution)/shard_map/ppermute | solution.py:42
  48.8 6.7 %collective-permute-start.14 = (bf16[64,512]{1,0:T(8,128)(2,1)S(1)}, bf16[64,512]{1,0:T(8,128)(2,1)S(1)}, u32[]{:S(2)}, u32[]{:S(2)}) collective-permute-start(bf16[64,512]{1,0:T(8,128)(2,1)S(1)} %get-tuple-element.89), channel_id=1, source_target_pairs={{0,1},{1,0},{2,3},{3,2},{4,6},{5,7},{6,4},{7,5},{8,9},{9,8},{10,11... | collective-permute-start | bytes 196616 | tf_op jit(solution)/shard_map/ppermute | solution.py:42
  53.5 7.2 %collective-permute-start.12 = (bf16[256,512]{1,0:T(8,128)(2,1)S(1)}, bf16[256,512]{1,0:T(8,128)(2,1)S(1)}, u32[]{:S(2)}, u32[]{:S(2)}) collective-permute-start(bf16[256,512]{1,0:T(8,128)(2,1)S(1)} %collective-permute-done.10.refs_3_), channel_id=1, source_target_pairs={{0,1},{1,0},{2,3},{3,2},{4,6},{5,7},{6,4},{7,5},{8,9},{9,8},{10,11... | collective-permute-start | bytes 786440 | tf_op jit(solution)/shard_map/ppermute | solution.py:42
  55.5 5.3 %collective-permute-start.17 = (bf16[64,512]{1,0:T(8,128)(2,1)S(1)}, bf16[64,512]{1,0:T(8,128)(2,1)S(1)}, u32[]{:S(2)}, u32[]{:S(2)}) collective-permute-start(bf16[64,512]{1,0:T(8,128)(2,1)S(1)} %add_convert_fusion.4), channel_id=1, source_target_pairs={{0,16},{4,12},{8,24},{12,4},{16,0},{20,28},{24,8},{28,20},{1,17},{... | collective-permute-start | bytes 196616 | tf_op jit(solution)/shard_map/ppermute | solution.py:32
  61.5 3.7 %collective-permute-start.18 = (bf16[512,512]{1,0:T(8,128)(2,1)S(1)}, bf16[512,512]{1,0:T(8,128)(2,1)S(1)}, u32[]{:S(2)}, u32[]{:S(2)}) collective-permute-start(bf16[512,512]{1,0:T(8,128)(2,1)S(1)} %backward.4), channel_id=1, source_target_pairs={{0,4},{4,0},{8,12},{12,8},{16,20},{20,16},{24,28},{28,24},{1,5},{5... | collective-permute-start | bytes 1572872 | tf_op jit(solution)/shard_map/ppermute | solution.py:26
  61.6 5.7 %collective-permute-start.22 = (bf16[64,512]{1,0:T(8,128)(2,1)S(1)}, bf16[64,512]{1,0:T(8,128)(2,1)S(1)}, u32[]{:S(2)}, u32[]{:S(2)}) collective-permute-start(bf16[64,512]{1,0:T(8,128)(2,1)S(1)} %add_convert_fusion.3), channel_id=1, source_target_pairs={{0,8},{4,20},{8,0},{12,28},{16,24},{20,4},{24,16},{28,12},{1,9},{5... | collective-permute-start | bytes 196616 | tf_op jit(solution)/shard_map/ppermute | solution.py:32
  65.4 14.9 %collective-permute-start.20 = (bf16[512,512]{1,0:T(8,128)(2,1)S(1)}, bf16[512,512]{1,0:T(8,128)(2,1)S(1)}, u32[]{:S(2)}, u32[]{:S(2)}) collective-permute-start(bf16[512,512]{1,0:T(8,128)(2,1)S(1)} %pad_maximum_fusion), channel_id=1, source_target_pairs={{0,8},{4,20},{8,0},{12,28},{16,24},{20,4},{24,16},{28,12},{1,9},{5... | collective-permute-start | bytes 1572872 | tf_op jit(solution)/shard_map/ppermute | solution.py:32
  67.3 10.7 %collective-permute-start.19 = (bf16[512,512]{1,0:T(8,128)(2,1)S(1)}, bf16[512,512]{1,0:T(8,128)(2,1)S(1)}, u32[]{:S(2)}, u32[]{:S(2)}) collective-permute-start(bf16[512,512]{1,0:T(8,128)(2,1)S(1)} %backward.7), channel_id=1, source_target_pairs={{0,4},{4,0},{8,12},{12,8},{16,20},{20,16},{24,28},{28,24},{1,5},{5... | collective-permute-start | bytes 1572872 | tf_op jit(solution)/shard_map/ppermute | solution.py:26
  67.4 6.3 %collective-permute-start.23 = (f32[64,512]{1,0:T(8,128)S(1)}, f32[64,512]{1,0:T(8,128)S(1)}, u32[]{:S(2)}, u32[]{:S(2)}) collective-permute-start(f32[64,512]{1,0:T(8,128)S(1)} %add_multiply_fusion.refs_0_), channel_id=1, source_target_pairs={{0,1},{1,0},{2,3},{3,2},{4,6},{5,7},{6,4},{7,5},{8,9},{9,8},{10,11... | collective-permute-start | bytes 393224 | tf_op jit(solution)/shard_map/ppermute | solution.py:42
  68.7 5.0 %collective-permute-start.24 = (f32[64,512]{1,0:T(8,128)S(1)}, f32[64,512]{1,0:T(8,128)S(1)}, u32[]{:S(2)}, u32[]{:S(2)}) collective-permute-start(f32[64,512]{1,0:T(8,128)S(1)} %add_multiply_fusion.refs_0_), channel_id=1, source_target_pairs={{0,2},{1,3},{2,0},{3,1},{4,5},{5,4},{6,7},{7,6},{8,10},{9,11},{10,... | collective-permute-start | bytes 393224 | tf_op jit(solution)/shard_map/ppermute | solution.py:42
  70.3 6.9 %collective-permute-start.25 = (f32[64,512]{1,0:T(8,128)S(1)}, f32[64,512]{1,0:T(8,128)S(1)}, u32[]{:S(2)}, u32[]{:S(2)}) collective-permute-start(f32[64,512]{1,0:T(8,128)S(1)} %add_multiply_fusion.refs_0_), channel_id=1, source_target_pairs={{0,3},{1,2},{2,1},{3,0},{4,7},{5,6},{6,5},{7,4},{8,11},{9,10},{10,... | collective-permute-start | bytes 393224 | tf_op jit(solution)/shard_map/ppermute | solution.py:42
  77.2 5.5 %collective-permute-start.26 = (f32[256,512]{1,0:T(8,128)S(1)}, f32[256,512]{1,0:T(8,128)S(1)}, u32[]{:S(2)}, u32[]{:S(2)}) collective-permute-start(f32[256,512]{1,0:T(8,128)S(1)} %pad_maximum_fusion.1), channel_id=1, source_target_pairs={{0,4},{4,0},{8,12},{12,8},{16,20},{20,16},{24,28},{28,24},{1,5},{5... | collective-permute-start | bytes 1572872 | tf_op jit(solution)/shard_map/ppermute | solution.py:26
  80.4 10.1 %collective-permute-start.21 = (bf16[256,512]{1,0:T(8,128)(2,1)S(1)}, bf16[256,512]{1,0:T(8,128)(2,1)S(1)}, u32[]{:S(2)}, u32[]{:S(2)}) collective-permute-start(bf16[256,512]{1,0:T(8,128)(2,1)S(1)} %get-tuple-element.86), channel_id=1, source_target_pairs={{0,16},{4,12},{8,24},{12,4},{16,0},{20,28},{24,8},{28,20},{1,17},{... | collective-permute-start | bytes 786440 | tf_op jit(solution)/shard_map/ppermute | solution.py:32

commit v12 on v11

--- a/solution.py
+++ b/solution.py
@@ -372,11 +372,7 @@
 
     grads = [grad]
     for k in range(1, groups):
-        if k == top_bit(k):
-            straight = grads[0]
-        else:
-            straight = after(grads[k - top_bit(k)], grads[top_bit(k)])
-        grads.append(swap_members(straight, top_bit(k)))
+        grads.append(swap_members(grads[k - top_bit(k)], top_bit(k)))
     part = parts[0]
     for k in range(1, groups):
         part = part + swap_members(parts[k].astype(jnp.bfloat16), k, turn=1).astype(jnp.float32)

time: 91.5 us -> 88.8 us (0.970)
  waiting for transfers between devices: 40.2 us -> 36.9 us
    ppermute x12, waiting for transfers between devices: 17.1 us -> 14.9 us  [swap_members(): return lax.ppermute(x, ('dom', 'repl'), pairs)]
    ppermute x7, waiting for transfers between devices: 22.3 us -> 21.2 us  [swap_chips(): lax.ppermute(x, 'dom', [(i, i ^ 2 * between(held, i % 2, bits)) for i in...]
where the time goes in v12:
time: 88.8 us; the launch traced here: 88.6 us
  waiting for transfers between devices  36.9 us (42%)
  starting transfers between devices  32.4 us (36%)
  Pallas kernels  14.1 us (16%)
  local copies, waits for them, and re-layouts  2.93 us (3%)
  other arithmetic  1.31 us (1%)
    ppermute x7, waiting for transfers between devices, swap_chips(): lax.ppermute(x, 'dom', [(i, i ^ 2 * between(held, i % 2, bits)) for i in...  21.2 us
    ppermute x7, starting transfers between devices, swap_chips(): lax.ppermute(x, 'dom', [(i, i ^ 2 * between(held, i % 2, bits)) for i in...  15.8 us
    ppermute x12, starting transfers between devices, swap_members(): return lax.ppermute(x, ('dom', 'repl'), pairs)  15.7 us
    ppermute x12, waiting for transfers between devices, swap_members(): return lax.ppermute(x, ('dom', 'repl'), pairs)  14.9 us
    pallas_call x4, Pallas kernels, forward(): pl.pallas_call(functools.partial(forward_kernel, which=which, base=base,...  2.82 us
    pallas_call x4, Pallas kernels, backward(): pl.pallas_call(functools.partial(backward_kernel, side=side, count=count,...  2.81 us
    pallas_call x1, Pallas kernels, densify(): pl.pallas_call(functools.partial(densify_kernel, col_tiles=col_tiles), ou...  2.69 us
    unnamed x8, local copies, waits for them, and re-layouts  2.2 us
  transfers between devices with their start and end apart: 27, of which 15 were waited for; matrix products, arithmetic and copies ran while one was open for 2% of the time, Pallas kernels for 11%

profile of v12, /device:TPU:0, one launch (start us, length us, event | category | flops | bytes accessed | tf_op | source)
XLA Modules:
  0.0 88.6 jit_solution(11051207982749200862)
XLA Ops:
  0.6 4.1 %collective-permute-start = (bf16[256,512]{1,0:T(8,128)(2,1)}, bf16[256,512]{1,0:T(8,128)(2,1)S(1)}, u32[]{:S(2)}, u32[]{:S(2)}) collective-permute-start(bf16[256,512]{1,0:T(8,128)(2,1)} %refs_1_.1), channel_id=1, source_target_pairs={{0,16},{4,12},{8,24},{12,4},{16,0},{20,28},{24,8},{28,20},{1,17},{... | collective-permute-start | bytes 786440 | tf_op jit(solution)/shard_map/ppermute | solution.py:32
  6.3 4.6 %collective-permute-done.refs_3_ = bf16[256,512]{1,0:T(8,128)(2,1)S(1)} collective-permute-done((bf16[256,512]{1,0:T(8,128)(2,1)}, bf16[256,512]{1,0:T(8,128)(2,1)S(1)}, u32[]{:S(2)}, u32[]{:S(2)}) %collective-permute-start) | collective-permute-done | bytes 262176 | tf_op jit(solution)/shard_map/ppermute | solution.py:32
  10.9 2.4 %collective-permute-start.1 = (bf16[256,512]{1,0:T(8,128)(2,1)}, bf16[256,512]{1,0:T(8,128)(2,1)S(1)}, u32[]{:S(2)}, u32[]{:S(2)}) collective-permute-start(bf16[256,512]{1,0:T(8,128)(2,1)} %refs_1_.1), channel_id=1, source_target_pairs={{0,8},{4,20},{8,0},{12,28},{16,24},{20,4},{24,16},{28,12},{1,9},{5... | collective-permute-start | bytes 786440 | tf_op jit(solution)/shard_map/ppermute | solution.py:32
  13.4 2.2 %copy-done = bf16[1,1,8,16,128,128]{5,4,3,2,1,0:T(8,128)(2,1)S(1)} copy-done((bf16[1,1,8,16,128,128]{5,4,3,2,1,0:T(8,128)(2,1)S(1)}, bf16[1,1,8,16,128,128]{5,4,3,2,1,0:T(8,128)(2,1)}, u32[]{:S(2)}) %copy-start) | copy-done | bytes 4194328
  15.6 2.7 %densify.1.refs_0_.a_ref = bf16[8,1024,256]{2,1,0:T(8,128)(2,1)S(1)} custom-call(s32[8,17]{1,0:T(8,128)S(1)} %pad_add_fusion.spots_ref, s32[2]{0:T(128)S(1)} %pad_add_fusion.1.place_ref, bf16[8,16,128,128]{3,2,1,0:T(8,128)(2,1)S(1)} %bitcast.26), custom_call_target="tpu_custom_call" | custom-call | flops 2097152 | bytes 16777216 | tf_op jit(solution)/shard_map/densify/pallas_call | solution.py:86
  18.3 1.2 %forward.4 = (f32[256,512]{1,0:T(8,128)S(1)}, f32[256,512]{1,0:T(8,128)S(1)}, f32[256,512]{1,0:T(8,128)S(1)}, f32[256,512]{1,0:T(8,128)S(1)}) custom-call(bf16[8,1024,256]{2,1,0:T(8,128)(2,1)S(1)} %densify.1.refs_0_.a_ref, bf16[256,512]{1,0:T(8,128)(2,1)S(1)} %copy-done.2, bf16[256,512]{1,0:T(8,128)(2,1)S(1)} %collective-permute-done.2.refs_2_, ...), custom_call_target="tpu_custom_call" | custom-call | flops 1073741824 | bytes 4194304 | tf_op jit(solution)/shard_map/forward/pallas_call | solution.py:140
  19.6 3.3 %collective-permute-done.1.refs_1_ = bf16[256,512]{1,0:T(8,128)(2,1)S(1)} collective-permute-done((bf16[256,512]{1,0:T(8,128)(2,1)}, bf16[256,512]{1,0:T(8,128)(2,1)S(1)}, u32[]{:S(2)}, u32[]{:S(2)}) %collective-permute-start.1) | collective-permute-done | bytes 262176 | tf_op jit(solution)/shard_map/ppermute | solution.py:32
  22.9 3.4 %collective-permute-done.5.refs_2_ = bf16[256,512]{1,0:T(8,128)(2,1)S(1)} collective-permute-done((bf16[256,512]{1,0:T(8,128)(2,1)S(1)}, bf16[256,512]{1,0:T(8,128)(2,1)S(1)}, u32[]{:S(2)}, u32[]{:S(2)}) %collective-permute-start.5) | collective-permute-done | bytes 262176 | tf_op jit(solution)/shard_map/ppermute | solution.py:32
  28.3 1.7 %collective-permute-start.8 = (bf16[256,512]{1,0:T(8,128)(2,1)S(1)}, bf16[256,512]{1,0:T(8,128)(2,1)S(1)}, u32[]{:S(2)}, u32[]{:S(2)}) collective-permute-start(bf16[256,512]{1,0:T(8,128)(2,1)S(1)} %get-tuple-element.55), channel_id=1, source_target_pairs={{0,1},{1,0},{2,3},{3,2},{4,6},{5,7},{6,4},{7,5},{8,9},{9,8},{10,11... | collective-permute-start | bytes 786440 | tf_op jit(solution)/shard_map/ppermute | solution.py:42
  30.8 3.9 %collective-permute-done.8 = bf16[256,512]{1,0:T(8,128)(2,1)S(1)} collective-permute-done((bf16[256,512]{1,0:T(8,128)(2,1)S(1)}, bf16[256,512]{1,0:T(8,128)(2,1)S(1)}, u32[]{:S(2)}, u32[]{:S(2)}) %collective-permute-start.8) | collective-permute-done | bytes 262176 | tf_op jit(solution)/shard_map/ppermute | solution.py:42
  34.8 1.8 %collective-permute-start.9 = (bf16[256,512]{1,0:T(8,128)(2,1)S(1)}, bf16[256,512]{1,0:T(8,128)(2,1)S(1)}, u32[]{:S(2)}, u32[]{:S(2)}) collective-permute-start(bf16[256,512]{1,0:T(8,128)(2,1)S(1)} %add_convert_fusion.2), channel_id=1, source_target_pairs={{0,2},{1,3},{2,0},{3,1},{4,5},{5,4},{6,7},{7,6},{8,10},{9,11},{10,... | collective-permute-start | bytes 786440 | tf_op jit(solution)/shard_map/ppermute | solution.py:42
  36.6 1.7 %collective-permute-done.7.refs_1_ = bf16[256,512]{1,0:T(8,128)(2,1)S(1)} collective-permute-done((bf16[256,512]{1,0:T(8,128)(2,1)S(1)}, bf16[256,512]{1,0:T(8,128)(2,1)S(1)}, u32[]{:S(2)}, u32[]{:S(2)}) %collective-permute-start.7) | collective-permute-done | bytes 262176 | tf_op jit(solution)/shard_map/ppermute | solution.py:42
  38.2 1.2 %transposed.1 = (bf16[2,256,1024]{2,1,0:T(8,128)(2,1)S(1)}, bf16[2,256,1024]{2,1,0:T(8,128)(2,1)S(1)}, bf16[2,256,1024]{2,1,0:T(8,128)(2,1)S(1)}, bf16[2,256,1024]{2,1,0:T(8,128)(2,1)S(1)}) custom-call(bf16[8,1024,256]{2,1,0:T(8,128)(2,1)S(1)} %densify.1.refs_0_.a_ref), custom_call_target="tpu_custom_call" | custom-call | bytes 8388608 | tf_op jit(solution)/shard_map/transposed/pallas_call | solution.py:111
  39.5 1.8 %collective-permute-done.9.refs_2_ = bf16[256,512]{1,0:T(8,128)(2,1)S(1)} collective-permute-done((bf16[256,512]{1,0:T(8,128)(2,1)S(1)}, bf16[256,512]{1,0:T(8,128)(2,1)S(1)}, u32[]{:S(2)}, u32[]{:S(2)}) %collective-permute-start.9) | collective-permute-done | bytes 262176 | tf_op jit(solution)/shard_map/ppermute | solution.py:42
  41.2 1.2 %middle.1 = (bf16[256,512]{1,0:T(8,128)(2,1)}, bf16[256,512]{1,0:T(8,128)(2,1)S(1)}, bf16[256,512]{1,0:T(8,128)(2,1)S(1)}, bf16[256,512]{1,0:T(8,128)(2,1)S(1)}) custom-call(f32[256,512]{1,0:T(8,128)S(1)} %get-tuple-element.59.refs_0_, bf16[256,512]{1,0:T(8,128)(2,1)S(1)} %collective-permute-done.7.refs_1_, ...), custom_call_target="tpu_custom_call" | custom-call | flops 268435456 | bytes 1310720 | tf_op jit(solution)/shard_map/middle/pallas_call | solution.py:175
  42.4 0.9 %weight_part.1 = (f32[64,512]{1,0:T(8,128)S(1)}, f32[64,512]{1,0:T(8,128)S(1)}, f32[64,512]{1,0:T(8,128)S(1)}, f32[64,512]{1,0:T(8,128)S(1)}, bf16[256,512]{1,0:T(8,128)(2,1)S(1)}) custom-call(s32[2]{0:T(128)S(1)} %pad_add_fusion.1.place_ref, bf16[256,512]{1,0:T(8,128)(2,1)S(1)} %get-tuple-element.69.agg_ref, bf16[256,512]{1,0:T(8,128)(2,1)S(1)} %get-tuple-element.70.pre_grad_ref), custom_call_target="tpu_custom_call" | custom-call | flops 134217728 | bytes 1572864 | tf_op jit(solution)/shard_map/weight_part/pallas_call | solution.py:208
  43.4 1.8 %collective-permute-start.10 = (bf16[256,512]{1,0:T(8,128)(2,1)S(1)}, bf16[256,512]{1,0:T(8,128)(2,1)S(1)}, u32[]{:S(2)}, u32[]{:S(2)}) collective-permute-start(bf16[256,512]{1,0:T(8,128)(2,1)S(1)} %get-tuple-element.80.refs_2_), channel_id=1, source_target_pairs={{0,2},{1,3},{2,0},{3,1},{4,5},{5,4},{6,7},{7,6},{8,10},{9,11},{10,... | collective-permute-start | bytes 786440 | tf_op jit(solution)/shard_map/ppermute | solution.py:42
  45.2 2.4 %collective-permute-start.16 = (bf16[64,512]{1,0:T(8,128)(2,1)S(1)}, bf16[64,512]{1,0:T(8,128)(2,1)S(1)}, u32[]{:S(2)}, u32[]{:S(2)}) collective-permute-start(bf16[64,512]{1,0:T(8,128)(2,1)S(1)} %get-tuple-element.88), channel_id=1, source_target_pairs={{0,3},{1,2},{2,1},{3,0},{4,7},{5,6},{6,5},{7,4},{8,11},{9,10},{10,... | collective-permute-start | bytes 196616 | tf_op jit(solution)/shard_map/ppermute | solution.py:42
  48.8 1.5 %collective-permute-start.11 = (bf16[256,512]{1,0:T(8,128)(2,1)S(1)}, bf16[256,512]{1,0:T(8,128)(2,1)S(1)}, u32[]{:S(2)}, u32[]{:S(2)}) collective-permute-start(bf16[256,512]{1,0:T(8,128)(2,1)S(1)} %get-tuple-element.80.refs_2_), channel_id=1, source_target_pairs={{0,1},{1,0},{2,3},{3,2},{4,6},{5,7},{6,4},{7,5},{8,9},{9,8},{10,11... | collective-permute-start | bytes 786440 | tf_op jit(solution)/shard_map/ppermute | solution.py:42
  51.1 1.5 %collective-permute-start.12 = (bf16[256,512]{1,0:T(8,128)(2,1)S(1)}, bf16[256,512]{1,0:T(8,128)(2,1)S(1)}, u32[]{:S(2)}, u32[]{:S(2)}) collective-permute-start(bf16[256,512]{1,0:T(8,128)(2,1)S(1)} %collective-permute-done.10.refs_3_), channel_id=1, source_target_pairs={{0,1},{1,0},{2,3},{3,2},{4,6},{5,7},{6,4},{7,5},{8,9},{9,8},{10,11... | collective-permute-start | bytes 786440 | tf_op jit(solution)/shard_map/ppermute | solution.py:42
  53.4 3.0 %collective-permute-start.17 = (bf16[64,512]{1,0:T(8,128)(2,1)S(1)}, bf16[64,512]{1,0:T(8,128)(2,1)S(1)}, u32[]{:S(2)}, u32[]{:S(2)}) collective-permute-start(bf16[64,512]{1,0:T(8,128)(2,1)S(1)} %add_convert_fusion.4), channel_id=1, source_target_pairs={{0,16},{4,12},{8,24},{12,4},{16,0},{20,28},{24,8},{28,20},{1,17},{... | collective-permute-start | bytes 196616 | tf_op jit(solution)/shard_map/ppermute | solution.py:32
  56.3 2.3 %collective-permute-done.17 = bf16[64,512]{1,0:T(8,128)(2,1)S(1)} collective-permute-done((bf16[64,512]{1,0:T(8,128)(2,1)S(1)}, bf16[64,512]{1,0:T(8,128)(2,1)S(1)}, u32[]{:S(2)}, u32[]{:S(2)}) %collective-permute-start.17) | collective-permute-done | bytes 65568 | tf_op jit(solution)/shard_map/ppermute | solution.py:32
  59.5 2.2 %collective-permute-start.22 = (bf16[64,512]{1,0:T(8,128)(2,1)S(1)}, bf16[64,512]{1,0:T(8,128)(2,1)S(1)}, u32[]{:S(2)}, u32[]{:S(2)}) collective-permute-start(bf16[64,512]{1,0:T(8,128)(2,1)S(1)} %add_convert_fusion.3), channel_id=1, source_target_pairs={{0,8},{4,20},{8,0},{12,28},{16,24},{20,4},{24,16},{28,12},{1,9},{5... | collective-permute-start | bytes 196616 | tf_op jit(solution)/shard_map/ppermute | solution.py:32
  62.7 1.1 %collective-permute-start.20 = (bf16[512,512]{1,0:T(8,128)(2,1)S(1)}, bf16[512,512]{1,0:T(8,128)(2,1)S(1)}, u32[]{:S(2)}, u32[]{:S(2)}) collective-permute-start(bf16[512,512]{1,0:T(8,128)(2,1)S(1)} %pad_maximum_fusion), channel_id=1, source_target_pairs={{0,8},{4,20},{8,0},{12,28},{16,24},{20,4},{24,16},{28,12},{1,9},{5... | collective-permute-start | bytes 1572872 | tf_op jit(solution)/shard_map/ppermute | solution.py:32
  65.1 1.1 %collective-permute-start.23 = (f32[64,512]{1,0:T(8,128)S(1)}, f32[64,512]{1,0:T(8,128)S(1)}, u32[]{:S(2)}, u32[]{:S(2)}) collective-permute-start(f32[64,512]{1,0:T(8,128)S(1)} %add_multiply_fusion.refs_0_), channel_id=1, source_target_pairs={{0,1},{1,0},{2,3},{3,2},{4,6},{5,7},{6,4},{7,5},{8,9},{9,8},{10,11... | collective-permute-start | bytes 393224 | tf_op jit(solution)/shard_map/ppermute | solution.py:42
  66.3 2.1 %collective-permute-start.24 = (f32[64,512]{1,0:T(8,128)S(1)}, f32[64,512]{1,0:T(8,128)S(1)}, u32[]{:S(2)}, u32[]{:S(2)}) collective-permute-start(f32[64,512]{1,0:T(8,128)S(1)} %add_multiply_fusion.refs_0_), channel_id=1, source_target_pairs={{0,2},{1,3},{2,0},{3,1},{4,5},{5,4},{6,7},{7,6},{8,10},{9,11},{10,... | collective-permute-start | bytes 393224 | tf_op jit(solution)/shard_map/ppermute | solution.py:42
  68.7 2.5 %collective-permute-done.23.refs_1_ = f32[64,512]{1,0:T(8,128)S(1)} collective-permute-done((f32[64,512]{1,0:T(8,128)S(1)}, f32[64,512]{1,0:T(8,128)S(1)}, u32[]{:S(2)}, u32[]{:S(2)}) %collective-permute-start.23) | collective-permute-done | bytes 131104 | tf_op jit(solution)/shard_map/ppermute | solution.py:42
  71.3 3.4 %collective-permute-done.25.refs_3_ = f32[64,512]{1,0:T(8,128)S(1)} collective-permute-done((f32[64,512]{1,0:T(8,128)S(1)}, f32[64,512]{1,0:T(8,128)S(1)}, u32[]{:S(2)}, u32[]{:S(2)}) %collective-permute-start.25) | collective-permute-done | bytes 131104 | tf_op jit(solution)/shard_map/ppermute | solution.py:42
  75.5 2.0 %collective-permute-done.20.refs_3_ = bf16[512,512]{1,0:T(8,128)(2,1)S(1)} collective-permute-done((bf16[512,512]{1,0:T(8,128)(2,1)S(1)}, bf16[512,512]{1,0:T(8,128)(2,1)S(1)}, u32[]{:S(2)}, u32[]{:S(2)}) %collective-permute-start.20) | collective-permute-done | bytes 524320 | tf_op jit(solution)/shard_map/ppermute | solution.py:32
  77.7 2.9 %collective-permute-start.21 = (bf16[256,512]{1,0:T(8,128)(2,1)S(1)}, bf16[256,512]{1,0:T(8,128)(2,1)S(1)}, u32[]{:S(2)}, u32[]{:S(2)}) collective-permute-start(bf16[256,512]{1,0:T(8,128)(2,1)S(1)} %get-tuple-element.84), channel_id=1, source_target_pairs={{0,16},{4,12},{8,24},{12,4},{16,0},{20,28},{24,8},{28,20},{1,17},{... | collective-permute-start | bytes 786440 | tf_op jit(solution)/shard_map/ppermute | solution.py:32
  80.6 1.6 %place_slices.1 = f32[512,512]{1,0:T(8,128)} custom-call(s32[2]{0:T(128)S(1)} %pad_add_fusion.1.place_ref, f32[64,512]{1,0:T(8,128)S(1)} %add_multiply_fusion.refs_0_, f32[64,512]{1,0:T(8,128)S(1)} %collective-permute-done.23.refs_1_, f32[64,512]{1,0:T(8,128)S(1)} %collective-permute-done.24.refs_2_, f32[64,512]{1,0:T(8,128)S(1)} %collective-permute-done.25.refs_3_, ...), custom_call_target="tpu_custom_call" | custom-call | bytes 2097152 | tf_op jit(solution)/shard_map/place_slices/pallas_call | solution.py:236
  82.2 5.6 %collective-permute-done.21.refs_1_ = bf16[256,512]{1,0:T(8,128)(2,1)S(1)} collective-permute-done((bf16[256,512]{1,0:T(8,128)(2,1)S(1)}, bf16[256,512]{1,0:T(8,128)(2,1)S(1)}, u32[]{:S(2)}, u32[]{:S(2)}) %collective-permute-start.21) | collective-permute-done | bytes 262176 | tf_op jit(solution)/shard_map/ppermute | solution.py:32
  (57 shorter events, 12.7 us)
Async XLA Ops:
  0.6 10.2 %collective-permute-start = (bf16[256,512]{1,0:T(8,128)(2,1)}, bf16[256,512]{1,0:T(8,128)(2,1)S(1)}, u32[]{:S(2)}, u32[]{:S(2)}) collective-permute-start(bf16[256,512]{1,0:T(8,128)(2,1)} %refs_1_.1), channel_id=1, source_target_pairs={{0,16},{4,12},{8,24},{12,4},{16,0},{20,28},{24,8},{28,20},{1,17},{... | collective-permute-start | bytes 786440 | tf_op jit(solution)/shard_map/ppermute | solution.py:32
  4.7 13.6 %collective-permute-start.2 = (bf16[256,512]{1,0:T(8,128)(2,1)}, bf16[256,512]{1,0:T(8,128)(2,1)S(1)}, u32[]{:S(2)}, u32[]{:S(2)}) collective-permute-start(bf16[256,512]{1,0:T(8,128)(2,1)} %refs_1_.1), channel_id=1, source_target_pairs={{0,4},{4,0},{8,12},{12,8},{16,20},{20,16},{24,28},{28,24},{1,5},{5... | collective-permute-start | bytes 786440 | tf_op jit(solution)/shard_map/ppermute | solution.py:26
  10.9 7.5 %collective-permute-start.3 = (bf16[256,512]{1,0:T(8,128)(2,1)S(1)}, bf16[256,512]{1,0:T(8,128)(2,1)S(1)}, u32[]{:S(2)}, u32[]{:S(2)}) collective-permute-start(bf16[256,512]{1,0:T(8,128)(2,1)S(1)} %collective-permute-done.refs_3_), channel_id=1, source_target_pairs={{0,4},{4,0},{8,12},{12,8},{16,20},{20,16},{24,28},{28,24},{1,5},{5... | collective-permute-start | bytes 786440 | tf_op jit(solution)/shard_map/ppermute | solution.py:26
  10.9 12.1 %collective-permute-start.1 = (bf16[256,512]{1,0:T(8,128)(2,1)}, bf16[256,512]{1,0:T(8,128)(2,1)S(1)}, u32[]{:S(2)}, u32[]{:S(2)}) collective-permute-start(bf16[256,512]{1,0:T(8,128)(2,1)} %refs_1_.1), channel_id=1, source_target_pairs={{0,8},{4,20},{8,0},{12,28},{16,24},{20,4},{24,16},{28,12},{1,9},{5... | collective-permute-start | bytes 786440 | tf_op jit(solution)/shard_map/ppermute | solution.py:32
  13.3 13.0 %collective-permute-start.5 = (bf16[256,512]{1,0:T(8,128)(2,1)S(1)}, bf16[256,512]{1,0:T(8,128)(2,1)S(1)}, u32[]{:S(2)}, u32[]{:S(2)}) collective-permute-start(bf16[256,512]{1,0:T(8,128)(2,1)S(1)} %collective-permute-done.refs_3_), channel_id=1, source_target_pairs={{0,8},{4,20},{8,0},{12,28},{16,24},{20,4},{24,16},{28,12},{1,9},{5... | collective-permute-start | bytes 786440 | tf_op jit(solution)/shard_map/ppermute | solution.py:32
  13.4 2.2 %copy-start = (bf16[1,1,8,16,128,128]{5,4,3,2,1,0:T(8,128)(2,1)S(1)}, bf16[1,1,8,16,128,128]{5,4,3,2,1,0:T(8,128)(2,1)}, u32[]{:S(2)}) copy-start(bf16[1,1,8,16,128,128]{5,4,3,2,1,0:T(8,128)(2,1)} %param.10) | copy-start | bytes 12582916
  15.6 2.7 %copy-start.2 = (bf16[256,512]{1,0:T(8,128)(2,1)S(1)}, bf16[256,512]{1,0:T(8,128)(2,1)}, u32[]{:S(2)}) copy-start(bf16[256,512]{1,0:T(8,128)(2,1)} %refs_1_.1) | copy-start | bytes 786436
  22.9 4.1 %collective-permute-start.4 = (bf16[256,512]{1,0:T(8,128)(2,1)S(1)}, bf16[256,512]{1,0:T(8,128)(2,1)S(1)}, u32[]{:S(2)}, u32[]{:S(2)}) collective-permute-start(bf16[256,512]{1,0:T(8,128)(2,1)S(1)} %collective-permute-done.1.refs_1_), channel_id=1, source_target_pairs={{0,4},{4,0},{8,12},{12,8},{16,20},{20,16},{24,28},{28,24},{1,5},{5... | collective-permute-start | bytes 786440 | tf_op jit(solution)/shard_map/ppermute | solution.py:26
  26.3 1.5 %collective-permute-start.6 = (bf16[256,512]{1,0:T(8,128)(2,1)S(1)}, bf16[256,512]{1,0:T(8,128)(2,1)S(1)}, u32[]{:S(2)}, u32[]{:S(2)}) collective-permute-start(bf16[256,512]{1,0:T(8,128)(2,1)S(1)} %collective-permute-done.5.refs_2_), channel_id=1, source_target_pairs={{0,4},{4,0},{8,12},{12,8},{16,20},{20,16},{24,28},{28,24},{1,5},{5... | collective-permute-start | bytes 786440 | tf_op jit(solution)/shard_map/ppermute | solution.py:26
  28.3 6.4 %collective-permute-start.8 = (bf16[256,512]{1,0:T(8,128)(2,1)S(1)}, bf16[256,512]{1,0:T(8,128)(2,1)S(1)}, u32[]{:S(2)}, u32[]{:S(2)}) collective-permute-start(bf16[256,512]{1,0:T(8,128)(2,1)S(1)} %get-tuple-element.55), channel_id=1, source_target_pairs={{0,1},{1,0},{2,3},{3,2},{4,6},{5,7},{6,4},{7,5},{8,9},{9,8},{10,11... | collective-permute-start | bytes 786440 | tf_op jit(solution)/shard_map/ppermute | solution.py:42
  30.0 8.2 %collective-permute-start.7 = (bf16[256,512]{1,0:T(8,128)(2,1)S(1)}, bf16[256,512]{1,0:T(8,128)(2,1)S(1)}, u32[]{:S(2)}, u32[]{:S(2)}) collective-permute-start(bf16[256,512]{1,0:T(8,128)(2,1)S(1)} %get-tuple-element.54), channel_id=1, source_target_pairs={{0,1},{1,0},{2,3},{3,2},{4,6},{5,7},{6,4},{7,5},{8,9},{9,8},{10,11... | collective-permute-start | bytes 786440 | tf_op jit(solution)/shard_map/ppermute | solution.py:42
  30.4 10.9 %copy-start.1 = (bf16[512,512]{1,0:T(8,128)(2,1)S(1)}, bf16[512,512]{1,0:T(8,128)(2,1)}, u32[]{:S(2)}) copy-start(bf16[512,512]{1,0:T(8,128)(2,1)} %refs_4_.1) | copy-start | bytes 1572868
  30.4 10.9 %copy-start.3 = (bf16[256,512]{1,0:T(8,128)(2,1)S(1)}, bf16[256,512]{1,0:T(8,128)(2,1)}, u32[]{:S(2)}) copy-start(bf16[256,512]{1,0:T(8,128)(2,1)} %refs_3_.1) | copy-start | bytes 786436
  34.8 6.4 %collective-permute-start.9 = (bf16[256,512]{1,0:T(8,128)(2,1)S(1)}, bf16[256,512]{1,0:T(8,128)(2,1)S(1)}, u32[]{:S(2)}, u32[]{:S(2)}) collective-permute-start(bf16[256,512]{1,0:T(8,128)(2,1)S(1)} %add_convert_fusion.2), channel_id=1, source_target_pairs={{0,2},{1,3},{2,0},{3,1},{4,5},{5,4},{6,7},{7,6},{8,10},{9,11},{10,... | collective-permute-start | bytes 786440 | tf_op jit(solution)/shard_map/ppermute | solution.py:42
  43.3 1.9 %collective-permute-start.13 = (bf16[256,512]{1,0:T(8,128)(2,1)S(1)}, bf16[256,512]{1,0:T(8,128)(2,1)S(1)}, u32[]{:S(2)}, u32[]{:S(2)}) collective-permute-start(bf16[256,512]{1,0:T(8,128)(2,1)S(1)} %get-tuple-element.72), channel_id=1, source_target_pairs={{0,4},{4,0},{8,12},{12,8},{16,20},{20,16},{24,28},{28,24},{1,5},{5... | collective-permute-start | bytes 786440 | tf_op jit(solution)/shard_map/ppermute | solution.py:26
  43.4 7.7 %collective-permute-start.10 = (bf16[256,512]{1,0:T(8,128)(2,1)S(1)}, bf16[256,512]{1,0:T(8,128)(2,1)S(1)}, u32[]{:S(2)}, u32[]{:S(2)}) collective-permute-start(bf16[256,512]{1,0:T(8,128)(2,1)S(1)} %get-tuple-element.80.refs_2_), channel_id=1, source_target_pairs={{0,2},{1,3},{2,0},{3,1},{4,5},{5,4},{6,7},{7,6},{8,10},{9,11},{10,... | collective-permute-start | bytes 786440 | tf_op jit(solution)/shard_map/ppermute | solution.py:42
  45.2 7.3 %collective-permute-start.16 = (bf16[64,512]{1,0:T(8,128)(2,1)S(1)}, bf16[64,512]{1,0:T(8,128)(2,1)S(1)}, u32[]{:S(2)}, u32[]{:S(2)}) collective-permute-start(bf16[64,512]{1,0:T(8,128)(2,1)S(1)} %get-tuple-element.88), channel_id=1, source_target_pairs={{0,3},{1,2},{2,1},{3,0},{4,7},{5,6},{6,5},{7,4},{8,11},{9,10},{10,... | collective-permute-start | bytes 196616 | tf_op jit(solution)/shard_map/ppermute | solution.py:42
  47.7 5.7 %collective-permute-start.15 = (bf16[64,512]{1,0:T(8,128)(2,1)S(1)}, bf16[64,512]{1,0:T(8,128)(2,1)S(1)}, u32[]{:S(2)}, u32[]{:S(2)}) collective-permute-start(bf16[64,512]{1,0:T(8,128)(2,1)S(1)} %get-tuple-element.89), channel_id=1, source_target_pairs={{0,2},{1,3},{2,0},{3,1},{4,5},{5,4},{6,7},{7,6},{8,10},{9,11},{10,... | collective-permute-start | bytes 196616 | tf_op jit(solution)/shard_map/ppermute | solution.py:42
  48.2 5.1 %collective-permute-start.14 = (bf16[64,512]{1,0:T(8,128)(2,1)S(1)}, bf16[64,512]{1,0:T(8,128)(2,1)S(1)}, u32[]{:S(2)}, u32[]{:S(2)}) collective-permute-start(bf16[64,512]{1,0:T(8,128)(2,1)S(1)} %get-tuple-element.87), channel_id=1, source_target_pairs={{0,1},{1,0},{2,3},{3,2},{4,6},{5,7},{6,4},{7,5},{8,9},{9,8},{10,11... | collective-permute-start | bytes 196616 | tf_op jit(solution)/shard_map/ppermute | solution.py:42
  48.8 9.8 %collective-permute-start.11 = (bf16[256,512]{1,0:T(8,128)(2,1)S(1)}, bf16[256,512]{1,0:T(8,128)(2,1)S(1)}, u32[]{:S(2)}, u32[]{:S(2)}) collective-permute-start(bf16[256,512]{1,0:T(8,128)(2,1)S(1)} %get-tuple-element.80.refs_2_), channel_id=1, source_target_pairs={{0,1},{1,0},{2,3},{3,2},{4,6},{5,7},{6,4},{7,5},{8,9},{9,8},{10,11... | collective-permute-start | bytes 786440 | tf_op jit(solution)/shard_map/ppermute | solution.py:42
  51.1 7.5 %collective-permute-start.12 = (bf16[256,512]{1,0:T(8,128)(2,1)S(1)}, bf16[256,512]{1,0:T(8,128)(2,1)S(1)}, u32[]{:S(2)}, u32[]{:S(2)}) collective-permute-start(bf16[256,512]{1,0:T(8,128)(2,1)S(1)} %collective-permute-done.10.refs_3_), channel_id=1, source_target_pairs={{0,1},{1,0},{2,3},{3,2},{4,6},{5,7},{6,4},{7,5},{8,9},{9,8},{10,11... | collective-permute-start | bytes 786440 | tf_op jit(solution)/shard_map/ppermute | solution.py:42
  53.4 5.2 %collective-permute-start.17 = (bf16[64,512]{1,0:T(8,128)(2,1)S(1)}, bf16[64,512]{1,0:T(8,128)(2,1)S(1)}, u32[]{:S(2)}, u32[]{:S(2)}) collective-permute-start(bf16[64,512]{1,0:T(8,128)(2,1)S(1)} %add_convert_fusion.4), channel_id=1, source_target_pairs={{0,16},{4,12},{8,24},{12,4},{16,0},{20,28},{24,8},{28,20},{1,17},{... | collective-permute-start | bytes 196616 | tf_op jit(solution)/shard_map/ppermute | solution.py:32
  59.3 3.1 %collective-permute-start.18 = (bf16[512,512]{1,0:T(8,128)(2,1)S(1)}, bf16[512,512]{1,0:T(8,128)(2,1)S(1)}, u32[]{:S(2)}, u32[]{:S(2)}) collective-permute-start(bf16[512,512]{1,0:T(8,128)(2,1)S(1)} %backward.4), channel_id=1, source_target_pairs={{0,4},{4,0},{8,12},{12,8},{16,20},{20,16},{24,28},{28,24},{1,5},{5... | collective-permute-start | bytes 1572872 | tf_op jit(solution)/shard_map/ppermute | solution.py:26
  59.5 5.6 %collective-permute-start.22 = (bf16[64,512]{1,0:T(8,128)(2,1)S(1)}, bf16[64,512]{1,0:T(8,128)(2,1)S(1)}, u32[]{:S(2)}, u32[]{:S(2)}) collective-permute-start(bf16[64,512]{1,0:T(8,128)(2,1)S(1)} %add_convert_fusion.3), channel_id=1, source_target_pairs={{0,8},{4,20},{8,0},{12,28},{16,24},{20,4},{24,16},{28,12},{1,9},{5... | collective-permute-start | bytes 196616 | tf_op jit(solution)/shard_map/ppermute | solution.py:32
  62.7 14.9 %collective-permute-start.20 = (bf16[512,512]{1,0:T(8,128)(2,1)S(1)}, bf16[512,512]{1,0:T(8,128)(2,1)S(1)}, u32[]{:S(2)}, u32[]{:S(2)}) collective-permute-start(bf16[512,512]{1,0:T(8,128)(2,1)S(1)} %pad_maximum_fusion), channel_id=1, source_target_pairs={{0,8},{4,20},{8,0},{12,28},{16,24},{20,4},{24,16},{28,12},{1,9},{5... | collective-permute-start | bytes 1572872 | tf_op jit(solution)/shard_map/ppermute | solution.py:32
  64.5 11.0 %collective-permute-start.19 = (bf16[512,512]{1,0:T(8,128)(2,1)S(1)}, bf16[512,512]{1,0:T(8,128)(2,1)S(1)}, u32[]{:S(2)}, u32[]{:S(2)}) collective-permute-start(bf16[512,512]{1,0:T(8,128)(2,1)S(1)} %backward.7), channel_id=1, source_target_pairs={{0,4},{4,0},{8,12},{12,8},{16,20},{20,16},{24,28},{28,24},{1,5},{5... | collective-permute-start | bytes 1572872 | tf_op jit(solution)/shard_map/ppermute | solution.py:26
  65.1 6.0 %collective-permute-start.23 = (f32[64,512]{1,0:T(8,128)S(1)}, f32[64,512]{1,0:T(8,128)S(1)}, u32[]{:S(2)}, u32[]{:S(2)}) collective-permute-start(f32[64,512]{1,0:T(8,128)S(1)} %add_multiply_fusion.refs_0_), channel_id=1, source_target_pairs={{0,1},{1,0},{2,3},{3,2},{4,6},{5,7},{6,4},{7,5},{8,9},{9,8},{10,11... | collective-permute-start | bytes 393224 | tf_op jit(solution)/shard_map/ppermute | solution.py:42
  66.3 5.0 %collective-permute-start.24 = (f32[64,512]{1,0:T(8,128)S(1)}, f32[64,512]{1,0:T(8,128)S(1)}, u32[]{:S(2)}, u32[]{:S(2)}) collective-permute-start(f32[64,512]{1,0:T(8,128)S(1)} %add_multiply_fusion.refs_0_), channel_id=1, source_target_pairs={{0,2},{1,3},{2,0},{3,1},{4,5},{5,4},{6,7},{7,6},{8,10},{9,11},{10,... | collective-permute-start | bytes 393224 | tf_op jit(solution)/shard_map/ppermute | solution.py:42
  68.3 6.4 %collective-permute-start.25 = (f32[64,512]{1,0:T(8,128)S(1)}, f32[64,512]{1,0:T(8,128)S(1)}, u32[]{:S(2)}, u32[]{:S(2)}) collective-permute-start(f32[64,512]{1,0:T(8,128)S(1)} %add_multiply_fusion.refs_0_), channel_id=1, source_target_pairs={{0,3},{1,2},{2,1},{3,0},{4,7},{5,6},{6,5},{7,4},{8,11},{9,10},{10,... | collective-permute-start | bytes 393224 | tf_op jit(solution)/shard_map/ppermute | solution.py:42
  74.7 5.9 %collective-permute-start.26 = (f32[256,512]{1,0:T(8,128)S(1)}, f32[256,512]{1,0:T(8,128)S(1)}, u32[]{:S(2)}, u32[]{:S(2)}) collective-permute-start(f32[256,512]{1,0:T(8,128)S(1)} %pad_maximum_fusion.1), channel_id=1, source_target_pairs={{0,4},{4,0},{8,12},{12,8},{16,20},{20,16},{24,28},{28,24},{1,5},{5... | collective-permute-start | bytes 1572872 | tf_op jit(solution)/shard_map/ppermute | solution.py:26
  77.7 10.1 %collective-permute-start.21 = (bf16[256,512]{1,0:T(8,128)(2,1)S(1)}, bf16[256,512]{1,0:T(8,128)(2,1)S(1)}, u32[]{:S(2)}, u32[]{:S(2)}) collective-permute-start(bf16[256,512]{1,0:T(8,128)(2,1)S(1)} %get-tuple-element.84), channel_id=1, source_target_pairs={{0,16},{4,12},{8,24},{12,4},{16,0},{20,28},{24,8},{28,20},{1,17},{... | collective-permute-start | bytes 786440 | tf_op jit(solution)/shard_map/ppermute | solution.py:32

commit v13 on v12

--- a/solution.py
+++ b/solution.py
@@ -184,39 +184,39 @@
     )(*pieces, cotangent, weight)
 
 
-def weight_kernel(place_ref, agg_ref, pre_grad_ref, *refs, groups):
-    owns, send_ref, part_ref = refs[:groups], refs[groups], refs[groups + 1]
-    core, member = place_ref[0] & 1, place_ref[1]
-    rows = owns[0].shape[0]
-    bits = bit_count(groups)
+def weight_kernel(place_ref, agg_ref, pre_grad_ref, *refs, groups, side):
+    outs, part_ref = refs[:-1], refs[-1]
+    core, member = (place_ref[0] & 1) ^ side, place_ref[1]
+    half = part_ref.shape[0]
+    rows = half // groups
     part_ref[...] = lax.dot_general(
-        agg_ref[...], pre_grad_ref[...], (((0,), (0,)), ((), ())), preferred_element_type=jnp.float32
+        agg_ref[:, pl.ds(pl.multiple_of(core * half, half), half)], pre_grad_ref[...], (((0,), (0,)), ((), ())),
+        preferred_element_type=jnp.float32,
     )
-
-    def piece(k, side):
-        start = (2 * (member ^ between(k, 1 - side, bits)) + side) * rows
-        return part_ref[pl.ds(pl.multiple_of(start, rows), rows), :]
-
     for k in range(groups):
-        owns[k][...] = piece(k, core)
-        send_ref[k * rows:(k + 1) * rows, :] = piece(k, 1 - core).astype(send_ref.dtype)
-
-
-def weight_part(agg, pre_grad, place, groups):
+        start = (member ^ between(k, 1 - core, bit_count(groups))) * rows
+        piece = part_ref[pl.ds(pl.multiple_of(start, rows), rows), :]
+        if side:
+            outs[0][k * rows:(k + 1) * rows, :] = piece.astype(outs[0].dtype)
+        else:
+            outs[k][...] = piece
+
+
+def weight_part(agg, pre_grad, place, groups, side):
     rows, width = agg.shape
-    part = width // (2 * groups)
-    out = pl.pallas_call(
-        functools.partial(weight_kernel, groups=groups),
-        out_shape=[like((part, width), jnp.float32)] * groups + [like((groups * part, width), jnp.bfloat16)],
+    half = width // 2
+    own = [like((half // groups, width), jnp.float32)] * groups
+    return pl.pallas_call(
+        functools.partial(weight_kernel, groups=groups, side=side),
+        out_shape=[like((half, width), jnp.bfloat16)] if side else own,
         in_specs=[SCALARS, WHOLE, WHOLE],
-        out_specs=[WHOLE] * (groups + 1),
-        scratch_shapes=[pltpu.VMEM((width, width), jnp.float32)],
+        out_specs=[WHOLE] * (1 if side else groups),
+        scratch_shapes=[pltpu.VMEM((half, width), jnp.float32)],
         compiler_params=params(8),
         cost_estimate=pl.CostEstimate(
-            flops=2 * rows * width * width, bytes_accessed=4 * rows * width + 4 * width * width, transcendentals=0),
+            flops=2 * rows * half * width, bytes_accessed=4 * rows * width + 2 * width * width, transcendentals=0),
         name="weight_part",
     )(place, agg, pre_grad)
-    return out[:-1], out[-1]
 
 
 def place_kernel(place_ref, *refs, groups):
@@ -226,7 +226,7 @@
     bits = bit_count(groups)
     for k in range(groups):
         for side, value in ((core, owns[k][...]), (1 - core, other_ref[k * rows:(k + 1) * rows, :])):
-            start = (2 * (member ^ between(k, 1 - side, bits)) + side) * rows
+            start = (side * groups + (member ^ between(k, 1 - side, bits))) * rows
             out_ref[pl.ds(pl.multiple_of(start, rows), rows), :] = value
 
 
@@ -367,7 +367,8 @@
     dense_t = transposed(after(dense, *totals, pieces[1]))
     pieces[-1] = after(pieces[-1], *dense_t)
     activated, agg, pre_grad, grad = middle(pieces, cotangent, weight)
-    owns, send = weight_part(agg, pre_grad, place, groups)
+    (send,) = weight_part(agg, pre_grad, place, groups, 1)
+    owns = weight_part(after(agg, send), pre_grad, place, groups, 0)
     parts = add_slots(owns, swap_cores(send))
 
     grads = [grad]

time: 88.8 us -> 89 us (level)
  transfers between devices with their start and end apart: 27 -> 27, of which waited for: 15 -> 16; matrix products, arithmetic and copies ran while one was open for 2% -> 2% of each run, Pallas kernels for 11% -> 12%
where the time goes in v13:
time: 89 us; the launch traced here: 88.8 us
  waiting for transfers between devices  36.7 us (41%)
  starting transfers between devices  32.3 us (36%)
  Pallas kernels  14.7 us (17%)
  local copies, waits for them, and re-layouts  2.93 us (3%)
  other arithmetic  1.32 us (1%)
    ppermute x7, waiting for transfers between devices, swap_chips(): lax.ppermute(x, 'dom', [(i, i ^ 2 * between(held, i % 2, bits)) for i in...  21.4 us
    ppermute x7, starting transfers between devices, swap_chips(): lax.ppermute(x, 'dom', [(i, i ^ 2 * between(held, i % 2, bits)) for i in...  15.8 us
    ppermute x12, starting transfers between devices, swap_members(): return lax.ppermute(x, ('dom', 'repl'), pairs)  15.6 us
    ppermute x12, waiting for transfers between devices, swap_members(): return lax.ppermute(x, ('dom', 'repl'), pairs)  14.5 us
    pallas_call x4, Pallas kernels, forward(): pl.pallas_call(functools.partial(forward_kernel, which=which, base=base,...  2.82 us
    pallas_call x4, Pallas kernels, backward(): pl.pallas_call(functools.partial(backward_kernel, side=side, count=count,...  2.82 us
    pallas_call x1, Pallas kernels, densify(): pl.pallas_call(functools.partial(densify_kernel, col_tiles=col_tiles), ou...  2.5 us
    unnamed x8, local copies, waits for them, and re-layouts  2.2 us
  transfers between devices with their start and end apart: 27, of which 16 were waited for; matrix products, arithmetic and copies ran while one was open for 2% of the time, Pallas kernels for 12%

profile of v13, /device:TPU:0, one launch (start us, length us, event | category | flops | bytes accessed | tf_op | source)
XLA Modules:
  0.0 88.8 jit_solution(12500317282102587142)
XLA Ops:
  0.6 4.1 %collective-permute-start = (bf16[256,512]{1,0:T(8,128)(2,1)}, bf16[256,512]{1,0:T(8,128)(2,1)S(1)}, u32[]{:S(2)}, u32[]{:S(2)}) collective-permute-start(bf16[256,512]{1,0:T(8,128)(2,1)} %refs_1_.1), channel_id=1, source_target_pairs={{0,16},{4,12},{8,24},{12,4},{16,0},{20,28},{24,8},{28,20},{1,17},{... | collective-permute-start | bytes 786440 | tf_op jit(solution)/shard_map/ppermute | solution.py:32
  6.3 4.6 %collective-permute-done.refs_3_ = bf16[256,512]{1,0:T(8,128)(2,1)S(1)} collective-permute-done((bf16[256,512]{1,0:T(8,128)(2,1)}, bf16[256,512]{1,0:T(8,128)(2,1)S(1)}, u32[]{:S(2)}, u32[]{:S(2)}) %collective-permute-start) | collective-permute-done | bytes 262176 | tf_op jit(solution)/shard_map/ppermute | solution.py:32
  10.9 2.4 %collective-permute-start.1 = (bf16[256,512]{1,0:T(8,128)(2,1)}, bf16[256,512]{1,0:T(8,128)(2,1)S(1)}, u32[]{:S(2)}, u32[]{:S(2)}) collective-permute-start(bf16[256,512]{1,0:T(8,128)(2,1)} %refs_1_.1), channel_id=1, source_target_pairs={{0,8},{4,20},{8,0},{12,28},{16,24},{20,4},{24,16},{28,12},{1,9},{5... | collective-permute-start | bytes 786440 | tf_op jit(solution)/shard_map/ppermute | solution.py:32
  13.4 2.2 %copy-done = bf16[1,1,8,16,128,128]{5,4,3,2,1,0:T(8,128)(2,1)S(1)} copy-done((bf16[1,1,8,16,128,128]{5,4,3,2,1,0:T(8,128)(2,1)S(1)}, bf16[1,1,8,16,128,128]{5,4,3,2,1,0:T(8,128)(2,1)}, u32[]{:S(2)}) %copy-start) | copy-done | bytes 4194328
  15.6 2.5 %densify.1.refs_0_.a_ref = bf16[8,1024,256]{2,1,0:T(8,128)(2,1)S(1)} custom-call(s32[8,17]{1,0:T(8,128)S(1)} %pad_add_fusion.spots_ref, s32[2]{0:T(128)S(1)} %pad_add_fusion.1.place_ref, bf16[8,16,128,128]{3,2,1,0:T(8,128)(2,1)S(1)} %bitcast.26), custom_call_target="tpu_custom_call" | custom-call | flops 2097152 | bytes 16777216 | tf_op jit(solution)/shard_map/densify/pallas_call | solution.py:86
  18.1 1.2 %forward.4 = (f32[256,512]{1,0:T(8,128)S(1)}, f32[256,512]{1,0:T(8,128)S(1)}, f32[256,512]{1,0:T(8,128)S(1)}, f32[256,512]{1,0:T(8,128)S(1)}) custom-call(bf16[8,1024,256]{2,1,0:T(8,128)(2,1)S(1)} %densify.1.refs_0_.a_ref, bf16[256,512]{1,0:T(8,128)(2,1)S(1)} %copy-done.2, bf16[256,512]{1,0:T(8,128)(2,1)S(1)} %collective-permute-done.2.refs_2_, ...), custom_call_target="tpu_custom_call" | custom-call | flops 1073741824 | bytes 4194304 | tf_op jit(solution)/shard_map/forward/pallas_call | solution.py:140
  19.4 3.5 %collective-permute-done.1.refs_1_ = bf16[256,512]{1,0:T(8,128)(2,1)S(1)} collective-permute-done((bf16[256,512]{1,0:T(8,128)(2,1)}, bf16[256,512]{1,0:T(8,128)(2,1)S(1)}, u32[]{:S(2)}, u32[]{:S(2)}) %collective-permute-start.1) | collective-permute-done | bytes 262176 | tf_op jit(solution)/shard_map/ppermute | solution.py:32
  22.9 3.4 %collective-permute-done.5.refs_2_ = bf16[256,512]{1,0:T(8,128)(2,1)S(1)} collective-permute-done((bf16[256,512]{1,0:T(8,128)(2,1)S(1)}, bf16[256,512]{1,0:T(8,128)(2,1)S(1)}, u32[]{:S(2)}, u32[]{:S(2)}) %collective-permute-start.5) | collective-permute-done | bytes 262176 | tf_op jit(solution)/shard_map/ppermute | solution.py:32
  28.3 1.7 %collective-permute-start.8 = (bf16[256,512]{1,0:T(8,128)(2,1)S(1)}, bf16[256,512]{1,0:T(8,128)(2,1)S(1)}, u32[]{:S(2)}, u32[]{:S(2)}) collective-permute-start(bf16[256,512]{1,0:T(8,128)(2,1)S(1)} %get-tuple-element.55), channel_id=1, source_target_pairs={{0,1},{1,0},{2,3},{3,2},{4,6},{5,7},{6,4},{7,5},{8,9},{9,8},{10,11... | collective-permute-start | bytes 786440 | tf_op jit(solution)/shard_map/ppermute | solution.py:42
  30.8 3.9 %collective-permute-done.8 = bf16[256,512]{1,0:T(8,128)(2,1)S(1)} collective-permute-done((bf16[256,512]{1,0:T(8,128)(2,1)S(1)}, bf16[256,512]{1,0:T(8,128)(2,1)S(1)}, u32[]{:S(2)}, u32[]{:S(2)}) %collective-permute-start.8) | collective-permute-done | bytes 262176 | tf_op jit(solution)/shard_map/ppermute | solution.py:42
  34.8 1.8 %collective-permute-start.9 = (bf16[256,512]{1,0:T(8,128)(2,1)S(1)}, bf16[256,512]{1,0:T(8,128)(2,1)S(1)}, u32[]{:S(2)}, u32[]{:S(2)}) collective-permute-start(bf16[256,512]{1,0:T(8,128)(2,1)S(1)} %add_convert_fusion.2), channel_id=1, source_target_pairs={{0,2},{1,3},{2,0},{3,1},{4,5},{5,4},{6,7},{7,6},{8,10},{9,11},{10,... | collective-permute-start | bytes 786440 | tf_op jit(solution)/shard_map/ppermute | solution.py:42
  36.6 1.7 %collective-permute-done.7.refs_1_ = bf16[256,512]{1,0:T(8,128)(2,1)S(1)} collective-permute-done((bf16[256,512]{1,0:T(8,128)(2,1)S(1)}, bf16[256,512]{1,0:T(8,128)(2,1)S(1)}, u32[]{:S(2)}, u32[]{:S(2)}) %collective-permute-start.7) | collective-permute-done | bytes 262176 | tf_op jit(solution)/shard_map/ppermute | solution.py:42
  38.2 1.2 %transposed.1 = (bf16[2,256,1024]{2,1,0:T(8,128)(2,1)S(1)}, bf16[2,256,1024]{2,1,0:T(8,128)(2,1)S(1)}, bf16[2,256,1024]{2,1,0:T(8,128)(2,1)S(1)}, bf16[2,256,1024]{2,1,0:T(8,128)(2,1)S(1)}) custom-call(bf16[8,1024,256]{2,1,0:T(8,128)(2,1)S(1)} %densify.1.refs_0_.a_ref), custom_call_target="tpu_custom_call" | custom-call | bytes 8388608 | tf_op jit(solution)/shard_map/transposed/pallas_call | solution.py:111
  39.5 1.8 %collective-permute-done.9.refs_2_ = bf16[256,512]{1,0:T(8,128)(2,1)S(1)} collective-permute-done((bf16[256,512]{1,0:T(8,128)(2,1)S(1)}, bf16[256,512]{1,0:T(8,128)(2,1)S(1)}, u32[]{:S(2)}, u32[]{:S(2)}) %collective-permute-start.9) | collective-permute-done | bytes 262176 | tf_op jit(solution)/shard_map/ppermute | solution.py:42
  41.2 1.2 %middle.1 = (bf16[256,512]{1,0:T(8,128)(2,1)}, bf16[256,512]{1,0:T(8,128)(2,1)S(1)}, bf16[256,512]{1,0:T(8,128)(2,1)S(1)}, bf16[256,512]{1,0:T(8,128)(2,1)S(1)}) custom-call(f32[256,512]{1,0:T(8,128)S(1)} %get-tuple-element.59.refs_0_, bf16[256,512]{1,0:T(8,128)(2,1)S(1)} %collective-permute-done.7.refs_1_, ...), custom_call_target="tpu_custom_call" | custom-call | flops 268435456 | bytes 1310720 | tf_op jit(solution)/shard_map/middle/pallas_call | solution.py:175
  43.3 1.8 %collective-permute-start.10 = (bf16[256,512]{1,0:T(8,128)(2,1)S(1)}, bf16[256,512]{1,0:T(8,128)(2,1)S(1)}, u32[]{:S(2)}, u32[]{:S(2)}) collective-permute-start(bf16[256,512]{1,0:T(8,128)(2,1)S(1)} %get-tuple-element.80.refs_2_), channel_id=1, source_target_pairs={{0,2},{1,3},{2,0},{3,1},{4,5},{5,4},{6,7},{7,6},{8,10},{9,11},{10,... | collective-permute-start | bytes 786440 | tf_op jit(solution)/shard_map/ppermute | solution.py:42
  46.0 1.6 %collective-permute-start.16 = (bf16[64,512]{1,0:T(8,128)(2,1)S(1)}, bf16[64,512]{1,0:T(8,128)(2,1)S(1)}, u32[]{:S(2)}, u32[]{:S(2)}) collective-permute-start(bf16[64,512]{1,0:T(8,128)(2,1)S(1)} %get-tuple-element.88), channel_id=1, source_target_pairs={{0,3},{1,2},{2,1},{3,0},{4,7},{5,6},{6,5},{7,4},{8,11},{9,10},{10,... | collective-permute-start | bytes 196616 | tf_op jit(solution)/shard_map/ppermute | solution.py:42
  47.6 1.4 %collective-permute-start.15 = (bf16[64,512]{1,0:T(8,128)(2,1)S(1)}, bf16[64,512]{1,0:T(8,128)(2,1)S(1)}, u32[]{:S(2)}, u32[]{:S(2)}) collective-permute-start(bf16[64,512]{1,0:T(8,128)(2,1)S(1)} %get-tuple-element.89), channel_id=1, source_target_pairs={{0,2},{1,3},{2,0},{3,1},{4,5},{5,4},{6,7},{7,6},{8,10},{9,11},{10,... | collective-permute-start | bytes 196616 | tf_op jit(solution)/shard_map/ppermute | solution.py:42
  49.5 1.5 %collective-permute-start.11 = (bf16[256,512]{1,0:T(8,128)(2,1)S(1)}, bf16[256,512]{1,0:T(8,128)(2,1)S(1)}, u32[]{:S(2)}, u32[]{:S(2)}) collective-permute-start(bf16[256,512]{1,0:T(8,128)(2,1)S(1)} %get-tuple-element.80.refs_2_), channel_id=1, source_target_pairs={{0,1},{1,0},{2,3},{3,2},{4,6},{5,7},{6,4},{7,5},{8,9},{9,8},{10,11... | collective-permute-start | bytes 786440 | tf_op jit(solution)/shard_map/ppermute | solution.py:42
  51.0 1.4 %collective-permute-start.12 = (bf16[256,512]{1,0:T(8,128)(2,1)S(1)}, bf16[256,512]{1,0:T(8,128)(2,1)S(1)}, u32[]{:S(2)}, u32[]{:S(2)}) collective-permute-start(bf16[256,512]{1,0:T(8,128)(2,1)S(1)} %collective-permute-done.10.refs_3_), channel_id=1, source_target_pairs={{0,1},{1,0},{2,3},{3,2},{4,6},{5,7},{6,4},{7,5},{8,9},{9,8},{10,11... | collective-permute-start | bytes 786440 | tf_op jit(solution)/shard_map/ppermute | solution.py:42
  53.3 3.0 %collective-permute-start.17 = (bf16[64,512]{1,0:T(8,128)(2,1)S(1)}, bf16[64,512]{1,0:T(8,128)(2,1)S(1)}, u32[]{:S(2)}, u32[]{:S(2)}) collective-permute-start(bf16[64,512]{1,0:T(8,128)(2,1)S(1)} %add_convert_fusion.4), channel_id=1, source_target_pairs={{0,16},{4,12},{8,24},{12,4},{16,0},{20,28},{24,8},{28,20},{1,17},{... | collective-permute-start | bytes 196616 | tf_op jit(solution)/shard_map/ppermute | solution.py:32
  56.3 2.3 %collective-permute-done.17 = bf16[64,512]{1,0:T(8,128)(2,1)S(1)} collective-permute-done((bf16[64,512]{1,0:T(8,128)(2,1)S(1)}, bf16[64,512]{1,0:T(8,128)(2,1)S(1)}, u32[]{:S(2)}, u32[]{:S(2)}) %collective-permute-start.17) | collective-permute-done | bytes 65568 | tf_op jit(solution)/shard_map/ppermute | solution.py:32
  59.7 2.2 %collective-permute-start.22 = (bf16[64,512]{1,0:T(8,128)(2,1)S(1)}, bf16[64,512]{1,0:T(8,128)(2,1)S(1)}, u32[]{:S(2)}, u32[]{:S(2)}) collective-permute-start(bf16[64,512]{1,0:T(8,128)(2,1)S(1)} %add_convert_fusion.3), channel_id=1, source_target_pairs={{0,8},{4,20},{8,0},{12,28},{16,24},{20,4},{24,16},{28,12},{1,9},{5... | collective-permute-start | bytes 196616 | tf_op jit(solution)/shard_map/ppermute | solution.py:32
  62.9 1.1 %collective-permute-start.20 = (bf16[512,512]{1,0:T(8,128)(2,1)S(1)}, bf16[512,512]{1,0:T(8,128)(2,1)S(1)}, u32[]{:S(2)}, u32[]{:S(2)}) collective-permute-start(bf16[512,512]{1,0:T(8,128)(2,1)S(1)} %pad_maximum_fusion), channel_id=1, source_target_pairs={{0,8},{4,20},{8,0},{12,28},{16,24},{20,4},{24,16},{28,12},{1,9},{5... | collective-permute-start | bytes 1572872 | tf_op jit(solution)/shard_map/ppermute | solution.py:32
  65.4 1.4 %collective-permute-start.23 = (f32[64,512]{1,0:T(8,128)S(1)}, f32[64,512]{1,0:T(8,128)S(1)}, u32[]{:S(2)}, u32[]{:S(2)}) collective-permute-start(f32[64,512]{1,0:T(8,128)S(1)} %add_multiply_fusion.refs_0_), channel_id=1, source_target_pairs={{0,1},{1,0},{2,3},{3,2},{4,6},{5,7},{6,4},{7,5},{8,9},{9,8},{10,11... | collective-permute-start | bytes 393224 | tf_op jit(solution)/shard_map/ppermute | solution.py:42
  66.8 1.4 %collective-permute-start.24 = (f32[64,512]{1,0:T(8,128)S(1)}, f32[64,512]{1,0:T(8,128)S(1)}, u32[]{:S(2)}, u32[]{:S(2)}) collective-permute-start(f32[64,512]{1,0:T(8,128)S(1)} %add_multiply_fusion.refs_0_), channel_id=1, source_target_pairs={{0,2},{1,3},{2,0},{3,1},{4,5},{5,4},{6,7},{7,6},{8,10},{9,11},{10,... | collective-permute-start | bytes 393224 | tf_op jit(solution)/shard_map/ppermute | solution.py:42
  69.0 2.8 %collective-permute-done.23.refs_1_ = f32[64,512]{1,0:T(8,128)S(1)} collective-permute-done((f32[64,512]{1,0:T(8,128)S(1)}, f32[64,512]{1,0:T(8,128)S(1)}, u32[]{:S(2)}, u32[]{:S(2)}) %collective-permute-start.23) | collective-permute-done | bytes 131104 | tf_op jit(solution)/shard_map/ppermute | solution.py:42
  71.9 3.0 %collective-permute-done.25.refs_3_ = f32[64,512]{1,0:T(8,128)S(1)} collective-permute-done((f32[64,512]{1,0:T(8,128)S(1)}, f32[64,512]{1,0:T(8,128)S(1)}, u32[]{:S(2)}, u32[]{:S(2)}) %collective-permute-start.25) | collective-permute-done | bytes 131104 | tf_op jit(solution)/shard_map/ppermute | solution.py:42
  75.8 2.0 %collective-permute-done.20.refs_3_ = bf16[512,512]{1,0:T(8,128)(2,1)S(1)} collective-permute-done((bf16[512,512]{1,0:T(8,128)(2,1)S(1)}, bf16[512,512]{1,0:T(8,128)(2,1)S(1)}, u32[]{:S(2)}, u32[]{:S(2)}) %collective-permute-start.20) | collective-permute-done | bytes 524320 | tf_op jit(solution)/shard_map/ppermute | solution.py:32
  77.9 2.9 %collective-permute-start.21 = (bf16[256,512]{1,0:T(8,128)(2,1)S(1)}, bf16[256,512]{1,0:T(8,128)(2,1)S(1)}, u32[]{:S(2)}, u32[]{:S(2)}) collective-permute-start(bf16[256,512]{1,0:T(8,128)(2,1)S(1)} %get-tuple-element.84), channel_id=1, source_target_pairs={{0,16},{4,12},{8,24},{12,4},{16,0},{20,28},{24,8},{28,20},{1,17},{... | collective-permute-start | bytes 786440 | tf_op jit(solution)/shard_map/ppermute | solution.py:32
  80.8 1.6 %place_slices.1 = f32[512,512]{1,0:T(8,128)} custom-call(s32[2]{0:T(128)S(1)} %pad_add_fusion.1.place_ref, f32[64,512]{1,0:T(8,128)S(1)} %add_multiply_fusion.refs_0_, f32[64,512]{1,0:T(8,128)S(1)} %collective-permute-done.23.refs_1_, f32[64,512]{1,0:T(8,128)S(1)} %collective-permute-done.24.refs_2_, f32[64,512]{1,0:T(8,128)S(1)} %collective-permute-done.25.refs_3_, ...), custom_call_target="tpu_custom_call" | custom-call | bytes 2097152 | tf_op jit(solution)/shard_map/place_slices/pallas_call | solution.py:236
  82.4 5.7 %collective-permute-done.21.refs_1_ = bf16[256,512]{1,0:T(8,128)(2,1)S(1)} collective-permute-done((bf16[256,512]{1,0:T(8,128)(2,1)S(1)}, bf16[256,512]{1,0:T(8,128)(2,1)S(1)}, u32[]{:S(2)}, u32[]{:S(2)}) %collective-permute-start.21) | collective-permute-done | bytes 262176 | tf_op jit(solution)/shard_map/ppermute | solution.py:32
  (58 shorter events, 13.7 us)
Async XLA Ops:
  0.6 10.2 %collective-permute-start = (bf16[256,512]{1,0:T(8,128)(2,1)}, bf16[256,512]{1,0:T(8,128)(2,1)S(1)}, u32[]{:S(2)}, u32[]{:S(2)}) collective-permute-start(bf16[256,512]{1,0:T(8,128)(2,1)} %refs_1_.1), channel_id=1, source_target_pairs={{0,16},{4,12},{8,24},{12,4},{16,0},{20,28},{24,8},{28,20},{1,17},{... | collective-permute-start | bytes 786440 | tf_op jit(solution)/shard_map/ppermute | solution.py:32
  4.7 13.4 %collective-permute-start.2 = (bf16[256,512]{1,0:T(8,128)(2,1)}, bf16[256,512]{1,0:T(8,128)(2,1)S(1)}, u32[]{:S(2)}, u32[]{:S(2)}) collective-permute-start(bf16[256,512]{1,0:T(8,128)(2,1)} %refs_1_.1), channel_id=1, source_target_pairs={{0,4},{4,0},{8,12},{12,8},{16,20},{20,16},{24,28},{28,24},{1,5},{5... | collective-permute-start | bytes 786440 | tf_op jit(solution)/shard_map/ppermute | solution.py:26
  10.9 7.3 %collective-permute-start.3 = (bf16[256,512]{1,0:T(8,128)(2,1)S(1)}, bf16[256,512]{1,0:T(8,128)(2,1)S(1)}, u32[]{:S(2)}, u32[]{:S(2)}) collective-permute-start(bf16[256,512]{1,0:T(8,128)(2,1)S(1)} %collective-permute-done.refs_3_), channel_id=1, source_target_pairs={{0,4},{4,0},{8,12},{12,8},{16,20},{20,16},{24,28},{28,24},{1,5},{5... | collective-permute-start | bytes 786440 | tf_op jit(solution)/shard_map/ppermute | solution.py:26
  10.9 12.1 %collective-permute-start.1 = (bf16[256,512]{1,0:T(8,128)(2,1)}, bf16[256,512]{1,0:T(8,128)(2,1)S(1)}, u32[]{:S(2)}, u32[]{:S(2)}) collective-permute-start(bf16[256,512]{1,0:T(8,128)(2,1)} %refs_1_.1), channel_id=1, source_target_pairs={{0,8},{4,20},{8,0},{12,28},{16,24},{20,4},{24,16},{28,12},{1,9},{5... | collective-permute-start | bytes 786440 | tf_op jit(solution)/shard_map/ppermute | solution.py:32
  13.3 13.0 %collective-permute-start.5 = (bf16[256,512]{1,0:T(8,128)(2,1)S(1)}, bf16[256,512]{1,0:T(8,128)(2,1)S(1)}, u32[]{:S(2)}, u32[]{:S(2)}) collective-permute-start(bf16[256,512]{1,0:T(8,128)(2,1)S(1)} %collective-permute-done.refs_3_), channel_id=1, source_target_pairs={{0,8},{4,20},{8,0},{12,28},{16,24},{20,4},{24,16},{28,12},{1,9},{5... | collective-permute-start | bytes 786440 | tf_op jit(solution)/shard_map/ppermute | solution.py:32
  13.4 2.2 %copy-start = (bf16[1,1,8,16,128,128]{5,4,3,2,1,0:T(8,128)(2,1)S(1)}, bf16[1,1,8,16,128,128]{5,4,3,2,1,0:T(8,128)(2,1)}, u32[]{:S(2)}) copy-start(bf16[1,1,8,16,128,128]{5,4,3,2,1,0:T(8,128)(2,1)} %param.10) | copy-start | bytes 12582916
  15.6 2.5 %copy-start.2 = (bf16[256,512]{1,0:T(8,128)(2,1)S(1)}, bf16[256,512]{1,0:T(8,128)(2,1)}, u32[]{:S(2)}) copy-start(bf16[256,512]{1,0:T(8,128)(2,1)} %refs_1_.1) | copy-start | bytes 786436
  22.9 4.1 %collective-permute-start.4 = (bf16[256,512]{1,0:T(8,128)(2,1)S(1)}, bf16[256,512]{1,0:T(8,128)(2,1)S(1)}, u32[]{:S(2)}, u32[]{:S(2)}) collective-permute-start(bf16[256,512]{1,0:T(8,128)(2,1)S(1)} %collective-permute-done.1.refs_1_), channel_id=1, source_target_pairs={{0,4},{4,0},{8,12},{12,8},{16,20},{20,16},{24,28},{28,24},{1,5},{5... | collective-permute-start | bytes 786440 | tf_op jit(solution)/shard_map/ppermute | solution.py:26
  26.3 1.5 %collective-permute-start.6 = (bf16[256,512]{1,0:T(8,128)(2,1)S(1)}, bf16[256,512]{1,0:T(8,128)(2,1)S(1)}, u32[]{:S(2)}, u32[]{:S(2)}) collective-permute-start(bf16[256,512]{1,0:T(8,128)(2,1)S(1)} %collective-permute-done.5.refs_2_), channel_id=1, source_target_pairs={{0,4},{4,0},{8,12},{12,8},{16,20},{20,16},{24,28},{28,24},{1,5},{5... | collective-permute-start | bytes 786440 | tf_op jit(solution)/shard_map/ppermute | solution.py:26
  28.3 6.4 %collective-permute-start.8 = (bf16[256,512]{1,0:T(8,128)(2,1)S(1)}, bf16[256,512]{1,0:T(8,128)(2,1)S(1)}, u32[]{:S(2)}, u32[]{:S(2)}) collective-permute-start(bf16[256,512]{1,0:T(8,128)(2,1)S(1)} %get-tuple-element.55), channel_id=1, source_target_pairs={{0,1},{1,0},{2,3},{3,2},{4,6},{5,7},{6,4},{7,5},{8,9},{9,8},{10,11... | collective-permute-start | bytes 786440 | tf_op jit(solution)/shard_map/ppermute | solution.py:42
  30.0 8.2 %collective-permute-start.7 = (bf16[256,512]{1,0:T(8,128)(2,1)S(1)}, bf16[256,512]{1,0:T(8,128)(2,1)S(1)}, u32[]{:S(2)}, u32[]{:S(2)}) collective-permute-start(bf16[256,512]{1,0:T(8,128)(2,1)S(1)} %get-tuple-element.54), channel_id=1, source_target_pairs={{0,1},{1,0},{2,3},{3,2},{4,6},{5,7},{6,4},{7,5},{8,9},{9,8},{10,11... | collective-permute-start | bytes 786440 | tf_op jit(solution)/shard_map/ppermute | solution.py:42
  30.4 10.9 %copy-start.1 = (bf16[512,512]{1,0:T(8,128)(2,1)S(1)}, bf16[512,512]{1,0:T(8,128)(2,1)}, u32[]{:S(2)}) copy-start(bf16[512,512]{1,0:T(8,128)(2,1)} %refs_4_.1) | copy-start | bytes 1572868
  30.4 10.9 %copy-start.3 = (bf16[256,512]{1,0:T(8,128)(2,1)S(1)}, bf16[256,512]{1,0:T(8,128)(2,1)}, u32[]{:S(2)}) copy-start(bf16[256,512]{1,0:T(8,128)(2,1)} %refs_3_.1) | copy-start | bytes 786436
  34.8 6.4 %collective-permute-start.9 = (bf16[256,512]{1,0:T(8,128)(2,1)S(1)}, bf16[256,512]{1,0:T(8,128)(2,1)S(1)}, u32[]{:S(2)}, u32[]{:S(2)}) collective-permute-start(bf16[256,512]{1,0:T(8,128)(2,1)S(1)} %add_convert_fusion.2), channel_id=1, source_target_pairs={{0,2},{1,3},{2,0},{3,1},{4,5},{5,4},{6,7},{7,6},{8,10},{9,11},{10,... | collective-permute-start | bytes 786440 | tf_op jit(solution)/shard_map/ppermute | solution.py:42
  43.2 2.7 %collective-permute-start.13 = (bf16[256,512]{1,0:T(8,128)(2,1)S(1)}, bf16[256,512]{1,0:T(8,128)(2,1)S(1)}, u32[]{:S(2)}, u32[]{:S(2)}) collective-permute-start(bf16[256,512]{1,0:T(8,128)(2,1)S(1)} %weight_part.2), channel_id=1, source_target_pairs={{0,4},{4,0},{8,12},{12,8},{16,20},{20,16},{24,28},{28,24},{1,5},{5... | collective-permute-start | bytes 786440 | tf_op jit(solution)/shard_map/ppermute | solution.py:26
  43.3 7.7 %collective-permute-start.10 = (bf16[256,512]{1,0:T(8,128)(2,1)S(1)}, bf16[256,512]{1,0:T(8,128)(2,1)S(1)}, u32[]{:S(2)}, u32[]{:S(2)}) collective-permute-start(bf16[256,512]{1,0:T(8,128)(2,1)S(1)} %get-tuple-element.80.refs_2_), channel_id=1, source_target_pairs={{0,2},{1,3},{2,0},{3,1},{4,5},{5,4},{6,7},{7,6},{8,10},{9,11},{10,... | collective-permute-start | bytes 786440 | tf_op jit(solution)/shard_map/ppermute | solution.py:42
  46.0 6.5 %collective-permute-start.16 = (bf16[64,512]{1,0:T(8,128)(2,1)S(1)}, bf16[64,512]{1,0:T(8,128)(2,1)S(1)}, u32[]{:S(2)}, u32[]{:S(2)}) collective-permute-start(bf16[64,512]{1,0:T(8,128)(2,1)S(1)} %get-tuple-element.88), channel_id=1, source_target_pairs={{0,3},{1,2},{2,1},{3,0},{4,7},{5,6},{6,5},{7,4},{8,11},{9,10},{10,... | collective-permute-start | bytes 196616 | tf_op jit(solution)/shard_map/ppermute | solution.py:42
  47.6 5.6 %collective-permute-start.15 = (bf16[64,512]{1,0:T(8,128)(2,1)S(1)}, bf16[64,512]{1,0:T(8,128)(2,1)S(1)}, u32[]{:S(2)}, u32[]{:S(2)}) collective-permute-start(bf16[64,512]{1,0:T(8,128)(2,1)S(1)} %get-tuple-element.89), channel_id=1, source_target_pairs={{0,2},{1,3},{2,0},{3,1},{4,5},{5,4},{6,7},{7,6},{8,10},{9,11},{10,... | collective-permute-start | bytes 196616 | tf_op jit(solution)/shard_map/ppermute | solution.py:42
  49.0 4.3 %collective-permute-start.14 = (bf16[64,512]{1,0:T(8,128)(2,1)S(1)}, bf16[64,512]{1,0:T(8,128)(2,1)S(1)}, u32[]{:S(2)}, u32[]{:S(2)}) collective-permute-start(bf16[64,512]{1,0:T(8,128)(2,1)S(1)} %get-tuple-element.87), channel_id=1, source_target_pairs={{0,1},{1,0},{2,3},{3,2},{4,6},{5,7},{6,4},{7,5},{8,9},{9,8},{10,11... | collective-permute-start | bytes 196616 | tf_op jit(solution)/shard_map/ppermute | solution.py:42
  49.5 9.3 %collective-permute-start.11 = (bf16[256,512]{1,0:T(8,128)(2,1)S(1)}, bf16[256,512]{1,0:T(8,128)(2,1)S(1)}, u32[]{:S(2)}, u32[]{:S(2)}) collective-permute-start(bf16[256,512]{1,0:T(8,128)(2,1)S(1)} %get-tuple-element.80.refs_2_), channel_id=1, source_target_pairs={{0,1},{1,0},{2,3},{3,2},{4,6},{5,7},{6,4},{7,5},{8,9},{9,8},{10,11... | collective-permute-start | bytes 786440 | tf_op jit(solution)/shard_map/ppermute | solution.py:42
  51.0 7.9 %collective-permute-start.12 = (bf16[256,512]{1,0:T(8,128)(2,1)S(1)}, bf16[256,512]{1,0:T(8,128)(2,1)S(1)}, u32[]{:S(2)}, u32[]{:S(2)}) collective-permute-start(bf16[256,512]{1,0:T(8,128)(2,1)S(1)} %collective-permute-done.10.refs_3_), channel_id=1, source_target_pairs={{0,1},{1,0},{2,3},{3,2},{4,6},{5,7},{6,4},{7,5},{8,9},{9,8},{10,11... | collective-permute-start | bytes 786440 | tf_op jit(solution)/shard_map/ppermute | solution.py:42
  53.3 5.2 %collective-permute-start.17 = (bf16[64,512]{1,0:T(8,128)(2,1)S(1)}, bf16[64,512]{1,0:T(8,128)(2,1)S(1)}, u32[]{:S(2)}, u32[]{:S(2)}) collective-permute-start(bf16[64,512]{1,0:T(8,128)(2,1)S(1)} %add_convert_fusion.4), channel_id=1, source_target_pairs={{0,16},{4,12},{8,24},{12,4},{16,0},{20,28},{24,8},{28,20},{1,17},{... | collective-permute-start | bytes 196616 | tf_op jit(solution)/shard_map/ppermute | solution.py:32
  59.6 3.1 %collective-permute-start.18 = (bf16[512,512]{1,0:T(8,128)(2,1)S(1)}, bf16[512,512]{1,0:T(8,128)(2,1)S(1)}, u32[]{:S(2)}, u32[]{:S(2)}) collective-permute-start(bf16[512,512]{1,0:T(8,128)(2,1)S(1)} %backward.4), channel_id=1, source_target_pairs={{0,4},{4,0},{8,12},{12,8},{16,20},{20,16},{24,28},{28,24},{1,5},{5... | collective-permute-start | bytes 1572872 | tf_op jit(solution)/shard_map/ppermute | solution.py:26
  59.7 5.7 %collective-permute-start.22 = (bf16[64,512]{1,0:T(8,128)(2,1)S(1)}, bf16[64,512]{1,0:T(8,128)(2,1)S(1)}, u32[]{:S(2)}, u32[]{:S(2)}) collective-permute-start(bf16[64,512]{1,0:T(8,128)(2,1)S(1)} %add_convert_fusion.3), channel_id=1, source_target_pairs={{0,8},{4,20},{8,0},{12,28},{16,24},{20,4},{24,16},{28,12},{1,9},{5... | collective-permute-start | bytes 196616 | tf_op jit(solution)/shard_map/ppermute | solution.py:32
  62.9 14.9 %collective-permute-start.20 = (bf16[512,512]{1,0:T(8,128)(2,1)S(1)}, bf16[512,512]{1,0:T(8,128)(2,1)S(1)}, u32[]{:S(2)}, u32[]{:S(2)}) collective-permute-start(bf16[512,512]{1,0:T(8,128)(2,1)S(1)} %pad_maximum_fusion), channel_id=1, source_target_pairs={{0,8},{4,20},{8,0},{12,28},{16,24},{20,4},{24,16},{28,12},{1,9},{5... | collective-permute-start | bytes 1572872 | tf_op jit(solution)/shard_map/ppermute | solution.py:32
  64.7 11.0 %collective-permute-start.19 = (bf16[512,512]{1,0:T(8,128)(2,1)S(1)}, bf16[512,512]{1,0:T(8,128)(2,1)S(1)}, u32[]{:S(2)}, u32[]{:S(2)}) collective-permute-start(bf16[512,512]{1,0:T(8,128)(2,1)S(1)} %backward.7), channel_id=1, source_target_pairs={{0,4},{4,0},{8,12},{12,8},{16,20},{20,16},{24,28},{28,24},{1,5},{5... | collective-permute-start | bytes 1572872 | tf_op jit(solution)/shard_map/ppermute | solution.py:26
  65.4 6.3 %collective-permute-start.23 = (f32[64,512]{1,0:T(8,128)S(1)}, f32[64,512]{1,0:T(8,128)S(1)}, u32[]{:S(2)}, u32[]{:S(2)}) collective-permute-start(f32[64,512]{1,0:T(8,128)S(1)} %add_multiply_fusion.refs_0_), channel_id=1, source_target_pairs={{0,1},{1,0},{2,3},{3,2},{4,6},{5,7},{6,4},{7,5},{8,9},{9,8},{10,11... | collective-permute-start | bytes 393224 | tf_op jit(solution)/shard_map/ppermute | solution.py:42
  66.8 5.1 %collective-permute-start.24 = (f32[64,512]{1,0:T(8,128)S(1)}, f32[64,512]{1,0:T(8,128)S(1)}, u32[]{:S(2)}, u32[]{:S(2)}) collective-permute-start(f32[64,512]{1,0:T(8,128)S(1)} %add_multiply_fusion.refs_0_), channel_id=1, source_target_pairs={{0,2},{1,3},{2,0},{3,1},{4,5},{5,4},{6,7},{7,6},{8,10},{9,11},{10,... | collective-permute-start | bytes 393224 | tf_op jit(solution)/shard_map/ppermute | solution.py:42
  68.2 6.7 %collective-permute-start.25 = (f32[64,512]{1,0:T(8,128)S(1)}, f32[64,512]{1,0:T(8,128)S(1)}, u32[]{:S(2)}, u32[]{:S(2)}) collective-permute-start(f32[64,512]{1,0:T(8,128)S(1)} %add_multiply_fusion.refs_0_), channel_id=1, source_target_pairs={{0,3},{1,2},{2,1},{3,0},{4,7},{5,6},{6,5},{7,4},{8,11},{9,10},{10,... | collective-permute-start | bytes 393224 | tf_op jit(solution)/shard_map/ppermute | solution.py:42
  75.0 5.8 %collective-permute-start.26 = (f32[256,512]{1,0:T(8,128)S(1)}, f32[256,512]{1,0:T(8,128)S(1)}, u32[]{:S(2)}, u32[]{:S(2)}) collective-permute-start(f32[256,512]{1,0:T(8,128)S(1)} %pad_maximum_fusion.1), channel_id=1, source_target_pairs={{0,4},{4,0},{8,12},{12,8},{16,20},{20,16},{24,28},{28,24},{1,5},{5... | collective-permute-start | bytes 1572872 | tf_op jit(solution)/shard_map/ppermute | solution.py:26
  77.9 10.1 %collective-permute-start.21 = (bf16[256,512]{1,0:T(8,128)(2,1)S(1)}, bf16[256,512]{1,0:T(8,128)(2,1)S(1)}, u32[]{:S(2)}, u32[]{:S(2)}) collective-permute-start(bf16[256,512]{1,0:T(8,128)(2,1)S(1)} %get-tuple-element.84), channel_id=1, source_target_pairs={{0,16},{4,12},{8,24},{12,4},{16,0},{20,28},{24,8},{28,20},{1,17},{... | collective-permute-start | bytes 786440 | tf_op jit(solution)/shard_map/ppermute | solution.py:32

commit v14 on v12

--- a/solution.py
+++ b/solution.py
@@ -9,6 +9,7 @@
 
 WHOLE = pl.BlockSpec(memory_space=pltpu.VMEM)
 SCALARS = pl.BlockSpec(memory_space=pltpu.SMEM)
+CHUNKS = 2
 
 
 def bit_count(n):
@@ -124,42 +125,47 @@
     dense_ref, sources = refs[0], refs[1:1 + count]
     rest = refs[1 + count:]
     prev, outs = (rest[:slots], rest[slots:]) if has_prev else (None, rest)
-    rows = outs[0].shape[0]
-    for k, out_ref in reversed(list(enumerate(outs))):
+    rows, width = outs[0].shape
+    for k in reversed(range(slots)):
         total = prev[k][...] if has_prev else None
         for j, source in zip(which, sources):
             part = bf16_dot(dense_ref[j, (base + k) * rows:(base + k + 1) * rows, :], source[...])
             total = part if total is None else total + part
-        out_ref[...] = total.astype(out_ref.dtype)
-
-
-def forward(dense, which, sources, base, prev, dtypes):
+        for c, out_ref in enumerate(outs[k::slots]):
+            out_ref[...] = total[:, c * width:(c + 1) * width].astype(out_ref.dtype)
+
+
+def forward(dense, which, sources, base, prev, dtypes, chunks=1):
     slots = len(dtypes)
     depth, width = sources[0].shape
     rows = slots * depth
-    return pl.pallas_call(
+    out = pl.pallas_call(
         functools.partial(
             forward_kernel, which=which, base=base, slots=slots, has_prev=prev is not None),
-        out_shape=[like((depth, width), dtype) for dtype in dtypes],
+        out_shape=[like((depth, width // chunks), dtype) for dtype in dtypes] * chunks,
         in_specs=[WHOLE] * (1 + len(sources) + (slots if prev is not None else 0)),
-        out_specs=[WHOLE] * slots,
+        out_specs=[WHOLE] * (slots * chunks),
         compiler_params=params(8),
         cost_estimate=pl.CostEstimate(
             flops=2 * len(sources) * rows * depth * width,
             bytes_accessed=2 * len(sources) * rows * depth + 4 * rows * width, transcendentals=0),
         name="forward",
     )(dense, *sources, *(prev or []))
-
-
-def middle_kernel(*refs):
+    return out if chunks == 1 else [out[c * slots:(c + 1) * slots] for c in range(chunks)]
+
+
+def middle_kernel(*refs, counts):
     pieces, (cot_ref, weight_ref, act_ref, agg_ref, pre_grad_ref, grad_ref) = refs[:-6], refs[-6:]
-    agg = pieces[0][...]
-    for piece in pieces[1:]:
-        agg = agg + piece[...].astype(jnp.float32)
-    agg = agg.astype(jnp.bfloat16)
-    agg_ref[...] = agg
+    start = 0
+    width = pieces[0].shape[1]
+    for c, count in enumerate(counts):
+        agg = pieces[start][...]
+        for piece in pieces[start + 1:start + count]:
+            agg = agg + piece[...].astype(jnp.float32)
+        agg_ref[:, c * width:(c + 1) * width] = agg.astype(jnp.bfloat16)
+        start += count
     weight = weight_ref[...]
-    preact = bf16_dot(agg, weight)
+    preact = bf16_dot(agg_ref[...], weight)
     sigma = jax.nn.sigmoid(preact)
     act_ref[...] = (preact * sigma).astype(act_ref.dtype)
     slope = sigma * (1.0 + preact * (1.0 - sigma))
@@ -170,10 +176,11 @@
     ).astype(jnp.bfloat16)
 
 
-def middle(pieces, cotangent, weight):
+def middle(chunks, cotangent, weight):
     rows, width = cotangent.shape
-    return pl.pallas_call(
-        middle_kernel,
+    pieces = [piece for chunk in chunks for piece in chunk]
+    return pl.pallas_call(
+        functools.partial(middle_kernel, counts=[len(chunk) for chunk in chunks]),
         out_shape=[like((rows, width), jnp.bfloat16)] * 4,
         in_specs=[WHOLE] * (2 + len(pieces)),
         out_specs=[WHOLE] * 4,
@@ -319,6 +326,22 @@
     return [total + got[k * rows:(k + 1) * rows].astype(jnp.float32) for k, total in enumerate(totals)]
 
 
+def add_kernel(total_ref, got_ref, out_ref):
+    out_ref[...] = (total_ref[...].astype(jnp.float32) + got_ref[...].astype(jnp.float32)).astype(out_ref.dtype)
+
+
+def add_rounded(total, got):
+    return pl.pallas_call(
+        add_kernel,
+        out_shape=like(total.shape, jnp.bfloat16),
+        in_specs=[WHOLE] * 2,
+        out_specs=WHOLE,
+        compiler_params=params(4),
+        cost_estimate=pl.CostEstimate(flops=total.size, bytes_accessed=8 * total.size, transcendentals=0),
+        name="add_rounded",
+    )(total, got)
+
+
 def collect(totals, swap):
     totals = list(totals)
     arrived = []
@@ -327,7 +350,7 @@
         if k == top_bit(k):
             arrived.append(got)
         else:
-            totals[k - top_bit(k)] = totals[k - top_bit(k)].astype(jnp.float32) + got.astype(jnp.float32)
+            totals[k - top_bit(k)] = add_rounded(totals[k - top_bit(k)], got)
     return [totals[0], *arrived]
 
 
@@ -359,13 +382,12 @@
     others = [swap_cores(own) for own in far]
     totals = forward(dense, list(range(2 * half, 2 * chips, 2)), far, 0, totals, [jnp.float32] * groups)
     odd = list(range(2 * half + 1, 2 * chips, 2))
-    high = forward(dense, odd, others, upper, totals[upper:], [jnp.bfloat16] * upper)
-    low = forward(after(dense, *high), odd, others, 0, totals[:upper], [jnp.float32] * upper)
-    totals = low + high
-
-    pieces = collect(totals, swap_members)
-    dense_t = transposed(after(dense, *totals, pieces[1]))
-    pieces[-1] = after(pieces[-1], *dense_t)
+    high = forward(dense, odd, others, upper, totals[upper:], [jnp.bfloat16] * upper, CHUNKS)
+    low = forward(after(dense, *high[0]), odd, others, 0, totals[:upper], [jnp.float32] * upper, CHUNKS)
+
+    pieces = [collect([*x, *y], swap_members) for x, y in zip(low, high)]
+    dense_t = transposed(after(dense, *high[0], *[piece[1] for piece in pieces]))
+    pieces[-1][-1] = after(pieces[-1][-1], *dense_t)
     activated, agg, pre_grad, grad = middle(pieces, cotangent, weight)
     owns, send = weight_part(agg, pre_grad, place, groups)
     parts = add_slots(owns, swap_cores(send))

time: 88.8 us -> 88.6 us (level)
  starting transfers between devices: 32.4 us -> 35.4 us
  waiting for transfers between devices: 36.9 us -> 34 us
    ppermute x12 -> x15, waiting for transfers between devices: 14.9 us -> 11.7 us  [swap_members(): return lax.ppermute(x, ('dom', 'repl'), pairs)]
    ppermute x12 -> x15, starting transfers between devices: 15.7 us -> 18.7 us  [swap_members(): return lax.ppermute(x, ('dom', 'repl'), pairs)]
  transfers between devices with their start and end apart: 27 -> 30, of which waited for: 15 -> 15; matrix products, arithmetic and copies ran while one was open for 2% -> 2% of each run, Pallas kernels for 11% -> 11%
where the time goes in v14:
time: 88.6 us; the launch traced here: 88.4 us
  starting transfers between devices  35.4 us (40%)
  waiting for transfers between devices  34 us (38%)
  Pallas kernels  14 us (16%)
  local copies, waits for them, and re-layouts  2.93 us (3%)
  other arithmetic  1.24 us (1%)
  between operations  0.89 us (1%)
    ppermute x7, waiting for transfers between devices, swap_chips(): lax.ppermute(x, 'dom', [(i, i ^ 2 * between(held, i % 2, bits)) for i in...  21.4 us
    ppermute x15, starting transfers between devices, swap_members(): return lax.ppermute(x, ('dom', 'repl'), pairs)  18.7 us
    ppermute x7, starting transfers between devices, swap_chips(): lax.ppermute(x, 'dom', [(i, i ^ 2 * between(held, i % 2, bits)) for i in...  15.7 us
    ppermute x15, waiting for transfers between devices, swap_members(): return lax.ppermute(x, ('dom', 'repl'), pairs)  11.7 us
    pallas_call x4, Pallas kernels, forward(): pl.pallas_call(functools.partial(forward_kernel, which=which, base=base,...  2.82 us
    pallas_call x4, Pallas kernels, backward(): pl.pallas_call(functools.partial(backward_kernel, side=side, count=count,...  2.81 us
    pallas_call x1, Pallas kernels, densify(): pl.pallas_call(functools.partial(densify_kernel, col_tiles=col_tiles), ou...  2.54 us
    unnamed x8, local copies, waits for them, and re-layouts  2.2 us
  transfers between devices with their start and end apart: 30, of which 15 were waited for; matrix products, arithmetic and copies ran while one was open for 2% of the time, Pallas kernels for 11%

profile of v14, /device:TPU:0, one launch (start us, length us, event | category | flops | bytes accessed | tf_op | source)
XLA Modules:
  0.0 88.4 jit_solution(11222628382518249616)
XLA Ops:
  0.6 4.1 %collective-permute-start = (bf16[256,512]{1,0:T(8,128)(2,1)}, bf16[256,512]{1,0:T(8,128)(2,1)S(1)}, u32[]{:S(2)}, u32[]{:S(2)}) collective-permute-start(bf16[256,512]{1,0:T(8,128)(2,1)} %refs_1_.1), channel_id=1, source_target_pairs={{0,16},{4,12},{8,24},{12,4},{16,0},{20,28},{24,8},{28,20},{1,17},{... | collective-permute-start | bytes 786440 | tf_op jit(solution)/shard_map/ppermute | solution.py:33
  6.3 4.6 %collective-permute-done.refs_3_ = bf16[256,512]{1,0:T(8,128)(2,1)S(1)} collective-permute-done((bf16[256,512]{1,0:T(8,128)(2,1)}, bf16[256,512]{1,0:T(8,128)(2,1)S(1)}, u32[]{:S(2)}, u32[]{:S(2)}) %collective-permute-start) | collective-permute-done | bytes 262176 | tf_op jit(solution)/shard_map/ppermute | solution.py:33
  10.9 2.4 %collective-permute-start.1 = (bf16[256,512]{1,0:T(8,128)(2,1)}, bf16[256,512]{1,0:T(8,128)(2,1)S(1)}, u32[]{:S(2)}, u32[]{:S(2)}) collective-permute-start(bf16[256,512]{1,0:T(8,128)(2,1)} %refs_1_.1), channel_id=1, source_target_pairs={{0,8},{4,20},{8,0},{12,28},{16,24},{20,4},{24,16},{28,12},{1,9},{5... | collective-permute-start | bytes 786440 | tf_op jit(solution)/shard_map/ppermute | solution.py:33
  13.4 2.2 %copy-done = bf16[1,1,8,16,128,128]{5,4,3,2,1,0:T(8,128)(2,1)S(1)} copy-done((bf16[1,1,8,16,128,128]{5,4,3,2,1,0:T(8,128)(2,1)S(1)}, bf16[1,1,8,16,128,128]{5,4,3,2,1,0:T(8,128)(2,1)}, u32[]{:S(2)}) %copy-start) | copy-done | bytes 4194328
  15.6 2.5 %densify.1.refs_0_.a_ref = bf16[8,1024,256]{2,1,0:T(8,128)(2,1)S(1)} custom-call(s32[8,17]{1,0:T(8,128)S(1)} %pad_add_fusion.spots_ref, s32[2]{0:T(128)S(1)} %pad_add_fusion.1.place_ref, bf16[8,16,128,128]{3,2,1,0:T(8,128)(2,1)S(1)} %bitcast.26), custom_call_target="tpu_custom_call" | custom-call | flops 2097152 | bytes 16777216 | tf_op jit(solution)/shard_map/densify/pallas_call | solution.py:87
  18.2 1.2 %forward.4 = (f32[256,512]{1,0:T(8,128)S(1)}, f32[256,512]{1,0:T(8,128)S(1)}, f32[256,512]{1,0:T(8,128)S(1)}, f32[256,512]{1,0:T(8,128)S(1)}) custom-call(bf16[8,1024,256]{2,1,0:T(8,128)(2,1)S(1)} %densify.1.refs_0_.a_ref, bf16[256,512]{1,0:T(8,128)(2,1)S(1)} %copy-done.2, bf16[256,512]{1,0:T(8,128)(2,1)S(1)} %collective-permute-done.2.refs_2_, ...), custom_call_target="tpu_custom_call" | custom-call | flops 1073741824 | bytes 4194304 | tf_op jit(solution)/shard_map/forward/pallas_call | solution.py:142
  19.4 3.5 %collective-permute-done.1.refs_1_ = bf16[256,512]{1,0:T(8,128)(2,1)S(1)} collective-permute-done((bf16[256,512]{1,0:T(8,128)(2,1)}, bf16[256,512]{1,0:T(8,128)(2,1)S(1)}, u32[]{:S(2)}, u32[]{:S(2)}) %collective-permute-start.1) | collective-permute-done | bytes 262176 | tf_op jit(solution)/shard_map/ppermute | solution.py:33
  22.9 3.4 %collective-permute-done.5.refs_2_ = bf16[256,512]{1,0:T(8,128)(2,1)S(1)} collective-permute-done((bf16[256,512]{1,0:T(8,128)(2,1)S(1)}, bf16[256,512]{1,0:T(8,128)(2,1)S(1)}, u32[]{:S(2)}, u32[]{:S(2)}) %collective-permute-start.5) | collective-permute-done | bytes 262176 | tf_op jit(solution)/shard_map/ppermute | solution.py:33
  28.3 1.7 %collective-permute-start.11 = (bf16[256,256]{1,0:T(8,128)(2,1)S(1)}, bf16[256,256]{1,0:T(8,128)(2,1)S(1)}, u32[]{:S(2)}, u32[]{:S(2)}) collective-permute-start(bf16[256,256]{1,0:T(8,128)(2,1)S(1)} %get-tuple-element.68), channel_id=1, source_target_pairs={{0,1},{1,0},{2,3},{3,2},{4,6},{5,7},{6,4},{7,5},{8,9},{9,8},{10,11... | collective-permute-start | bytes 393224 | tf_op jit(solution)/shard_map/ppermute | solution.py:43
  30.4 1.7 %collective-permute-start.7 = (bf16[256,256]{1,0:T(8,128)(2,1)S(1)}, bf16[256,256]{1,0:T(8,128)(2,1)S(1)}, u32[]{:S(2)}, u32[]{:S(2)}) collective-permute-start(bf16[256,256]{1,0:T(8,128)(2,1)S(1)} %get-tuple-element.58), channel_id=1, source_target_pairs={{0,1},{1,0},{2,3},{3,2},{4,6},{5,7},{6,4},{7,5},{8,9},{9,8},{10,11... | collective-permute-start | bytes 393224 | tf_op jit(solution)/shard_map/ppermute | solution.py:43
  33.3 1.8 %collective-permute-start.12 = (bf16[256,256]{1,0:T(8,128)(2,1)S(1)}, bf16[256,256]{1,0:T(8,128)(2,1)S(1)}, u32[]{:S(2)}, u32[]{:S(2)}) collective-permute-start(bf16[256,256]{1,0:T(8,128)(2,1)S(1)} %add_rounded.3), channel_id=1, source_target_pairs={{0,2},{1,3},{2,0},{3,1},{4,5},{5,4},{6,7},{7,6},{8,10},{9,11},{10,... | collective-permute-start | bytes 393224 | tf_op jit(solution)/shard_map/ppermute | solution.py:43
  35.1 1.5 %collective-permute-start.9 = (bf16[256,256]{1,0:T(8,128)(2,1)S(1)}, bf16[256,256]{1,0:T(8,128)(2,1)S(1)}, u32[]{:S(2)}, u32[]{:S(2)}) collective-permute-start(bf16[256,256]{1,0:T(8,128)(2,1)S(1)} %add_rounded.2), channel_id=1, source_target_pairs={{0,2},{1,3},{2,0},{3,1},{4,5},{5,4},{6,7},{7,6},{8,10},{9,11},{10,... | collective-permute-start | bytes 393224 | tf_op jit(solution)/shard_map/ppermute | solution.py:43
  37.4 2.8 %collective-permute-done.10.refs_4_ = bf16[256,256]{1,0:T(8,128)(2,1)S(1)} collective-permute-done((bf16[256,256]{1,0:T(8,128)(2,1)S(1)}, bf16[256,256]{1,0:T(8,128)(2,1)S(1)}, u32[]{:S(2)}, u32[]{:S(2)}) %collective-permute-start.10) | collective-permute-done | bytes 131104 | tf_op jit(solution)/shard_map/ppermute | solution.py:43
  40.2 1.2 %transposed.1 = (bf16[2,256,1024]{2,1,0:T(8,128)(2,1)S(1)}, bf16[2,256,1024]{2,1,0:T(8,128)(2,1)S(1)}, bf16[2,256,1024]{2,1,0:T(8,128)(2,1)S(1)}, bf16[2,256,1024]{2,1,0:T(8,128)(2,1)S(1)}) custom-call(bf16[8,1024,256]{2,1,0:T(8,128)(2,1)S(1)} %densify.1.refs_0_.a_ref), custom_call_target="tpu_custom_call" | custom-call | bytes 8388608 | tf_op jit(solution)/shard_map/transposed/pallas_call | solution.py:112
  41.5 1.2 %middle.1 = (bf16[256,512]{1,0:T(8,128)(2,1)}, bf16[256,512]{1,0:T(8,128)(2,1)S(1)}, bf16[256,512]{1,0:T(8,128)(2,1)S(1)}, bf16[256,512]{1,0:T(8,128)(2,1)S(1)}) custom-call(f32[256,256]{1,0:T(8,128)S(1)} %get-tuple-element.63.refs_0_, bf16[256,256]{1,0:T(8,128)(2,1)S(1)} %collective-permute-done.7.refs_1_, ...), custom_call_target="tpu_custom_call" | custom-call | flops 268435456 | bytes 1310720 | tf_op jit(solution)/shard_map/middle/pallas_call | solution.py:182
  43.7 1.4 %collective-permute-start.13 = (bf16[256,512]{1,0:T(8,128)(2,1)S(1)}, bf16[256,512]{1,0:T(8,128)(2,1)S(1)}, u32[]{:S(2)}, u32[]{:S(2)}) collective-permute-start(bf16[256,512]{1,0:T(8,128)(2,1)S(1)} %get-tuple-element.88.refs_2_), channel_id=1, source_target_pairs={{0,2},{1,3},{2,0},{3,1},{4,5},{5,4},{6,7},{7,6},{8,10},{9,11},{10,... | collective-permute-start | bytes 786440 | tf_op jit(solution)/shard_map/ppermute | solution.py:43
  45.2 2.2 %collective-permute-start.19 = (bf16[64,512]{1,0:T(8,128)(2,1)S(1)}, bf16[64,512]{1,0:T(8,128)(2,1)S(1)}, u32[]{:S(2)}, u32[]{:S(2)}) collective-permute-start(bf16[64,512]{1,0:T(8,128)(2,1)S(1)} %get-tuple-element.96), channel_id=1, source_target_pairs={{0,3},{1,2},{2,1},{3,0},{4,7},{5,6},{6,5},{7,4},{8,11},{9,10},{10,... | collective-permute-start | bytes 196616 | tf_op jit(solution)/shard_map/ppermute | solution.py:43
  48.8 1.2 %collective-permute-start.14 = (bf16[256,512]{1,0:T(8,128)(2,1)S(1)}, bf16[256,512]{1,0:T(8,128)(2,1)S(1)}, u32[]{:S(2)}, u32[]{:S(2)}) collective-permute-start(bf16[256,512]{1,0:T(8,128)(2,1)S(1)} %get-tuple-element.88.refs_2_), channel_id=1, source_target_pairs={{0,1},{1,0},{2,3},{3,2},{4,6},{5,7},{6,4},{7,5},{8,9},{9,8},{10,11... | collective-permute-start | bytes 786440 | tf_op jit(solution)/shard_map/ppermute | solution.py:43
  50.6 1.7 %collective-permute-start.15 = (bf16[256,512]{1,0:T(8,128)(2,1)S(1)}, bf16[256,512]{1,0:T(8,128)(2,1)S(1)}, u32[]{:S(2)}, u32[]{:S(2)}) collective-permute-start(bf16[256,512]{1,0:T(8,128)(2,1)S(1)} %collective-permute-done.13.refs_3_), channel_id=1, source_target_pairs={{0,1},{1,0},{2,3},{3,2},{4,6},{5,7},{6,4},{7,5},{8,9},{9,8},{10,11... | collective-permute-start | bytes 786440 | tf_op jit(solution)/shard_map/ppermute | solution.py:43
  52.3 1.0 %collective-permute-done.18 = bf16[64,512]{1,0:T(8,128)(2,1)S(1)} collective-permute-done((bf16[64,512]{1,0:T(8,128)(2,1)S(1)}, bf16[64,512]{1,0:T(8,128)(2,1)S(1)}, u32[]{:S(2)}, u32[]{:S(2)}) %collective-permute-start.18) | collective-permute-done | bytes 65568 | tf_op jit(solution)/shard_map/ppermute | solution.py:43
  53.3 2.9 %collective-permute-start.20 = (bf16[64,512]{1,0:T(8,128)(2,1)S(1)}, bf16[64,512]{1,0:T(8,128)(2,1)S(1)}, u32[]{:S(2)}, u32[]{:S(2)}) collective-permute-start(bf16[64,512]{1,0:T(8,128)(2,1)S(1)} %add_convert_fusion.3), channel_id=1, source_target_pairs={{0,16},{4,12},{8,24},{12,4},{16,0},{20,28},{24,8},{28,20},{1,17},{... | collective-permute-start | bytes 196616 | tf_op jit(solution)/shard_map/ppermute | solution.py:33
  56.2 2.4 %collective-permute-done.20 = bf16[64,512]{1,0:T(8,128)(2,1)S(1)} collective-permute-done((bf16[64,512]{1,0:T(8,128)(2,1)S(1)}, bf16[64,512]{1,0:T(8,128)(2,1)S(1)}, u32[]{:S(2)}, u32[]{:S(2)}) %collective-permute-start.20) | collective-permute-done | bytes 65568 | tf_op jit(solution)/shard_map/ppermute | solution.py:33
  59.5 2.1 %collective-permute-start.25 = (bf16[64,512]{1,0:T(8,128)(2,1)S(1)}, bf16[64,512]{1,0:T(8,128)(2,1)S(1)}, u32[]{:S(2)}, u32[]{:S(2)}) collective-permute-start(bf16[64,512]{1,0:T(8,128)(2,1)S(1)} %add_convert_fusion.2), channel_id=1, source_target_pairs={{0,8},{4,20},{8,0},{12,28},{16,24},{20,4},{24,16},{28,12},{1,9},{5... | collective-permute-start | bytes 196616 | tf_op jit(solution)/shard_map/ppermute | solution.py:33
  62.4 1.1 %collective-permute-start.23 = (bf16[512,512]{1,0:T(8,128)(2,1)S(1)}, bf16[512,512]{1,0:T(8,128)(2,1)S(1)}, u32[]{:S(2)}, u32[]{:S(2)}) collective-permute-start(bf16[512,512]{1,0:T(8,128)(2,1)S(1)} %pad_maximum_fusion), channel_id=1, source_target_pairs={{0,8},{4,20},{8,0},{12,28},{16,24},{20,4},{24,16},{28,12},{1,9},{5... | collective-permute-start | bytes 1572872 | tf_op jit(solution)/shard_map/ppermute | solution.py:33
  65.0 1.1 %collective-permute-start.26 = (f32[64,512]{1,0:T(8,128)S(1)}, f32[64,512]{1,0:T(8,128)S(1)}, u32[]{:S(2)}, u32[]{:S(2)}) collective-permute-start(f32[64,512]{1,0:T(8,128)S(1)} %add_multiply_fusion.refs_0_), channel_id=1, source_target_pairs={{0,1},{1,0},{2,3},{3,2},{4,6},{5,7},{6,4},{7,5},{8,9},{9,8},{10,11... | collective-permute-start | bytes 393224 | tf_op jit(solution)/shard_map/ppermute | solution.py:43
  66.0 2.0 %collective-permute-start.27 = (f32[64,512]{1,0:T(8,128)S(1)}, f32[64,512]{1,0:T(8,128)S(1)}, u32[]{:S(2)}, u32[]{:S(2)}) collective-permute-start(f32[64,512]{1,0:T(8,128)S(1)} %add_multiply_fusion.refs_0_), channel_id=1, source_target_pairs={{0,2},{1,3},{2,0},{3,1},{4,5},{5,4},{6,7},{7,6},{8,10},{9,11},{10,... | collective-permute-start | bytes 393224 | tf_op jit(solution)/shard_map/ppermute | solution.py:43
  68.5 2.5 %collective-permute-done.26.refs_1_ = f32[64,512]{1,0:T(8,128)S(1)} collective-permute-done((f32[64,512]{1,0:T(8,128)S(1)}, f32[64,512]{1,0:T(8,128)S(1)}, u32[]{:S(2)}, u32[]{:S(2)}) %collective-permute-start.26) | collective-permute-done | bytes 131104 | tf_op jit(solution)/shard_map/ppermute | solution.py:43
  71.0 3.5 %collective-permute-done.28.refs_3_ = f32[64,512]{1,0:T(8,128)S(1)} collective-permute-done((f32[64,512]{1,0:T(8,128)S(1)}, f32[64,512]{1,0:T(8,128)S(1)}, u32[]{:S(2)}, u32[]{:S(2)}) %collective-permute-start.28) | collective-permute-done | bytes 131104 | tf_op jit(solution)/shard_map/ppermute | solution.py:43
  75.3 2.0 %collective-permute-done.23.refs_3_ = bf16[512,512]{1,0:T(8,128)(2,1)S(1)} collective-permute-done((bf16[512,512]{1,0:T(8,128)(2,1)S(1)}, bf16[512,512]{1,0:T(8,128)(2,1)S(1)}, u32[]{:S(2)}, u32[]{:S(2)}) %collective-permute-start.23) | collective-permute-done | bytes 524320 | tf_op jit(solution)/shard_map/ppermute | solution.py:33
  77.5 3.0 %collective-permute-start.24 = (bf16[256,512]{1,0:T(8,128)(2,1)S(1)}, bf16[256,512]{1,0:T(8,128)(2,1)S(1)}, u32[]{:S(2)}, u32[]{:S(2)}) collective-permute-start(bf16[256,512]{1,0:T(8,128)(2,1)S(1)} %get-tuple-element.92), channel_id=1, source_target_pairs={{0,16},{4,12},{8,24},{12,4},{16,0},{20,28},{24,8},{28,20},{1,17},{... | collective-permute-start | bytes 786440 | tf_op jit(solution)/shard_map/ppermute | solution.py:33
  80.5 1.6 %place_slices.1 = f32[512,512]{1,0:T(8,128)} custom-call(s32[2]{0:T(128)S(1)} %pad_add_fusion.1.place_ref, f32[64,512]{1,0:T(8,128)S(1)} %add_multiply_fusion.refs_0_, f32[64,512]{1,0:T(8,128)S(1)} %collective-permute-done.26.refs_1_, f32[64,512]{1,0:T(8,128)S(1)} %collective-permute-done.27.refs_2_, f32[64,512]{1,0:T(8,128)S(1)} %collective-permute-done.28.refs_3_, ...), custom_call_target="tpu_custom_call" | custom-call | bytes 2097152 | tf_op jit(solution)/shard_map/place_slices/pallas_call | solution.py:243
  82.1 5.6 %collective-permute-done.24.refs_1_ = bf16[256,512]{1,0:T(8,128)(2,1)S(1)} collective-permute-done((bf16[256,512]{1,0:T(8,128)(2,1)S(1)}, bf16[256,512]{1,0:T(8,128)(2,1)S(1)}, u32[]{:S(2)}, u32[]{:S(2)}) %collective-permute-start.24) | collective-permute-done | bytes 262176 | tf_op jit(solution)/shard_map/ppermute | solution.py:33
  (64 shorter events, 14.7 us)
Async XLA Ops:
  0.6 10.2 %collective-permute-start = (bf16[256,512]{1,0:T(8,128)(2,1)}, bf16[256,512]{1,0:T(8,128)(2,1)S(1)}, u32[]{:S(2)}, u32[]{:S(2)}) collective-permute-start(bf16[256,512]{1,0:T(8,128)(2,1)} %refs_1_.1), channel_id=1, source_target_pairs={{0,16},{4,12},{8,24},{12,4},{16,0},{20,28},{24,8},{28,20},{1,17},{... | collective-permute-start | bytes 786440 | tf_op jit(solution)/shard_map/ppermute | solution.py:33
  4.7 13.4 %collective-permute-start.2 = (bf16[256,512]{1,0:T(8,128)(2,1)}, bf16[256,512]{1,0:T(8,128)(2,1)S(1)}, u32[]{:S(2)}, u32[]{:S(2)}) collective-permute-start(bf16[256,512]{1,0:T(8,128)(2,1)} %refs_1_.1), channel_id=1, source_target_pairs={{0,4},{4,0},{8,12},{12,8},{16,20},{20,16},{24,28},{28,24},{1,5},{5... | collective-permute-start | bytes 786440 | tf_op jit(solution)/shard_map/ppermute | solution.py:27
  10.9 7.3 %collective-permute-start.3 = (bf16[256,512]{1,0:T(8,128)(2,1)S(1)}, bf16[256,512]{1,0:T(8,128)(2,1)S(1)}, u32[]{:S(2)}, u32[]{:S(2)}) collective-permute-start(bf16[256,512]{1,0:T(8,128)(2,1)S(1)} %collective-permute-done.refs_3_), channel_id=1, source_target_pairs={{0,4},{4,0},{8,12},{12,8},{16,20},{20,16},{24,28},{28,24},{1,5},{5... | collective-permute-start | bytes 786440 | tf_op jit(solution)/shard_map/ppermute | solution.py:27
  10.9 12.1 %collective-permute-start.1 = (bf16[256,512]{1,0:T(8,128)(2,1)}, bf16[256,512]{1,0:T(8,128)(2,1)S(1)}, u32[]{:S(2)}, u32[]{:S(2)}) collective-permute-start(bf16[256,512]{1,0:T(8,128)(2,1)} %refs_1_.1), channel_id=1, source_target_pairs={{0,8},{4,20},{8,0},{12,28},{16,24},{20,4},{24,16},{28,12},{1,9},{5... | collective-permute-start | bytes 786440 | tf_op jit(solution)/shard_map/ppermute | solution.py:33
  13.3 13.0 %collective-permute-start.5 = (bf16[256,512]{1,0:T(8,128)(2,1)S(1)}, bf16[256,512]{1,0:T(8,128)(2,1)S(1)}, u32[]{:S(2)}, u32[]{:S(2)}) collective-permute-start(bf16[256,512]{1,0:T(8,128)(2,1)S(1)} %collective-permute-done.refs_3_), channel_id=1, source_target_pairs={{0,8},{4,20},{8,0},{12,28},{16,24},{20,4},{24,16},{28,12},{1,9},{5... | collective-permute-start | bytes 786440 | tf_op jit(solution)/shard_map/ppermute | solution.py:33
  22.9 4.1 %collective-permute-start.4 = (bf16[256,512]{1,0:T(8,128)(2,1)S(1)}, bf16[256,512]{1,0:T(8,128)(2,1)S(1)}, u32[]{:S(2)}, u32[]{:S(2)}) collective-permute-start(bf16[256,512]{1,0:T(8,128)(2,1)S(1)} %collective-permute-done.1.refs_1_), channel_id=1, source_target_pairs={{0,4},{4,0},{8,12},{12,8},{16,20},{20,16},{24,28},{28,24},{1,5},{5... | collective-permute-start | bytes 786440 | tf_op jit(solution)/shard_map/ppermute | solution.py:27
  26.3 1.5 %collective-permute-start.6 = (bf16[256,512]{1,0:T(8,128)(2,1)S(1)}, bf16[256,512]{1,0:T(8,128)(2,1)S(1)}, u32[]{:S(2)}, u32[]{:S(2)}) collective-permute-start(bf16[256,512]{1,0:T(8,128)(2,1)S(1)} %collective-permute-done.5.refs_2_), channel_id=1, source_target_pairs={{0,4},{4,0},{8,12},{12,8},{16,20},{20,16},{24,28},{28,24},{1,5},{5... | collective-permute-start | bytes 786440 | tf_op jit(solution)/shard_map/ppermute | solution.py:27
  28.3 5.0 %collective-permute-start.11 = (bf16[256,256]{1,0:T(8,128)(2,1)S(1)}, bf16[256,256]{1,0:T(8,128)(2,1)S(1)}, u32[]{:S(2)}, u32[]{:S(2)}) collective-permute-start(bf16[256,256]{1,0:T(8,128)(2,1)S(1)} %get-tuple-element.68), channel_id=1, source_target_pairs={{0,1},{1,0},{2,3},{3,2},{4,6},{5,7},{6,4},{7,5},{8,9},{9,8},{10,11... | collective-permute-start | bytes 393224 | tf_op jit(solution)/shard_map/ppermute | solution.py:43
  30.0 5.1 %collective-permute-start.8 = (bf16[256,256]{1,0:T(8,128)(2,1)S(1)}, bf16[256,256]{1,0:T(8,128)(2,1)S(1)}, u32[]{:S(2)}, u32[]{:S(2)}) collective-permute-start(bf16[256,256]{1,0:T(8,128)(2,1)S(1)} %get-tuple-element.59), channel_id=1, source_target_pairs={{0,1},{1,0},{2,3},{3,2},{4,6},{5,7},{6,4},{7,5},{8,9},{9,8},{10,11... | collective-permute-start | bytes 393224 | tf_op jit(solution)/shard_map/ppermute | solution.py:43
  30.4 7.1 %collective-permute-start.7 = (bf16[256,256]{1,0:T(8,128)(2,1)S(1)}, bf16[256,256]{1,0:T(8,128)(2,1)S(1)}, u32[]{:S(2)}, u32[]{:S(2)}) collective-permute-start(bf16[256,256]{1,0:T(8,128)(2,1)S(1)} %get-tuple-element.58), channel_id=1, source_target_pairs={{0,1},{1,0},{2,3},{3,2},{4,6},{5,7},{6,4},{7,5},{8,9},{9,8},{10,11... | collective-permute-start | bytes 393224 | tf_op jit(solution)/shard_map/ppermute | solution.py:43
  32.0 8.2 %collective-permute-start.10 = (bf16[256,256]{1,0:T(8,128)(2,1)S(1)}, bf16[256,256]{1,0:T(8,128)(2,1)S(1)}, u32[]{:S(2)}, u32[]{:S(2)}) collective-permute-start(bf16[256,256]{1,0:T(8,128)(2,1)S(1)} %get-tuple-element.66), channel_id=1, source_target_pairs={{0,1},{1,0},{2,3},{3,2},{4,6},{5,7},{6,4},{7,5},{8,9},{9,8},{10,11... | collective-permute-start | bytes 393224 | tf_op jit(solution)/shard_map/ppermute | solution.py:43
  32.4 9.1 %copy-start.1 = (bf16[512,512]{1,0:T(8,128)(2,1)S(1)}, bf16[512,512]{1,0:T(8,128)(2,1)}, u32[]{:S(2)}) copy-start(bf16[512,512]{1,0:T(8,128)(2,1)} %refs_7_.1) | copy-start | bytes 1572868
  32.4 9.1 %copy-start.3 = (bf16[256,512]{1,0:T(8,128)(2,1)S(1)}, bf16[256,512]{1,0:T(8,128)(2,1)}, u32[]{:S(2)}) copy-start(bf16[256,512]{1,0:T(8,128)(2,1)} %refs_6_.1) | copy-start | bytes 786436
  33.3 8.1 %collective-permute-start.12 = (bf16[256,256]{1,0:T(8,128)(2,1)S(1)}, bf16[256,256]{1,0:T(8,128)(2,1)S(1)}, u32[]{:S(2)}, u32[]{:S(2)}) collective-permute-start(bf16[256,256]{1,0:T(8,128)(2,1)S(1)} %add_rounded.3), channel_id=1, source_target_pairs={{0,2},{1,3},{2,0},{3,1},{4,5},{5,4},{6,7},{7,6},{8,10},{9,11},{10,... | collective-permute-start | bytes 393224 | tf_op jit(solution)/shard_map/ppermute | solution.py:43
  35.1 6.3 %collective-permute-start.9 = (bf16[256,256]{1,0:T(8,128)(2,1)S(1)}, bf16[256,256]{1,0:T(8,128)(2,1)S(1)}, u32[]{:S(2)}, u32[]{:S(2)}) collective-permute-start(bf16[256,256]{1,0:T(8,128)(2,1)S(1)} %add_rounded.2), channel_id=1, source_target_pairs={{0,2},{1,3},{2,0},{3,1},{4,5},{5,4},{6,7},{7,6},{8,10},{9,11},{10,... | collective-permute-start | bytes 393224 | tf_op jit(solution)/shard_map/ppermute | solution.py:43
  43.6 1.6 %collective-permute-start.16 = (bf16[256,512]{1,0:T(8,128)(2,1)S(1)}, bf16[256,512]{1,0:T(8,128)(2,1)S(1)}, u32[]{:S(2)}, u32[]{:S(2)}) collective-permute-start(bf16[256,512]{1,0:T(8,128)(2,1)S(1)} %get-tuple-element.80), channel_id=1, source_target_pairs={{0,4},{4,0},{8,12},{12,8},{16,20},{20,16},{24,28},{28,24},{1,5},{5... | collective-permute-start | bytes 786440 | tf_op jit(solution)/shard_map/ppermute | solution.py:27
  43.7 6.9 %collective-permute-start.13 = (bf16[256,512]{1,0:T(8,128)(2,1)S(1)}, bf16[256,512]{1,0:T(8,128)(2,1)S(1)}, u32[]{:S(2)}, u32[]{:S(2)}) collective-permute-start(bf16[256,512]{1,0:T(8,128)(2,1)S(1)} %get-tuple-element.88.refs_2_), channel_id=1, source_target_pairs={{0,2},{1,3},{2,0},{3,1},{4,5},{5,4},{6,7},{7,6},{8,10},{9,11},{10,... | collective-permute-start | bytes 786440 | tf_op jit(solution)/shard_map/ppermute | solution.py:43
  45.2 7.0 %collective-permute-start.19 = (bf16[64,512]{1,0:T(8,128)(2,1)S(1)}, bf16[64,512]{1,0:T(8,128)(2,1)S(1)}, u32[]{:S(2)}, u32[]{:S(2)}) collective-permute-start(bf16[64,512]{1,0:T(8,128)(2,1)S(1)} %get-tuple-element.96), channel_id=1, source_target_pairs={{0,3},{1,2},{2,1},{3,0},{4,7},{5,6},{6,5},{7,4},{8,11},{9,10},{10,... | collective-permute-start | bytes 196616 | tf_op jit(solution)/shard_map/ppermute | solution.py:43
  47.4 5.8 %collective-permute-start.18 = (bf16[64,512]{1,0:T(8,128)(2,1)S(1)}, bf16[64,512]{1,0:T(8,128)(2,1)S(1)}, u32[]{:S(2)}, u32[]{:S(2)}) collective-permute-start(bf16[64,512]{1,0:T(8,128)(2,1)S(1)} %get-tuple-element.97), channel_id=1, source_target_pairs={{0,2},{1,3},{2,0},{3,1},{4,5},{5,4},{6,7},{7,6},{8,10},{9,11},{10,... | collective-permute-start | bytes 196616 | tf_op jit(solution)/shard_map/ppermute | solution.py:43
  48.0 5.3 %collective-permute-start.17 = (bf16[64,512]{1,0:T(8,128)(2,1)S(1)}, bf16[64,512]{1,0:T(8,128)(2,1)S(1)}, u32[]{:S(2)}, u32[]{:S(2)}) collective-permute-start(bf16[64,512]{1,0:T(8,128)(2,1)S(1)} %get-tuple-element.95), channel_id=1, source_target_pairs={{0,1},{1,0},{2,3},{3,2},{4,6},{5,7},{6,4},{7,5},{8,9},{9,8},{10,11... | collective-permute-start | bytes 196616 | tf_op jit(solution)/shard_map/ppermute | solution.py:43
  48.8 9.7 %collective-permute-start.14 = (bf16[256,512]{1,0:T(8,128)(2,1)S(1)}, bf16[256,512]{1,0:T(8,128)(2,1)S(1)}, u32[]{:S(2)}, u32[]{:S(2)}) collective-permute-start(bf16[256,512]{1,0:T(8,128)(2,1)S(1)} %get-tuple-element.88.refs_2_), channel_id=1, source_target_pairs={{0,1},{1,0},{2,3},{3,2},{4,6},{5,7},{6,4},{7,5},{8,9},{9,8},{10,11... | collective-permute-start | bytes 786440 | tf_op jit(solution)/shard_map/ppermute | solution.py:43
  50.6 7.9 %collective-permute-start.15 = (bf16[256,512]{1,0:T(8,128)(2,1)S(1)}, bf16[256,512]{1,0:T(8,128)(2,1)S(1)}, u32[]{:S(2)}, u32[]{:S(2)}) collective-permute-start(bf16[256,512]{1,0:T(8,128)(2,1)S(1)} %collective-permute-done.13.refs_3_), channel_id=1, source_target_pairs={{0,1},{1,0},{2,3},{3,2},{4,6},{5,7},{6,4},{7,5},{8,9},{9,8},{10,11... | collective-permute-start | bytes 786440 | tf_op jit(solution)/shard_map/ppermute | solution.py:43
  53.3 5.2 %collective-permute-start.20 = (bf16[64,512]{1,0:T(8,128)(2,1)S(1)}, bf16[64,512]{1,0:T(8,128)(2,1)S(1)}, u32[]{:S(2)}, u32[]{:S(2)}) collective-permute-start(bf16[64,512]{1,0:T(8,128)(2,1)S(1)} %add_convert_fusion.3), channel_id=1, source_target_pairs={{0,16},{4,12},{8,24},{12,4},{16,0},{20,28},{24,8},{28,20},{1,17},{... | collective-permute-start | bytes 196616 | tf_op jit(solution)/shard_map/ppermute | solution.py:33
  59.2 3.0 %collective-permute-start.21 = (bf16[512,512]{1,0:T(8,128)(2,1)S(1)}, bf16[512,512]{1,0:T(8,128)(2,1)S(1)}, u32[]{:S(2)}, u32[]{:S(2)}) collective-permute-start(bf16[512,512]{1,0:T(8,128)(2,1)S(1)} %backward.4), channel_id=1, source_target_pairs={{0,4},{4,0},{8,12},{12,8},{16,20},{20,16},{24,28},{28,24},{1,5},{5... | collective-permute-start | bytes 1572872 | tf_op jit(solution)/shard_map/ppermute | solution.py:27
  59.5 5.5 %collective-permute-start.25 = (bf16[64,512]{1,0:T(8,128)(2,1)S(1)}, bf16[64,512]{1,0:T(8,128)(2,1)S(1)}, u32[]{:S(2)}, u32[]{:S(2)}) collective-permute-start(bf16[64,512]{1,0:T(8,128)(2,1)S(1)} %add_convert_fusion.2), channel_id=1, source_target_pairs={{0,8},{4,20},{8,0},{12,28},{16,24},{20,4},{24,16},{28,12},{1,9},{5... | collective-permute-start | bytes 196616 | tf_op jit(solution)/shard_map/ppermute | solution.py:33
  62.4 14.9 %collective-permute-start.23 = (bf16[512,512]{1,0:T(8,128)(2,1)S(1)}, bf16[512,512]{1,0:T(8,128)(2,1)S(1)}, u32[]{:S(2)}, u32[]{:S(2)}) collective-permute-start(bf16[512,512]{1,0:T(8,128)(2,1)S(1)} %pad_maximum_fusion), channel_id=1, source_target_pairs={{0,8},{4,20},{8,0},{12,28},{16,24},{20,4},{24,16},{28,12},{1,9},{5... | collective-permute-start | bytes 1572872 | tf_op jit(solution)/shard_map/ppermute | solution.py:33
  64.3 11.0 %collective-permute-start.22 = (bf16[512,512]{1,0:T(8,128)(2,1)S(1)}, bf16[512,512]{1,0:T(8,128)(2,1)S(1)}, u32[]{:S(2)}, u32[]{:S(2)}) collective-permute-start(bf16[512,512]{1,0:T(8,128)(2,1)S(1)} %backward.7), channel_id=1, source_target_pairs={{0,4},{4,0},{8,12},{12,8},{16,20},{20,16},{24,28},{28,24},{1,5},{5... | collective-permute-start | bytes 1572872 | tf_op jit(solution)/shard_map/ppermute | solution.py:27
  65.0 6.0 %collective-permute-start.26 = (f32[64,512]{1,0:T(8,128)S(1)}, f32[64,512]{1,0:T(8,128)S(1)}, u32[]{:S(2)}, u32[]{:S(2)}) collective-permute-start(f32[64,512]{1,0:T(8,128)S(1)} %add_multiply_fusion.refs_0_), channel_id=1, source_target_pairs={{0,1},{1,0},{2,3},{3,2},{4,6},{5,7},{6,4},{7,5},{8,9},{9,8},{10,11... | collective-permute-start | bytes 393224 | tf_op jit(solution)/shard_map/ppermute | solution.py:43
  66.0 5.0 %collective-permute-start.27 = (f32[64,512]{1,0:T(8,128)S(1)}, f32[64,512]{1,0:T(8,128)S(1)}, u32[]{:S(2)}, u32[]{:S(2)}) collective-permute-start(f32[64,512]{1,0:T(8,128)S(1)} %add_multiply_fusion.refs_0_), channel_id=1, source_target_pairs={{0,2},{1,3},{2,0},{3,1},{4,5},{5,4},{6,7},{7,6},{8,10},{9,11},{10,... | collective-permute-start | bytes 393224 | tf_op jit(solution)/shard_map/ppermute | solution.py:43
  68.0 6.4 %collective-permute-start.28 = (f32[64,512]{1,0:T(8,128)S(1)}, f32[64,512]{1,0:T(8,128)S(1)}, u32[]{:S(2)}, u32[]{:S(2)}) collective-permute-start(f32[64,512]{1,0:T(8,128)S(1)} %add_multiply_fusion.refs_0_), channel_id=1, source_target_pairs={{0,3},{1,2},{2,1},{3,0},{4,7},{5,6},{6,5},{7,4},{8,11},{9,10},{10,... | collective-permute-start | bytes 393224 | tf_op jit(solution)/shard_map/ppermute | solution.py:43
  74.5 6.0 %collective-permute-start.29 = (f32[256,512]{1,0:T(8,128)S(1)}, f32[256,512]{1,0:T(8,128)S(1)}, u32[]{:S(2)}, u32[]{:S(2)}) collective-permute-start(f32[256,512]{1,0:T(8,128)S(1)} %pad_maximum_fusion.1), channel_id=1, source_target_pairs={{0,4},{4,0},{8,12},{12,8},{16,20},{20,16},{24,28},{28,24},{1,5},{5... | collective-permute-start | bytes 1572872 | tf_op jit(solution)/shard_map/ppermute | solution.py:27
  77.5 10.2 %collective-permute-start.24 = (bf16[256,512]{1,0:T(8,128)(2,1)S(1)}, bf16[256,512]{1,0:T(8,128)(2,1)S(1)}, u32[]{:S(2)}, u32[]{:S(2)}) collective-permute-start(bf16[256,512]{1,0:T(8,128)(2,1)S(1)} %get-tuple-element.92), channel_id=1, source_target_pairs={{0,16},{4,12},{8,24},{12,4},{16,0},{20,28},{24,8},{28,20},{1,17},{... | collective-permute-start | bytes 786440 | tf_op jit(solution)/shard_map/ppermute | solution.py:33
  (2 other events, 4.8 us)

commit v15 on v14

--- a/solution.py
+++ b/solution.py
@@ -386,7 +386,7 @@
     low = forward(after(dense, *high[0]), odd, others, 0, totals[:upper], [jnp.float32] * upper, CHUNKS)
 
     pieces = [collect([*x, *y], swap_members) for x, y in zip(low, high)]
-    dense_t = transposed(after(dense, *high[0], *[piece[1] for piece in pieces]))
+    dense_t = transposed(after(dense, *high[0], pieces[0][1]))
     pieces[-1][-1] = after(pieces[-1][-1], *dense_t)
     activated, agg, pre_grad, grad = middle(pieces, cotangent, weight)
     owns, send = weight_part(agg, pre_grad, place, groups)

time: 88.6 us -> 88.9 us (level)
  waiting for transfers between devices: 34 us -> 36.6 us
  starting transfers between devices: 35.4 us -> 32.9 us
    ppermute x15, starting transfers between devices: 18.7 us -> 16.1 us  [swap_members(): return lax.ppermute(x, ('dom', 'repl'), pairs)]
    ppermute x15, waiting for transfers between devices: 11.7 us -> 13.6 us  [swap_members(): return lax.ppermute(x, ('dom', 'repl'), pairs)]
  transfers between devices with their start and end apart: 30 -> 30, of which waited for: 15 -> 17; matrix products, arithmetic and copies ran while one was open for 2% -> 2% of each run, Pallas kernels for 11% -> 12%
where the time goes in v15:
time: 88.9 us; the launch traced here: 88.7 us
  waiting for transfers between devices  36.6 us (41%)
  starting transfers between devices  32.9 us (37%)
  Pallas kernels  14.2 us (16%)
  local copies, waits for them, and re-layouts  2.93 us (3%)
  other arithmetic  1.24 us (1%)
    ppermute x7, waiting for transfers between devices, swap_chips(): lax.ppermute(x, 'dom', [(i, i ^ 2 * between(held, i % 2, bits)) for i in...  21.5 us
    ppermute x15, starting transfers between devices, swap_members(): return lax.ppermute(x, ('dom', 'repl'), pairs)  16.1 us
    ppermute x7, starting transfers between devices, swap_chips(): lax.ppermute(x, 'dom', [(i, i ^ 2 * between(held, i % 2, bits)) for i in...  15.8 us
    ppermute x15, waiting for transfers between devices, swap_members(): return lax.ppermute(x, ('dom', 'repl'), pairs)  13.6 us
    pallas_call x4, Pallas kernels, forward(): pl.pallas_call(functools.partial(forward_kernel, which=which, base=base,...  2.82 us
    pallas_call x4, Pallas kernels, backward(): pl.pallas_call(functools.partial(backward_kernel, side=side, count=count,...  2.81 us
    pallas_call x1, Pallas kernels, densify(): pl.pallas_call(functools.partial(densify_kernel, col_tiles=col_tiles), ou...  2.75 us
    unnamed x8, local copies, waits for them, and re-layouts  2.2 us
  transfers between devices with their start and end apart: 30, of which 17 were waited for; matrix products, arithmetic and copies ran while one was open for 2% of the time, Pallas kernels for 12%

profile of v15, /device:TPU:0, one launch (start us, length us, event | category | flops | bytes accessed | tf_op | source)
XLA Modules:
  0.0 88.7 jit_solution(9145603497537593938)
XLA Ops:
  0.6 4.1 %collective-permute-start = (bf16[256,512]{1,0:T(8,128)(2,1)}, bf16[256,512]{1,0:T(8,128)(2,1)S(1)}, u32[]{:S(2)}, u32[]{:S(2)}) collective-permute-start(bf16[256,512]{1,0:T(8,128)(2,1)} %refs_1_.1), channel_id=1, source_target_pairs={{0,16},{4,12},{8,24},{12,4},{16,0},{20,28},{24,8},{28,20},{1,17},{... | collective-permute-start | bytes 786440 | tf_op jit(solution)/shard_map/ppermute | solution.py:33
  6.3 4.6 %collective-permute-done.refs_3_ = bf16[256,512]{1,0:T(8,128)(2,1)S(1)} collective-permute-done((bf16[256,512]{1,0:T(8,128)(2,1)}, bf16[256,512]{1,0:T(8,128)(2,1)S(1)}, u32[]{:S(2)}, u32[]{:S(2)}) %collective-permute-start) | collective-permute-done | bytes 262176 | tf_op jit(solution)/shard_map/ppermute | solution.py:33
  10.9 2.4 %collective-permute-start.1 = (bf16[256,512]{1,0:T(8,128)(2,1)}, bf16[256,512]{1,0:T(8,128)(2,1)S(1)}, u32[]{:S(2)}, u32[]{:S(2)}) collective-permute-start(bf16[256,512]{1,0:T(8,128)(2,1)} %refs_1_.1), channel_id=1, source_target_pairs={{0,8},{4,20},{8,0},{12,28},{16,24},{20,4},{24,16},{28,12},{1,9},{5... | collective-permute-start | bytes 786440 | tf_op jit(solution)/shard_map/ppermute | solution.py:33
  13.4 2.2 %copy-done = bf16[1,1,8,16,128,128]{5,4,3,2,1,0:T(8,128)(2,1)S(1)} copy-done((bf16[1,1,8,16,128,128]{5,4,3,2,1,0:T(8,128)(2,1)S(1)}, bf16[1,1,8,16,128,128]{5,4,3,2,1,0:T(8,128)(2,1)}, u32[]{:S(2)}) %copy-start) | copy-done | bytes 4194328
  15.6 2.8 %densify.1.refs_0_.a_ref = bf16[8,1024,256]{2,1,0:T(8,128)(2,1)S(1)} custom-call(s32[8,17]{1,0:T(8,128)S(1)} %pad_add_fusion.spots_ref, s32[2]{0:T(128)S(1)} %pad_add_fusion.1.place_ref, bf16[8,16,128,128]{3,2,1,0:T(8,128)(2,1)S(1)} %bitcast.26), custom_call_target="tpu_custom_call" | custom-call | flops 2097152 | bytes 16777216 | tf_op jit(solution)/shard_map/densify/pallas_call | solution.py:87
  18.4 1.2 %forward.4 = (f32[256,512]{1,0:T(8,128)S(1)}, f32[256,512]{1,0:T(8,128)S(1)}, f32[256,512]{1,0:T(8,128)S(1)}, f32[256,512]{1,0:T(8,128)S(1)}) custom-call(bf16[8,1024,256]{2,1,0:T(8,128)(2,1)S(1)} %densify.1.refs_0_.a_ref, bf16[256,512]{1,0:T(8,128)(2,1)S(1)} %copy-done.2, bf16[256,512]{1,0:T(8,128)(2,1)S(1)} %collective-permute-done.2.refs_2_, ...), custom_call_target="tpu_custom_call" | custom-call | flops 1073741824 | bytes 4194304 | tf_op jit(solution)/shard_map/forward/pallas_call | solution.py:142
  19.6 3.3 %collective-permute-done.1.refs_1_ = bf16[256,512]{1,0:T(8,128)(2,1)S(1)} collective-permute-done((bf16[256,512]{1,0:T(8,128)(2,1)}, bf16[256,512]{1,0:T(8,128)(2,1)S(1)}, u32[]{:S(2)}, u32[]{:S(2)}) %collective-permute-start.1) | collective-permute-done | bytes 262176 | tf_op jit(solution)/shard_map/ppermute | solution.py:33
  22.9 3.4 %collective-permute-done.5.refs_2_ = bf16[256,512]{1,0:T(8,128)(2,1)S(1)} collective-permute-done((bf16[256,512]{1,0:T(8,128)(2,1)S(1)}, bf16[256,512]{1,0:T(8,128)(2,1)S(1)}, u32[]{:S(2)}, u32[]{:S(2)}) %collective-permute-start.5) | collective-permute-done | bytes 262176 | tf_op jit(solution)/shard_map/ppermute | solution.py:33
  28.3 1.7 %collective-permute-start.11 = (bf16[256,256]{1,0:T(8,128)(2,1)S(1)}, bf16[256,256]{1,0:T(8,128)(2,1)S(1)}, u32[]{:S(2)}, u32[]{:S(2)}) collective-permute-start(bf16[256,256]{1,0:T(8,128)(2,1)S(1)} %get-tuple-element.68), channel_id=1, source_target_pairs={{0,1},{1,0},{2,3},{3,2},{4,6},{5,7},{6,4},{7,5},{8,9},{9,8},{10,11... | collective-permute-start | bytes 393224 | tf_op jit(solution)/shard_map/ppermute | solution.py:43
  30.4 1.7 %collective-permute-start.7 = (bf16[256,256]{1,0:T(8,128)(2,1)S(1)}, bf16[256,256]{1,0:T(8,128)(2,1)S(1)}, u32[]{:S(2)}, u32[]{:S(2)}) collective-permute-start(bf16[256,256]{1,0:T(8,128)(2,1)S(1)} %get-tuple-element.58), channel_id=1, source_target_pairs={{0,1},{1,0},{2,3},{3,2},{4,6},{5,7},{6,4},{7,5},{8,9},{9,8},{10,11... | collective-permute-start | bytes 393224 | tf_op jit(solution)/shard_map/ppermute | solution.py:43
  33.3 1.8 %collective-permute-start.12 = (bf16[256,256]{1,0:T(8,128)(2,1)S(1)}, bf16[256,256]{1,0:T(8,128)(2,1)S(1)}, u32[]{:S(2)}, u32[]{:S(2)}) collective-permute-start(bf16[256,256]{1,0:T(8,128)(2,1)S(1)} %add_rounded.3), channel_id=1, source_target_pairs={{0,2},{1,3},{2,0},{3,1},{4,5},{5,4},{6,7},{7,6},{8,10},{9,11},{10,... | collective-permute-start | bytes 393224 | tf_op jit(solution)/shard_map/ppermute | solution.py:43
  35.1 1.5 %collective-permute-start.10 = (bf16[256,256]{1,0:T(8,128)(2,1)S(1)}, bf16[256,256]{1,0:T(8,128)(2,1)S(1)}, u32[]{:S(2)}, u32[]{:S(2)}) collective-permute-start(bf16[256,256]{1,0:T(8,128)(2,1)S(1)} %get-tuple-element.66), channel_id=1, source_target_pairs={{0,1},{1,0},{2,3},{3,2},{4,6},{5,7},{6,4},{7,5},{8,9},{9,8},{10,11... | collective-permute-start | bytes 393224 | tf_op jit(solution)/shard_map/ppermute | solution.py:43
  37.4 1.2 %transposed.1 = (bf16[2,256,1024]{2,1,0:T(8,128)(2,1)S(1)}, bf16[2,256,1024]{2,1,0:T(8,128)(2,1)S(1)}, bf16[2,256,1024]{2,1,0:T(8,128)(2,1)S(1)}, bf16[2,256,1024]{2,1,0:T(8,128)(2,1)S(1)}) custom-call(bf16[8,1024,256]{2,1,0:T(8,128)(2,1)S(1)} %densify.1.refs_0_.a_ref), custom_call_target="tpu_custom_call" | custom-call | bytes 8388608 | tf_op jit(solution)/shard_map/transposed/pallas_call | solution.py:112
  39.5 1.3 %collective-permute-done.10.refs_4_ = bf16[256,256]{1,0:T(8,128)(2,1)S(1)} collective-permute-done((bf16[256,256]{1,0:T(8,128)(2,1)S(1)}, bf16[256,256]{1,0:T(8,128)(2,1)S(1)}, u32[]{:S(2)}, u32[]{:S(2)}) %collective-permute-start.10) | collective-permute-done | bytes 131104 | tf_op jit(solution)/shard_map/ppermute | solution.py:43
  41.7 1.2 %middle.1 = (bf16[256,512]{1,0:T(8,128)(2,1)}, bf16[256,512]{1,0:T(8,128)(2,1)S(1)}, bf16[256,512]{1,0:T(8,128)(2,1)S(1)}, bf16[256,512]{1,0:T(8,128)(2,1)S(1)}) custom-call(f32[256,256]{1,0:T(8,128)S(1)} %get-tuple-element.63.refs_0_, bf16[256,256]{1,0:T(8,128)(2,1)S(1)} %collective-permute-done.7.refs_1_, ...), custom_call_target="tpu_custom_call" | custom-call | flops 268435456 | bytes 1310720 | tf_op jit(solution)/shard_map/middle/pallas_call | solution.py:182
  42.8 0.9 %weight_part.1 = (f32[64,512]{1,0:T(8,128)S(1)}, f32[64,512]{1,0:T(8,128)S(1)}, f32[64,512]{1,0:T(8,128)S(1)}, f32[64,512]{1,0:T(8,128)S(1)}, bf16[256,512]{1,0:T(8,128)(2,1)S(1)}) custom-call(s32[2]{0:T(128)S(1)} %pad_add_fusion.1.place_ref, bf16[256,512]{1,0:T(8,128)(2,1)S(1)} %get-tuple-element.77.agg_ref, bf16[256,512]{1,0:T(8,128)(2,1)S(1)} %get-tuple-element.78.pre_grad_ref), custom_call_target="tpu_custom_call" | custom-call | flops 134217728 | bytes 1572864 | tf_op jit(solution)/shard_map/weight_part/pallas_call | solution.py:215
  45.4 1.4 %collective-permute-start.19 = (bf16[64,512]{1,0:T(8,128)(2,1)S(1)}, bf16[64,512]{1,0:T(8,128)(2,1)S(1)}, u32[]{:S(2)}, u32[]{:S(2)}) collective-permute-start(bf16[64,512]{1,0:T(8,128)(2,1)S(1)} %get-tuple-element.96), channel_id=1, source_target_pairs={{0,3},{1,2},{2,1},{3,0},{4,7},{5,6},{6,5},{7,4},{8,11},{9,10},{10,... | collective-permute-start | bytes 196616 | tf_op jit(solution)/shard_map/ppermute | solution.py:43
  47.5 1.5 %collective-permute-start.17 = (bf16[64,512]{1,0:T(8,128)(2,1)S(1)}, bf16[64,512]{1,0:T(8,128)(2,1)S(1)}, u32[]{:S(2)}, u32[]{:S(2)}) collective-permute-start(bf16[64,512]{1,0:T(8,128)(2,1)S(1)} %get-tuple-element.95), channel_id=1, source_target_pairs={{0,1},{1,0},{2,3},{3,2},{4,6},{5,7},{6,4},{7,5},{8,9},{9,8},{10,11... | collective-permute-start | bytes 196616 | tf_op jit(solution)/shard_map/ppermute | solution.py:43
  49.5 2.5 %collective-permute-done.13.refs_3_ = bf16[256,512]{1,0:T(8,128)(2,1)S(1)} collective-permute-done((bf16[256,512]{1,0:T(8,128)(2,1)S(1)}, bf16[256,512]{1,0:T(8,128)(2,1)S(1)}, u32[]{:S(2)}, u32[]{:S(2)}) %collective-permute-start.13) | collective-permute-done | bytes 262176 | tf_op jit(solution)/shard_map/ppermute | solution.py:43
  52.1 1.4 %collective-permute-done.18 = bf16[64,512]{1,0:T(8,128)(2,1)S(1)} collective-permute-done((bf16[64,512]{1,0:T(8,128)(2,1)S(1)}, bf16[64,512]{1,0:T(8,128)(2,1)S(1)}, u32[]{:S(2)}, u32[]{:S(2)}) %collective-permute-start.18) | collective-permute-done | bytes 65568 | tf_op jit(solution)/shard_map/ppermute | solution.py:43
  53.5 3.0 %collective-permute-start.20 = (bf16[64,512]{1,0:T(8,128)(2,1)S(1)}, bf16[64,512]{1,0:T(8,128)(2,1)S(1)}, u32[]{:S(2)}, u32[]{:S(2)}) collective-permute-start(bf16[64,512]{1,0:T(8,128)(2,1)S(1)} %add_convert_fusion.3), channel_id=1, source_target_pairs={{0,16},{4,12},{8,24},{12,4},{16,0},{20,28},{24,8},{28,20},{1,17},{... | collective-permute-start | bytes 196616 | tf_op jit(solution)/shard_map/ppermute | solution.py:33
  56.5 2.3 %collective-permute-done.20 = bf16[64,512]{1,0:T(8,128)(2,1)S(1)} collective-permute-done((bf16[64,512]{1,0:T(8,128)(2,1)S(1)}, bf16[64,512]{1,0:T(8,128)(2,1)S(1)}, u32[]{:S(2)}, u32[]{:S(2)}) %collective-permute-start.20) | collective-permute-done | bytes 65568 | tf_op jit(solution)/shard_map/ppermute | solution.py:33
  59.6 2.2 %collective-permute-start.25 = (bf16[64,512]{1,0:T(8,128)(2,1)S(1)}, bf16[64,512]{1,0:T(8,128)(2,1)S(1)}, u32[]{:S(2)}, u32[]{:S(2)}) collective-permute-start(bf16[64,512]{1,0:T(8,128)(2,1)S(1)} %add_convert_fusion.2), channel_id=1, source_target_pairs={{0,8},{4,20},{8,0},{12,28},{16,24},{20,4},{24,16},{28,12},{1,9},{5... | collective-permute-start | bytes 196616 | tf_op jit(solution)/shard_map/ppermute | solution.py:33
  62.8 1.1 %collective-permute-start.23 = (bf16[512,512]{1,0:T(8,128)(2,1)S(1)}, bf16[512,512]{1,0:T(8,128)(2,1)S(1)}, u32[]{:S(2)}, u32[]{:S(2)}) collective-permute-start(bf16[512,512]{1,0:T(8,128)(2,1)S(1)} %pad_maximum_fusion), channel_id=1, source_target_pairs={{0,8},{4,20},{8,0},{12,28},{16,24},{20,4},{24,16},{28,12},{1,9},{5... | collective-permute-start | bytes 1572872 | tf_op jit(solution)/shard_map/ppermute | solution.py:33
  66.0 1.2 %collective-permute-start.27 = (f32[64,512]{1,0:T(8,128)S(1)}, f32[64,512]{1,0:T(8,128)S(1)}, u32[]{:S(2)}, u32[]{:S(2)}) collective-permute-start(f32[64,512]{1,0:T(8,128)S(1)} %add_multiply_fusion.refs_0_), channel_id=1, source_target_pairs={{0,2},{1,3},{2,0},{3,1},{4,5},{5,4},{6,7},{7,6},{8,10},{9,11},{10,... | collective-permute-start | bytes 393224 | tf_op jit(solution)/shard_map/ppermute | solution.py:43
  67.2 1.6 %collective-permute-start.28 = (f32[64,512]{1,0:T(8,128)S(1)}, f32[64,512]{1,0:T(8,128)S(1)}, u32[]{:S(2)}, u32[]{:S(2)}) collective-permute-start(f32[64,512]{1,0:T(8,128)S(1)} %add_multiply_fusion.refs_0_), channel_id=1, source_target_pairs={{0,3},{1,2},{2,1},{3,0},{4,7},{5,6},{6,5},{7,4},{8,11},{9,10},{10,... | collective-permute-start | bytes 393224 | tf_op jit(solution)/shard_map/ppermute | solution.py:43
  68.8 2.8 %collective-permute-done.26.refs_1_ = f32[64,512]{1,0:T(8,128)S(1)} collective-permute-done((f32[64,512]{1,0:T(8,128)S(1)}, f32[64,512]{1,0:T(8,128)S(1)}, u32[]{:S(2)}, u32[]{:S(2)}) %collective-permute-start.26) | collective-permute-done | bytes 131104 | tf_op jit(solution)/shard_map/ppermute | solution.py:43
  71.7 2.8 %collective-permute-done.28.refs_3_ = f32[64,512]{1,0:T(8,128)S(1)} collective-permute-done((f32[64,512]{1,0:T(8,128)S(1)}, f32[64,512]{1,0:T(8,128)S(1)}, u32[]{:S(2)}, u32[]{:S(2)}) %collective-permute-start.28) | collective-permute-done | bytes 131104 | tf_op jit(solution)/shard_map/ppermute | solution.py:43
  75.3 2.4 %collective-permute-done.23.refs_3_ = bf16[512,512]{1,0:T(8,128)(2,1)S(1)} collective-permute-done((bf16[512,512]{1,0:T(8,128)(2,1)S(1)}, bf16[512,512]{1,0:T(8,128)(2,1)S(1)}, u32[]{:S(2)}, u32[]{:S(2)}) %collective-permute-start.23) | collective-permute-done | bytes 524320 | tf_op jit(solution)/shard_map/ppermute | solution.py:33
  77.8 3.0 %collective-permute-start.24 = (bf16[256,512]{1,0:T(8,128)(2,1)S(1)}, bf16[256,512]{1,0:T(8,128)(2,1)S(1)}, u32[]{:S(2)}, u32[]{:S(2)}) collective-permute-start(bf16[256,512]{1,0:T(8,128)(2,1)S(1)} %get-tuple-element.92), channel_id=1, source_target_pairs={{0,16},{4,12},{8,24},{12,4},{16,0},{20,28},{24,8},{28,20},{1,17},{... | collective-permute-start | bytes 786440 | tf_op jit(solution)/shard_map/ppermute | solution.py:33
  80.8 1.6 %place_slices.1 = f32[512,512]{1,0:T(8,128)} custom-call(s32[2]{0:T(128)S(1)} %pad_add_fusion.1.place_ref, f32[64,512]{1,0:T(8,128)S(1)} %add_multiply_fusion.refs_0_, f32[64,512]{1,0:T(8,128)S(1)} %collective-permute-done.26.refs_1_, f32[64,512]{1,0:T(8,128)S(1)} %collective-permute-done.27.refs_2_, f32[64,512]{1,0:T(8,128)S(1)} %collective-permute-done.28.refs_3_, ...), custom_call_target="tpu_custom_call" | custom-call | bytes 2097152 | tf_op jit(solution)/shard_map/place_slices/pallas_call | solution.py:243
  82.4 5.6 %collective-permute-done.24.refs_1_ = bf16[256,512]{1,0:T(8,128)(2,1)S(1)} collective-permute-done((bf16[256,512]{1,0:T(8,128)(2,1)S(1)}, bf16[256,512]{1,0:T(8,128)(2,1)S(1)}, u32[]{:S(2)}, u32[]{:S(2)}) %collective-permute-start.24) | collective-permute-done | bytes 262176 | tf_op jit(solution)/shard_map/ppermute | solution.py:33
  (64 shorter events, 16.3 us)
Async XLA Ops:
  0.6 10.2 %collective-permute-start = (bf16[256,512]{1,0:T(8,128)(2,1)}, bf16[256,512]{1,0:T(8,128)(2,1)S(1)}, u32[]{:S(2)}, u32[]{:S(2)}) collective-permute-start(bf16[256,512]{1,0:T(8,128)(2,1)} %refs_1_.1), channel_id=1, source_target_pairs={{0,16},{4,12},{8,24},{12,4},{16,0},{20,28},{24,8},{28,20},{1,17},{... | collective-permute-start | bytes 786440 | tf_op jit(solution)/shard_map/ppermute | solution.py:33
  4.7 13.6 %collective-permute-start.2 = (bf16[256,512]{1,0:T(8,128)(2,1)}, bf16[256,512]{1,0:T(8,128)(2,1)S(1)}, u32[]{:S(2)}, u32[]{:S(2)}) collective-permute-start(bf16[256,512]{1,0:T(8,128)(2,1)} %refs_1_.1), channel_id=1, source_target_pairs={{0,4},{4,0},{8,12},{12,8},{16,20},{20,16},{24,28},{28,24},{1,5},{5... | collective-permute-start | bytes 786440 | tf_op jit(solution)/shard_map/ppermute | solution.py:27
  10.9 7.5 %collective-permute-start.3 = (bf16[256,512]{1,0:T(8,128)(2,1)S(1)}, bf16[256,512]{1,0:T(8,128)(2,1)S(1)}, u32[]{:S(2)}, u32[]{:S(2)}) collective-permute-start(bf16[256,512]{1,0:T(8,128)(2,1)S(1)} %collective-permute-done.refs_3_), channel_id=1, source_target_pairs={{0,4},{4,0},{8,12},{12,8},{16,20},{20,16},{24,28},{28,24},{1,5},{5... | collective-permute-start | bytes 786440 | tf_op jit(solution)/shard_map/ppermute | solution.py:27
  10.9 12.1 %collective-permute-start.1 = (bf16[256,512]{1,0:T(8,128)(2,1)}, bf16[256,512]{1,0:T(8,128)(2,1)S(1)}, u32[]{:S(2)}, u32[]{:S(2)}) collective-permute-start(bf16[256,512]{1,0:T(8,128)(2,1)} %refs_1_.1), channel_id=1, source_target_pairs={{0,8},{4,20},{8,0},{12,28},{16,24},{20,4},{24,16},{28,12},{1,9},{5... | collective-permute-start | bytes 786440 | tf_op jit(solution)/shard_map/ppermute | solution.py:33
  13.3 13.0 %collective-permute-start.5 = (bf16[256,512]{1,0:T(8,128)(2,1)S(1)}, bf16[256,512]{1,0:T(8,128)(2,1)S(1)}, u32[]{:S(2)}, u32[]{:S(2)}) collective-permute-start(bf16[256,512]{1,0:T(8,128)(2,1)S(1)} %collective-permute-done.refs_3_), channel_id=1, source_target_pairs={{0,8},{4,20},{8,0},{12,28},{16,24},{20,4},{24,16},{28,12},{1,9},{5... | collective-permute-start | bytes 786440 | tf_op jit(solution)/shard_map/ppermute | solution.py:33
  22.9 4.1 %collective-permute-start.4 = (bf16[256,512]{1,0:T(8,128)(2,1)S(1)}, bf16[256,512]{1,0:T(8,128)(2,1)S(1)}, u32[]{:S(2)}, u32[]{:S(2)}) collective-permute-start(bf16[256,512]{1,0:T(8,128)(2,1)S(1)} %collective-permute-done.1.refs_1_), channel_id=1, source_target_pairs={{0,4},{4,0},{8,12},{12,8},{16,20},{20,16},{24,28},{28,24},{1,5},{5... | collective-permute-start | bytes 786440 | tf_op jit(solution)/shard_map/ppermute | solution.py:27
  26.3 1.5 %collective-permute-start.6 = (bf16[256,512]{1,0:T(8,128)(2,1)S(1)}, bf16[256,512]{1,0:T(8,128)(2,1)S(1)}, u32[]{:S(2)}, u32[]{:S(2)}) collective-permute-start(bf16[256,512]{1,0:T(8,128)(2,1)S(1)} %collective-permute-done.5.refs_2_), channel_id=1, source_target_pairs={{0,4},{4,0},{8,12},{12,8},{16,20},{20,16},{24,28},{28,24},{1,5},{5... | collective-permute-start | bytes 786440 | tf_op jit(solution)/shard_map/ppermute | solution.py:27
  28.3 5.0 %collective-permute-start.11 = (bf16[256,256]{1,0:T(8,128)(2,1)S(1)}, bf16[256,256]{1,0:T(8,128)(2,1)S(1)}, u32[]{:S(2)}, u32[]{:S(2)}) collective-permute-start(bf16[256,256]{1,0:T(8,128)(2,1)S(1)} %get-tuple-element.68), channel_id=1, source_target_pairs={{0,1},{1,0},{2,3},{3,2},{4,6},{5,7},{6,4},{7,5},{8,9},{9,8},{10,11... | collective-permute-start | bytes 393224 | tf_op jit(solution)/shard_map/ppermute | solution.py:43
  30.0 6.6 %collective-permute-start.8 = (bf16[256,256]{1,0:T(8,128)(2,1)S(1)}, bf16[256,256]{1,0:T(8,128)(2,1)S(1)}, u32[]{:S(2)}, u32[]{:S(2)}) collective-permute-start(bf16[256,256]{1,0:T(8,128)(2,1)S(1)} %get-tuple-element.59), channel_id=1, source_target_pairs={{0,1},{1,0},{2,3},{3,2},{4,6},{5,7},{6,4},{7,5},{8,9},{9,8},{10,11... | collective-permute-start | bytes 393224 | tf_op jit(solution)/shard_map/ppermute | solution.py:43
  30.4 7.1 %collective-permute-start.7 = (bf16[256,256]{1,0:T(8,128)(2,1)S(1)}, bf16[256,256]{1,0:T(8,128)(2,1)S(1)}, u32[]{:S(2)}, u32[]{:S(2)}) collective-permute-start(bf16[256,256]{1,0:T(8,128)(2,1)S(1)} %get-tuple-element.58), channel_id=1, source_target_pairs={{0,1},{1,0},{2,3},{3,2},{4,6},{5,7},{6,4},{7,5},{8,9},{9,8},{10,11... | collective-permute-start | bytes 393224 | tf_op jit(solution)/shard_map/ppermute | solution.py:43
  32.0 9.6 %copy-start.1 = (bf16[512,512]{1,0:T(8,128)(2,1)S(1)}, bf16[512,512]{1,0:T(8,128)(2,1)}, u32[]{:S(2)}) copy-start(bf16[512,512]{1,0:T(8,128)(2,1)} %refs_7_.1) | copy-start | bytes 1572868
  32.0 9.6 %copy-start.3 = (bf16[256,512]{1,0:T(8,128)(2,1)S(1)}, bf16[256,512]{1,0:T(8,128)(2,1)}, u32[]{:S(2)}) copy-start(bf16[256,512]{1,0:T(8,128)(2,1)} %refs_6_.1) | copy-start | bytes 786436
  33.3 6.1 %collective-permute-start.12 = (bf16[256,256]{1,0:T(8,128)(2,1)S(1)}, bf16[256,256]{1,0:T(8,128)(2,1)S(1)}, u32[]{:S(2)}, u32[]{:S(2)}) collective-permute-start(bf16[256,256]{1,0:T(8,128)(2,1)S(1)} %add_rounded.3), channel_id=1, source_target_pairs={{0,2},{1,3},{2,0},{3,1},{4,5},{5,4},{6,7},{7,6},{8,10},{9,11},{10,... | collective-permute-start | bytes 393224 | tf_op jit(solution)/shard_map/ppermute | solution.py:43
  35.1 5.7 %collective-permute-start.10 = (bf16[256,256]{1,0:T(8,128)(2,1)S(1)}, bf16[256,256]{1,0:T(8,128)(2,1)S(1)}, u32[]{:S(2)}, u32[]{:S(2)}) collective-permute-start(bf16[256,256]{1,0:T(8,128)(2,1)S(1)} %get-tuple-element.66), channel_id=1, source_target_pairs={{0,1},{1,0},{2,3},{3,2},{4,6},{5,7},{6,4},{7,5},{8,9},{9,8},{10,11... | collective-permute-start | bytes 393224 | tf_op jit(solution)/shard_map/ppermute | solution.py:43
  36.6 5.0 %collective-permute-start.9 = (bf16[256,256]{1,0:T(8,128)(2,1)S(1)}, bf16[256,256]{1,0:T(8,128)(2,1)S(1)}, u32[]{:S(2)}, u32[]{:S(2)}) collective-permute-start(bf16[256,256]{1,0:T(8,128)(2,1)S(1)} %add_rounded.2), channel_id=1, source_target_pairs={{0,2},{1,3},{2,0},{3,1},{4,5},{5,4},{6,7},{7,6},{8,10},{9,11},{10,... | collective-permute-start | bytes 393224 | tf_op jit(solution)/shard_map/ppermute | solution.py:43
  43.8 1.6 %collective-permute-start.16 = (bf16[256,512]{1,0:T(8,128)(2,1)S(1)}, bf16[256,512]{1,0:T(8,128)(2,1)S(1)}, u32[]{:S(2)}, u32[]{:S(2)}) collective-permute-start(bf16[256,512]{1,0:T(8,128)(2,1)S(1)} %get-tuple-element.80), channel_id=1, source_target_pairs={{0,4},{4,0},{8,12},{12,8},{16,20},{20,16},{24,28},{28,24},{1,5},{5... | collective-permute-start | bytes 786440 | tf_op jit(solution)/shard_map/ppermute | solution.py:27
  43.9 8.2 %collective-permute-start.13 = (bf16[256,512]{1,0:T(8,128)(2,1)S(1)}, bf16[256,512]{1,0:T(8,128)(2,1)S(1)}, u32[]{:S(2)}, u32[]{:S(2)}) collective-permute-start(bf16[256,512]{1,0:T(8,128)(2,1)S(1)} %get-tuple-element.88.refs_2_), channel_id=1, source_target_pairs={{0,2},{1,3},{2,0},{3,1},{4,5},{5,4},{6,7},{7,6},{8,10},{9,11},{10,... | collective-permute-start | bytes 786440 | tf_op jit(solution)/shard_map/ppermute | solution.py:43
  45.4 6.6 %collective-permute-start.19 = (bf16[64,512]{1,0:T(8,128)(2,1)S(1)}, bf16[64,512]{1,0:T(8,128)(2,1)S(1)}, u32[]{:S(2)}, u32[]{:S(2)}) collective-permute-start(bf16[64,512]{1,0:T(8,128)(2,1)S(1)} %get-tuple-element.96), channel_id=1, source_target_pairs={{0,3},{1,2},{2,1},{3,0},{4,7},{5,6},{6,5},{7,4},{8,11},{9,10},{10,... | collective-permute-start | bytes 196616 | tf_op jit(solution)/shard_map/ppermute | solution.py:43
  46.8 6.7 %collective-permute-start.18 = (bf16[64,512]{1,0:T(8,128)(2,1)S(1)}, bf16[64,512]{1,0:T(8,128)(2,1)S(1)}, u32[]{:S(2)}, u32[]{:S(2)}) collective-permute-start(bf16[64,512]{1,0:T(8,128)(2,1)S(1)} %get-tuple-element.97), channel_id=1, source_target_pairs={{0,2},{1,3},{2,0},{3,1},{4,5},{5,4},{6,7},{7,6},{8,10},{9,11},{10,... | collective-permute-start | bytes 196616 | tf_op jit(solution)/shard_map/ppermute | solution.py:43
  47.5 6.0 %collective-permute-start.17 = (bf16[64,512]{1,0:T(8,128)(2,1)S(1)}, bf16[64,512]{1,0:T(8,128)(2,1)S(1)}, u32[]{:S(2)}, u32[]{:S(2)}) collective-permute-start(bf16[64,512]{1,0:T(8,128)(2,1)S(1)} %get-tuple-element.95), channel_id=1, source_target_pairs={{0,1},{1,0},{2,3},{3,2},{4,6},{5,7},{6,4},{7,5},{8,9},{9,8},{10,11... | collective-permute-start | bytes 196616 | tf_op jit(solution)/shard_map/ppermute | solution.py:43
  49.0 9.7 %collective-permute-start.14 = (bf16[256,512]{1,0:T(8,128)(2,1)S(1)}, bf16[256,512]{1,0:T(8,128)(2,1)S(1)}, u32[]{:S(2)}, u32[]{:S(2)}) collective-permute-start(bf16[256,512]{1,0:T(8,128)(2,1)S(1)} %get-tuple-element.88.refs_2_), channel_id=1, source_target_pairs={{0,1},{1,0},{2,3},{3,2},{4,6},{5,7},{6,4},{7,5},{8,9},{9,8},{10,11... | collective-permute-start | bytes 786440 | tf_op jit(solution)/shard_map/ppermute | solution.py:43
  52.0 6.7 %collective-permute-start.15 = (bf16[256,512]{1,0:T(8,128)(2,1)S(1)}, bf16[256,512]{1,0:T(8,128)(2,1)S(1)}, u32[]{:S(2)}, u32[]{:S(2)}) collective-permute-start(bf16[256,512]{1,0:T(8,128)(2,1)S(1)} %collective-permute-done.13.refs_3_), channel_id=1, source_target_pairs={{0,1},{1,0},{2,3},{3,2},{4,6},{5,7},{6,4},{7,5},{8,9},{9,8},{10,11... | collective-permute-start | bytes 786440 | tf_op jit(solution)/shard_map/ppermute | solution.py:43
  53.5 5.2 %collective-permute-start.20 = (bf16[64,512]{1,0:T(8,128)(2,1)S(1)}, bf16[64,512]{1,0:T(8,128)(2,1)S(1)}, u32[]{:S(2)}, u32[]{:S(2)}) collective-permute-start(bf16[64,512]{1,0:T(8,128)(2,1)S(1)} %add_convert_fusion.3), channel_id=1, source_target_pairs={{0,16},{4,12},{8,24},{12,4},{16,0},{20,28},{24,8},{28,20},{1,17},{... | collective-permute-start | bytes 196616 | tf_op jit(solution)/shard_map/ppermute | solution.py:33
  59.5 3.1 %collective-permute-start.21 = (bf16[512,512]{1,0:T(8,128)(2,1)S(1)}, bf16[512,512]{1,0:T(8,128)(2,1)S(1)}, u32[]{:S(2)}, u32[]{:S(2)}) collective-permute-start(bf16[512,512]{1,0:T(8,128)(2,1)S(1)} %backward.4), channel_id=1, source_target_pairs={{0,4},{4,0},{8,12},{12,8},{16,20},{20,16},{24,28},{28,24},{1,5},{5... | collective-permute-start | bytes 1572872 | tf_op jit(solution)/shard_map/ppermute | solution.py:27
  59.6 5.6 %collective-permute-start.25 = (bf16[64,512]{1,0:T(8,128)(2,1)S(1)}, bf16[64,512]{1,0:T(8,128)(2,1)S(1)}, u32[]{:S(2)}, u32[]{:S(2)}) collective-permute-start(bf16[64,512]{1,0:T(8,128)(2,1)S(1)} %add_convert_fusion.2), channel_id=1, source_target_pairs={{0,8},{4,20},{8,0},{12,28},{16,24},{20,4},{24,16},{28,12},{1,9},{5... | collective-permute-start | bytes 196616 | tf_op jit(solution)/shard_map/ppermute | solution.py:33
  62.8 14.9 %collective-permute-start.23 = (bf16[512,512]{1,0:T(8,128)(2,1)S(1)}, bf16[512,512]{1,0:T(8,128)(2,1)S(1)}, u32[]{:S(2)}, u32[]{:S(2)}) collective-permute-start(bf16[512,512]{1,0:T(8,128)(2,1)S(1)} %pad_maximum_fusion), channel_id=1, source_target_pairs={{0,8},{4,20},{8,0},{12,28},{16,24},{20,4},{24,16},{28,12},{1,9},{5... | collective-permute-start | bytes 1572872 | tf_op jit(solution)/shard_map/ppermute | solution.py:33
  64.6 10.6 %collective-permute-start.22 = (bf16[512,512]{1,0:T(8,128)(2,1)S(1)}, bf16[512,512]{1,0:T(8,128)(2,1)S(1)}, u32[]{:S(2)}, u32[]{:S(2)}) collective-permute-start(bf16[512,512]{1,0:T(8,128)(2,1)S(1)} %backward.7), channel_id=1, source_target_pairs={{0,4},{4,0},{8,12},{12,8},{16,20},{20,16},{24,28},{28,24},{1,5},{5... | collective-permute-start | bytes 1572872 | tf_op jit(solution)/shard_map/ppermute | solution.py:27
  65.3 6.4 %collective-permute-start.26 = (f32[64,512]{1,0:T(8,128)S(1)}, f32[64,512]{1,0:T(8,128)S(1)}, u32[]{:S(2)}, u32[]{:S(2)}) collective-permute-start(f32[64,512]{1,0:T(8,128)S(1)} %add_multiply_fusion.refs_0_), channel_id=1, source_target_pairs={{0,1},{1,0},{2,3},{3,2},{4,6},{5,7},{6,4},{7,5},{8,9},{9,8},{10,11... | collective-permute-start | bytes 393224 | tf_op jit(solution)/shard_map/ppermute | solution.py:43
  66.0 5.7 %collective-permute-start.27 = (f32[64,512]{1,0:T(8,128)S(1)}, f32[64,512]{1,0:T(8,128)S(1)}, u32[]{:S(2)}, u32[]{:S(2)}) collective-permute-start(f32[64,512]{1,0:T(8,128)S(1)} %add_multiply_fusion.refs_0_), channel_id=1, source_target_pairs={{0,2},{1,3},{2,0},{3,1},{4,5},{5,4},{6,7},{7,6},{8,10},{9,11},{10,... | collective-permute-start | bytes 393224 | tf_op jit(solution)/shard_map/ppermute | solution.py:43
  67.2 7.2 %collective-permute-start.28 = (f32[64,512]{1,0:T(8,128)S(1)}, f32[64,512]{1,0:T(8,128)S(1)}, u32[]{:S(2)}, u32[]{:S(2)}) collective-permute-start(f32[64,512]{1,0:T(8,128)S(1)} %add_multiply_fusion.refs_0_), channel_id=1, source_target_pairs={{0,3},{1,2},{2,1},{3,0},{4,7},{5,6},{6,5},{7,4},{8,11},{9,10},{10,... | collective-permute-start | bytes 393224 | tf_op jit(solution)/shard_map/ppermute | solution.py:43
  74.5 6.3 %collective-permute-start.29 = (f32[256,512]{1,0:T(8,128)S(1)}, f32[256,512]{1,0:T(8,128)S(1)}, u32[]{:S(2)}, u32[]{:S(2)}) collective-permute-start(f32[256,512]{1,0:T(8,128)S(1)} %pad_maximum_fusion.1), channel_id=1, source_target_pairs={{0,4},{4,0},{8,12},{12,8},{16,20},{20,16},{24,28},{28,24},{1,5},{5... | collective-permute-start | bytes 1572872 | tf_op jit(solution)/shard_map/ppermute | solution.py:27
  77.8 10.1 %collective-permute-start.24 = (bf16[256,512]{1,0:T(8,128)(2,1)S(1)}, bf16[256,512]{1,0:T(8,128)(2,1)S(1)}, u32[]{:S(2)}, u32[]{:S(2)}) collective-permute-start(bf16[256,512]{1,0:T(8,128)(2,1)S(1)} %get-tuple-element.92), channel_id=1, source_target_pairs={{0,16},{4,12},{8,24},{12,4},{16,0},{20,28},{24,8},{28,20},{1,17},{... | collective-permute-start | bytes 786440 | tf_op jit(solution)/shard_map/ppermute | solution.py:33
  (2 other events, 5.0 us)

commit v16 on v12

--- a/solution.py
+++ b/solution.py
@@ -186,15 +186,14 @@
 
 def weight_kernel(place_ref, agg_ref, pre_grad_ref, *refs, groups):
     owns, send_ref, part_ref = refs[:groups], refs[groups], refs[groups + 1]
-    core, member = place_ref[0] & 1, place_ref[1]
+    core = place_ref[0] & 1
     rows = owns[0].shape[0]
-    bits = bit_count(groups)
     part_ref[...] = lax.dot_general(
         agg_ref[...], pre_grad_ref[...], (((0,), (0,)), ((), ())), preferred_element_type=jnp.float32
     )
 
     def piece(k, side):
-        start = (2 * (member ^ between(k, 1 - side, bits)) + side) * rows
+        start = (2 * k + side) * rows
         return part_ref[pl.ds(pl.multiple_of(start, rows), rows), :]
 
     for k in range(groups):
@@ -373,10 +372,9 @@
     grads = [grad]
     for k in range(1, groups):
         grads.append(swap_members(grads[k - top_bit(k)], top_bit(k)))
-    part = parts[0]
-    for k in range(1, groups):
-        part = part + swap_members(parts[k].astype(jnp.bfloat16), k, turn=1).astype(jnp.float32)
-    part = part.astype(jnp.bfloat16)
+    parts = jnp.concatenate(parts).astype(jnp.bfloat16).reshape(groups, -1, width)
+    parts = lax.all_to_all(parts, "repl", 0, 0).astype(jnp.float32)
+    part = sum(parts[k] for k in range(groups)).astype(jnp.bfloat16)
     near = swap_chips(part, 1)
     part = part.astype(jnp.float32) + near.astype(jnp.float32)
     grads[-1] = after(grads[-1], near)

time: 88.8 us -> 94.4 us (1.063)
  local copies, waits for them, and re-layouts: 2.93 us -> 7.36 us
  waiting for transfers between devices: 36.9 us -> 38.1 us
    unnamed x8 -> x20, local copies, waits for them, and re-layouts: 2.2 us -> 6.63 us
    ppermute x12 -> x9, starting transfers between devices: 15.7 us -> 11.3 us  [swap_members(): return lax.ppermute(x, ('dom', 'repl'), pairs)]
    all_to_all x0 -> x1, waiting for transfers between devices: none -> 4.4 us  [local(): parts = lax.all_to_all(parts, 'repl', 0, 0).astype(jnp.float32)]
    all_to_all x0 -> x1, starting transfers between devices: none -> 3.65 us  [local(): parts = lax.all_to_all(parts, 'repl', 0, 0).astype(jnp.float32)]
    ppermute x12 -> x9, waiting for transfers between devices: 14.9 us -> 12.9 us  [swap_members(): return lax.ppermute(x, ('dom', 'repl'), pairs)]
    ppermute x7, waiting for transfers between devices: 21.2 us -> 19.9 us  [swap_chips(): lax.ppermute(x, 'dom', [(i, i ^ 2 * between(held, i % 2, bits)) for i in...]
  transfers between devices with their start and end apart: 27 -> 25, of which waited for: 15 -> 13; matrix products, arithmetic and copies ran while one was open for 2% -> 3% of each run, Pallas kernels for 11% -> 11%
where the time goes in v16:
time: 94.4 us; the launch traced here: 94.1 us
  waiting for transfers between devices  38.1 us (40%)
  starting transfers between devices  31.6 us (33%)
  Pallas kernels  14 us (15%)
  local copies, waits for them, and re-layouts  7.36 us (8%)
  other arithmetic  2.14 us (2%)
    ppermute x7, waiting for transfers between devices, swap_chips(): lax.ppermute(x, 'dom', [(i, i ^ 2 * between(held, i % 2, bits)) for i in...  19.9 us
    ppermute x7, starting transfers between devices, swap_chips(): lax.ppermute(x, 'dom', [(i, i ^ 2 * between(held, i % 2, bits)) for i in...  15.8 us
    ppermute x9, waiting for transfers between devices, swap_members(): return lax.ppermute(x, ('dom', 'repl'), pairs)  12.9 us
    ppermute x9, starting transfers between devices, swap_members(): return lax.ppermute(x, ('dom', 'repl'), pairs)  11.3 us
    unnamed x20, local copies, waits for them, and re-layouts  6.63 us
    all_to_all x1, waiting for transfers between devices, local(): parts = lax.all_to_all(parts, 'repl', 0, 0).astype(jnp.float32)  4.4 us
    all_to_all x1, starting transfers between devices, local(): parts = lax.all_to_all(parts, 'repl', 0, 0).astype(jnp.float32)  3.65 us
    pallas_call x4, Pallas kernels, forward(): pl.pallas_call(functools.partial(forward_kernel, which=which, base=base,...  2.82 us
  transfers between devices with their start and end apart: 25, of which 13 were waited for; matrix products, arithmetic and copies ran while one was open for 3% of the time, Pallas kernels for 11%

profile of v16, /device:TPU:0, one launch (start us, length us, event | category | flops | bytes accessed | tf_op | source)
XLA Modules:
  0.0 94.1 jit_solution(7911952133170007824)
XLA Ops:
  0.6 4.1 %collective-permute-start = (bf16[256,512]{1,0:T(8,128)(2,1)}, bf16[256,512]{1,0:T(8,128)(2,1)S(1)}, u32[]{:S(2)}, u32[]{:S(2)}) collective-permute-start(bf16[256,512]{1,0:T(8,128)(2,1)} %refs_1_.1), channel_id=1, source_target_pairs={{0,16},{4,12},{8,24},{12,4},{16,0},{20,28},{24,8},{28,20},{1,17},{... | collective-permute-start | bytes 786440 | tf_op jit(solution)/shard_map/ppermute | solution.py:32
  6.3 4.6 %collective-permute-done.refs_3_ = bf16[256,512]{1,0:T(8,128)(2,1)S(1)} collective-permute-done((bf16[256,512]{1,0:T(8,128)(2,1)}, bf16[256,512]{1,0:T(8,128)(2,1)S(1)}, u32[]{:S(2)}, u32[]{:S(2)}) %collective-permute-start) | collective-permute-done | bytes 262176 | tf_op jit(solution)/shard_map/ppermute | solution.py:32
  10.9 2.4 %collective-permute-start.1 = (bf16[256,512]{1,0:T(8,128)(2,1)}, bf16[256,512]{1,0:T(8,128)(2,1)S(1)}, u32[]{:S(2)}, u32[]{:S(2)}) collective-permute-start(bf16[256,512]{1,0:T(8,128)(2,1)} %refs_1_.1), channel_id=1, source_target_pairs={{0,8},{4,20},{8,0},{12,28},{16,24},{20,4},{24,16},{28,12},{1,9},{5... | collective-permute-start | bytes 786440 | tf_op jit(solution)/shard_map/ppermute | solution.py:32
  13.4 2.2 %copy-done.6 = bf16[1,1,8,16,128,128]{5,4,3,2,1,0:T(8,128)(2,1)S(1)} copy-done((bf16[1,1,8,16,128,128]{5,4,3,2,1,0:T(8,128)(2,1)S(1)}, bf16[1,1,8,16,128,128]{5,4,3,2,1,0:T(8,128)(2,1)}, u32[]{:S(2)}) %copy-start.6) | copy-done | bytes 4194328
  15.6 2.6 %densify.1.refs_0_.a_ref = bf16[8,1024,256]{2,1,0:T(8,128)(2,1)S(1)} custom-call(s32[8,17]{1,0:T(8,128)S(1)} %pad_add_fusion.spots_ref, s32[2]{0:T(128)S(1)} %pad_add_fusion.1.place_ref, bf16[8,16,128,128]{3,2,1,0:T(8,128)(2,1)S(1)} %bitcast.31), custom_call_target="tpu_custom_call" | custom-call | flops 2097152 | bytes 16777216 | tf_op jit(solution)/shard_map/densify/pallas_call | solution.py:86
  18.2 1.2 %forward.4 = (f32[256,512]{1,0:T(8,128)S(1)}, f32[256,512]{1,0:T(8,128)S(1)}, f32[256,512]{1,0:T(8,128)S(1)}, f32[256,512]{1,0:T(8,128)S(1)}) custom-call(bf16[8,1024,256]{2,1,0:T(8,128)(2,1)S(1)} %densify.1.refs_0_.a_ref, bf16[256,512]{1,0:T(8,128)(2,1)S(1)} %copy-done.8, bf16[256,512]{1,0:T(8,128)(2,1)S(1)} %collective-permute-done.2.refs_2_, ...), custom_call_target="tpu_custom_call" | custom-call | flops 1073741824 | bytes 4194304 | tf_op jit(solution)/shard_map/forward/pallas_call | solution.py:140
  19.5 3.4 %collective-permute-done.1.refs_1_ = bf16[256,512]{1,0:T(8,128)(2,1)S(1)} collective-permute-done((bf16[256,512]{1,0:T(8,128)(2,1)}, bf16[256,512]{1,0:T(8,128)(2,1)S(1)}, u32[]{:S(2)}, u32[]{:S(2)}) %collective-permute-start.1) | collective-permute-done | bytes 262176 | tf_op jit(solution)/shard_map/ppermute | solution.py:32
  22.9 3.4 %collective-permute-done.5.refs_2_ = bf16[256,512]{1,0:T(8,128)(2,1)S(1)} collective-permute-done((bf16[256,512]{1,0:T(8,128)(2,1)S(1)}, bf16[256,512]{1,0:T(8,128)(2,1)S(1)}, u32[]{:S(2)}, u32[]{:S(2)}) %collective-permute-start.5) | collective-permute-done | bytes 262176 | tf_op jit(solution)/shard_map/ppermute | solution.py:32
  28.3 1.7 %collective-permute-start.8 = (bf16[256,512]{1,0:T(8,128)(2,1)S(1)}, bf16[256,512]{1,0:T(8,128)(2,1)S(1)}, u32[]{:S(2)}, u32[]{:S(2)}) collective-permute-start(bf16[256,512]{1,0:T(8,128)(2,1)S(1)} %get-tuple-element.55), channel_id=1, source_target_pairs={{0,1},{1,0},{2,3},{3,2},{4,6},{5,7},{6,4},{7,5},{8,9},{9,8},{10,11... | collective-permute-start | bytes 786440 | tf_op jit(solution)/shard_map/ppermute | solution.py:42
  30.8 3.9 %collective-permute-done.8 = bf16[256,512]{1,0:T(8,128)(2,1)S(1)} collective-permute-done((bf16[256,512]{1,0:T(8,128)(2,1)S(1)}, bf16[256,512]{1,0:T(8,128)(2,1)S(1)}, u32[]{:S(2)}, u32[]{:S(2)}) %collective-permute-start.8) | collective-permute-done | bytes 262176 | tf_op jit(solution)/shard_map/ppermute | solution.py:42
  34.8 1.8 %collective-permute-start.9 = (bf16[256,512]{1,0:T(8,128)(2,1)S(1)}, bf16[256,512]{1,0:T(8,128)(2,1)S(1)}, u32[]{:S(2)}, u32[]{:S(2)}) collective-permute-start(bf16[256,512]{1,0:T(8,128)(2,1)S(1)} %add_convert_fusion.2), channel_id=1, source_target_pairs={{0,2},{1,3},{2,0},{3,1},{4,5},{5,4},{6,7},{7,6},{8,10},{9,11},{10,... | collective-permute-start | bytes 786440 | tf_op jit(solution)/shard_map/ppermute | solution.py:42
  36.6 1.7 %collective-permute-done.7.refs_1_ = bf16[256,512]{1,0:T(8,128)(2,1)S(1)} collective-permute-done((bf16[256,512]{1,0:T(8,128)(2,1)S(1)}, bf16[256,512]{1,0:T(8,128)(2,1)S(1)}, u32[]{:S(2)}, u32[]{:S(2)}) %collective-permute-start.7) | collective-permute-done | bytes 262176 | tf_op jit(solution)/shard_map/ppermute | solution.py:42
  38.2 1.2 %transposed.1 = (bf16[2,256,1024]{2,1,0:T(8,128)(2,1)S(1)}, bf16[2,256,1024]{2,1,0:T(8,128)(2,1)S(1)}, bf16[2,256,1024]{2,1,0:T(8,128)(2,1)S(1)}, bf16[2,256,1024]{2,1,0:T(8,128)(2,1)S(1)}) custom-call(bf16[8,1024,256]{2,1,0:T(8,128)(2,1)S(1)} %densify.1.refs_0_.a_ref), custom_call_target="tpu_custom_call" | custom-call | bytes 8388608 | tf_op jit(solution)/shard_map/transposed/pallas_call | solution.py:111
  41.4 1.2 %middle.1 = (bf16[256,512]{1,0:T(8,128)(2,1)}, bf16[256,512]{1,0:T(8,128)(2,1)S(1)}, bf16[256,512]{1,0:T(8,128)(2,1)S(1)}, bf16[256,512]{1,0:T(8,128)(2,1)S(1)}) custom-call(f32[256,512]{1,0:T(8,128)S(1)} %get-tuple-element.59.refs_0_, bf16[256,512]{1,0:T(8,128)(2,1)S(1)} %collective-permute-done.7.refs_1_, ...), custom_call_target="tpu_custom_call" | custom-call | flops 268435456 | bytes 1310720 | tf_op jit(solution)/shard_map/middle/pallas_call | solution.py:175
  43.6 1.8 %collective-permute-start.10 = (bf16[256,512]{1,0:T(8,128)(2,1)S(1)}, bf16[256,512]{1,0:T(8,128)(2,1)S(1)}, u32[]{:S(2)}, u32[]{:S(2)}) collective-permute-start(bf16[256,512]{1,0:T(8,128)(2,1)S(1)} %get-tuple-element.80.refs_2_), channel_id=1, source_target_pairs={{0,2},{1,3},{2,0},{3,1},{4,5},{5,4},{6,7},{7,6},{8,10},{9,11},{10,... | collective-permute-start | bytes 786440 | tf_op jit(solution)/shard_map/ppermute | solution.py:42
  46.2 3.6 %all-to-all-start = ((bf16[4,64,512]{2,1,0:T(8,128)(2,1)}), bf16[4,64,512]{2,1,0:T(8,128)(2,1)S(1)}, u32[]{:S(2)}, u32[]{:S(2)}) async-start(bf16[4,64,512]{2,1,0:T(8,128)(2,1)} %bitcast.6), calls=%async_computation | async-start | bytes 524288 | tf_op jit(solution)/shard_map/all_to_all | solution.py:376
  49.9 2.0 %collective-permute-start.11 = (bf16[256,512]{1,0:T(8,128)(2,1)S(1)}, bf16[256,512]{1,0:T(8,128)(2,1)S(1)}, u32[]{:S(2)}, u32[]{:S(2)}) collective-permute-start(bf16[256,512]{1,0:T(8,128)(2,1)S(1)} %get-tuple-element.80.refs_2_), channel_id=1, source_target_pairs={{0,1},{1,0},{2,3},{3,2},{4,6},{5,7},{6,4},{7,5},{8,9},{9,8},{10,11... | collective-permute-start | bytes 786440 | tf_op jit(solution)/shard_map/ppermute | solution.py:42
  51.9 4.4 %all-to-all-done = bf16[4,64,512]{2,1,0:T(8,128)(2,1)S(1)} async-done(((bf16[4,64,512]{2,1,0:T(8,128)(2,1)}), bf16[4,64,512]{2,1,0:T(8,128)(2,1)S(1)}, u32[]{:S(2)}, u32[]{:S(2)}) %all-to-all-start) | async-done | bytes 262176 | tf_op jit(solution)/shard_map/all_to_all | solution.py:376
  56.4 3.0 %collective-permute-start.14 = (bf16[64,512]{1,0:T(8,128)(2,1)S(1)}, bf16[64,512]{1,0:T(8,128)(2,1)S(1)}, u32[]{:S(2)}, u32[]{:S(2)}) collective-permute-start(bf16[64,512]{1,0:T(8,128)(2,1)S(1)} %fusion.1), channel_id=1, source_target_pairs={{0,16},{4,12},{8,24},{12,4},{16,0},{20,28},{24,8},{28,20},{1,17},{... | collective-permute-start | bytes 196616 | tf_op jit(solution)/shard_map/ppermute | solution.py:32
  59.4 1.5 %collective-permute-done.12.refs_5_ = bf16[256,512]{1,0:T(8,128)(2,1)S(1)} collective-permute-done((bf16[256,512]{1,0:T(8,128)(2,1)S(1)}, bf16[256,512]{1,0:T(8,128)(2,1)S(1)}, u32[]{:S(2)}, u32[]{:S(2)}) %collective-permute-start.12) | collective-permute-done | bytes 262176 | tf_op jit(solution)/shard_map/ppermute | solution.py:42
  61.7 1.2 %copy-done.1 = bf16[2,256,1024]{2,1,0:T(8,128)(2,1)S(1)} copy-done((bf16[2,256,1024]{2,1,0:T(8,128)(2,1)S(1)}, bf16[2,256,1024]{2,1,0:T(8,128)(2,1)}, u32[]{:S(2)}) %copy-start.1) | copy-done | bytes 1048600
  62.9 1.2 %copy-done.4 = bf16[2,256,1024]{2,1,0:T(8,128)(2,1)S(1)} copy-done((bf16[2,256,1024]{2,1,0:T(8,128)(2,1)S(1)}, bf16[2,256,1024]{2,1,0:T(8,128)(2,1)}, u32[]{:S(2)}) %copy-start.4) | copy-done | bytes 1048600
  65.0 2.3 %collective-permute-start.19 = (bf16[64,512]{1,0:T(8,128)(2,1)S(1)}, bf16[64,512]{1,0:T(8,128)(2,1)S(1)}, u32[]{:S(2)}, u32[]{:S(2)}) collective-permute-start(bf16[64,512]{1,0:T(8,128)(2,1)S(1)} %add_convert_fusion.3), channel_id=1, source_target_pairs={{0,8},{4,20},{8,0},{12,28},{16,24},{20,4},{24,16},{28,12},{1,9},{5... | collective-permute-start | bytes 196616 | tf_op jit(solution)/shard_map/ppermute | solution.py:32
  68.2 1.1 %collective-permute-start.17 = (bf16[512,512]{1,0:T(8,128)(2,1)S(1)}, bf16[512,512]{1,0:T(8,128)(2,1)S(1)}, u32[]{:S(2)}, u32[]{:S(2)}) collective-permute-start(bf16[512,512]{1,0:T(8,128)(2,1)S(1)} %pad_maximum_fusion), channel_id=1, source_target_pairs={{0,8},{4,20},{8,0},{12,28},{16,24},{20,4},{24,16},{28,12},{1,9},{5... | collective-permute-start | bytes 1572872 | tf_op jit(solution)/shard_map/ppermute | solution.py:32
  70.7 1.3 %collective-permute-start.20 = (f32[64,512]{1,0:T(8,128)S(1)}, f32[64,512]{1,0:T(8,128)S(1)}, u32[]{:S(2)}, u32[]{:S(2)}) collective-permute-start(f32[64,512]{1,0:T(8,128)S(1)} %add_multiply_fusion.refs_0_), channel_id=1, source_target_pairs={{0,1},{1,0},{2,3},{3,2},{4,6},{5,7},{6,4},{7,5},{8,9},{9,8},{10,11... | collective-permute-start | bytes 393224 | tf_op jit(solution)/shard_map/ppermute | solution.py:42
  72.5 1.7 %collective-permute-start.22 = (f32[64,512]{1,0:T(8,128)S(1)}, f32[64,512]{1,0:T(8,128)S(1)}, u32[]{:S(2)}, u32[]{:S(2)}) collective-permute-start(f32[64,512]{1,0:T(8,128)S(1)} %add_multiply_fusion.refs_0_), channel_id=1, source_target_pairs={{0,3},{1,2},{2,1},{3,0},{4,7},{5,6},{6,5},{7,4},{8,11},{9,10},{10,... | collective-permute-start | bytes 393224 | tf_op jit(solution)/shard_map/ppermute | solution.py:42
  74.2 2.8 %collective-permute-done.20.refs_1_ = f32[64,512]{1,0:T(8,128)S(1)} collective-permute-done((f32[64,512]{1,0:T(8,128)S(1)}, f32[64,512]{1,0:T(8,128)S(1)}, u32[]{:S(2)}, u32[]{:S(2)}) %collective-permute-start.20) | collective-permute-done | bytes 131104 | tf_op jit(solution)/shard_map/ppermute | solution.py:42
  77.0 3.0 %collective-permute-done.22.refs_3_ = f32[64,512]{1,0:T(8,128)S(1)} collective-permute-done((f32[64,512]{1,0:T(8,128)S(1)}, f32[64,512]{1,0:T(8,128)S(1)}, u32[]{:S(2)}, u32[]{:S(2)}) %collective-permute-start.22) | collective-permute-done | bytes 131104 | tf_op jit(solution)/shard_map/ppermute | solution.py:42
  81.0 2.1 %collective-permute-done.17.refs_3_ = bf16[512,512]{1,0:T(8,128)(2,1)S(1)} collective-permute-done((bf16[512,512]{1,0:T(8,128)(2,1)S(1)}, bf16[512,512]{1,0:T(8,128)(2,1)S(1)}, u32[]{:S(2)}, u32[]{:S(2)}) %collective-permute-start.17) | collective-permute-done | bytes 524320 | tf_op jit(solution)/shard_map/ppermute | solution.py:32
  83.2 2.8 %collective-permute-start.18 = (bf16[256,512]{1,0:T(8,128)(2,1)S(1)}, bf16[256,512]{1,0:T(8,128)(2,1)S(1)}, u32[]{:S(2)}, u32[]{:S(2)}) collective-permute-start(bf16[256,512]{1,0:T(8,128)(2,1)S(1)} %get-tuple-element.84), channel_id=1, source_target_pairs={{0,16},{4,12},{8,24},{12,4},{16,0},{20,28},{24,8},{28,20},{1,17},{... | collective-permute-start | bytes 786440 | tf_op jit(solution)/shard_map/ppermute | solution.py:32
  86.0 1.6 %place_slices.1 = f32[512,512]{1,0:T(8,128)} custom-call(s32[2]{0:T(128)S(1)} %pad_add_fusion.1.place_ref, f32[64,512]{1,0:T(8,128)S(1)} %add_multiply_fusion.refs_0_, f32[64,512]{1,0:T(8,128)S(1)} %collective-permute-done.20.refs_1_, f32[64,512]{1,0:T(8,128)S(1)} %collective-permute-done.21.refs_2_, f32[64,512]{1,0:T(8,128)S(1)} %collective-permute-done.22.refs_3_, ...), custom_call_target="tpu_custom_call" | custom-call | bytes 2097152 | tf_op jit(solution)/shard_map/place_slices/pallas_call | solution.py:235
  87.6 5.7 %collective-permute-done.18.refs_1_ = bf16[256,512]{1,0:T(8,128)(2,1)S(1)} collective-permute-done((bf16[256,512]{1,0:T(8,128)(2,1)S(1)}, bf16[256,512]{1,0:T(8,128)(2,1)S(1)}, u32[]{:S(2)}, u32[]{:S(2)}) %collective-permute-start.18) | collective-permute-done | bytes 262176 | tf_op jit(solution)/shard_map/ppermute | solution.py:32
  (67 shorter events, 14.6 us)
Async XLA Ops:
  0.6 10.2 %collective-permute-start = (bf16[256,512]{1,0:T(8,128)(2,1)}, bf16[256,512]{1,0:T(8,128)(2,1)S(1)}, u32[]{:S(2)}, u32[]{:S(2)}) collective-permute-start(bf16[256,512]{1,0:T(8,128)(2,1)} %refs_1_.1), channel_id=1, source_target_pairs={{0,16},{4,12},{8,24},{12,4},{16,0},{20,28},{24,8},{28,20},{1,17},{... | collective-permute-start | bytes 786440 | tf_op jit(solution)/shard_map/ppermute | solution.py:32
  4.7 13.5 %collective-permute-start.2 = (bf16[256,512]{1,0:T(8,128)(2,1)}, bf16[256,512]{1,0:T(8,128)(2,1)S(1)}, u32[]{:S(2)}, u32[]{:S(2)}) collective-permute-start(bf16[256,512]{1,0:T(8,128)(2,1)} %refs_1_.1), channel_id=1, source_target_pairs={{0,4},{4,0},{8,12},{12,8},{16,20},{20,16},{24,28},{28,24},{1,5},{5... | collective-permute-start | bytes 786440 | tf_op jit(solution)/shard_map/ppermute | solution.py:26
  10.9 7.3 %collective-permute-start.3 = (bf16[256,512]{1,0:T(8,128)(2,1)S(1)}, bf16[256,512]{1,0:T(8,128)(2,1)S(1)}, u32[]{:S(2)}, u32[]{:S(2)}) collective-permute-start(bf16[256,512]{1,0:T(8,128)(2,1)S(1)} %collective-permute-done.refs_3_), channel_id=1, source_target_pairs={{0,4},{4,0},{8,12},{12,8},{16,20},{20,16},{24,28},{28,24},{1,5},{5... | collective-permute-start | bytes 786440 | tf_op jit(solution)/shard_map/ppermute | solution.py:26
  10.9 12.1 %collective-permute-start.1 = (bf16[256,512]{1,0:T(8,128)(2,1)}, bf16[256,512]{1,0:T(8,128)(2,1)S(1)}, u32[]{:S(2)}, u32[]{:S(2)}) collective-permute-start(bf16[256,512]{1,0:T(8,128)(2,1)} %refs_1_.1), channel_id=1, source_target_pairs={{0,8},{4,20},{8,0},{12,28},{16,24},{20,4},{24,16},{28,12},{1,9},{5... | collective-permute-start | bytes 786440 | tf_op jit(solution)/shard_map/ppermute | solution.py:32
  13.3 13.0 %collective-permute-start.5 = (bf16[256,512]{1,0:T(8,128)(2,1)S(1)}, bf16[256,512]{1,0:T(8,128)(2,1)S(1)}, u32[]{:S(2)}, u32[]{:S(2)}) collective-permute-start(bf16[256,512]{1,0:T(8,128)(2,1)S(1)} %collective-permute-done.refs_3_), channel_id=1, source_target_pairs={{0,8},{4,20},{8,0},{12,28},{16,24},{20,4},{24,16},{28,12},{1,9},{5... | collective-permute-start | bytes 786440 | tf_op jit(solution)/shard_map/ppermute | solution.py:32
  13.4 2.2 %copy-start.6 = (bf16[1,1,8,16,128,128]{5,4,3,2,1,0:T(8,128)(2,1)S(1)}, bf16[1,1,8,16,128,128]{5,4,3,2,1,0:T(8,128)(2,1)}, u32[]{:S(2)}) copy-start(bf16[1,1,8,16,128,128]{5,4,3,2,1,0:T(8,128)(2,1)} %param.10) | copy-start | bytes 12582916
  15.6 2.6 %copy-start.8 = (bf16[256,512]{1,0:T(8,128)(2,1)S(1)}, bf16[256,512]{1,0:T(8,128)(2,1)}, u32[]{:S(2)}) copy-start(bf16[256,512]{1,0:T(8,128)(2,1)} %refs_1_.1) | copy-start | bytes 786436
  22.9 4.1 %collective-permute-start.4 = (bf16[256,512]{1,0:T(8,128)(2,1)S(1)}, bf16[256,512]{1,0:T(8,128)(2,1)S(1)}, u32[]{:S(2)}, u32[]{:S(2)}) collective-permute-start(bf16[256,512]{1,0:T(8,128)(2,1)S(1)} %collective-permute-done.1.refs_1_), channel_id=1, source_target_pairs={{0,4},{4,0},{8,12},{12,8},{16,20},{20,16},{24,28},{28,24},{1,5},{5... | collective-permute-start | bytes 786440 | tf_op jit(solution)/shard_map/ppermute | solution.py:26
  26.3 1.5 %collective-permute-start.6 = (bf16[256,512]{1,0:T(8,128)(2,1)S(1)}, bf16[256,512]{1,0:T(8,128)(2,1)S(1)}, u32[]{:S(2)}, u32[]{:S(2)}) collective-permute-start(bf16[256,512]{1,0:T(8,128)(2,1)S(1)} %collective-permute-done.5.refs_2_), channel_id=1, source_target_pairs={{0,4},{4,0},{8,12},{12,8},{16,20},{20,16},{24,28},{28,24},{1,5},{5... | collective-permute-start | bytes 786440 | tf_op jit(solution)/shard_map/ppermute | solution.py:26
  28.3 6.4 %collective-permute-start.8 = (bf16[256,512]{1,0:T(8,128)(2,1)S(1)}, bf16[256,512]{1,0:T(8,128)(2,1)S(1)}, u32[]{:S(2)}, u32[]{:S(2)}) collective-permute-start(bf16[256,512]{1,0:T(8,128)(2,1)S(1)} %get-tuple-element.55), channel_id=1, source_target_pairs={{0,1},{1,0},{2,3},{3,2},{4,6},{5,7},{6,4},{7,5},{8,9},{9,8},{10,11... | collective-permute-start | bytes 786440 | tf_op jit(solution)/shard_map/ppermute | solution.py:42
  30.0 8.2 %collective-permute-start.7 = (bf16[256,512]{1,0:T(8,128)(2,1)S(1)}, bf16[256,512]{1,0:T(8,128)(2,1)S(1)}, u32[]{:S(2)}, u32[]{:S(2)}) collective-permute-start(bf16[256,512]{1,0:T(8,128)(2,1)S(1)} %get-tuple-element.54), channel_id=1, source_target_pairs={{0,1},{1,0},{2,3},{3,2},{4,6},{5,7},{6,4},{7,5},{8,9},{9,8},{10,11... | collective-permute-start | bytes 786440 | tf_op jit(solution)/shard_map/ppermute | solution.py:42
  30.4 11.1 %copy-start.7 = (bf16[512,512]{1,0:T(8,128)(2,1)S(1)}, bf16[512,512]{1,0:T(8,128)(2,1)}, u32[]{:S(2)}) copy-start(bf16[512,512]{1,0:T(8,128)(2,1)} %refs_4_.1) | copy-start | bytes 1572868
  30.4 11.1 %copy-start.9 = (bf16[256,512]{1,0:T(8,128)(2,1)S(1)}, bf16[256,512]{1,0:T(8,128)(2,1)}, u32[]{:S(2)}) copy-start(bf16[256,512]{1,0:T(8,128)(2,1)} %refs_3_.1) | copy-start | bytes 786436
  34.8 6.6 %collective-permute-start.9 = (bf16[256,512]{1,0:T(8,128)(2,1)S(1)}, bf16[256,512]{1,0:T(8,128)(2,1)S(1)}, u32[]{:S(2)}, u32[]{:S(2)}) collective-permute-start(bf16[256,512]{1,0:T(8,128)(2,1)S(1)} %add_convert_fusion.2), channel_id=1, source_target_pairs={{0,2},{1,3},{2,0},{3,1},{4,5},{5,4},{6,7},{7,6},{8,10},{9,11},{10,... | collective-permute-start | bytes 786440 | tf_op jit(solution)/shard_map/ppermute | solution.py:42
  43.6 1.9 %collective-permute-start.13 = (bf16[256,512]{1,0:T(8,128)(2,1)S(1)}, bf16[256,512]{1,0:T(8,128)(2,1)S(1)}, u32[]{:S(2)}, u32[]{:S(2)}) collective-permute-start(bf16[256,512]{1,0:T(8,128)(2,1)S(1)} %get-tuple-element.72), channel_id=1, source_target_pairs={{0,4},{4,0},{8,12},{12,8},{16,20},{20,16},{24,28},{28,24},{1,5},{5... | collective-permute-start | bytes 786440 | tf_op jit(solution)/shard_map/ppermute | solution.py:26
  43.6 8.3 %collective-permute-start.10 = (bf16[256,512]{1,0:T(8,128)(2,1)S(1)}, bf16[256,512]{1,0:T(8,128)(2,1)S(1)}, u32[]{:S(2)}, u32[]{:S(2)}) collective-permute-start(bf16[256,512]{1,0:T(8,128)(2,1)S(1)} %get-tuple-element.80.refs_2_), channel_id=1, source_target_pairs={{0,2},{1,3},{2,0},{3,1},{4,5},{5,4},{6,7},{7,6},{8,10},{9,11},{10,... | collective-permute-start | bytes 786440 | tf_op jit(solution)/shard_map/ppermute | solution.py:42
  46.2 10.1 %all-to-all-start = ((bf16[4,64,512]{2,1,0:T(8,128)(2,1)}), bf16[4,64,512]{2,1,0:T(8,128)(2,1)S(1)}, u32[]{:S(2)}, u32[]{:S(2)}) async-start(bf16[4,64,512]{2,1,0:T(8,128)(2,1)} %bitcast.6), calls=%async_computation | async-start | bytes 524288 | tf_op jit(solution)/shard_map/all_to_all | solution.py:376
  49.9 11.8 %collective-permute-start.11 = (bf16[256,512]{1,0:T(8,128)(2,1)S(1)}, bf16[256,512]{1,0:T(8,128)(2,1)S(1)}, u32[]{:S(2)}, u32[]{:S(2)}) collective-permute-start(bf16[256,512]{1,0:T(8,128)(2,1)S(1)} %get-tuple-element.80.refs_2_), channel_id=1, source_target_pairs={{0,1},{1,0},{2,3},{3,2},{4,6},{5,7},{6,4},{7,5},{8,9},{9,8},{10,11... | collective-permute-start | bytes 786440 | tf_op jit(solution)/shard_map/ppermute | solution.py:42
  51.9 9.1 %collective-permute-start.12 = (bf16[256,512]{1,0:T(8,128)(2,1)S(1)}, bf16[256,512]{1,0:T(8,128)(2,1)S(1)}, u32[]{:S(2)}, u32[]{:S(2)}) collective-permute-start(bf16[256,512]{1,0:T(8,128)(2,1)S(1)} %collective-permute-done.10.refs_3_), channel_id=1, source_target_pairs={{0,1},{1,0},{2,3},{3,2},{4,6},{5,7},{6,4},{7,5},{8,9},{9,8},{10,11... | collective-permute-start | bytes 786440 | tf_op jit(solution)/shard_map/ppermute | solution.py:42
  56.3 10.9 %copy-start.2 = (bf16[2,256,1024]{2,1,0:T(8,128)(2,1)S(1)}, bf16[2,256,1024]{2,1,0:T(8,128)(2,1)}, u32[]{:S(2)}) copy-start(bf16[2,256,1024]{2,1,0:T(8,128)(2,1)} %copy-done) | copy-start | bytes 3145732
  56.4 5.2 %collective-permute-start.14 = (bf16[64,512]{1,0:T(8,128)(2,1)S(1)}, bf16[64,512]{1,0:T(8,128)(2,1)S(1)}, u32[]{:S(2)}, u32[]{:S(2)}) collective-permute-start(bf16[64,512]{1,0:T(8,128)(2,1)S(1)} %fusion.1), channel_id=1, source_target_pairs={{0,16},{4,12},{8,24},{12,4},{16,0},{20,28},{24,8},{28,20},{1,17},{... | collective-permute-start | bytes 196616 | tf_op jit(solution)/shard_map/ppermute | solution.py:32
  61.7 1.2 %copy-start.1 = (bf16[2,256,1024]{2,1,0:T(8,128)(2,1)S(1)}, bf16[2,256,1024]{2,1,0:T(8,128)(2,1)}, u32[]{:S(2)}) copy-start(bf16[2,256,1024]{2,1,0:T(8,128)(2,1)} %copy-done) | copy-start | bytes 3145732
  64.1 3.1 %copy-start.5 = (bf16[2,256,1024]{2,1,0:T(8,128)(2,1)S(1)}, bf16[2,256,1024]{2,1,0:T(8,128)(2,1)}, u32[]{:S(2)}) copy-start(bf16[2,256,1024]{2,1,0:T(8,128)(2,1)} %copy-done.3) | copy-start | bytes 3145732
  64.8 3.1 %collective-permute-start.15 = (bf16[512,512]{1,0:T(8,128)(2,1)S(1)}, bf16[512,512]{1,0:T(8,128)(2,1)S(1)}, u32[]{:S(2)}, u32[]{:S(2)}) collective-permute-start(bf16[512,512]{1,0:T(8,128)(2,1)S(1)} %backward.4), channel_id=1, source_target_pairs={{0,4},{4,0},{8,12},{12,8},{16,20},{20,16},{24,28},{28,24},{1,5},{5... | collective-permute-start | bytes 1572872 | tf_op jit(solution)/shard_map/ppermute | solution.py:26
  65.0 5.7 %collective-permute-start.19 = (bf16[64,512]{1,0:T(8,128)(2,1)S(1)}, bf16[64,512]{1,0:T(8,128)(2,1)S(1)}, u32[]{:S(2)}, u32[]{:S(2)}) collective-permute-start(bf16[64,512]{1,0:T(8,128)(2,1)S(1)} %add_convert_fusion.3), channel_id=1, source_target_pairs={{0,8},{4,20},{8,0},{12,28},{16,24},{20,4},{24,16},{28,12},{1,9},{5... | collective-permute-start | bytes 196616 | tf_op jit(solution)/shard_map/ppermute | solution.py:32
  68.2 14.9 %collective-permute-start.17 = (bf16[512,512]{1,0:T(8,128)(2,1)S(1)}, bf16[512,512]{1,0:T(8,128)(2,1)S(1)}, u32[]{:S(2)}, u32[]{:S(2)}) collective-permute-start(bf16[512,512]{1,0:T(8,128)(2,1)S(1)} %pad_maximum_fusion), channel_id=1, source_target_pairs={{0,8},{4,20},{8,0},{12,28},{16,24},{20,4},{24,16},{28,12},{1,9},{5... | collective-permute-start | bytes 1572872 | tf_op jit(solution)/shard_map/ppermute | solution.py:32
  70.0 11.0 %collective-permute-start.16 = (bf16[512,512]{1,0:T(8,128)(2,1)S(1)}, bf16[512,512]{1,0:T(8,128)(2,1)S(1)}, u32[]{:S(2)}, u32[]{:S(2)}) collective-permute-start(bf16[512,512]{1,0:T(8,128)(2,1)S(1)} %backward.7), channel_id=1, source_target_pairs={{0,4},{4,0},{8,12},{12,8},{16,20},{20,16},{24,28},{28,24},{1,5},{5... | collective-permute-start | bytes 1572872 | tf_op jit(solution)/shard_map/ppermute | solution.py:26
  70.7 6.4 %collective-permute-start.20 = (f32[64,512]{1,0:T(8,128)S(1)}, f32[64,512]{1,0:T(8,128)S(1)}, u32[]{:S(2)}, u32[]{:S(2)}) collective-permute-start(f32[64,512]{1,0:T(8,128)S(1)} %add_multiply_fusion.refs_0_), channel_id=1, source_target_pairs={{0,1},{1,0},{2,3},{3,2},{4,6},{5,7},{6,4},{7,5},{8,9},{9,8},{10,11... | collective-permute-start | bytes 393224 | tf_op jit(solution)/shard_map/ppermute | solution.py:42
  72.0 5.0 %collective-permute-start.21 = (f32[64,512]{1,0:T(8,128)S(1)}, f32[64,512]{1,0:T(8,128)S(1)}, u32[]{:S(2)}, u32[]{:S(2)}) collective-permute-start(f32[64,512]{1,0:T(8,128)S(1)} %add_multiply_fusion.refs_0_), channel_id=1, source_target_pairs={{0,2},{1,3},{2,0},{3,1},{4,5},{5,4},{6,7},{7,6},{8,10},{9,11},{10,... | collective-permute-start | bytes 393224 | tf_op jit(solution)/shard_map/ppermute | solution.py:42
  72.5 7.5 %collective-permute-start.22 = (f32[64,512]{1,0:T(8,128)S(1)}, f32[64,512]{1,0:T(8,128)S(1)}, u32[]{:S(2)}, u32[]{:S(2)}) collective-permute-start(f32[64,512]{1,0:T(8,128)S(1)} %add_multiply_fusion.refs_0_), channel_id=1, source_target_pairs={{0,3},{1,2},{2,1},{3,0},{4,7},{5,6},{6,5},{7,4},{8,11},{9,10},{10,... | collective-permute-start | bytes 393224 | tf_op jit(solution)/shard_map/ppermute | solution.py:42
  80.1 6.0 %collective-permute-start.23 = (f32[256,512]{1,0:T(8,128)S(1)}, f32[256,512]{1,0:T(8,128)S(1)}, u32[]{:S(2)}, u32[]{:S(2)}) collective-permute-start(f32[256,512]{1,0:T(8,128)S(1)} %pad_maximum_fusion.1), channel_id=1, source_target_pairs={{0,4},{4,0},{8,12},{12,8},{16,20},{20,16},{24,28},{28,24},{1,5},{5... | collective-permute-start | bytes 1572872 | tf_op jit(solution)/shard_map/ppermute | solution.py:26
  83.2 10.1 %collective-permute-start.18 = (bf16[256,512]{1,0:T(8,128)(2,1)S(1)}, bf16[256,512]{1,0:T(8,128)(2,1)S(1)}, u32[]{:S(2)}, u32[]{:S(2)}) collective-permute-start(bf16[256,512]{1,0:T(8,128)(2,1)S(1)} %get-tuple-element.84), channel_id=1, source_target_pairs={{0,16},{4,12},{8,24},{12,4},{16,0},{20,28},{24,8},{28,20},{1,17},{... | collective-permute-start | bytes 786440 | tf_op jit(solution)/shard_map/ppermute | solution.py:32
  (3 other events, 3.2 us)

commit v17 on v12

--- a/solution.py
+++ b/solution.py
@@ -30,6 +30,10 @@
     blocks = lax.axis_size("dom")
     bits = bit_count(blocks // 2)
     return lax.ppermute(x, "dom", [(i, i ^ (2 * between(held, i % 2, bits))) for i in range(blocks)])
+
+
+def swap_line(x, mask):
+    return lax.ppermute(x, "dom", [(i, i ^ (2 * mask)) for i in range(lax.axis_size("dom"))])
 
 
 def swap_members(x, held, turn=0):
@@ -377,7 +381,7 @@
     for k in range(1, groups):
         part = part + swap_members(parts[k].astype(jnp.bfloat16), k, turn=1).astype(jnp.float32)
     part = part.astype(jnp.bfloat16)
-    near = swap_chips(part, 1)
+    near = swap_line(part, 1)
     part = part.astype(jnp.float32) + near.astype(jnp.float32)
     grads[-1] = after(grads[-1], near)
 
@@ -399,7 +403,7 @@
     bit = 2
     while bit < chips:
         part = part.astype(jnp.bfloat16)
-        part = part.astype(jnp.float32) + swap_chips(part, bit).astype(jnp.float32)
+        part = part.astype(jnp.float32) + swap_line(part, bit).astype(jnp.float32)
         bit *= 2
     part = part * scale
     parts = [part] + [swap_members(part, k, turn=1) for k in range(1, groups)]

time: 88.8 us -> 89.2 us (level)
  the two profiles are of different devices: /device:TPU:0 before, /device:TPU:12 now
where the time goes in v17:
time: 89.2 us; the launch traced here: 89 us
  waiting for transfers between devices  41.5 us (47%)
  starting transfers between devices  28.3 us (32%)
  Pallas kernels  14 us (16%)
  local copies, waits for them, and re-layouts  2.93 us (3%)
  other arithmetic  1.31 us (1%)
    ppermute x12, waiting for transfers between devices, swap_members(): return lax.ppermute(x, ('dom', 'repl'), pairs)  16.6 us
    ppermute x5, waiting for transfers between devices, swap_chips(): lax.ppermute(x, 'dom', [(i, i ^ 2 * between(held, i % 2, bits)) for i in...  16.1 us
    ppermute x12, starting transfers between devices, swap_members(): return lax.ppermute(x, ('dom', 'repl'), pairs)  13.4 us
    ppermute x5, starting transfers between devices, swap_chips(): lax.ppermute(x, 'dom', [(i, i ^ 2 * between(held, i % 2, bits)) for i in...  8.43 us
    ppermute x2, waiting for transfers between devices, swap_line(): lax.ppermute(x, 'dom', [(i, i ^ 2 * mask) for i in range(lax.axis_size('d...  7.37 us
    ppermute x8, starting transfers between devices, swap_cores(): lax.ppermute(x, 'dom', [(i, i ^ 1) for i in range(lax.axis_size('dom'))])  3.41 us
    ppermute x2, starting transfers between devices, swap_line(): lax.ppermute(x, 'dom', [(i, i ^ 2 * mask) for i in range(lax.axis_size('d...  3.13 us
    pallas_call x4, Pallas kernels, backward(): pl.pallas_call(functools.partial(backward_kernel, side=side, count=count,...  2.82 us
  transfers between devices with their start and end apart: 27, of which 15 were waited for; matrix products, arithmetic and copies ran while one was open for 2% of the time, Pallas kernels for 11%

profile of v17, /device:TPU:12, one launch (start us, length us, event | category | flops | bytes accessed | tf_op | source)
XLA Modules:
  0.0 89.0 jit_solution(60409419652851279)
XLA Ops:
  0.6 2.7 %collective-permute-start = (bf16[256,512]{1,0:T(8,128)(2,1)}, bf16[256,512]{1,0:T(8,128)(2,1)S(1)}, u32[]{:S(2)}, u32[]{:S(2)}) collective-permute-start(bf16[256,512]{1,0:T(8,128)(2,1)} %refs_1_.1), channel_id=1, source_target_pairs={{0,16},{4,12},{8,24},{12,4},{16,0},{20,28},{24,8},{28,20},{1,17},{... | collective-permute-start | bytes 786440 | tf_op jit(solution)/shard_map/ppermute | solution.py:32
  4.8 5.5 %collective-permute-done.refs_3_ = bf16[256,512]{1,0:T(8,128)(2,1)S(1)} collective-permute-done((bf16[256,512]{1,0:T(8,128)(2,1)}, bf16[256,512]{1,0:T(8,128)(2,1)S(1)}, u32[]{:S(2)}, u32[]{:S(2)}) %collective-permute-start) | collective-permute-done | bytes 262176 | tf_op jit(solution)/shard_map/ppermute | solution.py:32
  10.5 1.8 %collective-permute-start.5 = (bf16[256,512]{1,0:T(8,128)(2,1)S(1)}, bf16[256,512]{1,0:T(8,128)(2,1)S(1)}, u32[]{:S(2)}, u32[]{:S(2)}) collective-permute-start(bf16[256,512]{1,0:T(8,128)(2,1)S(1)} %collective-permute-done.refs_3_), channel_id=1, source_target_pairs={{0,8},{4,20},{8,0},{12,28},{16,24},{20,4},{24,16},{28,12},{1,9},{5... | collective-permute-start | bytes 786440 | tf_op jit(solution)/shard_map/ppermute | solution.py:32
  12.4 2.2 %copy-done = bf16[1,1,8,16,128,128]{5,4,3,2,1,0:T(8,128)(2,1)S(1)} copy-done((bf16[1,1,8,16,128,128]{5,4,3,2,1,0:T(8,128)(2,1)S(1)}, bf16[1,1,8,16,128,128]{5,4,3,2,1,0:T(8,128)(2,1)}, u32[]{:S(2)}) %copy-start) | copy-done | bytes 4194328
  14.6 2.6 %densify.1.refs_0_.a_ref = bf16[8,1024,256]{2,1,0:T(8,128)(2,1)S(1)} custom-call(s32[8,17]{1,0:T(8,128)S(1)} %pad_add_fusion.spots_ref, s32[2]{0:T(128)S(1)} %pad_add_fusion.1.place_ref, bf16[8,16,128,128]{3,2,1,0:T(8,128)(2,1)S(1)} %bitcast.26), custom_call_target="tpu_custom_call" | custom-call | flops 2097152 | bytes 16777216 | tf_op jit(solution)/shard_map/densify/pallas_call | solution.py:90
  17.2 1.2 %forward.4 = (f32[256,512]{1,0:T(8,128)S(1)}, f32[256,512]{1,0:T(8,128)S(1)}, f32[256,512]{1,0:T(8,128)S(1)}, f32[256,512]{1,0:T(8,128)S(1)}) custom-call(bf16[8,1024,256]{2,1,0:T(8,128)(2,1)S(1)} %densify.1.refs_0_.a_ref, bf16[256,512]{1,0:T(8,128)(2,1)S(1)} %copy-done.2, bf16[256,512]{1,0:T(8,128)(2,1)S(1)} %collective-permute-done.2.refs_2_, ...), custom_call_target="tpu_custom_call" | custom-call | flops 1073741824 | bytes 4194304 | tf_op jit(solution)/shard_map/forward/pallas_call | solution.py:144
  18.5 1.2 %collective-permute-done.1.refs_1_ = bf16[256,512]{1,0:T(8,128)(2,1)S(1)} collective-permute-done((bf16[256,512]{1,0:T(8,128)(2,1)}, bf16[256,512]{1,0:T(8,128)(2,1)S(1)}, u32[]{:S(2)}, u32[]{:S(2)}) %collective-permute-start.1) | collective-permute-done | bytes 262176 | tf_op jit(solution)/shard_map/ppermute | solution.py:32
  20.4 4.1 %collective-permute-done.5.refs_2_ = bf16[256,512]{1,0:T(8,128)(2,1)S(1)} collective-permute-done((bf16[256,512]{1,0:T(8,128)(2,1)S(1)}, bf16[256,512]{1,0:T(8,128)(2,1)S(1)}, u32[]{:S(2)}, u32[]{:S(2)}) %collective-permute-start.5) | collective-permute-done | bytes 262176 | tf_op jit(solution)/shard_map/ppermute | solution.py:32
  24.5 1.5 %collective-permute-start.6 = (bf16[256,512]{1,0:T(8,128)(2,1)S(1)}, bf16[256,512]{1,0:T(8,128)(2,1)S(1)}, u32[]{:S(2)}, u32[]{:S(2)}) collective-permute-start(bf16[256,512]{1,0:T(8,128)(2,1)S(1)} %collective-permute-done.5.refs_2_), channel_id=1, source_target_pairs={{0,4},{4,0},{8,12},{12,8},{16,20},{20,16},{24,28},{28,24},{1,5},{5... | collective-permute-start | bytes 786440 | tf_op jit(solution)/shard_map/ppermute | solution.py:26
  27.6 1.6 %collective-permute-start.8 = (bf16[256,512]{1,0:T(8,128)(2,1)S(1)}, bf16[256,512]{1,0:T(8,128)(2,1)S(1)}, u32[]{:S(2)}, u32[]{:S(2)}) collective-permute-start(bf16[256,512]{1,0:T(8,128)(2,1)S(1)} %get-tuple-element.55), channel_id=1, source_target_pairs={{0,1},{1,0},{2,3},{3,2},{4,6},{5,7},{6,4},{7,5},{8,9},{9,8},{10,11... | collective-permute-start | bytes 786440 | tf_op jit(solution)/shard_map/ppermute | solution.py:46
  30.1 3.9 %collective-permute-done.8 = bf16[256,512]{1,0:T(8,128)(2,1)S(1)} collective-permute-done((bf16[256,512]{1,0:T(8,128)(2,1)S(1)}, bf16[256,512]{1,0:T(8,128)(2,1)S(1)}, u32[]{:S(2)}, u32[]{:S(2)}) %collective-permute-start.8) | collective-permute-done | bytes 262176 | tf_op jit(solution)/shard_map/ppermute | solution.py:46
  34.7 2.6 %collective-permute-done.7.refs_1_ = bf16[256,512]{1,0:T(8,128)(2,1)S(1)} collective-permute-done((bf16[256,512]{1,0:T(8,128)(2,1)S(1)}, bf16[256,512]{1,0:T(8,128)(2,1)S(1)}, u32[]{:S(2)}, u32[]{:S(2)}) %collective-permute-start.7) | collective-permute-done | bytes 262176 | tf_op jit(solution)/shard_map/ppermute | solution.py:46
  37.3 1.2 %transposed.1 = (bf16[2,256,1024]{2,1,0:T(8,128)(2,1)S(1)}, bf16[2,256,1024]{2,1,0:T(8,128)(2,1)S(1)}, bf16[2,256,1024]{2,1,0:T(8,128)(2,1)S(1)}, bf16[2,256,1024]{2,1,0:T(8,128)(2,1)S(1)}) custom-call(bf16[8,1024,256]{2,1,0:T(8,128)(2,1)S(1)} %densify.1.refs_0_.a_ref), custom_call_target="tpu_custom_call" | custom-call | bytes 8388608 | tf_op jit(solution)/shard_map/transposed/pallas_call | solution.py:115
  38.5 2.0 %collective-permute-done.9.refs_2_ = bf16[256,512]{1,0:T(8,128)(2,1)S(1)} collective-permute-done((bf16[256,512]{1,0:T(8,128)(2,1)S(1)}, bf16[256,512]{1,0:T(8,128)(2,1)S(1)}, u32[]{:S(2)}, u32[]{:S(2)}) %collective-permute-start.9) | collective-permute-done | bytes 262176 | tf_op jit(solution)/shard_map/ppermute | solution.py:46
  40.6 1.2 %middle.1 = (bf16[256,512]{1,0:T(8,128)(2,1)}, bf16[256,512]{1,0:T(8,128)(2,1)S(1)}, bf16[256,512]{1,0:T(8,128)(2,1)S(1)}, bf16[256,512]{1,0:T(8,128)(2,1)S(1)}) custom-call(f32[256,512]{1,0:T(8,128)S(1)} %get-tuple-element.59.refs_0_, bf16[256,512]{1,0:T(8,128)(2,1)S(1)} %collective-permute-done.7.refs_1_, ...), custom_call_target="tpu_custom_call" | custom-call | flops 268435456 | bytes 1310720 | tf_op jit(solution)/shard_map/middle/pallas_call | solution.py:179
  41.7 0.9 %weight_part.1 = (f32[64,512]{1,0:T(8,128)S(1)}, f32[64,512]{1,0:T(8,128)S(1)}, f32[64,512]{1,0:T(8,128)S(1)}, f32[64,512]{1,0:T(8,128)S(1)}, bf16[256,512]{1,0:T(8,128)(2,1)S(1)}) custom-call(s32[2]{0:T(128)S(1)} %pad_add_fusion.1.place_ref, bf16[256,512]{1,0:T(8,128)(2,1)S(1)} %get-tuple-element.69.agg_ref, bf16[256,512]{1,0:T(8,128)(2,1)S(1)} %get-tuple-element.70.pre_grad_ref), custom_call_target="tpu_custom_call" | custom-call | flops 134217728 | bytes 1572864 | tf_op jit(solution)/shard_map/weight_part/pallas_call | solution.py:212
  43.3 0.9 %collective-permute-done.13 = bf16[256,512]{1,0:T(8,128)(2,1)S(1)} collective-permute-done((bf16[256,512]{1,0:T(8,128)(2,1)S(1)}, bf16[256,512]{1,0:T(8,128)(2,1)S(1)}, u32[]{:S(2)}, u32[]{:S(2)}) %collective-permute-start.13) | collective-permute-done | bytes 262176 | tf_op jit(solution)/shard_map/ppermute | solution.py:26
  44.3 1.6 %collective-permute-start.16 = (bf16[64,512]{1,0:T(8,128)(2,1)S(1)}, bf16[64,512]{1,0:T(8,128)(2,1)S(1)}, u32[]{:S(2)}, u32[]{:S(2)}) collective-permute-start(bf16[64,512]{1,0:T(8,128)(2,1)S(1)} %get-tuple-element.88), channel_id=1, source_target_pairs={{0,3},{1,2},{2,1},{3,0},{4,7},{5,6},{6,5},{7,4},{8,11},{9,10},{10,... | collective-permute-start | bytes 196616 | tf_op jit(solution)/shard_map/ppermute | solution.py:46
  45.9 1.5 %collective-permute-start.15 = (bf16[64,512]{1,0:T(8,128)(2,1)S(1)}, bf16[64,512]{1,0:T(8,128)(2,1)S(1)}, u32[]{:S(2)}, u32[]{:S(2)}) collective-permute-start(bf16[64,512]{1,0:T(8,128)(2,1)S(1)} %get-tuple-element.89), channel_id=1, source_target_pairs={{0,2},{1,3},{2,0},{3,1},{4,5},{5,4},{6,7},{7,6},{8,10},{9,11},{10,... | collective-permute-start | bytes 196616 | tf_op jit(solution)/shard_map/ppermute | solution.py:46
  47.9 1.5 %collective-permute-start.11 = (bf16[256,512]{1,0:T(8,128)(2,1)S(1)}, bf16[256,512]{1,0:T(8,128)(2,1)S(1)}, u32[]{:S(2)}, u32[]{:S(2)}) collective-permute-start(bf16[256,512]{1,0:T(8,128)(2,1)S(1)} %get-tuple-element.80.refs_2_), channel_id=1, source_target_pairs={{0,1},{1,0},{2,3},{3,2},{4,6},{5,7},{6,4},{7,5},{8,9},{9,8},{10,11... | collective-permute-start | bytes 786440 | tf_op jit(solution)/shard_map/ppermute | solution.py:46
  49.4 1.8 %collective-permute-done.10.refs_3_ = bf16[256,512]{1,0:T(8,128)(2,1)S(1)} collective-permute-done((bf16[256,512]{1,0:T(8,128)(2,1)S(1)}, bf16[256,512]{1,0:T(8,128)(2,1)S(1)}, u32[]{:S(2)}, u32[]{:S(2)}) %collective-permute-start.10) | collective-permute-done | bytes 262176 | tf_op jit(solution)/shard_map/ppermute | solution.py:46
  51.1 1.5 %collective-permute-start.12 = (bf16[256,512]{1,0:T(8,128)(2,1)S(1)}, bf16[256,512]{1,0:T(8,128)(2,1)S(1)}, u32[]{:S(2)}, u32[]{:S(2)}) collective-permute-start(bf16[256,512]{1,0:T(8,128)(2,1)S(1)} %collective-permute-done.10.refs_3_), channel_id=1, source_target_pairs={{0,1},{1,0},{2,3},{3,2},{4,6},{5,7},{6,4},{7,5},{8,9},{9,8},{10,11... | collective-permute-start | bytes 786440 | tf_op jit(solution)/shard_map/ppermute | solution.py:46
  52.8 4.3 %collective-permute-done.17 = bf16[64,512]{1,0:T(8,128)(2,1)S(1)} collective-permute-done((bf16[64,512]{1,0:T(8,128)(2,1)S(1)}, bf16[64,512]{1,0:T(8,128)(2,1)S(1)}, u32[]{:S(2)}, u32[]{:S(2)}) %collective-permute-start.17) | collective-permute-done | bytes 65568 | tf_op jit(solution)/shard_map/ppermute | solution.py:36
  58.4 3.1 %collective-permute-start.22 = (bf16[64,512]{1,0:T(8,128)(2,1)S(1)}, bf16[64,512]{1,0:T(8,128)(2,1)S(1)}, u32[]{:S(2)}, u32[]{:S(2)}) collective-permute-start(bf16[64,512]{1,0:T(8,128)(2,1)S(1)} %add_convert_fusion.3), channel_id=1, source_target_pairs={{0,16},{4,20},{8,24},{12,28},{16,0},{20,4},{24,8},{28,12},{1,17},{... | collective-permute-start | bytes 196616 | tf_op jit(solution)/shard_map/ppermute | solution.py:36
  64.0 3.1 %collective-permute-done.22 = bf16[64,512]{1,0:T(8,128)(2,1)S(1)} collective-permute-done((bf16[64,512]{1,0:T(8,128)(2,1)S(1)}, bf16[64,512]{1,0:T(8,128)(2,1)S(1)}, u32[]{:S(2)}, u32[]{:S(2)}) %collective-permute-start.22) | collective-permute-done | bytes 65568 | tf_op jit(solution)/shard_map/ppermute | solution.py:36
  67.2 1.6 %collective-permute-start.23 = (f32[64,512]{1,0:T(8,128)S(1)}, f32[64,512]{1,0:T(8,128)S(1)}, u32[]{:S(2)}, u32[]{:S(2)}) collective-permute-start(f32[64,512]{1,0:T(8,128)S(1)} %add_multiply_fusion.refs_0_), channel_id=1, source_target_pairs={{0,1},{1,0},{2,3},{3,2},{4,6},{5,7},{6,4},{7,5},{8,9},{9,8},{10,11... | collective-permute-start | bytes 393224 | tf_op jit(solution)/shard_map/ppermute | solution.py:46
  68.8 2.0 %collective-permute-start.25 = (f32[64,512]{1,0:T(8,128)S(1)}, f32[64,512]{1,0:T(8,128)S(1)}, u32[]{:S(2)}, u32[]{:S(2)}) collective-permute-start(f32[64,512]{1,0:T(8,128)S(1)} %add_multiply_fusion.refs_0_), channel_id=1, source_target_pairs={{0,3},{1,2},{2,1},{3,0},{4,7},{5,6},{6,5},{7,4},{8,11},{9,10},{10,... | collective-permute-start | bytes 393224 | tf_op jit(solution)/shard_map/ppermute | solution.py:46
  70.7 2.1 %collective-permute-done.23.refs_1_ = f32[64,512]{1,0:T(8,128)S(1)} collective-permute-done((f32[64,512]{1,0:T(8,128)S(1)}, f32[64,512]{1,0:T(8,128)S(1)}, u32[]{:S(2)}, u32[]{:S(2)}) %collective-permute-start.23) | collective-permute-done | bytes 131104 | tf_op jit(solution)/shard_map/ppermute | solution.py:46
  72.8 3.7 %collective-permute-done.24.refs_2_ = f32[64,512]{1,0:T(8,128)S(1)} collective-permute-done((f32[64,512]{1,0:T(8,128)S(1)}, f32[64,512]{1,0:T(8,128)S(1)}, u32[]{:S(2)}, u32[]{:S(2)}) %collective-permute-start.24) | collective-permute-done | bytes 131104 | tf_op jit(solution)/shard_map/ppermute | solution.py:46
  77.5 3.7 %collective-permute-start.21 = (bf16[256,512]{1,0:T(8,128)(2,1)S(1)}, bf16[256,512]{1,0:T(8,128)(2,1)S(1)}, u32[]{:S(2)}, u32[]{:S(2)}) collective-permute-start(bf16[256,512]{1,0:T(8,128)(2,1)S(1)} %get-tuple-element.84), channel_id=1, source_target_pairs={{0,16},{4,12},{8,24},{12,4},{16,0},{20,28},{24,8},{28,20},{1,17},{... | collective-permute-start | bytes 786440 | tf_op jit(solution)/shard_map/ppermute | solution.py:32
  81.2 1.6 %place_slices.1 = f32[512,512]{1,0:T(8,128)} custom-call(s32[2]{0:T(128)S(1)} %pad_add_fusion.1.place_ref, f32[64,512]{1,0:T(8,128)S(1)} %add_multiply_fusion.refs_0_, f32[64,512]{1,0:T(8,128)S(1)} %collective-permute-done.23.refs_1_, f32[64,512]{1,0:T(8,128)S(1)} %collective-permute-done.24.refs_2_, f32[64,512]{1,0:T(8,128)S(1)} %collective-permute-done.25.refs_3_, ...), custom_call_target="tpu_custom_call" | custom-call | bytes 2097152 | tf_op jit(solution)/shard_map/place_slices/pallas_call | solution.py:240
  82.8 5.4 %collective-permute-done.21.refs_1_ = bf16[256,512]{1,0:T(8,128)(2,1)S(1)} collective-permute-done((bf16[256,512]{1,0:T(8,128)(2,1)S(1)}, bf16[256,512]{1,0:T(8,128)(2,1)S(1)}, u32[]{:S(2)}, u32[]{:S(2)}) %collective-permute-start.21) | collective-permute-done | bytes 262176 | tf_op jit(solution)/shard_map/ppermute | solution.py:32
  (57 shorter events, 12.7 us)
Async XLA Ops:
  0.6 9.6 %collective-permute-start = (bf16[256,512]{1,0:T(8,128)(2,1)}, bf16[256,512]{1,0:T(8,128)(2,1)S(1)}, u32[]{:S(2)}, u32[]{:S(2)}) collective-permute-start(bf16[256,512]{1,0:T(8,128)(2,1)} %refs_1_.1), channel_id=1, source_target_pairs={{0,16},{4,12},{8,24},{12,4},{16,0},{20,28},{24,8},{28,20},{1,17},{... | collective-permute-start | bytes 786440 | tf_op jit(solution)/shard_map/ppermute | solution.py:32
  3.3 13.9 %collective-permute-start.2 = (bf16[256,512]{1,0:T(8,128)(2,1)}, bf16[256,512]{1,0:T(8,128)(2,1)S(1)}, u32[]{:S(2)}, u32[]{:S(2)}) collective-permute-start(bf16[256,512]{1,0:T(8,128)(2,1)} %refs_1_.1), channel_id=1, source_target_pairs={{0,4},{4,0},{8,12},{12,8},{16,20},{20,16},{24,28},{28,24},{1,5},{5... | collective-permute-start | bytes 786440 | tf_op jit(solution)/shard_map/ppermute | solution.py:26
  10.3 6.9 %collective-permute-start.3 = (bf16[256,512]{1,0:T(8,128)(2,1)S(1)}, bf16[256,512]{1,0:T(8,128)(2,1)S(1)}, u32[]{:S(2)}, u32[]{:S(2)}) collective-permute-start(bf16[256,512]{1,0:T(8,128)(2,1)S(1)} %collective-permute-done.refs_3_), channel_id=1, source_target_pairs={{0,4},{4,0},{8,12},{12,8},{16,20},{20,16},{24,28},{28,24},{1,5},{5... | collective-permute-start | bytes 786440 | tf_op jit(solution)/shard_map/ppermute | solution.py:26
  10.3 9.4 %collective-permute-start.1 = (bf16[256,512]{1,0:T(8,128)(2,1)}, bf16[256,512]{1,0:T(8,128)(2,1)S(1)}, u32[]{:S(2)}, u32[]{:S(2)}) collective-permute-start(bf16[256,512]{1,0:T(8,128)(2,1)} %refs_1_.1), channel_id=1, source_target_pairs={{0,8},{4,20},{8,0},{12,28},{16,24},{20,4},{24,16},{28,12},{1,9},{5... | collective-permute-start | bytes 786440 | tf_op jit(solution)/shard_map/ppermute | solution.py:32
  10.5 14.0 %collective-permute-start.5 = (bf16[256,512]{1,0:T(8,128)(2,1)S(1)}, bf16[256,512]{1,0:T(8,128)(2,1)S(1)}, u32[]{:S(2)}, u32[]{:S(2)}) collective-permute-start(bf16[256,512]{1,0:T(8,128)(2,1)S(1)} %collective-permute-done.refs_3_), channel_id=1, source_target_pairs={{0,8},{4,20},{8,0},{12,28},{16,24},{20,4},{24,16},{28,12},{1,9},{5... | collective-permute-start | bytes 786440 | tf_op jit(solution)/shard_map/ppermute | solution.py:32
  12.4 2.2 %copy-start = (bf16[1,1,8,16,128,128]{5,4,3,2,1,0:T(8,128)(2,1)S(1)}, bf16[1,1,8,16,128,128]{5,4,3,2,1,0:T(8,128)(2,1)}, u32[]{:S(2)}) copy-start(bf16[1,1,8,16,128,128]{5,4,3,2,1,0:T(8,128)(2,1)} %param.10) | copy-start | bytes 12582916
  14.6 2.6 %copy-start.2 = (bf16[256,512]{1,0:T(8,128)(2,1)S(1)}, bf16[256,512]{1,0:T(8,128)(2,1)}, u32[]{:S(2)}) copy-start(bf16[256,512]{1,0:T(8,128)(2,1)} %refs_1_.1) | copy-start | bytes 786436
  19.6 7.1 %collective-permute-start.4 = (bf16[256,512]{1,0:T(8,128)(2,1)S(1)}, bf16[256,512]{1,0:T(8,128)(2,1)S(1)}, u32[]{:S(2)}, u32[]{:S(2)}) collective-permute-start(bf16[256,512]{1,0:T(8,128)(2,1)S(1)} %collective-permute-done.1.refs_1_), channel_id=1, source_target_pairs={{0,4},{4,0},{8,12},{12,8},{16,20},{20,16},{24,28},{28,24},{1,5},{5... | collective-permute-start | bytes 786440 | tf_op jit(solution)/shard_map/ppermute | solution.py:26
  24.5 2.7 %collective-permute-start.6 = (bf16[256,512]{1,0:T(8,128)(2,1)S(1)}, bf16[256,512]{1,0:T(8,128)(2,1)S(1)}, u32[]{:S(2)}, u32[]{:S(2)}) collective-permute-start(bf16[256,512]{1,0:T(8,128)(2,1)S(1)} %collective-permute-done.5.refs_2_), channel_id=1, source_target_pairs={{0,4},{4,0},{8,12},{12,8},{16,20},{20,16},{24,28},{28,24},{1,5},{5... | collective-permute-start | bytes 786440 | tf_op jit(solution)/shard_map/ppermute | solution.py:26
  27.6 6.4 %collective-permute-start.8 = (bf16[256,512]{1,0:T(8,128)(2,1)S(1)}, bf16[256,512]{1,0:T(8,128)(2,1)S(1)}, u32[]{:S(2)}, u32[]{:S(2)}) collective-permute-start(bf16[256,512]{1,0:T(8,128)(2,1)S(1)} %get-tuple-element.55), channel_id=1, source_target_pairs={{0,1},{1,0},{2,3},{3,2},{4,6},{5,7},{6,4},{7,5},{8,9},{9,8},{10,11... | collective-permute-start | bytes 786440 | tf_op jit(solution)/shard_map/ppermute | solution.py:46
  29.2 8.2 %collective-permute-start.7 = (bf16[256,512]{1,0:T(8,128)(2,1)S(1)}, bf16[256,512]{1,0:T(8,128)(2,1)S(1)}, u32[]{:S(2)}, u32[]{:S(2)}) collective-permute-start(bf16[256,512]{1,0:T(8,128)(2,1)S(1)} %get-tuple-element.54), channel_id=1, source_target_pairs={{0,1},{1,0},{2,3},{3,2},{4,6},{5,7},{6,4},{7,5},{8,9},{9,8},{10,11... | collective-permute-start | bytes 786440 | tf_op jit(solution)/shard_map/ppermute | solution.py:46
  29.7 10.9 %copy-start.1 = (bf16[512,512]{1,0:T(8,128)(2,1)S(1)}, bf16[512,512]{1,0:T(8,128)(2,1)}, u32[]{:S(2)}) copy-start(bf16[512,512]{1,0:T(8,128)(2,1)} %refs_4_.1) | copy-start | bytes 1572868
  29.7 10.9 %copy-start.3 = (bf16[256,512]{1,0:T(8,128)(2,1)S(1)}, bf16[256,512]{1,0:T(8,128)(2,1)}, u32[]{:S(2)}) copy-start(bf16[256,512]{1,0:T(8,128)(2,1)} %refs_3_.1) | copy-start | bytes 786436
  34.1 6.4 %collective-permute-start.9 = (bf16[256,512]{1,0:T(8,128)(2,1)S(1)}, bf16[256,512]{1,0:T(8,128)(2,1)S(1)}, u32[]{:S(2)}, u32[]{:S(2)}) collective-permute-start(bf16[256,512]{1,0:T(8,128)(2,1)S(1)} %add_convert_fusion.2), channel_id=1, source_target_pairs={{0,2},{1,3},{2,0},{3,1},{4,5},{5,4},{6,7},{7,6},{8,10},{9,11},{10,... | collective-permute-start | bytes 786440 | tf_op jit(solution)/shard_map/ppermute | solution.py:46
  42.7 1.6 %collective-permute-start.13 = (bf16[256,512]{1,0:T(8,128)(2,1)S(1)}, bf16[256,512]{1,0:T(8,128)(2,1)S(1)}, u32[]{:S(2)}, u32[]{:S(2)}) collective-permute-start(bf16[256,512]{1,0:T(8,128)(2,1)S(1)} %get-tuple-element.72), channel_id=1, source_target_pairs={{0,4},{4,0},{8,12},{12,8},{16,20},{20,16},{24,28},{28,24},{1,5},{5... | collective-permute-start | bytes 786440 | tf_op jit(solution)/shard_map/ppermute | solution.py:26
  42.7 8.4 %collective-permute-start.10 = (bf16[256,512]{1,0:T(8,128)(2,1)S(1)}, bf16[256,512]{1,0:T(8,128)(2,1)S(1)}, u32[]{:S(2)}, u32[]{:S(2)}) collective-permute-start(bf16[256,512]{1,0:T(8,128)(2,1)S(1)} %get-tuple-element.80.refs_2_), channel_id=1, source_target_pairs={{0,2},{1,3},{2,0},{3,1},{4,5},{5,4},{6,7},{7,6},{8,10},{9,11},{10,... | collective-permute-start | bytes 786440 | tf_op jit(solution)/shard_map/ppermute | solution.py:46
  44.3 8.3 %collective-permute-start.16 = (bf16[64,512]{1,0:T(8,128)(2,1)S(1)}, bf16[64,512]{1,0:T(8,128)(2,1)S(1)}, u32[]{:S(2)}, u32[]{:S(2)}) collective-permute-start(bf16[64,512]{1,0:T(8,128)(2,1)S(1)} %get-tuple-element.88), channel_id=1, source_target_pairs={{0,3},{1,2},{2,1},{3,0},{4,7},{5,6},{6,5},{7,4},{8,11},{9,10},{10,... | collective-permute-start | bytes 196616 | tf_op jit(solution)/shard_map/ppermute | solution.py:46
  45.9 6.8 %collective-permute-start.15 = (bf16[64,512]{1,0:T(8,128)(2,1)S(1)}, bf16[64,512]{1,0:T(8,128)(2,1)S(1)}, u32[]{:S(2)}, u32[]{:S(2)}) collective-permute-start(bf16[64,512]{1,0:T(8,128)(2,1)S(1)} %get-tuple-element.89), channel_id=1, source_target_pairs={{0,2},{1,3},{2,0},{3,1},{4,5},{5,4},{6,7},{7,6},{8,10},{9,11},{10,... | collective-permute-start | bytes 196616 | tf_op jit(solution)/shard_map/ppermute | solution.py:46
  47.3 5.3 %collective-permute-start.14 = (bf16[64,512]{1,0:T(8,128)(2,1)S(1)}, bf16[64,512]{1,0:T(8,128)(2,1)S(1)}, u32[]{:S(2)}, u32[]{:S(2)}) collective-permute-start(bf16[64,512]{1,0:T(8,128)(2,1)S(1)} %get-tuple-element.87), channel_id=1, source_target_pairs={{0,1},{1,0},{2,3},{3,2},{4,6},{5,7},{6,4},{7,5},{8,9},{9,8},{10,11... | collective-permute-start | bytes 196616 | tf_op jit(solution)/shard_map/ppermute | solution.py:46
  47.9 9.6 %collective-permute-start.11 = (bf16[256,512]{1,0:T(8,128)(2,1)S(1)}, bf16[256,512]{1,0:T(8,128)(2,1)S(1)}, u32[]{:S(2)}, u32[]{:S(2)}) collective-permute-start(bf16[256,512]{1,0:T(8,128)(2,1)S(1)} %get-tuple-element.80.refs_2_), channel_id=1, source_target_pairs={{0,1},{1,0},{2,3},{3,2},{4,6},{5,7},{6,4},{7,5},{8,9},{9,8},{10,11... | collective-permute-start | bytes 786440 | tf_op jit(solution)/shard_map/ppermute | solution.py:46
  51.1 6.4 %collective-permute-start.12 = (bf16[256,512]{1,0:T(8,128)(2,1)S(1)}, bf16[256,512]{1,0:T(8,128)(2,1)S(1)}, u32[]{:S(2)}, u32[]{:S(2)}) collective-permute-start(bf16[256,512]{1,0:T(8,128)(2,1)S(1)} %collective-permute-done.10.refs_3_), channel_id=1, source_target_pairs={{0,1},{1,0},{2,3},{3,2},{4,6},{5,7},{6,4},{7,5},{8,9},{9,8},{10,11... | collective-permute-start | bytes 786440 | tf_op jit(solution)/shard_map/ppermute | solution.py:46
  52.7 4.3 %collective-permute-start.17 = (bf16[64,512]{1,0:T(8,128)(2,1)S(1)}, bf16[64,512]{1,0:T(8,128)(2,1)S(1)}, u32[]{:S(2)}, u32[]{:S(2)}) collective-permute-start(bf16[64,512]{1,0:T(8,128)(2,1)S(1)} %add_convert_fusion.4), channel_id=1, source_target_pairs={{0,8},{4,12},{8,0},{12,4},{16,24},{20,28},{24,16},{28,20},{1,9},{5... | collective-permute-start | bytes 196616 | tf_op jit(solution)/shard_map/ppermute | solution.py:36
  58.2 4.0 %collective-permute-start.18 = (bf16[512,512]{1,0:T(8,128)(2,1)S(1)}, bf16[512,512]{1,0:T(8,128)(2,1)S(1)}, u32[]{:S(2)}, u32[]{:S(2)}) collective-permute-start(bf16[512,512]{1,0:T(8,128)(2,1)S(1)} %backward.4), channel_id=1, source_target_pairs={{0,4},{4,0},{8,12},{12,8},{16,20},{20,16},{24,28},{28,24},{1,5},{5... | collective-permute-start | bytes 1572872 | tf_op jit(solution)/shard_map/ppermute | solution.py:26
  58.4 8.8 %collective-permute-start.22 = (bf16[64,512]{1,0:T(8,128)(2,1)S(1)}, bf16[64,512]{1,0:T(8,128)(2,1)S(1)}, u32[]{:S(2)}, u32[]{:S(2)}) collective-permute-start(bf16[64,512]{1,0:T(8,128)(2,1)S(1)} %add_convert_fusion.3), channel_id=1, source_target_pairs={{0,16},{4,20},{8,24},{12,28},{16,0},{20,4},{24,8},{28,12},{1,17},{... | collective-permute-start | bytes 196616 | tf_op jit(solution)/shard_map/ppermute | solution.py:36
  62.4 15.0 %collective-permute-start.20 = (bf16[512,512]{1,0:T(8,128)(2,1)S(1)}, bf16[512,512]{1,0:T(8,128)(2,1)S(1)}, u32[]{:S(2)}, u32[]{:S(2)}) collective-permute-start(bf16[512,512]{1,0:T(8,128)(2,1)S(1)} %pad_maximum_fusion), channel_id=1, source_target_pairs={{0,8},{4,20},{8,0},{12,28},{16,24},{20,4},{24,16},{28,12},{1,9},{5... | collective-permute-start | bytes 1572872 | tf_op jit(solution)/shard_map/ppermute | solution.py:32
  63.2 14.2 %collective-permute-start.19 = (bf16[512,512]{1,0:T(8,128)(2,1)S(1)}, bf16[512,512]{1,0:T(8,128)(2,1)S(1)}, u32[]{:S(2)}, u32[]{:S(2)}) collective-permute-start(bf16[512,512]{1,0:T(8,128)(2,1)S(1)} %backward.7), channel_id=1, source_target_pairs={{0,4},{4,0},{8,12},{12,8},{16,20},{20,16},{24,28},{28,24},{1,5},{5... | collective-permute-start | bytes 1572872 | tf_op jit(solution)/shard_map/ppermute | solution.py:26
  67.2 5.6 %collective-permute-start.23 = (f32[64,512]{1,0:T(8,128)S(1)}, f32[64,512]{1,0:T(8,128)S(1)}, u32[]{:S(2)}, u32[]{:S(2)}) collective-permute-start(f32[64,512]{1,0:T(8,128)S(1)} %add_multiply_fusion.refs_0_), channel_id=1, source_target_pairs={{0,1},{1,0},{2,3},{3,2},{4,6},{5,7},{6,4},{7,5},{8,9},{9,8},{10,11... | collective-permute-start | bytes 393224 | tf_op jit(solution)/shard_map/ppermute | solution.py:46
  68.8 7.8 %collective-permute-start.24 = (f32[64,512]{1,0:T(8,128)S(1)}, f32[64,512]{1,0:T(8,128)S(1)}, u32[]{:S(2)}, u32[]{:S(2)}) collective-permute-start(f32[64,512]{1,0:T(8,128)S(1)} %add_multiply_fusion.refs_0_), channel_id=1, source_target_pairs={{0,2},{1,3},{2,0},{3,1},{4,5},{5,4},{6,7},{7,6},{8,10},{9,11},{10,... | collective-permute-start | bytes 393224 | tf_op jit(solution)/shard_map/ppermute | solution.py:46
  68.8 7.8 %collective-permute-start.25 = (f32[64,512]{1,0:T(8,128)S(1)}, f32[64,512]{1,0:T(8,128)S(1)}, u32[]{:S(2)}, u32[]{:S(2)}) collective-permute-start(f32[64,512]{1,0:T(8,128)S(1)} %add_multiply_fusion.refs_0_), channel_id=1, source_target_pairs={{0,3},{1,2},{2,1},{3,0},{4,7},{5,6},{6,5},{7,4},{8,11},{9,10},{10,... | collective-permute-start | bytes 393224 | tf_op jit(solution)/shard_map/ppermute | solution.py:46
  76.6 4.6 %collective-permute-start.26 = (f32[256,512]{1,0:T(8,128)S(1)}, f32[256,512]{1,0:T(8,128)S(1)}, u32[]{:S(2)}, u32[]{:S(2)}) collective-permute-start(f32[256,512]{1,0:T(8,128)S(1)} %pad_maximum_fusion.1), channel_id=1, source_target_pairs={{0,4},{4,0},{8,12},{12,8},{16,20},{20,16},{24,28},{28,24},{1,5},{5... | collective-permute-start | bytes 1572872 | tf_op jit(solution)/shard_map/ppermute | solution.py:26
  77.5 10.6 %collective-permute-start.21 = (bf16[256,512]{1,0:T(8,128)(2,1)S(1)}, bf16[256,512]{1,0:T(8,128)(2,1)S(1)}, u32[]{:S(2)}, u32[]{:S(2)}) collective-permute-start(bf16[256,512]{1,0:T(8,128)(2,1)S(1)} %get-tuple-element.84), channel_id=1, source_target_pairs={{0,16},{4,12},{8,24},{12,4},{16,0},{20,28},{24,8},{28,20},{1,17},{... | collective-permute-start | bytes 786440 | tf_op jit(solution)/shard_map/ppermute | solution.py:32
